TPU v7x, 32 devices: a whole 2x2x4 slice. The times are simulated.
32 devices in a mesh: ctx: 8 (over y, x, core), fsdp: 4 (over z).
Axes of the slice: x: 2, y: 2, z: 4, core: 2. Of those that a mesh axis runs over, the one named last changes fastest.
Arguments:
- query_mr: bfloat16 [1024, 4096], P('ctx', 'fsdp'), may hold values from -6 to 6
- key_mr: bfloat16 [1024, 4096], P('ctx', 'fsdp'), may hold values from -6 to 6
- value_mr: bfloat16 [1024, 4096], P('ctx', 'fsdp'), may hold values from -6 to 6
- query_li: bfloat16 [1024, 4096], P('ctx', 'fsdp'), may hold values from -6 to 6
- key_li: bfloat16 [1024, 4096], P('ctx', 'fsdp'), may hold values from -6 to 6
- mr_taps: float32 [128, 4096], P(None, 'fsdp'), may hold values from -0.5 to 0.5
- li_time: float32 [16, 4096], P(None, 'fsdp'), may hold values from 30 to 20480
- li_residue: float32 [16, 4096], P(None, 'fsdp'), may hold values from -5 to 5
- li_skip: float32 [4096], P('fsdp'), may hold values from -6 to 6
- out_weight: bfloat16 [4096, 4096], P('ctx', 'fsdp'), may hold values from -0.09375 to 0.09375
- cotangent: bfloat16 [1024, 4096], P('ctx', 'fsdp'), may hold values from -6 to 6
Outputs:
- output: float32 [1024, 4096], P('ctx', 'fsdp')
- grad_query_mr: float32 [1024, 4096], P('ctx', 'fsdp')
- grad_key_mr: float32 [1024, 4096], P('ctx', 'fsdp')
- grad_value_mr: float32 [1024, 4096], P('ctx', 'fsdp')
- grad_query_li: float32 [1024, 4096], P('ctx', 'fsdp')
- grad_key_li: float32 [1024, 4096], P('ctx', 'fsdp')
- grad_taps: float32 [128, 4096], P(None, 'fsdp')
- grad_weight: float32 [4096, 4096], P('ctx', 'fsdp')
All inputs are finite; a program needn't handle non-finite values.
Results may differ from a plain program's by a relative error of at most 0.014.
Values may be sent and summed in bfloat16 or wider, within the bound.
No kernel may reach another device: no remote copies, remote signals or barrier semaphores. Data moves between devices by JAX's collectives and lax.ppermute only.
A program may use at most 128 MiB of HBM per device.

v0:
```python
import functools
import math

import jax
import jax.numpy as jnp
import ml_dtypes
import numpy as np
from jax import lax
from jax.experimental import pallas as pl
from jax.experimental.pallas import tpu as pltpu
from jax.sharding import PartitionSpec as P

F32 = jnp.float32
BF16 = jnp.bfloat16
TILE = 256
GROUP = 8


def split_parts(matrix):
    high = matrix.astype(ml_dtypes.bfloat16)
    low = (matrix - high.astype(np.float64)).astype(ml_dtypes.bfloat16)
    return high, low


def two_fold(matrix):
    high, low = split_parts(matrix)
    return np.concatenate([high, low], axis=1)


def three_fold(matrix):
    high, low = split_parts(matrix)
    return np.concatenate([high, low, high], axis=1)


@functools.lru_cache(maxsize=None)
def dft_tables(rows):
    size = 2 * rows
    angle = 2.0 * np.pi * (np.arange(rows)[:, None] + 0.5) * np.arange(size)[None, :] / size
    ahead = np.concatenate([np.cos(angle), -np.sin(angle)], axis=0)
    back = ahead.T * (2.0 / size)
    signed = np.concatenate([back[:rows], -back[rows:]], axis=0)
    lags = back[rows - np.arange(rows)]
    return {
        "full2": two_fold(ahead),
        "half2": two_fold(ahead[:, :rows]),
        "half3": three_fold(ahead[:, :rows]),
        "first3": three_fold(back[:rows]),
        "last3": three_fold(back[rows:]),
        "both3": three_fold(signed),
        "lags3": three_fold(lags),
    }


def apply2(table, x):
    return jnp.dot(table, jnp.concatenate([x, x], axis=0), preferred_element_type=F32)


def apply3(table, x):
    high = x.astype(BF16)
    low = (x - high.astype(F32)).astype(BF16)
    return jnp.dot(table, jnp.concatenate([high, high, low], axis=0), preferred_element_type=F32)


def times(x, y):
    half = x.shape[0] // 2
    xr, xi, yr, yi = x[:half], x[half:], y[:half], y[half:]
    return jnp.concatenate([xr * yr - xi * yi, xr * yi + xi * yr], axis=0)


def times_conj(x, y):
    half = x.shape[0] // 2
    xr, xi, yr, yi = x[:half], x[half:], y[:half], y[half:]
    return jnp.concatenate([xr * yr + xi * yi, xi * yr - xr * yi], axis=0)


def group_places(columns):
    return lax.broadcasted_iota(jnp.int32, (GROUP, columns), 0).astype(F32)


def spread_modes(rate, weight, rows, shift, backward):
    columns = rate.shape[1]
    places = group_places(columns)
    if backward:
        places = (GROUP - 1.0) - places
    count = rows // GROUP
    order = range(count - 1, -1, -1) if backward else range(count)
    sums = [None] * count
    for m in range(rate.shape[0]):
        rate_m = rate[m : m + 1]
        current = weight[m : m + 1] * jnp.exp(-rate_m * (places + shift))
        stride = jnp.broadcast_to(jnp.exp(-rate_m * GROUP), current.shape)
        for step, g in enumerate(order):
            sums[g] = current if sums[g] is None else sums[g] + current
            if step < count - 1:
                current = current * stride
    return jnp.concatenate(sums, axis=0)


def fold_modes(signal, rate, backward):
    columns = rate.shape[1]
    places = group_places(columns)
    if not backward:
        places = (GROUP - 1.0) - places
    count = signal.shape[0] // GROUP
    order = range(count - 1, -1, -1) if backward else range(count)
    found = []
    for m in range(rate.shape[0]):
        rate_m = rate[m : m + 1]
        stride = jnp.broadcast_to(jnp.exp(-rate_m * GROUP), (GROUP, columns))
        running = None
        for g in order:
            piece = signal[g * GROUP : (g + 1) * GROUP]
            running = piece if running is None else running * stride + piece
        found.append(jnp.sum(running * jnp.exp(-rate_m * places), axis=0, keepdims=True))
    return jnp.concatenate(found, axis=0)


def gather_states(rate, gaps, states, sibling, inner, rows):
    total = jnp.zeros_like(rate)
    for gap, state in zip(gaps, states):
        weight = jnp.exp(-rate * (jnp.maximum(gap, 0.0) * (2.0 * rows)))
        total = total + jnp.where(gap >= 0.0, weight * state, 0.0)
    return jnp.where(inner > 0.0, jnp.exp(-rate * float(rows)) * total + sibling, total)


def spectra_body(taps, rate, coef, skip, half3, mr_spec, li_spec):
    rows = taps.shape[0]
    mr_spec[...] = apply3(half3[...], taps[...])
    kernel = spread_modes(rate[...], coef[...], rows, 0.0, False)
    first = lax.broadcasted_iota(jnp.int32, kernel.shape, 0) == 0
    kernel = kernel + jnp.where(first, skip[...], 0.0)
    li_spec[...] = apply3(half3[...], kernel)


def short_body(before, product, query, key, mr_spec, rate, full2, last3, spec, conv, mixed, signal, ends):
    x = jnp.concatenate([before[...], product[...]], axis=0)
    found = apply2(full2[...], x)
    spec[...] = found
    filtered = apply3(last3[...], times(found, mr_spec[...]))
    conv[...] = filtered
    mixed_rows = (query[...].astype(F32) * filtered).astype(BF16)
    mixed[...] = mixed_rows
    rounded = (key[...].astype(F32) * mixed_rows.astype(F32)).astype(BF16)
    signal[...] = rounded
    ends[...] = fold_modes(rounded.astype(F32), rate[...], False)


def inner_body(signal, li_spec, half2, first3, inner):
    inner[...] = apply3(first3[...], times(apply2(half2[...], signal[...]), li_spec[...]))


def long_body(count, scalars, inner, query, rate, coef, sibling, *rest):
    states, (li_out, mixed) = rest[:count], rest[count:]
    rows = inner.shape[0]
    rates = rate[...]
    entering = gather_states(
        rates,
        [scalars[1 + k] for k in range(count)],
        [state[...] for state in states],
        sibling[...],
        scalars[0],
        rows,
    )
    total = inner[...] + spread_modes(rates, coef[...] * entering, rows, 1.0, False)
    li_out[...] = total
    mixed[...] = (query[...].astype(F32) * total).astype(BF16)


def grad_gate_body(count, own, query, rate, *rest):
    parts, (grad_mixed, grad_out, ends) = rest[:count], rest[count:]
    total = own[...]
    for part in parts:
        total = total + part[...].astype(F32)
    grad_mixed[...] = total
    gated = total * query[...].astype(F32)
    grad_out[...] = gated
    ends[...] = fold_modes(gated, rate[...], True)


def grad_inner_body(grad_out, li_spec, half3, first3, inner):
    inner[...] = apply3(first3[...], times_conj(apply3(half3[...], grad_out[...]), li_spec[...]))


def grad_long_body(
    count, scalars, inner, rate, coef, sibling, mixed_mr, key_li, query_mr, conv, spec, mr_spec, half3, both3, lags3, *rest
):
    states = rest[:count]
    grad_key_li, grad_query_mr, own_product, prev_product, taps = rest[count:]
    rows = inner.shape[0]
    rates = rate[...]
    entering = gather_states(
        rates,
        [scalars[1 + k] for k in range(count)],
        [state[...] for state in states],
        sibling[...],
        scalars[0],
        rows,
    )
    grad_input = inner[...] + spread_modes(rates, coef[...] * entering, rows, 1.0, True)
    grad_key_li[...] = grad_input * mixed_mr[...].astype(F32)
    grad_mixed_mr = grad_input * key_li[...].astype(F32)
    grad_query_mr[...] = grad_mixed_mr * conv[...]
    grad_conv = grad_mixed_mr * query_mr[...].astype(F32)
    found = apply3(half3[...], grad_conv)
    products = apply3(both3[...], times_conj(found, mr_spec[...]))
    own_product[...] = products[:rows]
    prev_product[...] = products[rows:].astype(BF16)
    taps[...] = apply3(lags3[...], times_conj(spec[...], found))


def grad_product_body(own, arrived, key, value, grad_key, grad_value):
    total = own[...] + arrived[...].astype(F32)
    grad_key[...] = total * value[...].astype(F32)
    grad_value[...] = total * key[...].astype(F32)


def run(body, columns, inputs, outputs, flops):
    tile = min(TILE, columns)
    in_specs = []
    moved = 0
    for kind, array in inputs:
        if kind == "tile":
            in_specs.append(pl.BlockSpec((array.shape[0], tile), lambda c: (0, c)))
        elif kind == "whole":
            in_specs.append(pl.BlockSpec(array.shape, lambda c: (0, 0)))
        else:
            in_specs.append(pl.BlockSpec(memory_space=pltpu.SMEM))
        moved += math.prod(array.shape) * array.dtype.itemsize
    for rows, dtype in outputs:
        moved += rows * columns * jnp.dtype(dtype).itemsize
    return pl.pallas_call(
        body,
        grid=(columns // tile,),
        in_specs=in_specs,
        out_specs=[pl.BlockSpec((rows, tile), lambda c: (0, c)) for rows, _ in outputs],
        out_shape=[jax.ShapeDtypeStruct((rows, columns), dtype) for rows, dtype in outputs],
        compiler_params=pltpu.CompilerParams(vmem_limit_bytes=32 * 1024 * 1024),
        cost_estimate=pl.CostEstimate(flops=flops, bytes_accessed=moved, transcendentals=0),
    )(*[array for _, array in inputs])


def chip_swap(x, by):
    size = lax.axis_size("ctx")
    return lax.ppermute(x, "ctx", [(i, i ^ (2 * by)) for i in range(size)])


def core_swap(x):
    size = lax.axis_size("ctx")
    return lax.ppermute(x, "ctx", [(i, i ^ 1) for i in range(size)])


def line_swap(x, by):
    size = lax.axis_size("fsdp")
    return lax.ppermute(x, "fsdp", [(i, i ^ by) for i in range(size)])


def shifted(x, by):
    size = lax.axis_size("ctx")
    return lax.ppermute(x, "ctx", [(i, i + by) for i in range(size) if 0 <= i + by < size])


def columns_at(x, index, width):
    return lax.dynamic_slice_in_dim(x, index * width, width, 1)


def placed(pieces):
    width = pieces[0][1].shape[1]
    whole = jnp.zeros((pieces[0][1].shape[0], width * len(pieces)), pieces[0][1].dtype)
    for index, piece in pieces:
        whole = lax.dynamic_update_slice_in_dim(whole, piece, index * width, 1)
    return whole


def pair_sum(values):
    while len(values) > 1:
        values = [values[k] + values[k + 1] for k in range(0, len(values), 2)]
    return values[0]


def shards(
    query_mr,
    key_mr,
    value_mr,
    query_li,
    key_li,
    mr_taps,
    li_time,
    li_residue,
    li_skip,
    out_weight,
    cotangent,
):
    rows, columns = query_mr.shape
    ctx_count = lax.axis_size("ctx")
    line_count = lax.axis_size("fsdp")
    chips = ctx_count // 2
    here = lax.axis_index("ctx")
    chip, core = here // 2, here % 2
    line = lax.axis_index("fsdp")
    grad_scale = 1.0 / math.sqrt(rows * ctx_count)
    tables = {name: jnp.asarray(table) for name, table in dft_tables(rows).items()}
    width = out_weight.shape[0]
    chip_width = 2 * width
    pass_flops = 2 * (2 * rows) * (2 * rows) * columns

    def tile(x):
        return ("tile", x)

    def table(name):
        return ("whole", tables[name])

    mr_product = (key_mr.astype(F32) * value_mr.astype(F32)).astype(BF16)
    before = shifted(mr_product, 1)

    cot_line = [cotangent] + [line_swap(cotangent, r) for r in range(1, line_count)]
    other_weight = core_swap(out_weight)
    weight_pair = jnp.where(
        core == 0,
        jnp.concatenate([out_weight, other_weight], axis=0),
        jnp.concatenate([other_weight, out_weight], axis=0),
    )
    cot_full = placed([(line ^ r, piece) for r, piece in enumerate(cot_line)])
    cot_parts = [columns_at(cot_full, chip, chip_width)]
    for s in range(1, chips):
        cot_parts.append(chip_swap(columns_at(cot_full, chip ^ s, chip_width), s))

    rate = 1.0 / li_time
    coef = li_residue * jnp.sqrt(-jnp.expm1(-2.0 * rate))
    block_decay = jnp.exp(-rate * float(rows))
    inner_ahead = (core == 1).astype(F32)[None]
    peers = jnp.stack([chip ^ s for s in range(1, chips)]).astype(F32)
    chip_f = chip.astype(F32)
    ahead_scalars = jnp.concatenate([inner_ahead, chip_f - 1.0 - peers])
    back_scalars = jnp.concatenate([1.0 - inner_ahead, peers - chip_f - 1.0])

    mr_spec, li_spec = run(
        spectra_body,
        columns,
        [tile(mr_taps), tile(rate), tile(coef), tile(li_skip[None, :]), table("half3")],
        [(2 * rows, F32), (2 * rows, F32)],
        3 * pass_flops,
    )
    spec, mr_conv, mixed_mr, li_input, ends = run(
        short_body,
        columns,
        [
            tile(before),
            tile(mr_product),
            tile(query_mr),
            tile(key_li),
            tile(mr_spec),
            tile(rate),
            table("full2"),
            table("last3"),
        ],
        [(2 * rows, F32), (rows, F32), (rows, BF16), (rows, BF16), (rate.shape[0], F32)],
        4 * pass_flops,
    )

    def exchange(ends, backward):
        sibling = core_swap(ends)
        near, far = (sibling, ends) if backward else (ends, sibling)
        chip_state = jnp.where(core == 0, block_decay * near + far, block_decay * far + near)
        return sibling, [chip_swap(chip_state, s) for s in range(1, chips)]

    sibling, states = exchange(ends, False)
    (li_inner,) = run(
        inner_body,
        columns,
        [tile(li_input), tile(li_spec), table("half2"), table("first3")],
        [(rows, F32)],
        3 * pass_flops,
    )
    li_out, mixed_li = run(
        functools.partial(long_body, chips - 1),
        columns,
        [("scalar", ahead_scalars), tile(li_inner), tile(query_li), tile(rate), tile(coef), tile(sibling)]
        + [tile(state) for state in states],
        [(rows, F32), (rows, BF16)],
        pass_flops,
    )

    mixed_parts = [mixed_li] + [chip_swap(mixed_li, s) for s in range(1, chips)]
    out_parts = []
    for s, part in enumerate(mixed_parts):
        found = lax.dot_general(
            part, weight_pair, (((1,), (1,)), ((), ())), preferred_element_type=F32
        ).astype(BF16)
        out_parts.append((chip ^ s, found if s == 0 else chip_swap(found, s)))
    out_full = placed(out_parts)
    line_width = out_full.shape[1] // line_count
    out_sum = columns_at(out_full, line, line_width).astype(F32)
    for r in range(1, line_count):
        out_sum = out_sum + line_swap(columns_at(out_full, line ^ r, line_width), r).astype(F32)
    output = out_sum

    grad_parts = []
    for s, part in enumerate(cot_parts):
        found = jnp.dot(part, weight_pair, preferred_element_type=F32)
        grad_parts.append(found if s == 0 else chip_swap(found.astype(BF16), s))
    grad_mixed, grad_li_out, back_ends = run(
        functools.partial(grad_gate_body, chips - 1),
        columns,
        [tile(grad_parts[0]), tile(query_li), tile(rate)] + [tile(part) for part in grad_parts[1:]],
        [(rows, F32), (rows, F32), (rate.shape[0], F32)],
        pass_flops,
    )
    back_sibling, back_states = exchange(back_ends, True)
    (grad_inner,) = run(
        grad_inner_body,
        columns,
        [tile(grad_li_out), tile(li_spec), table("half3"), table("first3")],
        [(rows, F32)],
        3 * pass_flops,
    )
    grad_query_li = grad_mixed * li_out
    grad_key_li, grad_query_mr, own_product, prev_product, tap_partial = run(
        functools.partial(grad_long_body, chips - 1),
        columns,
        [
            ("scalar", back_scalars),
            tile(grad_inner),
            tile(rate),
            tile(coef),
            tile(back_sibling),
            tile(mixed_mr),
            tile(key_li),
            tile(query_mr),
            tile(mr_conv),
            tile(spec),
            tile(mr_spec),
            table("half3"),
            table("both3"),
            table("lags3"),
        ]
        + [tile(state) for state in back_states],
        [(rows, F32), (rows, F32), (rows, F32), (rows, BF16), (rows, F32)],
        7 * pass_flops,
    )
    arrived = shifted(prev_product, -1)
    grad_key_mr, grad_value_mr = run(
        grad_product_body,
        columns,
        [tile(own_product), tile(arrived), tile(key_mr), tile(value_mr)],
        [(rows, F32), (rows, F32)],
        rows * columns,
    )

    tap_half = tap_partial.shape[0] // 2
    halves = tap_partial.reshape(2, tap_half, columns)
    own_half = lax.dynamic_index_in_dim(halves, core, 0, keepdims=False)
    far_half = lax.dynamic_index_in_dim(halves, 1 - core, 0, keepdims=False)
    chip_half = (own_half + core_swap(far_half)).astype(BF16)
    everywhere = [chip_half] + [chip_swap(chip_half, s) for s in range(1, chips)]
    plane_half = pair_sum([part.astype(F32) for part in everywhere]) * grad_scale
    other_half = core_swap(plane_half)
    grad_taps = jnp.where(
        core == 0,
        jnp.concatenate([plane_half, other_half], axis=0),
        jnp.concatenate([other_half, plane_half], axis=0),
    )

    cot_rows = jnp.concatenate(cot_parts, axis=0)
    mixed_rows = jnp.concatenate(mixed_parts, axis=0)

    def weight_share(which):
        return lax.dot_general(
            columns_at(cot_rows, which, width),
            mixed_rows,
            (((0,), (0,)), ((), ())),
            preferred_element_type=F32,
        )

    far_share = core_swap(weight_share(1 - core).astype(BF16))
    grad_weight = (weight_share(core) + far_share.astype(F32)) * grad_scale
    return (
        output,
        grad_query_mr,
        grad_key_mr,
        grad_value_mr,
        grad_query_li,
        grad_key_li,
        grad_taps,
        grad_weight,
    )


def solution(mesh):
    rows = P("ctx", "fsdp")
    channels = P(None, "fsdp")
    return jax.shard_map(
        shards,
        mesh=mesh,
        in_specs=(rows,) * 5 + (channels,) * 3 + (P("fsdp"),) + (rows,) * 2,
        out_specs=(rows,) * 6 + (channels, rows),
        check_vma=False,
    )
```

profile of v0, /device:TPU:0, one launch (start us, length us, event | category | flops | bytes accessed | tf_op | source)
XLA Modules:
  0.0 153.9 jit_solution(8273876842626522753)
XLA Ops:
  0.6 3.1 %collective-permute-start.15 = (bf16[128,1024]{1,0:T(8,128)(2,1)}, bf16[128,1024]{1,0:T(8,128)(2,1)S(1)}, u32[]{:S(2)}, u32[]{:S(2)}) collective-permute-start(bf16[128,1024]{1,0:T(8,128)(2,1)} %param.28), channel_id=1, source_target_pairs={{0,1},{1,0},{2,3},{3,2},{4,5},{5,4},{6,7},{7,6},{8,9},{9,8},{10,11... | collective-permute-start | bytes 786440 | tf_op jit(solution)/shard_map/ppermute | solution.py:254
  3.7 2.5 %collective-permute-start.17 = (bf16[128,1024]{1,0:T(8,128)(2,1)}, bf16[128,1024]{1,0:T(8,128)(2,1)S(1)}, u32[]{:S(2)}, u32[]{:S(2)}) collective-permute-start(bf16[128,1024]{1,0:T(8,128)(2,1)} %param.28), channel_id=1, source_target_pairs={{0,3},{1,2},{2,1},{3,0},{4,7},{5,6},{6,5},{7,4},{8,11},{9,10},{10,... | collective-permute-start | bytes 786440 | tf_op jit(solution)/shard_map/ppermute | solution.py:254
  8.7 2.3 %collective-permute-start.5 = (bf16[512,1024]{1,0:T(8,128)(2,1)}, bf16[512,1024]{1,0:T(8,128)(2,1)}, u32[]{:S(2)}, u32[]{:S(2)}) collective-permute-start(bf16[512,1024]{1,0:T(8,128)(2,1)} %param.27), channel_id=1, source_target_pairs={{0,4},{4,0},{8,12},{12,8},{16,20},{20,16},{24,28},{28,24},{1,5},{5... | collective-permute-start | bytes 3145736 | tf_op jit(solution)/shard_map/ppermute | solution.py:249
  12.2 17.3 %collective-permute-done.16 = bf16[128,1024]{1,0:T(8,128)(2,1)} collective-permute-done((bf16[128,1024]{1,0:T(8,128)(2,1)}, bf16[128,1024]{1,0:T(8,128)(2,1)}, u32[]{:S(2)}, u32[]{:S(2)}) %collective-permute-start.16) | collective-permute-done | bytes 262176 | tf_op jit(solution)/shard_map/ppermute | solution.py:254
  34.9 2.7 %maximum_select_fusion = bf16[1024,1024]{1,0:T(8,128)(2,1)S(1)} fusion(bf16[512,1024]{1,0:T(8,128)(2,1)} %collective-permute-done.5, bf16[512,1024]{1,0:T(8,128)(2,1)S(1)} %copy-done.18, pred[]{:T(512)S(6)} %eq.12), kind=kLoop, calls=%fused_computation | loop fusion | flops 9437184 | bytes 4194305 | tf_op jit(solution)/shard_map/jit(_where)/select_n | solution.py:317
  37.6 3.2 %collective-permute-done.18 = bf16[128,1024]{1,0:T(8,128)(2,1)S(1)} collective-permute-done((bf16[128,1024]{1,0:T(8,128)(2,1)}, bf16[128,1024]{1,0:T(8,128)(2,1)S(1)}, u32[]{:S(2)}, u32[]{:S(2)}) %collective-permute-start.18) | collective-permute-done | bytes 262176 | tf_op jit(solution)/shard_map/ppermute | solution.py:244
  42.8 5.0 %collective-permute-done.20 = bf16[128,1024]{1,0:T(8,128)(2,1)S(1)} collective-permute-done((bf16[128,1024]{1,0:T(8,128)(2,1)S(1)}, bf16[128,1024]{1,0:T(8,128)(2,1)S(1)}, u32[]{:S(2)}, u32[]{:S(2)}) %collective-permute-start.20) | collective-permute-done | bytes 262176 | tf_op jit(solution)/shard_map/ppermute | solution.py:244
  49.3 2.5 %collective-permute-start.23 = (bf16[128,1024]{1,0:T(8,128)(2,1)S(1)}, bf16[128,1024]{1,0:T(8,128)(2,1)S(1)}, u32[]{:S(2)}, u32[]{:S(2)}) collective-permute-start(bf16[128,1024]{1,0:T(8,128)(2,1)S(1)} %convolution_convert_fusion.1), channel_id=1, source_target_pairs={{0,24},{4,28},{8,16},{12,20},{16,8},{20,12},{24,0},{28,4},{1,25},{... | collective-permute-start | bytes 786440 | tf_op jit(solution)/shard_map/ppermute | solution.py:244
  52.3 6.5 %collective-permute-done.21.rest_1_ = bf16[128,1024]{1,0:T(8,128)(2,1)S(1)} collective-permute-done((bf16[128,1024]{1,0:T(8,128)(2,1)S(1)}, bf16[128,1024]{1,0:T(8,128)(2,1)S(1)}, u32[]{:S(2)}, u32[]{:S(2)}) %collective-permute-start.21) | collective-permute-done | bytes 262176 | tf_op jit(solution)/shard_map/ppermute | solution.py:244
  67.3 3.4 %shard_map.234 = (f32[256,1024]{1,0:T(8,128)S(1)}, f32[128,1024]{1,0:T(8,128)S(1)}, bf16[128,1024]{1,0:T(8,128)(2,1)S(1)}, bf16[128,1024]{1,0:T(8,128)(2,1)S(1)}, f32[16,1024]{1,0:T(8,128)S(1)}) custom-call(bf16[128,1024]{1,0:T(8,128)(2,1)S(1)} %collective-permute-done.before, bf16[128,1024]{1,0:T(8,128)(2,1)S(1)} %multiply_convert_fusion.product, ...), custom_call_target="tpu_custom_call" | custom-call | flops 536870912 | bytes 4784128 | tf_op jit(solution)/shard_map/pallas_call | solution.py:231
  70.7 2.3 %shard_map.238.inner = f32[128,1024]{1,0:T(8,128)S(1)} custom-call(f32[128,1024]{1,0:T(8,128)S(1)} %get-tuple-element.32.grad_out, f32[256,1024]{1,0:T(8,128)S(1)} %get-tuple-element.29.li_spec, bf16[256,384]{1,0:T(8,128)(2,1)S(1)} %copy-done.6, bf16[128,768]{1,0:T(8,128)(2,1)S(1)} %copy-done.5), custom_call_target="tpu_custom_call" | custom-call | flops 402653184 | bytes 2490368 | tf_op jit(solution)/shard_map/pallas_call | solution.py:231
  78.7 5.1 %shard_map.239 = (f32[128,1024]{1,0:T(8,128)}, f32[128,1024]{1,0:T(8,128)}, f32[128,1024]{1,0:T(8,128)S(1)}, bf16[128,1024]{1,0:T(8,128)(2,1)S(1)}, f32[128,1024]{1,0:T(8,128)S(1)}) custom-call(f32[4]{0:T(128)S(1)} %pad_maximum_fusion.2.scalars, f32[128,1024]{1,0:T(8,128)S(1)} %shard_map.238.inner, f32[16,1024]{1,0:T(8,128)S(1)} %broadcast_divide_fusion.rate, ...), custom_call_target="tpu_custom_call" | custom-call | flops 939524096 | bytes 7471120 | tf_op jit(solution)/shard_map/pallas_call | solution.py:231
  87.1 2.7 %collective-permute-start.10 = (bf16[128,1024]{1,0:T(8,128)(2,1)S(1)}, bf16[128,1024]{1,0:T(8,128)(2,1)S(1)}, u32[]{:S(2)}, u32[]{:S(2)}) collective-permute-start(bf16[128,1024]{1,0:T(8,128)(2,1)S(1)} %get-tuple-element.31), channel_id=1, source_target_pairs={{0,24},{4,28},{8,16},{12,20},{16,8},{20,12},{24,0},{28,4},{1,25},{... | collective-permute-start | bytes 786440 | tf_op jit(solution)/shard_map/ppermute | solution.py:244
  94.9 3.4 %collective-permute-done.10 = bf16[128,1024]{1,0:T(8,128)(2,1)S(1)} collective-permute-done((bf16[128,1024]{1,0:T(8,128)(2,1)S(1)}, bf16[128,1024]{1,0:T(8,128)(2,1)S(1)}, u32[]{:S(2)}, u32[]{:S(2)}) %collective-permute-start.10) | collective-permute-done | bytes 262176 | tf_op jit(solution)/shard_map/ppermute | solution.py:244
  98.3 2.7 %collective-permute-start.31 = (bf16[64,1024]{1,0:T(8,128)(2,1)S(1)}, bf16[64,1024]{1,0:T(8,128)(2,1)S(1)}, u32[]{:S(2)}, u32[]{:S(2)}) collective-permute-start(bf16[64,1024]{1,0:T(8,128)(2,1)S(1)} %fusion.3), channel_id=1, source_target_pairs={{0,16},{4,20},{8,24},{12,28},{16,0},{20,4},{24,8},{28,12},{1,17},{... | collective-permute-start | bytes 393224 | tf_op jit(solution)/shard_map/ppermute | solution.py:244
  101.9 3.3 %collective-permute-done.6 = bf16[128,1024]{1,0:T(8,128)(2,1)S(1)} collective-permute-done((bf16[128,1024]{1,0:T(8,128)(2,1)S(1)}, bf16[128,1024]{1,0:T(8,128)(2,1)S(1)}, u32[]{:S(2)}, u32[]{:S(2)}) %collective-permute-start.6) | collective-permute-done | bytes 262176 | tf_op jit(solution)/shard_map/ppermute | solution.py:244
  110.8 2.1 %collective-permute-start.11 = (bf16[128,1024]{1,0:T(8,128)(2,1)S(1)}, bf16[128,1024]{1,0:T(8,128)(2,1)S(1)}, u32[]{:S(2)}, u32[]{:S(2)}) collective-permute-start(bf16[128,1024]{1,0:T(8,128)(2,1)S(1)} %convolution_convert_fusion.4), channel_id=1, source_target_pairs={{0,24},{4,28},{8,16},{12,20},{16,8},{20,12},{24,0},{28,4},{1,25},{... | collective-permute-start | bytes 786440 | tf_op jit(solution)/shard_map/ppermute | solution.py:244
  113.8 3.3 %collective-permute-done.7 = bf16[128,1024]{1,0:T(8,128)(2,1)S(1)} collective-permute-done((bf16[128,1024]{1,0:T(8,128)(2,1)S(1)}, bf16[128,1024]{1,0:T(8,128)(2,1)S(1)}, u32[]{:S(2)}, u32[]{:S(2)}) %collective-permute-start.7) | collective-permute-done | bytes 262176 | tf_op jit(solution)/shard_map/ppermute | solution.py:244
  117.2 6.3 %collective-permute-done.9 = bf16[128,1024]{1,0:T(8,128)(2,1)S(1)} collective-permute-done((bf16[128,1024]{1,0:T(8,128)(2,1)S(1)}, bf16[128,1024]{1,0:T(8,128)(2,1)S(1)}, u32[]{:S(2)}, u32[]{:S(2)}) %collective-permute-start.9) | collective-permute-done | bytes 262176 | tf_op jit(solution)/shard_map/ppermute | solution.py:244
  124.5 2.1 %collective-permute-start.14 = (bf16[128,1024]{1,0:T(8,128)(2,1)}, bf16[128,1024]{1,0:T(8,128)(2,1)}, u32[]{:S(2)}, u32[]{:S(2)}) collective-permute-start(bf16[128,1024]{1,0:T(8,128)(2,1)} %get-tuple-element.53), channel_id=1, source_target_pairs={{0,3},{1,2},{2,1},{3,0},{4,7},{5,6},{6,5},{7,4},{8,11},{9,10},{10,... | collective-permute-start | bytes 786440 | tf_op jit(solution)/shard_map/ppermute | solution.py:254
  132.6 2.7 %collective-permute-done.12 = bf16[128,1024]{1,0:T(8,128)(2,1)} collective-permute-done((bf16[128,1024]{1,0:T(8,128)(2,1)}, bf16[128,1024]{1,0:T(8,128)(2,1)}, u32[]{:S(2)}, u32[]{:S(2)}) %collective-permute-start.12) | collective-permute-done | bytes 262176 | tf_op jit(solution)/shard_map/ppermute | solution.py:254
  135.3 4.0 %collective-permute-done.14 = bf16[128,1024]{1,0:T(8,128)(2,1)} collective-permute-done((bf16[128,1024]{1,0:T(8,128)(2,1)}, bf16[128,1024]{1,0:T(8,128)(2,1)}, u32[]{:S(2)}, u32[]{:S(2)}) %collective-permute-start.14) | collective-permute-done | bytes 262176 | tf_op jit(solution)/shard_map/ppermute | solution.py:254
  139.3 9.2 %collective-permute-done.13 = bf16[128,1024]{1,0:T(8,128)(2,1)} collective-permute-done((bf16[128,1024]{1,0:T(8,128)(2,1)}, bf16[128,1024]{1,0:T(8,128)(2,1)}, u32[]{:S(2)}, u32[]{:S(2)}) %collective-permute-start.13) | collective-permute-done | bytes 262176 | tf_op jit(solution)/shard_map/ppermute | solution.py:254
  150.6 3.3 %add_multiply_fusion = f32[512,1024]{1,0:T(8,128)} fusion(bf16[512,1024]{1,0:T(8,128)(2,1)} %collective-permute-done.34, bf16[512,1024]{1,0:T(8,128)(2,1)S(1)} %copy-done.17, bf16[512,1024]{1,0:T(8,128)(2,1)S(1)} %copy-done.15, s32[]{:T(128)S(6)} %select_n.103), kind=kOutput, calls=%fused_computation.1 | convolution fusion | flops 538443776 | bytes 4718596 | tf_op jit(solution)/shard_map/dot_general | solution.py:467
  (139 shorter events, 51.5 us)
Async XLA Ops:
  0.6 11.6 %collective-permute-start.15 = (bf16[128,1024]{1,0:T(8,128)(2,1)}, bf16[128,1024]{1,0:T(8,128)(2,1)S(1)}, u32[]{:S(2)}, u32[]{:S(2)}) collective-permute-start(bf16[128,1024]{1,0:T(8,128)(2,1)} %param.28), channel_id=1, source_target_pairs={{0,1},{1,0},{2,3},{3,2},{4,5},{5,4},{6,7},{7,6},{8,9},{9,8},{10,11... | collective-permute-start | bytes 786440 | tf_op jit(solution)/shard_map/ppermute | solution.py:254
  3.7 26.8 %collective-permute-start.17 = (bf16[128,1024]{1,0:T(8,128)(2,1)}, bf16[128,1024]{1,0:T(8,128)(2,1)S(1)}, u32[]{:S(2)}, u32[]{:S(2)}) collective-permute-start(bf16[128,1024]{1,0:T(8,128)(2,1)} %param.28), channel_id=1, source_target_pairs={{0,3},{1,2},{2,1},{3,0},{4,7},{5,6},{6,5},{7,4},{8,11},{9,10},{10,... | collective-permute-start | bytes 786440 | tf_op jit(solution)/shard_map/ppermute | solution.py:254
  6.2 23.3 %collective-permute-start.16 = (bf16[128,1024]{1,0:T(8,128)(2,1)}, bf16[128,1024]{1,0:T(8,128)(2,1)}, u32[]{:S(2)}, u32[]{:S(2)}) collective-permute-start(bf16[128,1024]{1,0:T(8,128)(2,1)} %param.28), channel_id=1, source_target_pairs={{0,2},{1,3},{2,0},{3,1},{4,6},{5,7},{6,4},{7,5},{8,10},{9,11},{10,... | collective-permute-start | bytes 786440 | tf_op jit(solution)/shard_map/ppermute | solution.py:254
  7.4 59.8 %collective-permute-start = (bf16[128,1024]{1,0:T(8,128)(2,1)S(1)}, bf16[128,1024]{1,0:T(8,128)(2,1)S(1)}, u32[]{:S(2)}, u32[]{:S(2)}) collective-permute-start(bf16[128,1024]{1,0:T(8,128)(2,1)S(1)} %multiply_convert_fusion.product), channel_id=1, source_target_pairs={{0,4},{4,8},{8,12},{12,16},{16,20},{20,24},{24,28},{1,5},{5,9},{9,... | collective-permute-start | bytes 786440 | tf_op jit(solution)/shard_map/ppermute | solution.py:259
  8.7 26.2 %collective-permute-start.5 = (bf16[512,1024]{1,0:T(8,128)(2,1)}, bf16[512,1024]{1,0:T(8,128)(2,1)}, u32[]{:S(2)}, u32[]{:S(2)}) collective-permute-start(bf16[512,1024]{1,0:T(8,128)(2,1)} %param.27), channel_id=1, source_target_pairs={{0,4},{4,0},{8,12},{12,8},{16,20},{20,16},{24,28},{28,24},{1,5},{5... | collective-permute-start | bytes 3145736 | tf_op jit(solution)/shard_map/ppermute | solution.py:249
  32.9 15.9 %collective-permute-start.22 = (bf16[128,1024]{1,0:T(8,128)(2,1)S(1)}, bf16[128,1024]{1,0:T(8,128)(2,1)S(1)}, u32[]{:S(2)}, u32[]{:S(2)}) collective-permute-start(bf16[128,1024]{1,0:T(8,128)(2,1)S(1)} %get-tuple-element.48), channel_id=1, source_target_pairs={{0,24},{4,28},{8,16},{12,20},{16,8},{20,12},{24,0},{28,4},{1,25},{... | collective-permute-start | bytes 786440 | tf_op jit(solution)/shard_map/ppermute | solution.py:244
  34.4 13.4 %collective-permute-start.20 = (bf16[128,1024]{1,0:T(8,128)(2,1)S(1)}, bf16[128,1024]{1,0:T(8,128)(2,1)S(1)}, u32[]{:S(2)}, u32[]{:S(2)}) collective-permute-start(bf16[128,1024]{1,0:T(8,128)(2,1)S(1)} %get-tuple-element.49), channel_id=1, source_target_pairs={{0,16},{4,20},{8,24},{12,28},{16,0},{20,4},{24,8},{28,12},{1,17},{... | collective-permute-start | bytes 786440 | tf_op jit(solution)/shard_map/ppermute | solution.py:244
  41.3 11.1 %collective-permute-start.19 = (bf16[128,1024]{1,0:T(8,128)(2,1)S(1)}, bf16[128,1024]{1,0:T(8,128)(2,1)S(1)}, u32[]{:S(2)}, u32[]{:S(2)}) collective-permute-start(bf16[128,1024]{1,0:T(8,128)(2,1)S(1)} %convolution_convert_fusion.3), channel_id=1, source_target_pairs={{0,8},{4,12},{8,0},{12,4},{16,24},{20,28},{24,16},{28,20},{1,9},{5... | collective-permute-start | bytes 786440 | tf_op jit(solution)/shard_map/ppermute | solution.py:244
  61.6 16.6 %collective-permute-start.27 = (f32[16,1024]{1,0:T(8,128)S(1)}, f32[16,1024]{1,0:T(8,128)S(1)}, u32[]{:S(2)}, u32[]{:S(2)}) collective-permute-start(f32[16,1024]{1,0:T(8,128)S(1)} %get-tuple-element.55), channel_id=1, source_target_pairs={{0,24},{4,28},{8,16},{12,20},{16,8},{20,12},{24,0},{28,4},{1,25},{... | collective-permute-start | bytes 196616 | tf_op jit(solution)/shard_map/ppermute | solution.py:244
  63.1 15.6 %collective-permute-start.26 = (f32[16,1024]{1,0:T(8,128)S(1)}, f32[16,1024]{1,0:T(8,128)S(1)}, u32[]{:S(2)}, u32[]{:S(2)}) collective-permute-start(f32[16,1024]{1,0:T(8,128)S(1)} %get-tuple-element.55), channel_id=1, source_target_pairs={{0,16},{4,20},{8,24},{12,28},{16,0},{20,4},{24,8},{28,12},{1,17},{... | collective-permute-start | bytes 196616 | tf_op jit(solution)/shard_map/ppermute | solution.py:244
  64.6 14.1 %collective-permute-start.25 = (f32[16,1024]{1,0:T(8,128)S(1)}, f32[16,1024]{1,0:T(8,128)S(1)}, u32[]{:S(2)}, u32[]{:S(2)}) collective-permute-start(f32[16,1024]{1,0:T(8,128)S(1)} %get-tuple-element.55), channel_id=1, source_target_pairs={{0,8},{4,12},{8,0},{12,4},{16,24},{20,28},{24,16},{28,20},{1,9},{5... | collective-permute-start | bytes 196616 | tf_op jit(solution)/shard_map/ppermute | solution.py:244
  84.0 42.6 %collective-permute-start.28 = (bf16[128,1024]{1,0:T(8,128)(2,1)S(1)}, bf16[128,1024]{1,0:T(8,128)(2,1)S(1)}, u32[]{:S(2)}, u32[]{:S(2)}) collective-permute-start(bf16[128,1024]{1,0:T(8,128)(2,1)S(1)} %get-tuple-element.39), channel_id=1, source_target_pairs={{4,0},{8,4},{12,8},{16,12},{20,16},{24,20},{28,24},{5,1},{9,5},{13... | collective-permute-start | bytes 786440 | tf_op jit(solution)/shard_map/ppermute | solution.py:259
  87.1 11.2 %collective-permute-start.10 = (bf16[128,1024]{1,0:T(8,128)(2,1)S(1)}, bf16[128,1024]{1,0:T(8,128)(2,1)S(1)}, u32[]{:S(2)}, u32[]{:S(2)}) collective-permute-start(bf16[128,1024]{1,0:T(8,128)(2,1)S(1)} %get-tuple-element.31), channel_id=1, source_target_pairs={{0,24},{4,28},{8,16},{12,20},{16,8},{20,12},{24,0},{28,4},{1,25},{... | collective-permute-start | bytes 786440 | tf_op jit(solution)/shard_map/ppermute | solution.py:244
  89.9 16.2 %collective-permute-start.8 = (bf16[128,1024]{1,0:T(8,128)(2,1)S(1)}, bf16[128,1024]{1,0:T(8,128)(2,1)S(1)}, u32[]{:S(2)}, u32[]{:S(2)}) collective-permute-start(bf16[128,1024]{1,0:T(8,128)(2,1)S(1)} %get-tuple-element.31), channel_id=1, source_target_pairs={{0,16},{4,20},{8,24},{12,28},{16,0},{20,4},{24,8},{28,12},{1,17},{... | collective-permute-start | bytes 786440 | tf_op jit(solution)/shard_map/ppermute | solution.py:244
  91.4 13.8 %collective-permute-start.6 = (bf16[128,1024]{1,0:T(8,128)(2,1)S(1)}, bf16[128,1024]{1,0:T(8,128)(2,1)S(1)}, u32[]{:S(2)}, u32[]{:S(2)}) collective-permute-start(bf16[128,1024]{1,0:T(8,128)(2,1)S(1)} %get-tuple-element.31), channel_id=1, source_target_pairs={{0,8},{4,12},{8,0},{12,4},{16,24},{20,28},{24,16},{28,20},{1,9},{5... | collective-permute-start | bytes 786440 | tf_op jit(solution)/shard_map/ppermute | solution.py:244
  93.3 17.5 %collective-permute-start.32 = (bf16[64,1024]{1,0:T(8,128)(2,1)S(1)}, bf16[64,1024]{1,0:T(8,128)(2,1)S(1)}, u32[]{:S(2)}, u32[]{:S(2)}) collective-permute-start(bf16[64,1024]{1,0:T(8,128)(2,1)S(1)} %fusion.3), channel_id=1, source_target_pairs={{0,24},{4,28},{8,16},{12,20},{16,8},{20,12},{24,0},{28,4},{1,25},{... | collective-permute-start | bytes 393224 | tf_op jit(solution)/shard_map/ppermute | solution.py:244
  98.3 14.6 %collective-permute-start.31 = (bf16[64,1024]{1,0:T(8,128)(2,1)S(1)}, bf16[64,1024]{1,0:T(8,128)(2,1)S(1)}, u32[]{:S(2)}, u32[]{:S(2)}) collective-permute-start(bf16[64,1024]{1,0:T(8,128)(2,1)S(1)} %fusion.3), channel_id=1, source_target_pairs={{0,16},{4,20},{8,24},{12,28},{16,0},{20,4},{24,8},{28,12},{1,17},{... | collective-permute-start | bytes 393224 | tf_op jit(solution)/shard_map/ppermute | solution.py:244
  106.0 11.1 %collective-permute-start.7 = (bf16[128,1024]{1,0:T(8,128)(2,1)S(1)}, bf16[128,1024]{1,0:T(8,128)(2,1)S(1)}, u32[]{:S(2)}, u32[]{:S(2)}) collective-permute-start(bf16[128,1024]{1,0:T(8,128)(2,1)S(1)} %convolution_convert_fusion.6), channel_id=1, source_target_pairs={{0,8},{4,12},{8,0},{12,4},{16,24},{20,28},{24,16},{28,20},{1,9},{5... | collective-permute-start | bytes 786440 | tf_op jit(solution)/shard_map/ppermute | solution.py:244
  110.8 12.7 %collective-permute-start.11 = (bf16[128,1024]{1,0:T(8,128)(2,1)S(1)}, bf16[128,1024]{1,0:T(8,128)(2,1)S(1)}, u32[]{:S(2)}, u32[]{:S(2)}) collective-permute-start(bf16[128,1024]{1,0:T(8,128)(2,1)S(1)} %convolution_convert_fusion.4), channel_id=1, source_target_pairs={{0,24},{4,28},{8,16},{12,20},{16,8},{20,12},{24,0},{28,4},{1,25},{... | collective-permute-start | bytes 786440 | tf_op jit(solution)/shard_map/ppermute | solution.py:244
  113.0 37.6 %collective-permute-start.34 = (bf16[512,1024]{1,0:T(8,128)(2,1)}, bf16[512,1024]{1,0:T(8,128)(2,1)}, u32[]{:S(2)}, u32[]{:S(2)}) collective-permute-start(bf16[512,1024]{1,0:T(8,128)(2,1)} %convolution_convert_fusion), channel_id=1, source_target_pairs={{0,4},{4,0},{8,12},{12,8},{16,20},{20,16},{24,28},{28,24},{1,5},{5... | collective-permute-start | bytes 3145736 | tf_op jit(solution)/shard_map/ppermute | solution.py:249
  117.1 13.4 %collective-permute-start.33 = (f32[64,1024]{1,0:T(8,128)}, f32[64,1024]{1,0:T(8,128)}, u32[]{:S(2)}, u32[]{:S(2)}) collective-permute-start(f32[64,1024]{1,0:T(8,128)} %add_multiply_fusion.1), channel_id=1, source_target_pairs={{0,4},{4,0},{8,12},{12,8},{16,20},{20,16},{24,28},{28,24},{1,5},{5... | collective-permute-start | bytes 786440 | tf_op jit(solution)/shard_map/ppermute | solution.py:249
  124.5 10.8 %collective-permute-start.12 = (bf16[128,1024]{1,0:T(8,128)(2,1)}, bf16[128,1024]{1,0:T(8,128)(2,1)}, u32[]{:S(2)}, u32[]{:S(2)}) collective-permute-start(bf16[128,1024]{1,0:T(8,128)(2,1)} %get-tuple-element.52), channel_id=1, source_target_pairs={{0,1},{1,0},{2,3},{3,2},{4,5},{5,4},{6,7},{7,6},{8,9},{9,8},{10,11... | collective-permute-start | bytes 786440 | tf_op jit(solution)/shard_map/ppermute | solution.py:254
  124.5 14.8 %collective-permute-start.14 = (bf16[128,1024]{1,0:T(8,128)(2,1)}, bf16[128,1024]{1,0:T(8,128)(2,1)}, u32[]{:S(2)}, u32[]{:S(2)}) collective-permute-start(bf16[128,1024]{1,0:T(8,128)(2,1)} %get-tuple-element.53), channel_id=1, source_target_pairs={{0,3},{1,2},{2,1},{3,0},{4,7},{5,6},{6,5},{7,4},{8,11},{9,10},{10,... | collective-permute-start | bytes 786440 | tf_op jit(solution)/shard_map/ppermute | solution.py:254
  126.6 21.9 %collective-permute-start.13 = (bf16[128,1024]{1,0:T(8,128)(2,1)}, bf16[128,1024]{1,0:T(8,128)(2,1)}, u32[]{:S(2)}, u32[]{:S(2)}) collective-permute-start(bf16[128,1024]{1,0:T(8,128)(2,1)} %get-tuple-element.54), channel_id=1, source_target_pairs={{0,2},{1,3},{2,0},{3,1},{4,6},{5,7},{6,4},{7,5},{8,10},{9,11},{10,... | collective-permute-start | bytes 786440 | tf_op jit(solution)/shard_map/ppermute | solution.py:254
  (33 other events, 373.2 us)
where the time goes:
time: 154 us
  waiting for transfers between devices  65.5 us (43%)
  starting transfers between devices  43.4 us (28%)
  Pallas kernels  19.5 us (13%)
  other arithmetic  10.9 us (7%)
  matrix products  10.1 us (7%)
  local copies, waits for them, and re-layouts  3.24 us (2%)
    ppermute x6, waiting for transfers between devices, line_swap(): return lax.ppermute(x, 'fsdp', [(i, i ^ by) for i in range(size)])  33.2 us
    ppermute x21, waiting for transfers between devices, chip_swap(): return lax.ppermute(x, 'ctx', [(i, i ^ 2 * by) for i in range(size)])  31 us
    ppermute x21, starting transfers between devices, chip_swap(): return lax.ppermute(x, 'ctx', [(i, i ^ 2 * by) for i in range(size)])  28.9 us
    pallas_call x8, Pallas kernels, run(): pl.pallas_call(body, grid=(columns // tile,), in_specs=in_specs, out_spec...  19.5 us
    ppermute x6, starting transfers between devices, line_swap(): return lax.ppermute(x, 'fsdp', [(i, i ^ by) for i in range(size)])  9.17 us
    dot_general x2, matrix products, weight_share(): lax.dot_general(columns_at(cot_rows, which, width), mixed_rows, (((0,), (...  5.02 us
    dot_general x4, matrix products, shards(): lax.dot_general(part, weight_pair, (((1,), (1,)), ((), ())), preferred_el...  3.32 us
  transfers between devices with their start and end apart: 35, of which 12 were waited for; matrix products, arithmetic and copies ran while one was open for 14% of the time, Pallas kernels for 13%

commit v1 on v0

--- a/solution.py
+++ b/solution.py
@@ -115,14 +115,6 @@
     return jnp.concatenate(found, axis=0)
 
 
-def gather_states(rate, gaps, states, sibling, inner, rows):
-    total = jnp.zeros_like(rate)
-    for gap, state in zip(gaps, states):
-        weight = jnp.exp(-rate * (jnp.maximum(gap, 0.0) * (2.0 * rows)))
-        total = total + jnp.where(gap >= 0.0, weight * state, 0.0)
-    return jnp.where(inner > 0.0, jnp.exp(-rate * float(rows)) * total + sibling, total)
-
-
 def spectra_body(taps, rate, coef, skip, half3, mr_spec, li_spec):
     rows = taps.shape[0]
     mr_spec[...] = apply3(half3[...], taps[...])
@@ -149,28 +141,18 @@
     inner[...] = apply3(first3[...], times(apply2(half2[...], signal[...]), li_spec[...]))
 
 
-def long_body(count, scalars, inner, query, rate, coef, sibling, *rest):
-    states, (li_out, mixed) = rest[:count], rest[count:]
+def long_body(inner, query, rate, coef, entering, li_out, mixed):
     rows = inner.shape[0]
-    rates = rate[...]
-    entering = gather_states(
-        rates,
-        [scalars[1 + k] for k in range(count)],
-        [state[...] for state in states],
-        sibling[...],
-        scalars[0],
-        rows,
-    )
-    total = inner[...] + spread_modes(rates, coef[...] * entering, rows, 1.0, False)
+    total = inner[...] + spread_modes(rate[...], coef[...] * entering[...], rows, 1.0, False)
     li_out[...] = total
     mixed[...] = (query[...].astype(F32) * total).astype(BF16)
 
 
-def grad_gate_body(count, own, query, rate, *rest):
-    parts, (grad_mixed, grad_out, ends) = rest[:count], rest[count:]
-    total = own[...]
-    for part in parts:
-        total = total + part[...].astype(F32)
+def grad_gate_body(parts, query, rate, grad_mixed, grad_out, ends):
+    rows = query.shape[0]
+    total = parts[:rows].astype(F32)
+    for k in range(1, parts.shape[0] // rows):
+        total = total + parts[k * rows : (k + 1) * rows].astype(F32)
     grad_mixed[...] = total
     gated = total * query[...].astype(F32)
     grad_out[...] = gated
@@ -182,21 +164,11 @@
 
 
 def grad_long_body(
-    count, scalars, inner, rate, coef, sibling, mixed_mr, key_li, query_mr, conv, spec, mr_spec, half3, both3, lags3, *rest
+    inner, rate, coef, entering, mixed_mr, key_li, query_mr, conv, spec, mr_spec, half3, both3, lags3,
+    grad_key_li, grad_query_mr, own_product, prev_product, taps,
 ):
-    states = rest[:count]
-    grad_key_li, grad_query_mr, own_product, prev_product, taps = rest[count:]
     rows = inner.shape[0]
-    rates = rate[...]
-    entering = gather_states(
-        rates,
-        [scalars[1 + k] for k in range(count)],
-        [state[...] for state in states],
-        sibling[...],
-        scalars[0],
-        rows,
-    )
-    grad_input = inner[...] + spread_modes(rates, coef[...] * entering, rows, 1.0, True)
+    grad_input = inner[...] + spread_modes(rate[...], coef[...] * entering[...], rows, 1.0, True)
     grad_key_li[...] = grad_input * mixed_mr[...].astype(F32)
     grad_mixed_mr = grad_input * key_li[...].astype(F32)
     grad_query_mr[...] = grad_mixed_mr * conv[...]
@@ -221,10 +193,8 @@
     for kind, array in inputs:
         if kind == "tile":
             in_specs.append(pl.BlockSpec((array.shape[0], tile), lambda c: (0, c)))
-        elif kind == "whole":
+        else:
             in_specs.append(pl.BlockSpec(array.shape, lambda c: (0, 0)))
-        else:
-            in_specs.append(pl.BlockSpec(memory_space=pltpu.SMEM))
         moved += math.prod(array.shape) * array.dtype.itemsize
     for rows, dtype in outputs:
         moved += rows * columns * jnp.dtype(dtype).itemsize
@@ -239,42 +209,59 @@
     )(*[array for _, array in inputs])
 
 
-def chip_swap(x, by):
-    size = lax.axis_size("ctx")
-    return lax.ppermute(x, "ctx", [(i, i ^ (2 * by)) for i in range(size)])
-
-
 def core_swap(x):
     size = lax.axis_size("ctx")
     return lax.ppermute(x, "ctx", [(i, i ^ 1) for i in range(size)])
 
 
-def line_swap(x, by):
-    size = lax.axis_size("fsdp")
-    return lax.ppermute(x, "fsdp", [(i, i ^ by) for i in range(size)])
-
-
 def shifted(x, by):
     size = lax.axis_size("ctx")
     return lax.ppermute(x, "ctx", [(i, i + by) for i in range(size) if 0 <= i + by < size])
 
 
-def columns_at(x, index, width):
-    return lax.dynamic_slice_in_dim(x, index * width, width, 1)
-
-
-def placed(pieces):
-    width = pieces[0][1].shape[1]
-    whole = jnp.zeros((pieces[0][1].shape[0], width * len(pieces)), pieces[0][1].dtype)
-    for index, piece in pieces:
-        whole = lax.dynamic_update_slice_in_dim(whole, piece, index * width, 1)
-    return whole
-
-
-def pair_sum(values):
-    while len(values) > 1:
-        values = [values[k] + values[k + 1] for k in range(0, len(values), 2)]
-    return values[0]
+def plane_trade(x):
+    size = lax.axis_size("ctx")
+    groups = [list(range(core, size, 2)) for core in range(2)]
+    return lax.all_to_all(x, "ctx", 0, 0, axis_index_groups=groups, tiled=True)
+
+
+def line_trade(x):
+    return lax.all_to_all(x, "fsdp", 0, 0, tiled=True)
+
+
+def copies(x, count):
+    return jnp.concatenate([x] * count, axis=0)
+
+
+def rows_to_columns(x, count):
+    return jnp.concatenate(jnp.split(x, count, axis=0), axis=1)
+
+
+def columns_to_rows(x, count):
+    return jnp.concatenate(jnp.split(x, count, axis=1), axis=0)
+
+
+def after(x, *others):
+    return lax.optimization_barrier((x,) + others)[0]
+
+
+def entering_state(ends, rate, rows, here, backward):
+    size = lax.axis_size("ctx")
+    total, entering = ends, jnp.zeros_like(ends)
+    by = 1
+    while by < size:
+        arrived = lax.ppermute(total, "ctx", [(i, i ^ by) for i in range(size)])
+        later = (here & by) != 0
+        offset = here & (by - 1)
+        if backward:
+            later = jnp.logical_not(later)
+            offset = by - 1 - offset
+        to_here = jnp.exp(-rate * (rows * offset).astype(F32))
+        entering = entering + jnp.where(later, to_here * arrived, 0.0)
+        across = jnp.exp(-rate * float(rows * by))
+        total = jnp.where(later, across * arrived + total, across * total + arrived)
+        by *= 2
+    return entering
 
 
 def shards(
@@ -295,12 +282,10 @@
     line_count = lax.axis_size("fsdp")
     chips = ctx_count // 2
     here = lax.axis_index("ctx")
-    chip, core = here // 2, here % 2
-    line = lax.axis_index("fsdp")
+    core = here % 2
     grad_scale = 1.0 / math.sqrt(rows * ctx_count)
     tables = {name: jnp.asarray(table) for name, table in dft_tables(rows).items()}
     width = out_weight.shape[0]
-    chip_width = 2 * width
     pass_flops = 2 * (2 * rows) * (2 * rows) * columns
 
     def tile(x):
@@ -312,27 +297,10 @@
     mr_product = (key_mr.astype(F32) * value_mr.astype(F32)).astype(BF16)
     before = shifted(mr_product, 1)
 
-    cot_line = [cotangent] + [line_swap(cotangent, r) for r in range(1, line_count)]
-    other_weight = core_swap(out_weight)
-    weight_pair = jnp.where(
-        core == 0,
-        jnp.concatenate([out_weight, other_weight], axis=0),
-        jnp.concatenate([other_weight, out_weight], axis=0),
-    )
-    cot_full = placed([(line ^ r, piece) for r, piece in enumerate(cot_line)])
-    cot_parts = [columns_at(cot_full, chip, chip_width)]
-    for s in range(1, chips):
-        cot_parts.append(chip_swap(columns_at(cot_full, chip ^ s, chip_width), s))
+    cot_line = line_trade(copies(cotangent, line_count))
 
     rate = 1.0 / li_time
     coef = li_residue * jnp.sqrt(-jnp.expm1(-2.0 * rate))
-    block_decay = jnp.exp(-rate * float(rows))
-    inner_ahead = (core == 1).astype(F32)[None]
-    peers = jnp.stack([chip ^ s for s in range(1, chips)]).astype(F32)
-    chip_f = chip.astype(F32)
-    ahead_scalars = jnp.concatenate([inner_ahead, chip_f - 1.0 - peers])
-    back_scalars = jnp.concatenate([1.0 - inner_ahead, peers - chip_f - 1.0])
-
     mr_spec, li_spec = run(
         spectra_body,
         columns,
@@ -340,6 +308,7 @@
         [(2 * rows, F32), (2 * rows, F32)],
         3 * pass_flops,
     )
+    other_weight = core_swap(after(out_weight, mr_spec))
     spec, mr_conv, mixed_mr, li_input, ends = run(
         short_body,
         columns,
@@ -356,14 +325,7 @@
         [(2 * rows, F32), (rows, F32), (rows, BF16), (rows, BF16), (rate.shape[0], F32)],
         4 * pass_flops,
     )
-
-    def exchange(ends, backward):
-        sibling = core_swap(ends)
-        near, far = (sibling, ends) if backward else (ends, sibling)
-        chip_state = jnp.where(core == 0, block_decay * near + far, block_decay * far + near)
-        return sibling, [chip_swap(chip_state, s) for s in range(1, chips)]
-
-    sibling, states = exchange(ends, False)
+    entering = entering_state(ends, rate, rows, here, False)
     (li_inner,) = run(
         inner_body,
         columns,
@@ -372,40 +334,54 @@
         3 * pass_flops,
     )
     li_out, mixed_li = run(
-        functools.partial(long_body, chips - 1),
-        columns,
-        [("scalar", ahead_scalars), tile(li_inner), tile(query_li), tile(rate), tile(coef), tile(sibling)]
-        + [tile(state) for state in states],
+        long_body,
+        columns,
+        [tile(li_inner), tile(query_li), tile(rate), tile(coef), tile(entering)],
         [(rows, F32), (rows, BF16)],
         pass_flops,
     )
 
-    mixed_parts = [mixed_li] + [chip_swap(mixed_li, s) for s in range(1, chips)]
-    out_parts = []
-    for s, part in enumerate(mixed_parts):
-        found = lax.dot_general(
-            part, weight_pair, (((1,), (1,)), ((), ())), preferred_element_type=F32
-        ).astype(BF16)
-        out_parts.append((chip ^ s, found if s == 0 else chip_swap(found, s)))
-    out_full = placed(out_parts)
-    line_width = out_full.shape[1] // line_count
-    out_sum = columns_at(out_full, line, line_width).astype(F32)
-    for r in range(1, line_count):
-        out_sum = out_sum + line_swap(columns_at(out_full, line ^ r, line_width), r).astype(F32)
-    output = out_sum
-
-    grad_parts = []
-    for s, part in enumerate(cot_parts):
-        found = jnp.dot(part, weight_pair, preferred_element_type=F32)
-        grad_parts.append(found if s == 0 else chip_swap(found.astype(BF16), s))
+    mixed_rows = plane_trade(copies(mixed_li, chips))
+    cot_full = rows_to_columns(after(cot_line, mixed_li), line_count)
+    cot_rows = plane_trade(columns_to_rows(cot_full, chips))
+    weight_pair = jnp.where(
+        core == 0,
+        jnp.concatenate([out_weight, other_weight], axis=0),
+        jnp.concatenate([other_weight, out_weight], axis=0),
+    )
+
+    grad_share = jnp.dot(cot_rows, weight_pair, preferred_element_type=F32).astype(BF16)
+    grad_parts = plane_trade(grad_share)
+
+    out_share = lax.dot_general(
+        mixed_rows, after(weight_pair, grad_share), (((1,), (1,)), ((), ())), preferred_element_type=F32
+    ).astype(BF16)
+    out_full = rows_to_columns(plane_trade(out_share), chips)
+    out_parts = line_trade(columns_to_rows(out_full, line_count)).reshape(line_count, rows, -1)
+    output = jnp.sum(out_parts.astype(F32), axis=0)
+
+    mixed_after = after(mixed_rows, out_share)
+
+    def weight_share(which):
+        return lax.dot_general(
+            lax.dynamic_slice_in_dim(cot_rows, which * width, width, 1),
+            mixed_after,
+            (((0,), (0,)), ((), ())),
+            preferred_element_type=F32,
+        )
+
+    sent_share = weight_share(1 - core).astype(BF16)
+    far_share = core_swap(sent_share)
+    grad_weight = (weight_share(core) + far_share.astype(F32)) * grad_scale
+
     grad_mixed, grad_li_out, back_ends = run(
-        functools.partial(grad_gate_body, chips - 1),
-        columns,
-        [tile(grad_parts[0]), tile(query_li), tile(rate)] + [tile(part) for part in grad_parts[1:]],
+        grad_gate_body,
+        columns,
+        [tile(after(grad_parts, sent_share)), tile(query_li), tile(rate)],
         [(rows, F32), (rows, F32), (rate.shape[0], F32)],
         pass_flops,
     )
-    back_sibling, back_states = exchange(back_ends, True)
+    back_entering = entering_state(back_ends, rate, rows, here, True)
     (grad_inner,) = run(
         grad_inner_body,
         columns,
@@ -415,14 +391,13 @@
     )
     grad_query_li = grad_mixed * li_out
     grad_key_li, grad_query_mr, own_product, prev_product, tap_partial = run(
-        functools.partial(grad_long_body, chips - 1),
+        grad_long_body,
         columns,
         [
-            ("scalar", back_scalars),
             tile(grad_inner),
             tile(rate),
             tile(coef),
-            tile(back_sibling),
+            tile(back_entering),
             tile(mixed_mr),
             tile(key_li),
             tile(query_mr),
@@ -432,8 +407,7 @@
             table("half3"),
             table("both3"),
             table("lags3"),
-        ]
-        + [tile(state) for state in back_states],
+        ],
         [(rows, F32), (rows, F32), (rows, F32), (rows, BF16), (rows, F32)],
         7 * pass_flops,
     )
@@ -451,28 +425,14 @@
     own_half = lax.dynamic_index_in_dim(halves, core, 0, keepdims=False)
     far_half = lax.dynamic_index_in_dim(halves, 1 - core, 0, keepdims=False)
     chip_half = (own_half + core_swap(far_half)).astype(BF16)
-    everywhere = [chip_half] + [chip_swap(chip_half, s) for s in range(1, chips)]
-    plane_half = pair_sum([part.astype(F32) for part in everywhere]) * grad_scale
+    everywhere = plane_trade(copies(chip_half, chips)).reshape(chips, tap_half, columns)
+    plane_half = jnp.sum(everywhere.astype(F32), axis=0) * grad_scale
     other_half = core_swap(plane_half)
     grad_taps = jnp.where(
         core == 0,
         jnp.concatenate([plane_half, other_half], axis=0),
         jnp.concatenate([other_half, plane_half], axis=0),
     )
-
-    cot_rows = jnp.concatenate(cot_parts, axis=0)
-    mixed_rows = jnp.concatenate(mixed_parts, axis=0)
-
-    def weight_share(which):
-        return lax.dot_general(
-            columns_at(cot_rows, which, width),
-            mixed_rows,
-            (((0,), (0,)), ((), ())),
-            preferred_element_type=F32,
-        )
-
-    far_share = core_swap(weight_share(1 - core).astype(BF16))
-    grad_weight = (weight_share(core) + far_share.astype(F32)) * grad_scale
     return (
         output,
         grad_query_mr,

time: 154 us -> 169 us (1.097)
  the two profiles are of different devices: /device:TPU:0 before, /device:TPU:1 now
where the time goes in v1:
time: 169 us; the launch traced here: 166 us
  starting transfers between devices  45.5 us (27%)
  waiting for transfers between devices  44.2 us (26%)
  Pallas kernels  18.9 us (11%)
  other arithmetic  15.8 us (9%)
  local copies, waits for them, and re-layouts  15.5 us (9%)
  matrix products  14 us (8%)
  blocking collectives  11.2 us (7%)
    all_to_all x4, waiting for transfers between devices, plane_trade(): return lax.all_to_all(x, 'ctx', 0, 0, axis_index_groups=groups, tiled=True)  23.6 us
    pallas_call x8, Pallas kernels, run(): pl.pallas_call(body, grid=(columns // tile,), in_specs=in_specs, out_spec...  18.9 us
    all_to_all x4, starting transfers between devices, plane_trade(): return lax.all_to_all(x, 'ctx', 0, 0, axis_index_groups=groups, tiled=True)  15.7 us
    unnamed x96, local copies, waits for them, and re-layouts  15.5 us
    all_to_all x2, waiting for transfers between devices, line_trade(): return lax.all_to_all(x, 'fsdp', 0, 0, tiled=True)  11.5 us
    all_to_all x1, blocking collectives, plane_trade(): return lax.all_to_all(x, 'ctx', 0, 0, axis_index_groups=groups, tiled=True)  11.2 us
    all_to_all x2, starting transfers between devices, line_trade(): return lax.all_to_all(x, 'fsdp', 0, 0, tiled=True)  10.5 us
    ppermute x6, starting transfers between devices, entering_state(): arrived = lax.ppermute(total, 'ctx', [(i, i ^ by) for i in range(size)])  7.32 us
  transfers between devices with their start and end apart: 18, of which 10 were waited for; matrix products, arithmetic and copies ran while one was open for 14% of the time, Pallas kernels for 10%

profile of v1, /device:TPU:1, one launch (start us, length us, event | category | flops | bytes accessed | tf_op | source)
XLA Modules:
  0.0 166.3 jit_solution(6106660282776397795)
XLA Ops:
  0.7 2.5 %pad_maximum_fusion.1 = bf16[512,1024]{1,0:T(8,128)(2,1)} fusion(bf16[128,1024]{1,0:T(8,128)(2,1)} %param.28), kind=kLoop, calls=%fused_computation.7 | loop fusion | flops 4194304 | bytes 1310720 | tf_op jit(solution)/shard_map/concatenate | solution.py:233
  3.2 5.6 %all-to-all-start.1 = ((bf16[4,128,1024]{2,1,0:T(8,128)(2,1)}), bf16[4,128,1024]{2,1,0:T(8,128)(2,1)}, u32[]{:S(2)}, u32[]{:S(2)}) async-start(bf16[4,128,1024]{2,1,0:T(8,128)(2,1)} %bitcast.3), calls=%async_computation.1 | async-start | bytes 2097152 | tf_op jit(solution)/shard_map/all_to_all | solution.py:229
  8.9 4.1 %collective-permute-start = (bf16[128,1024]{1,0:T(8,128)(2,1)S(1)}, bf16[128,1024]{1,0:T(8,128)(2,1)S(1)}, u32[]{:S(2)}, u32[]{:S(2)}) collective-permute-start(bf16[128,1024]{1,0:T(8,128)(2,1)S(1)} %multiply_convert_fusion.product), channel_id=1, source_target_pairs={{0,4},{4,8},{8,12},{12,16},{16,20},{20,24},{24,28},{1,5},{5,9},{9,... | collective-permute-start | bytes 786440 | tf_op jit(solution)/shard_map/ppermute | solution.py:219
  17.1 3.4 %shard_map.234 = (f32[256,1024]{1,0:T(8,128)S(1)}, f32[128,1024]{1,0:T(8,128)S(1)}, bf16[128,1024]{1,0:T(8,128)(2,1)S(1)}, bf16[128,1024]{1,0:T(8,128)(2,1)S(1)}, f32[16,1024]{1,0:T(8,128)S(1)}) custom-call(bf16[128,1024]{1,0:T(8,128)(2,1)S(1)} %collective-permute-done.before, bf16[128,1024]{1,0:T(8,128)(2,1)S(1)} %multiply_convert_fusion.product, ...), custom_call_target="tpu_custom_call" | custom-call | flops 536870912 | bytes 4784128 | tf_op jit(solution)/shard_map/pallas_call | solution.py:201
  26.4 2.2 %collective-permute-done.2 = f32[16,1024]{1,0:T(8,128)S(1)} collective-permute-done((f32[16,1024]{1,0:T(8,128)S(1)}, f32[16,1024]{1,0:T(8,128)S(1)}, u32[]{:S(2)}, u32[]{:S(2)}) %collective-permute-start.2) | collective-permute-done | bytes 65568 | tf_op jit(solution)/shard_map/ppermute | solution.py:253
  37.2 4.3 %all-to-all-start.2 = ((bf16[4,128,1024]{2,1,0:T(8,128)(2,1)}), bf16[4,128,1024]{2,1,0:T(8,128)(2,1)}, u32[]{:S(2)}, u32[]{:S(2)}) async-start(bf16[4,128,1024]{2,1,0:T(8,128)(2,1)} %bitcast.5), calls=%async_computation.2 | async-start | bytes 2097152 | tf_op jit(solution)/shard_map/all_to_all | solution.py:225
  42.5 12.8 %all-to-all-done.2 = bf16[4,128,1024]{2,1,0:T(8,128)(2,1)} async-done(((bf16[4,128,1024]{2,1,0:T(8,128)(2,1)}), bf16[4,128,1024]{2,1,0:T(8,128)(2,1)}, u32[]{:S(2)}, u32[]{:S(2)}) %all-to-all-start.2) | async-done | bytes 1048608 | tf_op jit(solution)/shard_map/all_to_all | solution.py:225
  55.3 3.5 %all-to-all-start = ((bf16[4,128,1024]{2,1,0:T(8,128)(2,1)}), bf16[4,128,1024]{2,1,0:T(8,128)(2,1)S(1)}, u32[]{:S(2)}, u32[]{:S(2)}) async-start(bf16[4,128,1024]{2,1,0:T(8,128)(2,1)} %bitcast.31), calls=%async_computation | async-start | bytes 2097152 | tf_op jit(solution)/shard_map/all_to_all | solution.py:225
  58.8 3.4 %maximum_select_fusion = bf16[1024,1024]{1,0:T(8,128)(2,1)S(1)} fusion(bf16[512,1024]{1,0:T(8,128)(2,1)} %collective-permute-done.4, bf16[512,1024]{1,0:T(8,128)(2,1)} %param.27, pred[]{:T(512)S(6)} %eq.6), kind=kLoop, calls=%fused_computation | loop fusion | flops 9437184 | bytes 4194305 | tf_op jit(solution)/shard_map/jit(_where)/select_n | solution.py:347
  63.5 3.5 %convolution_convert_fusion.1 = bf16[512,1024]{1,0:T(8,128)(2,1)} fusion(bf16[512,1024]{1,0:T(8,128)(2,1)} %bitcast.6, bf16[1024,1024]{1,0:T(8,128)(2,1)S(1)} %maximum_select_fusion), kind=kOutput, calls=%fused_computation.4 | convolution fusion | flops 1074266112 | bytes 4194304 | tf_op jit(solution)/shard_map/dot_general | solution.py:353
  67.0 4.8 %all-to-all-done = bf16[4,128,1024]{2,1,0:T(8,128)(2,1)S(1)} async-done(((bf16[4,128,1024]{2,1,0:T(8,128)(2,1)}), bf16[4,128,1024]{2,1,0:T(8,128)(2,1)S(1)}, u32[]{:S(2)}, u32[]{:S(2)}) %all-to-all-start) | async-done | bytes 1048608 | tf_op jit(solution)/shard_map/all_to_all | solution.py:225
  72.9 3.5 %all-to-all-start.5 = ((bf16[4,128,1024]{2,1,0:T(8,128)(2,1)}), bf16[4,128,1024]{2,1,0:T(8,128)(2,1)S(1)}, u32[]{:S(2)}, u32[]{:S(2)}) async-start(bf16[4,128,1024]{2,1,0:T(8,128)(2,1)} %bitcast.34), calls=%async_computation.5 | async-start | bytes 2097152 | tf_op jit(solution)/shard_map/all_to_all | solution.py:225
  76.4 4.3 %convolution_convert_fusion = bf16[512,1024]{1,0:T(8,128)(2,1)} fusion(bf16[512,1024]{1,0:T(8,128)(2,1)} %bitcast.28, bf16[1024,1024]{1,0:T(8,128)(2,1)} %copy-done.42), kind=kOutput, calls=%fused_computation.3 | convolution fusion | flops 1074266112 | bytes 4194304 | tf_op jit(solution)/shard_map/dot_general | solution.py:356
  80.7 2.7 %convolution_convert_fusion.2 = bf16[512,1024]{1,0:T(8,128)(2,1)} fusion(bf16[512,1024]{1,0:T(8,128)(2,1)S(1)} %bitcast.29, bf16[512,1024]{1,0:T(8,128)(2,1)} %bitcast.6, s32[]{:T(128)S(6)} %select_n.103), kind=kOutput, calls=%fused_computation.5 | convolution fusion | flops 537395200 | bytes 2621444 | tf_op jit(solution)/shard_map/dot_general | solution.py:366
  83.4 6.0 %all-to-all-done.5 = bf16[4,128,1024]{2,1,0:T(8,128)(2,1)S(1)} async-done(((bf16[4,128,1024]{2,1,0:T(8,128)(2,1)}), bf16[4,128,1024]{2,1,0:T(8,128)(2,1)S(1)}, u32[]{:S(2)}, u32[]{:S(2)}) %all-to-all-start.5) | async-done | bytes 1048608 | tf_op jit(solution)/shard_map/all_to_all | solution.py:225
  103.6 4.4 %all-to-all-start.3 = ((bf16[4,128,1024]{2,1,0:T(8,128)(2,1)}), bf16[4,128,1024]{2,1,0:T(8,128)(2,1)}, u32[]{:S(2)}, u32[]{:S(2)}) async-start(bf16[4,128,1024]{2,1,0:T(8,128)(2,1)} %bitcast.33), calls=%async_computation.3 | async-start | bytes 2097152 | tf_op jit(solution)/shard_map/all_to_all | solution.py:225
  111.0 2.3 %shard_map.238.inner = f32[128,1024]{1,0:T(8,128)S(1)} custom-call(f32[128,1024]{1,0:T(8,128)S(1)} %copy-done.23, f32[256,1024]{1,0:T(8,128)S(1)} %get-tuple-element.34.li_spec, bf16[256,384]{1,0:T(8,128)(2,1)S(1)} %copy-done.12, bf16[128,768]{1,0:T(8,128)(2,1)S(1)} %copy-done.15), custom_call_target="tpu_custom_call" | custom-call | flops 402653184 | bytes 2490368 | tf_op jit(solution)/shard_map/pallas_call | solution.py:201
  114.3 4.5 %shard_map.239 = (f32[128,1024]{1,0:T(8,128)}, f32[128,1024]{1,0:T(8,128)}, f32[128,1024]{1,0:T(8,128)S(1)}, bf16[128,1024]{1,0:T(8,128)(2,1)S(1)}, f32[128,1024]{1,0:T(8,128)S(1)}) custom-call(f32[128,1024]{1,0:T(8,128)S(1)} %shard_map.238.inner, f32[16,1024]{1,0:T(8,128)S(1)} %get-tuple-element.57.rate, f32[16,1024]{1,0:T(8,128)S(1)} %get-tuple-element.56.coef, ...), custom_call_target="tpu_custom_call" | custom-call | flops 939524096 | bytes 7274496 | tf_op jit(solution)/shard_map/pallas_call | solution.py:201
  122.6 11.2 %all_to_all.72 = bf16[4,64,1024]{2,1,0:T(8,128)(2,1)} all-to-all(bf16[4,64,1024]{2,1,0:T(8,128)(2,1)S(1)} %bitcast.32), channel_id=1, replica_groups={{0,8,16,24},{4,12,20,28},{1,9,17,25},{5,13,21,29},{2,10,18,26},{6,14,22..., dimensions={0} | all-to-all | bytes 1048576 | tf_op jit(solution)/shard_map/all_to_all | solution.py:225
  133.8 4.9 %all-to-all-start.4 = ((bf16[4,128,1024]{2,1,0:T(8,128)(2,1)}), bf16[4,128,1024]{2,1,0:T(8,128)(2,1)}, u32[]{:S(2)}, u32[]{:S(2)}) async-start(bf16[4,128,1024]{2,1,0:T(8,128)(2,1)} %all-to-all-done.3), calls=%async_computation.4 | async-start | bytes 2097152 | tf_op jit(solution)/shard_map/all_to_all | solution.py:229
  138.7 2.4 %collective-permute-start.11 = (bf16[512,1024]{1,0:T(8,128)(2,1)}, bf16[512,1024]{1,0:T(8,128)(2,1)}, u32[]{:S(2)}, u32[]{:S(2)}) collective-permute-start(bf16[512,1024]{1,0:T(8,128)(2,1)} %convolution_convert_fusion.2), channel_id=1, source_target_pairs={{0,4},{4,0},{8,12},{12,8},{16,20},{20,16},{24,28},{28,24},{1,5},{5... | collective-permute-start | bytes 3145736 | tf_op jit(solution)/shard_map/ppermute | solution.py:214
  145.2 3.5 %add_multiply_fusion = f32[512,1024]{1,0:T(8,128)} fusion(bf16[512,1024]{1,0:T(8,128)(2,1)} %collective-permute-done.11, bf16[512,1024]{1,0:T(8,128)(2,1)S(1)} %bitcast.30, bf16[512,1024]{1,0:T(8,128)(2,1)} %bitcast.6, s32[]{:T(128)S(6)} %select_n.116), kind=kOutput, calls=%fused_computation.1 | convolution fusion | flops 538443776 | bytes 4718596 | tf_op jit(solution)/shard_map/dot_general | solution.py:366
  152.6 11.5 %all-to-all-done.4 = bf16[4,128,1024]{2,1,0:T(8,128)(2,1)} async-done(((bf16[4,128,1024]{2,1,0:T(8,128)(2,1)}), bf16[4,128,1024]{2,1,0:T(8,128)(2,1)}, u32[]{:S(2)}, u32[]{:S(2)}) %all-to-all-start.4) | async-done | bytes 1048608 | tf_op jit(solution)/shard_map/all_to_all | solution.py:229
  164.1 2.3 %convert_reduce_fusion = f32[128,1024]{1,0:T(8,128)} fusion(bf16[4,128,1024]{2,1,0:T(8,128)(2,1)} %all-to-all-done.4), kind=kLoop, calls=%fused_computation.2 | loop fusion | flops 917504 | bytes 1572864 | tf_op jit(solution)/shard_map/reduce_sum | solution.py:361
  (140 shorter events, 51.8 us)
Async XLA Ops:
  3.2 13.9 %copy-start.2 = (bf16[128,1024]{1,0:T(8,128)(2,1)S(1)}, bf16[128,1024]{1,0:T(8,128)(2,1)}, u32[]{:S(2)}) copy-start(bf16[128,1024]{1,0:T(8,128)(2,1)} %query_mr.1) | copy-start | bytes 786436
  3.2 13.9 %copy-start.3 = (bf16[128,1024]{1,0:T(8,128)(2,1)S(1)}, bf16[128,1024]{1,0:T(8,128)(2,1)}, u32[]{:S(2)}) copy-start(bf16[128,1024]{1,0:T(8,128)(2,1)} %key_li.1) | copy-start | bytes 786436
  3.2 34.0 %all-to-all-start.1 = ((bf16[4,128,1024]{2,1,0:T(8,128)(2,1)}), bf16[4,128,1024]{2,1,0:T(8,128)(2,1)}, u32[]{:S(2)}, u32[]{:S(2)}) async-start(bf16[4,128,1024]{2,1,0:T(8,128)(2,1)} %bitcast.3), calls=%async_computation.1 | async-start | bytes 2097152 | tf_op jit(solution)/shard_map/all_to_all | solution.py:229
  8.9 8.2 %collective-permute-start = (bf16[128,1024]{1,0:T(8,128)(2,1)S(1)}, bf16[128,1024]{1,0:T(8,128)(2,1)S(1)}, u32[]{:S(2)}, u32[]{:S(2)}) collective-permute-start(bf16[128,1024]{1,0:T(8,128)(2,1)S(1)} %multiply_convert_fusion.product), channel_id=1, source_target_pairs={{0,4},{4,8},{8,12},{12,16},{16,20},{20,24},{24,28},{1,5},{5,9},{9,... | collective-permute-start | bytes 786440 | tf_op jit(solution)/shard_map/ppermute | solution.py:219
  15.0 17.3 %copy-start.14 = (bf16[128,768]{1,0:T(8,128)(2,1)S(1)}, bf16[128,768]{1,0:T(8,128)(2,1)}, u32[]{:S(2)}) copy-start(bf16[128,768]{1,0:T(8,128)(2,1)} %constant.69.clone.first3) | copy-start | bytes 589828
  17.1 15.3 %copy-start.32 = (bf16[256,256]{1,0:T(8,128)(2,1)S(1)}, bf16[256,256]{1,0:T(8,128)(2,1)}, u32[]{:S(2)}) copy-start(bf16[256,256]{1,0:T(8,128)(2,1)} %constant.67.clone.half2) | copy-start | bytes 393220
  23.7 1.3 collective-permute-start.1
  24.9 3.6 %collective-permute-start.2 = (f32[16,1024]{1,0:T(8,128)S(1)}, f32[16,1024]{1,0:T(8,128)S(1)}, u32[]{:S(2)}, u32[]{:S(2)}) collective-permute-start(f32[16,1024]{1,0:T(8,128)S(1)} %add_select_fusion.3), channel_id=1, source_target_pairs={{0,8},{4,12},{8,0},{12,4},{16,24},{20,28},{24,16},{28,20},{1,9},{5... | collective-permute-start | bytes 196616 | tf_op jit(solution)/shard_map/ppermute | solution.py:253
  28.6 6.7 %collective-permute-start.3 = (f32[16,1024]{1,0:T(8,128)S(1)}, f32[16,1024]{1,0:T(8,128)S(1)}, u32[]{:S(2)}, u32[]{:S(2)}) collective-permute-start(f32[16,1024]{1,0:T(8,128)S(1)} %add_select_fusion.2), channel_id=1, source_target_pairs={{0,16},{4,20},{8,24},{12,28},{16,0},{20,4},{24,8},{28,12},{1,17},{... | collective-permute-start | bytes 196616 | tf_op jit(solution)/shard_map/ppermute | solution.py:253
  30.6 28.3 %collective-permute-start.4 = (bf16[512,1024]{1,0:T(8,128)(2,1)}, bf16[512,1024]{1,0:T(8,128)(2,1)}, u32[]{:S(2)}, u32[]{:S(2)}) collective-permute-start(bf16[512,1024]{1,0:T(8,128)(2,1)} %param.27), channel_id=1, source_target_pairs={{0,4},{4,0},{8,12},{12,8},{16,20},{20,16},{24,28},{28,24},{1,5},{5... | collective-permute-start | bytes 3145736 | tf_op jit(solution)/shard_map/ppermute | solution.py:214
  37.2 18.1 %all-to-all-start.2 = ((bf16[4,128,1024]{2,1,0:T(8,128)(2,1)}), bf16[4,128,1024]{2,1,0:T(8,128)(2,1)}, u32[]{:S(2)}, u32[]{:S(2)}) async-start(bf16[4,128,1024]{2,1,0:T(8,128)(2,1)} %bitcast.5), calls=%async_computation.2 | async-start | bytes 2097152 | tf_op jit(solution)/shard_map/all_to_all | solution.py:225
  55.3 16.6 %all-to-all-start = ((bf16[4,128,1024]{2,1,0:T(8,128)(2,1)}), bf16[4,128,1024]{2,1,0:T(8,128)(2,1)S(1)}, u32[]{:S(2)}, u32[]{:S(2)}) async-start(bf16[4,128,1024]{2,1,0:T(8,128)(2,1)} %bitcast.31), calls=%async_computation | async-start | bytes 2097152 | tf_op jit(solution)/shard_map/all_to_all | solution.py:225
  72.9 16.6 %all-to-all-start.5 = ((bf16[4,128,1024]{2,1,0:T(8,128)(2,1)}), bf16[4,128,1024]{2,1,0:T(8,128)(2,1)S(1)}, u32[]{:S(2)}, u32[]{:S(2)}) async-start(bf16[4,128,1024]{2,1,0:T(8,128)(2,1)} %bitcast.34), calls=%async_computation.5 | async-start | bytes 2097152 | tf_op jit(solution)/shard_map/all_to_all | solution.py:225
  94.1 2.6 %collective-permute-start.5 = (f32[16,1024]{1,0:T(8,128)}, f32[16,1024]{1,0:T(8,128)S(1)}, u32[]{:S(2)}, u32[]{:S(2)}) collective-permute-start(f32[16,1024]{1,0:T(8,128)} %get-tuple-element.43), channel_id=1, source_target_pairs={{0,4},{4,0},{8,12},{12,8},{16,20},{20,16},{24,28},{28,24},{1,5},{5... | collective-permute-start | bytes 196616 | tf_op jit(solution)/shard_map/ppermute | solution.py:253
  97.7 3.2 %collective-permute-start.6 = (f32[16,1024]{1,0:T(8,128)S(1)}, f32[16,1024]{1,0:T(8,128)S(1)}, u32[]{:S(2)}, u32[]{:S(2)}) collective-permute-start(f32[16,1024]{1,0:T(8,128)S(1)} %add_select_fusion.1), channel_id=1, source_target_pairs={{0,8},{4,12},{8,0},{12,4},{16,24},{20,28},{24,16},{28,20},{1,9},{5... | collective-permute-start | bytes 196616 | tf_op jit(solution)/shard_map/ppermute | solution.py:253
  102.4 10.9 %collective-permute-start.7 = (f32[16,1024]{1,0:T(8,128)}, f32[16,1024]{1,0:T(8,128)}, u32[]{:S(2)}, u32[]{:S(2)}) collective-permute-start(f32[16,1024]{1,0:T(8,128)} %add_select_fusion), channel_id=1, source_target_pairs={{0,16},{4,20},{8,24},{12,28},{16,0},{20,4},{24,8},{28,12},{1,17},{... | collective-permute-start | bytes 196616 | tf_op jit(solution)/shard_map/ppermute | solution.py:253
  103.6 19.0 %all-to-all-start.3 = ((bf16[4,128,1024]{2,1,0:T(8,128)(2,1)}), bf16[4,128,1024]{2,1,0:T(8,128)(2,1)}, u32[]{:S(2)}, u32[]{:S(2)}) async-start(bf16[4,128,1024]{2,1,0:T(8,128)(2,1)} %bitcast.33), calls=%async_computation.3 | async-start | bytes 2097152 | tf_op jit(solution)/shard_map/all_to_all | solution.py:225
  119.5 3.0 %collective-permute-start.9 = (f32[64,1024]{1,0:T(8,128)S(1)}, f32[64,1024]{1,0:T(8,128)S(1)}, u32[]{:S(2)}, u32[]{:S(2)}) collective-permute-start(f32[64,1024]{1,0:T(8,128)S(1)} %dynamic-slice_bitcast_fusion), channel_id=1, source_target_pairs={{0,4},{4,0},{8,12},{12,8},{16,20},{20,16},{24,28},{28,24},{1,5},{5... | collective-permute-start | bytes 786440 | tf_op jit(solution)/shard_map/ppermute | solution.py:214
  121.3 19.7 %copy-start.19 = (f32[128,1024]{1,0:T(8,128)S(1)}, f32[128,1024]{1,0:T(8,128)}, u32[]{:S(2)}) copy-start(f32[128,1024]{1,0:T(8,128)} %copy-done.18) | copy-start | bytes 1572868
  121.4 19.7 %copy-start.21 = (f32[128,1024]{1,0:T(8,128)S(1)}, f32[128,1024]{1,0:T(8,128)}, u32[]{:S(2)}) copy-start(f32[128,1024]{1,0:T(8,128)} %copy-done.20) | copy-start | bytes 1572868
  133.8 30.3 %all-to-all-start.4 = ((bf16[4,128,1024]{2,1,0:T(8,128)(2,1)}), bf16[4,128,1024]{2,1,0:T(8,128)(2,1)}, u32[]{:S(2)}, u32[]{:S(2)}) async-start(bf16[4,128,1024]{2,1,0:T(8,128)(2,1)} %all-to-all-done.3), calls=%async_computation.4 | async-start | bytes 2097152 | tf_op jit(solution)/shard_map/all_to_all | solution.py:229
  138.7 6.4 %collective-permute-start.11 = (bf16[512,1024]{1,0:T(8,128)(2,1)}, bf16[512,1024]{1,0:T(8,128)(2,1)}, u32[]{:S(2)}, u32[]{:S(2)}) collective-permute-start(bf16[512,1024]{1,0:T(8,128)(2,1)} %convolution_convert_fusion.2), channel_id=1, source_target_pairs={{0,4},{4,0},{8,12},{12,8},{16,20},{20,16},{24,28},{28,24},{1,5},{5... | collective-permute-start | bytes 3145736 | tf_op jit(solution)/shard_map/ppermute | solution.py:214
  141.9 8.1 %collective-permute-start.8 = (bf16[128,1024]{1,0:T(8,128)(2,1)S(1)}, bf16[128,1024]{1,0:T(8,128)(2,1)S(1)}, u32[]{:S(2)}, u32[]{:S(2)}) collective-permute-start(bf16[128,1024]{1,0:T(8,128)(2,1)S(1)} %copy-done.35), channel_id=1, source_target_pairs={{4,0},{8,4},{12,8},{16,12},{20,16},{24,20},{28,24},{5,1},{9,5},{13... | collective-permute-start | bytes 786440 | tf_op jit(solution)/shard_map/ppermute | solution.py:219
  145.1 6.6 %collective-permute-start.10 = (f32[64,1024]{1,0:T(8,128)S(1)}, f32[64,1024]{1,0:T(8,128)S(1)}, u32[]{:S(2)}, u32[]{:S(2)}) collective-permute-start(f32[64,1024]{1,0:T(8,128)S(1)} %broadcast_multiply_fusion), channel_id=1, source_target_pairs={{0,4},{4,0},{8,12},{12,8},{16,20},{20,16},{24,28},{28,24},{1,5},{5... | collective-permute-start | bytes 786440 | tf_op jit(solution)/shard_map/ppermute | solution.py:214
  (42 other events, 181.3 us)

commit v2 on v1

--- a/solution.py
+++ b/solution.py
@@ -148,24 +148,56 @@
     mixed[...] = (query[...].astype(F32) * total).astype(BF16)
 
 
-def grad_gate_body(parts, query, rate, grad_mixed, grad_out, ends):
-    rows = query.shape[0]
-    total = parts[:rows].astype(F32)
-    for k in range(1, parts.shape[0] // rows):
-        total = total + parts[k * rows : (k + 1) * rows].astype(F32)
+def weighted(total, starts, cotangent, pieces):
+    for k, piece in enumerate(pieces):
+        count = piece.shape[0]
+        block = cotangent[:, pl.ds(pl.multiple_of(starts[k], 128), count)]
+        found = jnp.dot(block, piece[...], preferred_element_type=F32)
+        total = found if total is None else total + found
+    return total
+
+
+def grad_early_body(starts, cotangent, *rest):
+    pieces, (total,) = rest[:-1], rest[-1:]
+    total[...] = weighted(None, starts, cotangent, pieces)
+
+
+def grad_gate_body(count, starts, early, cotangent, query, rate, *rest):
+    pieces, (grad_mixed, grad_out, ends) = rest[:count], rest[count:]
+    total = weighted(early[...], starts, cotangent, pieces)
     grad_mixed[...] = total
     gated = total * query[...].astype(F32)
     grad_out[...] = gated
     ends[...] = fold_modes(gated, rate[...], True)
 
 
+def out_block(starts, mixed, pieces, result):
+    for k, piece in enumerate(pieces):
+        count = piece.shape[0]
+        found = lax.dot_general(mixed[...], piece[...], (((1,), (1,)), ((), ())), preferred_element_type=F32)
+        result[:, pl.ds(pl.multiple_of(starts[k], 128), count)] = found.astype(BF16)
+
+
+def out_early_body(starts, mixed, *rest):
+    out_block(starts, mixed, rest[:-1], rest[-1])
+
+
+def out_late_body(count, starts, early, mixed, *rest):
+    pieces, parts, whole = rest[:count], rest[count:-1], rest[-1]
+    whole[...] = early[...]
+    out_block(starts, mixed, pieces, whole)
+    width = parts[0].shape[1]
+    for r, part in enumerate(parts):
+        part[...] = whole[:, pl.ds(pl.multiple_of(starts[count + r], 128), width)]
+
+
 def grad_inner_body(grad_out, li_spec, half3, first3, inner):
     inner[...] = apply3(first3[...], times_conj(apply3(half3[...], grad_out[...]), li_spec[...]))
 
 
 def grad_long_body(
-    inner, rate, coef, entering, mixed_mr, key_li, query_mr, conv, spec, mr_spec, half3, both3, lags3,
-    grad_key_li, grad_query_mr, own_product, prev_product, taps,
+    inner, rate, coef, entering, mixed_mr, key_li, query_mr, conv, spec, half3, lags3,
+    grad_key_li, grad_query_mr, grad_spec, taps,
 ):
     rows = inner.shape[0]
     grad_input = inner[...] + spread_modes(rate[...], coef[...] * entering[...], rows, 1.0, True)
@@ -174,10 +206,15 @@
     grad_query_mr[...] = grad_mixed_mr * conv[...]
     grad_conv = grad_mixed_mr * query_mr[...].astype(F32)
     found = apply3(half3[...], grad_conv)
-    products = apply3(both3[...], times_conj(found, mr_spec[...]))
+    grad_spec[...] = found
+    taps[...] = apply3(lags3[...], times_conj(spec[...], found))
+
+
+def grad_taps_body(grad_spec, mr_spec, both3, own_product, prev_product):
+    rows = own_product.shape[0]
+    products = apply3(both3[...], times_conj(grad_spec[...], mr_spec[...]))
     own_product[...] = products[:rows]
     prev_product[...] = products[rows:].astype(BF16)
-    taps[...] = apply3(lags3[...], times_conj(spec[...], found))
 
 
 def grad_product_body(own, arrived, key, value, grad_key, grad_value):
@@ -193,8 +230,10 @@
     for kind, array in inputs:
         if kind == "tile":
             in_specs.append(pl.BlockSpec((array.shape[0], tile), lambda c: (0, c)))
+        elif kind == "whole":
+            in_specs.append(pl.BlockSpec(array.shape, lambda c: (0, 0)))
         else:
-            in_specs.append(pl.BlockSpec(array.shape, lambda c: (0, 0)))
+            in_specs.append(pl.BlockSpec(memory_space=pltpu.SMEM))
         moved += math.prod(array.shape) * array.dtype.itemsize
     for rows, dtype in outputs:
         moved += rows * columns * jnp.dtype(dtype).itemsize
@@ -209,6 +248,20 @@
     )(*[array for _, array in inputs])
 
 
+def run_once(body, inputs, outputs, scratch, flops):
+    moved = sum(math.prod(array.shape) * array.dtype.itemsize for array in inputs)
+    return pl.pallas_call(
+        body,
+        in_specs=[pl.BlockSpec(memory_space=pltpu.SMEM)]
+        + [pl.BlockSpec(memory_space=pltpu.VMEM)] * (len(inputs) - 1),
+        out_specs=[pl.BlockSpec(memory_space=pltpu.VMEM)] * len(outputs),
+        out_shape=[jax.ShapeDtypeStruct(shape, dtype) for shape, dtype in outputs],
+        scratch_shapes=scratch,
+        compiler_params=pltpu.CompilerParams(vmem_limit_bytes=32 * 1024 * 1024),
+        cost_estimate=pl.CostEstimate(flops=flops, bytes_accessed=moved, transcendentals=0),
+    )(*inputs)
+
+
 def core_swap(x):
     size = lax.axis_size("ctx")
     return lax.ppermute(x, "ctx", [(i, i ^ 1) for i in range(size)])
@@ -217,6 +270,16 @@
 def shifted(x, by):
     size = lax.axis_size("ctx")
     return lax.ppermute(x, "ctx", [(i, i + by) for i in range(size) if 0 <= i + by < size])
+
+
+def chip_swap(x, by):
+    size = lax.axis_size("ctx")
+    return lax.ppermute(x, "ctx", [(i, i ^ (2 * by)) for i in range(size)])
+
+
+def line_swap(x, by):
+    size = lax.axis_size("fsdp")
+    return lax.ppermute(x, "fsdp", [(i, i ^ by) for i in range(size)])
 
 
 def plane_trade(x):
@@ -225,20 +288,39 @@
     return lax.all_to_all(x, "ctx", 0, 0, axis_index_groups=groups, tiled=True)
 
 
-def line_trade(x):
-    return lax.all_to_all(x, "fsdp", 0, 0, tiled=True)
-
-
-def copies(x, count):
-    return jnp.concatenate([x] * count, axis=0)
-
-
-def rows_to_columns(x, count):
-    return jnp.concatenate(jnp.split(x, count, axis=0), axis=1)
-
-
 def columns_to_rows(x, count):
     return jnp.concatenate(jnp.split(x, count, axis=1), axis=0)
+
+
+def placed(pieces):
+    width = pieces[0][1].shape[1]
+    whole = jnp.zeros((pieces[0][1].shape[0], width * len(pieces)), pieces[0][1].dtype)
+    for index, piece in pieces:
+        whole = lax.dynamic_update_slice_in_dim(whole, piece, index * width, 1)
+    return whole
+
+
+def columns_at(x, index, width):
+    return lax.dynamic_slice_in_dim(x, index * width, width, 1)
+
+
+def weight_arrivals(weight, chips):
+    direct = (1, 2) if chips == 4 else range(1, chips)
+    return [(s, chip_swap(weight, s)) for s in direct]
+
+
+def weight_pieces(weight, arrivals, chips):
+    early = [(0, 0, weight)] + [(2 * s, 0, piece) for s, piece in arrivals]
+    if chips == 4:
+        (_, beside), (_, across) = arrivals
+        half = weight.shape[0] // 2
+        late = [(6, 0, chip_swap(across[:half], 1)), (6, half, chip_swap(beside[half:], 2))]
+    else:
+        late = [early.pop()]
+    return [
+        pieces + [(mask ^ 1, first, core_swap(piece)) for mask, first, piece in pieces]
+        for pieces in (early, late)
+    ]
 
 
 def after(x, *others):
@@ -262,6 +344,22 @@
         total = jnp.where(later, across * arrived + total, across * total + arrived)
         by *= 2
     return entering
+
+
+def entering_direct(ends, rate, rows, here, backward):
+    chips = lax.axis_size("ctx") // 2
+    chip, later_core = here // 2, (here & 1) != 0
+    if backward:
+        later_core = jnp.logical_not(later_core)
+    sibling = core_swap(ends)
+    block = jnp.exp(-rate * float(rows))
+    total = jnp.where(later_core, block * sibling + ends, block * ends + sibling)
+    entering = jnp.zeros_like(ends)
+    for s in range(1, chips):
+        gap = (chip ^ s) - chip - 1 if backward else chip - (chip ^ s) - 1
+        weight = jnp.exp(-rate * (2 * rows * jnp.maximum(gap, 0)).astype(F32))
+        entering = entering + jnp.where(gap >= 0, weight * chip_swap(total, s), 0.0)
+    return jnp.where(later_core, block * entering + sibling, entering)
 
 
 def shards(
@@ -283,6 +381,7 @@
     chips = ctx_count // 2
     here = lax.axis_index("ctx")
     core = here % 2
+    line = lax.axis_index("fsdp")
     grad_scale = 1.0 / math.sqrt(rows * ctx_count)
     tables = {name: jnp.asarray(table) for name, table in dft_tables(rows).items()}
     width = out_weight.shape[0]
@@ -296,8 +395,16 @@
 
     mr_product = (key_mr.astype(F32) * value_mr.astype(F32)).astype(BF16)
     before = shifted(mr_product, 1)
-
-    cot_line = line_trade(copies(cotangent, line_count))
+    arrivals = weight_arrivals(out_weight, chips)
+    cot_line = [(line, cotangent)]
+    for r in range(1, line_count):
+        cot_line.append((line ^ r, line_swap(cotangent, r)))
+
+    def starts_of(pieces):
+        return [(here ^ mask) * width + first for mask, first, piece in pieces]
+
+    def arrays_of(pieces):
+        return [piece for mask, first, piece in pieces]
 
     rate = 1.0 / li_time
     coef = li_residue * jnp.sqrt(-jnp.expm1(-2.0 * rate))
@@ -308,12 +415,11 @@
         [(2 * rows, F32), (2 * rows, F32)],
         3 * pass_flops,
     )
-    other_weight = core_swap(after(out_weight, mr_spec))
     spec, mr_conv, mixed_mr, li_input, ends = run(
         short_body,
         columns,
         [
-            tile(before),
+            tile(after(before, cot_line[1][1])),
             tile(mr_product),
             tile(query_mr),
             tile(key_li),
@@ -326,10 +432,12 @@
         4 * pass_flops,
     )
     entering = entering_state(ends, rate, rows, here, False)
+    arrivals = [(s, after(piece, entering)) for s, piece in arrivals]
+    early, late = weight_pieces(out_weight, arrivals, chips)
     (li_inner,) = run(
         inner_body,
         columns,
-        [tile(li_input), tile(li_spec), table("half2"), table("first3")],
+        [tile(after(li_input, *[piece for _, piece in cot_line])), tile(li_spec), table("half2"), table("first3")],
         [(rows, F32)],
         3 * pass_flops,
     )
@@ -341,56 +449,64 @@
         pass_flops,
     )
 
-    mixed_rows = plane_trade(copies(mixed_li, chips))
-    cot_full = rows_to_columns(after(cot_line, mixed_li), line_count)
-    cot_rows = plane_trade(columns_to_rows(cot_full, chips))
-    weight_pair = jnp.where(
-        core == 0,
-        jnp.concatenate([out_weight, other_weight], axis=0),
-        jnp.concatenate([other_weight, out_weight], axis=0),
-    )
-
-    grad_share = jnp.dot(cot_rows, weight_pair, preferred_element_type=F32).astype(BF16)
-    grad_parts = plane_trade(grad_share)
-
-    out_share = lax.dot_general(
-        mixed_rows, after(weight_pair, grad_share), (((1,), (1,)), ((), ())), preferred_element_type=F32
-    ).astype(BF16)
-    out_full = rows_to_columns(plane_trade(out_share), chips)
-    out_parts = line_trade(columns_to_rows(out_full, line_count)).reshape(line_count, rows, -1)
-    output = jnp.sum(out_parts.astype(F32), axis=0)
-
-    mixed_after = after(mixed_rows, out_share)
-
-    def weight_share(which):
-        return lax.dot_general(
-            lax.dynamic_slice_in_dim(cot_rows, which * width, width, 1),
-            mixed_after,
-            (((0,), (0,)), ((), ())),
-            preferred_element_type=F32,
-        )
-
-    sent_share = weight_share(1 - core).astype(BF16)
-    far_share = core_swap(sent_share)
-    grad_weight = (weight_share(core) + far_share.astype(F32)) * grad_scale
-
+    mixed_all = lax.all_gather(mixed_li, "ctx", axis=0, tiled=True)
+    cot_full = placed([(index, after(piece, mixed_li)) for index, piece in cot_line])
+
+    full_width = cot_full.shape[1]
+    line_width = full_width // line_count
+    whole_flops = 2 * rows * columns * full_width
+    (out_early,) = run_once(
+        out_early_body,
+        [jnp.stack(starts_of(early)), mixed_li] + arrays_of(early),
+        [((rows, full_width), BF16)],
+        [],
+        whole_flops,
+    )
+    cot_full = after(cot_full, out_early)
+    (grad_early,) = run(
+        grad_early_body,
+        columns,
+        [("scalar", jnp.stack(starts_of(early))), ("whole", cot_full)] + [tile(piece) for piece in arrays_of(early)],
+        [(rows, F32)],
+        whole_flops,
+    )
+    cot_rows = plane_trade(columns_to_rows(after(cot_full, grad_early), chips))
     grad_mixed, grad_li_out, back_ends = run(
-        grad_gate_body,
-        columns,
-        [tile(after(grad_parts, sent_share)), tile(query_li), tile(rate)],
+        functools.partial(grad_gate_body, len(late)),
+        columns,
+        [
+            ("scalar", jnp.stack(starts_of(late))),
+            tile(grad_early),
+            ("whole", cot_full),
+            tile(query_li),
+            tile(rate),
+        ]
+        + [tile(piece) for piece in arrays_of(late)],
         [(rows, F32), (rows, F32), (rate.shape[0], F32)],
-        pass_flops,
-    )
-    back_entering = entering_state(back_ends, rate, rows, here, True)
+        whole_flops,
+    )
+    out_starts = starts_of(late) + [(line ^ r) * line_width for r in range(line_count)]
+    out_parts = run_once(
+        functools.partial(out_late_body, len(late)),
+        [jnp.stack(out_starts), after(out_early, back_ends), mixed_li] + arrays_of(late),
+        [((rows, line_width), BF16)] * line_count,
+        [pltpu.VMEM((rows, full_width), BF16)],
+        whole_flops,
+    )
+    output = out_parts[0].astype(F32)
+    for r in range(1, line_count):
+        output = output + line_swap(out_parts[r], r).astype(F32)
+
+    back_entering = entering_direct(back_ends, rate, rows, here, True)
     (grad_inner,) = run(
         grad_inner_body,
         columns,
-        [tile(grad_li_out), tile(li_spec), table("half3"), table("first3")],
+        [tile(after(grad_li_out, out_parts[0])), tile(li_spec), table("half3"), table("first3")],
         [(rows, F32)],
         3 * pass_flops,
     )
     grad_query_li = grad_mixed * li_out
-    grad_key_li, grad_query_mr, own_product, prev_product, tap_partial = run(
+    grad_key_li, grad_query_mr, grad_spec, tap_partial = run(
         grad_long_body,
         columns,
         [
@@ -403,13 +519,18 @@
             tile(query_mr),
             tile(mr_conv),
             tile(spec),
-            tile(mr_spec),
             table("half3"),
-            table("both3"),
             table("lags3"),
         ],
-        [(rows, F32), (rows, F32), (rows, F32), (rows, BF16), (rows, F32)],
-        7 * pass_flops,
+        [(rows, F32), (rows, F32), (2 * rows, F32), (rows, F32)],
+        4 * pass_flops,
+    )
+    own_product, prev_product = run(
+        grad_taps_body,
+        columns,
+        [tile(grad_spec), tile(mr_spec), table("both3")],
+        [(rows, F32), (rows, BF16)],
+        3 * pass_flops,
     )
     arrived = shifted(prev_product, -1)
     grad_key_mr, grad_value_mr = run(
@@ -424,14 +545,33 @@
     halves = tap_partial.reshape(2, tap_half, columns)
     own_half = lax.dynamic_index_in_dim(halves, core, 0, keepdims=False)
     far_half = lax.dynamic_index_in_dim(halves, 1 - core, 0, keepdims=False)
-    chip_half = (own_half + core_swap(far_half)).astype(BF16)
-    everywhere = plane_trade(copies(chip_half, chips)).reshape(chips, tap_half, columns)
-    plane_half = jnp.sum(everywhere.astype(F32), axis=0) * grad_scale
+    plane_half = own_half + core_swap(far_half)
+    by = 1
+    while by < chips:
+        sent = plane_half.astype(BF16)
+        plane_half = sent.astype(F32) + chip_swap(sent, by).astype(F32)
+        by *= 2
+    plane_half = plane_half * grad_scale
     other_half = core_swap(plane_half)
     grad_taps = jnp.where(
         core == 0,
         jnp.concatenate([plane_half, other_half], axis=0),
         jnp.concatenate([other_half, plane_half], axis=0),
+    )
+
+    near_rows = columns_at(cot_rows, core, width).reshape(chips, 1, rows, width)
+    far_rows = core_swap(columns_at(cot_rows, 1 - core, width)).reshape(chips, 1, rows, width)
+    both = jnp.zeros((chips, 2, rows, width), BF16)
+    both = lax.dynamic_update_slice_in_dim(both, near_rows, core, 1)
+    both = lax.dynamic_update_slice_in_dim(both, far_rows, 1 - core, 1)
+    grad_weight = (
+        lax.dot_general(
+            both.reshape(rows * ctx_count, width),
+            mixed_all,
+            (((0,), (0,)), ((), ())),
+            preferred_element_type=F32,
+        )
+        * grad_scale
     )
     return (
         output,

time: 169 us -> 171 us (1.012)
  Pallas kernels: 18.9 us -> 34 us
  between operations: 1.22 us -> 14.6 us
  blocking collectives: 11.2 us -> 0 us
  matrix products: 14 us -> 4.18 us
  waiting for transfers between devices: 44.2 us -> 35.6 us
  local copies, waits for them, and re-layouts: 15.5 us -> 21.9 us
  other arithmetic: 15.8 us -> 13.1 us
    ppermute x0 -> x15, starting transfers between devices: none -> 23.6 us  [the longest x6 13.4 us: line_swap(): return lax.ppermute(x, 'fsdp', [(i, i ^ by) for i in range(size)])]
    all_to_all x4 -> x1, waiting for transfers between devices: 23.6 us -> 0.01 us  [plane_trade(): return lax.all_to_all(x, 'ctx', 0, 0, axis_index_groups=groups, tiled=True)]
    ppermute x0 -> x15, waiting for transfers between devices: none -> 18.4 us  [the longest x6 15.5 us: line_swap(): return lax.ppermute(x, 'fsdp', [(i, i ^ by) for i in range(size)])]
    all_to_all x2 -> x0, waiting for transfers between devices: 11.5 us -> none  [line_trade(): return lax.all_to_all(x, 'fsdp', 0, 0, tiled=True)]
    all_to_all x4 -> x1, starting transfers between devices: 15.7 us -> 4.41 us  [plane_trade(): return lax.all_to_all(x, 'ctx', 0, 0, axis_index_groups=groups, tiled=True)]
    all_to_all x1 -> x0, blocking collectives: 11.2 us -> none  [plane_trade(): return lax.all_to_all(x, 'ctx', 0, 0, axis_index_groups=groups, tiled=True)]
    ppermute x2, waiting for transfers between devices: 1.39 us -> 12.4 us  [shifted(): lax.ppermute(x, 'ctx', [(i, i + by) for i in range(size) if 0 <= i + by <...]
    all_to_all x2 -> x0, starting transfers between devices: 10.5 us -> none  [line_trade(): return lax.all_to_all(x, 'fsdp', 0, 0, tiled=True)]
  transfers between devices with their start and end apart: 18 -> 31, of which waited for: 10 -> 7; matrix products, arithmetic and copies ran while one was open for 14% -> 13% of each run, Pallas kernels for 10% -> 20%
where the time goes in v2:
time: 171 us; the launch traced here: 170 us
  starting transfers between devices  46.2 us (27%)
  waiting for transfers between devices  35.6 us (21%)
  Pallas kernels  34 us (20%)
  local copies, waits for them, and re-layouts  21.9 us (13%)
  between operations  14.6 us (9%)
  other arithmetic  13.1 us (8%)
  matrix products  4.18 us (2%)
    pallas_call x10, Pallas kernels, run(): pl.pallas_call(body, grid=(columns // tile,), in_specs=in_specs, out_spec...  27.5 us
    ppermute x6, waiting for transfers between devices, line_swap(): return lax.ppermute(x, 'fsdp', [(i, i ^ by) for i in range(size)])  15.5 us
    unnamed x82, local copies, waits for them, and re-layouts  13.7 us
    ppermute x6, starting transfers between devices, line_swap(): return lax.ppermute(x, 'fsdp', [(i, i ^ by) for i in range(size)])  13.4 us
    ppermute x2, waiting for transfers between devices, shifted(): lax.ppermute(x, 'ctx', [(i, i + by) for i in range(size) if 0 <= i + by <...  12.4 us
    ppermute x9, starting transfers between devices, chip_swap(): return lax.ppermute(x, 'ctx', [(i, i ^ 2 * by) for i in range(size)])  10.2 us
    ppermute x9, starting transfers between devices, core_swap(): return lax.ppermute(x, 'ctx', [(i, i ^ 1) for i in range(size)])  8.63 us
    pallas_call x2, Pallas kernels, run_once(): pl.pallas_call(body, in_specs=[pl.BlockSpec(memory_space=pltpu.SMEM)] + [...  6.51 us
  transfers between devices with their start and end apart: 31, of which 7 were waited for; matrix products, arithmetic and copies ran while one was open for 13% of the time, Pallas kernels for 20%

profile of v2, /device:TPU:1, one launch (start us, length us, event | category | flops | bytes accessed | tf_op | source)
XLA Modules:
  0.0 169.6 jit_solution(9687421112577490064)
XLA Ops:
  7.3 2.1 %collective-permute-start.7 = (bf16[512,1024]{1,0:T(8,128)(2,1)}, bf16[512,1024]{1,0:T(8,128)(2,1)S(1)}, u32[]{:S(2)}, u32[]{:S(2)}) collective-permute-start(bf16[512,1024]{1,0:T(8,128)(2,1)} %rest_0_.3), channel_id=1, source_target_pairs={{0,8},{4,12},{8,0},{12,4},{16,24},{20,28},{24,16},{28,20},{1,9},{5... | collective-permute-start | bytes 3145736 | tf_op jit(solution)/shard_map/ppermute | solution.py:277
  11.7 3.3 %collective-permute-start = (bf16[128,1024]{1,0:T(8,128)(2,1)S(1)}, bf16[128,1024]{1,0:T(8,128)(2,1)S(1)}, u32[]{:S(2)}, u32[]{:S(2)}) collective-permute-start(bf16[128,1024]{1,0:T(8,128)(2,1)S(1)} %multiply_convert_fusion.product), channel_id=1, source_target_pairs={{0,4},{4,8},{8,12},{12,16},{16,20},{20,24},{24,28},{1,5},{5,9},{9,... | collective-permute-start | bytes 786440 | tf_op jit(solution)/shard_map/ppermute | solution.py:272
  23.0 12.4 %collective-permute-done.before = bf16[128,1024]{1,0:T(8,128)(2,1)S(1)} collective-permute-done((bf16[128,1024]{1,0:T(8,128)(2,1)S(1)}, bf16[128,1024]{1,0:T(8,128)(2,1)S(1)}, u32[]{:S(2)}, u32[]{:S(2)}) %collective-permute-start) | collective-permute-done | bytes 262176 | tf_op jit(solution)/shard_map/ppermute | solution.py:272
  35.4 4.0 %shard_map.234 = (f32[256,1024]{1,0:T(8,128)S(1)}, f32[128,1024]{1,0:T(8,128)S(1)}, bf16[128,1024]{1,0:T(8,128)(2,1)S(1)}, bf16[128,1024]{1,0:T(8,128)(2,1)S(1)}, f32[16,1024]{1,0:T(8,128)}) custom-call(bf16[128,1024]{1,0:T(8,128)(2,1)S(1)} %collective-permute-done.before, bf16[128,1024]{1,0:T(8,128)(2,1)S(1)} %multiply_convert_fusion.product, ...), custom_call_target="tpu_custom_call" | custom-call | flops 536870912 | bytes 4784128 | tf_op jit(solution)/shard_map/pallas_call | solution.py:240
  45.9 2.3 %collective-permute-start.5 = (f32[16,1024]{1,0:T(8,128)S(1)}, f32[16,1024]{1,0:T(8,128)S(1)}, u32[]{:S(2)}, u32[]{:S(2)}) collective-permute-start(f32[16,1024]{1,0:T(8,128)S(1)} %add_select_fusion.3), channel_id=1, source_target_pairs={{0,8},{4,12},{8,0},{12,4},{16,24},{20,28},{24,16},{28,20},{1,9},{5... | collective-permute-start | bytes 196616 | tf_op jit(solution)/shard_map/ppermute | solution.py:335
  48.2 2.2 %collective-permute-done.5 = f32[16,1024]{1,0:T(8,128)S(1)} collective-permute-done((f32[16,1024]{1,0:T(8,128)S(1)}, f32[16,1024]{1,0:T(8,128)S(1)}, u32[]{:S(2)}, u32[]{:S(2)}) %collective-permute-start.5) | collective-permute-done | bytes 65568 | tf_op jit(solution)/shard_map/ppermute | solution.py:335
  52.1 2.6 %collective-permute-start.2 = (bf16[128,1024]{1,0:T(8,128)(2,1)}, bf16[128,1024]{1,0:T(8,128)(2,1)}, u32[]{:S(2)}, u32[]{:S(2)}) collective-permute-start(bf16[128,1024]{1,0:T(8,128)(2,1)} %param.28), channel_id=1, source_target_pairs={{0,2},{1,3},{2,0},{3,1},{4,6},{5,7},{6,4},{7,5},{8,10},{9,11},{10,... | collective-permute-start | bytes 786440 | tf_op jit(solution)/shard_map/ppermute | solution.py:282
  55.8 2.3 %collective-permute-start.9 = (bf16[512,1024]{1,0:T(8,128)(2,1)S(1)}, bf16[512,1024]{1,0:T(8,128)(2,1)}, u32[]{:S(2)}, u32[]{:S(2)}) collective-permute-start(bf16[512,1024]{1,0:T(8,128)(2,1)S(1)} %copy-done), channel_id=1, source_target_pairs={{0,4},{4,0},{8,12},{12,8},{16,20},{20,16},{24,28},{28,24},{1,5},{5... | collective-permute-start | bytes 3145736 | tf_op jit(solution)/shard_map/ppermute | solution.py:267
  61.9 10.0 %collective-permute-done.2 = bf16[128,1024]{1,0:T(8,128)(2,1)} collective-permute-done((bf16[128,1024]{1,0:T(8,128)(2,1)}, bf16[128,1024]{1,0:T(8,128)(2,1)}, u32[]{:S(2)}, u32[]{:S(2)}) %collective-permute-start.2) | collective-permute-done | bytes 262176 | tf_op jit(solution)/shard_map/ppermute | solution.py:282
  83.6 3.4 %collective-permute-start.14 = (bf16[256,1024]{1,0:T(8,128)(2,1)}, bf16[256,1024]{1,0:T(8,128)(2,1)S(1)}, u32[]{:S(2)}, u32[]{:S(2)}) collective-permute-start(bf16[256,1024]{1,0:T(8,128)(2,1)} %collective-permute-done.12.rest_0_), channel_id=1, source_target_pairs={{0,4},{4,0},{8,12},{12,8},{16,20},{20,16},{24,28},{28,24},{1,5},{5... | collective-permute-start | bytes 1572872 | tf_op jit(solution)/shard_map/ppermute | solution.py:267
  90.8 4.2 %shard_map.237.early = bf16[128,4096]{1,0:T(8,128)(2,1)S(1)} custom-call(s32[6]{0:T(128)S(1)} %stack.77.starts, bf16[128,1024]{1,0:T(8,128)(2,1)} %get-tuple-element.50.mixed, bf16[512,1024]{1,0:T(8,128)(2,1)S(1)} %copy-done, bf16[512,1024]{1,0:T(8,128)(2,1)S(1)} %collective-permute-done.7.rest_1_, bf16[512,1024]{1,0:T(8,128)(2,1)S(1)} %collective-permute-done.8.rest_2_, ...), custom_call_target="tpu_custom_call" | custom-call | flops 1073741824 | bytes 6553624 | tf_op jit(solution)/shard_map/pallas_call | solution.py:253
  94.9 3.9 %shard_map.238.early = f32[128,1024]{1,0:T(8,128)S(1)} custom-call(s32[6]{0:T(128)S(1)} %stack.77.starts, bf16[128,4096]{1,0:T(8,128)(2,1)S(1)} %constant_dynamic-update-slice_fusion.2.cotangent, bf16[512,1024]{1,0:T(8,128)(2,1)S(1)} %copy-done, bf16[512,1024]{1,0:T(8,128)(2,1)S(1)} %collective-permute-done.7.rest_1_, ...), custom_call_target="tpu_custom_call" | custom-call | flops 1073741824 | bytes 7864344 | tf_op jit(solution)/shard_map/pallas_call | solution.py:240
  98.9 3.5 %shard_map.239 = (f32[128,1024]{1,0:T(8,128)S(1)}, f32[128,1024]{1,0:T(8,128)S(1)}, f32[16,1024]{1,0:T(8,128)S(1)}) custom-call(s32[4]{0:T(128)S(1)} %pad_add_fusion.starts, f32[128,1024]{1,0:T(8,128)S(1)} %shard_map.238.early, bf16[128,4096]{1,0:T(8,128)(2,1)S(1)} %constant_dynamic-update-slice_fusion.2.cotangent, bf16[128,1024]{1,0:T(8,128)(2,1)S(1)} %copy-done.10, ...), custom_call_target="tpu_custom_call" | custom-call | flops 1073741824 | bytes 5111824 | tf_op jit(solution)/shard_map/pallas_call | solution.py:240
  106.5 2.4 %shard_map.240 = (bf16[128,1024]{1,0:T(8,128)(2,1)S(1)}, bf16[128,1024]{1,0:T(8,128)(2,1)S(1)}, bf16[128,1024]{1,0:T(8,128)(2,1)S(1)}, bf16[128,1024]{1,0:T(8,128)(2,1)S(1)}) custom-call(s32[8]{0:T(128)S(1)} %stack.70.starts, bf16[128,4096]{1,0:T(8,128)(2,1)S(1)} %shard_map.237.early, bf16[128,1024]{1,0:T(8,128)(2,1)} %get-tuple-element.50.mixed, ...), custom_call_target="tpu_custom_call" | custom-call | flops 1073741824 | bytes 3407904 | tf_op jit(solution)/shard_map/pallas_call | solution.py:253
  109.0 2.3 %shard_map.241.inner = f32[128,1024]{1,0:T(8,128)S(1)} custom-call(f32[128,1024]{1,0:T(8,128)S(1)} %get-tuple-element.65.grad_out, f32[256,1024]{1,0:T(8,128)S(1)} %copy-done.5, bf16[256,384]{1,0:T(8,128)(2,1)S(1)} %copy-done.18, bf16[128,768]{1,0:T(8,128)(2,1)S(1)} %copy-done.16), custom_call_target="tpu_custom_call" | custom-call | flops 402653184 | bytes 2490368 | tf_op jit(solution)/shard_map/pallas_call | solution.py:240
  111.5 3.8 %shard_map.242 = (f32[128,1024]{1,0:T(8,128)}, f32[128,1024]{1,0:T(8,128)}, f32[256,1024]{1,0:T(8,128)S(1)}, f32[128,1024]{1,0:T(8,128)S(1)}) custom-call(f32[128,1024]{1,0:T(8,128)S(1)} %shard_map.241.inner, f32[16,1024]{1,0:T(8,128)S(1)} %get-tuple-element.87.rate, f32[16,1024]{1,0:T(8,128)S(1)} %get-tuple-element.86.coef, ...), custom_call_target="tpu_custom_call" | custom-call | flops 536870912 | bytes 6094848 | tf_op jit(solution)/shard_map/pallas_call | solution.py:240
  117.9 4.4 %all-to-all-start = ((bf16[4,128,1024]{2,1,0:T(8,128)(2,1)}), bf16[4,128,1024]{2,1,0:T(8,128)(2,1)}, u32[]{:S(2)}, u32[]{:S(2)}) async-start(bf16[4,128,1024]{2,1,0:T(8,128)(2,1)} %bitcast.33), calls=%async_computation | async-start | bytes 2097152 | tf_op jit(solution)/shard_map/all_to_all | solution.py:288
  125.5 4.3 %collective-permute-start.18 = (bf16[128,1024]{1,0:T(8,128)(2,1)}, bf16[128,1024]{1,0:T(8,128)(2,1)}, u32[]{:S(2)}, u32[]{:S(2)}) collective-permute-start(bf16[128,1024]{1,0:T(8,128)(2,1)} %copy-done.37), channel_id=1, source_target_pairs={{0,3},{1,2},{2,1},{3,0},{4,7},{5,6},{6,5},{7,4},{8,11},{9,10},{10,... | collective-permute-start | bytes 786440 | tf_op jit(solution)/shard_map/ppermute | solution.py:282
  129.8 3.9 %collective-permute-start.17 = (bf16[128,1024]{1,0:T(8,128)(2,1)}, bf16[128,1024]{1,0:T(8,128)(2,1)}, u32[]{:S(2)}, u32[]{:S(2)}) collective-permute-start(bf16[128,1024]{1,0:T(8,128)(2,1)} %copy-done.36), channel_id=1, source_target_pairs={{0,2},{1,3},{2,0},{3,1},{4,6},{5,7},{6,4},{7,5},{8,10},{9,11},{10,... | collective-permute-start | bytes 786440 | tf_op jit(solution)/shard_map/ppermute | solution.py:282
  135.8 2.3 %shard_map.243 = (f32[128,1024]{1,0:T(8,128)S(1)}, bf16[128,1024]{1,0:T(8,128)(2,1)}) custom-call(f32[256,1024]{1,0:T(8,128)S(1)} %get-tuple-element.70.grad_spec, f32[256,1024]{1,0:T(8,128)S(1)} %copy-done.2, bf16[256,768]{1,0:T(8,128)(2,1)S(1)} %copy-done.24), custom_call_target="tpu_custom_call" | custom-call | flops 402653184 | bytes 3276800 | tf_op jit(solution)/shard_map/pallas_call | solution.py:240
  138.1 3.0 %collective-permute-start.23 = (bf16[128,1024]{1,0:T(8,128)(2,1)}, bf16[128,1024]{1,0:T(8,128)(2,1)S(1)}, u32[]{:S(2)}, u32[]{:S(2)}) collective-permute-start(bf16[128,1024]{1,0:T(8,128)(2,1)} %get-tuple-element.72), channel_id=1, source_target_pairs={{4,0},{8,4},{12,8},{16,12},{20,16},{24,20},{28,24},{5,1},{9,5},{13... | collective-permute-start | bytes 786440 | tf_op jit(solution)/shard_map/ppermute | solution.py:272
  144.7 2.8 %collective-permute-done.26 = bf16[64,1024]{1,0:T(8,128)(2,1)S(1)} collective-permute-done((bf16[64,1024]{1,0:T(8,128)(2,1)S(1)}, bf16[64,1024]{1,0:T(8,128)(2,1)S(1)}, u32[]{:S(2)}, u32[]{:S(2)}) %collective-permute-start.26) | collective-permute-done | bytes 131104 | tf_op jit(solution)/shard_map/ppermute | solution.py:277
  148.2 5.5 %collective-permute-done.17 = bf16[128,1024]{1,0:T(8,128)(2,1)} collective-permute-done((bf16[128,1024]{1,0:T(8,128)(2,1)}, bf16[128,1024]{1,0:T(8,128)(2,1)}, u32[]{:S(2)}, u32[]{:S(2)}) %collective-permute-start.17) | collective-permute-done | bytes 262176 | tf_op jit(solution)/shard_map/ppermute | solution.py:282
  158.5 4.2 %convolution_multiply_fusion = f32[512,1024]{1,0:T(8,128)} fusion(bf16[1024,512]{1,0:T(8,128)(2,1)S(1)} %bitcast.32, bf16[1024,1024]{1,0:T(8,128)(2,1)} %all-gather.2.cloned.1.call-done), kind=kOutput, calls=%fused_computation | convolution fusion | flops 1074266112 | bytes 5242880 | tf_op jit(solution)/shard_map/dot_general | solution.py:568
  (164 shorter events, 59.9 us)
Async XLA Ops:
  7.2 151.4 %all-gather.2.cloned.1.call-start = ((), (), s32[]{:S(2)}) async-start(), calls=%async_computation.1 | async-start | bytes 2359296 | tf_op jit(solution)/shard_map/all_gather | solution.py:452
  7.3 52.4 %collective-permute-start.7 = (bf16[512,1024]{1,0:T(8,128)(2,1)}, bf16[512,1024]{1,0:T(8,128)(2,1)S(1)}, u32[]{:S(2)}, u32[]{:S(2)}) collective-permute-start(bf16[512,1024]{1,0:T(8,128)(2,1)} %rest_0_.3), channel_id=1, source_target_pairs={{0,8},{4,12},{8,0},{12,4},{16,24},{20,28},{24,16},{28,20},{1,9},{5... | collective-permute-start | bytes 3145736 | tf_op jit(solution)/shard_map/ppermute | solution.py:277
  9.4 50.3 %collective-permute-start.8 = (bf16[512,1024]{1,0:T(8,128)(2,1)}, bf16[512,1024]{1,0:T(8,128)(2,1)S(1)}, u32[]{:S(2)}, u32[]{:S(2)}) collective-permute-start(bf16[512,1024]{1,0:T(8,128)(2,1)} %rest_0_.3), channel_id=1, source_target_pairs={{0,16},{4,20},{8,24},{12,28},{16,0},{20,4},{24,8},{28,12},{1,17},{... | collective-permute-start | bytes 3145736 | tf_op jit(solution)/shard_map/ppermute | solution.py:277
  11.7 23.7 %collective-permute-start = (bf16[128,1024]{1,0:T(8,128)(2,1)S(1)}, bf16[128,1024]{1,0:T(8,128)(2,1)S(1)}, u32[]{:S(2)}, u32[]{:S(2)}) collective-permute-start(bf16[128,1024]{1,0:T(8,128)(2,1)S(1)} %multiply_convert_fusion.product), channel_id=1, source_target_pairs={{0,4},{4,8},{8,12},{12,16},{16,20},{20,24},{24,28},{1,5},{5,9},{9,... | collective-permute-start | bytes 786440 | tf_op jit(solution)/shard_map/ppermute | solution.py:272
  15.0 20.4 %collective-permute-start.1 = (bf16[128,1024]{1,0:T(8,128)(2,1)}, bf16[128,1024]{1,0:T(8,128)(2,1)S(1)}, u32[]{:S(2)}, u32[]{:S(2)}) collective-permute-start(bf16[128,1024]{1,0:T(8,128)(2,1)} %param.28), channel_id=1, source_target_pairs={{0,1},{1,0},{2,3},{3,2},{4,5},{5,4},{6,7},{7,6},{8,9},{9,8},{10,11... | collective-permute-start | bytes 786440 | tf_op jit(solution)/shard_map/ppermute | solution.py:282
  52.1 19.7 %collective-permute-start.2 = (bf16[128,1024]{1,0:T(8,128)(2,1)}, bf16[128,1024]{1,0:T(8,128)(2,1)}, u32[]{:S(2)}, u32[]{:S(2)}) collective-permute-start(bf16[128,1024]{1,0:T(8,128)(2,1)} %param.28), channel_id=1, source_target_pairs={{0,2},{1,3},{2,0},{3,1},{4,6},{5,7},{6,4},{7,5},{8,10},{9,11},{10,... | collective-permute-start | bytes 786440 | tf_op jit(solution)/shard_map/ppermute | solution.py:282
  54.7 18.5 %collective-permute-start.3 = (bf16[128,1024]{1,0:T(8,128)(2,1)}, bf16[128,1024]{1,0:T(8,128)(2,1)}, u32[]{:S(2)}, u32[]{:S(2)}) collective-permute-start(bf16[128,1024]{1,0:T(8,128)(2,1)} %param.28), channel_id=1, source_target_pairs={{0,3},{1,2},{2,1},{3,0},{4,7},{5,6},{6,5},{7,4},{8,11},{9,10},{10,... | collective-permute-start | bytes 786440 | tf_op jit(solution)/shard_map/ppermute | solution.py:282
  55.8 35.0 %collective-permute-start.9 = (bf16[512,1024]{1,0:T(8,128)(2,1)S(1)}, bf16[512,1024]{1,0:T(8,128)(2,1)}, u32[]{:S(2)}, u32[]{:S(2)}) collective-permute-start(bf16[512,1024]{1,0:T(8,128)(2,1)S(1)} %copy-done), channel_id=1, source_target_pairs={{0,4},{4,0},{8,12},{12,8},{16,20},{20,16},{24,28},{28,24},{1,5},{5... | collective-permute-start | bytes 3145736 | tf_op jit(solution)/shard_map/ppermute | solution.py:267
  59.6 31.1 %collective-permute-start.10 = (bf16[512,1024]{1,0:T(8,128)(2,1)S(1)}, bf16[512,1024]{1,0:T(8,128)(2,1)}, u32[]{:S(2)}, u32[]{:S(2)}) collective-permute-start(bf16[512,1024]{1,0:T(8,128)(2,1)S(1)} %collective-permute-done.7.rest_1_), channel_id=1, source_target_pairs={{0,4},{4,0},{8,12},{12,8},{16,20},{20,16},{24,28},{28,24},{1,5},{5... | collective-permute-start | bytes 3145736 | tf_op jit(solution)/shard_map/ppermute | solution.py:267
  59.7 31.0 %collective-permute-start.11 = (bf16[512,1024]{1,0:T(8,128)(2,1)S(1)}, bf16[512,1024]{1,0:T(8,128)(2,1)}, u32[]{:S(2)}, u32[]{:S(2)}) collective-permute-start(bf16[512,1024]{1,0:T(8,128)(2,1)S(1)} %collective-permute-done.8.rest_2_), channel_id=1, source_target_pairs={{0,4},{4,0},{8,12},{12,8},{16,20},{20,16},{24,28},{28,24},{1,5},{5... | collective-permute-start | bytes 3145736 | tf_op jit(solution)/shard_map/ppermute | solution.py:267
  71.9 11.7 %collective-permute-start.12 = (bf16[256,1024]{1,0:T(8,128)(2,1)}, bf16[256,1024]{1,0:T(8,128)(2,1)}, u32[]{:S(2)}, u32[]{:S(2)}) collective-permute-start(bf16[256,1024]{1,0:T(8,128)(2,1)} %slice.6), channel_id=1, source_target_pairs={{0,8},{4,12},{8,0},{12,4},{16,24},{20,28},{24,16},{28,20},{1,9},{5... | collective-permute-start | bytes 1572872 | tf_op jit(solution)/shard_map/ppermute | solution.py:277
  73.1 13.8 %collective-permute-start.13 = (bf16[256,1024]{1,0:T(8,128)(2,1)}, bf16[256,1024]{1,0:T(8,128)(2,1)}, u32[]{:S(2)}, u32[]{:S(2)}) collective-permute-start(bf16[256,1024]{1,0:T(8,128)(2,1)} %slice.7), channel_id=1, source_target_pairs={{0,16},{4,20},{8,24},{12,28},{16,0},{20,4},{24,8},{28,12},{1,17},{... | collective-permute-start | bytes 1572872 | tf_op jit(solution)/shard_map/ppermute | solution.py:277
  83.6 15.3 %collective-permute-start.14 = (bf16[256,1024]{1,0:T(8,128)(2,1)}, bf16[256,1024]{1,0:T(8,128)(2,1)S(1)}, u32[]{:S(2)}, u32[]{:S(2)}) collective-permute-start(bf16[256,1024]{1,0:T(8,128)(2,1)} %collective-permute-done.12.rest_0_), channel_id=1, source_target_pairs={{0,4},{4,0},{8,12},{12,8},{16,20},{20,16},{24,28},{28,24},{1,5},{5... | collective-permute-start | bytes 1572872 | tf_op jit(solution)/shard_map/ppermute | solution.py:267
  86.9 12.0 %collective-permute-start.15 = (bf16[256,1024]{1,0:T(8,128)(2,1)}, bf16[256,1024]{1,0:T(8,128)(2,1)S(1)}, u32[]{:S(2)}, u32[]{:S(2)}) collective-permute-start(bf16[256,1024]{1,0:T(8,128)(2,1)} %collective-permute-done.13.rest_1_), channel_id=1, source_target_pairs={{0,4},{4,0},{8,12},{12,8},{16,20},{20,16},{24,28},{28,24},{1,5},{5... | collective-permute-start | bytes 1572872 | tf_op jit(solution)/shard_map/ppermute | solution.py:267
  103.8 7.5 %collective-permute-start.22 = (f32[16,1024]{1,0:T(8,128)S(1)}, f32[16,1024]{1,0:T(8,128)S(1)}, u32[]{:S(2)}, u32[]{:S(2)}) collective-permute-start(f32[16,1024]{1,0:T(8,128)S(1)} %add_select_fusion.1), channel_id=1, source_target_pairs={{0,24},{4,28},{8,16},{12,20},{16,8},{20,12},{24,0},{28,4},{1,25},{... | collective-permute-start | bytes 196616 | tf_op jit(solution)/shard_map/ppermute | solution.py:277
  104.5 6.9 %collective-permute-start.21 = (f32[16,1024]{1,0:T(8,128)S(1)}, f32[16,1024]{1,0:T(8,128)S(1)}, u32[]{:S(2)}, u32[]{:S(2)}) collective-permute-start(f32[16,1024]{1,0:T(8,128)S(1)} %add_select_fusion.1), channel_id=1, source_target_pairs={{0,16},{4,20},{8,24},{12,28},{16,0},{20,4},{24,8},{28,12},{1,17},{... | collective-permute-start | bytes 196616 | tf_op jit(solution)/shard_map/ppermute | solution.py:277
  117.9 25.5 %all-to-all-start = ((bf16[4,128,1024]{2,1,0:T(8,128)(2,1)}), bf16[4,128,1024]{2,1,0:T(8,128)(2,1)}, u32[]{:S(2)}, u32[]{:S(2)}) async-start(bf16[4,128,1024]{2,1,0:T(8,128)(2,1)} %bitcast.33), calls=%async_computation | async-start | bytes 2097152 | tf_op jit(solution)/shard_map/all_to_all | solution.py:288
  124.1 17.0 %collective-permute-start.25 = (bf16[64,1024]{1,0:T(8,128)(2,1)}, bf16[64,1024]{1,0:T(8,128)(2,1)}, u32[]{:S(2)}, u32[]{:S(2)}) collective-permute-start(bf16[64,1024]{1,0:T(8,128)(2,1)} %fusion), channel_id=1, source_target_pairs={{0,8},{4,12},{8,0},{12,4},{16,24},{20,28},{24,16},{28,20},{1,9},{5... | collective-permute-start | bytes 393224 | tf_op jit(solution)/shard_map/ppermute | solution.py:277
  125.5 22.5 %collective-permute-start.18 = (bf16[128,1024]{1,0:T(8,128)(2,1)}, bf16[128,1024]{1,0:T(8,128)(2,1)}, u32[]{:S(2)}, u32[]{:S(2)}) collective-permute-start(bf16[128,1024]{1,0:T(8,128)(2,1)} %copy-done.37), channel_id=1, source_target_pairs={{0,3},{1,2},{2,1},{3,0},{4,7},{5,6},{6,5},{7,4},{8,11},{9,10},{10,... | collective-permute-start | bytes 786440 | tf_op jit(solution)/shard_map/ppermute | solution.py:282
  129.8 23.9 %collective-permute-start.17 = (bf16[128,1024]{1,0:T(8,128)(2,1)}, bf16[128,1024]{1,0:T(8,128)(2,1)}, u32[]{:S(2)}, u32[]{:S(2)}) collective-permute-start(bf16[128,1024]{1,0:T(8,128)(2,1)} %copy-done.36), channel_id=1, source_target_pairs={{0,2},{1,3},{2,0},{3,1},{4,6},{5,7},{6,4},{7,5},{8,10},{9,11},{10,... | collective-permute-start | bytes 786440 | tf_op jit(solution)/shard_map/ppermute | solution.py:282
  133.7 20.1 %collective-permute-start.16 = (bf16[128,1024]{1,0:T(8,128)(2,1)}, bf16[128,1024]{1,0:T(8,128)(2,1)}, u32[]{:S(2)}, u32[]{:S(2)}) collective-permute-start(bf16[128,1024]{1,0:T(8,128)(2,1)} %copy-done.35), channel_id=1, source_target_pairs={{0,1},{1,0},{2,3},{3,2},{4,5},{5,4},{6,7},{7,6},{8,9},{9,8},{10,11... | collective-permute-start | bytes 786440 | tf_op jit(solution)/shard_map/ppermute | solution.py:282
  138.1 17.7 %collective-permute-start.23 = (bf16[128,1024]{1,0:T(8,128)(2,1)}, bf16[128,1024]{1,0:T(8,128)(2,1)S(1)}, u32[]{:S(2)}, u32[]{:S(2)}) collective-permute-start(bf16[128,1024]{1,0:T(8,128)(2,1)} %get-tuple-element.72), channel_id=1, source_target_pairs={{4,0},{8,4},{12,8},{16,12},{20,16},{24,20},{28,24},{5,1},{9,5},{13... | collective-permute-start | bytes 786440 | tf_op jit(solution)/shard_map/ppermute | solution.py:272
  147.6 10.9 %collective-permute-start.28 = (bf16[512,512]{1,0:T(8,128)(2,1)S(1)}, bf16[512,512]{1,0:T(8,128)(2,1)S(1)}, u32[]{:S(2)}, u32[]{:S(2)}) collective-permute-start(bf16[512,512]{1,0:T(8,128)(2,1)S(1)} %get-tuple-element.80), channel_id=1, source_target_pairs={{0,4},{4,0},{8,12},{12,8},{16,20},{20,16},{24,28},{28,24},{1,5},{5... | collective-permute-start | bytes 1572872 | tf_op jit(solution)/shard_map/ppermute | solution.py:267
  148.0 9.6 %collective-permute-start.27 = (f32[64,1024]{1,0:T(8,128)S(1)}, f32[64,1024]{1,0:T(8,128)S(1)}, u32[]{:S(2)}, u32[]{:S(2)}) collective-permute-start(f32[64,1024]{1,0:T(8,128)S(1)} %add_multiply_fusion), channel_id=1, source_target_pairs={{0,4},{4,0},{8,12},{12,8},{16,20},{20,16},{24,28},{28,24},{1,5},{5... | collective-permute-start | bytes 786440 | tf_op jit(solution)/shard_map/ppermute | solution.py:267
  (48 other events, 338.9 us)
Sparse Core Ops, SparseCore 0:
  82.6 34.7 all-gather.1

commit v3 on v1

v3 whole, which is shorter than its diff:
```python
import functools
import math

import jax
import jax.numpy as jnp
import ml_dtypes
import numpy as np
from jax import lax
from jax.experimental import pallas as pl
from jax.experimental.pallas import tpu as pltpu
from jax.sharding import PartitionSpec as P

F32 = jnp.float32
BF16 = jnp.bfloat16
TILE = 256
GROUP = 8
SWAPS = 3


def split_parts(matrix):
    high = matrix.astype(ml_dtypes.bfloat16)
    low = (matrix - high.astype(np.float64)).astype(ml_dtypes.bfloat16)
    return high, low


def two_fold(matrix):
    high, low = split_parts(matrix)
    return np.concatenate([high, low], axis=1)


def three_fold(matrix):
    high, low = split_parts(matrix)
    return np.concatenate([high, low, high], axis=1)


@functools.lru_cache(maxsize=None)
def dft_tables(rows):
    size = 2 * rows
    angle = 2.0 * np.pi * (np.arange(rows)[:, None] + 0.5) * np.arange(size)[None, :] / size
    ahead = np.concatenate([np.cos(angle), -np.sin(angle)], axis=0)
    back = ahead.T * (2.0 / size)
    signed = np.concatenate([back[:rows], -back[rows:]], axis=0)
    lags = back[rows - np.arange(rows)]
    return {"ahead": two_fold(ahead), "back": three_fold(signed), "lags": three_fold(lags)}


def half_table(ahead):
    rows = ahead.shape[0] // 2
    high, low = ahead[:, :rows], ahead[:, 2 * rows : 3 * rows]
    return high, low


def apply2(table, x):
    return jnp.dot(table, jnp.concatenate([x, x], axis=0), preferred_element_type=F32)


def apply3(table, x):
    high = x.astype(BF16)
    low = (x - high.astype(F32)).astype(BF16)
    return jnp.dot(table, jnp.concatenate([high, high, low], axis=0), preferred_element_type=F32)


def to_spectrum(ahead, x):
    high, low = half_table(ahead)
    return apply3(jnp.concatenate([high, low, high], axis=1), x)


def to_spectrum_exact(ahead, x):
    return apply2(jnp.concatenate(half_table(ahead), axis=1), x)


def times(x, y):
    half = x.shape[0] // 2
    xr, xi, yr, yi = x[:half], x[half:], y[:half], y[half:]
    return jnp.concatenate([xr * yr - xi * yi, xr * yi + xi * yr], axis=0)


def times_conj(x, y):
    half = x.shape[0] // 2
    xr, xi, yr, yi = x[:half], x[half:], y[:half], y[half:]
    return jnp.concatenate([xr * yr + xi * yi, xi * yr - xr * yi], axis=0)


def group_places(columns):
    return lax.broadcasted_iota(jnp.int32, (GROUP, columns), 0).astype(F32)


def spread_modes(rate, weight, rows, shift, backward):
    columns = rate.shape[1]
    places = group_places(columns)
    if backward:
        places = (GROUP - 1.0) - places
    count = rows // GROUP
    order = range(count - 1, -1, -1) if backward else range(count)
    sums = [None] * count
    for m in range(rate.shape[0]):
        rate_m = rate[m : m + 1]
        current = weight[m : m + 1] * jnp.exp(-rate_m * (places + shift))
        stride = jnp.broadcast_to(jnp.exp(-rate_m * GROUP), current.shape)
        for step, g in enumerate(order):
            sums[g] = current if sums[g] is None else sums[g] + current
            if step < count - 1:
                current = current * stride
    return jnp.concatenate(sums, axis=0)


def fold_modes(signal, rate, backward):
    columns = rate.shape[1]
    places = group_places(columns)
    if not backward:
        places = (GROUP - 1.0) - places
    count = signal.shape[0] // GROUP
    order = range(count - 1, -1, -1) if backward else range(count)
    found = []
    for m in range(rate.shape[0]):
        rate_m = rate[m : m + 1]
        stride = jnp.broadcast_to(jnp.exp(-rate_m * GROUP), (GROUP, columns))
        running = None
        for g in order:
            piece = signal[g * GROUP : (g + 1) * GROUP]
            running = piece if running is None else running * stride + piece
        found.append(jnp.sum(running * jnp.exp(-rate_m * places), axis=0, keepdims=True))
    return jnp.concatenate(found, axis=0)


def spectra_body(taps, rate, coef, skip, ahead, mr_spec, li_spec):
    rows = taps.shape[0]
    table = ahead[...]
    mr_spec[...] = to_spectrum(table, taps[...])
    kernel = spread_modes(rate[...], coef[...], rows, 0.0, False)
    first = lax.broadcasted_iota(jnp.int32, kernel.shape, 0) == 0
    kernel = kernel + jnp.where(first, skip[...], 0.0)
    li_spec[...] = to_spectrum(table, kernel)


def short_body(before, product, query, key, mr_spec, rate, ahead, back, spec, conv, mixed, signal, ends):
    rows = product.shape[0]
    x = jnp.concatenate([before[...], product[...]], axis=0)
    found = apply2(ahead[...], x)
    spec[...] = found
    filtered = -apply3(back[rows:], times(found, mr_spec[...]))
    conv[...] = filtered
    mixed_rows = (query[...].astype(F32) * filtered).astype(BF16)
    mixed[...] = mixed_rows
    rounded = (key[...].astype(F32) * mixed_rows.astype(F32)).astype(BF16)
    signal[...] = rounded
    ends[...] = fold_modes(rounded.astype(F32), rate[...], False)


def inner_body(signal, li_spec, ahead, back, inner):
    rows = signal.shape[0]
    inner[...] = apply3(back[:rows], times(to_spectrum_exact(ahead[...], signal[...]), li_spec[...]))


def long_body(inner, query, rate, coef, entering, li_out, mixed):
    rows = inner.shape[0]
    total = inner[...] + spread_modes(rate[...], coef[...] * entering[...], rows, 1.0, False)
    li_out[...] = total
    mixed[...] = (query[...].astype(F32) * total).astype(BF16)


def split_body(width, count, starts, *rest):
    pieces, near, shares = rest[:count], rest[count], rest[count + 1 : -1]
    far = rest[-1]
    for r, piece in enumerate(pieces):
        for k in range(piece.shape[1] // (2 * width)):
            place = pl.multiple_of(starts[r], 128) + k * width
            near[:, pl.ds(place, width)] = piece[:, pl.ds(pl.multiple_of(starts[count], 128) + 2 * k * width, width)]
            far[:, pl.ds(place, width)] = piece[:, pl.ds(pl.multiple_of(starts[count + 1], 128) + 2 * k * width, width)]
    part = far.shape[1] // len(shares)
    for k, share in enumerate(shares):
        share[...] = far[:, k * part : (k + 1) * part]


def grad_share_body(near, far, weight, own, sent):
    own[...] = jnp.dot(near[...], weight[...], preferred_element_type=F32)
    sent[...] = jnp.dot(far[...], weight[...], preferred_element_type=F32).astype(BF16)


def grad_gate_body(own, arrived, query, rate, grad_mixed, grad_out, ends):
    total = own[...] + arrived[...].astype(F32)
    grad_mixed[...] = total
    gated = total * query[...].astype(F32)
    grad_out[...] = gated
    ends[...] = fold_modes(gated, rate[...], True)


def out_share_body(starts, near, far, weight, *rest):
    parts, whole = rest[:-1], rest[-1]
    rows = near.shape[0]
    contract = (((1,), (1,)), ((), ()))
    whole[:rows] = lax.dot_general(near[...], weight[...], contract, preferred_element_type=F32).astype(BF16)
    whole[rows:] = lax.dot_general(far[...], weight[...], contract, preferred_element_type=F32).astype(BF16)
    width = parts[0].shape[1]
    for r, part in enumerate(parts):
        part[...] = whole[:, pl.ds(pl.multiple_of(starts[r], 128), width)]


def grad_inner_body(grad_out, li_spec, ahead, back, inner):
    rows = grad_out.shape[0]
    inner[...] = apply3(back[:rows], times_conj(to_spectrum(ahead[...], grad_out[...]), li_spec[...]))


def grad_long_body(
    inner, rate, coef, entering, mixed_mr, key_li, query_mr, conv, spec, ahead, lags,
    grad_key_li, grad_query_mr, grad_spec, taps,
):
    rows = inner.shape[0]
    grad_input = inner[...] + spread_modes(rate[...], coef[...] * entering[...], rows, 1.0, True)
    grad_key_li[...] = grad_input * mixed_mr[...].astype(F32)
    grad_mixed_mr = grad_input * key_li[...].astype(F32)
    grad_query_mr[...] = grad_mixed_mr * conv[...]
    grad_conv = grad_mixed_mr * query_mr[...].astype(F32)
    found = to_spectrum(ahead[...], grad_conv)
    grad_spec[...] = found
    taps[...] = apply3(lags[...], times_conj(spec[...], found))


def grad_taps_body(grad_spec, mr_spec, back, own_product, prev_product):
    rows = own_product.shape[0]
    products = apply3(back[...], times_conj(grad_spec[...], mr_spec[...]))
    own_product[...] = products[:rows]
    prev_product[...] = products[rows:].astype(BF16)


def grad_product_body(own, arrived, key, value, grad_key, grad_value):
    total = own[...] + arrived[...].astype(F32)
    grad_key[...] = total * value[...].astype(F32)
    grad_value[...] = total * key[...].astype(F32)


def run(body, columns, inputs, outputs, flops):
    tile = min(TILE, columns)
    in_specs = []
    moved = 0
    for kind, array in inputs:
        if kind == "tile":
            in_specs.append(pl.BlockSpec((array.shape[0], tile), lambda c: (0, c)))
        elif kind == "whole":
            in_specs.append(pl.BlockSpec(array.shape, lambda c: (0, 0)))
        else:
            in_specs.append(pl.BlockSpec(memory_space=pltpu.SMEM))
        moved += math.prod(array.shape) * array.dtype.itemsize
    for rows, dtype in outputs:
        moved += rows * columns * jnp.dtype(dtype).itemsize
    return pl.pallas_call(
        body,
        grid=(columns // tile,),
        in_specs=in_specs,
        out_specs=[pl.BlockSpec((rows, tile), lambda c: (0, c)) for rows, _ in outputs],
        out_shape=[jax.ShapeDtypeStruct((rows, columns), dtype) for rows, dtype in outputs],
        compiler_params=pltpu.CompilerParams(vmem_limit_bytes=32 * 1024 * 1024),
        cost_estimate=pl.CostEstimate(flops=flops, bytes_accessed=moved, transcendentals=0),
    )(*[array for _, array in inputs])


def run_once(body, inputs, outputs, scratch, flops):
    moved = sum(math.prod(array.shape) * array.dtype.itemsize for array in inputs)
    return pl.pallas_call(
        body,
        in_specs=[pl.BlockSpec(memory_space=pltpu.SMEM)]
        + [pl.BlockSpec(memory_space=pltpu.VMEM)] * (len(inputs) - 1),
        out_specs=[pl.BlockSpec(memory_space=pltpu.VMEM)] * len(outputs),
        out_shape=[jax.ShapeDtypeStruct(shape, dtype) for shape, dtype in outputs],
        scratch_shapes=scratch,
        compiler_params=pltpu.CompilerParams(vmem_limit_bytes=32 * 1024 * 1024),
        cost_estimate=pl.CostEstimate(flops=flops, bytes_accessed=moved, transcendentals=0),
    )(*inputs)


def core_swap(x):
    size = lax.axis_size("ctx")
    return lax.ppermute(x, "ctx", [(i, i ^ 1) for i in range(size)])


def shifted(x, by):
    size = lax.axis_size("ctx")
    return lax.ppermute(x, "ctx", [(i, i + by) for i in range(size) if 0 <= i + by < size])


def chip_swap(x, by):
    size = lax.axis_size("ctx")
    return lax.ppermute(x, "ctx", [(i, i ^ (2 * by)) for i in range(size)])


def line_swap(x, by):
    size = lax.axis_size("fsdp")
    return lax.ppermute(x, "fsdp", [(i, i ^ by) for i in range(size)])


def plane_trade(x):
    return lax.all_to_all(x, "ctx", 0, 0, axis_index_groups=plane_groups(), tiled=True)


def columns_to_rows(x, count):
    return jnp.concatenate(jnp.split(x, count, axis=1), axis=0)


def plane_groups():
    size = lax.axis_size("ctx")
    return [list(range(core, size, 2)) for core in range(2)]


def after(x, *others):
    return lax.optimization_barrier((x,) + others)[0]


def doubling_factors(rate, rows, here, backward):
    factors = []
    by = 1
    while by < lax.axis_size("ctx"):
        offset = here & (by - 1)
        if backward:
            offset = by - 1 - offset
        factors.append((jnp.exp(-rate * (rows * offset).astype(F32)), jnp.exp(-rate * float(rows * by))))
        by *= 2
    return factors


def entering_state(ends, factors, here, backward):
    size = lax.axis_size("ctx")
    total, entering = ends, jnp.zeros_like(ends)
    by = 1
    for to_here, across in factors:
        arrived = lax.ppermute(total, "ctx", [(i, i ^ by) for i in range(size)])
        later = ((here & by) != 0) != backward
        entering = entering + jnp.where(later, to_here * arrived, 0.0)
        total = jnp.where(later, across * arrived + total, across * total + arrived)
        by *= 2
    return entering


def direct_factors(rate, rows, chip, backward):
    factors = [jnp.exp(-rate * float(rows))]
    for s in range(1, lax.axis_size("ctx") // 2):
        gap = (chip ^ s) - chip - 1 if backward else chip - (chip ^ s) - 1
        weight = jnp.exp(-rate * (2 * rows * jnp.maximum(gap, 0)).astype(F32))
        factors.append(jnp.where(gap >= 0, weight, 0.0))
    return factors


def entering_direct(ends, factors, here, backward):
    block = factors[0]
    later_core = ((here & 1) != 0) != backward
    sibling = core_swap(ends)
    total = jnp.where(later_core, block * sibling + ends, block * ends + sibling)
    entering = jnp.zeros_like(ends)
    for s, weight in enumerate(factors[1:], 1):
        entering = entering + weight * chip_swap(total, s)
    return jnp.where(later_core, block * entering + sibling, entering)


def shards(
    query_mr,
    key_mr,
    value_mr,
    query_li,
    key_li,
    mr_taps,
    li_time,
    li_residue,
    li_skip,
    out_weight,
    cotangent,
):
    rows, columns = query_mr.shape
    ctx_count = lax.axis_size("ctx")
    line_count = lax.axis_size("fsdp")
    chips = ctx_count // 2
    here = lax.axis_index("ctx")
    core = here % 2
    line = lax.axis_index("fsdp")
    grad_scale = 1.0 / math.sqrt(rows * ctx_count)
    tables = {name: jnp.asarray(table) for name, table in dft_tables(rows).items()}
    width = out_weight.shape[0]
    pass_flops = 2 * (2 * rows) * (2 * rows) * columns

    def tile(x):
        return ("tile", x)

    def table(name):
        return ("whole", tables[name])

    mr_product = (key_mr.astype(F32) * value_mr.astype(F32)).astype(BF16)
    before = shifted(mr_product, 1)
    weight_rows = lax.all_gather(out_weight, "ctx", axis=0, tiled=True, axis_index_groups=plane_groups())
    cot_line = [(line, cotangent)]
    for r in range(1, line_count):
        cot_line.append((line ^ r, line_swap(cotangent, r)))

    rate = 1.0 / li_time
    coef = li_residue * jnp.sqrt(-jnp.expm1(-2.0 * rate))
    ahead_factors, back_factors = lax.optimization_barrier(
        (doubling_factors(rate, rows, here, False), direct_factors(rate, rows, here // 2, True))
    )
    mr_spec, li_spec = run(
        spectra_body,
        columns,
        [tile(mr_taps), tile(rate), tile(coef), tile(li_skip[None, :]), table("ahead")],
        [(2 * rows, F32), (2 * rows, F32)],
        3 * pass_flops,
    )
    spec, mr_conv, mixed_mr, li_input, ends = run(
        short_body,
        columns,
        [
            tile(before),
            tile(mr_product),
            tile(query_mr),
            tile(key_li),
            tile(mr_spec),
            tile(rate),
            table("ahead"),
            table("back"),
        ],
        [(2 * rows, F32), (rows, F32), (rows, BF16), (rows, BF16), (rate.shape[0], F32)],
        4 * pass_flops,
    )
    entering = entering_state(ends, ahead_factors, here, False)
    (li_inner,) = run(
        inner_body,
        columns,
        [tile(li_input), tile(li_spec), table("ahead"), table("back")],
        [(rows, F32)],
        3 * pass_flops,
    )
    li_out, mixed_li = run(
        long_body,
        columns,
        [tile(li_inner), tile(query_li), tile(rate), tile(coef), tile(entering)],
        [(rows, F32), (rows, BF16)],
        pass_flops,
    )

    other_mixed = core_swap(mixed_li)
    mixed_all = lax.all_gather(mixed_li, "ctx", axis=0, tiled=True)

    part_width = chips * width // line_count
    near, *to_far = run_once(
        functools.partial(split_body, width, line_count),
        [jnp.stack([index * part_width for index, _ in cot_line] + [core * width, (1 - core) * width])]
        + [piece for _, piece in cot_line],
        [((rows, chips * width), BF16)] + [((rows, chips * width // 4), BF16)] * 4,
        [pltpu.VMEM((rows, chips * width), BF16)],
        0,
    )
    far_parts = [core_swap(to_far[0]), core_swap(to_far[1])]
    for part in to_far[2:]:
        far_parts.append(core_swap(after(part, far_parts[-1])))
    far = jnp.concatenate(far_parts, axis=1)
    near = after(near, mixed_li)
    cot_rows = plane_trade(
        columns_to_rows(
            jnp.where(core == 0, jnp.concatenate([near, far], axis=0), jnp.concatenate([far, near], axis=0)), chips
        )
    )

    share_flops = 4 * rows * columns * chips * width
    own_share, sent_share = run(
        grad_share_body,
        columns,
        [("whole", near), ("whole", far), tile(weight_rows)],
        [(rows, F32), (rows, BF16)],
        share_flops,
    )
    arrived_share = core_swap(sent_share)
    out_parts = run_once(
        out_share_body,
        [
            jnp.stack([(line ^ r) * part_width for r in range(line_count)]),
            after(mixed_li, sent_share),
            other_mixed,
            weight_rows,
        ],
        [((2 * rows, part_width), BF16)] * line_count,
        [pltpu.VMEM((2 * rows, chips * width), BF16)],
        share_flops,
    )
    out_sum = out_parts[0].astype(F32)
    for r in range(1, line_count):
        out_sum = out_sum + line_swap(out_parts[r], r).astype(F32)
    near_out, far_out = out_sum[:rows], core_swap(out_sum[rows:])
    output = jnp.where(
        core == 0, jnp.concatenate([near_out, far_out], axis=1), jnp.concatenate([far_out, near_out], axis=1)
    )

    grad_mixed, grad_li_out, back_ends = run(
        grad_gate_body,
        columns,
        [tile(after(own_share, out_parts[0])), tile(arrived_share), tile(query_li), tile(rate)],
        [(rows, F32), (rows, F32), (rate.shape[0], F32)],
        rows * columns,
    )
    back_entering = entering_direct(back_ends, back_factors, here, True)
    (grad_inner,) = run(
        grad_inner_body,
        columns,
        [tile(grad_li_out), tile(li_spec), table("ahead"), table("back")],
        [(rows, F32)],
        3 * pass_flops,
    )
    grad_query_li = grad_mixed * li_out
    grad_key_li, grad_query_mr, grad_spec, tap_partial = run(
        grad_long_body,
        columns,
        [
            tile(grad_inner),
            tile(rate),
            tile(coef),
            tile(back_entering),
            tile(mixed_mr),
            tile(key_li),
            tile(query_mr),
            tile(mr_conv),
            tile(spec),
            table("ahead"),
            table("lags"),
        ],
        [(rows, F32), (rows, F32), (2 * rows, F32), (rows, F32)],
        4 * pass_flops,
    )
    own_product, prev_product = run(
        grad_taps_body,
        columns,
        [tile(grad_spec), tile(mr_spec), table("back")],
        [(rows, F32), (rows, BF16)],
        3 * pass_flops,
    )
    arrived = shifted(prev_product, -1)
    grad_key_mr, grad_value_mr = run(
        grad_product_body,
        columns,
        [tile(own_product), tile(arrived), tile(key_mr), tile(value_mr)],
        [(rows, F32), (rows, F32)],
        rows * columns,
    )

    tap_half = tap_partial.shape[0] // 2
    halves = tap_partial.reshape(2, tap_half, columns)
    own_half = lax.dynamic_index_in_dim(halves, core, 0, keepdims=False)
    far_half = lax.dynamic_index_in_dim(halves, 1 - core, 0, keepdims=False)
    plane_half = own_half + core_swap(far_half)
    by = 1
    while by < chips:
        sent = plane_half.astype(BF16)
        plane_half = sent.astype(F32) + chip_swap(sent, by).astype(F32)
        by *= 2
    plane_half = plane_half * grad_scale
    other_half = core_swap(plane_half)
    grad_taps = jnp.where(
        core == 0,
        jnp.concatenate([plane_half, other_half], axis=0),
        jnp.concatenate([other_half, plane_half], axis=0),
    )

    grad_weight = (
        lax.dot_general(cot_rows, mixed_all, (((0,), (0,)), ((), ())), preferred_element_type=F32) * grad_scale
    )
    return (
        output,
        grad_query_mr,
        grad_key_mr,
        grad_value_mr,
        grad_query_li,
        grad_key_li,
        grad_taps,
        grad_weight,
    )


def solution(mesh):
    rows = P("ctx", "fsdp")
    channels = P(None, "fsdp")
    return jax.shard_map(
        shards,
        mesh=mesh,
        in_specs=(rows,) * 5 + (channels,) * 3 + (P("fsdp"),) + (rows,) * 2,
        out_specs=(rows,) * 6 + (channels, rows),
        check_vma=False,
    )
```

time: 169 us -> 150 us (0.89)
  between operations: 1.22 us -> 14.7 us
  blocking collectives: 11.2 us -> 0 us
  Pallas kernels: 18.9 us -> 30 us
  waiting for transfers between devices: 44.2 us -> 33.8 us
  matrix products: 14 us -> 4.59 us
  starting transfers between devices: 45.5 us -> 36.4 us
  local copies, waits for them, and re-layouts: 15.5 us -> 12.7 us
    all_to_all x6 -> x1, waiting for transfers between devices: 35.1 us -> 0.01 us  [plane_trade(): lax.all_to_all(x, 'ctx', 0, 0, axis_index_groups=plane_groups(), tiled=True)]
    ppermute x0 -> x11, waiting for transfers between devices: none -> 23.7 us  [the longest x6 23.7 us: line_swap(): return lax.ppermute(x, 'fsdp', [(i, i ^ by) for i in range(size)])]
    all_to_all x6 -> x1, starting transfers between devices: 26.1 us -> 4.39 us  [plane_trade(): lax.all_to_all(x, 'ctx', 0, 0, axis_index_groups=plane_groups(), tiled=True)]
    ppermute x0 -> x11, starting transfers between devices: none -> 13.9 us  [the longest x6 8.86 us: line_swap(): return lax.ppermute(x, 'fsdp', [(i, i ^ by) for i in range(size)])]
    all_to_all x1 -> x0, blocking collectives: 11.2 us -> none  [plane_trade(): return lax.all_to_all(x, 'ctx', 0, 0, axis_index_groups=groups, tiled=True)]
    dot_general x4 -> x1, matrix products: 14 us -> 4.59 us  [shards(): lax.dot_general(cot_rows, mixed_all, (((0,), (0,)), ((), ())), preferred_...]
    pallas_call x0 -> x2, Pallas kernels: none -> 6.06 us  [run_once(): pl.pallas_call(body, in_specs=[pl.BlockSpec(memory_space=pltpu.SMEM)] + [...]
    pallas_call x8 -> x10, Pallas kernels: 18.9 us -> 23.9 us  [run(): pl.pallas_call(body, grid=(columns // tile,), in_specs=in_specs, out_spec...]
  transfers between devices with their start and end apart: 18 -> 29, of which waited for: 10 -> 10; matrix products, arithmetic and copies ran while one was open for 14% -> 15% of each run, Pallas kernels for 10% -> 20%
where the time goes in v3:
time: 150 us; the launch traced here: 148 us
  starting transfers between devices  36.4 us (24%)
  waiting for transfers between devices  33.8 us (23%)
  Pallas kernels  30 us (20%)
  other arithmetic  16.2 us (11%)
  between operations  14.7 us (10%)
  local copies, waits for them, and re-layouts  12.7 us (8%)
  matrix products  4.59 us (3%)
    pallas_call x10, Pallas kernels, run(): pl.pallas_call(body, grid=(columns // tile,), in_specs=in_specs, out_spec...  23.9 us
    ppermute x6, waiting for transfers between devices, line_swap(): return lax.ppermute(x, 'fsdp', [(i, i ^ by) for i in range(size)])  23.7 us
    unnamed x91, local copies, waits for them, and re-layouts  10.9 us
    ppermute x6, starting transfers between devices, line_swap(): return lax.ppermute(x, 'fsdp', [(i, i ^ by) for i in range(size)])  8.86 us
    ppermute x10, starting transfers between devices, core_swap(): return lax.ppermute(x, 'ctx', [(i, i ^ 1) for i in range(size)])  8.44 us
    ppermute x2, starting transfers between devices, shifted(): lax.ppermute(x, 'ctx', [(i, i + by) for i in range(size) if 0 <= i + by <...  6.43 us
    pallas_call x2, Pallas kernels, run_once(): pl.pallas_call(body, in_specs=[pl.BlockSpec(memory_space=pltpu.SMEM)] + [...  6.06 us
    ppermute x3, waiting for transfers between devices, entering_state(): arrived = lax.ppermute(total, 'ctx', [(i, i ^ by) for i in range(size)])  5.45 us
  transfers between devices with their start and end apart: 29, of which 10 were waited for; matrix products, arithmetic and copies ran while one was open for 15% of the time, Pallas kernels for 20%

profile of v3, /device:TPU:1, one launch (start us, length us, event | category | flops | bytes accessed | tf_op | source)
XLA Modules:
  0.0 148.3 jit_solution(9194950472766166302)
XLA Ops:
  8.0 1.8 %multiply_convert_fusion.product = bf16[128,1024]{1,0:T(8,128)(2,1)} fusion(bf16[128,1024]{1,0:T(8,128)(2,1)} %value.1, bf16[128,1024]{1,0:T(8,128)(2,1)} %key.3), kind=kLoop, calls=%fused_computation.6 | loop fusion | flops 524288 | bytes 786432 | tf_op jit(solution)/shard_map/convert_element_type | solution.py:384
  9.8 4.5 %collective-permute-start = (bf16[128,1024]{1,0:T(8,128)(2,1)}, bf16[128,1024]{1,0:T(8,128)(2,1)}, u32[]{:S(2)}, u32[]{:S(2)}) collective-permute-start(bf16[128,1024]{1,0:T(8,128)(2,1)} %multiply_convert_fusion.product), channel_id=1, source_target_pairs={{0,4},{4,8},{8,12},{12,16},{16,20},{20,24},{24,28},{1,5},{5,9},{9,... | collective-permute-start | bytes 786440 | tf_op jit(solution)/shard_map/ppermute | solution.py:278
  17.1 2.0 %shard_map.197 = (f32[256,1024]{1,0:T(8,128)S(1)}, f32[256,1024]{1,0:T(8,128)S(1)}) custom-call(f32[128,1024]{1,0:T(8,128)S(1)} %copy-done.34, f32[16,1024]{1,0:T(8,128)S(1)} %get-tuple-element.113.rate, f32[16,1024]{1,0:T(8,128)S(1)} %get-tuple-element.105.coef, f32[1,1024]{1,0:T(1,128)S(1)} %bitcast.20, bf16[256,512]{1,0:T(8,128)(2,1)S(1)} %copy-done.3), custom_call_target="tpu_custom_call" | custom-call | flops 402653184 | bytes 3018752 | tf_op jit(solution)/shard_map/pallas_call | solution.py:246
  19.2 4.2 %shard_map.198 = (f32[256,1024]{1,0:T(8,128)S(1)}, f32[128,1024]{1,0:T(8,128)S(1)}, bf16[128,1024]{1,0:T(8,128)(2,1)S(1)}, bf16[128,1024]{1,0:T(8,128)(2,1)S(1)}, f32[16,1024]{1,0:T(8,128)S(1)}) custom-call(bf16[128,1024]{1,0:T(8,128)(2,1)} %collective-permute-done.before, bf16[128,1024]{1,0:T(8,128)(2,1)} %multiply_convert_fusion.product, ...), custom_call_target="tpu_custom_call" | custom-call | flops 536870912 | bytes 4980736 | tf_op jit(solution)/shard_map/pallas_call | solution.py:246
  29.1 4.2 %collective-permute-done.2 = f32[16,1024]{1,0:T(8,128)S(1)} collective-permute-done((f32[16,1024]{1,0:T(8,128)S(1)}, f32[16,1024]{1,0:T(8,128)S(1)}, u32[]{:S(2)}, u32[]{:S(2)}) %collective-permute-start.2) | collective-permute-done | bytes 65568 | tf_op jit(solution)/shard_map/ppermute | solution.py:325
  34.8 1.9 %collective-permute-start.3 = (f32[16,1024]{1,0:T(8,128)}, f32[16,1024]{1,0:T(8,128)}, u32[]{:S(2)}, u32[]{:S(2)}) collective-permute-start(f32[16,1024]{1,0:T(8,128)} %add_select_fusion.2), channel_id=1, source_target_pairs={{0,16},{4,20},{8,24},{12,28},{16,0},{20,4},{24,8},{28,12},{1,17},{... | collective-permute-start | bytes 196616 | tf_op jit(solution)/shard_map/ppermute | solution.py:325
  38.0 2.3 %collective-permute-start.5 = (bf16[128,1024]{1,0:T(8,128)(2,1)}, bf16[128,1024]{1,0:T(8,128)(2,1)}, u32[]{:S(2)}, u32[]{:S(2)}) collective-permute-start(bf16[128,1024]{1,0:T(8,128)(2,1)} %rest_0_.1), channel_id=1, source_target_pairs={{0,2},{1,3},{2,0},{3,1},{4,6},{5,7},{6,4},{7,5},{8,10},{9,11},{10,... | collective-permute-start | bytes 786440 | tf_op jit(solution)/shard_map/ppermute | solution.py:288
  41.2 2.0 %shard_map.199.inner = f32[128,1024]{1,0:T(8,128)S(1)} custom-call(bf16[128,1024]{1,0:T(8,128)(2,1)S(1)} %copy-done.29, f32[256,1024]{1,0:T(8,128)S(1)} %get-tuple-element.55.li_spec, bf16[256,512]{1,0:T(8,128)(2,1)S(1)} %copy-done.3, bf16[256,768]{1,0:T(8,128)(2,1)S(1)} %copy-done.2), custom_call_target="tpu_custom_call" | custom-call | flops 402653184 | bytes 2490368 | tf_op jit(solution)/shard_map/pallas_call | solution.py:246
  44.2 2.0 %shard_map.200 = (f32[128,1024]{1,0:T(8,128)S(1)}, bf16[128,1024]{1,0:T(8,128)(2,1)}) custom-call(f32[128,1024]{1,0:T(8,128)S(1)} %shard_map.199.inner, bf16[128,1024]{1,0:T(8,128)(2,1)S(1)} %copy-done.10, f32[16,1024]{1,0:T(8,128)S(1)} %get-tuple-element.113.rate, f32[16,1024]{1,0:T(8,128)S(1)} %get-tuple-element.105.coef, ...), custom_call_target="tpu_custom_call" | custom-call | flops 134217728 | bytes 1769472 | tf_op jit(solution)/shard_map/pallas_call | solution.py:246
  48.2 8.5 %collective-permute-done.6.rest_3_ = bf16[128,1024]{1,0:T(8,128)(2,1)} collective-permute-done((bf16[128,1024]{1,0:T(8,128)(2,1)}, bf16[128,1024]{1,0:T(8,128)(2,1)}, u32[]{:S(2)}, u32[]{:S(2)}) %collective-permute-start.6) | collective-permute-done | bytes 262176 | tf_op jit(solution)/shard_map/ppermute | solution.py:288
  58.0 4.7 %collective-permute-start.8 = (bf16[128,512]{1,0:T(8,128)(2,1)S(1)}, bf16[128,512]{1,0:T(8,128)(2,1)S(1)}, u32[]{:S(2)}, u32[]{:S(2)}) collective-permute-start(bf16[128,512]{1,0:T(8,128)(2,1)S(1)} %get-tuple-element.66), channel_id=1, source_target_pairs={{0,4},{4,0},{8,12},{12,8},{16,20},{20,16},{24,28},{28,24},{1,5},{5... | collective-permute-start | bytes 393224 | tf_op jit(solution)/shard_map/ppermute | solution.py:273
  66.4 2.2 %copy-done = bf16[2048,1024]{1,0:T(8,128)(2,1)S(1)} copy-done((bf16[2048,1024]{1,0:T(8,128)(2,1)S(1)}, bf16[2048,1024]{1,0:T(8,128)(2,1)}, u32[]{:S(2)}) %copy-start) | copy-done | bytes 4194328
  69.6 2.5 %shard_map.202 = (f32[128,1024]{1,0:T(8,128)S(1)}, bf16[128,1024]{1,0:T(8,128)(2,1)S(1)}) custom-call(bf16[128,2048]{1,0:T(8,128)(2,1)S(1)} %copy-done.5, bf16[128,2048]{1,0:T(8,128)(2,1)S(1)} %constant_dynamic-update-slice_fusion.far, bf16[2048,1024]{1,0:T(8,128)(2,1)S(1)} %copy-done), custom_call_target="tpu_custom_call" | custom-call | flops 1073741824 | bytes 6029312 | tf_op jit(solution)/shard_map/pallas_call | solution.py:246
  72.6 4.8 %shard_map.203 = (bf16[256,512]{1,0:T(8,128)(2,1)S(1)}, bf16[256,512]{1,0:T(8,128)(2,1)}, bf16[256,512]{1,0:T(8,128)(2,1)}, bf16[256,512]{1,0:T(8,128)(2,1)}) custom-call(s32[4]{0:T(128)S(1)} %pad_add_fusion.starts, bf16[128,1024]{1,0:T(8,128)(2,1)} %get-tuple-element.72.near, bf16[128,1024]{1,0:T(8,128)(2,1)} %collective-permute-done.11.far, ...), custom_call_target="tpu_custom_call" | custom-call | flops 1073741824 | bytes 4718608 | tf_op jit(solution)/shard_map/pallas_call | solution.py:259
  86.8 2.3 %shard_map.205.inner = f32[128,1024]{1,0:T(8,128)S(1)} custom-call(f32[128,1024]{1,0:T(8,128)S(1)} %copy-done.25, f32[256,1024]{1,0:T(8,128)S(1)} %get-tuple-element.55.li_spec, bf16[256,512]{1,0:T(8,128)(2,1)S(1)} %copy-done.3, bf16[256,768]{1,0:T(8,128)(2,1)S(1)} %copy-done.2), custom_call_target="tpu_custom_call" | custom-call | flops 402653184 | bytes 2752512 | tf_op jit(solution)/shard_map/pallas_call | solution.py:246
  90.2 3.8 %shard_map.206 = (f32[128,1024]{1,0:T(8,128)}, f32[128,1024]{1,0:T(8,128)}, f32[256,1024]{1,0:T(8,128)S(1)}, f32[128,1024]{1,0:T(8,128)S(1)}) custom-call(f32[128,1024]{1,0:T(8,128)S(1)} %shard_map.205.inner, f32[16,1024]{1,0:T(8,128)S(1)} %get-tuple-element.113.rate, f32[16,1024]{1,0:T(8,128)S(1)} %get-tuple-element.105.coef, ...), custom_call_target="tpu_custom_call" | custom-call | flops 536870912 | bytes 6160384 | tf_op jit(solution)/shard_map/pallas_call | solution.py:246
  96.1 3.1 %collective-permute-start.14 = (bf16[256,512]{1,0:T(8,128)(2,1)}, bf16[256,512]{1,0:T(8,128)(2,1)}, u32[]{:S(2)}, u32[]{:S(2)}) collective-permute-start(bf16[256,512]{1,0:T(8,128)(2,1)} %get-tuple-element.76), channel_id=1, source_target_pairs={{0,3},{1,2},{2,1},{3,0},{4,7},{5,6},{6,5},{7,4},{8,11},{9,10},{10,... | collective-permute-start | bytes 786440 | tf_op jit(solution)/shard_map/ppermute | solution.py:288
  99.3 2.0 %collective-permute-start.13 = (bf16[256,512]{1,0:T(8,128)(2,1)}, bf16[256,512]{1,0:T(8,128)(2,1)}, u32[]{:S(2)}, u32[]{:S(2)}) collective-permute-start(bf16[256,512]{1,0:T(8,128)(2,1)} %get-tuple-element.75), channel_id=1, source_target_pairs={{0,2},{1,3},{2,0},{3,1},{4,6},{5,7},{6,4},{7,5},{8,10},{9,11},{10,... | collective-permute-start | bytes 786440 | tf_op jit(solution)/shard_map/ppermute | solution.py:288
  102.5 4.4 %all-to-all-start = ((bf16[4,256,512]{2,1,0:T(8,128)(2,1)}), bf16[4,256,512]{2,1,0:T(8,128)(2,1)}, u32[]{:S(2)}, u32[]{:S(2)}) async-start(bf16[4,256,512]{2,1,0:T(8,128)(2,1)} %bitcast.21), calls=%async_computation | async-start | bytes 2097152 | tf_op jit(solution)/shard_map/all_to_all | solution.py:292
  109.3 14.1 %collective-permute-done.13 = bf16[256,512]{1,0:T(8,128)(2,1)} collective-permute-done((bf16[256,512]{1,0:T(8,128)(2,1)}, bf16[256,512]{1,0:T(8,128)(2,1)}, u32[]{:S(2)}, u32[]{:S(2)}) %collective-permute-start.13) | collective-permute-done | bytes 262176 | tf_op jit(solution)/shard_map/ppermute | solution.py:288
  127.2 2.3 %shard_map.207 = (f32[128,1024]{1,0:T(8,128)S(1)}, bf16[128,1024]{1,0:T(8,128)(2,1)}) custom-call(f32[256,1024]{1,0:T(8,128)S(1)} %get-tuple-element.89.grad_spec, f32[256,1024]{1,0:T(8,128)S(1)} %get-tuple-element.53.mr_spec, bf16[256,768]{1,0:T(8,128)(2,1)S(1)} %copy-done.2), custom_call_target="tpu_custom_call" | custom-call | flops 402653184 | bytes 3276800 | tf_op jit(solution)/shard_map/pallas_call | solution.py:246
  129.5 1.9 %collective-permute-start.21 = (bf16[128,1024]{1,0:T(8,128)(2,1)}, bf16[128,1024]{1,0:T(8,128)(2,1)S(1)}, u32[]{:S(2)}, u32[]{:S(2)}) collective-permute-start(bf16[128,1024]{1,0:T(8,128)(2,1)} %get-tuple-element.91), channel_id=1, source_target_pairs={{4,0},{8,4},{12,8},{16,12},{20,16},{24,20},{28,24},{5,1},{9,5},{13... | collective-permute-start | bytes 786440 | tf_op jit(solution)/shard_map/ppermute | solution.py:278
  131.6 4.6 %convolution_multiply_fusion = f32[512,1024]{1,0:T(8,128)} fusion(bf16[1024,512]{1,0:T(8,128)(2,1)} %bitcast.11, bf16[1024,1024]{1,0:T(8,128)(2,1)} %all-gather.5.cloned.1.call-done), kind=kOutput, calls=%fused_computation | convolution fusion | flops 1074266112 | bytes 5242880 | tf_op jit(solution)/shard_map/dot_general | solution.py:557
  137.1 1.9 %maximum_select_fusion.1 = f32[128,1024]{1,0:T(8,128)} fusion(f32[128,512]{1,0:T(8,128)} %collective-permute-done.15, f32[128,512]{1,0:T(8,128)S(1)} %copy-done.36, pred[]{:T(512)S(6)} %eq.4), kind=kLoop, calls=%fused_computation.3 | loop fusion | flops 393216 | bytes 1048577 | tf_op jit(solution)/shard_map/jit(_where)/select_n | solution.py:483
  (162 shorter events, 45.6 us)
Async XLA Ops:
  7.2 59.1 %all-gather.3.cloned.1.call-start = ((), (), s32[]{:S(2)}) async-start(), calls=%async_computation.1 | async-start | bytes 5242880 | tf_op jit(solution)/shard_map/all_gather | solution.py:386
  8.0 123.6 %all-gather.5.cloned.1.call-start = ((), (), s32[]{:S(2)}) async-start(), calls=%async_computation.2 | async-start | bytes 2359296 | tf_op jit(solution)/shard_map/all_gather | solution.py:436
  9.8 9.3 %collective-permute-start = (bf16[128,1024]{1,0:T(8,128)(2,1)}, bf16[128,1024]{1,0:T(8,128)(2,1)}, u32[]{:S(2)}, u32[]{:S(2)}) collective-permute-start(bf16[128,1024]{1,0:T(8,128)(2,1)} %multiply_convert_fusion.product), channel_id=1, source_target_pairs={{0,4},{4,8},{8,12},{12,16},{16,20},{20,24},{24,28},{1,5},{5,9},{9,... | collective-permute-start | bytes 786440 | tf_op jit(solution)/shard_map/ppermute | solution.py:278
  27.9 5.5 %collective-permute-start.2 = (f32[16,1024]{1,0:T(8,128)S(1)}, f32[16,1024]{1,0:T(8,128)S(1)}, u32[]{:S(2)}, u32[]{:S(2)}) collective-permute-start(f32[16,1024]{1,0:T(8,128)S(1)} %add_select_fusion.3), channel_id=1, source_target_pairs={{0,8},{4,12},{8,0},{12,4},{16,24},{20,28},{24,16},{28,20},{1,9},{5... | collective-permute-start | bytes 196616 | tf_op jit(solution)/shard_map/ppermute | solution.py:325
  34.8 8.4 %collective-permute-start.3 = (f32[16,1024]{1,0:T(8,128)}, f32[16,1024]{1,0:T(8,128)}, u32[]{:S(2)}, u32[]{:S(2)}) collective-permute-start(f32[16,1024]{1,0:T(8,128)} %add_select_fusion.2), channel_id=1, source_target_pairs={{0,16},{4,20},{8,24},{12,28},{16,0},{20,4},{24,8},{28,12},{1,17},{... | collective-permute-start | bytes 196616 | tf_op jit(solution)/shard_map/ppermute | solution.py:325
  36.7 10.7 %collective-permute-start.4 = (bf16[128,1024]{1,0:T(8,128)(2,1)}, bf16[128,1024]{1,0:T(8,128)(2,1)}, u32[]{:S(2)}, u32[]{:S(2)}) collective-permute-start(bf16[128,1024]{1,0:T(8,128)(2,1)} %rest_0_.1), channel_id=1, source_target_pairs={{0,1},{1,0},{2,3},{3,2},{4,5},{5,4},{6,7},{7,6},{8,9},{9,8},{10,11... | collective-permute-start | bytes 786440 | tf_op jit(solution)/shard_map/ppermute | solution.py:288
  38.0 10.2 %collective-permute-start.5 = (bf16[128,1024]{1,0:T(8,128)(2,1)}, bf16[128,1024]{1,0:T(8,128)(2,1)}, u32[]{:S(2)}, u32[]{:S(2)}) collective-permute-start(bf16[128,1024]{1,0:T(8,128)(2,1)} %rest_0_.1), channel_id=1, source_target_pairs={{0,2},{1,3},{2,0},{3,1},{4,6},{5,7},{6,4},{7,5},{8,10},{9,11},{10,... | collective-permute-start | bytes 786440 | tf_op jit(solution)/shard_map/ppermute | solution.py:288
  40.3 16.5 %collective-permute-start.6 = (bf16[128,1024]{1,0:T(8,128)(2,1)}, bf16[128,1024]{1,0:T(8,128)(2,1)}, u32[]{:S(2)}, u32[]{:S(2)}) collective-permute-start(bf16[128,1024]{1,0:T(8,128)(2,1)} %rest_0_.1), channel_id=1, source_target_pairs={{0,3},{1,2},{2,1},{3,0},{4,7},{5,6},{6,5},{7,4},{8,11},{9,10},{10,... | collective-permute-start | bytes 786440 | tf_op jit(solution)/shard_map/ppermute | solution.py:288
  58.0 5.6 %collective-permute-start.8 = (bf16[128,512]{1,0:T(8,128)(2,1)S(1)}, bf16[128,512]{1,0:T(8,128)(2,1)S(1)}, u32[]{:S(2)}, u32[]{:S(2)}) collective-permute-start(bf16[128,512]{1,0:T(8,128)(2,1)S(1)} %get-tuple-element.66), channel_id=1, source_target_pairs={{0,4},{4,0},{8,12},{12,8},{16,20},{20,16},{24,28},{28,24},{1,5},{5... | collective-permute-start | bytes 393224 | tf_op jit(solution)/shard_map/ppermute | solution.py:273
  65.3 7.3 %collective-permute-start.11 = (bf16[128,1024]{1,0:T(8,128)(2,1)}, bf16[128,1024]{1,0:T(8,128)(2,1)}, u32[]{:S(2)}, u32[]{:S(2)}) collective-permute-start(bf16[128,1024]{1,0:T(8,128)(2,1)} %get-tuple-element.72.near), channel_id=1, source_target_pairs={{0,4},{4,0},{8,12},{12,8},{16,20},{20,16},{24,28},{28,24},{1,5},{5... | collective-permute-start | bytes 786440 | tf_op jit(solution)/shard_map/ppermute | solution.py:273
  72.1 5.3 %collective-permute-start.16 = (bf16[128,1024]{1,0:T(8,128)(2,1)S(1)}, bf16[128,1024]{1,0:T(8,128)(2,1)S(1)}, u32[]{:S(2)}, u32[]{:S(2)}) collective-permute-start(bf16[128,1024]{1,0:T(8,128)(2,1)S(1)} %get-tuple-element.71), channel_id=1, source_target_pairs={{0,4},{4,0},{8,12},{12,8},{16,20},{20,16},{24,28},{28,24},{1,5},{5... | collective-permute-start | bytes 786440 | tf_op jit(solution)/shard_map/ppermute | solution.py:273
  82.5 6.7 %collective-permute-start.20 = (f32[16,1024]{1,0:T(8,128)S(1)}, f32[16,1024]{1,0:T(8,128)S(1)}, u32[]{:S(2)}, u32[]{:S(2)}) collective-permute-start(f32[16,1024]{1,0:T(8,128)S(1)} %add_select_fusion.1), channel_id=1, source_target_pairs={{0,24},{4,28},{8,16},{12,20},{16,8},{20,12},{24,0},{28,4},{1,25},{... | collective-permute-start | bytes 196616 | tf_op jit(solution)/shard_map/ppermute | solution.py:283
  83.3 5.9 %collective-permute-start.19 = (f32[16,1024]{1,0:T(8,128)S(1)}, f32[16,1024]{1,0:T(8,128)S(1)}, u32[]{:S(2)}, u32[]{:S(2)}) collective-permute-start(f32[16,1024]{1,0:T(8,128)S(1)} %add_select_fusion.1), channel_id=1, source_target_pairs={{0,16},{4,20},{8,24},{12,28},{16,0},{20,4},{24,8},{28,12},{1,17},{... | collective-permute-start | bytes 196616 | tf_op jit(solution)/shard_map/ppermute | solution.py:283
  84.5 4.7 %collective-permute-start.18 = (f32[16,1024]{1,0:T(8,128)S(1)}, f32[16,1024]{1,0:T(8,128)S(1)}, u32[]{:S(2)}, u32[]{:S(2)}) collective-permute-start(f32[16,1024]{1,0:T(8,128)S(1)} %add_select_fusion.1), channel_id=1, source_target_pairs={{0,8},{4,12},{8,0},{12,4},{16,24},{20,28},{24,16},{28,20},{1,9},{5... | collective-permute-start | bytes 196616 | tf_op jit(solution)/shard_map/ppermute | solution.py:283
  94.7 12.2 %collective-permute-start.22 = (f32[64,1024]{1,0:T(8,128)}, f32[64,1024]{1,0:T(8,128)}, u32[]{:S(2)}, u32[]{:S(2)}) collective-permute-start(f32[64,1024]{1,0:T(8,128)} %dynamic-slice_bitcast_fusion), channel_id=1, source_target_pairs={{0,4},{4,0},{8,12},{12,8},{16,20},{20,16},{24,28},{28,24},{1,5},{5... | collective-permute-start | bytes 786440 | tf_op jit(solution)/shard_map/ppermute | solution.py:273
  96.1 13.2 %collective-permute-start.14 = (bf16[256,512]{1,0:T(8,128)(2,1)}, bf16[256,512]{1,0:T(8,128)(2,1)}, u32[]{:S(2)}, u32[]{:S(2)}) collective-permute-start(bf16[256,512]{1,0:T(8,128)(2,1)} %get-tuple-element.76), channel_id=1, source_target_pairs={{0,3},{1,2},{2,1},{3,0},{4,7},{5,6},{6,5},{7,4},{8,11},{9,10},{10,... | collective-permute-start | bytes 786440 | tf_op jit(solution)/shard_map/ppermute | solution.py:288
  99.3 24.2 %collective-permute-start.13 = (bf16[256,512]{1,0:T(8,128)(2,1)}, bf16[256,512]{1,0:T(8,128)(2,1)}, u32[]{:S(2)}, u32[]{:S(2)}) collective-permute-start(bf16[256,512]{1,0:T(8,128)(2,1)} %get-tuple-element.75), channel_id=1, source_target_pairs={{0,2},{1,3},{2,0},{3,1},{4,6},{5,7},{6,4},{7,5},{8,10},{9,11},{10,... | collective-permute-start | bytes 786440 | tf_op jit(solution)/shard_map/ppermute | solution.py:288
  101.3 22.2 %collective-permute-start.12 = (bf16[256,512]{1,0:T(8,128)(2,1)}, bf16[256,512]{1,0:T(8,128)(2,1)}, u32[]{:S(2)}, u32[]{:S(2)}) collective-permute-start(bf16[256,512]{1,0:T(8,128)(2,1)} %get-tuple-element.74), channel_id=1, source_target_pairs={{0,1},{1,0},{2,3},{3,2},{4,5},{5,4},{6,7},{7,6},{8,9},{9,8},{10,11... | collective-permute-start | bytes 786440 | tf_op jit(solution)/shard_map/ppermute | solution.py:288
  102.5 29.0 %all-to-all-start = ((bf16[4,256,512]{2,1,0:T(8,128)(2,1)}), bf16[4,256,512]{2,1,0:T(8,128)(2,1)}, u32[]{:S(2)}, u32[]{:S(2)}) async-start(bf16[4,256,512]{2,1,0:T(8,128)(2,1)} %bitcast.21), calls=%async_computation | async-start | bytes 2097152 | tf_op jit(solution)/shard_map/all_to_all | solution.py:292
  107.9 16.8 %collective-permute-start.23 = (bf16[64,1024]{1,0:T(8,128)(2,1)S(1)}, bf16[64,1024]{1,0:T(8,128)(2,1)S(1)}, u32[]{:S(2)}, u32[]{:S(2)}) collective-permute-start(bf16[64,1024]{1,0:T(8,128)(2,1)S(1)} %fusion), channel_id=1, source_target_pairs={{0,8},{4,12},{8,0},{12,4},{16,24},{20,28},{24,16},{28,20},{1,9},{5... | collective-permute-start | bytes 393224 | tf_op jit(solution)/shard_map/ppermute | solution.py:283
  124.8 6.6 %collective-permute-start.24 = (bf16[64,1024]{1,0:T(8,128)(2,1)S(1)}, bf16[64,1024]{1,0:T(8,128)(2,1)S(1)}, u32[]{:S(2)}, u32[]{:S(2)}) collective-permute-start(bf16[64,1024]{1,0:T(8,128)(2,1)S(1)} %add_convert_fusion), channel_id=1, source_target_pairs={{0,16},{4,20},{8,24},{12,28},{16,0},{20,4},{24,8},{28,12},{1,17},{... | collective-permute-start | bytes 393224 | tf_op jit(solution)/shard_map/ppermute | solution.py:283
  126.5 10.6 %collective-permute-start.15 = (f32[128,512]{1,0:T(8,128)}, f32[128,512]{1,0:T(8,128)}, u32[]{:S(2)}, u32[]{:S(2)}) collective-permute-start(f32[128,512]{1,0:T(8,128)} %get-tuple-element.103), channel_id=1, source_target_pairs={{0,4},{4,0},{8,12},{12,8},{16,20},{20,16},{24,28},{28,24},{1,5},{5... | collective-permute-start | bytes 786440 | tf_op jit(solution)/shard_map/ppermute | solution.py:273
  129.5 9.5 %collective-permute-start.21 = (bf16[128,1024]{1,0:T(8,128)(2,1)}, bf16[128,1024]{1,0:T(8,128)(2,1)S(1)}, u32[]{:S(2)}, u32[]{:S(2)}) collective-permute-start(bf16[128,1024]{1,0:T(8,128)(2,1)} %get-tuple-element.91), channel_id=1, source_target_pairs={{4,0},{8,4},{12,8},{16,12},{20,16},{24,20},{28,24},{5,1},{9,5},{13... | collective-permute-start | bytes 786440 | tf_op jit(solution)/shard_map/ppermute | solution.py:278
  131.4 9.2 %collective-permute-start.25 = (f32[64,1024]{1,0:T(8,128)S(1)}, f32[64,1024]{1,0:T(8,128)S(1)}, u32[]{:S(2)}, u32[]{:S(2)}) collective-permute-start(f32[64,1024]{1,0:T(8,128)S(1)} %add_multiply_fusion), channel_id=1, source_target_pairs={{0,4},{4,0},{8,12},{12,8},{16,20},{20,16},{24,28},{28,24},{1,5},{5... | collective-permute-start | bytes 786440 | tf_op jit(solution)/shard_map/ppermute | solution.py:273
  (49 other events, 246.4 us)
Sparse Core Ops, SparseCore 0:
  9.9 55.6 all-gather.2
  67.5 28.7 all-gather.4

commit v4 on v3

--- a/solution.py
+++ b/solution.py
@@ -14,7 +14,6 @@
 BF16 = jnp.bfloat16
 TILE = 256
 GROUP = 8
-SWAPS = 3
 
 
 def split_parts(matrix):
@@ -159,41 +158,49 @@
     mixed[...] = (query[...].astype(F32) * total).astype(BF16)
 
 
-def split_body(width, count, starts, *rest):
-    pieces, near, shares = rest[:count], rest[count], rest[count + 1 : -1]
-    far = rest[-1]
+def split_body(width, starts, *rest):
+    pieces, (first, second, stack) = rest[:-3], rest[-3:]
+    rows = first.shape[0]
+    half = width // 2
     for r, piece in enumerate(pieces):
-        for k in range(piece.shape[1] // (2 * width)):
-            place = pl.multiple_of(starts[r], 128) + k * width
-            near[:, pl.ds(place, width)] = piece[:, pl.ds(pl.multiple_of(starts[count], 128) + 2 * k * width, width)]
-            far[:, pl.ds(place, width)] = piece[:, pl.ds(pl.multiple_of(starts[count + 1], 128) + 2 * k * width, width)]
-    part = far.shape[1] // len(shares)
-    for k, share in enumerate(shares):
-        share[...] = far[:, k * part : (k + 1) * part]
-
-
-def grad_share_body(near, far, weight, own, sent):
-    own[...] = jnp.dot(near[...], weight[...], preferred_element_type=F32)
-    sent[...] = jnp.dot(far[...], weight[...], preferred_element_type=F32).astype(BF16)
-
-
-def grad_gate_body(own, arrived, query, rate, grad_mixed, grad_out, ends):
-    total = own[...] + arrived[...].astype(F32)
+        for k in range(piece.shape[1] // width):
+            block = starts[r] + k
+            place = pl.ds(pl.multiple_of(block * half, 128), half)
+            first[:, place] = piece[:, k * width : k * width + half]
+            second[:, place] = piece[:, k * width + half : (k + 1) * width]
+            stack[pl.ds(pl.multiple_of(block * rows, 128), rows), :] = piece[:, k * width : (k + 1) * width]
+
+
+def grad_early_body(cotangent, weight, total):
+    total[...] = jnp.dot(cotangent[...], weight[...], preferred_element_type=F32)
+
+
+def grad_gate_body(early, cotangent, weight, query, rate, grad_mixed, grad_out, ends):
+    total = early[...] + jnp.dot(cotangent[...], weight[...], preferred_element_type=F32)
     grad_mixed[...] = total
     gated = total * query[...].astype(F32)
     grad_out[...] = gated
     ends[...] = fold_modes(gated, rate[...], True)
 
 
-def out_share_body(starts, near, far, weight, *rest):
+def out_body(starts, mixed, weight, *rest):
     parts, whole = rest[:-1], rest[-1]
-    rows = near.shape[0]
     contract = (((1,), (1,)), ((), ()))
-    whole[:rows] = lax.dot_general(near[...], weight[...], contract, preferred_element_type=F32).astype(BF16)
-    whole[rows:] = lax.dot_general(far[...], weight[...], contract, preferred_element_type=F32).astype(BF16)
+    whole[...] = lax.dot_general(mixed[...], weight[...], contract, preferred_element_type=F32).astype(BF16)
     width = parts[0].shape[1]
     for r, part in enumerate(parts):
         part[...] = whole[:, pl.ds(pl.multiple_of(starts[r], 128), width)]
+
+
+def out_sum_body(width, count, *rest):
+    parts, result = rest[:-1], rest[-1]
+    half = width // 2
+    for h in range(2):
+        total = parts[h * count][...].astype(F32)
+        for part in parts[h * count + 1 : (h + 1) * count]:
+            total = total + part[...].astype(F32)
+        for k in range(total.shape[1] // half):
+            result[:, k * width + h * half : k * width + (h + 1) * half] = total[:, k * half : (k + 1) * half]
 
 
 def grad_inner_body(grad_out, li_spec, ahead, back, inner):
@@ -255,11 +262,15 @@
 
 
 def run_once(body, inputs, outputs, scratch, flops):
+    in_specs = [pl.BlockSpec(memory_space=pltpu.VMEM)] * (len(inputs) - 1)
+    if inputs[0] is None:
+        inputs = inputs[1:]
+    else:
+        in_specs = [pl.BlockSpec(memory_space=pltpu.SMEM)] + in_specs
     moved = sum(math.prod(array.shape) * array.dtype.itemsize for array in inputs)
     return pl.pallas_call(
         body,
-        in_specs=[pl.BlockSpec(memory_space=pltpu.SMEM)]
-        + [pl.BlockSpec(memory_space=pltpu.VMEM)] * (len(inputs) - 1),
+        in_specs=in_specs,
         out_specs=[pl.BlockSpec(memory_space=pltpu.VMEM)] * len(outputs),
         out_shape=[jax.ShapeDtypeStruct(shape, dtype) for shape, dtype in outputs],
         scratch_shapes=scratch,
@@ -288,17 +299,8 @@
     return lax.ppermute(x, "fsdp", [(i, i ^ by) for i in range(size)])
 
 
-def plane_trade(x):
-    return lax.all_to_all(x, "ctx", 0, 0, axis_index_groups=plane_groups(), tiled=True)
-
-
 def columns_to_rows(x, count):
     return jnp.concatenate(jnp.split(x, count, axis=1), axis=0)
-
-
-def plane_groups():
-    size = lax.axis_size("ctx")
-    return [list(range(core, size, 2)) for core in range(2)]
 
 
 def after(x, *others):
@@ -383,7 +385,10 @@
 
     mr_product = (key_mr.astype(F32) * value_mr.astype(F32)).astype(BF16)
     before = shifted(mr_product, 1)
-    weight_rows = lax.all_gather(out_weight, "ctx", axis=0, tiled=True, axis_index_groups=plane_groups())
+    half = width // 2
+    weight_halves = [
+        lax.all_gather(out_weight[h * half : (h + 1) * half], "ctx", axis=0, tiled=True) for h in range(2)
+    ]
     cot_line = [(line, cotangent)]
     for r in range(1, line_count):
         cot_line.append((line ^ r, line_swap(cotangent, r)))
@@ -432,70 +437,70 @@
         pass_flops,
     )
 
-    other_mixed = core_swap(mixed_li)
     mixed_all = lax.all_gather(mixed_li, "ctx", axis=0, tiled=True)
 
-    part_width = chips * width // line_count
-    near, *to_far = run_once(
-        functools.partial(split_body, width, line_count),
-        [jnp.stack([index * part_width for index, _ in cot_line] + [core * width, (1 - core) * width])]
-        + [piece for _, piece in cot_line],
-        [((rows, chips * width), BF16)] + [((rows, chips * width // 4), BF16)] * 4,
-        [pltpu.VMEM((rows, chips * width), BF16)],
+    blocks = ctx_count // line_count
+    first, second, stack = run_once(
+        functools.partial(split_body, width),
+        [jnp.stack([index * blocks for index, _ in cot_line])] + [piece for _, piece in cot_line],
+        [((rows, ctx_count * half), BF16)] * 2 + [((ctx_count * rows, width), BF16)],
+        [],
         0,
     )
-    far_parts = [core_swap(to_far[0]), core_swap(to_far[1])]
-    for part in to_far[2:]:
-        far_parts.append(core_swap(after(part, far_parts[-1])))
-    far = jnp.concatenate(far_parts, axis=1)
-    near = after(near, mixed_li)
-    cot_rows = plane_trade(
-        columns_to_rows(
-            jnp.where(core == 0, jnp.concatenate([near, far], axis=0), jnp.concatenate([far, near], axis=0)), chips
-        )
-    )
-
-    share_flops = 4 * rows * columns * chips * width
-    own_share, sent_share = run(
-        grad_share_body,
-        columns,
-        [("whole", near), ("whole", far), tile(weight_rows)],
-        [(rows, F32), (rows, BF16)],
+    cot_rows = lax.all_to_all(stack, "ctx", 0, 0, tiled=True)
+
+    share_flops = rows * columns * ctx_count * width
+    part_width = blocks * half
+    out_starts = jnp.stack([(line ^ r) * part_width for r in range(line_count)])
+
+    (grad_early,) = run(
+        grad_early_body,
+        columns,
+        [("whole", first), tile(weight_halves[0])],
+        [(rows, F32)],
         share_flops,
     )
-    arrived_share = core_swap(sent_share)
-    out_parts = run_once(
-        out_share_body,
-        [
-            jnp.stack([(line ^ r) * part_width for r in range(line_count)]),
-            after(mixed_li, sent_share),
-            other_mixed,
-            weight_rows,
-        ],
-        [((2 * rows, part_width), BF16)] * line_count,
-        [pltpu.VMEM((2 * rows, chips * width), BF16)],
+    out_early = run_once(
+        out_body,
+        [out_starts, mixed_li, weight_halves[0]],
+        [((rows, part_width), BF16)] * line_count,
+        [pltpu.VMEM((rows, ctx_count * half), BF16)],
         share_flops,
     )
-    out_sum = out_parts[0].astype(F32)
-    for r in range(1, line_count):
-        out_sum = out_sum + line_swap(out_parts[r], r).astype(F32)
-    near_out, far_out = out_sum[:rows], core_swap(out_sum[rows:])
-    output = jnp.where(
-        core == 0, jnp.concatenate([near_out, far_out], axis=1), jnp.concatenate([far_out, near_out], axis=1)
-    )
-
+    out_arrived = [out_early[0]] + [line_swap(out_early[r], r) for r in range(1, line_count)]
     grad_mixed, grad_li_out, back_ends = run(
         grad_gate_body,
         columns,
-        [tile(after(own_share, out_parts[0])), tile(arrived_share), tile(query_li), tile(rate)],
+        [
+            tile(after(grad_early, cot_rows, *out_arrived)),
+            ("whole", second),
+            tile(weight_halves[1]),
+            tile(query_li),
+            tile(rate),
+        ],
         [(rows, F32), (rows, F32), (rate.shape[0], F32)],
-        rows * columns,
+        share_flops,
+    )
+    out_late = run_once(
+        out_body,
+        [out_starts, after(mixed_li, back_ends), weight_halves[1]],
+        [((rows, part_width), BF16)] * line_count,
+        [pltpu.VMEM((rows, ctx_count * half), BF16)],
+        share_flops,
+    )
+    late_arrived = [out_late[0]] + [line_swap(out_late[r], r) for r in range(1, line_count)]
+    (output,) = run_once(
+        functools.partial(out_sum_body, width, line_count),
+        [None] + out_arrived + late_arrived,
+        [((rows, 2 * part_width), F32)],
+        [],
+        0,
     )
     back_entering = entering_direct(back_ends, back_factors, here, True)
     (grad_inner,) = run(
         grad_inner_body,
         columns,
-        [tile(grad_li_out), tile(li_spec), table("ahead"), table("back")],
+        [tile(after(grad_li_out, out_late[0])), tile(li_spec), table("ahead"), table("back")],
         [(rows, F32)],
         3 * pass_flops,
     )
@@ -545,7 +550,7 @@
         sent = plane_half.astype(BF16)
         plane_half = sent.astype(F32) + chip_swap(sent, by).astype(F32)
         by *= 2
-    plane_half = plane_half * grad_scale
+    plane_half = after(plane_half * grad_scale, *late_arrived)
     other_half = core_swap(plane_half)
     grad_taps = jnp.where(
         core == 0,

time: 150 us -> 172 us (1.15)
  local copies, waits for them, and re-layouts: 12.7 us -> 24.1 us
  starting transfers between devices: 36.4 us -> 47.2 us
  other arithmetic: 16.2 us -> 10.5 us
  Pallas kernels: 30 us -> 34.5 us
  waiting for transfers between devices: 33.8 us -> 35.6 us
    unnamed x91 -> x118, local copies, waits for them, and re-layouts: 10.9 us -> 21.8 us
    ppermute x6 -> x9, waiting for transfers between devices: 23.7 us -> 14.8 us  [line_swap(): return lax.ppermute(x, 'fsdp', [(i, i ^ by) for i in range(size)])]
    all_to_all x1, waiting for transfers between devices: 0.01 us -> 7.76 us  [shards(): cot_rows = lax.all_to_all(stack, 'ctx', 0, 0, tiled=True)]
    all_to_all x1, starting transfers between devices: 4.39 us -> 10.7 us  [shards(): cot_rows = lax.all_to_all(stack, 'ctx', 0, 0, tiled=True)]
    ppermute x6 -> x9, starting transfers between devices: 8.86 us -> 13.2 us  [line_swap(): return lax.ppermute(x, 'fsdp', [(i, i ^ by) for i in range(size)])]
    select_n x2 -> x0, other arithmetic: 3.43 us -> none  [the longest x1 1.89 us: shards(): jnp.where(core == 0, jnp.concatenate([near_out, far_out], axis=1), jnp.co...]
    ppermute x5, waiting for transfers between devices: 0.01 us -> 3.44 us  [chip_swap(): return lax.ppermute(x, 'ctx', [(i, i ^ 2 * by) for i in range(size)])]
    pallas_call x2 -> x4, Pallas kernels: 6.06 us -> 9.09 us  [run_once(): pl.pallas_call(body, in_specs=in_specs, out_specs=[pl.BlockSpec(memory_sp...]
  transfers between devices with their start and end apart: 29 -> 26, of which waited for: 10 -> 11; matrix products, arithmetic and copies ran while one was open for 15% -> 8% of each run, Pallas kernels for 20% -> 20%
where the time goes in v4:
time: 172 us; the launch traced here: 171 us
  starting transfers between devices  47.2 us (27%)
  waiting for transfers between devices  35.6 us (21%)
  Pallas kernels  34.5 us (20%)
  local copies, waits for them, and re-layouts  24.1 us (14%)
  between operations  14.4 us (8%)
  other arithmetic  10.5 us (6%)
  matrix products  4.53 us (3%)
    pallas_call x10, Pallas kernels, run(): pl.pallas_call(body, grid=(columns // tile,), in_specs=in_specs, out_spec...  25.5 us
    unnamed x118, local copies, waits for them, and re-layouts  21.8 us
    ppermute x9, waiting for transfers between devices, line_swap(): return lax.ppermute(x, 'fsdp', [(i, i ^ by) for i in range(size)])  14.8 us
    ppermute x9, starting transfers between devices, line_swap(): return lax.ppermute(x, 'fsdp', [(i, i ^ by) for i in range(size)])  13.2 us
    all_to_all x1, starting transfers between devices, shards(): cot_rows = lax.all_to_all(stack, 'ctx', 0, 0, tiled=True)  10.7 us
    pallas_call x4, Pallas kernels, run_once(): pl.pallas_call(body, in_specs=in_specs, out_specs=[pl.BlockSpec(memory_sp...  9.09 us
    ppermute x2, starting transfers between devices, shifted(): lax.ppermute(x, 'ctx', [(i, i + by) for i in range(size) if 0 <= i + by <...  8.44 us
    all_to_all x1, waiting for transfers between devices, shards(): cot_rows = lax.all_to_all(stack, 'ctx', 0, 0, tiled=True)  7.76 us
  transfers between devices with their start and end apart: 26, of which 11 were waited for; matrix products, arithmetic and copies ran while one was open for 8% of the time, Pallas kernels for 20%

profile of v4, /device:TPU:1, one launch (start us, length us, event | category | flops | bytes accessed | tf_op | source)
XLA Modules:
  0.0 170.8 jit_solution(14837625679947044059)
XLA Ops:
  7.3 2.3 %fusion.1 = (bf16[256,1024]{1,0:T(8,128)(2,1)}, bf16[256,1024]{1,0:T(8,128)(2,1)}) fusion(bf16[512,1024]{1,0:T(8,128)(2,1)} %param.23), kind=kLoop, calls=%fused_computation.25 | loop fusion | bytes 2097152 | tf_op jit(solution)/shard_map/slice | solution.py:390
  11.2 4.5 %collective-permute-start = (bf16[128,1024]{1,0:T(8,128)(2,1)}, bf16[128,1024]{1,0:T(8,128)(2,1)}, u32[]{:S(2)}, u32[]{:S(2)}) collective-permute-start(bf16[128,1024]{1,0:T(8,128)(2,1)} %multiply_convert_fusion.product), channel_id=1, source_target_pairs={{0,4},{4,8},{8,12},{12,16},{16,20},{20,24},{24,28},{1,5},{5,9},{9,... | collective-permute-start | bytes 786440 | tf_op jit(solution)/shard_map/ppermute | solution.py:289
  19.7 4.2 %shard_map.198 = (f32[256,1024]{1,0:T(8,128)S(1)}, f32[128,1024]{1,0:T(8,128)S(1)}, bf16[128,1024]{1,0:T(8,128)(2,1)S(1)}, bf16[128,1024]{1,0:T(8,128)(2,1)S(1)}, f32[16,1024]{1,0:T(8,128)S(1)}) custom-call(bf16[128,1024]{1,0:T(8,128)(2,1)} %collective-permute-done.before, bf16[128,1024]{1,0:T(8,128)(2,1)} %multiply_convert_fusion.product, ...), custom_call_target="tpu_custom_call" | custom-call | flops 536870912 | bytes 4980736 | tf_op jit(solution)/shard_map/pallas_call | solution.py:253
  44.2 2.3 %collective-permute-start.8 = (bf16[128,1024]{1,0:T(8,128)(2,1)S(1)}, bf16[128,1024]{1,0:T(8,128)(2,1)}, u32[]{:S(2)}, u32[]{:S(2)}) collective-permute-start(bf16[128,1024]{1,0:T(8,128)(2,1)S(1)} %copy-done.35), channel_id=1, source_target_pairs={{0,2},{1,3},{2,0},{3,1},{4,6},{5,7},{6,4},{7,5},{8,10},{9,11},{10,... | collective-permute-start | bytes 786440 | tf_op jit(solution)/shard_map/ppermute | solution.py:299
  46.6 5.5 %collective-permute-done.7.rest_1_ = bf16[128,1024]{1,0:T(8,128)(2,1)S(1)} collective-permute-done((bf16[128,1024]{1,0:T(8,128)(2,1)S(1)}, bf16[128,1024]{1,0:T(8,128)(2,1)S(1)}, u32[]{:S(2)}, u32[]{:S(2)}) %collective-permute-start.7) | collective-permute-done | bytes 262176 | tf_op jit(solution)/shard_map/ppermute | solution.py:299
  53.0 8.4 %collective-permute-done.9.rest_3_ = bf16[128,1024]{1,0:T(8,128)(2,1)} collective-permute-done((bf16[128,1024]{1,0:T(8,128)(2,1)S(1)}, bf16[128,1024]{1,0:T(8,128)(2,1)}, u32[]{:S(2)}, u32[]{:S(2)}) %collective-permute-start.9) | collective-permute-done | bytes 262176 | tf_op jit(solution)/shard_map/ppermute | solution.py:299
  65.2 10.7 %all-to-all-start = ((bf16[8,128,512]{2,1,0:T(8,128)(2,1)}), bf16[8,128,512]{2,1,0:T(8,128)(2,1)}, u32[]{:S(2)}, u32[]{:S(2)}) async-start(bf16[8,128,512]{2,1,0:T(8,128)(2,1)} %bitcast.20), calls=%async_computation | async-start | bytes 2097152 | tf_op jit(solution)/shard_map/all_to_all | solution.py:450
  76.0 2.2 %copy-done = bf16[2048,1024]{1,0:T(8,128)(2,1)S(1)} copy-done((bf16[2048,1024]{1,0:T(8,128)(2,1)S(1)}, bf16[2048,1024]{1,0:T(8,128)(2,1)}, u32[]{:S(2)}) %copy-start) | copy-done | bytes 4194328
  78.2 3.3 %shard_map.201 = (bf16[128,512]{1,0:T(8,128)(2,1)S(1)}, bf16[128,512]{1,0:T(8,128)(2,1)}, bf16[128,512]{1,0:T(8,128)(2,1)}, bf16[128,512]{1,0:T(8,128)(2,1)}) custom-call(s32[4]{0:T(128)S(1)} %pad_add_fusion.starts, bf16[128,1024]{1,0:T(8,128)(2,1)} %get-tuple-element.71.mixed, bf16[2048,1024]{1,0:T(8,128)(2,1)S(1)} %copy-done), custom_call_target="tpu_custom_call" | custom-call | flops 536870912 | bytes 4456464 | tf_op jit(solution)/shard_map/pallas_call | solution.py:271
  81.5 3.2 %collective-permute-start.4 = (bf16[128,512]{1,0:T(8,128)(2,1)}, bf16[128,512]{1,0:T(8,128)(2,1)}, u32[]{:S(2)}, u32[]{:S(2)}) collective-permute-start(bf16[128,512]{1,0:T(8,128)(2,1)} %get-tuple-element.63), channel_id=1, source_target_pairs={{0,1},{1,0},{2,3},{3,2},{4,5},{5,4},{6,7},{7,6},{8,9},{9,8},{10,11... | collective-permute-start | bytes 393224 | tf_op jit(solution)/shard_map/ppermute | solution.py:299
  89.9 7.8 %all-to-all-done = bf16[8,128,512]{2,1,0:T(8,128)(2,1)} async-done(((bf16[8,128,512]{2,1,0:T(8,128)(2,1)}), bf16[8,128,512]{2,1,0:T(8,128)(2,1)}, u32[]{:S(2)}, u32[]{:S(2)}) %all-to-all-start) | async-done | bytes 1048608 | tf_op jit(solution)/shard_map/all_to_all | solution.py:450
  97.6 2.6 %all-gather.6.cloned.1.call-done.weight = bf16[2048,1024]{1,0:T(8,128)(2,1)} async-done(((bf16[256,1024]{1,0:T(8,128)(2,1)}), bf16[2048,1024]{1,0:T(8,128)(2,1)}) %all-gather.6.cloned.1.call-update) | async-done | bytes 4194320 | tf_op jit(solution)/shard_map/all_gather | solution.py:390
  100.2 2.2 %copy-done.2 = bf16[2048,1024]{1,0:T(8,128)(2,1)S(1)} copy-done((bf16[2048,1024]{1,0:T(8,128)(2,1)S(1)}, bf16[2048,1024]{1,0:T(8,128)(2,1)}, u32[]{:S(2)}) %copy-start.2) | copy-done | bytes 4194328
  104.4 3.3 %shard_map.204 = (f32[128,1024]{1,0:T(8,128)S(1)}, f32[128,1024]{1,0:T(8,128)S(1)}, f32[16,1024]{1,0:T(8,128)}) custom-call(f32[128,1024]{1,0:T(8,128)S(1)} %shard_map.203.early, bf16[128,2048]{1,0:T(8,128)(2,1)S(1)} %copy-done.30, bf16[2048,1024]{1,0:T(8,128)(2,1)S(1)} %copy-done.2, bf16[128,1024]{1,0:T(8,128)(2,1)S(1)} %copy-done.14, ...), custom_call_target="tpu_custom_call" | custom-call | flops 536870912 | bytes 6684672 | tf_op jit(solution)/shard_map/pallas_call | solution.py:253
  115.6 2.2 %copy-done.3 = bf16[2048,1024]{1,0:T(8,128)(2,1)S(1)} copy-done((bf16[2048,1024]{1,0:T(8,128)(2,1)S(1)}, bf16[2048,1024]{1,0:T(8,128)(2,1)}, u32[]{:S(2)}) %copy-start.3) | copy-done | bytes 4194328
  117.8 2.5 %shard_map.205 = (bf16[128,512]{1,0:T(8,128)(2,1)S(1)}, bf16[128,512]{1,0:T(8,128)(2,1)S(1)}, bf16[128,512]{1,0:T(8,128)(2,1)S(1)}, bf16[128,512]{1,0:T(8,128)(2,1)S(1)}) custom-call(s32[4]{0:T(128)S(1)} %pad_add_fusion.starts, bf16[128,1024]{1,0:T(8,128)(2,1)} %get-tuple-element.71.mixed, bf16[2048,1024]{1,0:T(8,128)(2,1)S(1)} %copy-done.3), custom_call_target="tpu_custom_call" | custom-call | flops 536870912 | bytes 4456464 | tf_op jit(solution)/shard_map/pallas_call | solution.py:271
  120.5 2.3 %shard_map.207.inner = f32[128,1024]{1,0:T(8,128)S(1)} custom-call(f32[128,1024]{1,0:T(8,128)S(1)} %copy-done.28, f32[256,1024]{1,0:T(8,128)S(1)} %get-tuple-element.54.li_spec, bf16[256,512]{1,0:T(8,128)(2,1)S(1)} %copy-done.5, bf16[256,768]{1,0:T(8,128)(2,1)S(1)} %copy-done.4), custom_call_target="tpu_custom_call" | custom-call | flops 402653184 | bytes 2752512 | tf_op jit(solution)/shard_map/pallas_call | solution.py:253
  123.0 3.8 %shard_map.208 = (f32[128,1024]{1,0:T(8,128)}, f32[128,1024]{1,0:T(8,128)}, f32[256,1024]{1,0:T(8,128)S(1)}, f32[128,1024]{1,0:T(8,128)S(1)}) custom-call(f32[128,1024]{1,0:T(8,128)S(1)} %shard_map.207.inner, f32[16,1024]{1,0:T(8,128)S(1)} %get-tuple-element.107.rate, f32[16,1024]{1,0:T(8,128)S(1)} %get-tuple-element.99.coef, ...), custom_call_target="tpu_custom_call" | custom-call | flops 536870912 | bytes 6160384 | tf_op jit(solution)/shard_map/pallas_call | solution.py:253
  131.7 3.4 %collective-permute-done.19 = bf16[64,1024]{1,0:T(8,128)(2,1)S(1)} collective-permute-done((bf16[64,1024]{1,0:T(8,128)(2,1)S(1)}, bf16[64,1024]{1,0:T(8,128)(2,1)S(1)}, u32[]{:S(2)}, u32[]{:S(2)}) %collective-permute-start.19) | collective-permute-done | bytes 131104 | tf_op jit(solution)/shard_map/ppermute | solution.py:294
  137.4 2.9 %collective-permute-start.11 = (bf16[128,512]{1,0:T(8,128)(2,1)}, bf16[128,512]{1,0:T(8,128)(2,1)S(1)}, u32[]{:S(2)}, u32[]{:S(2)}) collective-permute-start(bf16[128,512]{1,0:T(8,128)(2,1)} %copy-done.47), channel_id=1, source_target_pairs={{0,2},{1,3},{2,0},{3,1},{4,6},{5,7},{6,4},{7,5},{8,10},{9,11},{10,... | collective-permute-start | bytes 393224 | tf_op jit(solution)/shard_map/ppermute | solution.py:299
  140.3 2.3 %shard_map.209 = (f32[128,1024]{1,0:T(8,128)S(1)}, bf16[128,1024]{1,0:T(8,128)(2,1)}) custom-call(f32[256,1024]{1,0:T(8,128)S(1)} %get-tuple-element.86.grad_spec, f32[256,1024]{1,0:T(8,128)S(1)} %get-tuple-element.52.mr_spec, bf16[256,768]{1,0:T(8,128)(2,1)S(1)} %copy-done.4), custom_call_target="tpu_custom_call" | custom-call | flops 402653184 | bytes 3276800 | tf_op jit(solution)/shard_map/pallas_call | solution.py:253
  142.6 3.9 %collective-permute-start.17 = (bf16[128,1024]{1,0:T(8,128)(2,1)}, bf16[128,1024]{1,0:T(8,128)(2,1)S(1)}, u32[]{:S(2)}, u32[]{:S(2)}) collective-permute-start(bf16[128,1024]{1,0:T(8,128)(2,1)} %get-tuple-element.88), channel_id=1, source_target_pairs={{4,0},{8,4},{12,8},{16,12},{20,16},{24,20},{28,24},{5,1},{9,5},{13... | collective-permute-start | bytes 786440 | tf_op jit(solution)/shard_map/ppermute | solution.py:289
  149.6 3.8 %collective-permute-start.21 = (f32[64,1024]{1,0:T(8,128)S(1)}, f32[64,1024]{1,0:T(8,128)}, u32[]{:S(2)}, u32[]{:S(2)}) collective-permute-start(f32[64,1024]{1,0:T(8,128)S(1)} %add_multiply_fusion), channel_id=1, source_target_pairs={{0,4},{4,0},{8,12},{12,8},{16,20},{20,16},{24,28},{28,24},{1,5},{5... | collective-permute-start | bytes 786440 | tf_op jit(solution)/shard_map/ppermute | solution.py:284
  153.3 4.5 %convolution_multiply_fusion = f32[512,1024]{1,0:T(8,128)} fusion(bf16[1024,512]{1,0:T(8,128)(2,1)} %bitcast.10, bf16[1024,1024]{1,0:T(8,128)(2,1)} %all-gather.8.cloned.1.call-done), kind=kOutput, calls=%fused_computation | convolution fusion | flops 1074266112 | bytes 5242880 | tf_op jit(solution)/shard_map/dot_general | solution.py:562
  (180 shorter events, 62.3 us)
Async XLA Ops:
  7.2 68.8 %all-gather.4.cloned.1.call-start = ((), (), s32[]{:S(2)}) async-start(), calls=%async_computation.1 | async-start | bytes 4718592 | tf_op jit(solution)/shard_map/all_gather | solution.py:390
  9.6 90.6 %all-gather.6.cloned.1.call-start = ((), (), s32[]{:S(2)}) async-start(), calls=%async_computation.2 | async-start | bytes 4718592 | tf_op jit(solution)/shard_map/all_gather | solution.py:390
  10.4 143.0 %all-gather.8.cloned.1.call-start = ((), (), s32[]{:S(2)}) async-start(), calls=%async_computation.3 | async-start | bytes 2359296 | tf_op jit(solution)/shard_map/all_gather | solution.py:440
  11.2 8.5 %collective-permute-start = (bf16[128,1024]{1,0:T(8,128)(2,1)}, bf16[128,1024]{1,0:T(8,128)(2,1)}, u32[]{:S(2)}, u32[]{:S(2)}) collective-permute-start(bf16[128,1024]{1,0:T(8,128)(2,1)} %multiply_convert_fusion.product), channel_id=1, source_target_pairs={{0,4},{4,8},{8,12},{12,16},{16,20},{20,24},{24,28},{1,5},{5,9},{9,... | collective-permute-start | bytes 786440 | tf_op jit(solution)/shard_map/ppermute | solution.py:289
  28.4 4.1 %collective-permute-start.2 = (f32[16,1024]{1,0:T(8,128)S(1)}, f32[16,1024]{1,0:T(8,128)S(1)}, u32[]{:S(2)}, u32[]{:S(2)}) collective-permute-start(f32[16,1024]{1,0:T(8,128)S(1)} %add_select_fusion.3), channel_id=1, source_target_pairs={{0,8},{4,12},{8,0},{12,4},{16,24},{20,28},{24,16},{28,20},{1,9},{5... | collective-permute-start | bytes 196616 | tf_op jit(solution)/shard_map/ppermute | solution.py:327
  33.9 5.2 %collective-permute-start.3 = (f32[16,1024]{1,0:T(8,128)}, f32[16,1024]{1,0:T(8,128)S(1)}, u32[]{:S(2)}, u32[]{:S(2)}) collective-permute-start(f32[16,1024]{1,0:T(8,128)} %add_select_fusion.2), channel_id=1, source_target_pairs={{0,16},{4,20},{8,24},{12,28},{16,0},{20,4},{24,8},{28,12},{1,17},{... | collective-permute-start | bytes 196616 | tf_op jit(solution)/shard_map/ppermute | solution.py:327
  42.9 9.2 %collective-permute-start.7 = (bf16[128,1024]{1,0:T(8,128)(2,1)S(1)}, bf16[128,1024]{1,0:T(8,128)(2,1)S(1)}, u32[]{:S(2)}, u32[]{:S(2)}) collective-permute-start(bf16[128,1024]{1,0:T(8,128)(2,1)S(1)} %copy-done.35), channel_id=1, source_target_pairs={{0,1},{1,0},{2,3},{3,2},{4,5},{5,4},{6,7},{7,6},{8,9},{9,8},{10,11... | collective-permute-start | bytes 786440 | tf_op jit(solution)/shard_map/ppermute | solution.py:299
  44.2 8.8 %collective-permute-start.8 = (bf16[128,1024]{1,0:T(8,128)(2,1)S(1)}, bf16[128,1024]{1,0:T(8,128)(2,1)}, u32[]{:S(2)}, u32[]{:S(2)}) collective-permute-start(bf16[128,1024]{1,0:T(8,128)(2,1)S(1)} %copy-done.35), channel_id=1, source_target_pairs={{0,2},{1,3},{2,0},{3,1},{4,6},{5,7},{6,4},{7,5},{8,10},{9,11},{10,... | collective-permute-start | bytes 786440 | tf_op jit(solution)/shard_map/ppermute | solution.py:299
  46.5 14.9 %collective-permute-start.9 = (bf16[128,1024]{1,0:T(8,128)(2,1)S(1)}, bf16[128,1024]{1,0:T(8,128)(2,1)}, u32[]{:S(2)}, u32[]{:S(2)}) collective-permute-start(bf16[128,1024]{1,0:T(8,128)(2,1)S(1)} %copy-done.35), channel_id=1, source_target_pairs={{0,3},{1,2},{2,1},{3,0},{4,7},{5,6},{6,5},{7,4},{8,11},{9,10},{10,... | collective-permute-start | bytes 786440 | tf_op jit(solution)/shard_map/ppermute | solution.py:299
  65.2 32.4 %all-to-all-start = ((bf16[8,128,512]{2,1,0:T(8,128)(2,1)}), bf16[8,128,512]{2,1,0:T(8,128)(2,1)}, u32[]{:S(2)}, u32[]{:S(2)}) async-start(bf16[8,128,512]{2,1,0:T(8,128)(2,1)} %bitcast.20), calls=%async_computation | async-start | bytes 2097152 | tf_op jit(solution)/shard_map/all_to_all | solution.py:450
  81.5 16.1 %collective-permute-start.4 = (bf16[128,512]{1,0:T(8,128)(2,1)}, bf16[128,512]{1,0:T(8,128)(2,1)}, u32[]{:S(2)}, u32[]{:S(2)}) collective-permute-start(bf16[128,512]{1,0:T(8,128)(2,1)} %get-tuple-element.63), channel_id=1, source_target_pairs={{0,1},{1,0},{2,3},{3,2},{4,5},{5,4},{6,7},{7,6},{8,9},{9,8},{10,11... | collective-permute-start | bytes 393224 | tf_op jit(solution)/shard_map/ppermute | solution.py:299
  84.7 12.9 %collective-permute-start.5 = (bf16[128,512]{1,0:T(8,128)(2,1)}, bf16[128,512]{1,0:T(8,128)(2,1)}, u32[]{:S(2)}, u32[]{:S(2)}) collective-permute-start(bf16[128,512]{1,0:T(8,128)(2,1)} %get-tuple-element.64), channel_id=1, source_target_pairs={{0,2},{1,3},{2,0},{3,1},{4,6},{5,7},{6,4},{7,5},{8,10},{9,11},{10,... | collective-permute-start | bytes 393224 | tf_op jit(solution)/shard_map/ppermute | solution.py:299
  85.7 11.9 %collective-permute-start.6 = (bf16[128,512]{1,0:T(8,128)(2,1)}, bf16[128,512]{1,0:T(8,128)(2,1)}, u32[]{:S(2)}, u32[]{:S(2)}) collective-permute-start(bf16[128,512]{1,0:T(8,128)(2,1)} %get-tuple-element.65), channel_id=1, source_target_pairs={{0,3},{1,2},{2,1},{3,0},{4,7},{5,6},{6,5},{7,4},{8,11},{9,10},{10,... | collective-permute-start | bytes 393224 | tf_op jit(solution)/shard_map/ppermute | solution.py:299
  112.3 10.5 %collective-permute-start.14 = (f32[16,1024]{1,0:T(8,128)S(1)}, f32[16,1024]{1,0:T(8,128)S(1)}, u32[]{:S(2)}, u32[]{:S(2)}) collective-permute-start(f32[16,1024]{1,0:T(8,128)S(1)} %add_select_fusion.1), channel_id=1, source_target_pairs={{0,8},{4,12},{8,0},{12,4},{16,24},{20,28},{24,16},{28,20},{1,9},{5... | collective-permute-start | bytes 196616 | tf_op jit(solution)/shard_map/ppermute | solution.py:294
  114.4 8.5 %collective-permute-start.15 = (f32[16,1024]{1,0:T(8,128)S(1)}, f32[16,1024]{1,0:T(8,128)S(1)}, u32[]{:S(2)}, u32[]{:S(2)}) collective-permute-start(f32[16,1024]{1,0:T(8,128)S(1)} %add_select_fusion.1), channel_id=1, source_target_pairs={{0,16},{4,20},{8,24},{12,28},{16,0},{20,4},{24,8},{28,12},{1,17},{... | collective-permute-start | bytes 196616 | tf_op jit(solution)/shard_map/ppermute | solution.py:294
  114.7 8.2 %collective-permute-start.16 = (f32[16,1024]{1,0:T(8,128)S(1)}, f32[16,1024]{1,0:T(8,128)S(1)}, u32[]{:S(2)}, u32[]{:S(2)}) collective-permute-start(f32[16,1024]{1,0:T(8,128)S(1)} %add_select_fusion.1), channel_id=1, source_target_pairs={{0,24},{4,28},{8,16},{12,20},{16,8},{20,12},{24,0},{28,4},{1,25},{... | collective-permute-start | bytes 196616 | tf_op jit(solution)/shard_map/ppermute | solution.py:294
  126.8 2.2 %collective-permute-start.18 = (f32[64,1024]{1,0:T(8,128)S(1)}, f32[64,1024]{1,0:T(8,128)}, u32[]{:S(2)}, u32[]{:S(2)}) collective-permute-start(f32[64,1024]{1,0:T(8,128)S(1)} %dynamic-slice_bitcast_fusion), channel_id=1, source_target_pairs={{0,4},{4,0},{8,12},{12,8},{16,20},{20,16},{24,28},{28,24},{1,5},{5... | collective-permute-start | bytes 786440 | tf_op jit(solution)/shard_map/ppermute | solution.py:284
  130.1 5.1 %collective-permute-start.19 = (bf16[64,1024]{1,0:T(8,128)(2,1)S(1)}, bf16[64,1024]{1,0:T(8,128)(2,1)S(1)}, u32[]{:S(2)}, u32[]{:S(2)}) collective-permute-start(bf16[64,1024]{1,0:T(8,128)(2,1)S(1)} %fusion), channel_id=1, source_target_pairs={{0,8},{4,12},{8,0},{12,4},{16,24},{20,28},{24,16},{28,20},{1,9},{5... | collective-permute-start | bytes 393224 | tf_op jit(solution)/shard_map/ppermute | solution.py:294
  135.8 10.7 %collective-permute-start.20 = (bf16[64,1024]{1,0:T(8,128)(2,1)}, bf16[64,1024]{1,0:T(8,128)(2,1)}, u32[]{:S(2)}, u32[]{:S(2)}) collective-permute-start(bf16[64,1024]{1,0:T(8,128)(2,1)} %add_convert_fusion), channel_id=1, source_target_pairs={{0,16},{4,20},{8,24},{12,28},{16,0},{20,4},{24,8},{28,12},{1,17},{... | collective-permute-start | bytes 393224 | tf_op jit(solution)/shard_map/ppermute | solution.py:294
  136.2 11.4 %collective-permute-start.10 = (bf16[128,512]{1,0:T(8,128)(2,1)}, bf16[128,512]{1,0:T(8,128)(2,1)S(1)}, u32[]{:S(2)}, u32[]{:S(2)}) collective-permute-start(bf16[128,512]{1,0:T(8,128)(2,1)} %copy-done.48), channel_id=1, source_target_pairs={{0,1},{1,0},{2,3},{3,2},{4,5},{5,4},{6,7},{7,6},{8,9},{9,8},{10,11... | collective-permute-start | bytes 393224 | tf_op jit(solution)/shard_map/ppermute | solution.py:299
  137.4 10.9 %collective-permute-start.11 = (bf16[128,512]{1,0:T(8,128)(2,1)}, bf16[128,512]{1,0:T(8,128)(2,1)S(1)}, u32[]{:S(2)}, u32[]{:S(2)}) collective-permute-start(bf16[128,512]{1,0:T(8,128)(2,1)} %copy-done.47), channel_id=1, source_target_pairs={{0,2},{1,3},{2,0},{3,1},{4,6},{5,7},{6,4},{7,5},{8,10},{9,11},{10,... | collective-permute-start | bytes 393224 | tf_op jit(solution)/shard_map/ppermute | solution.py:299
  140.3 8.6 %collective-permute-start.12 = (bf16[128,512]{1,0:T(8,128)(2,1)}, bf16[128,512]{1,0:T(8,128)(2,1)S(1)}, u32[]{:S(2)}, u32[]{:S(2)}) collective-permute-start(bf16[128,512]{1,0:T(8,128)(2,1)} %copy-done.46), channel_id=1, source_target_pairs={{0,3},{1,2},{2,1},{3,0},{4,7},{5,6},{6,5},{7,4},{8,11},{9,10},{10,... | collective-permute-start | bytes 393224 | tf_op jit(solution)/shard_map/ppermute | solution.py:299
  142.6 18.1 %collective-permute-start.17 = (bf16[128,1024]{1,0:T(8,128)(2,1)}, bf16[128,1024]{1,0:T(8,128)(2,1)S(1)}, u32[]{:S(2)}, u32[]{:S(2)}) collective-permute-start(bf16[128,1024]{1,0:T(8,128)(2,1)} %get-tuple-element.88), channel_id=1, source_target_pairs={{4,0},{8,4},{12,8},{16,12},{20,16},{24,20},{28,24},{5,1},{9,5},{13... | collective-permute-start | bytes 786440 | tf_op jit(solution)/shard_map/ppermute | solution.py:289
  149.6 12.8 %collective-permute-start.21 = (f32[64,1024]{1,0:T(8,128)S(1)}, f32[64,1024]{1,0:T(8,128)}, u32[]{:S(2)}, u32[]{:S(2)}) collective-permute-start(f32[64,1024]{1,0:T(8,128)S(1)} %add_multiply_fusion), channel_id=1, source_target_pairs={{0,4},{4,0},{8,12},{12,8},{16,20},{20,16},{24,28},{28,24},{1,5},{5... | collective-permute-start | bytes 786440 | tf_op jit(solution)/shard_map/ppermute | solution.py:284
  (61 other events, 264.9 us)
Sparse Core Ops, SparseCore 0:
  10.5 40.6 all-gather.3
  53.7 46.4 all-gather.5
  102.1 29.9 all-gather.7

commit v5 on v4

--- a/solution.py
+++ b/solution.py
@@ -151,56 +151,45 @@
     inner[...] = apply3(back[:rows], times(to_spectrum_exact(ahead[...], signal[...]), li_spec[...]))
 
 
-def long_body(inner, query, rate, coef, entering, li_out, mixed):
+def gather_states(rate, gaps, states, rows):
+    modes = rate.shape[0]
+    total = jnp.zeros_like(rate)
+    for k in range(states.shape[0] // modes):
+        weight = jnp.exp(-rate * (jnp.maximum(gaps[k], 0.0) * float(rows)))
+        total = total + jnp.where(gaps[k] >= 0.0, weight * states[k * modes : (k + 1) * modes], 0.0)
+    return total
+
+
+def long_body(gaps, inner, query, rate, coef, states, li_out, mixed):
     rows = inner.shape[0]
-    total = inner[...] + spread_modes(rate[...], coef[...] * entering[...], rows, 1.0, False)
+    entering = gather_states(rate[...], gaps, states, rows)
+    total = inner[...] + spread_modes(rate[...], coef[...] * entering, rows, 1.0, False)
     li_out[...] = total
     mixed[...] = (query[...].astype(F32) * total).astype(BF16)
 
 
 def split_body(width, starts, *rest):
-    pieces, (first, second, stack) = rest[:-3], rest[-3:]
-    rows = first.shape[0]
-    half = width // 2
+    pieces, (whole, stack) = rest[:-2], rest[-2:]
+    rows = whole.shape[0]
     for r, piece in enumerate(pieces):
-        for k in range(piece.shape[1] // width):
-            block = starts[r] + k
-            place = pl.ds(pl.multiple_of(block * half, 128), half)
-            first[:, place] = piece[:, k * width : k * width + half]
-            second[:, place] = piece[:, k * width + half : (k + 1) * width]
-            stack[pl.ds(pl.multiple_of(block * rows, 128), rows), :] = piece[:, k * width : (k + 1) * width]
-
-
-def grad_early_body(cotangent, weight, total):
-    total[...] = jnp.dot(cotangent[...], weight[...], preferred_element_type=F32)
-
-
-def grad_gate_body(early, cotangent, weight, query, rate, grad_mixed, grad_out, ends):
-    total = early[...] + jnp.dot(cotangent[...], weight[...], preferred_element_type=F32)
+        span = piece.shape[1]
+        whole[:, pl.ds(pl.multiple_of(starts[r] * width, 128), span)] = piece[...]
+        for k in range(span // width):
+            stack[pl.ds(pl.multiple_of((starts[r] + k) * rows, 128), rows), :] = piece[:, k * width : (k + 1) * width]
+
+
+def grad_gate_body(cotangent, weight, query, rate, grad_mixed, grad_out, ends):
+    total = jnp.dot(cotangent[...], weight[...], preferred_element_type=F32)
     grad_mixed[...] = total
     gated = total * query[...].astype(F32)
     grad_out[...] = gated
     ends[...] = fold_modes(gated, rate[...], True)
 
 
-def out_body(starts, mixed, weight, *rest):
-    parts, whole = rest[:-1], rest[-1]
-    contract = (((1,), (1,)), ((), ()))
-    whole[...] = lax.dot_general(mixed[...], weight[...], contract, preferred_element_type=F32).astype(BF16)
-    width = parts[0].shape[1]
-    for r, part in enumerate(parts):
-        part[...] = whole[:, pl.ds(pl.multiple_of(starts[r], 128), width)]
-
-
-def out_sum_body(width, count, *rest):
-    parts, result = rest[:-1], rest[-1]
-    half = width // 2
-    for h in range(2):
-        total = parts[h * count][...].astype(F32)
-        for part in parts[h * count + 1 : (h + 1) * count]:
-            total = total + part[...].astype(F32)
-        for k in range(total.shape[1] // half):
-            result[:, k * width + h * half : k * width + (h + 1) * half] = total[:, k * half : (k + 1) * half]
+def out_body(mixed, weight, stack):
+    stack[...] = lax.dot_general(
+        mixed[...], weight[...], (((1,), (1,)), ((), ())), preferred_element_type=F32
+    ).astype(BF16)
 
 
 def grad_inner_body(grad_out, li_spec, ahead, back, inner):
@@ -256,12 +245,26 @@
         in_specs=in_specs,
         out_specs=[pl.BlockSpec((rows, tile), lambda c: (0, c)) for rows, _ in outputs],
         out_shape=[jax.ShapeDtypeStruct((rows, columns), dtype) for rows, dtype in outputs],
-        compiler_params=pltpu.CompilerParams(vmem_limit_bytes=32 * 1024 * 1024),
+        compiler_params=pltpu.CompilerParams(vmem_limit_bytes=12 * 1024 * 1024),
         cost_estimate=pl.CostEstimate(flops=flops, bytes_accessed=moved, transcendentals=0),
     )(*[array for _, array in inputs])
 
 
-def run_once(body, inputs, outputs, scratch, flops):
+def run_lines(body, lines, x, weight, flops):
+    rows, depth = x.shape
+    span = weight.shape[0] // lines
+    return pl.pallas_call(
+        body,
+        grid=(lines,),
+        in_specs=[pl.BlockSpec((rows, depth), lambda k: (0, 0)), pl.BlockSpec((span, depth), lambda k: (k, 0))],
+        out_specs=pl.BlockSpec((rows, span), lambda k: (k, 0)),
+        out_shape=jax.ShapeDtypeStruct((lines * rows, span), BF16),
+        compiler_params=pltpu.CompilerParams(vmem_limit_bytes=16 * 1024 * 1024),
+        cost_estimate=pl.CostEstimate(flops=flops, bytes_accessed=2 * weight.size, transcendentals=0),
+    )(x, weight)
+
+
+def run_once(body, inputs, outputs, flops):
     in_specs = [pl.BlockSpec(memory_space=pltpu.VMEM)] * (len(inputs) - 1)
     if inputs[0] is None:
         inputs = inputs[1:]
@@ -273,8 +276,7 @@
         in_specs=in_specs,
         out_specs=[pl.BlockSpec(memory_space=pltpu.VMEM)] * len(outputs),
         out_shape=[jax.ShapeDtypeStruct(shape, dtype) for shape, dtype in outputs],
-        scratch_shapes=scratch,
-        compiler_params=pltpu.CompilerParams(vmem_limit_bytes=32 * 1024 * 1024),
+        compiler_params=pltpu.CompilerParams(vmem_limit_bytes=24 * 1024 * 1024),
         cost_estimate=pl.CostEstimate(flops=flops, bytes_accessed=moved, transcendentals=0),
     )(*inputs)
 
@@ -305,31 +307,6 @@
 
 def after(x, *others):
     return lax.optimization_barrier((x,) + others)[0]
-
-
-def doubling_factors(rate, rows, here, backward):
-    factors = []
-    by = 1
-    while by < lax.axis_size("ctx"):
-        offset = here & (by - 1)
-        if backward:
-            offset = by - 1 - offset
-        factors.append((jnp.exp(-rate * (rows * offset).astype(F32)), jnp.exp(-rate * float(rows * by))))
-        by *= 2
-    return factors
-
-
-def entering_state(ends, factors, here, backward):
-    size = lax.axis_size("ctx")
-    total, entering = ends, jnp.zeros_like(ends)
-    by = 1
-    for to_here, across in factors:
-        arrived = lax.ppermute(total, "ctx", [(i, i ^ by) for i in range(size)])
-        later = ((here & by) != 0) != backward
-        entering = entering + jnp.where(later, to_here * arrived, 0.0)
-        total = jnp.where(later, across * arrived + total, across * total + arrived)
-        by *= 2
-    return entering
 
 
 def direct_factors(rate, rows, chip, backward):
@@ -385,19 +362,14 @@
 
     mr_product = (key_mr.astype(F32) * value_mr.astype(F32)).astype(BF16)
     before = shifted(mr_product, 1)
-    half = width // 2
-    weight_halves = [
-        lax.all_gather(out_weight[h * half : (h + 1) * half], "ctx", axis=0, tiled=True) for h in range(2)
-    ]
+    weight_rows = lax.all_gather(out_weight, "ctx", axis=0, tiled=True)
     cot_line = [(line, cotangent)]
     for r in range(1, line_count):
         cot_line.append((line ^ r, line_swap(cotangent, r)))
 
     rate = 1.0 / li_time
     coef = li_residue * jnp.sqrt(-jnp.expm1(-2.0 * rate))
-    ahead_factors, back_factors = lax.optimization_barrier(
-        (doubling_factors(rate, rows, here, False), direct_factors(rate, rows, here // 2, True))
-    )
+    back_factors = lax.optimization_barrier(direct_factors(rate, rows, here // 2, True))
     mr_spec, li_spec = run(
         spectra_body,
         columns,
@@ -421,7 +393,8 @@
         [(2 * rows, F32), (rows, F32), (rows, BF16), (rows, BF16), (rate.shape[0], F32)],
         4 * pass_flops,
     )
-    entering = entering_state(ends, ahead_factors, here, False)
+    states = lax.all_gather(ends, "ctx").reshape(-1, columns)
+    gaps = (here - 1 - jnp.arange(ctx_count, dtype=jnp.int32)).astype(F32)
     (li_inner,) = run(
         inner_body,
         columns,
@@ -432,7 +405,7 @@
     li_out, mixed_li = run(
         long_body,
         columns,
-        [tile(li_inner), tile(query_li), tile(rate), tile(coef), tile(entering)],
+        [("scalar", gaps), tile(li_inner), tile(query_li), tile(rate), tile(coef), tile(states)],
         [(rows, F32), (rows, BF16)],
         pass_flops,
     )
@@ -440,67 +413,30 @@
     mixed_all = lax.all_gather(mixed_li, "ctx", axis=0, tiled=True)
 
     blocks = ctx_count // line_count
-    first, second, stack = run_once(
+    cot_full, stack = run_once(
         functools.partial(split_body, width),
         [jnp.stack([index * blocks for index, _ in cot_line])] + [piece for _, piece in cot_line],
-        [((rows, ctx_count * half), BF16)] * 2 + [((ctx_count * rows, width), BF16)],
-        [],
+        [((rows, ctx_count * width), BF16), ((ctx_count * rows, width), BF16)],
         0,
     )
     cot_rows = lax.all_to_all(stack, "ctx", 0, 0, tiled=True)
 
-    share_flops = rows * columns * ctx_count * width
-    part_width = blocks * half
-    out_starts = jnp.stack([(line ^ r) * part_width for r in range(line_count)])
-
-    (grad_early,) = run(
-        grad_early_body,
-        columns,
-        [("whole", first), tile(weight_halves[0])],
-        [(rows, F32)],
-        share_flops,
-    )
-    out_early = run_once(
-        out_body,
-        [out_starts, mixed_li, weight_halves[0]],
-        [((rows, part_width), BF16)] * line_count,
-        [pltpu.VMEM((rows, ctx_count * half), BF16)],
-        share_flops,
-    )
-    out_arrived = [out_early[0]] + [line_swap(out_early[r], r) for r in range(1, line_count)]
+    share_flops = 2 * rows * columns * ctx_count * width
     grad_mixed, grad_li_out, back_ends = run(
         grad_gate_body,
         columns,
-        [
-            tile(after(grad_early, cot_rows, *out_arrived)),
-            ("whole", second),
-            tile(weight_halves[1]),
-            tile(query_li),
-            tile(rate),
-        ],
+        [("whole", after(cot_full, mixed_li, cot_rows)), tile(weight_rows), tile(query_li), tile(rate)],
         [(rows, F32), (rows, F32), (rate.shape[0], F32)],
         share_flops,
     )
-    out_late = run_once(
-        out_body,
-        [out_starts, after(mixed_li, back_ends), weight_halves[1]],
-        [((rows, part_width), BF16)] * line_count,
-        [pltpu.VMEM((rows, ctx_count * half), BF16)],
-        share_flops,
-    )
-    late_arrived = [out_late[0]] + [line_swap(out_late[r], r) for r in range(1, line_count)]
-    (output,) = run_once(
-        functools.partial(out_sum_body, width, line_count),
-        [None] + out_arrived + late_arrived,
-        [((rows, 2 * part_width), F32)],
-        [],
-        0,
-    )
+    out_stack = run_lines(out_body, line_count, after(mixed_li, back_ends), weight_rows, share_flops)
+    out_parts = lax.all_to_all(out_stack, "fsdp", 0, 0, tiled=True).reshape(line_count, rows, -1)
+    output = jnp.sum(out_parts.astype(F32), axis=0)
     back_entering = entering_direct(back_ends, back_factors, here, True)
     (grad_inner,) = run(
         grad_inner_body,
         columns,
-        [tile(after(grad_li_out, out_late[0])), tile(li_spec), table("ahead"), table("back")],
+        [tile(after(grad_li_out, out_stack)), tile(li_spec), table("ahead"), table("back")],
         [(rows, F32)],
         3 * pass_flops,
     )
@@ -550,7 +486,7 @@
         sent = plane_half.astype(BF16)
         plane_half = sent.astype(F32) + chip_swap(sent, by).astype(F32)
         by *= 2
-    plane_half = after(plane_half * grad_scale, *late_arrived)
+    plane_half = plane_half * grad_scale
     other_half = core_swap(plane_half)
     grad_taps = jnp.where(
         core == 0,

time: 172 us -> 165 us (0.959)
  blocking collectives: 0 us -> 33.6 us
  starting transfers between devices: 47.2 us -> 26.2 us
  local copies, waits for them, and re-layouts: 24.1 us -> 16 us
  waiting for transfers between devices: 35.6 us -> 30.2 us
  Pallas kernels: 34.5 us -> 30.1 us
  other arithmetic: 10.5 us -> 8.53 us
    all_to_all x0 -> x1, blocking collectives: none -> 22.1 us  [shards(): cot_rows = lax.all_to_all(stack, 'ctx', 0, 0, tiled=True)]
    all_gather x0 -> x1, blocking collectives: none -> 11.5 us  [shards(): states = lax.all_gather(ends, 'ctx').reshape(-1, columns)]
    ppermute x9 -> x3, starting transfers between devices: 13.2 us -> 3.67 us  [line_swap(): return lax.ppermute(x, 'fsdp', [(i, i ^ by) for i in range(size)])]
    pallas_call x4 -> x1, Pallas kernels: 9.09 us -> 1.26 us  [run_once(): pl.pallas_call(body, in_specs=in_specs, out_specs=[pl.BlockSpec(memory_sp...]
    unnamed x118 -> x66, local copies, waits for them, and re-layouts: 21.8 us -> 16 us
    pallas_call x0 -> x1, Pallas kernels: none -> 5.04 us  [run_lines(): pl.pallas_call(body, grid=(lines,), in_specs=[pl.BlockSpec((rows, depth),...]
    ppermute x3 -> x0, starting transfers between devices: 3.81 us -> none  [entering_state(): arrived = lax.ppermute(total, 'ctx', [(i, i ^ by) for i in range(size)])]
    ppermute x3 -> x0, waiting for transfers between devices: 3.79 us -> none  [entering_state(): arrived = lax.ppermute(total, 'ctx', [(i, i ^ by) for i in range(size)])]
  transfers between devices with their start and end apart: 26 -> 16, of which waited for: 11 -> 5; matrix products, arithmetic and copies ran while one was open for 8% -> 7% of each run, Pallas kernels for 20% -> 18%
where the time goes in v5:
time: 165 us; the launch traced here: 164 us
  blocking collectives  33.6 us (20%)
  waiting for transfers between devices  30.2 us (18%)
  Pallas kernels  30.1 us (18%)
  starting transfers between devices  26.2 us (16%)
  local copies, waits for them, and re-layouts  16 us (10%)
  between operations  14.5 us (9%)
  other arithmetic  8.53 us (5%)
  matrix products  4.51 us (3%)
    pallas_call x9, Pallas kernels, run(): pl.pallas_call(body, grid=(columns // tile,), in_specs=in_specs, out_spec...  23.8 us
    all_to_all x1, blocking collectives, shards(): cot_rows = lax.all_to_all(stack, 'ctx', 0, 0, tiled=True)  22.1 us
    ppermute x3, waiting for transfers between devices, line_swap(): return lax.ppermute(x, 'fsdp', [(i, i ^ by) for i in range(size)])  17.7 us
    unnamed x66, local copies, waits for them, and re-layouts  16 us
    all_gather x1, blocking collectives, shards(): states = lax.all_gather(ends, 'ctx').reshape(-1, columns)  11.5 us
    ppermute x2, starting transfers between devices, shifted(): lax.ppermute(x, 'ctx', [(i, i + by) for i in range(size) if 0 <= i + by <...  7.86 us
    all_to_all x1, starting transfers between devices, shards(): lax.all_to_all(out_stack, 'fsdp', 0, 0, tiled=True)  7.17 us
    all_to_all x1, waiting for transfers between devices, shards(): lax.all_to_all(out_stack, 'fsdp', 0, 0, tiled=True)  6.55 us
  transfers between devices with their start and end apart: 16, of which 5 were waited for; matrix products, arithmetic and copies ran while one was open for 7% of the time, Pallas kernels for 18%

profile of v5, /device:TPU:1, one launch (start us, length us, event | category | flops | bytes accessed | tf_op | source)
XLA Modules:
  0.0 163.7 jit_solution(6904648243842599453)
XLA Ops:
  8.0 1.8 %multiply_convert_fusion.product = bf16[128,1024]{1,0:T(8,128)(2,1)} fusion(bf16[128,1024]{1,0:T(8,128)(2,1)} %value.1, bf16[128,1024]{1,0:T(8,128)(2,1)} %key.3), kind=kLoop, calls=%fused_computation.3 | loop fusion | flops 524288 | bytes 786432 | tf_op jit(solution)/shard_map/convert_element_type | solution.py:363
  9.8 4.5 %collective-permute-start = (bf16[128,1024]{1,0:T(8,128)(2,1)}, bf16[128,1024]{1,0:T(8,128)(2,1)}, u32[]{:S(2)}, u32[]{:S(2)}) collective-permute-start(bf16[128,1024]{1,0:T(8,128)(2,1)} %multiply_convert_fusion.product), channel_id=1, source_target_pairs={{0,4},{4,8},{8,12},{12,16},{16,20},{20,24},{24,28},{1,5},{5,9},{9,... | collective-permute-start | bytes 786440 | tf_op jit(solution)/shard_map/ppermute | solution.py:291
  17.0 2.0 %shard_map.197 = (f32[256,1024]{1,0:T(8,128)S(1)}, f32[256,1024]{1,0:T(8,128)S(1)}) custom-call(f32[128,1024]{1,0:T(8,128)S(1)} %copy-done.28, f32[16,1024]{1,0:T(8,128)S(1)} %get-tuple-element.71.rate, f32[16,1024]{1,0:T(8,128)S(1)} %get-tuple-element.67.coef, f32[1,1024]{1,0:T(1,128)S(1)} %bitcast.20, bf16[256,512]{1,0:T(8,128)(2,1)S(1)} %copy-done.3), custom_call_target="tpu_custom_call" | custom-call | flops 402653184 | bytes 3018752 | tf_op jit(solution)/shard_map/pallas_call | solution.py:242
  19.1 4.2 %shard_map.198 = (f32[256,1024]{1,0:T(8,128)S(1)}, f32[128,1024]{1,0:T(8,128)S(1)}, bf16[128,1024]{1,0:T(8,128)(2,1)S(1)}, bf16[128,1024]{1,0:T(8,128)(2,1)S(1)}, f32[16,1024]{1,0:T(8,128)S(1)}) custom-call(bf16[128,1024]{1,0:T(8,128)(2,1)} %collective-permute-done.before, bf16[128,1024]{1,0:T(8,128)(2,1)} %multiply_convert_fusion.product, ...), custom_call_target="tpu_custom_call" | custom-call | flops 536870912 | bytes 4980736 | tf_op jit(solution)/shard_map/pallas_call | solution.py:242
  25.1 2.0 %shard_map.199.inner = f32[128,1024]{1,0:T(8,128)S(1)} custom-call(bf16[128,1024]{1,0:T(8,128)(2,1)S(1)} %get-tuple-element.38.signal, f32[256,1024]{1,0:T(8,128)S(1)} %get-tuple-element.39.li_spec, bf16[256,512]{1,0:T(8,128)(2,1)S(1)} %copy-done.3, bf16[256,768]{1,0:T(8,128)(2,1)S(1)} %copy-done.2), custom_call_target="tpu_custom_call" | custom-call | flops 402653184 | bytes 2490368 | tf_op jit(solution)/shard_map/pallas_call | solution.py:242
  27.1 11.5 %all-gather.states = f32[128,1024]{1,0:T(8,128)S(1)} all-gather(f32[16,1024]{1,0:T(8,128)S(1)} %get-tuple-element.40), channel_id=2, replica_groups=mesh['ctx'=8,'fsdp'=4] {'ctx'}, dimensions={0}, use_global_device_ids=true | all-gather | bytes 589824 | tf_op jit(solution)/shard_map/all_gather | solution.py:396
  38.6 2.6 %shard_map.200 = (f32[128,1024]{1,0:T(8,128)S(1)}, bf16[128,1024]{1,0:T(8,128)(2,1)}) custom-call(f32[8]{0:T(128)S(1)} %subtract_convert_fusion.gaps, f32[128,1024]{1,0:T(8,128)S(1)} %shard_map.199.inner, bf16[128,1024]{1,0:T(8,128)(2,1)S(1)} %copy-done.10, f32[16,1024]{1,0:T(8,128)S(1)} %get-tuple-element.71.rate, f32[16,1024]{1,0:T(8,128)S(1)} %get-tuple-element.67.coef, ...), custom_call_target="tpu_custom_call" | custom-call | flops 134217728 | bytes 2228256 | tf_op jit(solution)/shard_map/pallas_call | solution.py:242
  43.4 2.3 %collective-permute-start.2 = (bf16[128,1024]{1,0:T(8,128)(2,1)}, bf16[128,1024]{1,0:T(8,128)(2,1)}, u32[]{:S(2)}, u32[]{:S(2)}) collective-permute-start(bf16[128,1024]{1,0:T(8,128)(2,1)} %rest_0_.1), channel_id=1, source_target_pairs={{0,2},{1,3},{2,0},{3,1},{4,6},{5,7},{6,4},{7,5},{8,10},{9,11},{10,... | collective-permute-start | bytes 786440 | tf_op jit(solution)/shard_map/ppermute | solution.py:301
  45.8 9.5 %collective-permute-done.1.rest_1_ = bf16[128,1024]{1,0:T(8,128)(2,1)} collective-permute-done((bf16[128,1024]{1,0:T(8,128)(2,1)}, bf16[128,1024]{1,0:T(8,128)(2,1)}, u32[]{:S(2)}, u32[]{:S(2)}) %collective-permute-start.1) | collective-permute-done | bytes 262176 | tf_op jit(solution)/shard_map/ppermute | solution.py:301
  55.3 8.2 %collective-permute-done.3.rest_3_ = bf16[128,1024]{1,0:T(8,128)(2,1)} collective-permute-done((bf16[128,1024]{1,0:T(8,128)(2,1)}, bf16[128,1024]{1,0:T(8,128)(2,1)}, u32[]{:S(2)}, u32[]{:S(2)}) %collective-permute-start.3) | collective-permute-done | bytes 262176 | tf_op jit(solution)/shard_map/ppermute | solution.py:301
  66.6 22.1 %all_to_all.21 = bf16[8,128,512]{2,1,0:T(8,128)(2,1)} all-to-all(bf16[8,128,512]{2,1,0:T(8,128)(2,1)S(1)} %bitcast.17), channel_id=1, replica_groups=mesh['ctx'=8,'fsdp'=4] {'ctx'}, dimensions={0} | all-to-all | bytes 2097152 | tf_op jit(solution)/shard_map/all_to_all | solution.py:422
  88.7 3.4 %copy-done = bf16[4096,1024]{1,0:T(8,128)(2,1)S(1)} copy-done((bf16[4096,1024]{1,0:T(8,128)(2,1)S(1)}, bf16[4096,1024]{1,0:T(8,128)(2,1)}, u32[]{:S(2)}) %copy-start) | copy-done | bytes 8388632
  93.3 3.8 %shard_map.202 = (f32[128,1024]{1,0:T(8,128)S(1)}, f32[128,1024]{1,0:T(8,128)S(1)}, f32[16,1024]{1,0:T(8,128)S(1)}) custom-call(bf16[128,4096]{1,0:T(8,128)(2,1)S(1)} %copy-done.7, bf16[4096,1024]{1,0:T(8,128)(2,1)S(1)} %copy-done, bf16[128,1024]{1,0:T(8,128)(2,1)S(1)} %copy-done.10, f32[16,1024]{1,0:T(8,128)S(1)} %get-tuple-element.71.rate), custom_call_target="tpu_custom_call" | custom-call | flops 1073741824 | bytes 10878976 | tf_op jit(solution)/shard_map/pallas_call | solution.py:242
  101.6 2.4 %collective-permute-start.7 = (f32[16,1024]{1,0:T(8,128)S(1)}, f32[16,1024]{1,0:T(8,128)S(1)}, u32[]{:S(2)}, u32[]{:S(2)}) collective-permute-start(f32[16,1024]{1,0:T(8,128)S(1)} %add_select_fusion.1), channel_id=1, source_target_pairs={{0,24},{4,28},{8,16},{12,20},{16,8},{20,12},{24,0},{28,4},{1,25},{... | collective-permute-start | bytes 196616 | tf_op jit(solution)/shard_map/ppermute | solution.py:296
  104.0 3.4 %copy-done.1 = bf16[4096,1024]{1,0:T(8,128)(2,1)S(1)} copy-done((bf16[4096,1024]{1,0:T(8,128)(2,1)S(1)}, bf16[4096,1024]{1,0:T(8,128)(2,1)}, u32[]{:S(2)}) %copy-start.1) | copy-done | bytes 8388632
  107.4 5.0 %shard_map.203 = bf16[512,1024]{1,0:T(8,128)(2,1)} custom-call(bf16[128,1024]{1,0:T(8,128)(2,1)} %get-tuple-element.46.mixed, bf16[4096,1024]{1,0:T(8,128)(2,1)S(1)} %copy-done.1), custom_call_target="tpu_custom_call" | custom-call | flops 1073741824 | bytes 8388608 | tf_op jit(solution)/shard_map/pallas_call | solution.py:256
  112.5 2.3 %shard_map.204.inner = f32[128,1024]{1,0:T(8,128)S(1)} custom-call(f32[128,1024]{1,0:T(8,128)S(1)} %copy-done.23, f32[256,1024]{1,0:T(8,128)S(1)} %get-tuple-element.39.li_spec, bf16[256,512]{1,0:T(8,128)(2,1)S(1)} %copy-done.3, bf16[256,768]{1,0:T(8,128)(2,1)S(1)} %copy-done.2), custom_call_target="tpu_custom_call" | custom-call | flops 402653184 | bytes 2752512 | tf_op jit(solution)/shard_map/pallas_call | solution.py:242
  115.0 3.8 %shard_map.205 = (f32[128,1024]{1,0:T(8,128)}, f32[128,1024]{1,0:T(8,128)}, f32[256,1024]{1,0:T(8,128)S(1)}, f32[128,1024]{1,0:T(8,128)S(1)}) custom-call(f32[128,1024]{1,0:T(8,128)S(1)} %shard_map.204.inner, f32[16,1024]{1,0:T(8,128)S(1)} %get-tuple-element.71.rate, f32[16,1024]{1,0:T(8,128)S(1)} %get-tuple-element.67.coef, ...), custom_call_target="tpu_custom_call" | custom-call | flops 536870912 | bytes 6160384 | tf_op jit(solution)/shard_map/pallas_call | solution.py:242
  120.8 7.2 %all-to-all-start.1 = ((bf16[4,128,1024]{2,1,0:T(8,128)(2,1)}), bf16[4,128,1024]{2,1,0:T(8,128)(2,1)}, u32[]{:S(2)}, u32[]{:S(2)}) async-start(bf16[4,128,1024]{2,1,0:T(8,128)(2,1)} %bitcast.7), calls=%async_computation.1 | async-start | bytes 2097152 | tf_op jit(solution)/shard_map/all_to_all | solution.py:433
  129.4 4.4 %collective-permute-done.10 = bf16[64,1024]{1,0:T(8,128)(2,1)S(1)} collective-permute-done((bf16[64,1024]{1,0:T(8,128)(2,1)S(1)}, bf16[64,1024]{1,0:T(8,128)(2,1)S(1)}, u32[]{:S(2)}, u32[]{:S(2)}) %collective-permute-start.10) | collective-permute-done | bytes 131104 | tf_op jit(solution)/shard_map/ppermute | solution.py:296
  135.6 3.4 %collective-permute-start.8 = (bf16[128,1024]{1,0:T(8,128)(2,1)S(1)}, bf16[128,1024]{1,0:T(8,128)(2,1)S(1)}, u32[]{:S(2)}, u32[]{:S(2)}) collective-permute-start(bf16[128,1024]{1,0:T(8,128)(2,1)S(1)} %get-tuple-element.59), channel_id=1, source_target_pairs={{4,0},{8,4},{12,8},{16,12},{20,16},{24,20},{28,24},{5,1},{9,5},{13... | collective-permute-start | bytes 786440 | tf_op jit(solution)/shard_map/ppermute | solution.py:291
  140.2 4.5 %convolution_multiply_fusion = f32[512,1024]{1,0:T(8,128)} fusion(bf16[1024,512]{1,0:T(8,128)(2,1)} %bitcast.21, bf16[1024,1024]{1,0:T(8,128)(2,1)} %all-gather.6.cloned.1.call-done), kind=kOutput, calls=%fused_computation.1 | convolution fusion | flops 1074266112 | bytes 5242880 | tf_op jit(solution)/shard_map/dot_general | solution.py:498
  148.1 6.5 %all-to-all-done.1 = bf16[4,128,1024]{2,1,0:T(8,128)(2,1)} async-done(((bf16[4,128,1024]{2,1,0:T(8,128)(2,1)}), bf16[4,128,1024]{2,1,0:T(8,128)(2,1)}, u32[]{:S(2)}, u32[]{:S(2)}) %all-to-all-start.1) | async-done | bytes 1048608 | tf_op jit(solution)/shard_map/all_to_all | solution.py:433
  154.6 2.3 %convert_reduce_fusion = f32[128,1024]{1,0:T(8,128)} fusion(bf16[4,128,1024]{2,1,0:T(8,128)(2,1)} %all-to-all-done.1), kind=kLoop, calls=%fused_computation | loop fusion | flops 917504 | bytes 1572864 | tf_op jit(solution)/shard_map/reduce_sum | solution.py:434
  (103 shorter events, 26.2 us)
Async XLA Ops:
  7.2 8.8 %copy-start.3 = (bf16[256,512]{1,0:T(8,128)(2,1)S(1)}, bf16[256,512]{1,0:T(8,128)(2,1)}, u32[]{:S(2)}) copy-start(bf16[256,512]{1,0:T(8,128)(2,1)} %constant.69.clone.ahead) | copy-start | bytes 786436
  7.2 11.9 %copy-start.2 = (bf16[256,768]{1,0:T(8,128)(2,1)S(1)}, bf16[256,768]{1,0:T(8,128)(2,1)}, u32[]{:S(2)}) copy-start(bf16[256,768]{1,0:T(8,128)(2,1)} %constant.70.clone.back) | copy-start | bytes 1179652
  7.2 8.8 %copy-start.29 = (f32[1024]{0:T(1024)S(1)}, f32[1024]{0:T(1024)}, u32[]{:S(2)}) copy-start(f32[1024]{0:T(1024)} %param.22) | copy-start | bytes 12292
  7.2 11.9 %copy-start.11 = (bf16[128,1024]{1,0:T(8,128)(2,1)S(1)}, bf16[128,1024]{1,0:T(8,128)(2,1)}, u32[]{:S(2)}) copy-start(bf16[128,1024]{1,0:T(8,128)(2,1)} %query_mr.1) | copy-start | bytes 786436
  7.2 11.9 %copy-start.12 = (bf16[128,1024]{1,0:T(8,128)(2,1)S(1)}, bf16[128,1024]{1,0:T(8,128)(2,1)}, u32[]{:S(2)}) copy-start(bf16[128,1024]{1,0:T(8,128)(2,1)} %key_li.1) | copy-start | bytes 786436
  7.2 81.5 %all-gather.4.cloned.1.call-start = ((), (), s32[]{:S(2)}) async-start(), calls=%async_computation.2 | async-start | bytes 9437184 | tf_op jit(solution)/shard_map/all_gather | solution.py:365
  8.0 132.2 %all-gather.6.cloned.1.call-start = ((), (), s32[]{:S(2)}) async-start(), calls=%async_computation.3 | async-start | bytes 2359296 | tf_op jit(solution)/shard_map/all_gather | solution.py:413
  9.8 9.2 %collective-permute-start = (bf16[128,1024]{1,0:T(8,128)(2,1)}, bf16[128,1024]{1,0:T(8,128)(2,1)}, u32[]{:S(2)}, u32[]{:S(2)}) collective-permute-start(bf16[128,1024]{1,0:T(8,128)(2,1)} %multiply_convert_fusion.product), channel_id=1, source_target_pairs={{0,4},{4,8},{8,12},{12,16},{16,20},{20,24},{24,28},{1,5},{5,9},{9,... | collective-permute-start | bytes 786440 | tf_op jit(solution)/shard_map/ppermute | solution.py:291
  25.1 13.5 %copy-start.10 = (bf16[128,1024]{1,0:T(8,128)(2,1)S(1)}, bf16[128,1024]{1,0:T(8,128)(2,1)}, u32[]{:S(2)}) copy-start(bf16[128,1024]{1,0:T(8,128)(2,1)} %query.5) | copy-start | bytes 786436
  42.0 13.3 %collective-permute-start.1 = (bf16[128,1024]{1,0:T(8,128)(2,1)}, bf16[128,1024]{1,0:T(8,128)(2,1)}, u32[]{:S(2)}, u32[]{:S(2)}) collective-permute-start(bf16[128,1024]{1,0:T(8,128)(2,1)} %rest_0_.1), channel_id=1, source_target_pairs={{0,1},{1,0},{2,3},{3,2},{4,5},{5,4},{6,7},{7,6},{8,9},{9,8},{10,11... | collective-permute-start | bytes 786440 | tf_op jit(solution)/shard_map/ppermute | solution.py:301
  43.4 11.9 %collective-permute-start.2 = (bf16[128,1024]{1,0:T(8,128)(2,1)}, bf16[128,1024]{1,0:T(8,128)(2,1)}, u32[]{:S(2)}, u32[]{:S(2)}) collective-permute-start(bf16[128,1024]{1,0:T(8,128)(2,1)} %rest_0_.1), channel_id=1, source_target_pairs={{0,2},{1,3},{2,0},{3,1},{4,6},{5,7},{6,4},{7,5},{8,10},{9,11},{10,... | collective-permute-start | bytes 786440 | tf_op jit(solution)/shard_map/ppermute | solution.py:301
  45.7 17.8 %collective-permute-start.3 = (bf16[128,1024]{1,0:T(8,128)(2,1)}, bf16[128,1024]{1,0:T(8,128)(2,1)}, u32[]{:S(2)}, u32[]{:S(2)}) collective-permute-start(bf16[128,1024]{1,0:T(8,128)(2,1)} %rest_0_.1), channel_id=1, source_target_pairs={{0,3},{1,2},{2,1},{3,0},{4,7},{5,6},{6,5},{7,4},{8,11},{9,10},{10,... | collective-permute-start | bytes 786440 | tf_op jit(solution)/shard_map/ppermute | solution.py:301
  98.7 2.5 %collective-permute-start.4 = (f32[16,1024]{1,0:T(8,128)S(1)}, f32[16,1024]{1,0:T(8,128)S(1)}, u32[]{:S(2)}, u32[]{:S(2)}) collective-permute-start(f32[16,1024]{1,0:T(8,128)S(1)} %get-tuple-element.45), channel_id=1, source_target_pairs={{0,4},{4,0},{8,12},{12,8},{16,20},{20,16},{24,28},{28,24},{1,5},{5... | collective-permute-start | bytes 196616 | tf_op jit(solution)/shard_map/ppermute | solution.py:286
  101.3 13.5 %collective-permute-start.5 = (f32[16,1024]{1,0:T(8,128)S(1)}, f32[16,1024]{1,0:T(8,128)S(1)}, u32[]{:S(2)}, u32[]{:S(2)}) collective-permute-start(f32[16,1024]{1,0:T(8,128)S(1)} %add_select_fusion.1), channel_id=1, source_target_pairs={{0,8},{4,12},{8,0},{12,4},{16,24},{20,28},{24,16},{28,20},{1,9},{5... | collective-permute-start | bytes 196616 | tf_op jit(solution)/shard_map/ppermute | solution.py:296
  101.3 13.5 %collective-permute-start.6 = (f32[16,1024]{1,0:T(8,128)S(1)}, f32[16,1024]{1,0:T(8,128)S(1)}, u32[]{:S(2)}, u32[]{:S(2)}) collective-permute-start(f32[16,1024]{1,0:T(8,128)S(1)} %add_select_fusion.1), channel_id=1, source_target_pairs={{0,16},{4,20},{8,24},{12,28},{16,0},{20,4},{24,8},{28,12},{1,17},{... | collective-permute-start | bytes 196616 | tf_op jit(solution)/shard_map/ppermute | solution.py:296
  101.6 13.2 %collective-permute-start.7 = (f32[16,1024]{1,0:T(8,128)S(1)}, f32[16,1024]{1,0:T(8,128)S(1)}, u32[]{:S(2)}, u32[]{:S(2)}) collective-permute-start(f32[16,1024]{1,0:T(8,128)S(1)} %add_select_fusion.1), channel_id=1, source_target_pairs={{0,24},{4,28},{8,16},{12,20},{16,8},{20,12},{24,0},{28,4},{1,25},{... | collective-permute-start | bytes 196616 | tf_op jit(solution)/shard_map/ppermute | solution.py:296
  119.5 8.4 %copy-start.21 = (f32[128,1024]{1,0:T(8,128)S(1)}, f32[128,1024]{1,0:T(8,128)}, u32[]{:S(2)}) copy-start(f32[128,1024]{1,0:T(8,128)} %copy-done.20) | copy-start | bytes 1572868
  119.5 8.4 %collective-permute-start.9 = (f32[64,1024]{1,0:T(8,128)S(1)}, f32[64,1024]{1,0:T(8,128)}, u32[]{:S(2)}, u32[]{:S(2)}) collective-permute-start(f32[64,1024]{1,0:T(8,128)S(1)} %dynamic-slice_bitcast_fusion), channel_id=1, source_target_pairs={{0,4},{4,0},{8,12},{12,8},{16,20},{20,16},{24,28},{28,24},{1,5},{5... | collective-permute-start | bytes 786440 | tf_op jit(solution)/shard_map/ppermute | solution.py:286
  120.8 33.8 %all-to-all-start.1 = ((bf16[4,128,1024]{2,1,0:T(8,128)(2,1)}), bf16[4,128,1024]{2,1,0:T(8,128)(2,1)}, u32[]{:S(2)}, u32[]{:S(2)}) async-start(bf16[4,128,1024]{2,1,0:T(8,128)(2,1)} %bitcast.7), calls=%async_computation.1 | async-start | bytes 2097152 | tf_op jit(solution)/shard_map/all_to_all | solution.py:433
  129.0 4.8 %collective-permute-start.10 = (bf16[64,1024]{1,0:T(8,128)(2,1)S(1)}, bf16[64,1024]{1,0:T(8,128)(2,1)S(1)}, u32[]{:S(2)}, u32[]{:S(2)}) collective-permute-start(bf16[64,1024]{1,0:T(8,128)(2,1)S(1)} %fusion), channel_id=1, source_target_pairs={{0,8},{4,12},{8,0},{12,4},{16,24},{20,28},{24,16},{28,20},{1,9},{5... | collective-permute-start | bytes 393224 | tf_op jit(solution)/shard_map/ppermute | solution.py:296
  133.8 5.2 %collective-permute-start.11 = (bf16[64,1024]{1,0:T(8,128)(2,1)S(1)}, bf16[64,1024]{1,0:T(8,128)(2,1)S(1)}, u32[]{:S(2)}, u32[]{:S(2)}) collective-permute-start(bf16[64,1024]{1,0:T(8,128)(2,1)S(1)} %add_convert_fusion), channel_id=1, source_target_pairs={{0,16},{4,20},{8,24},{12,28},{16,0},{20,4},{24,8},{28,12},{1,17},{... | collective-permute-start | bytes 393224 | tf_op jit(solution)/shard_map/ppermute | solution.py:296
  135.6 9.9 %collective-permute-start.8 = (bf16[128,1024]{1,0:T(8,128)(2,1)S(1)}, bf16[128,1024]{1,0:T(8,128)(2,1)S(1)}, u32[]{:S(2)}, u32[]{:S(2)}) collective-permute-start(bf16[128,1024]{1,0:T(8,128)(2,1)S(1)} %get-tuple-element.59), channel_id=1, source_target_pairs={{4,0},{8,4},{12,8},{16,12},{20,16},{24,20},{28,24},{5,1},{9,5},{13... | collective-permute-start | bytes 786440 | tf_op jit(solution)/shard_map/ppermute | solution.py:291
  139.1 6.4 %copy-start.8 = (bf16[128,1024]{1,0:T(8,128)(2,1)S(1)}, bf16[128,1024]{1,0:T(8,128)(2,1)}, u32[]{:S(2)}) copy-start(bf16[128,1024]{1,0:T(8,128)(2,1)} %value.1) | copy-start | bytes 786436
  139.1 8.1 %collective-permute-start.12 = (f32[64,1024]{1,0:T(8,128)S(1)}, f32[64,1024]{1,0:T(8,128)S(1)}, u32[]{:S(2)}, u32[]{:S(2)}) collective-permute-start(f32[64,1024]{1,0:T(8,128)S(1)} %add_multiply_fusion), channel_id=1, source_target_pairs={{0,4},{4,0},{8,12},{12,8},{16,20},{20,16},{24,28},{28,24},{1,5},{5... | collective-permute-start | bytes 786440 | tf_op jit(solution)/shard_map/ppermute | solution.py:286
  (25 other events, 60.5 us)
Sparse Core Ops, SparseCore 0:
  9.9 57.8 all-gather.3
  70.3 32.8 all-gather.5

commit v6 on v5

--- a/solution.py
+++ b/solution.py
@@ -169,13 +169,9 @@
 
 
 def split_body(width, starts, *rest):
-    pieces, (whole, stack) = rest[:-2], rest[-2:]
-    rows = whole.shape[0]
+    pieces, whole = rest[:-1], rest[-1]
     for r, piece in enumerate(pieces):
-        span = piece.shape[1]
-        whole[:, pl.ds(pl.multiple_of(starts[r] * width, 128), span)] = piece[...]
-        for k in range(span // width):
-            stack[pl.ds(pl.multiple_of((starts[r] + k) * rows, 128), rows), :] = piece[:, k * width : (k + 1) * width]
+        whole[:, pl.ds(pl.multiple_of(starts[r] * width, 128), piece.shape[1])] = piece[...]
 
 
 def grad_gate_body(cotangent, weight, query, rate, grad_mixed, grad_out, ends):
@@ -225,7 +221,7 @@
     grad_value[...] = total * key[...].astype(F32)
 
 
-def run(body, columns, inputs, outputs, flops):
+def run(body, columns, inputs, outputs, flops, limit=12):
     tile = min(TILE, columns)
     in_specs = []
     moved = 0
@@ -245,7 +241,7 @@
         in_specs=in_specs,
         out_specs=[pl.BlockSpec((rows, tile), lambda c: (0, c)) for rows, _ in outputs],
         out_shape=[jax.ShapeDtypeStruct((rows, columns), dtype) for rows, dtype in outputs],
-        compiler_params=pltpu.CompilerParams(vmem_limit_bytes=12 * 1024 * 1024),
+        compiler_params=pltpu.CompilerParams(vmem_limit_bytes=limit * 1024 * 1024),
         cost_estimate=pl.CostEstimate(flops=flops, bytes_accessed=moved, transcendentals=0),
     )(*[array for _, array in inputs])
 
@@ -259,7 +255,7 @@
         in_specs=[pl.BlockSpec((rows, depth), lambda k: (0, 0)), pl.BlockSpec((span, depth), lambda k: (k, 0))],
         out_specs=pl.BlockSpec((rows, span), lambda k: (k, 0)),
         out_shape=jax.ShapeDtypeStruct((lines * rows, span), BF16),
-        compiler_params=pltpu.CompilerParams(vmem_limit_bytes=16 * 1024 * 1024),
+        compiler_params=pltpu.CompilerParams(vmem_limit_bytes=48 * 1024 * 1024),
         cost_estimate=pl.CostEstimate(flops=flops, bytes_accessed=2 * weight.size, transcendentals=0),
     )(x, weight)
 
@@ -367,6 +363,14 @@
     for r in range(1, line_count):
         cot_line.append((line ^ r, line_swap(cotangent, r)))
 
+    blocks = ctx_count // line_count
+    (cot_full,) = run_once(
+        functools.partial(split_body, width),
+        [jnp.stack([index * blocks for index, _ in cot_line])] + [piece for _, piece in cot_line],
+        [((rows, ctx_count * width), BF16)],
+        0,
+    )
+
     rate = 1.0 / li_time
     coef = li_residue * jnp.sqrt(-jnp.expm1(-2.0 * rate))
     back_factors = lax.optimization_barrier(direct_factors(rate, rows, here // 2, True))
@@ -393,7 +397,7 @@
         [(2 * rows, F32), (rows, F32), (rows, BF16), (rows, BF16), (rate.shape[0], F32)],
         4 * pass_flops,
     )
-    states = lax.all_gather(ends, "ctx").reshape(-1, columns)
+    states = lax.all_gather(after(ends, cot_full), "ctx").reshape(-1, columns)
     gaps = (here - 1 - jnp.arange(ctx_count, dtype=jnp.int32)).astype(F32)
     (li_inner,) = run(
         inner_body,
@@ -412,14 +416,20 @@
 
     mixed_all = lax.all_gather(mixed_li, "ctx", axis=0, tiled=True)
 
-    blocks = ctx_count // line_count
-    cot_full, stack = run_once(
-        functools.partial(split_body, width),
-        [jnp.stack([index * blocks for index, _ in cot_line])] + [piece for _, piece in cot_line],
-        [((rows, ctx_count * width), BF16), ((ctx_count * rows, width), BF16)],
-        0,
-    )
-    cot_rows = lax.all_to_all(stack, "ctx", 0, 0, tiled=True)
+    def columns_at(x, index, count):
+        return lax.dynamic_slice_in_dim(x, index * count, count, 1)
+
+    chip = here // 2
+    parts = [columns_at(cot_full, chip ^ s, 2 * width) for s in range(chips)]
+    parts = [parts[0]] + [chip_swap(after(parts[s], ends), s) for s in range(1, chips)]
+    near = [columns_at(part, core, width) for part in parts]
+    far = core_swap(jnp.concatenate([columns_at(part, 1 - core, width) for part in parts], axis=0))
+    cot_rows = jnp.zeros((rows * ctx_count, width), BF16)
+    for s in range(chips):
+        cot_rows = lax.dynamic_update_slice_in_dim(cot_rows, near[s], (here ^ (2 * s)) * rows, 0)
+        cot_rows = lax.dynamic_update_slice_in_dim(
+            cot_rows, far[s * rows : (s + 1) * rows], (here ^ (2 * s) ^ 1) * rows, 0
+        )
 
     share_flops = 2 * rows * columns * ctx_count * width
     grad_mixed, grad_li_out, back_ends = run(
@@ -428,6 +438,7 @@
         [("whole", after(cot_full, mixed_li, cot_rows)), tile(weight_rows), tile(query_li), tile(rate)],
         [(rows, F32), (rows, F32), (rate.shape[0], F32)],
         share_flops,
+        48,
     )
     out_stack = run_lines(out_body, line_count, after(mixed_li, back_ends), weight_rows, share_flops)
     out_parts = lax.all_to_all(out_stack, "fsdp", 0, 0, tiled=True).reshape(line_count, rows, -1)

time: 165 us -> 177 us (1.073)
  blocking collectives: 33.6 us -> 9.69 us
  local copies, waits for them, and re-layouts: 16 us -> 35.4 us
  waiting for transfers between devices: 30.2 us -> 37.2 us
  starting transfers between devices: 26.2 us -> 31.2 us
  Pallas kernels: 30.1 us -> 32.7 us
    all_to_all x1 -> x0, blocking collectives: 22.1 us -> none  [shards(): cot_rows = lax.all_to_all(stack, 'ctx', 0, 0, tiled=True)]
    ppermute x5 -> x8, waiting for transfers between devices: 4.4 us -> 23 us  [chip_swap(): return lax.ppermute(x, 'ctx', [(i, i ^ 2 * by) for i in range(size)])]
    ppermute x3, waiting for transfers between devices: 17.7 us -> 4.51 us  [line_swap(): return lax.ppermute(x, 'fsdp', [(i, i ^ by) for i in range(size)])]
    dynamic_update_slice x0 -> x7, local copies, waits for them, and re-layouts: none -> 11 us  [the longest x4 6.26 us: shards(): lax.dynamic_update_slice_in_dim(cot_rows, far[s * rows:(s + 1) * rows], (...]
    unnamed x66 -> x104, local copies, waits for them, and re-layouts: 16 us -> 19.8 us
    dynamic_slice x0 -> x5, local copies, waits for them, and re-layouts: none -> 3.53 us  [columns_at(): return lax.dynamic_slice_in_dim(x, index * count, count, 1)]
    ppermute x5 -> x8, starting transfers between devices: 3.56 us -> 6.47 us  [chip_swap(): return lax.ppermute(x, 'ctx', [(i, i ^ 2 * by) for i in range(size)])]
    ppermute x3 -> x4, starting transfers between devices: 3.91 us -> 6.67 us  [core_swap(): return lax.ppermute(x, 'ctx', [(i, i ^ 1) for i in range(size)])]
  transfers between devices with their start and end apart: 16 -> 20, of which waited for: 5 -> 7; matrix products, arithmetic and copies ran while one was open for 7% -> 16% of each run, Pallas kernels for 18% -> 19%
where the time goes in v6:
time: 177 us; the launch traced here: 175 us
  waiting for transfers between devices  37.2 us (21%)
  local copies, waits for them, and re-layouts  35.4 us (20%)
  Pallas kernels  32.7 us (18%)
  starting transfers between devices  31.2 us (18%)
  between operations  14.7 us (8%)
  blocking collectives  9.69 us (5%)
  other arithmetic  9.42 us (5%)
  matrix products  4.51 us (3%)
    pallas_call x9, Pallas kernels, run(): pl.pallas_call(body, grid=(columns // tile,), in_specs=in_specs, out_spec...  24.9 us
    ppermute x8, waiting for transfers between devices, chip_swap(): return lax.ppermute(x, 'ctx', [(i, i ^ 2 * by) for i in range(size)])  23 us
    unnamed x104, local copies, waits for them, and re-layouts  19.8 us
    all_gather x1, blocking collectives, shards(): states = lax.all_gather(after(ends, cot_full), 'ctx').reshape(-1, columns)  9.69 us
    ppermute x2, starting transfers between devices, shifted(): lax.ppermute(x, 'ctx', [(i, i + by) for i in range(size) if 0 <= i + by <...  7.66 us
    all_to_all x1, waiting for transfers between devices, shards(): lax.all_to_all(out_stack, 'fsdp', 0, 0, tiled=True)  7.62 us
    pallas_call x1, Pallas kernels, run_lines(): pl.pallas_call(body, grid=(lines,), in_specs=[pl.BlockSpec((rows, depth),...  6.74 us
    ppermute x4, starting transfers between devices, core_swap(): return lax.ppermute(x, 'ctx', [(i, i ^ 1) for i in range(size)])  6.67 us
  transfers between devices with their start and end apart: 20, of which 7 were waited for; matrix products, arithmetic and copies ran while one was open for 16% of the time, Pallas kernels for 19%

profile of v6, /device:TPU:1, one launch (start us, length us, event | category | flops | bytes accessed | tf_op | source)
XLA Modules:
  0.0 174.8 jit_solution(1931977338378647414)
XLA Ops:
  8.0 2.2 %collective-permute-start.1 = (bf16[128,1024]{1,0:T(8,128)(2,1)}, bf16[128,1024]{1,0:T(8,128)(2,1)S(1)}, u32[]{:S(2)}, u32[]{:S(2)}) collective-permute-start(bf16[128,1024]{1,0:T(8,128)(2,1)} %rest_0_.1), channel_id=1, source_target_pairs={{0,1},{1,0},{2,3},{3,2},{4,5},{5,4},{6,7},{7,6},{8,9},{9,8},{10,11... | collective-permute-start | bytes 786440 | tf_op jit(solution)/shard_map/ppermute | solution.py:297
  10.2 2.3 %collective-permute-start.2 = (bf16[128,1024]{1,0:T(8,128)(2,1)}, bf16[128,1024]{1,0:T(8,128)(2,1)S(1)}, u32[]{:S(2)}, u32[]{:S(2)}) collective-permute-start(bf16[128,1024]{1,0:T(8,128)(2,1)} %rest_0_.1), channel_id=1, source_target_pairs={{0,2},{1,3},{2,0},{3,1},{4,6},{5,7},{6,4},{7,5},{8,10},{9,11},{10,... | collective-permute-start | bytes 786440 | tf_op jit(solution)/shard_map/ppermute | solution.py:297
  12.5 1.8 %multiply_convert_fusion.product = bf16[128,1024]{1,0:T(8,128)(2,1)} fusion(bf16[128,1024]{1,0:T(8,128)(2,1)} %value.1, bf16[128,1024]{1,0:T(8,128)(2,1)} %key.3), kind=kLoop, calls=%fused_computation.4 | loop fusion | flops 524288 | bytes 786432 | tf_op jit(solution)/shard_map/convert_element_type | solution.py:359
  14.3 4.4 %collective-permute-start = (bf16[128,1024]{1,0:T(8,128)(2,1)}, bf16[128,1024]{1,0:T(8,128)(2,1)}, u32[]{:S(2)}, u32[]{:S(2)}) collective-permute-start(bf16[128,1024]{1,0:T(8,128)(2,1)} %multiply_convert_fusion.product), channel_id=1, source_target_pairs={{0,4},{4,8},{8,12},{12,16},{16,20},{20,24},{24,28},{1,5},{5,9},{9,... | collective-permute-start | bytes 786440 | tf_op jit(solution)/shard_map/ppermute | solution.py:287
  21.6 2.0 %shard_map.197 = (f32[256,1024]{1,0:T(8,128)S(1)}, f32[256,1024]{1,0:T(8,128)S(1)}) custom-call(f32[128,1024]{1,0:T(8,128)S(1)} %copy-done.45, f32[16,1024]{1,0:T(8,128)S(1)} %get-tuple-element.80.rate, f32[16,1024]{1,0:T(8,128)S(1)} %get-tuple-element.76.coef, f32[1,1024]{1,0:T(1,128)S(1)} %bitcast.17, bf16[256,512]{1,0:T(8,128)(2,1)S(1)} %copy-done.1), custom_call_target="tpu_custom_call" | custom-call | flops 402653184 | bytes 3018752 | tf_op jit(solution)/shard_map/pallas_call | solution.py:238
  25.2 4.5 %collective-permute-done.3.rest_3_ = bf16[128,1024]{1,0:T(8,128)(2,1)} collective-permute-done((bf16[128,1024]{1,0:T(8,128)(2,1)}, bf16[128,1024]{1,0:T(8,128)(2,1)}, u32[]{:S(2)}, u32[]{:S(2)}) %collective-permute-start.3) | collective-permute-done | bytes 262176 | tf_op jit(solution)/shard_map/ppermute | solution.py:297
  36.5 4.2 %shard_map.198 = (f32[256,1024]{1,0:T(8,128)S(1)}, f32[128,1024]{1,0:T(8,128)S(1)}, bf16[128,1024]{1,0:T(8,128)(2,1)S(1)}, bf16[128,1024]{1,0:T(8,128)(2,1)S(1)}, f32[16,1024]{1,0:T(8,128)S(1)}) custom-call(bf16[128,1024]{1,0:T(8,128)(2,1)} %collective-permute-done.before, bf16[128,1024]{1,0:T(8,128)(2,1)} %multiply_convert_fusion.product, ...), custom_call_target="tpu_custom_call" | custom-call | flops 536870912 | bytes 4980736 | tf_op jit(solution)/shard_map/pallas_call | solution.py:238
  45.3 2.2 %collective-permute-start.6 = (bf16[128,1024]{1,0:T(8,128)(2,1)}, bf16[128,1024]{1,0:T(8,128)(2,1)}, u32[]{:S(2)}, u32[]{:S(2)}) collective-permute-start(bf16[128,1024]{1,0:T(8,128)(2,1)} %get-tuple-element.47), channel_id=1, source_target_pairs={{0,24},{4,28},{8,16},{12,20},{16,8},{20,12},{24,0},{28,4},{1,25},{... | collective-permute-start | bytes 786440 | tf_op jit(solution)/shard_map/ppermute | solution.py:292
  49.9 9.2 %collective-permute-done.6 = bf16[128,1024]{1,0:T(8,128)(2,1)} collective-permute-done((bf16[128,1024]{1,0:T(8,128)(2,1)}, bf16[128,1024]{1,0:T(8,128)(2,1)}, u32[]{:S(2)}, u32[]{:S(2)}) %collective-permute-start.6) | collective-permute-done | bytes 262176 | tf_op jit(solution)/shard_map/ppermute | solution.py:292
  60.0 6.0 %collective-permute-done.5 = bf16[128,1024]{1,0:T(8,128)(2,1)} collective-permute-done((bf16[128,1024]{1,0:T(8,128)(2,1)}, bf16[128,1024]{1,0:T(8,128)(2,1)}, u32[]{:S(2)}, u32[]{:S(2)}) %collective-permute-start.5) | collective-permute-done | bytes 262176 | tf_op jit(solution)/shard_map/ppermute | solution.py:292
  66.9 3.4 %collective-permute-done.4 = bf16[128,1024]{1,0:T(8,128)(2,1)S(1)} collective-permute-done((bf16[128,1024]{1,0:T(8,128)(2,1)}, bf16[128,1024]{1,0:T(8,128)(2,1)S(1)}, u32[]{:S(2)}, u32[]{:S(2)}) %collective-permute-start.4) | collective-permute-done | bytes 262176 | tf_op jit(solution)/shard_map/ppermute | solution.py:292
  71.2 4.5 %collective-permute-start.7 = (bf16[512,512]{1,0:T(8,128)(2,1)}, bf16[512,512]{1,0:T(8,128)(2,1)}, u32[]{:S(2)}, u32[]{:S(2)}) collective-permute-start(bf16[512,512]{1,0:T(8,128)(2,1)} %pad_maximum_fusion), channel_id=1, source_target_pairs={{0,4},{4,0},{8,12},{12,8},{16,20},{20,16},{24,28},{28,24},{1,5},{5... | collective-permute-start | bytes 1572872 | tf_op jit(solution)/shard_map/ppermute | solution.py:282
  77.7 2.0 %shard_map.199.inner = f32[128,1024]{1,0:T(8,128)S(1)} custom-call(bf16[128,1024]{1,0:T(8,128)(2,1)S(1)} %copy-done.41, f32[256,1024]{1,0:T(8,128)S(1)} %get-tuple-element.41.li_spec, bf16[256,512]{1,0:T(8,128)(2,1)S(1)} %copy-done.3, bf16[256,768]{1,0:T(8,128)(2,1)S(1)} %copy-done), custom_call_target="tpu_custom_call" | custom-call | flops 402653184 | bytes 2490368 | tf_op jit(solution)/shard_map/pallas_call | solution.py:238
  79.7 9.7 %all-gather.states = f32[128,1024]{1,0:T(8,128)S(1)} all-gather(f32[16,1024]{1,0:T(8,128)S(1)} %copy-done.44), channel_id=2, replica_groups=mesh['ctx'=8,'fsdp'=4] {'ctx'}, dimensions={0}, use_global_device_ids=true | all-gather | bytes 589824 | tf_op jit(solution)/shard_map/all_gather | solution.py:400
  105.4 5.9 %shard_map.202 = (f32[128,1024]{1,0:T(8,128)S(1)}, f32[128,1024]{1,0:T(8,128)S(1)}, f32[16,1024]{1,0:T(8,128)}) custom-call(bf16[128,4096]{1,0:T(8,128)(2,1)S(1)} %shard_map.200.cotangent, bf16[4096,1024]{1,0:T(8,128)(2,1)} %all-gather.4.cloned.1.call-done.weight, bf16[128,1024]{1,0:T(8,128)(2,1)S(1)} %copy-done.17, f32[16,1024]{1,0:T(8,128)S(1)} %copy-done.8), custom_call_target="tpu_custom_call" | custom-call | flops 1073741824 | bytes 10878976 | tf_op jit(solution)/shard_map/pallas_call | solution.py:238
  118.9 6.7 %shard_map.203 = bf16[512,1024]{1,0:T(8,128)(2,1)} custom-call(bf16[128,1024]{1,0:T(8,128)(2,1)S(1)} %copy-done.15, bf16[4096,1024]{1,0:T(8,128)(2,1)} %all-gather.4.cloned.1.call-done.weight), custom_call_target="tpu_custom_call" | custom-call | flops 1073741824 | bytes 8388608 | tf_op jit(solution)/shard_map/pallas_call | solution.py:252
  125.7 2.3 %shard_map.204.inner = f32[128,1024]{1,0:T(8,128)S(1)} custom-call(f32[128,1024]{1,0:T(8,128)S(1)} %copy-done.32, f32[256,1024]{1,0:T(8,128)S(1)} %get-tuple-element.41.li_spec, bf16[256,512]{1,0:T(8,128)(2,1)S(1)} %copy-done.4, bf16[256,768]{1,0:T(8,128)(2,1)S(1)} %copy-done), custom_call_target="tpu_custom_call" | custom-call | flops 402653184 | bytes 2752512 | tf_op jit(solution)/shard_map/pallas_call | solution.py:238
  128.3 3.8 %shard_map.205 = (f32[128,1024]{1,0:T(8,128)}, f32[128,1024]{1,0:T(8,128)}, f32[256,1024]{1,0:T(8,128)S(1)}, f32[128,1024]{1,0:T(8,128)S(1)}) custom-call(f32[128,1024]{1,0:T(8,128)S(1)} %shard_map.204.inner, f32[16,1024]{1,0:T(8,128)S(1)} %copy-done.9, f32[16,1024]{1,0:T(8,128)S(1)} %copy-done.24, f32[16,1024]{1,0:T(8,128)S(1)} %add_select_fusion.entering, ...), custom_call_target="tpu_custom_call" | custom-call | flops 536870912 | bytes 6160384 | tf_op jit(solution)/shard_map/pallas_call | solution.py:238
  133.1 5.8 %all-to-all-start = ((bf16[4,128,1024]{2,1,0:T(8,128)(2,1)}), bf16[4,128,1024]{2,1,0:T(8,128)(2,1)}, u32[]{:S(2)}, u32[]{:S(2)}) async-start(bf16[4,128,1024]{2,1,0:T(8,128)(2,1)} %bitcast.5), calls=%async_computation | async-start | bytes 2097152 | tf_op jit(solution)/shard_map/all_to_all | solution.py:444
  139.5 4.4 %collective-permute-done.14 = bf16[64,1024]{1,0:T(8,128)(2,1)S(1)} collective-permute-done((bf16[64,1024]{1,0:T(8,128)(2,1)S(1)}, bf16[64,1024]{1,0:T(8,128)(2,1)S(1)}, u32[]{:S(2)}, u32[]{:S(2)}) %collective-permute-start.14) | collective-permute-done | bytes 131104 | tf_op jit(solution)/shard_map/ppermute | solution.py:292
  145.9 3.2 %collective-permute-start.12 = (bf16[128,1024]{1,0:T(8,128)(2,1)S(1)}, bf16[128,1024]{1,0:T(8,128)(2,1)S(1)}, u32[]{:S(2)}, u32[]{:S(2)}) collective-permute-start(bf16[128,1024]{1,0:T(8,128)(2,1)S(1)} %get-tuple-element.63), channel_id=1, source_target_pairs={{4,0},{8,4},{12,8},{16,12},{20,16},{24,20},{28,24},{5,1},{9,5},{13... | collective-permute-start | bytes 786440 | tf_op jit(solution)/shard_map/ppermute | solution.py:287
  150.2 4.5 %convolution_multiply_fusion = f32[512,1024]{1,0:T(8,128)} fusion(bf16[1024,512]{1,0:T(8,128)(2,1)} %slice_dynamic-update-slice_fusion, bf16[1024,1024]{1,0:T(8,128)(2,1)} %all-gather.6.cloned.1.call-done), kind=kOutput, calls=%fused_computation.1 | convolution fusion | flops 1074266112 | bytes 5242880 | tf_op jit(solution)/shard_map/dot_general | solution.py:509
  158.1 7.6 %all-to-all-done = bf16[4,128,1024]{2,1,0:T(8,128)(2,1)} async-done(((bf16[4,128,1024]{2,1,0:T(8,128)(2,1)}), bf16[4,128,1024]{2,1,0:T(8,128)(2,1)}, u32[]{:S(2)}, u32[]{:S(2)}) %all-to-all-start) | async-done | bytes 1048608 | tf_op jit(solution)/shard_map/all_to_all | solution.py:444
  165.7 2.3 %convert_reduce_fusion = f32[128,1024]{1,0:T(8,128)} fusion(bf16[4,128,1024]{2,1,0:T(8,128)(2,1)} %all-to-all-done), kind=kLoop, calls=%fused_computation | loop fusion | flops 917504 | bytes 1572864 | tf_op jit(solution)/shard_map/reduce_sum | solution.py:445
  (162 shorter events, 55.2 us)
Async XLA Ops:
  7.2 13.3 %copy-start.1 = (bf16[256,512]{1,0:T(8,128)(2,1)S(1)}, bf16[256,512]{1,0:T(8,128)(2,1)}, u32[]{:S(2)}) copy-start(bf16[256,512]{1,0:T(8,128)(2,1)} %constant.104.clone.ahead) | copy-start | bytes 786436
  7.2 13.3 %copy-start.46 = (f32[1024]{0:T(1024)S(1)}, f32[1024]{0:T(1024)}, u32[]{:S(2)}) copy-start(f32[1024]{0:T(1024)} %param.22) | copy-start | bytes 12292
  7.2 96.4 %all-gather.4.cloned.1.call-start = ((), (), s32[]{:S(2)}) async-start(), calls=%async_computation.1 | async-start | bytes 9437184 | tf_op jit(solution)/shard_map/all_gather | solution.py:361
  7.9 142.3 %all-gather.6.cloned.1.call-start = ((), (), s32[]{:S(2)}) async-start(), calls=%async_computation.2 | async-start | bytes 2359296 | tf_op jit(solution)/shard_map/all_gather | solution.py:417
  8.0 15.8 %collective-permute-start.1 = (bf16[128,1024]{1,0:T(8,128)(2,1)}, bf16[128,1024]{1,0:T(8,128)(2,1)S(1)}, u32[]{:S(2)}, u32[]{:S(2)}) collective-permute-start(bf16[128,1024]{1,0:T(8,128)(2,1)} %rest_0_.1), channel_id=1, source_target_pairs={{0,1},{1,0},{2,3},{3,2},{4,5},{5,4},{6,7},{7,6},{8,9},{9,8},{10,11... | collective-permute-start | bytes 786440 | tf_op jit(solution)/shard_map/ppermute | solution.py:297
  10.2 14.3 %collective-permute-start.2 = (bf16[128,1024]{1,0:T(8,128)(2,1)}, bf16[128,1024]{1,0:T(8,128)(2,1)S(1)}, u32[]{:S(2)}, u32[]{:S(2)}) collective-permute-start(bf16[128,1024]{1,0:T(8,128)(2,1)} %rest_0_.1), channel_id=1, source_target_pairs={{0,2},{1,3},{2,0},{3,1},{4,6},{5,7},{6,4},{7,5},{8,10},{9,11},{10,... | collective-permute-start | bytes 786440 | tf_op jit(solution)/shard_map/ppermute | solution.py:297
  12.5 17.2 %collective-permute-start.3 = (bf16[128,1024]{1,0:T(8,128)(2,1)}, bf16[128,1024]{1,0:T(8,128)(2,1)}, u32[]{:S(2)}, u32[]{:S(2)}) collective-permute-start(bf16[128,1024]{1,0:T(8,128)(2,1)} %rest_0_.1), channel_id=1, source_target_pairs={{0,3},{1,2},{2,1},{3,0},{4,7},{5,6},{6,5},{7,4},{8,11},{9,10},{10,... | collective-permute-start | bytes 786440 | tf_op jit(solution)/shard_map/ppermute | solution.py:297
  14.3 19.3 %collective-permute-start = (bf16[128,1024]{1,0:T(8,128)(2,1)}, bf16[128,1024]{1,0:T(8,128)(2,1)}, u32[]{:S(2)}, u32[]{:S(2)}) collective-permute-start(bf16[128,1024]{1,0:T(8,128)(2,1)} %multiply_convert_fusion.product), channel_id=1, source_target_pairs={{0,4},{4,8},{8,12},{12,16},{16,20},{20,24},{24,28},{1,5},{5,9},{9,... | collective-permute-start | bytes 786440 | tf_op jit(solution)/shard_map/ppermute | solution.py:287
  18.8 14.8 %copy-start = (bf16[256,768]{1,0:T(8,128)(2,1)S(1)}, bf16[256,768]{1,0:T(8,128)(2,1)}, u32[]{:S(2)}) copy-start(bf16[256,768]{1,0:T(8,128)(2,1)} %constant.105.clone.back) | copy-start | bytes 1179652
  45.3 13.7 %collective-permute-start.6 = (bf16[128,1024]{1,0:T(8,128)(2,1)}, bf16[128,1024]{1,0:T(8,128)(2,1)}, u32[]{:S(2)}, u32[]{:S(2)}) collective-permute-start(bf16[128,1024]{1,0:T(8,128)(2,1)} %get-tuple-element.47), channel_id=1, source_target_pairs={{0,24},{4,28},{8,16},{12,20},{16,8},{20,12},{24,0},{28,4},{1,25},{... | collective-permute-start | bytes 786440 | tf_op jit(solution)/shard_map/ppermute | solution.py:292
  47.5 18.5 %collective-permute-start.5 = (bf16[128,1024]{1,0:T(8,128)(2,1)}, bf16[128,1024]{1,0:T(8,128)(2,1)}, u32[]{:S(2)}, u32[]{:S(2)}) collective-permute-start(bf16[128,1024]{1,0:T(8,128)(2,1)} %get-tuple-element.46), channel_id=1, source_target_pairs={{0,16},{4,20},{8,24},{12,28},{16,0},{20,4},{24,8},{28,12},{1,17},{... | collective-permute-start | bytes 786440 | tf_op jit(solution)/shard_map/ppermute | solution.py:292
  47.7 22.6 %collective-permute-start.4 = (bf16[128,1024]{1,0:T(8,128)(2,1)}, bf16[128,1024]{1,0:T(8,128)(2,1)S(1)}, u32[]{:S(2)}, u32[]{:S(2)}) collective-permute-start(bf16[128,1024]{1,0:T(8,128)(2,1)} %get-tuple-element.45), channel_id=1, source_target_pairs={{0,8},{4,12},{8,0},{12,4},{16,24},{20,28},{24,16},{28,20},{1,9},{5... | collective-permute-start | bytes 786440 | tf_op jit(solution)/shard_map/ppermute | solution.py:292
  71.2 21.4 %collective-permute-start.7 = (bf16[512,512]{1,0:T(8,128)(2,1)}, bf16[512,512]{1,0:T(8,128)(2,1)}, u32[]{:S(2)}, u32[]{:S(2)}) collective-permute-start(bf16[512,512]{1,0:T(8,128)(2,1)} %pad_maximum_fusion), channel_id=1, source_target_pairs={{0,4},{4,0},{8,12},{12,8},{16,20},{20,16},{24,28},{28,24},{1,5},{5... | collective-permute-start | bytes 1572872 | tf_op jit(solution)/shard_map/ppermute | solution.py:282
  77.6 11.7 %copy-start.23 = (f32[16,1024]{1,0:T(8,128)S(1)}, f32[16,1024]{1,0:T(8,128)}, u32[]{:S(2)}) copy-start(f32[16,1024]{1,0:T(8,128)} %copy-done.22) | copy-start | bytes 196612
  112.9 1.5 collective-permute-start.8
  115.2 12.8 %collective-permute-start.10 = (f32[16,1024]{1,0:T(8,128)S(1)}, f32[16,1024]{1,0:T(8,128)S(1)}, u32[]{:S(2)}, u32[]{:S(2)}) collective-permute-start(f32[16,1024]{1,0:T(8,128)S(1)} %add_select_fusion.1), channel_id=1, source_target_pairs={{0,16},{4,20},{8,24},{12,28},{16,0},{20,4},{24,8},{28,12},{1,17},{... | collective-permute-start | bytes 196616 | tf_op jit(solution)/shard_map/ppermute | solution.py:292
  115.6 12.5 %collective-permute-start.11 = (f32[16,1024]{1,0:T(8,128)S(1)}, f32[16,1024]{1,0:T(8,128)S(1)}, u32[]{:S(2)}, u32[]{:S(2)}) collective-permute-start(f32[16,1024]{1,0:T(8,128)S(1)} %add_select_fusion.1), channel_id=1, source_target_pairs={{0,24},{4,28},{8,16},{12,20},{16,8},{20,12},{24,0},{28,4},{1,25},{... | collective-permute-start | bytes 196616 | tf_op jit(solution)/shard_map/ppermute | solution.py:292
  116.8 11.3 %collective-permute-start.9 = (f32[16,1024]{1,0:T(8,128)S(1)}, f32[16,1024]{1,0:T(8,128)S(1)}, u32[]{:S(2)}, u32[]{:S(2)}) collective-permute-start(f32[16,1024]{1,0:T(8,128)S(1)} %add_select_fusion.1), channel_id=1, source_target_pairs={{0,8},{4,12},{8,0},{12,4},{16,24},{20,28},{24,16},{28,20},{1,9},{5... | collective-permute-start | bytes 196616 | tf_op jit(solution)/shard_map/ppermute | solution.py:292
  132.0 6.9 %collective-permute-start.13 = (f32[64,1024]{1,0:T(8,128)S(1)}, f32[64,1024]{1,0:T(8,128)S(1)}, u32[]{:S(2)}, u32[]{:S(2)}) collective-permute-start(f32[64,1024]{1,0:T(8,128)S(1)} %dynamic-slice_bitcast_fusion), channel_id=1, source_target_pairs={{0,4},{4,0},{8,12},{12,8},{16,20},{20,16},{24,28},{28,24},{1,5},{5... | collective-permute-start | bytes 786440 | tf_op jit(solution)/shard_map/ppermute | solution.py:282
  133.1 32.6 %all-to-all-start = ((bf16[4,128,1024]{2,1,0:T(8,128)(2,1)}), bf16[4,128,1024]{2,1,0:T(8,128)(2,1)}, u32[]{:S(2)}, u32[]{:S(2)}) async-start(bf16[4,128,1024]{2,1,0:T(8,128)(2,1)} %bitcast.5), calls=%async_computation | async-start | bytes 2097152 | tf_op jit(solution)/shard_map/all_to_all | solution.py:444
  139.0 5.0 %collective-permute-start.14 = (bf16[64,1024]{1,0:T(8,128)(2,1)S(1)}, bf16[64,1024]{1,0:T(8,128)(2,1)S(1)}, u32[]{:S(2)}, u32[]{:S(2)}) collective-permute-start(bf16[64,1024]{1,0:T(8,128)(2,1)S(1)} %fusion), channel_id=1, source_target_pairs={{0,8},{4,12},{8,0},{12,4},{16,24},{20,28},{24,16},{28,20},{1,9},{5... | collective-permute-start | bytes 393224 | tf_op jit(solution)/shard_map/ppermute | solution.py:292
  144.0 5.2 %collective-permute-start.15 = (bf16[64,1024]{1,0:T(8,128)(2,1)S(1)}, bf16[64,1024]{1,0:T(8,128)(2,1)S(1)}, u32[]{:S(2)}, u32[]{:S(2)}) collective-permute-start(bf16[64,1024]{1,0:T(8,128)(2,1)S(1)} %add_convert_fusion), channel_id=1, source_target_pairs={{0,16},{4,20},{8,24},{12,28},{16,0},{20,4},{24,8},{28,12},{1,17},{... | collective-permute-start | bytes 393224 | tf_op jit(solution)/shard_map/ppermute | solution.py:292
  145.9 9.6 %collective-permute-start.12 = (bf16[128,1024]{1,0:T(8,128)(2,1)S(1)}, bf16[128,1024]{1,0:T(8,128)(2,1)S(1)}, u32[]{:S(2)}, u32[]{:S(2)}) collective-permute-start(bf16[128,1024]{1,0:T(8,128)(2,1)S(1)} %get-tuple-element.63), channel_id=1, source_target_pairs={{4,0},{8,4},{12,8},{16,12},{20,16},{24,20},{28,24},{5,1},{9,5},{13... | collective-permute-start | bytes 786440 | tf_op jit(solution)/shard_map/ppermute | solution.py:287
  149.3 8.0 %collective-permute-start.16 = (f32[64,1024]{1,0:T(8,128)S(1)}, f32[64,1024]{1,0:T(8,128)S(1)}, u32[]{:S(2)}, u32[]{:S(2)}) collective-permute-start(f32[64,1024]{1,0:T(8,128)S(1)} %add_multiply_fusion), channel_id=1, source_target_pairs={{0,4},{4,0},{8,12},{12,8},{16,20},{20,16},{24,28},{28,24},{1,5},{5... | collective-permute-start | bytes 786440 | tf_op jit(solution)/shard_map/ppermute | solution.py:282
  (48 other events, 146.6 us)
Sparse Core Ops, SparseCore 0:
  9.9 69.2 all-gather.3
  92.7 32.1 all-gather.5

commit v7 on v5

--- a/solution.py
+++ b/solution.py
@@ -168,28 +168,15 @@
     mixed[...] = (query[...].astype(F32) * total).astype(BF16)
 
 
-def split_body(width, starts, *rest):
-    pieces, (whole, stack) = rest[:-2], rest[-2:]
-    rows = whole.shape[0]
-    for r, piece in enumerate(pieces):
-        span = piece.shape[1]
-        whole[:, pl.ds(pl.multiple_of(starts[r] * width, 128), span)] = piece[...]
-        for k in range(span // width):
-            stack[pl.ds(pl.multiple_of((starts[r] + k) * rows, 128), rows), :] = piece[:, k * width : (k + 1) * width]
-
-
-def grad_gate_body(cotangent, weight, query, rate, grad_mixed, grad_out, ends):
-    total = jnp.dot(cotangent[...], weight[...], preferred_element_type=F32)
+def grad_gate_body(count, own, query, rate, *rest):
+    parts, (grad_mixed, grad_out, ends) = rest[:count], rest[count:]
+    total = own[...]
+    for part in parts:
+        total = total + part[...].astype(F32)
     grad_mixed[...] = total
     gated = total * query[...].astype(F32)
     grad_out[...] = gated
     ends[...] = fold_modes(gated, rate[...], True)
-
-
-def out_body(mixed, weight, stack):
-    stack[...] = lax.dot_general(
-        mixed[...], weight[...], (((1,), (1,)), ((), ())), preferred_element_type=F32
-    ).astype(BF16)
 
 
 def grad_inner_body(grad_out, li_spec, ahead, back, inner):
@@ -250,35 +237,9 @@
     )(*[array for _, array in inputs])
 
 
-def run_lines(body, lines, x, weight, flops):
-    rows, depth = x.shape
-    span = weight.shape[0] // lines
-    return pl.pallas_call(
-        body,
-        grid=(lines,),
-        in_specs=[pl.BlockSpec((rows, depth), lambda k: (0, 0)), pl.BlockSpec((span, depth), lambda k: (k, 0))],
-        out_specs=pl.BlockSpec((rows, span), lambda k: (k, 0)),
-        out_shape=jax.ShapeDtypeStruct((lines * rows, span), BF16),
-        compiler_params=pltpu.CompilerParams(vmem_limit_bytes=16 * 1024 * 1024),
-        cost_estimate=pl.CostEstimate(flops=flops, bytes_accessed=2 * weight.size, transcendentals=0),
-    )(x, weight)
-
-
-def run_once(body, inputs, outputs, flops):
-    in_specs = [pl.BlockSpec(memory_space=pltpu.VMEM)] * (len(inputs) - 1)
-    if inputs[0] is None:
-        inputs = inputs[1:]
-    else:
-        in_specs = [pl.BlockSpec(memory_space=pltpu.SMEM)] + in_specs
-    moved = sum(math.prod(array.shape) * array.dtype.itemsize for array in inputs)
-    return pl.pallas_call(
-        body,
-        in_specs=in_specs,
-        out_specs=[pl.BlockSpec(memory_space=pltpu.VMEM)] * len(outputs),
-        out_shape=[jax.ShapeDtypeStruct(shape, dtype) for shape, dtype in outputs],
-        compiler_params=pltpu.CompilerParams(vmem_limit_bytes=24 * 1024 * 1024),
-        cost_estimate=pl.CostEstimate(flops=flops, bytes_accessed=moved, transcendentals=0),
-    )(*inputs)
+def chip_swap(x, by):
+    size = lax.axis_size("ctx")
+    return lax.ppermute(x, "ctx", [(i, i ^ (2 * by)) for i in range(size)])
 
 
 def core_swap(x):
@@ -291,18 +252,22 @@
     return lax.ppermute(x, "ctx", [(i, i + by) for i in range(size) if 0 <= i + by < size])
 
 
-def chip_swap(x, by):
-    size = lax.axis_size("ctx")
-    return lax.ppermute(x, "ctx", [(i, i ^ (2 * by)) for i in range(size)])
-
-
-def line_swap(x, by):
-    size = lax.axis_size("fsdp")
-    return lax.ppermute(x, "fsdp", [(i, i ^ by) for i in range(size)])
-
-
-def columns_to_rows(x, count):
-    return jnp.concatenate(jnp.split(x, count, axis=1), axis=0)
+def columns_at(x, index, width):
+    return lax.dynamic_slice_in_dim(x, index * width, width, 1)
+
+
+def placed(pieces):
+    width = pieces[0][1].shape[1]
+    whole = jnp.zeros((pieces[0][1].shape[0], width * len(pieces)), pieces[0][1].dtype)
+    for index, piece in pieces:
+        whole = lax.dynamic_update_slice_in_dim(whole, piece, index * width, 1)
+    return whole
+
+
+def pair_sum(values):
+    while len(values) > 1:
+        values = [values[k] + values[k + 1] for k in range(0, len(values), 2)]
+    return values[0]
 
 
 def after(x, *others):
@@ -347,11 +312,12 @@
     line_count = lax.axis_size("fsdp")
     chips = ctx_count // 2
     here = lax.axis_index("ctx")
-    core = here % 2
+    chip, core = here // 2, here % 2
     line = lax.axis_index("fsdp")
     grad_scale = 1.0 / math.sqrt(rows * ctx_count)
     tables = {name: jnp.asarray(table) for name, table in dft_tables(rows).items()}
     width = out_weight.shape[0]
+    chip_width = 2 * width
     pass_flops = 2 * (2 * rows) * (2 * rows) * columns
 
     def tile(x):
@@ -362,11 +328,14 @@
 
     mr_product = (key_mr.astype(F32) * value_mr.astype(F32)).astype(BF16)
     before = shifted(mr_product, 1)
-    weight_rows = lax.all_gather(out_weight, "ctx", axis=0, tiled=True)
-    cot_line = [(line, cotangent)]
-    for r in range(1, line_count):
-        cot_line.append((line ^ r, line_swap(cotangent, r)))
-
+    cot_full = lax.all_gather(cotangent, "fsdp", axis=1, tiled=True)
+
+    other_weight = core_swap(out_weight)
+    weight_pair = jnp.where(
+        core == 0,
+        jnp.concatenate([out_weight, other_weight], axis=0),
+        jnp.concatenate([other_weight, out_weight], axis=0),
+    )
     rate = 1.0 / li_time
     coef = li_residue * jnp.sqrt(-jnp.expm1(-2.0 * rate))
     back_factors = lax.optimization_barrier(direct_factors(rate, rows, here // 2, True))
@@ -393,6 +362,7 @@
         [(2 * rows, F32), (rows, F32), (rows, BF16), (rows, BF16), (rate.shape[0], F32)],
         4 * pass_flops,
     )
+
     states = lax.all_gather(ends, "ctx").reshape(-1, columns)
     gaps = (here - 1 - jnp.arange(ctx_count, dtype=jnp.int32)).astype(F32)
     (li_inner,) = run(
@@ -410,33 +380,37 @@
         pass_flops,
     )
 
-    mixed_all = lax.all_gather(mixed_li, "ctx", axis=0, tiled=True)
-
-    blocks = ctx_count // line_count
-    cot_full, stack = run_once(
-        functools.partial(split_body, width),
-        [jnp.stack([index * blocks for index, _ in cot_line])] + [piece for _, piece in cot_line],
-        [((rows, ctx_count * width), BF16), ((ctx_count * rows, width), BF16)],
-        0,
-    )
-    cot_rows = lax.all_to_all(stack, "ctx", 0, 0, tiled=True)
-
-    share_flops = 2 * rows * columns * ctx_count * width
+    cot_full = after(cot_full, mixed_li)
+    cot_parts = [columns_at(cot_full, chip, chip_width)]
+    for s in range(1, chips):
+        cot_parts.append(chip_swap(columns_at(cot_full, chip ^ s, chip_width), s))
+
+    mixed_parts = [mixed_li] + [chip_swap(mixed_li, s) for s in range(1, chips)]
+    out_parts = []
+    for s, part in enumerate(mixed_parts):
+        found = lax.dot_general(
+            part, weight_pair, (((1,), (1,)), ((), ())), preferred_element_type=F32
+        ).astype(BF16)
+        out_parts.append((chip ^ s, found if s == 0 else chip_swap(found, s)))
+    out_full = placed(out_parts)
+    output = lax.psum_scatter(out_full, "fsdp", scatter_dimension=1, tiled=True).astype(F32)
+
+    grad_parts = []
+    for s, part in enumerate(cot_parts):
+        found = jnp.dot(part, weight_pair, preferred_element_type=F32)
+        grad_parts.append(found if s == 0 else chip_swap(found.astype(BF16), s))
     grad_mixed, grad_li_out, back_ends = run(
-        grad_gate_body,
-        columns,
-        [("whole", after(cot_full, mixed_li, cot_rows)), tile(weight_rows), tile(query_li), tile(rate)],
+        functools.partial(grad_gate_body, chips - 1),
+        columns,
+        [tile(grad_parts[0]), tile(query_li), tile(rate)] + [tile(part) for part in grad_parts[1:]],
         [(rows, F32), (rows, F32), (rate.shape[0], F32)],
-        share_flops,
-    )
-    out_stack = run_lines(out_body, line_count, after(mixed_li, back_ends), weight_rows, share_flops)
-    out_parts = lax.all_to_all(out_stack, "fsdp", 0, 0, tiled=True).reshape(line_count, rows, -1)
-    output = jnp.sum(out_parts.astype(F32), axis=0)
+        pass_flops,
+    )
     back_entering = entering_direct(back_ends, back_factors, here, True)
     (grad_inner,) = run(
         grad_inner_body,
         columns,
-        [tile(after(grad_li_out, out_stack)), tile(li_spec), table("ahead"), table("back")],
+        [tile(grad_li_out), tile(li_spec), table("ahead"), table("back")],
         [(rows, F32)],
         3 * pass_flops,
     )
@@ -480,13 +454,9 @@
     halves = tap_partial.reshape(2, tap_half, columns)
     own_half = lax.dynamic_index_in_dim(halves, core, 0, keepdims=False)
     far_half = lax.dynamic_index_in_dim(halves, 1 - core, 0, keepdims=False)
-    plane_half = own_half + core_swap(far_half)
-    by = 1
-    while by < chips:
-        sent = plane_half.astype(BF16)
-        plane_half = sent.astype(F32) + chip_swap(sent, by).astype(F32)
-        by *= 2
-    plane_half = plane_half * grad_scale
+    chip_half = (own_half + core_swap(far_half)).astype(BF16)
+    everywhere = [chip_half] + [chip_swap(chip_half, s) for s in range(1, chips)]
+    plane_half = pair_sum([part.astype(F32) for part in everywhere]) * grad_scale
     other_half = core_swap(plane_half)
     grad_taps = jnp.where(
         core == 0,
@@ -494,9 +464,19 @@
         jnp.concatenate([other_half, plane_half], axis=0),
     )
 
-    grad_weight = (
-        lax.dot_general(cot_rows, mixed_all, (((0,), (0,)), ((), ())), preferred_element_type=F32) * grad_scale
-    )
+    cot_rows = jnp.concatenate(cot_parts, axis=0)
+    mixed_rows = jnp.concatenate(mixed_parts, axis=0)
+
+    def weight_share(which):
+        return lax.dot_general(
+            columns_at(cot_rows, which, width),
+            mixed_rows,
+            (((0,), (0,)), ((), ())),
+            preferred_element_type=F32,
+        )
+
+    far_share = core_swap(weight_share(1 - core).astype(BF16))
+    grad_weight = (weight_share(core) + far_share.astype(F32)) * grad_scale
     return (
         output,
         grad_query_mr,

time: 165 us -> 165 us (level)
  blocking collectives: 33.6 us -> 10.2 us
  matrix products: 4.51 us -> 16.3 us
  Pallas kernels: 30.1 us -> 22 us
  local copies, waits for them, and re-layouts: 16 us -> 22 us
  other arithmetic: 8.53 us -> 14.1 us
  waiting for transfers between devices: 30.2 us -> 34.6 us
  starting transfers between devices: 26.2 us -> 30 us
    ppermute x5 -> x18, waiting for transfers between devices: 4.4 us -> 30.1 us  [chip_swap(): return lax.ppermute(x, 'ctx', [(i, i ^ 2 * by) for i in range(size)])]
    all_to_all x1 -> x0, blocking collectives: 22.1 us -> none  [shards(): cot_rows = lax.all_to_all(stack, 'ctx', 0, 0, tiled=True)]
    ppermute x3 -> x0, waiting for transfers between devices: 17.7 us -> none  [line_swap(): return lax.ppermute(x, 'fsdp', [(i, i ^ by) for i in range(size)])]
    ppermute x5 -> x18, starting transfers between devices: 3.56 us -> 18.2 us  [chip_swap(): return lax.ppermute(x, 'ctx', [(i, i ^ 2 * by) for i in range(size)])]
    dot_general x1 -> x10, matrix products: 4.51 us -> 16.3 us  [the longest x4 9.52 us: shards(): lax.dot_general(part, weight_pair, (((1,), (1,)), ((), ())), preferred_el...]
    all_to_all x1 -> x0, starting transfers between devices: 7.17 us -> none  [shards(): lax.all_to_all(out_stack, 'fsdp', 0, 0, tiled=True)]
    all_to_all x1 -> x0, waiting for transfers between devices: 6.55 us -> none  [shards(): lax.all_to_all(out_stack, 'fsdp', 0, 0, tiled=True)]
    pallas_call x2 -> x0, Pallas kernels: 6.29 us -> none  [the longest x1 5.04 us: run_lines(): pl.pallas_call(body, grid=(lines,), in_specs=[pl.BlockSpec((rows, depth),...]
  transfers between devices with their start and end apart: 16 -> 27, of which waited for: 5 -> 8; matrix products, arithmetic and copies ran while one was open for 7% -> 23% of each run, Pallas kernels for 18% -> 13%
where the time goes in v7:
time: 165 us; the launch traced here: 164 us
  waiting for transfers between devices  34.6 us (21%)
  starting transfers between devices  30 us (18%)
  local copies, waits for them, and re-layouts  22 us (13%)
  Pallas kernels  22 us (13%)
  matrix products  16.3 us (10%)
  between operations  14.7 us (9%)
  other arithmetic  14.1 us (9%)
  blocking collectives  10.2 us (6%)
    ppermute x18, waiting for transfers between devices, chip_swap(): return lax.ppermute(x, 'ctx', [(i, i ^ 2 * by) for i in range(size)])  30.1 us
    pallas_call x9, Pallas kernels, run(): pl.pallas_call(body, grid=(columns // tile,), in_specs=in_specs, out_spec...  22 us
    ppermute x18, starting transfers between devices, chip_swap(): return lax.ppermute(x, 'ctx', [(i, i ^ 2 * by) for i in range(size)])  18.2 us
    unnamed x91, local copies, waits for them, and re-layouts  14.6 us
    all_gather x1, blocking collectives, shards(): states = lax.all_gather(ends, 'ctx').reshape(-1, columns)  10.2 us
    dot_general x4, matrix products, shards(): lax.dot_general(part, weight_pair, (((1,), (1,)), ((), ())), preferred_el...  9.52 us
    ppermute x2, starting transfers between devices, shifted(): lax.ppermute(x, 'ctx', [(i, i + by) for i in range(size) if 0 <= i + by <...  7.79 us
    dot_general x2, matrix products, weight_share(): lax.dot_general(columns_at(cot_rows, which, width), mixed_rows, (((0,), (...  5.03 us
  transfers between devices with their start and end apart: 27, of which 8 were waited for; matrix products, arithmetic and copies ran while one was open for 23% of the time, Pallas kernels for 13%

profile of v7, /device:TPU:1, one launch (start us, length us, event | category | flops | bytes accessed | tf_op | source)
XLA Modules:
  0.0 163.9 jit_solution(4266512974967588632)
XLA Ops:
  8.4 4.5 %collective-permute-start = (bf16[128,1024]{1,0:T(8,128)(2,1)S(1)}, bf16[128,1024]{1,0:T(8,128)(2,1)}, u32[]{:S(2)}, u32[]{:S(2)}) collective-permute-start(bf16[128,1024]{1,0:T(8,128)(2,1)S(1)} %multiply_convert_fusion.product), channel_id=1, source_target_pairs={{0,4},{4,8},{8,12},{12,16},{16,20},{20,24},{24,28},{1,5},{5,9},{9,... | collective-permute-start | bytes 786440 | tf_op jit(solution)/shard_map/ppermute | solution.py:252
  17.3 2.0 %shard_map.197 = (f32[256,1024]{1,0:T(8,128)S(1)}, f32[256,1024]{1,0:T(8,128)S(1)}) custom-call(f32[128,1024]{1,0:T(8,128)S(1)} %copy-done.26, f32[16,1024]{1,0:T(8,128)S(1)} %get-tuple-element.67.rate, f32[16,1024]{1,0:T(8,128)S(1)} %get-tuple-element.63.coef, f32[1,1024]{1,0:T(1,128)S(1)} %bitcast.28, bf16[256,512]{1,0:T(8,128)(2,1)S(1)} %copy-done.1), custom_call_target="tpu_custom_call" | custom-call | flops 402653184 | bytes 3018752 | tf_op jit(solution)/shard_map/pallas_call | solution.py:229
  19.4 4.1 %shard_map.198 = (f32[256,1024]{1,0:T(8,128)S(1)}, f32[128,1024]{1,0:T(8,128)S(1)}, bf16[128,1024]{1,0:T(8,128)(2,1)S(1)}, bf16[128,1024]{1,0:T(8,128)(2,1)S(1)}, f32[16,1024]{1,0:T(8,128)S(1)}) custom-call(bf16[128,1024]{1,0:T(8,128)(2,1)} %collective-permute-done.before, bf16[128,1024]{1,0:T(8,128)(2,1)S(1)} %multiply_convert_fusion.product, ...), custom_call_target="tpu_custom_call" | custom-call | flops 536870912 | bytes 4980736 | tf_op jit(solution)/shard_map/pallas_call | solution.py:229
  24.3 2.0 %shard_map.199.inner = f32[128,1024]{1,0:T(8,128)S(1)} custom-call(bf16[128,1024]{1,0:T(8,128)(2,1)S(1)} %get-tuple-element.34.signal, f32[256,1024]{1,0:T(8,128)S(1)} %get-tuple-element.35.li_spec, bf16[256,512]{1,0:T(8,128)(2,1)S(1)} %copy-done.1, bf16[256,768]{1,0:T(8,128)(2,1)S(1)} %copy-done), custom_call_target="tpu_custom_call" | custom-call | flops 402653184 | bytes 2490368 | tf_op jit(solution)/shard_map/pallas_call | solution.py:229
  26.3 10.2 %all-gather.states = f32[128,1024]{1,0:T(8,128)S(1)} all-gather(f32[16,1024]{1,0:T(8,128)S(1)} %get-tuple-element.36), channel_id=2, replica_groups=mesh['ctx'=8,'fsdp'=4] {'ctx'}, dimensions={0}, use_global_device_ids=true | all-gather | bytes 589824 | tf_op jit(solution)/shard_map/all_gather | solution.py:366
  36.5 2.6 %shard_map.200 = (f32[128,1024]{1,0:T(8,128)S(1)}, bf16[128,1024]{1,0:T(8,128)(2,1)}) custom-call(f32[8]{0:T(128)S(1)} %subtract_convert_fusion.gaps, f32[128,1024]{1,0:T(8,128)S(1)} %shard_map.199.inner, bf16[128,1024]{1,0:T(8,128)(2,1)S(1)} %copy-done.9, f32[16,1024]{1,0:T(8,128)S(1)} %get-tuple-element.67.rate, f32[16,1024]{1,0:T(8,128)S(1)} %get-tuple-element.63.coef, ...), custom_call_target="tpu_custom_call" | custom-call | flops 134217728 | bytes 2228256 | tf_op jit(solution)/shard_map/pallas_call | solution.py:229
  44.0 4.0 %collective-permute-done.2 = bf16[128,1024]{1,0:T(8,128)(2,1)} collective-permute-done((bf16[128,1024]{1,0:T(8,128)(2,1)}, bf16[128,1024]{1,0:T(8,128)(2,1)}, u32[]{:S(2)}, u32[]{:S(2)}) %collective-permute-start.2) | collective-permute-done | bytes 262176 | tf_op jit(solution)/shard_map/ppermute | solution.py:242
  50.0 3.5 %collective-permute-done.6 = bf16[128,1024]{1,0:T(8,128)(2,1)S(1)} collective-permute-done((bf16[128,1024]{1,0:T(8,128)(2,1)}, bf16[128,1024]{1,0:T(8,128)(2,1)S(1)}, u32[]{:S(2)}, u32[]{:S(2)}) %collective-permute-start.6) | collective-permute-done | bytes 262176 | tf_op jit(solution)/shard_map/ppermute | solution.py:242
  55.2 2.6 %maximum_select_fusion = bf16[1024,1024]{1,0:T(8,128)(2,1)S(1)} fusion(bf16[512,1024]{1,0:T(8,128)(2,1)} %collective-permute-done.1, bf16[512,1024]{1,0:T(8,128)(2,1)S(1)} %copy-done.36, pred[]{:T(512)S(6)} %eq.6), kind=kLoop, calls=%fused_computation | loop fusion | flops 9437184 | bytes 4194305 | tf_op jit(solution)/shard_map/jit(_where)/select_n | solution.py:334
  57.8 2.7 %convolution_convert_fusion.6 = bf16[128,1024]{1,0:T(8,128)(2,1)} fusion(bf16[128,1024]{1,0:T(8,128)(2,1)} %collective-permute-done.2, bf16[1024,1024]{1,0:T(8,128)(2,1)S(1)} %maximum_select_fusion), kind=kOutput, calls=%fused_computation.8 | convolution fusion | flops 268566528 | bytes 2621440 | tf_op jit(solution)/shard_map/dot_general | solution.py:391
  61.7 2.5 %convolution_convert_fusion.5 = bf16[128,1024]{1,0:T(8,128)(2,1)} fusion(bf16[128,1024]{1,0:T(8,128)(2,1)} %collective-permute-done.4, bf16[1024,1024]{1,0:T(8,128)(2,1)S(1)} %maximum_select_fusion), kind=kOutput, calls=%fused_computation.7 | convolution fusion | flops 268566528 | bytes 2621440 | tf_op jit(solution)/shard_map/dot_general | solution.py:391
  65.6 2.5 %fusion = bf16[128,4096]{1,0:T(8,128)(2,1)} fusion(bf16[128,4096]{1,0:T(8,128)(2,1)} %broadcast_in_dim.12, s32[]{:T(128)S(6)} %select_n.93, bf16[128,1024]{1,0:T(8,128)(2,1)} %get-tuple-element.37, bf16[1024,1024]{1,0:T(8,128)(2,1)S(1)} %maximum_select_fusion), kind=kOutput, calls=%fused_computation.10 | convolution fusion | flops 268566528 | bytes 2621444 | tf_op jit(solution)/shard_map/dot_general | solution.py:391
  72.4 1.8 %convolution_convert_fusion.4 = bf16[128,1024]{1,0:T(8,128)(2,1)S(1)} fusion(bf16[128,1024]{1,0:T(8,128)(2,1)} %copy-done.37, bf16[1024,1024]{1,0:T(8,128)(2,1)S(1)} %copy-done.29), kind=kOutput, calls=%fused_computation.6 | convolution fusion | flops 268566528 | bytes 2621440 | tf_op jit(solution)/shard_map/dot_general | solution.py:391
  79.2 2.0 %collective-permute-start.12 = (bf16[128,1024]{1,0:T(8,128)(2,1)S(1)}, bf16[128,1024]{1,0:T(8,128)(2,1)S(1)}, u32[]{:S(2)}, u32[]{:S(2)}) collective-permute-start(bf16[128,1024]{1,0:T(8,128)(2,1)S(1)} %get-tuple-element.58), channel_id=1, source_target_pairs={{0,24},{4,28},{8,16},{12,20},{16,8},{20,12},{24,0},{28,4},{1,25},{... | collective-permute-start | bytes 786440 | tf_op jit(solution)/shard_map/ppermute | solution.py:242
  82.1 14.4 %collective-permute-done.10 = bf16[128,1024]{1,0:T(8,128)(2,1)S(1)} collective-permute-done((bf16[128,1024]{1,0:T(8,128)(2,1)S(1)}, bf16[128,1024]{1,0:T(8,128)(2,1)S(1)}, u32[]{:S(2)}, u32[]{:S(2)}) %collective-permute-start.10) | collective-permute-done | bytes 262176 | tf_op jit(solution)/shard_map/ppermute | solution.py:242
  99.5 2.3 %collective-permute-start.13 = (bf16[128,1024]{1,0:T(8,128)(2,1)S(1)}, bf16[128,1024]{1,0:T(8,128)(2,1)S(1)}, u32[]{:S(2)}, u32[]{:S(2)}) collective-permute-start(bf16[128,1024]{1,0:T(8,128)(2,1)S(1)} %convolution_convert_fusion.1), channel_id=1, source_target_pairs={{0,24},{4,28},{8,16},{12,20},{16,8},{20,12},{24,0},{28,4},{1,25},{... | collective-permute-start | bytes 786440 | tf_op jit(solution)/shard_map/ppermute | solution.py:242
  102.3 8.0 %collective-permute-done.11.rest_1_ = bf16[128,1024]{1,0:T(8,128)(2,1)S(1)} collective-permute-done((bf16[128,1024]{1,0:T(8,128)(2,1)S(1)}, bf16[128,1024]{1,0:T(8,128)(2,1)S(1)}, u32[]{:S(2)}, u32[]{:S(2)}) %collective-permute-start.11) | collective-permute-done | bytes 262176 | tf_op jit(solution)/shard_map/ppermute | solution.py:242
  121.2 2.3 %shard_map.202.inner = f32[128,1024]{1,0:T(8,128)S(1)} custom-call(f32[128,1024]{1,0:T(8,128)S(1)} %copy-done.22, f32[256,1024]{1,0:T(8,128)S(1)} %get-tuple-element.35.li_spec, bf16[256,512]{1,0:T(8,128)(2,1)S(1)} %copy-done.2, bf16[256,768]{1,0:T(8,128)(2,1)S(1)} %copy-done), custom_call_target="tpu_custom_call" | custom-call | flops 402653184 | bytes 2752512 | tf_op jit(solution)/shard_map/pallas_call | solution.py:229
  124.5 3.8 %shard_map.203 = (f32[128,1024]{1,0:T(8,128)}, f32[128,1024]{1,0:T(8,128)}, f32[256,1024]{1,0:T(8,128)S(1)}, f32[128,1024]{1,0:T(8,128)S(1)}) custom-call(f32[128,1024]{1,0:T(8,128)S(1)} %shard_map.202.inner, f32[16,1024]{1,0:T(8,128)S(1)} %get-tuple-element.67.rate, f32[16,1024]{1,0:T(8,128)S(1)} %get-tuple-element.63.coef, ...), custom_call_target="tpu_custom_call" | custom-call | flops 536870912 | bytes 6160384 | tf_op jit(solution)/shard_map/pallas_call | solution.py:229
  137.7 2.3 %shard_map.204 = (f32[128,1024]{1,0:T(8,128)S(1)}, bf16[128,1024]{1,0:T(8,128)(2,1)}) custom-call(f32[256,1024]{1,0:T(8,128)S(1)} %copy-done.8, f32[256,1024]{1,0:T(8,128)S(1)} %get-tuple-element.33.mr_spec, bf16[256,768]{1,0:T(8,128)(2,1)S(1)} %copy-done), custom_call_target="tpu_custom_call" | custom-call | flops 402653184 | bytes 3276800 | tf_op jit(solution)/shard_map/pallas_call | solution.py:229
  140.8 3.3 %collective-permute-start.18 = (bf16[128,1024]{1,0:T(8,128)(2,1)}, bf16[128,1024]{1,0:T(8,128)(2,1)S(1)}, u32[]{:S(2)}, u32[]{:S(2)}) collective-permute-start(bf16[128,1024]{1,0:T(8,128)(2,1)} %get-tuple-element.51), channel_id=1, source_target_pairs={{4,0},{8,4},{12,8},{16,12},{20,16},{24,20},{28,24},{5,1},{9,5},{13... | collective-permute-start | bytes 786440 | tf_op jit(solution)/shard_map/ppermute | solution.py:252
  144.8 2.0 %mul.125 = f32[128,1024]{1,0:T(8,128)} multiply(f32[128,1024]{1,0:T(8,128)} %copy-done.16, f32[128,1024]{1,0:T(8,128)S(1)} %copy-done.13) | non-fusion elementwise | flops 131072 | bytes 1572864 | tf_op jit(solution)/shard_map/mul | solution.py:417
  146.8 2.6 %collective-permute-done.18.arrived = bf16[128,1024]{1,0:T(8,128)(2,1)S(1)} collective-permute-done((bf16[128,1024]{1,0:T(8,128)(2,1)}, bf16[128,1024]{1,0:T(8,128)(2,1)S(1)}, u32[]{:S(2)}, u32[]{:S(2)}) %collective-permute-start.18) | collective-permute-done | bytes 262176 | tf_op jit(solution)/shard_map/ppermute | solution.py:252
  151.9 3.3 %add_multiply_fusion = f32[512,1024]{1,0:T(8,128)} fusion(bf16[512,1024]{1,0:T(8,128)(2,1)} %collective-permute-done.24, bf16[512,1024]{1,0:T(8,128)(2,1)S(1)} %copy-done.35, bf16[512,1024]{1,0:T(8,128)(2,1)S(1)} %copy-done.31, s32[]{:T(128)S(6)} %select_n.110), kind=kOutput, calls=%fused_computation.1 | convolution fusion | flops 538443776 | bytes 4718596 | tf_op jit(solution)/shard_map/dot_general | solution.py:471
  (162 shorter events, 58.0 us)
Async XLA Ops:
  7.2 62.5 %all-gather.3.cloned.1.call-start = ((), (), s32[]{:S(2)}) async-start(), calls=%async_computation.2 | async-start | bytes 1310720 | tf_op jit(solution)/shard_map/all_gather | solution.py:331
  8.4 11.0 %collective-permute-start = (bf16[128,1024]{1,0:T(8,128)(2,1)S(1)}, bf16[128,1024]{1,0:T(8,128)(2,1)}, u32[]{:S(2)}, u32[]{:S(2)}) collective-permute-start(bf16[128,1024]{1,0:T(8,128)(2,1)S(1)} %multiply_convert_fusion.product), channel_id=1, source_target_pairs={{0,4},{4,8},{8,12},{12,16},{16,20},{20,24},{24,28},{1,5},{5,9},{9,... | collective-permute-start | bytes 786440 | tf_op jit(solution)/shard_map/ppermute | solution.py:252
  12.9 42.3 %collective-permute-start.1 = (bf16[512,1024]{1,0:T(8,128)(2,1)}, bf16[512,1024]{1,0:T(8,128)(2,1)}, u32[]{:S(2)}, u32[]{:S(2)}) collective-permute-start(bf16[512,1024]{1,0:T(8,128)(2,1)} %param.23), channel_id=1, source_target_pairs={{0,4},{4,0},{8,12},{12,8},{16,20},{20,16},{24,28},{28,24},{1,5},{5... | collective-permute-start | bytes 3145736 | tf_op jit(solution)/shard_map/ppermute | solution.py:247
  39.9 8.1 %collective-permute-start.2 = (bf16[128,1024]{1,0:T(8,128)(2,1)}, bf16[128,1024]{1,0:T(8,128)(2,1)}, u32[]{:S(2)}, u32[]{:S(2)}) collective-permute-start(bf16[128,1024]{1,0:T(8,128)(2,1)} %get-tuple-element.37), channel_id=1, source_target_pairs={{0,8},{4,12},{8,0},{12,4},{16,24},{20,28},{24,16},{28,20},{1,9},{5... | collective-permute-start | bytes 786440 | tf_op jit(solution)/shard_map/ppermute | solution.py:242
  40.1 8.8 %collective-permute-start.4 = (bf16[128,1024]{1,0:T(8,128)(2,1)}, bf16[128,1024]{1,0:T(8,128)(2,1)}, u32[]{:S(2)}, u32[]{:S(2)}) collective-permute-start(bf16[128,1024]{1,0:T(8,128)(2,1)} %get-tuple-element.37), channel_id=1, source_target_pairs={{0,16},{4,20},{8,24},{12,28},{16,0},{20,4},{24,8},{28,12},{1,17},{... | collective-permute-start | bytes 786440 | tf_op jit(solution)/shard_map/ppermute | solution.py:242
  41.4 113.8 %reduce-scatter.2.cloned.1.call-start = ((), (), s32[]{:S(2)}) async-start(), calls=%async_computation.1 | async-start | bytes 1310720 | tf_op jit(solution)/shard_map/reduce_scatter | solution.py:396
  41.7 11.8 %collective-permute-start.6 = (bf16[128,1024]{1,0:T(8,128)(2,1)}, bf16[128,1024]{1,0:T(8,128)(2,1)S(1)}, u32[]{:S(2)}, u32[]{:S(2)}) collective-permute-start(bf16[128,1024]{1,0:T(8,128)(2,1)} %get-tuple-element.37), channel_id=1, source_target_pairs={{0,24},{4,28},{8,16},{12,20},{16,8},{20,12},{24,0},{28,4},{1,25},{... | collective-permute-start | bytes 786440 | tf_op jit(solution)/shard_map/ppermute | solution.py:242
  60.5 15.1 %collective-permute-start.3 = (bf16[128,1024]{1,0:T(8,128)(2,1)}, bf16[128,1024]{1,0:T(8,128)(2,1)}, u32[]{:S(2)}, u32[]{:S(2)}) collective-permute-start(bf16[128,1024]{1,0:T(8,128)(2,1)} %convolution_convert_fusion.6), channel_id=1, source_target_pairs={{0,8},{4,12},{8,0},{12,4},{16,24},{20,28},{24,16},{28,20},{1,9},{5... | collective-permute-start | bytes 786440 | tf_op jit(solution)/shard_map/ppermute | solution.py:242
  64.2 13.0 %collective-permute-start.5 = (bf16[128,1024]{1,0:T(8,128)(2,1)}, bf16[128,1024]{1,0:T(8,128)(2,1)}, u32[]{:S(2)}, u32[]{:S(2)}) collective-permute-start(bf16[128,1024]{1,0:T(8,128)(2,1)} %convolution_convert_fusion.5), channel_id=1, source_target_pairs={{0,16},{4,20},{8,24},{12,28},{16,0},{20,4},{24,8},{28,12},{1,17},{... | collective-permute-start | bytes 786440 | tf_op jit(solution)/shard_map/ppermute | solution.py:242
  71.1 10.1 %collective-permute-start.8 = (bf16[128,1024]{1,0:T(8,128)(2,1)S(1)}, bf16[128,1024]{1,0:T(8,128)(2,1)S(1)}, u32[]{:S(2)}, u32[]{:S(2)}) collective-permute-start(bf16[128,1024]{1,0:T(8,128)(2,1)S(1)} %get-tuple-element.60), channel_id=1, source_target_pairs={{0,8},{4,12},{8,0},{12,4},{16,24},{20,28},{24,16},{28,20},{1,9},{5... | collective-permute-start | bytes 786440 | tf_op jit(solution)/shard_map/ppermute | solution.py:242
  74.2 40.8 %collective-permute-start.7 = (bf16[128,1024]{1,0:T(8,128)(2,1)S(1)}, bf16[128,1024]{1,0:T(8,128)(2,1)S(1)}, u32[]{:S(2)}, u32[]{:S(2)}) collective-permute-start(bf16[128,1024]{1,0:T(8,128)(2,1)S(1)} %convolution_convert_fusion.4), channel_id=1, source_target_pairs={{0,24},{4,28},{8,16},{12,20},{16,8},{20,12},{24,0},{28,4},{1,25},{... | collective-permute-start | bytes 786440 | tf_op jit(solution)/shard_map/ppermute | solution.py:242
  78.9 17.5 %collective-permute-start.10 = (bf16[128,1024]{1,0:T(8,128)(2,1)S(1)}, bf16[128,1024]{1,0:T(8,128)(2,1)S(1)}, u32[]{:S(2)}, u32[]{:S(2)}) collective-permute-start(bf16[128,1024]{1,0:T(8,128)(2,1)S(1)} %get-tuple-element.59), channel_id=1, source_target_pairs={{0,16},{4,20},{8,24},{12,28},{16,0},{20,4},{24,8},{28,12},{1,17},{... | collective-permute-start | bytes 786440 | tf_op jit(solution)/shard_map/ppermute | solution.py:242
  79.2 19.1 %collective-permute-start.12 = (bf16[128,1024]{1,0:T(8,128)(2,1)S(1)}, bf16[128,1024]{1,0:T(8,128)(2,1)S(1)}, u32[]{:S(2)}, u32[]{:S(2)}) collective-permute-start(bf16[128,1024]{1,0:T(8,128)(2,1)S(1)} %get-tuple-element.58), channel_id=1, source_target_pairs={{0,24},{4,28},{8,16},{12,20},{16,8},{20,12},{24,0},{28,4},{1,25},{... | collective-permute-start | bytes 786440 | tf_op jit(solution)/shard_map/ppermute | solution.py:242
  81.6 20.6 %collective-permute-start.9 = (bf16[128,1024]{1,0:T(8,128)(2,1)S(1)}, bf16[128,1024]{1,0:T(8,128)(2,1)S(1)}, u32[]{:S(2)}, u32[]{:S(2)}) collective-permute-start(bf16[128,1024]{1,0:T(8,128)(2,1)S(1)} %convolution_convert_fusion.3), channel_id=1, source_target_pairs={{0,8},{4,12},{8,0},{12,4},{16,24},{20,28},{24,16},{28,20},{1,9},{5... | collective-permute-start | bytes 786440 | tf_op jit(solution)/shard_map/ppermute | solution.py:242
  97.7 12.6 %collective-permute-start.11 = (bf16[128,1024]{1,0:T(8,128)(2,1)S(1)}, bf16[128,1024]{1,0:T(8,128)(2,1)S(1)}, u32[]{:S(2)}, u32[]{:S(2)}) collective-permute-start(bf16[128,1024]{1,0:T(8,128)(2,1)S(1)} %convolution_convert_fusion.2), channel_id=1, source_target_pairs={{0,16},{4,20},{8,24},{12,28},{16,0},{20,4},{24,8},{28,12},{1,17},{... | collective-permute-start | bytes 786440 | tf_op jit(solution)/shard_map/ppermute | solution.py:242
  99.5 10.8 %collective-permute-start.13 = (bf16[128,1024]{1,0:T(8,128)(2,1)S(1)}, bf16[128,1024]{1,0:T(8,128)(2,1)S(1)}, u32[]{:S(2)}, u32[]{:S(2)}) collective-permute-start(bf16[128,1024]{1,0:T(8,128)(2,1)S(1)} %convolution_convert_fusion.1), channel_id=1, source_target_pairs={{0,24},{4,28},{8,16},{12,20},{16,8},{20,12},{24,0},{28,4},{1,25},{... | collective-permute-start | bytes 786440 | tf_op jit(solution)/shard_map/ppermute | solution.py:242
  116.9 6.7 %collective-permute-start.17 = (f32[16,1024]{1,0:T(8,128)S(1)}, f32[16,1024]{1,0:T(8,128)S(1)}, u32[]{:S(2)}, u32[]{:S(2)}) collective-permute-start(f32[16,1024]{1,0:T(8,128)S(1)} %add_select_fusion.1), channel_id=1, source_target_pairs={{0,24},{4,28},{8,16},{12,20},{16,8},{20,12},{24,0},{28,4},{1,25},{... | collective-permute-start | bytes 196616 | tf_op jit(solution)/shard_map/ppermute | solution.py:242
  118.3 5.2 %collective-permute-start.16 = (f32[16,1024]{1,0:T(8,128)S(1)}, f32[16,1024]{1,0:T(8,128)S(1)}, u32[]{:S(2)}, u32[]{:S(2)}) collective-permute-start(f32[16,1024]{1,0:T(8,128)S(1)} %add_select_fusion.1), channel_id=1, source_target_pairs={{0,16},{4,20},{8,24},{12,28},{16,0},{20,4},{24,8},{28,12},{1,17},{... | collective-permute-start | bytes 196616 | tf_op jit(solution)/shard_map/ppermute | solution.py:242
  133.9 18.1 %collective-permute-start.24 = (bf16[512,1024]{1,0:T(8,128)(2,1)}, bf16[512,1024]{1,0:T(8,128)(2,1)}, u32[]{:S(2)}, u32[]{:S(2)}) collective-permute-start(bf16[512,1024]{1,0:T(8,128)(2,1)} %convolution_convert_fusion), channel_id=1, source_target_pairs={{0,4},{4,0},{8,12},{12,8},{16,20},{20,16},{24,28},{28,24},{1,5},{5... | collective-permute-start | bytes 3145736 | tf_op jit(solution)/shard_map/ppermute | solution.py:247
  135.0 9.1 %collective-permute-start.22 = (bf16[64,1024]{1,0:T(8,128)(2,1)S(1)}, bf16[64,1024]{1,0:T(8,128)(2,1)S(1)}, u32[]{:S(2)}, u32[]{:S(2)}) collective-permute-start(bf16[64,1024]{1,0:T(8,128)(2,1)S(1)} %fusion.3), channel_id=1, source_target_pairs={{0,24},{4,28},{8,16},{12,20},{16,8},{20,12},{24,0},{28,4},{1,25},{... | collective-permute-start | bytes 393224 | tf_op jit(solution)/shard_map/ppermute | solution.py:242
  135.9 8.2 %collective-permute-start.21 = (bf16[64,1024]{1,0:T(8,128)(2,1)S(1)}, bf16[64,1024]{1,0:T(8,128)(2,1)S(1)}, u32[]{:S(2)}, u32[]{:S(2)}) collective-permute-start(bf16[64,1024]{1,0:T(8,128)(2,1)S(1)} %fusion.3), channel_id=1, source_target_pairs={{0,16},{4,20},{8,24},{12,28},{16,0},{20,4},{24,8},{28,12},{1,17},{... | collective-permute-start | bytes 393224 | tf_op jit(solution)/shard_map/ppermute | solution.py:242
  137.4 6.7 %collective-permute-start.20 = (bf16[64,1024]{1,0:T(8,128)(2,1)S(1)}, bf16[64,1024]{1,0:T(8,128)(2,1)S(1)}, u32[]{:S(2)}, u32[]{:S(2)}) collective-permute-start(bf16[64,1024]{1,0:T(8,128)(2,1)S(1)} %fusion.3), channel_id=1, source_target_pairs={{0,8},{4,12},{8,0},{12,4},{16,24},{20,28},{24,16},{28,20},{1,9},{5... | collective-permute-start | bytes 393224 | tf_op jit(solution)/shard_map/ppermute | solution.py:242
  140.8 8.6 %collective-permute-start.18 = (bf16[128,1024]{1,0:T(8,128)(2,1)}, bf16[128,1024]{1,0:T(8,128)(2,1)S(1)}, u32[]{:S(2)}, u32[]{:S(2)}) collective-permute-start(bf16[128,1024]{1,0:T(8,128)(2,1)} %get-tuple-element.51), channel_id=1, source_target_pairs={{4,0},{8,4},{12,8},{16,12},{20,16},{24,20},{28,24},{5,1},{9,5},{13... | collective-permute-start | bytes 786440 | tf_op jit(solution)/shard_map/ppermute | solution.py:252
  144.2 6.8 %collective-permute-start.23 = (f32[64,1024]{1,0:T(8,128)S(1)}, f32[64,1024]{1,0:T(8,128)S(1)}, u32[]{:S(2)}, u32[]{:S(2)}) collective-permute-start(f32[64,1024]{1,0:T(8,128)S(1)} %add_multiply_fusion.1), channel_id=1, source_target_pairs={{0,4},{4,0},{8,12},{12,8},{16,20},{20,16},{24,28},{28,24},{1,5},{5... | collective-permute-start | bytes 786440 | tf_op jit(solution)/shard_map/ppermute | solution.py:247
  (47 other events, 293.3 us)
Sparse Core Ops, SparseCore 0:
  41.5 28.0 all-gather.2
  115.8 25.5 reduce-scatter.1

commit v8 on v7

--- a/solution.py
+++ b/solution.py
@@ -233,7 +233,7 @@
         out_specs=[pl.BlockSpec((rows, tile), lambda c: (0, c)) for rows, _ in outputs],
         out_shape=[jax.ShapeDtypeStruct((rows, columns), dtype) for rows, dtype in outputs],
         compiler_params=pltpu.CompilerParams(vmem_limit_bytes=12 * 1024 * 1024),
-        cost_estimate=pl.CostEstimate(flops=flops, bytes_accessed=moved, transcendentals=0),
+        cost_estimate=pl.CostEstimate(flops=flops, bytes_accessed=moved if flops else 0, transcendentals=0),
     )(*[array for _, array in inputs])
 
 
@@ -344,7 +344,7 @@
         columns,
         [tile(mr_taps), tile(rate), tile(coef), tile(li_skip[None, :]), table("ahead")],
         [(2 * rows, F32), (2 * rows, F32)],
-        3 * pass_flops,
+        0,
     )
     spec, mr_conv, mixed_mr, li_input, ends = run(
         short_body,
@@ -360,7 +360,7 @@
             table("back"),
         ],
         [(2 * rows, F32), (rows, F32), (rows, BF16), (rows, BF16), (rate.shape[0], F32)],
-        4 * pass_flops,
+        0,
     )
 
     states = lax.all_gather(ends, "ctx").reshape(-1, columns)
@@ -370,17 +370,17 @@
         columns,
         [tile(li_input), tile(li_spec), table("ahead"), table("back")],
         [(rows, F32)],
-        3 * pass_flops,
+        0,
     )
     li_out, mixed_li = run(
         long_body,
         columns,
         [("scalar", gaps), tile(li_inner), tile(query_li), tile(rate), tile(coef), tile(states)],
         [(rows, F32), (rows, BF16)],
-        pass_flops,
-    )
-
-    cot_full = after(cot_full, mixed_li)
+        0,
+    )
+
+    cot_full, mixed_li = lax.optimization_barrier((cot_full, mixed_li))
     cot_parts = [columns_at(cot_full, chip, chip_width)]
     for s in range(1, chips):
         cot_parts.append(chip_swap(columns_at(cot_full, chip ^ s, chip_width), s))

time: 165 us -> 146 us (0.88)
  local copies, waits for them, and re-layouts: 22 us -> 15.9 us
  matrix products: 16.3 us -> 10.8 us
  starting transfers between devices: 30 us -> 25.8 us
  waiting for transfers between devices: 34.6 us -> 31.2 us
    dot_general x4, matrix products: 9.52 us -> 4.03 us  [shards(): lax.dot_general(part, weight_pair, (((1,), (1,)), ((), ())), preferred_el...]
    unnamed x91 -> x79, local copies, waits for them, and re-layouts: 14.6 us -> 11.3 us
    ppermute x18, waiting for transfers between devices: 30.1 us -> 26.9 us  [chip_swap(): return lax.ppermute(x, 'ctx', [(i, i ^ 2 * by) for i in range(size)])]
    ppermute x5, starting transfers between devices: 3.82 us -> 1.83 us  [core_swap(): return lax.ppermute(x, 'ctx', [(i, i ^ 1) for i in range(size)])]
    ppermute x18, starting transfers between devices: 18.2 us -> 16.2 us  [chip_swap(): return lax.ppermute(x, 'ctx', [(i, i ^ 2 * by) for i in range(size)])]
    dynamic_update_slice x3, local copies, waits for them, and re-layouts: 4.14 us -> 2.21 us  [placed(): whole = lax.dynamic_update_slice_in_dim(whole, piece, index * width, 1)]
  transfers between devices with their start and end apart: 27 -> 27, of which waited for: 8 -> 5; matrix products, arithmetic and copies ran while one was open for 23% -> 21% of each run, Pallas kernels for 13% -> 15%
where the time goes in v8:
time: 146 us; the launch traced here: 145 us
  waiting for transfers between devices  31.2 us (21%)
  starting transfers between devices  25.8 us (18%)
  Pallas kernels  21.2 us (15%)
  local copies, waits for them, and re-layouts  15.9 us (11%)
  other arithmetic  15.5 us (11%)
  between operations  14.6 us (10%)
  matrix products  10.8 us (7%)
  blocking collectives  9.79 us (7%)
    ppermute x18, waiting for transfers between devices, chip_swap(): return lax.ppermute(x, 'ctx', [(i, i ^ 2 * by) for i in range(size)])  26.9 us
    pallas_call x9, Pallas kernels, run(): pl.pallas_call(body, grid=(columns // tile,), in_specs=in_specs, out_spec...  21.2 us
    ppermute x18, starting transfers between devices, chip_swap(): return lax.ppermute(x, 'ctx', [(i, i ^ 2 * by) for i in range(size)])  16.2 us
    unnamed x79, local copies, waits for them, and re-layouts  11.3 us
    all_gather x1, blocking collectives, shards(): states = lax.all_gather(ends, 'ctx').reshape(-1, columns)  9.79 us
    ppermute x2, starting transfers between devices, shifted(): lax.ppermute(x, 'ctx', [(i, i + by) for i in range(size) if 0 <= i + by <...  7.64 us
    dot_general x2, matrix products, weight_share(): lax.dot_general(columns_at(cot_rows, which, width), mixed_rows, (((0,), (...  5.02 us
    dot_general x4, matrix products, shards(): lax.dot_general(part, weight_pair, (((1,), (1,)), ((), ())), preferred_el...  4.03 us
  transfers between devices with their start and end apart: 27, of which 5 were waited for; matrix products, arithmetic and copies ran while one was open for 21% of the time, Pallas kernels for 15%

profile of v8, /device:TPU:1, one launch (start us, length us, event | category | flops | bytes accessed | tf_op | source)
XLA Modules:
  0.0 144.8 jit_solution(2936590341135337573)
XLA Ops:
  8.1 1.8 %multiply_convert_fusion.product = bf16[128,1024]{1,0:T(8,128)(2,1)} fusion(bf16[128,1024]{1,0:T(8,128)(2,1)} %value.1, bf16[128,1024]{1,0:T(8,128)(2,1)} %key.3), kind=kLoop, calls=%fused_computation.15 | loop fusion | flops 524288 | bytes 786432 | tf_op jit(solution)/shard_map/convert_element_type | solution.py:329
  9.9 4.5 %collective-permute-start = (bf16[128,1024]{1,0:T(8,128)(2,1)}, bf16[128,1024]{1,0:T(8,128)(2,1)}, u32[]{:S(2)}, u32[]{:S(2)}) collective-permute-start(bf16[128,1024]{1,0:T(8,128)(2,1)} %multiply_convert_fusion.product), channel_id=1, source_target_pairs={{0,4},{4,8},{8,12},{12,16},{16,20},{20,24},{24,28},{1,5},{5,9},{9,... | collective-permute-start | bytes 786440 | tf_op jit(solution)/shard_map/ppermute | solution.py:252
  14.4 1.6 %exponential_select_fusion = (f32[16,1024]{1,0:T(8,128)}, f32[16,1024]{1,0:T(8,128)S(1)}, f32[16,1024]{1,0:T(8,128)S(1)}, f32[16,1024]{1,0:T(8,128)}, f32[16,1024]{1,0:T(8,128)}, /*index=5*/f32[16,1024]{1,0:T(8,128)S(1)}) fusion(f32[]{:T(128)S(6)} %convert_element_type.80, pred[]{:T(512)S(6)} %ge.11, f32[16,1024]{1,0:T(8,128)} %param.20, ...), kind=kLoop, calls=%fused_computation.22 | loop fusion | flops 196608 | bytes 524303 | tf_op jit(solution)/shard_map/jit(_where)/select_n | solution.py:282
  18.7 2.0 %shard_map.197 = (f32[256,1024]{1,0:T(8,128)S(1)}, f32[256,1024]{1,0:T(8,128)S(1)}) custom-call(f32[128,1024]{1,0:T(8,128)S(1)} %copy-done.21, f32[16,1024]{1,0:T(8,128)S(1)} %get-tuple-element.69.rate, f32[16,1024]{1,0:T(8,128)S(1)} %get-tuple-element.65.coef, f32[1,1024]{1,0:T(1,128)S(1)} %bitcast.28, bf16[256,512]{1,0:T(8,128)(2,1)S(1)} %copy-done), custom_call_target="tpu_custom_call" | custom-call | tf_op jit(solution)/shard_map/pallas_call | solution.py:229
  20.8 4.2 %shard_map.198 = (f32[256,1024]{1,0:T(8,128)S(1)}, f32[128,1024]{1,0:T(8,128)S(1)}, bf16[128,1024]{1,0:T(8,128)(2,1)S(1)}, bf16[128,1024]{1,0:T(8,128)(2,1)S(1)}, f32[16,1024]{1,0:T(8,128)S(1)}) custom-call(bf16[128,1024]{1,0:T(8,128)(2,1)} %collective-permute-done.before, bf16[128,1024]{1,0:T(8,128)(2,1)} %multiply_convert_fusion.product, ...), custom_call_target="tpu_custom_call" | custom-call | tf_op jit(solution)/shard_map/pallas_call | solution.py:229
  26.0 2.0 %shard_map.199.inner = f32[128,1024]{1,0:T(8,128)S(1)} custom-call(bf16[128,1024]{1,0:T(8,128)(2,1)S(1)} %get-tuple-element.35.signal, f32[256,1024]{1,0:T(8,128)S(1)} %get-tuple-element.36.li_spec, bf16[256,512]{1,0:T(8,128)(2,1)S(1)} %copy-done.1, bf16[256,768]{1,0:T(8,128)(2,1)S(1)} %copy-done.2), custom_call_target="tpu_custom_call" | custom-call | tf_op jit(solution)/shard_map/pallas_call | solution.py:229
  28.0 9.8 %all-gather.states = f32[128,1024]{1,0:T(8,128)S(1)} all-gather(f32[16,1024]{1,0:T(8,128)S(1)} %get-tuple-element.37), channel_id=2, replica_groups=mesh['ctx'=8,'fsdp'=4] {'ctx'}, dimensions={0}, use_global_device_ids=true | all-gather | bytes 589824 | tf_op jit(solution)/shard_map/all_gather | solution.py:366
  37.8 1.7 %shard_map.200 = (f32[128,1024]{1,0:T(8,128)S(1)}, bf16[128,1024]{1,0:T(8,128)(2,1)S(1)}) custom-call(f32[8]{0:T(128)S(1)} %subtract_convert_fusion.gaps, f32[128,1024]{1,0:T(8,128)S(1)} %shard_map.199.inner, bf16[128,1024]{1,0:T(8,128)(2,1)S(1)} %copy-done.9, f32[16,1024]{1,0:T(8,128)S(1)} %get-tuple-element.69.rate, ...), custom_call_target="tpu_custom_call" | custom-call | tf_op jit(solution)/shard_map/pallas_call | solution.py:229
  41.0 3.9 %maximum_select_fusion = bf16[1024,1024]{1,0:T(8,128)(2,1)} fusion(bf16[512,1024]{1,0:T(8,128)(2,1)} %collective-permute-done.1, bf16[512,1024]{1,0:T(8,128)(2,1)S(1)} %copy-done.34, pred[]{:T(512)S(6)} %eq.6), kind=kLoop, calls=%fused_computation | loop fusion | flops 9437184 | bytes 4194305 | tf_op jit(solution)/shard_map/jit(_where)/select_n | solution.py:334
  52.9 1.5 %fusion = bf16[128,4096]{1,0:T(8,128)(2,1)} fusion(bf16[128,4096]{1,0:T(8,128)(2,1)} %broadcast_in_dim.12, s32[]{:T(128)S(6)} %select_n.93, bf16[128,1024]{1,0:T(8,128)(2,1)S(1)} %copy-done.14, bf16[1024,1024]{1,0:T(8,128)(2,1)S(1)} %copy-done.28), kind=kOutput, calls=%fused_computation.10 | convolution fusion | flops 268566528 | bytes 2621444 | tf_op jit(solution)/shard_map/dot_general | solution.py:391
  57.9 6.2 %collective-permute-done.8 = bf16[128,1024]{1,0:T(8,128)(2,1)S(1)} collective-permute-done((bf16[128,1024]{1,0:T(8,128)(2,1)S(1)}, bf16[128,1024]{1,0:T(8,128)(2,1)S(1)}, u32[]{:S(2)}, u32[]{:S(2)}) %collective-permute-start.8) | collective-permute-done | bytes 262176 | tf_op jit(solution)/shard_map/ppermute | solution.py:242
  66.6 3.5 %collective-permute-done.12 = bf16[128,1024]{1,0:T(8,128)(2,1)S(1)} collective-permute-done((bf16[128,1024]{1,0:T(8,128)(2,1)S(1)}, bf16[128,1024]{1,0:T(8,128)(2,1)S(1)}, u32[]{:S(2)}, u32[]{:S(2)}) %collective-permute-start.12) | collective-permute-done | bytes 262176 | tf_op jit(solution)/shard_map/ppermute | solution.py:242
  74.8 6.2 %collective-permute-done.9.rest_0_ = bf16[128,1024]{1,0:T(8,128)(2,1)S(1)} collective-permute-done((bf16[128,1024]{1,0:T(8,128)(2,1)S(1)}, bf16[128,1024]{1,0:T(8,128)(2,1)S(1)}, u32[]{:S(2)}, u32[]{:S(2)}) %collective-permute-start.9) | collective-permute-done | bytes 262176 | tf_op jit(solution)/shard_map/ppermute | solution.py:242
  82.2 11.0 %collective-permute-done.11.rest_1_ = bf16[128,1024]{1,0:T(8,128)(2,1)S(1)} collective-permute-done((bf16[128,1024]{1,0:T(8,128)(2,1)S(1)}, bf16[128,1024]{1,0:T(8,128)(2,1)S(1)}, u32[]{:S(2)}, u32[]{:S(2)}) %collective-permute-start.11) | collective-permute-done | bytes 262176 | tf_op jit(solution)/shard_map/ppermute | solution.py:242
  103.3 2.3 %shard_map.202.inner = f32[128,1024]{1,0:T(8,128)S(1)} custom-call(f32[128,1024]{1,0:T(8,128)S(1)} %copy-done.23, f32[256,1024]{1,0:T(8,128)S(1)} %get-tuple-element.36.li_spec, bf16[256,512]{1,0:T(8,128)(2,1)S(1)} %copy-done.1, bf16[256,768]{1,0:T(8,128)(2,1)S(1)} %copy-done.2), custom_call_target="tpu_custom_call" | custom-call | flops 402653184 | bytes 2752512 | tf_op jit(solution)/shard_map/pallas_call | solution.py:229
  106.7 3.8 %shard_map.203 = (f32[128,1024]{1,0:T(8,128)}, f32[128,1024]{1,0:T(8,128)}, f32[256,1024]{1,0:T(8,128)S(1)}, f32[128,1024]{1,0:T(8,128)S(1)}) custom-call(f32[128,1024]{1,0:T(8,128)S(1)} %shard_map.202.inner, f32[16,1024]{1,0:T(8,128)S(1)} %get-tuple-element.69.rate, f32[16,1024]{1,0:T(8,128)S(1)} %get-tuple-element.65.coef, ...), custom_call_target="tpu_custom_call" | custom-call | flops 536870912 | bytes 6160384 | tf_op jit(solution)/shard_map/pallas_call | solution.py:229
  112.4 1.7 %convolution_convert_fusion = bf16[512,1024]{1,0:T(8,128)(2,1)} fusion(bf16[512,1024]{1,0:T(8,128)(2,1)S(1)} %copy-done.32, bf16[512,1024]{1,0:T(8,128)(2,1)S(1)} %copy-done.29, s32[]{:T(128)S(6)} %select_n.111), kind=kOutput, calls=%fused_computation.2 | convolution fusion | flops 537395200 | bytes 2621444 | tf_op jit(solution)/shard_map/dot_general | solution.py:471
  118.2 2.3 %shard_map.204 = (f32[128,1024]{1,0:T(8,128)S(1)}, bf16[128,1024]{1,0:T(8,128)(2,1)}) custom-call(f32[256,1024]{1,0:T(8,128)S(1)} %copy-done.8, f32[256,1024]{1,0:T(8,128)S(1)} %get-tuple-element.34.mr_spec, bf16[256,768]{1,0:T(8,128)(2,1)S(1)} %copy-done.2), custom_call_target="tpu_custom_call" | custom-call | flops 402653184 | bytes 3276800 | tf_op jit(solution)/shard_map/pallas_call | solution.py:229
  120.4 3.2 %collective-permute-start.18 = (bf16[128,1024]{1,0:T(8,128)(2,1)}, bf16[128,1024]{1,0:T(8,128)(2,1)S(1)}, u32[]{:S(2)}, u32[]{:S(2)}) collective-permute-start(bf16[128,1024]{1,0:T(8,128)(2,1)} %get-tuple-element.53), channel_id=1, source_target_pairs={{4,0},{8,4},{12,8},{16,12},{20,16},{24,20},{28,24},{5,1},{9,5},{13... | collective-permute-start | bytes 786440 | tf_op jit(solution)/shard_map/ppermute | solution.py:252
  125.5 3.6 %collective-permute-done.18.arrived = bf16[128,1024]{1,0:T(8,128)(2,1)S(1)} collective-permute-done((bf16[128,1024]{1,0:T(8,128)(2,1)}, bf16[128,1024]{1,0:T(8,128)(2,1)S(1)}, u32[]{:S(2)}, u32[]{:S(2)}) %collective-permute-start.18) | collective-permute-done | bytes 262176 | tf_op jit(solution)/shard_map/ppermute | solution.py:252
  129.1 1.7 %shard_map.205 = (f32[128,1024]{1,0:T(8,128)}, f32[128,1024]{1,0:T(8,128)}) custom-call(f32[128,1024]{1,0:T(8,128)S(1)} %get-tuple-element.52.own, bf16[128,1024]{1,0:T(8,128)(2,1)S(1)} %collective-permute-done.18.arrived, bf16[128,1024]{1,0:T(8,128)(2,1)S(1)} %copy-done.6, bf16[128,1024]{1,0:T(8,128)(2,1)S(1)} %copy-done.5), custom_call_target="tpu_custom_call" | custom-call | flops 131072 | bytes 2359296 | tf_op jit(solution)/shard_map/pallas_call | solution.py:229
  130.8 2.1 %maximum_select_fusion.1 = f32[128,1024]{1,0:T(8,128)} fusion(f32[64,1024]{1,0:T(8,128)} %collective-permute-done.23, f32[64,1024]{1,0:T(8,128)} %add_multiply_fusion.1, pred[]{:T(512)S(6)} %eq.6), kind=kLoop, calls=%fused_computation.12 | loop fusion | flops 393216 | bytes 1048577 | tf_op jit(solution)/shard_map/jit(_where)/select_n | solution.py:461
  132.9 3.3 %add_multiply_fusion = f32[512,1024]{1,0:T(8,128)} fusion(bf16[512,1024]{1,0:T(8,128)(2,1)} %collective-permute-done.24, bf16[512,1024]{1,0:T(8,128)(2,1)S(1)} %copy-done.33, bf16[512,1024]{1,0:T(8,128)(2,1)S(1)} %copy-done.30, s32[]{:T(128)S(6)} %select_n.110), kind=kOutput, calls=%fused_computation.1 | convolution fusion | flops 538443776 | bytes 4718596 | tf_op jit(solution)/shard_map/dot_general | solution.py:471
  136.2 1.8 %convert_element_type.74 = f32[128,1024]{1,0:T(8,128)} convert(bf16[128,1024]{1,0:T(8,128)(2,1)} %reduce-scatter.2.cloned.1.call-done) | non-fusion elementwise | flops 131072 | bytes 786432 | tf_op jit(solution)/shard_map/convert_element_type | solution.py:396
  (150 shorter events, 44.7 us)
Async XLA Ops:
  7.2 37.6 %all-gather.3.cloned.1.call-start = ((), (), s32[]{:S(2)}) async-start(), calls=%async_computation.1 | async-start | bytes 1310720 | tf_op jit(solution)/shard_map/all_gather | solution.py:331
  7.9 128.2 %reduce-scatter.2.cloned.1.call-start = ((), (), s32[]{:S(2)}) async-start(), calls=%async_computation.2 | async-start | bytes 1310720 | tf_op jit(solution)/shard_map/reduce_scatter | solution.py:396
  8.0 33.0 %collective-permute-start.1 = (bf16[512,1024]{1,0:T(8,128)(2,1)}, bf16[512,1024]{1,0:T(8,128)(2,1)}, u32[]{:S(2)}, u32[]{:S(2)}) collective-permute-start(bf16[512,1024]{1,0:T(8,128)(2,1)} %param.23), channel_id=1, source_target_pairs={{0,4},{4,0},{8,12},{12,8},{16,20},{20,16},{24,28},{28,24},{1,5},{5... | collective-permute-start | bytes 3145736 | tf_op jit(solution)/shard_map/ppermute | solution.py:247
  9.9 10.9 %collective-permute-start = (bf16[128,1024]{1,0:T(8,128)(2,1)}, bf16[128,1024]{1,0:T(8,128)(2,1)}, u32[]{:S(2)}, u32[]{:S(2)}) collective-permute-start(bf16[128,1024]{1,0:T(8,128)(2,1)} %multiply_convert_fusion.product), channel_id=1, source_target_pairs={{0,4},{4,8},{8,12},{12,16},{16,20},{20,24},{24,28},{1,5},{5,9},{9,... | collective-permute-start | bytes 786440 | tf_op jit(solution)/shard_map/ppermute | solution.py:252
  44.9 9.6 %collective-permute-start.2 = (bf16[128,1024]{1,0:T(8,128)(2,1)}, bf16[128,1024]{1,0:T(8,128)(2,1)S(1)}, u32[]{:S(2)}, u32[]{:S(2)}) collective-permute-start(bf16[128,1024]{1,0:T(8,128)(2,1)} %copy-done.13), channel_id=1, source_target_pairs={{0,8},{4,12},{8,0},{12,4},{16,24},{20,28},{24,16},{28,20},{1,9},{5... | collective-permute-start | bytes 786440 | tf_op jit(solution)/shard_map/ppermute | solution.py:242
  45.4 11.1 %collective-permute-start.4 = (bf16[128,1024]{1,0:T(8,128)(2,1)}, bf16[128,1024]{1,0:T(8,128)(2,1)S(1)}, u32[]{:S(2)}, u32[]{:S(2)}) collective-permute-start(bf16[128,1024]{1,0:T(8,128)(2,1)} %copy-done.13), channel_id=1, source_target_pairs={{0,16},{4,20},{8,24},{12,28},{16,0},{20,4},{24,8},{28,12},{1,17},{... | collective-permute-start | bytes 786440 | tf_op jit(solution)/shard_map/ppermute | solution.py:242
  46.3 25.1 %collective-permute-start.6 = (bf16[128,1024]{1,0:T(8,128)(2,1)}, bf16[128,1024]{1,0:T(8,128)(2,1)S(1)}, u32[]{:S(2)}, u32[]{:S(2)}) collective-permute-start(bf16[128,1024]{1,0:T(8,128)(2,1)} %copy-done.13), channel_id=1, source_target_pairs={{0,24},{4,28},{8,16},{12,20},{16,8},{20,12},{24,0},{28,4},{1,25},{... | collective-permute-start | bytes 786440 | tf_op jit(solution)/shard_map/ppermute | solution.py:242
  49.8 14.3 %collective-permute-start.8 = (bf16[128,1024]{1,0:T(8,128)(2,1)S(1)}, bf16[128,1024]{1,0:T(8,128)(2,1)S(1)}, u32[]{:S(2)}, u32[]{:S(2)}) collective-permute-start(bf16[128,1024]{1,0:T(8,128)(2,1)S(1)} %get-tuple-element.62), channel_id=1, source_target_pairs={{0,8},{4,12},{8,0},{12,4},{16,24},{20,28},{24,16},{28,20},{1,9},{5... | collective-permute-start | bytes 786440 | tf_op jit(solution)/shard_map/ppermute | solution.py:242
  50.4 14.7 %collective-permute-start.10 = (bf16[128,1024]{1,0:T(8,128)(2,1)S(1)}, bf16[128,1024]{1,0:T(8,128)(2,1)S(1)}, u32[]{:S(2)}, u32[]{:S(2)}) collective-permute-start(bf16[128,1024]{1,0:T(8,128)(2,1)S(1)} %get-tuple-element.61), channel_id=1, source_target_pairs={{0,16},{4,20},{8,24},{12,28},{16,0},{20,4},{24,8},{28,12},{1,17},{... | collective-permute-start | bytes 786440 | tf_op jit(solution)/shard_map/ppermute | solution.py:242
  54.5 15.6 %collective-permute-start.12 = (bf16[128,1024]{1,0:T(8,128)(2,1)S(1)}, bf16[128,1024]{1,0:T(8,128)(2,1)S(1)}, u32[]{:S(2)}, u32[]{:S(2)}) collective-permute-start(bf16[128,1024]{1,0:T(8,128)(2,1)S(1)} %get-tuple-element.60), channel_id=1, source_target_pairs={{0,24},{4,28},{8,16},{12,20},{16,8},{20,12},{24,0},{28,4},{1,25},{... | collective-permute-start | bytes 786440 | tf_op jit(solution)/shard_map/ppermute | solution.py:242
  56.5 40.0 %collective-permute-start.3 = (bf16[128,1024]{1,0:T(8,128)(2,1)S(1)}, bf16[128,1024]{1,0:T(8,128)(2,1)S(1)}, u32[]{:S(2)}, u32[]{:S(2)}) collective-permute-start(bf16[128,1024]{1,0:T(8,128)(2,1)S(1)} %convolution_convert_fusion.6), channel_id=1, source_target_pairs={{0,8},{4,12},{8,0},{12,4},{16,24},{20,28},{24,16},{28,20},{1,9},{5... | collective-permute-start | bytes 786440 | tf_op jit(solution)/shard_map/ppermute | solution.py:242
  64.1 33.2 %collective-permute-start.5 = (bf16[128,1024]{1,0:T(8,128)(2,1)S(1)}, bf16[128,1024]{1,0:T(8,128)(2,1)S(1)}, u32[]{:S(2)}, u32[]{:S(2)}) collective-permute-start(bf16[128,1024]{1,0:T(8,128)(2,1)S(1)} %convolution_convert_fusion.5), channel_id=1, source_target_pairs={{0,16},{4,20},{8,24},{12,28},{16,0},{20,4},{24,8},{28,12},{1,17},{... | collective-permute-start | bytes 786440 | tf_op jit(solution)/shard_map/ppermute | solution.py:242
  65.1 15.9 %collective-permute-start.9 = (bf16[128,1024]{1,0:T(8,128)(2,1)S(1)}, bf16[128,1024]{1,0:T(8,128)(2,1)S(1)}, u32[]{:S(2)}, u32[]{:S(2)}) collective-permute-start(bf16[128,1024]{1,0:T(8,128)(2,1)S(1)} %convolution_convert_fusion.3), channel_id=1, source_target_pairs={{0,8},{4,12},{8,0},{12,4},{16,24},{20,28},{24,16},{28,20},{1,9},{5... | collective-permute-start | bytes 786440 | tf_op jit(solution)/shard_map/ppermute | solution.py:242
  70.0 23.2 %collective-permute-start.11 = (bf16[128,1024]{1,0:T(8,128)(2,1)S(1)}, bf16[128,1024]{1,0:T(8,128)(2,1)S(1)}, u32[]{:S(2)}, u32[]{:S(2)}) collective-permute-start(bf16[128,1024]{1,0:T(8,128)(2,1)S(1)} %convolution_convert_fusion.2), channel_id=1, source_target_pairs={{0,16},{4,20},{8,24},{12,28},{16,0},{20,4},{24,8},{28,12},{1,17},{... | collective-permute-start | bytes 786440 | tf_op jit(solution)/shard_map/ppermute | solution.py:242
  71.4 21.8 %collective-permute-start.13 = (bf16[128,1024]{1,0:T(8,128)(2,1)S(1)}, bf16[128,1024]{1,0:T(8,128)(2,1)S(1)}, u32[]{:S(2)}, u32[]{:S(2)}) collective-permute-start(bf16[128,1024]{1,0:T(8,128)(2,1)S(1)} %convolution_convert_fusion.1), channel_id=1, source_target_pairs={{0,24},{4,28},{8,16},{12,20},{16,8},{20,12},{24,0},{28,4},{1,25},{... | collective-permute-start | bytes 786440 | tf_op jit(solution)/shard_map/ppermute | solution.py:242
  81.0 20.3 %collective-permute-start.7 = (bf16[128,1024]{1,0:T(8,128)(2,1)S(1)}, bf16[128,1024]{1,0:T(8,128)(2,1)S(1)}, u32[]{:S(2)}, u32[]{:S(2)}) collective-permute-start(bf16[128,1024]{1,0:T(8,128)(2,1)S(1)} %convolution_convert_fusion.4), channel_id=1, source_target_pairs={{0,24},{4,28},{8,16},{12,20},{16,8},{20,12},{24,0},{28,4},{1,25},{... | collective-permute-start | bytes 786440 | tf_op jit(solution)/shard_map/ppermute | solution.py:242
  98.7 7.0 %collective-permute-start.17 = (f32[16,1024]{1,0:T(8,128)}, f32[16,1024]{1,0:T(8,128)}, u32[]{:S(2)}, u32[]{:S(2)}) collective-permute-start(f32[16,1024]{1,0:T(8,128)} %add_select_fusion.1), channel_id=1, source_target_pairs={{0,24},{4,28},{8,16},{12,20},{16,8},{20,12},{24,0},{28,4},{1,25},{... | collective-permute-start | bytes 196616 | tf_op jit(solution)/shard_map/ppermute | solution.py:242
  99.8 5.8 %collective-permute-start.16 = (f32[16,1024]{1,0:T(8,128)}, f32[16,1024]{1,0:T(8,128)}, u32[]{:S(2)}, u32[]{:S(2)}) collective-permute-start(f32[16,1024]{1,0:T(8,128)} %add_select_fusion.1), channel_id=1, source_target_pairs={{0,16},{4,20},{8,24},{12,28},{16,0},{20,4},{24,8},{28,12},{1,17},{... | collective-permute-start | bytes 196616 | tf_op jit(solution)/shard_map/ppermute | solution.py:242
  114.1 18.7 %collective-permute-start.24 = (bf16[512,1024]{1,0:T(8,128)(2,1)}, bf16[512,1024]{1,0:T(8,128)(2,1)}, u32[]{:S(2)}, u32[]{:S(2)}) collective-permute-start(bf16[512,1024]{1,0:T(8,128)(2,1)} %convolution_convert_fusion), channel_id=1, source_target_pairs={{0,4},{4,0},{8,12},{12,8},{16,20},{20,16},{24,28},{28,24},{1,5},{5... | collective-permute-start | bytes 3145736 | tf_op jit(solution)/shard_map/ppermute | solution.py:247
  114.2 9.4 %collective-permute-start.22 = (bf16[64,1024]{1,0:T(8,128)(2,1)S(1)}, bf16[64,1024]{1,0:T(8,128)(2,1)S(1)}, u32[]{:S(2)}, u32[]{:S(2)}) collective-permute-start(bf16[64,1024]{1,0:T(8,128)(2,1)S(1)} %fusion.3), channel_id=1, source_target_pairs={{0,24},{4,28},{8,16},{12,20},{16,8},{20,12},{24,0},{28,4},{1,25},{... | collective-permute-start | bytes 393224 | tf_op jit(solution)/shard_map/ppermute | solution.py:242
  115.4 8.2 %collective-permute-start.21 = (bf16[64,1024]{1,0:T(8,128)(2,1)S(1)}, bf16[64,1024]{1,0:T(8,128)(2,1)S(1)}, u32[]{:S(2)}, u32[]{:S(2)}) collective-permute-start(bf16[64,1024]{1,0:T(8,128)(2,1)S(1)} %fusion.3), channel_id=1, source_target_pairs={{0,16},{4,20},{8,24},{12,28},{16,0},{20,4},{24,8},{28,12},{1,17},{... | collective-permute-start | bytes 393224 | tf_op jit(solution)/shard_map/ppermute | solution.py:242
  116.4 7.3 %collective-permute-start.20 = (bf16[64,1024]{1,0:T(8,128)(2,1)S(1)}, bf16[64,1024]{1,0:T(8,128)(2,1)S(1)}, u32[]{:S(2)}, u32[]{:S(2)}) collective-permute-start(bf16[64,1024]{1,0:T(8,128)(2,1)S(1)} %fusion.3), channel_id=1, source_target_pairs={{0,8},{4,12},{8,0},{12,4},{16,24},{20,28},{24,16},{28,20},{1,9},{5... | collective-permute-start | bytes 393224 | tf_op jit(solution)/shard_map/ppermute | solution.py:242
  120.4 8.7 %collective-permute-start.18 = (bf16[128,1024]{1,0:T(8,128)(2,1)}, bf16[128,1024]{1,0:T(8,128)(2,1)S(1)}, u32[]{:S(2)}, u32[]{:S(2)}) collective-permute-start(bf16[128,1024]{1,0:T(8,128)(2,1)} %get-tuple-element.53), channel_id=1, source_target_pairs={{4,0},{8,4},{12,8},{16,12},{20,16},{24,20},{28,24},{5,1},{9,5},{13... | collective-permute-start | bytes 786440 | tf_op jit(solution)/shard_map/ppermute | solution.py:252
  124.4 6.3 %collective-permute-start.23 = (f32[64,1024]{1,0:T(8,128)}, f32[64,1024]{1,0:T(8,128)}, u32[]{:S(2)}, u32[]{:S(2)}) collective-permute-start(f32[64,1024]{1,0:T(8,128)} %add_multiply_fusion.1), channel_id=1, source_target_pairs={{0,4},{4,0},{8,12},{12,8},{16,20},{20,16},{24,28},{28,24},{1,5},{5... | collective-permute-start | bytes 786440 | tf_op jit(solution)/shard_map/ppermute | solution.py:247
  (41 other events, 238.9 us)
Sparse Core Ops, SparseCore 0:
  9.6 29.8 all-gather.2
  102.2 27.4 reduce-scatter.1

commit v9 on v8

--- a/solution.py
+++ b/solution.py
@@ -168,12 +168,50 @@
     mixed[...] = (query[...].astype(F32) * total).astype(BF16)
 
 
-def grad_gate_body(count, own, query, rate, *rest):
-    parts, (grad_mixed, grad_out, ends) = rest[:count], rest[count:]
+def split_body(count, starts, *rest):
+    pieces, parts, whole = rest[: -count - 1], rest[-count - 1 : -1], rest[-1]
+    for r, piece in enumerate(pieces):
+        whole[:, pl.ds(pl.multiple_of(starts[r], 128), piece.shape[1])] = piece[...]
+    for h, part in enumerate(parts):
+        place = pl.multiple_of(starts[len(pieces) + h], 128)
+        part[...] = whole[:, pl.ds(place, part.shape[1])]
+
+
+def pair_grad_body(count, starts, *rest):
+    parts, weights, (own, *others) = rest[:count], rest[count : count + 4], rest[count + 4 :]
+    for part, result in zip(parts, (own, *others)):
+        total = None
+        for m, weight in enumerate(weights):
+            block = part[:, pl.ds(pl.multiple_of(starts[m], 128), weight.shape[0])]
+            found = jnp.dot(block, weight[...], preferred_element_type=F32)
+            total = found if total is None else total + found
+        result[...] = total.astype(result.dtype)
+
+
+def pair_out_body(count, starts, *rest):
+    mixed, weights, results = rest[:count], rest[count : count + 4], rest[count + 4 :]
+    for rows, result in zip(mixed, results):
+        for m, weight in enumerate(weights):
+            found = lax.dot_general(rows[...], weight[...], (((1,), (1,)), ((), ())), preferred_element_type=F32)
+            result[:, pl.ds(pl.multiple_of(starts[m], 128), weight.shape[0])] = found.astype(BF16)
+
+
+def stack_body(count, starts, *rest):
+    pieces, stack, whole = rest[:-2], rest[-2], rest[-1]
+    rows = whole.shape[0]
+    for r, piece in enumerate(pieces):
+        whole[:, pl.ds(pl.multiple_of(starts[r], 128), piece.shape[1])] = piece[...]
+    for h in range(count):
+        place = pl.multiple_of(starts[len(pieces) + h], 128)
+        stack[h * rows : (h + 1) * rows] = whole[:, pl.ds(place, stack.shape[1])]
+
+
+def grad_gate_body(count, own, query, rate, li_out, *rest):
+    parts, (grad_query, grad_out, ends) = rest[:count], rest[count:]
     total = own[...]
     for part in parts:
         total = total + part[...].astype(F32)
-    grad_mixed[...] = total
+    grad_query[...] = total * li_out[...]
     gated = total * query[...].astype(F32)
     grad_out[...] = gated
     ends[...] = fold_modes(gated, rate[...], True)
@@ -237,9 +275,27 @@
     )(*[array for _, array in inputs])
 
 
+def run_once(body, inputs, outputs, scratch=()):
+    return pl.pallas_call(
+        body,
+        in_specs=[pl.BlockSpec(memory_space=pltpu.SMEM)]
+        + [pl.BlockSpec(memory_space=pltpu.VMEM)] * (len(inputs) - 1),
+        out_specs=[pl.BlockSpec(memory_space=pltpu.VMEM)] * len(outputs),
+        out_shape=[jax.ShapeDtypeStruct(shape, dtype) for shape, dtype in outputs],
+        scratch_shapes=scratch,
+        compiler_params=pltpu.CompilerParams(vmem_limit_bytes=16 * 1024 * 1024),
+        cost_estimate=pl.CostEstimate(flops=0, bytes_accessed=0, transcendentals=0),
+    )(*inputs)
+
+
 def chip_swap(x, by):
     size = lax.axis_size("ctx")
     return lax.ppermute(x, "ctx", [(i, i ^ (2 * by)) for i in range(size)])
+
+
+def line_swap(x, by):
+    size = lax.axis_size("fsdp")
+    return lax.ppermute(x, "fsdp", [(i, i ^ by) for i in range(size)])
 
 
 def core_swap(x):
@@ -328,14 +384,12 @@
 
     mr_product = (key_mr.astype(F32) * value_mr.astype(F32)).astype(BF16)
     before = shifted(mr_product, 1)
-    cot_full = lax.all_gather(cotangent, "fsdp", axis=1, tiled=True)
-
-    other_weight = core_swap(out_weight)
-    weight_pair = jnp.where(
-        core == 0,
-        jnp.concatenate([out_weight, other_weight], axis=0),
-        jnp.concatenate([other_weight, out_weight], axis=0),
-    )
+    cot_line = [cotangent] + [line_swap(cotangent, r) for r in range(1, line_count)]
+    beside = chip_swap(out_weight, 1)
+    pairs = chips // 2
+    pair = chip // 2
+    pair_width = 4 * width
+
     rate = 1.0 / li_time
     coef = li_residue * jnp.sqrt(-jnp.expm1(-2.0 * rate))
     back_factors = lax.optimization_barrier(direct_factors(rate, rows, here // 2, True))
@@ -350,7 +404,7 @@
         short_body,
         columns,
         [
-            tile(before),
+            tile(after(before, *cot_line)),
             tile(mr_product),
             tile(query_mr),
             tile(key_li),
@@ -380,29 +434,57 @@
         0,
     )
 
-    cot_full, mixed_li = lax.optimization_barrier((cot_full, mixed_li))
-    cot_parts = [columns_at(cot_full, chip, chip_width)]
-    for s in range(1, chips):
-        cot_parts.append(chip_swap(columns_at(cot_full, chip ^ s, chip_width), s))
-
-    mixed_parts = [mixed_li] + [chip_swap(mixed_li, s) for s in range(1, chips)]
-    out_parts = []
-    for s, part in enumerate(mixed_parts):
-        found = lax.dot_general(
-            part, weight_pair, (((1,), (1,)), ((), ())), preferred_element_type=F32
-        ).astype(BF16)
-        out_parts.append((chip ^ s, found if s == 0 else chip_swap(found, s)))
-    out_full = placed(out_parts)
-    output = lax.psum_scatter(out_full, "fsdp", scatter_dimension=1, tiled=True).astype(F32)
-
-    grad_parts = []
-    for s, part in enumerate(cot_parts):
-        found = jnp.dot(part, weight_pair, preferred_element_type=F32)
-        grad_parts.append(found if s == 0 else chip_swap(found.astype(BF16), s))
-    grad_mixed, grad_li_out, back_ends = run(
-        functools.partial(grad_gate_body, chips - 1),
-        columns,
-        [tile(grad_parts[0]), tile(query_li), tile(rate)] + [tile(part) for part in grad_parts[1:]],
+    line_width = cotangent.shape[1]
+    whole_width = line_width * line_count
+    split_starts = [(line ^ r) * line_width for r in range(line_count)]
+    split_starts += [(pair ^ h) * pair_width for h in range(pairs)]
+    cot_pairs = run_once(
+        functools.partial(split_body, pairs),
+        [jnp.stack(split_starts)] + cot_line,
+        [((rows, pair_width), BF16)] * pairs,
+        [pltpu.VMEM((rows, whole_width), BF16)],
+    )
+    cot_parts = [cot_pairs[0]] + [chip_swap(cot_pairs[h], 2 * h) for h in range(1, pairs)]
+    mixed_parts = [mixed_li] + [chip_swap(mixed_li, 2 * h) for h in range(1, pairs)]
+    weights = [out_weight, core_swap(out_weight), beside, core_swap(beside)]
+    pair_starts = jnp.stack([((here & 3) ^ m) * width for m in range(4)])
+
+    share_flops = 2 * rows * columns * pair_width * pairs
+    grad_own, *grad_sent = run(
+        functools.partial(pair_grad_body, pairs),
+        columns,
+        [("scalar", pair_starts)] + [("whole", after(part, mixed_li)) for part in cot_parts] + [tile(weight) for weight in weights],
+        [(rows, F32)] + [(rows, BF16)] * (pairs - 1),
+        share_flops,
+    )
+    grad_parts = [chip_swap(part, 2 * h) for h, part in enumerate(grad_sent, 1)]
+
+    out_own, *out_sent = run_once(
+        functools.partial(pair_out_body, pairs),
+        [pair_starts, after(mixed_parts[0], grad_own)] + mixed_parts[1:] + weights,
+        [((rows, pair_width), BF16)] * pairs,
+    )
+    out_pairs = [out_own] + [chip_swap(part, 2 * h) for h, part in enumerate(out_sent, 1)]
+    out_starts = [(pair ^ h) * pair_width for h in range(pairs)]
+    out_starts += [(line ^ r) * line_width for r in range(line_count)]
+    (out_line,) = run_once(
+        functools.partial(stack_body, line_count),
+        [jnp.stack(out_starts)] + out_pairs,
+        [((line_count * rows, line_width), BF16)],
+        [pltpu.VMEM((rows, whole_width), BF16)],
+    )
+    by = line_count // 2
+    kept, arrived_out = out_line[: by * rows], line_swap(out_line[by * rows :], by)
+    while by > 1:
+        by //= 2
+        total = kept.astype(F32) + arrived_out.astype(F32)
+        kept, arrived_out = total[: by * rows], line_swap(total[by * rows :].astype(BF16), by)
+    output = kept.astype(F32) + arrived_out.astype(F32)
+
+    grad_query_li, grad_li_out, back_ends = run(
+        functools.partial(grad_gate_body, pairs - 1),
+        columns,
+        [tile(after(grad_own, out_own)), tile(query_li), tile(rate), tile(li_out)] + [tile(part) for part in grad_parts],
         [(rows, F32), (rows, F32), (rate.shape[0], F32)],
         pass_flops,
     )
@@ -414,7 +496,6 @@
         [(rows, F32)],
         3 * pass_flops,
     )
-    grad_query_li = grad_mixed * li_out
     grad_key_li, grad_query_mr, grad_spec, tap_partial = run(
         grad_long_body,
         columns,
@@ -457,15 +538,25 @@
     chip_half = (own_half + core_swap(far_half)).astype(BF16)
     everywhere = [chip_half] + [chip_swap(chip_half, s) for s in range(1, chips)]
     plane_half = pair_sum([part.astype(F32) for part in everywhere]) * grad_scale
-    other_half = core_swap(plane_half)
+    other_half = core_swap(after(plane_half, arrived_out))
     grad_taps = jnp.where(
         core == 0,
         jnp.concatenate([plane_half, other_half], axis=0),
         jnp.concatenate([other_half, plane_half], axis=0),
     )
 
-    cot_rows = jnp.concatenate(cot_parts, axis=0)
-    mixed_rows = jnp.concatenate(mixed_parts, axis=0)
+    side = chip % 2
+    near_cot = jnp.concatenate([columns_at(part, side, chip_width) for part in cot_parts], axis=0)
+    far_cot = jnp.concatenate([columns_at(part, 1 - side, chip_width) for part in cot_parts], axis=0)
+    far_cot = after(far_cot, back_ends)
+    near_mixed = jnp.concatenate(mixed_parts, axis=0)
+    if chip_width == columns:
+        passed = chip_swap(jnp.concatenate([far_cot, near_mixed], axis=0), 1)
+        got_cot, got_mixed = passed[: rows * pairs], passed[rows * pairs :]
+    else:
+        got_cot, got_mixed = chip_swap(far_cot, 1), chip_swap(near_mixed, 1)
+    cot_rows = jnp.concatenate([near_cot, after(got_cot, tap_partial)], axis=0)
+    mixed_rows = jnp.concatenate([near_mixed, got_mixed], axis=0)
 
     def weight_share(which):
         return lax.dot_general(

time: 146 us -> 184 us (1.26)
  waiting for transfers between devices: 31.2 us -> 71.2 us
  between operations: 14.6 us -> 1.22 us
  Pallas kernels: 21.2 us -> 31.6 us
  starting transfers between devices: 25.8 us -> 34.8 us
  matrix products: 10.8 us -> 5.07 us
  other arithmetic: 15.5 us -> 11 us
  blocking collectives: 9.79 us -> 12.3 us
    ppermute x0 -> x5, waiting for transfers between devices: none -> 31.2 us  [line_swap(): return lax.ppermute(x, 'fsdp', [(i, i ^ by) for i in range(size)])]
    ppermute x18 -> x12, waiting for transfers between devices: 26.9 us -> 39.6 us  [chip_swap(): return lax.ppermute(x, 'ctx', [(i, i ^ 2 * by) for i in range(size)])]
    ppermute x0 -> x5, starting transfers between devices: none -> 9.49 us  [line_swap(): return lax.ppermute(x, 'fsdp', [(i, i ^ by) for i in range(size)])]
    pallas_call x0 -> x3, Pallas kernels: none -> 6.88 us  [run_once(): pl.pallas_call(body, in_specs=[pl.BlockSpec(memory_space=pltpu.SMEM)] + [...]
    dot_general x8 -> x0, matrix products: 5.81 us -> none  [the longest x4 4.03 us: shards(): lax.dot_general(part, weight_pair, (((1,), (1,)), ((), ())), preferred_el...]
    ppermute x5 -> x6, starting transfers between devices: 1.83 us -> 7.08 us  [core_swap(): return lax.ppermute(x, 'ctx', [(i, i ^ 1) for i in range(size)])]
    ppermute x18 -> x12, starting transfers between devices: 16.2 us -> 11.9 us  [chip_swap(): return lax.ppermute(x, 'ctx', [(i, i ^ 2 * by) for i in range(size)])]
    select_n x1 -> x0, other arithmetic: 3.86 us -> none  [shards(): jnp.where(core == 0, jnp.concatenate([out_weight, other_weight], axis=0),...]
  transfers between devices with their start and end apart: 27 -> 25, of which waited for: 5 -> 9; matrix products, arithmetic and copies ran while one was open for 21% -> 9% of each run, Pallas kernels for 15% -> 16%
where the time goes in v9:
time: 184 us; the launch traced here: 183 us
  waiting for transfers between devices  71.2 us (39%)
  starting transfers between devices  34.8 us (19%)
  Pallas kernels  31.6 us (17%)
  local copies, waits for them, and re-layouts  16.1 us (9%)
  blocking collectives  12.3 us (7%)
  other arithmetic  11 us (6%)
  matrix products  5.07 us (3%)
    ppermute x12, waiting for transfers between devices, chip_swap(): return lax.ppermute(x, 'ctx', [(i, i ^ 2 * by) for i in range(size)])  39.6 us
    ppermute x5, waiting for transfers between devices, line_swap(): return lax.ppermute(x, 'fsdp', [(i, i ^ by) for i in range(size)])  31.2 us
    pallas_call x10, Pallas kernels, run(): pl.pallas_call(body, grid=(columns // tile,), in_specs=in_specs, out_spec...  24.7 us
    all_gather x1, blocking collectives, shards(): states = lax.all_gather(ends, 'ctx').reshape(-1, columns)  12.3 us
    unnamed x96, local copies, waits for them, and re-layouts  12.1 us
    ppermute x12, starting transfers between devices, chip_swap(): return lax.ppermute(x, 'ctx', [(i, i ^ 2 * by) for i in range(size)])  11.9 us
    ppermute x5, starting transfers between devices, line_swap(): return lax.ppermute(x, 'fsdp', [(i, i ^ by) for i in range(size)])  9.49 us
    ppermute x6, starting transfers between devices, core_swap(): return lax.ppermute(x, 'ctx', [(i, i ^ 1) for i in range(size)])  7.08 us
  transfers between devices with their start and end apart: 25, of which 9 were waited for; matrix products, arithmetic and copies ran while one was open for 9% of the time, Pallas kernels for 16%

profile of v9, /device:TPU:1, one launch (start us, length us, event | category | flops | bytes accessed | tf_op | source)
XLA Modules:
  0.0 183.3 jit_solution(5925000858101055606)
XLA Ops:
  0.7 2.1 %collective-permute-start.6 = (bf16[512,1024]{1,0:T(8,128)(2,1)}, bf16[512,1024]{1,0:T(8,128)(2,1)S(1)}, u32[]{:S(2)}, u32[]{:S(2)}) collective-permute-start(bf16[512,1024]{1,0:T(8,128)(2,1)} %rest_2_.3), channel_id=1, source_target_pairs={{0,8},{4,12},{8,0},{12,4},{16,24},{20,28},{24,16},{28,20},{1,9},{5... | collective-permute-start | bytes 3145736 | tf_op jit(solution)/shard_map/ppermute | solution.py:293
  3.7 22.1 %collective-permute-done.6.rest_4_ = bf16[512,1024]{1,0:T(8,128)(2,1)S(1)} collective-permute-done((bf16[512,1024]{1,0:T(8,128)(2,1)}, bf16[512,1024]{1,0:T(8,128)(2,1)S(1)}, u32[]{:S(2)}, u32[]{:S(2)}) %collective-permute-start.6) | collective-permute-done | bytes 1048608 | tf_op jit(solution)/shard_map/ppermute | solution.py:293
  28.6 2.3 %collective-permute-start.2 = (bf16[128,1024]{1,0:T(8,128)(2,1)}, bf16[128,1024]{1,0:T(8,128)(2,1)S(1)}, u32[]{:S(2)}, u32[]{:S(2)}) collective-permute-start(bf16[128,1024]{1,0:T(8,128)(2,1)} %rest_0_.1), channel_id=1, source_target_pairs={{0,2},{1,3},{2,0},{3,1},{4,6},{5,7},{6,4},{7,5},{8,10},{9,11},{10,... | collective-permute-start | bytes 786440 | tf_op jit(solution)/shard_map/ppermute | solution.py:298
  31.0 1.8 multiply_convert_fusion.product
  32.8 7.8 %collective-permute-done.1.rest_1_ = bf16[128,1024]{1,0:T(8,128)(2,1)S(1)} collective-permute-done((bf16[128,1024]{1,0:T(8,128)(2,1)}, bf16[128,1024]{1,0:T(8,128)(2,1)S(1)}, u32[]{:S(2)}, u32[]{:S(2)}) %collective-permute-start.1) | collective-permute-done | bytes 262176 | tf_op jit(solution)/shard_map/ppermute | solution.py:298
  41.3 3.9 %collective-permute-start = (bf16[128,1024]{1,0:T(8,128)(2,1)}, bf16[128,1024]{1,0:T(8,128)(2,1)}, u32[]{:S(2)}, u32[]{:S(2)}) collective-permute-start(bf16[128,1024]{1,0:T(8,128)(2,1)} %multiply_convert_fusion.product), channel_id=1, source_target_pairs={{0,4},{4,8},{8,12},{12,16},{16,20},{20,24},{24,28},{1,5},{5,9},{9,... | collective-permute-start | bytes 786440 | tf_op jit(solution)/shard_map/ppermute | solution.py:308
  45.9 2.9 %collective-permute-done.3.rest_3_ = bf16[128,1024]{1,0:T(8,128)(2,1)S(1)} collective-permute-done((bf16[128,1024]{1,0:T(8,128)(2,1)}, bf16[128,1024]{1,0:T(8,128)(2,1)S(1)}, u32[]{:S(2)}, u32[]{:S(2)}) %collective-permute-start.3) | collective-permute-done | bytes 262176 | tf_op jit(solution)/shard_map/ppermute | solution.py:298
  58.7 2.0 %shard_map.197 = (f32[256,1024]{1,0:T(8,128)S(1)}, f32[256,1024]{1,0:T(8,128)S(1)}) custom-call(f32[128,1024]{1,0:T(8,128)S(1)} %copy-done.24, f32[16,1024]{1,0:T(8,128)S(1)} %get-tuple-element.95.rate, f32[16,1024]{1,0:T(8,128)S(1)} %get-tuple-element.91.coef, f32[1,1024]{1,0:T(1,128)S(1)} %bitcast.20, bf16[256,512]{1,0:T(8,128)(2,1)S(1)} %copy-done), custom_call_target="tpu_custom_call" | custom-call | tf_op jit(solution)/shard_map/pallas_call | solution.py:267
  62.9 4.2 %shard_map.198 = (f32[256,1024]{1,0:T(8,128)S(1)}, f32[128,1024]{1,0:T(8,128)S(1)}, bf16[128,1024]{1,0:T(8,128)(2,1)S(1)}, bf16[128,1024]{1,0:T(8,128)(2,1)S(1)}, f32[16,1024]{1,0:T(8,128)S(1)}) custom-call(bf16[128,1024]{1,0:T(8,128)(2,1)} %collective-permute-done.before, bf16[128,1024]{1,0:T(8,128)(2,1)} %multiply_convert_fusion.product, ...), custom_call_target="tpu_custom_call" | custom-call | tf_op jit(solution)/shard_map/pallas_call | solution.py:267
  68.1 2.0 %shard_map.199.inner = f32[128,1024]{1,0:T(8,128)S(1)} custom-call(bf16[128,1024]{1,0:T(8,128)(2,1)S(1)} %get-tuple-element.48.signal, f32[256,1024]{1,0:T(8,128)S(1)} %get-tuple-element.49.li_spec, bf16[256,512]{1,0:T(8,128)(2,1)S(1)} %copy-done, bf16[256,768]{1,0:T(8,128)(2,1)S(1)} %copy-done.1), custom_call_target="tpu_custom_call" | custom-call | tf_op jit(solution)/shard_map/pallas_call | solution.py:267
  70.1 12.3 %all-gather.states = f32[128,1024]{1,0:T(8,128)S(1)} all-gather(f32[16,1024]{1,0:T(8,128)S(1)} %get-tuple-element.50), channel_id=2, replica_groups=mesh['ctx'=8,'fsdp'=4] {'ctx'}, dimensions={0}, use_global_device_ids=true | all-gather | bytes 589824 | tf_op jit(solution)/shard_map/all_gather | solution.py:420
  84.5 3.9 %shard_map.202 = (f32[128,1024]{1,0:T(8,128)S(1)}, bf16[128,1024]{1,0:T(8,128)(2,1)S(1)}) custom-call(s32[4]{0:T(128)S(1)} %pad_add_fusion.starts, bf16[128,2048]{1,0:T(8,128)(2,1)S(1)} %get-tuple-element.53.rest_0_, bf16[128,2048]{1,0:T(8,128)(2,1)} %collective-permute-done.4.rest_1_, bf16[512,1024]{1,0:T(8,128)(2,1)S(1)} %copy-done.2, ...), custom_call_target="tpu_custom_call" | custom-call | flops 1073741824 | bytes 6029328 | tf_op jit(solution)/shard_map/pallas_call | solution.py:267
  92.3 4.2 %shard_map.203 = (bf16[128,2048]{1,0:T(8,128)(2,1)S(1)}, bf16[128,2048]{1,0:T(8,128)(2,1)S(1)}) custom-call(s32[4]{0:T(128)S(1)} %pad_add_fusion.starts, bf16[128,1024]{1,0:T(8,128)(2,1)S(1)} %get-tuple-element.57.rest_0_, bf16[128,1024]{1,0:T(8,128)(2,1)S(1)} %collective-permute-done.8.rest_1_, bf16[512,1024]{1,0:T(8,128)(2,1)S(1)} %copy-done.2, ...), custom_call_target="tpu_custom_call" | custom-call | tf_op jit(solution)/shard_map/pallas_call | solution.py:279
  109.3 2.3 %shard_map.206.inner = f32[128,1024]{1,0:T(8,128)S(1)} custom-call(f32[128,1024]{1,0:T(8,128)S(1)} %copy-done.26, f32[256,1024]{1,0:T(8,128)S(1)} %copy-done.4, bf16[256,512]{1,0:T(8,128)(2,1)S(1)} %copy-done, bf16[256,768]{1,0:T(8,128)(2,1)S(1)} %copy-done.1), custom_call_target="tpu_custom_call" | custom-call | flops 402653184 | bytes 2752512 | tf_op jit(solution)/shard_map/pallas_call | solution.py:267
  111.6 14.8 %collective-permute-done.16 = f32[16,1024]{1,0:T(8,128)} collective-permute-done((f32[16,1024]{1,0:T(8,128)}, f32[16,1024]{1,0:T(8,128)}, u32[]{:S(2)}, u32[]{:S(2)}) %collective-permute-start.16) | collective-permute-done | bytes 65568 | tf_op jit(solution)/shard_map/ppermute | solution.py:293
  129.1 3.8 %shard_map.207 = (f32[128,1024]{1,0:T(8,128)}, f32[128,1024]{1,0:T(8,128)}, f32[256,1024]{1,0:T(8,128)S(1)}, f32[128,1024]{1,0:T(8,128)S(1)}) custom-call(f32[128,1024]{1,0:T(8,128)S(1)} %shard_map.206.inner, f32[16,1024]{1,0:T(8,128)S(1)} %get-tuple-element.95.rate, f32[16,1024]{1,0:T(8,128)S(1)} %get-tuple-element.91.coef, ...), custom_call_target="tpu_custom_call" | custom-call | flops 536870912 | bytes 6160384 | tf_op jit(solution)/shard_map/pallas_call | solution.py:267
  132.9 2.0 %collective-permute-start.18 = (f32[64,1024]{1,0:T(8,128)S(1)}, f32[64,1024]{1,0:T(8,128)S(1)}, u32[]{:S(2)}, u32[]{:S(2)}) collective-permute-start(f32[64,1024]{1,0:T(8,128)S(1)} %dynamic-slice_bitcast_fusion), channel_id=1, source_target_pairs={{0,4},{4,0},{8,12},{12,8},{16,20},{20,16},{24,28},{28,24},{1,5},{5... | collective-permute-start | bytes 786440 | tf_op jit(solution)/shard_map/ppermute | solution.py:303
  136.1 5.6 %collective-permute-start.10 = (bf16[256,1024]{1,0:T(8,128)(2,1)S(1)}, bf16[256,1024]{1,0:T(8,128)(2,1)S(1)}, u32[]{:S(2)}, u32[]{:S(2)}) collective-permute-start(bf16[256,1024]{1,0:T(8,128)(2,1)S(1)} %slice.26), channel_id=1, source_target_pairs={{0,2},{1,3},{2,0},{3,1},{4,6},{5,7},{6,4},{7,5},{8,10},{9,11},{10,... | collective-permute-start | bytes 1572872 | tf_op jit(solution)/shard_map/ppermute | solution.py:298
  147.9 17.3 %collective-permute-done.10 = bf16[256,1024]{1,0:T(8,128)(2,1)S(1)} collective-permute-done((bf16[256,1024]{1,0:T(8,128)(2,1)S(1)}, bf16[256,1024]{1,0:T(8,128)(2,1)S(1)}, u32[]{:S(2)}, u32[]{:S(2)}) %collective-permute-start.10) | collective-permute-done | bytes 524320 | tf_op jit(solution)/shard_map/ppermute | solution.py:298
  167.0 2.5 %collective-permute-start.17 = (bf16[128,1024]{1,0:T(8,128)(2,1)S(1)}, bf16[128,1024]{1,0:T(8,128)(2,1)S(1)}, u32[]{:S(2)}, u32[]{:S(2)}) collective-permute-start(bf16[128,1024]{1,0:T(8,128)(2,1)S(1)} %get-tuple-element.75), channel_id=1, source_target_pairs={{4,0},{8,4},{12,8},{16,12},{20,16},{24,20},{28,24},{5,1},{9,5},{13... | collective-permute-start | bytes 786440 | tf_op jit(solution)/shard_map/ppermute | solution.py:308
  169.6 3.3 %collective-permute-done.11 = bf16[128,1024]{1,0:T(8,128)(2,1)} collective-permute-done((bf16[128,1024]{1,0:T(8,128)(2,1)S(1)}, bf16[128,1024]{1,0:T(8,128)(2,1)}, u32[]{:S(2)}, u32[]{:S(2)}) %collective-permute-start.11) | collective-permute-done | bytes 262176 | tf_op jit(solution)/shard_map/ppermute | solution.py:298
  176.3 1.8 slice_add_fusion
  178.1 1.9 %maximum_select_fusion = f32[128,1024]{1,0:T(8,128)} fusion(f32[64,1024]{1,0:T(8,128)} %collective-permute-done.22, f32[64,1024]{1,0:T(8,128)S(1)} %add_multiply_fusion.1, pred[]{:T(512)S(6)} %eq.6), kind=kLoop, calls=%fused_computation.8 | loop fusion | flops 393216 | bytes 1048577 | tf_op jit(solution)/shard_map/jit(_where)/select_n | solution.py:542
  180.0 3.3 %add_multiply_fusion = f32[512,1024]{1,0:T(8,128)} fusion(bf16[512,1024]{1,0:T(8,128)(2,1)} %collective-permute-done.24, bf16[512,1024]{1,0:T(8,128)(2,1)S(1)} %copy-done.40, s32[]{:T(128)S(6)} %select_n.99, bf16[256,1024]{1,0:T(8,128)(2,1)S(1)} %copy-done.44, bf16[128,1024]{1,0:T(8,128)(2,1)S(1)} %copy-done.19, bf16[128,1024]{1,0:T(8,128)(2,1)S(1)} %copy-done.17), kind=kOutput, calls=%fused_computation | convolution fusion | flops 541589504 | bytes 4718596 | tf_op jit(solution)/shard_map/dot_general | solution.py:562
  (160 shorter events, 52.1 us)
Async XLA Ops:
  0.7 25.2 %collective-permute-start.6 = (bf16[512,1024]{1,0:T(8,128)(2,1)}, bf16[512,1024]{1,0:T(8,128)(2,1)S(1)}, u32[]{:S(2)}, u32[]{:S(2)}) collective-permute-start(bf16[512,1024]{1,0:T(8,128)(2,1)} %rest_2_.3), channel_id=1, source_target_pairs={{0,8},{4,12},{8,0},{12,4},{16,24},{20,28},{24,16},{28,20},{1,9},{5... | collective-permute-start | bytes 3145736 | tf_op jit(solution)/shard_map/ppermute | solution.py:293
  2.8 81.7 %collective-permute-start.5 = (bf16[512,1024]{1,0:T(8,128)(2,1)}, bf16[512,1024]{1,0:T(8,128)(2,1)S(1)}, u32[]{:S(2)}, u32[]{:S(2)}) collective-permute-start(bf16[512,1024]{1,0:T(8,128)(2,1)} %rest_2_.3), channel_id=1, source_target_pairs={{0,4},{4,0},{8,12},{12,8},{16,20},{20,16},{24,28},{28,24},{1,5},{5... | collective-permute-start | bytes 3145736 | tf_op jit(solution)/shard_map/ppermute | solution.py:303
  25.9 58.6 %collective-permute-start.7 = (bf16[512,1024]{1,0:T(8,128)(2,1)S(1)}, bf16[512,1024]{1,0:T(8,128)(2,1)}, u32[]{:S(2)}, u32[]{:S(2)}) collective-permute-start(bf16[512,1024]{1,0:T(8,128)(2,1)S(1)} %collective-permute-done.6.rest_4_), channel_id=1, source_target_pairs={{0,4},{4,0},{8,12},{12,8},{16,20},{20,16},{24,28},{28,24},{1,5},{5... | collective-permute-start | bytes 3145736 | tf_op jit(solution)/shard_map/ppermute | solution.py:303
  27.1 13.5 %collective-permute-start.1 = (bf16[128,1024]{1,0:T(8,128)(2,1)}, bf16[128,1024]{1,0:T(8,128)(2,1)S(1)}, u32[]{:S(2)}, u32[]{:S(2)}) collective-permute-start(bf16[128,1024]{1,0:T(8,128)(2,1)} %rest_0_.1), channel_id=1, source_target_pairs={{0,1},{1,0},{2,3},{3,2},{4,5},{5,4},{6,7},{7,6},{8,9},{9,8},{10,11... | collective-permute-start | bytes 786440 | tf_op jit(solution)/shard_map/ppermute | solution.py:298
  28.6 16.5 %collective-permute-start.2 = (bf16[128,1024]{1,0:T(8,128)(2,1)}, bf16[128,1024]{1,0:T(8,128)(2,1)S(1)}, u32[]{:S(2)}, u32[]{:S(2)}) collective-permute-start(bf16[128,1024]{1,0:T(8,128)(2,1)} %rest_0_.1), channel_id=1, source_target_pairs={{0,2},{1,3},{2,0},{3,1},{4,6},{5,7},{6,4},{7,5},{8,10},{9,11},{10,... | collective-permute-start | bytes 786440 | tf_op jit(solution)/shard_map/ppermute | solution.py:298
  31.0 17.8 %collective-permute-start.3 = (bf16[128,1024]{1,0:T(8,128)(2,1)}, bf16[128,1024]{1,0:T(8,128)(2,1)S(1)}, u32[]{:S(2)}, u32[]{:S(2)}) collective-permute-start(bf16[128,1024]{1,0:T(8,128)(2,1)} %rest_0_.1), channel_id=1, source_target_pairs={{0,3},{1,2},{2,1},{3,0},{4,7},{5,6},{6,5},{7,4},{8,11},{9,10},{10,... | collective-permute-start | bytes 786440 | tf_op jit(solution)/shard_map/ppermute | solution.py:298
  41.3 19.5 %collective-permute-start = (bf16[128,1024]{1,0:T(8,128)(2,1)}, bf16[128,1024]{1,0:T(8,128)(2,1)}, u32[]{:S(2)}, u32[]{:S(2)}) collective-permute-start(bf16[128,1024]{1,0:T(8,128)(2,1)} %multiply_convert_fusion.product), channel_id=1, source_target_pairs={{0,4},{4,8},{8,12},{12,16},{16,20},{20,24},{24,28},{1,5},{5,9},{9,... | collective-permute-start | bytes 786440 | tf_op jit(solution)/shard_map/ppermute | solution.py:308
  54.8 29.7 %collective-permute-start.4 = (bf16[128,2048]{1,0:T(8,128)(2,1)}, bf16[128,2048]{1,0:T(8,128)(2,1)}, u32[]{:S(2)}, u32[]{:S(2)}) collective-permute-start(bf16[128,2048]{1,0:T(8,128)(2,1)} %get-tuple-element.54), channel_id=1, source_target_pairs={{0,16},{4,20},{8,24},{12,28},{16,0},{20,4},{24,8},{28,12},{1,17},{... | collective-permute-start | bytes 1572872 | tf_op jit(solution)/shard_map/ppermute | solution.py:293
  84.1 8.1 %collective-permute-start.8 = (bf16[128,1024]{1,0:T(8,128)(2,1)S(1)}, bf16[128,1024]{1,0:T(8,128)(2,1)S(1)}, u32[]{:S(2)}, u32[]{:S(2)}) collective-permute-start(bf16[128,1024]{1,0:T(8,128)(2,1)S(1)} %get-tuple-element.57.rest_0_), channel_id=1, source_target_pairs={{0,16},{4,20},{8,24},{12,28},{16,0},{20,4},{24,8},{28,12},{1,17},{... | collective-permute-start | bytes 786440 | tf_op jit(solution)/shard_map/ppermute | solution.py:293
  88.4 9.1 %collective-permute-start.12 = (bf16[128,1024]{1,0:T(8,128)(2,1)S(1)}, bf16[128,1024]{1,0:T(8,128)(2,1)S(1)}, u32[]{:S(2)}, u32[]{:S(2)}) collective-permute-start(bf16[128,1024]{1,0:T(8,128)(2,1)S(1)} %get-tuple-element.62), channel_id=1, source_target_pairs={{0,16},{4,20},{8,24},{12,28},{16,0},{20,4},{24,8},{28,12},{1,17},{... | collective-permute-start | bytes 786440 | tf_op jit(solution)/shard_map/ppermute | solution.py:293
  101.2 40.5 %collective-permute-start.23 = (bf16[512,1024]{1,0:T(8,128)(2,1)}, bf16[512,1024]{1,0:T(8,128)(2,1)}, u32[]{:S(2)}, u32[]{:S(2)}) collective-permute-start(bf16[512,1024]{1,0:T(8,128)(2,1)} %pad_maximum_fusion), channel_id=1, source_target_pairs={{0,8},{4,12},{8,0},{12,4},{16,24},{20,28},{24,16},{28,20},{1,9},{5... | collective-permute-start | bytes 3145736 | tf_op jit(solution)/shard_map/ppermute | solution.py:293
  102.8 32.1 %collective-permute-start.9 = (bf16[128,2048]{1,0:T(8,128)(2,1)}, bf16[128,2048]{1,0:T(8,128)(2,1)}, u32[]{:S(2)}, u32[]{:S(2)}) collective-permute-start(bf16[128,2048]{1,0:T(8,128)(2,1)} %copy-done.38), channel_id=1, source_target_pairs={{0,16},{4,20},{8,24},{12,28},{16,0},{20,4},{24,8},{28,12},{1,17},{... | collective-permute-start | bytes 1572872 | tf_op jit(solution)/shard_map/ppermute | solution.py:293
  105.4 21.0 %collective-permute-start.16 = (f32[16,1024]{1,0:T(8,128)}, f32[16,1024]{1,0:T(8,128)}, u32[]{:S(2)}, u32[]{:S(2)}) collective-permute-start(f32[16,1024]{1,0:T(8,128)} %add_select_fusion.1), channel_id=1, source_target_pairs={{0,24},{4,28},{8,16},{12,20},{16,8},{20,12},{24,0},{28,4},{1,25},{... | collective-permute-start | bytes 196616 | tf_op jit(solution)/shard_map/ppermute | solution.py:293
  106.6 19.8 %collective-permute-start.15 = (f32[16,1024]{1,0:T(8,128)}, f32[16,1024]{1,0:T(8,128)}, u32[]{:S(2)}, u32[]{:S(2)}) collective-permute-start(f32[16,1024]{1,0:T(8,128)} %add_select_fusion.1), channel_id=1, source_target_pairs={{0,16},{4,20},{8,24},{12,28},{16,0},{20,4},{24,8},{28,12},{1,17},{... | collective-permute-start | bytes 196616 | tf_op jit(solution)/shard_map/ppermute | solution.py:293
  107.7 20.4 %collective-permute-start.14 = (f32[16,1024]{1,0:T(8,128)}, f32[16,1024]{1,0:T(8,128)}, u32[]{:S(2)}, u32[]{:S(2)}) collective-permute-start(f32[16,1024]{1,0:T(8,128)} %add_select_fusion.1), channel_id=1, source_target_pairs={{0,8},{4,12},{8,0},{12,4},{16,24},{20,28},{24,16},{28,20},{1,9},{5... | collective-permute-start | bytes 196616 | tf_op jit(solution)/shard_map/ppermute | solution.py:293
  132.9 12.3 %collective-permute-start.18 = (f32[64,1024]{1,0:T(8,128)S(1)}, f32[64,1024]{1,0:T(8,128)S(1)}, u32[]{:S(2)}, u32[]{:S(2)}) collective-permute-start(f32[64,1024]{1,0:T(8,128)S(1)} %dynamic-slice_bitcast_fusion), channel_id=1, source_target_pairs={{0,4},{4,0},{8,12},{12,8},{16,20},{20,16},{24,28},{28,24},{1,5},{5... | collective-permute-start | bytes 786440 | tf_op jit(solution)/shard_map/ppermute | solution.py:303
  136.1 29.1 %collective-permute-start.10 = (bf16[256,1024]{1,0:T(8,128)(2,1)S(1)}, bf16[256,1024]{1,0:T(8,128)(2,1)S(1)}, u32[]{:S(2)}, u32[]{:S(2)}) collective-permute-start(bf16[256,1024]{1,0:T(8,128)(2,1)S(1)} %slice.26), channel_id=1, source_target_pairs={{0,2},{1,3},{2,0},{3,1},{4,6},{5,7},{6,4},{7,5},{8,10},{9,11},{10,... | collective-permute-start | bytes 1572872 | tf_op jit(solution)/shard_map/ppermute | solution.py:298
  144.9 35.1 %collective-permute-start.24 = (bf16[512,1024]{1,0:T(8,128)(2,1)}, bf16[512,1024]{1,0:T(8,128)(2,1)}, u32[]{:S(2)}, u32[]{:S(2)}) collective-permute-start(bf16[512,1024]{1,0:T(8,128)(2,1)} %convolution_convert_fusion), channel_id=1, source_target_pairs={{0,4},{4,0},{8,12},{12,8},{16,20},{20,16},{24,28},{28,24},{1,5},{5... | collective-permute-start | bytes 3145736 | tf_op jit(solution)/shard_map/ppermute | solution.py:303
  145.2 21.8 %collective-permute-start.21 = (bf16[64,1024]{1,0:T(8,128)(2,1)S(1)}, bf16[64,1024]{1,0:T(8,128)(2,1)S(1)}, u32[]{:S(2)}, u32[]{:S(2)}) collective-permute-start(bf16[64,1024]{1,0:T(8,128)(2,1)S(1)} %fusion.2), channel_id=1, source_target_pairs={{0,24},{4,28},{8,16},{12,20},{16,8},{20,12},{24,0},{28,4},{1,25},{... | collective-permute-start | bytes 393224 | tf_op jit(solution)/shard_map/ppermute | solution.py:293
  146.4 23.0 %collective-permute-start.20 = (bf16[64,1024]{1,0:T(8,128)(2,1)S(1)}, bf16[64,1024]{1,0:T(8,128)(2,1)S(1)}, u32[]{:S(2)}, u32[]{:S(2)}) collective-permute-start(bf16[64,1024]{1,0:T(8,128)(2,1)S(1)} %fusion.2), channel_id=1, source_target_pairs={{0,16},{4,20},{8,24},{12,28},{16,0},{20,4},{24,8},{28,12},{1,17},{... | collective-permute-start | bytes 393224 | tf_op jit(solution)/shard_map/ppermute | solution.py:293
  146.9 22.5 %collective-permute-start.19 = (bf16[64,1024]{1,0:T(8,128)(2,1)S(1)}, bf16[64,1024]{1,0:T(8,128)(2,1)S(1)}, u32[]{:S(2)}, u32[]{:S(2)}) collective-permute-start(bf16[64,1024]{1,0:T(8,128)(2,1)S(1)} %fusion.2), channel_id=1, source_target_pairs={{0,8},{4,12},{8,0},{12,4},{16,24},{20,28},{24,16},{28,20},{1,9},{5... | collective-permute-start | bytes 393224 | tf_op jit(solution)/shard_map/ppermute | solution.py:293
  165.4 7.4 %collective-permute-start.11 = (bf16[128,1024]{1,0:T(8,128)(2,1)S(1)}, bf16[128,1024]{1,0:T(8,128)(2,1)}, u32[]{:S(2)}, u32[]{:S(2)}) collective-permute-start(bf16[128,1024]{1,0:T(8,128)(2,1)S(1)} %slice.34), channel_id=1, source_target_pairs={{0,1},{1,0},{2,3},{3,2},{4,5},{5,4},{6,7},{7,6},{8,9},{9,8},{10,11... | collective-permute-start | bytes 786440 | tf_op jit(solution)/shard_map/ppermute | solution.py:298
  167.0 7.7 %collective-permute-start.17 = (bf16[128,1024]{1,0:T(8,128)(2,1)S(1)}, bf16[128,1024]{1,0:T(8,128)(2,1)S(1)}, u32[]{:S(2)}, u32[]{:S(2)}) collective-permute-start(bf16[128,1024]{1,0:T(8,128)(2,1)S(1)} %get-tuple-element.75), channel_id=1, source_target_pairs={{4,0},{8,4},{12,8},{16,12},{20,16},{24,20},{28,24},{5,1},{9,5},{13... | collective-permute-start | bytes 786440 | tf_op jit(solution)/shard_map/ppermute | solution.py:308
  172.9 5.3 %collective-permute-start.22 = (f32[64,1024]{1,0:T(8,128)S(1)}, f32[64,1024]{1,0:T(8,128)}, u32[]{:S(2)}, u32[]{:S(2)}) collective-permute-start(f32[64,1024]{1,0:T(8,128)S(1)} %add_multiply_fusion.1), channel_id=1, source_target_pairs={{0,4},{4,0},{8,12},{12,8},{16,20},{20,16},{24,28},{28,24},{1,5},{5... | collective-permute-start | bytes 786440 | tf_op jit(solution)/shard_map/ppermute | solution.py:303
  (49 other events, 603.6 us)

commit v10 on v9

--- a/solution.py
+++ b/solution.py
@@ -178,7 +178,7 @@
 
 
 def pair_grad_body(count, starts, *rest):
-    parts, weights, (own, *others) = rest[:count], rest[count : count + 4], rest[count + 4 :]
+    parts, weights, (own, *others) = rest[:count], rest[count : count + 6], rest[count + 6 :]
     for part, result in zip(parts, (own, *others)):
         total = None
         for m, weight in enumerate(weights):
@@ -189,7 +189,7 @@
 
 
 def pair_out_body(count, starts, *rest):
-    mixed, weights, results = rest[:count], rest[count : count + 4], rest[count + 4 :]
+    mixed, weights, results = rest[:count], rest[count : count + 6], rest[count + 6 :]
     for rows, result in zip(mixed, results):
         for m, weight in enumerate(weights):
             found = lax.dot_general(rows[...], weight[...], (((1,), (1,)), ((), ())), preferred_element_type=F32)
@@ -270,20 +270,23 @@
         in_specs=in_specs,
         out_specs=[pl.BlockSpec((rows, tile), lambda c: (0, c)) for rows, _ in outputs],
         out_shape=[jax.ShapeDtypeStruct((rows, columns), dtype) for rows, dtype in outputs],
-        compiler_params=pltpu.CompilerParams(vmem_limit_bytes=12 * 1024 * 1024),
+        compiler_params=pltpu.CompilerParams(vmem_limit_bytes=56 * 1024 * 1024),
         cost_estimate=pl.CostEstimate(flops=flops, bytes_accessed=moved if flops else 0, transcendentals=0),
     )(*[array for _, array in inputs])
 
 
 def run_once(body, inputs, outputs, scratch=()):
+    def block(shape):
+        return pl.BlockSpec(shape, lambda c: (0, 0))
+
     return pl.pallas_call(
         body,
-        in_specs=[pl.BlockSpec(memory_space=pltpu.SMEM)]
-        + [pl.BlockSpec(memory_space=pltpu.VMEM)] * (len(inputs) - 1),
-        out_specs=[pl.BlockSpec(memory_space=pltpu.VMEM)] * len(outputs),
+        grid=(1,),
+        in_specs=[pl.BlockSpec(memory_space=pltpu.SMEM)] + [block(array.shape) for array in inputs[1:]],
+        out_specs=[block(shape) for shape, _ in outputs],
         out_shape=[jax.ShapeDtypeStruct(shape, dtype) for shape, dtype in outputs],
         scratch_shapes=scratch,
-        compiler_params=pltpu.CompilerParams(vmem_limit_bytes=16 * 1024 * 1024),
+        compiler_params=pltpu.CompilerParams(vmem_limit_bytes=56 * 1024 * 1024),
         cost_estimate=pl.CostEstimate(flops=0, bytes_accessed=0, transcendentals=0),
     )(*inputs)
 
@@ -306,6 +309,13 @@
 def shifted(x, by):
     size = lax.axis_size("ctx")
     return lax.ppermute(x, "ctx", [(i, i + by) for i in range(size) if 0 <= i + by < size])
+
+
+def bit_reversed(count):
+    order = [0]
+    while len(order) < count:
+        order = [2 * k for k in order] + [2 * k + 1 for k in order]
+    return order
 
 
 def columns_at(x, index, width):
@@ -384,8 +394,13 @@
 
     mr_product = (key_mr.astype(F32) * value_mr.astype(F32)).astype(BF16)
     before = shifted(mr_product, 1)
-    cot_line = [cotangent] + [line_swap(cotangent, r) for r in range(1, line_count)]
-    beside = chip_swap(out_weight, 1)
+    def line_go(numbers, *ready):
+        return [line_swap(after(cotangent, *ready), r) for r in numbers]
+
+    middle = 1 + line_count // 2
+    half = width // 2
+    first_go = line_go(range(1, 2), mr_product)
+    first_rows = chip_swap(after(out_weight[:half], before), 1)
     pairs = chips // 2
     pair = chip // 2
     pair_width = 4 * width
@@ -400,11 +415,12 @@
         [(2 * rows, F32), (2 * rows, F32)],
         0,
     )
+    second_go = line_go(range(2, middle), mr_spec, *first_go)
     spec, mr_conv, mixed_mr, li_input, ends = run(
         short_body,
         columns,
         [
-            tile(after(before, *cot_line)),
+            tile(after(before, *first_go)),
             tile(mr_product),
             tile(query_mr),
             tile(key_li),
@@ -417,7 +433,9 @@
         0,
     )
 
-    states = lax.all_gather(ends, "ctx").reshape(-1, columns)
+    third_go = line_go(range(middle, line_count), ends, *second_go)
+    second_rows = chip_swap(after(out_weight[half:], ends, first_rows), 1)
+    states = lax.all_gather(after(ends, first_rows, *second_go), "ctx").reshape(-1, columns)
     gaps = (here - 1 - jnp.arange(ctx_count, dtype=jnp.int32)).astype(F32)
     (li_inner,) = run(
         inner_body,
@@ -429,11 +447,13 @@
     li_out, mixed_li = run(
         long_body,
         columns,
-        [("scalar", gaps), tile(li_inner), tile(query_li), tile(rate), tile(coef), tile(states)],
+        [("scalar", gaps), tile(after(li_inner, second_rows, *third_go)), tile(query_li), tile(rate), tile(coef), tile(states)],
         [(rows, F32), (rows, BF16)],
         0,
     )
 
+    beside = [first_rows, second_rows]
+    cot_line = [after(piece, mixed_li) for piece in [cotangent] + first_go + second_go + third_go]
     line_width = cotangent.shape[1]
     whole_width = line_width * line_count
     split_starts = [(line ^ r) * line_width for r in range(line_count)]
@@ -446,14 +466,15 @@
     )
     cot_parts = [cot_pairs[0]] + [chip_swap(cot_pairs[h], 2 * h) for h in range(1, pairs)]
     mixed_parts = [mixed_li] + [chip_swap(mixed_li, 2 * h) for h in range(1, pairs)]
-    weights = [out_weight, core_swap(out_weight), beside, core_swap(beside)]
-    pair_starts = jnp.stack([((here & 3) ^ m) * width for m in range(4)])
+    weights = [out_weight, core_swap(out_weight)] + beside + [core_swap(piece) for piece in beside]
+    places = [(0, 0), (1, 0), (2, 0), (2, half), (3, 0), (3, half)]
+    pair_starts = jnp.stack([((here & 3) ^ m) * width + row for m, row in places])
 
     share_flops = 2 * rows * columns * pair_width * pairs
     grad_own, *grad_sent = run(
         functools.partial(pair_grad_body, pairs),
         columns,
-        [("scalar", pair_starts)] + [("whole", after(part, mixed_li)) for part in cot_parts] + [tile(weight) for weight in weights],
+        [("scalar", pair_starts)] + [("whole", after(part, *mixed_parts)) for part in cot_parts] + [tile(weight) for weight in weights],
         [(rows, F32)] + [(rows, BF16)] * (pairs - 1),
         share_flops,
     )
@@ -466,25 +487,32 @@
     )
     out_pairs = [out_own] + [chip_swap(part, 2 * h) for h, part in enumerate(out_sent, 1)]
     out_starts = [(pair ^ h) * pair_width for h in range(pairs)]
-    out_starts += [(line ^ r) * line_width for r in range(line_count)]
+    out_starts += [(line ^ r) * line_width for r in bit_reversed(line_count)]
     (out_line,) = run_once(
         functools.partial(stack_body, line_count),
         [jnp.stack(out_starts)] + out_pairs,
         [((line_count * rows, line_width), BF16)],
         [pltpu.VMEM((rows, whole_width), BF16)],
     )
-    by = line_count // 2
-    kept, arrived_out = out_line[: by * rows], line_swap(out_line[by * rows :], by)
-    while by > 1:
-        by //= 2
+    count, by = line_count // 2, 1
+    kept, arrived_out = out_line[: count * rows], line_swap(out_line[count * rows :], by)
+    first_out = arrived_out
+    while count > 1:
+        count //= 2
+        by *= 2
         total = kept.astype(F32) + arrived_out.astype(F32)
-        kept, arrived_out = total[: by * rows], line_swap(total[by * rows :].astype(BF16), by)
+        kept, arrived_out = total[: count * rows], line_swap(total[count * rows :].astype(BF16), by)
     output = kept.astype(F32) + arrived_out.astype(F32)
+
+    side = chip % 2
+    near_cot = jnp.concatenate([columns_at(part, side, chip_width) for part in cot_parts], axis=0)
+    far_cot = jnp.concatenate([columns_at(part, 1 - side, chip_width) for part in cot_parts], axis=0)
+    got_cot = chip_swap(after(far_cot, grad_own), 1)
 
     grad_query_li, grad_li_out, back_ends = run(
         functools.partial(grad_gate_body, pairs - 1),
         columns,
-        [tile(after(grad_own, out_own)), tile(query_li), tile(rate), tile(li_out)] + [tile(part) for part in grad_parts],
+        [tile(after(grad_own, out_own, got_cot)), tile(query_li), tile(rate), tile(li_out)] + [tile(part) for part in grad_parts],
         [(rows, F32), (rows, F32), (rate.shape[0], F32)],
         pass_flops,
     )
@@ -515,6 +543,9 @@
         [(rows, F32), (rows, F32), (2 * rows, F32), (rows, F32)],
         4 * pass_flops,
     )
+    near_mixed = jnp.concatenate(mixed_parts, axis=0)
+    got_mixed = chip_swap(after(near_mixed, back_entering), 1)
+    grad_spec = after(grad_spec, got_mixed, first_out)
     own_product, prev_product = run(
         grad_taps_body,
         columns,
@@ -545,17 +576,7 @@
         jnp.concatenate([other_half, plane_half], axis=0),
     )
 
-    side = chip % 2
-    near_cot = jnp.concatenate([columns_at(part, side, chip_width) for part in cot_parts], axis=0)
-    far_cot = jnp.concatenate([columns_at(part, 1 - side, chip_width) for part in cot_parts], axis=0)
-    far_cot = after(far_cot, back_ends)
-    near_mixed = jnp.concatenate(mixed_parts, axis=0)
-    if chip_width == columns:
-        passed = chip_swap(jnp.concatenate([far_cot, near_mixed], axis=0), 1)
-        got_cot, got_mixed = passed[: rows * pairs], passed[rows * pairs :]
-    else:
-        got_cot, got_mixed = chip_swap(far_cot, 1), chip_swap(near_mixed, 1)
-    cot_rows = jnp.concatenate([near_cot, after(got_cot, tap_partial)], axis=0)
+    cot_rows = jnp.concatenate([near_cot, got_cot], axis=0)
     mixed_rows = jnp.concatenate([near_mixed, got_mixed], axis=0)
 
     def weight_share(which):

time: 184 us -> 173 us (0.940)
  waiting for transfers between devices: 71.2 us -> 44.4 us
  Pallas kernels: 31.6 us -> 55.9 us
  other arithmetic: 11 us -> 6.01 us
  local copies, waits for them, and re-layouts: 16.1 us -> 13.8 us
    ppermute x5, waiting for transfers between devices: 31.2 us -> 3.95 us  [line_swap(): return lax.ppermute(x, 'fsdp', [(i, i ^ by) for i in range(size)])]
    pallas_call x10, Pallas kernels: 24.7 us -> 45.2 us  [run(): pl.pallas_call(body, grid=(columns // tile,), in_specs=in_specs, out_spec...]
    unnamed x96 -> x52, local copies, waits for them, and re-layouts: 12.1 us -> 3.97 us
    pallas_call x3, Pallas kernels: 6.88 us -> 10.6 us  [run_once(): pl.pallas_call(body, grid=(1,), in_specs=[pl.BlockSpec(memory_space=pltpu...]
    ppermute x2, waiting for transfers between devices: 0.31 us -> 3.4 us  [shifted(): lax.ppermute(x, 'ctx', [(i, i + by) for i in range(size) if 0 <= i + by <...]
    ppermute x12 -> x14, waiting for transfers between devices: 39.6 us -> 37.1 us  [chip_swap(): return lax.ppermute(x, 'ctx', [(i, i ^ 2 * by) for i in range(size)])]
    slice x3, local copies, waits for them, and re-layouts: 1.34 us -> 3.23 us  [the longest x1 2.06 us: shards(): first_rows = chip_swap(after(out_weight[:half], before), 1)]
    ppermute x6 -> x7, starting transfers between devices: 7.08 us -> 8.22 us  [core_swap(): return lax.ppermute(x, 'ctx', [(i, i ^ 1) for i in range(size)])]
  transfers between devices with their start and end apart: 25 -> 28, of which waited for: 9 -> 10; matrix products, arithmetic and copies ran while one was open for 9% -> 10% of each run, Pallas kernels for 16% -> 27%
where the time goes in v10:
time: 173 us; the launch traced here: 172 us
  Pallas kernels  55.9 us (32%)
  waiting for transfers between devices  44.4 us (26%)
  starting transfers between devices  34.7 us (20%)
  local copies, waits for them, and re-layouts  13.8 us (8%)
  blocking collectives  11.2 us (6%)
  other arithmetic  6.01 us (3%)
  matrix products  5.36 us (3%)
    pallas_call x10, Pallas kernels, run(): pl.pallas_call(body, grid=(columns // tile,), in_specs=in_specs, out_spec...  45.2 us
    ppermute x14, waiting for transfers between devices, chip_swap(): return lax.ppermute(x, 'ctx', [(i, i ^ 2 * by) for i in range(size)])  37.1 us
    ppermute x14, starting transfers between devices, chip_swap(): return lax.ppermute(x, 'ctx', [(i, i ^ 2 * by) for i in range(size)])  11.7 us
    all_gather x1, blocking collectives, shards(): lax.all_gather(after(ends, first_rows, *second_go), 'ctx')  11.2 us
    pallas_call x3, Pallas kernels, run_once(): pl.pallas_call(body, grid=(1,), in_specs=[pl.BlockSpec(memory_space=pltpu...  10.6 us
    ppermute x7, starting transfers between devices, core_swap(): return lax.ppermute(x, 'ctx', [(i, i ^ 1) for i in range(size)])  8.22 us
    ppermute x5, starting transfers between devices, line_swap(): return lax.ppermute(x, 'fsdp', [(i, i ^ by) for i in range(size)])  7.84 us
    ppermute x2, starting transfers between devices, shifted(): lax.ppermute(x, 'ctx', [(i, i + by) for i in range(size) if 0 <= i + by <...  6.9 us
  transfers between devices with their start and end apart: 28, of which 10 were waited for; matrix products, arithmetic and copies ran while one was open for 10% of the time, Pallas kernels for 27%

profile of v10, /device:TPU:1, one launch (start us, length us, event | category | flops | bytes accessed | tf_op | source)
XLA Modules:
  0.0 172.3 jit_solution(14394099271913176195)
XLA Ops:
  1.8 4.5 %collective-permute-start = (bf16[128,1024]{1,0:T(8,128)(2,1)S(1)}, bf16[128,1024]{1,0:T(8,128)(2,1)S(1)}, u32[]{:S(2)}, u32[]{:S(2)}) collective-permute-start(bf16[128,1024]{1,0:T(8,128)(2,1)S(1)} %multiply_convert_fusion.product), channel_id=1, source_target_pairs={{0,4},{4,8},{8,12},{12,16},{16,20},{20,24},{24,28},{1,5},{5,9},{9,... | collective-permute-start | bytes 786440 | tf_op jit(solution)/shard_map/ppermute | solution.py:311
  12.9 4.5 %shard_map.197 = (f32[256,1024]{1,0:T(8,128)}, f32[256,1024]{1,0:T(8,128)}) custom-call(f32[128,1024]{1,0:T(8,128)} %taps.1, f32[16,1024]{1,0:T(8,128)} %get-tuple-element.119.rate, f32[16,1024]{1,0:T(8,128)} %get-tuple-element.115.coef, f32[1,1024]{1,0:T(1,128)} %bitcast.24, bf16[256,512]{1,0:T(8,128)(2,1)} %constant.88.clone.ahead), custom_call_target="tpu_custom_call" | custom-call | tf_op jit(solution)/shard_map/pallas_call | solution.py:267
  17.4 2.4 %collective-permute-start.4 = (bf16[128,1024]{1,0:T(8,128)(2,1)S(1)}, bf16[128,1024]{1,0:T(8,128)(2,1)S(1)}, u32[]{:S(2)}, u32[]{:S(2)}) collective-permute-start(bf16[128,1024]{1,0:T(8,128)(2,1)S(1)} %copy-done.16), channel_id=1, source_target_pairs={{0,2},{1,3},{2,0},{3,1},{4,6},{5,7},{6,4},{7,5},{8,10},{9,11},{10,... | collective-permute-start | bytes 786440 | tf_op jit(solution)/shard_map/ppermute | solution.py:301
  19.8 5.3 %shard_map.198 = (f32[256,1024]{1,0:T(8,128)}, f32[128,1024]{1,0:T(8,128)}, bf16[128,1024]{1,0:T(8,128)(2,1)}, bf16[128,1024]{1,0:T(8,128)(2,1)}, f32[16,1024]{1,0:T(8,128)}) custom-call(bf16[128,1024]{1,0:T(8,128)(2,1)} %copy-done.19, bf16[128,1024]{1,0:T(8,128)(2,1)} %copy-done.11, bf16[128,1024]{1,0:T(8,128)(2,1)} %query_mr.1, bf16[128,1024]{1,0:T(8,128)(2,1)} %key_li.1, ...), custom_call_target="tpu_custom_call" | custom-call | tf_op jit(solution)/shard_map/pallas_call | solution.py:267
  25.4 2.7 %collective-permute-start.8 = (bf16[512,1024]{1,0:T(8,128)(2,1)S(1)}, bf16[512,1024]{1,0:T(8,128)(2,1)S(1)}, u32[]{:S(2)}, u32[]{:S(2)}) collective-permute-start(bf16[512,1024]{1,0:T(8,128)(2,1)S(1)} %copy-done), channel_id=1, source_target_pairs={{0,4},{4,0},{8,12},{12,8},{16,20},{20,16},{24,28},{28,24},{1,5},{5... | collective-permute-start | bytes 3145736 | tf_op jit(solution)/shard_map/ppermute | solution.py:306
  28.1 3.5 %collective-permute-done.4.rest_2_ = bf16[128,1024]{1,0:T(8,128)(2,1)S(1)} collective-permute-done((bf16[128,1024]{1,0:T(8,128)(2,1)S(1)}, bf16[128,1024]{1,0:T(8,128)(2,1)S(1)}, u32[]{:S(2)}, u32[]{:S(2)}) %collective-permute-start.4) | collective-permute-done | bytes 262176 | tf_op jit(solution)/shard_map/ppermute | solution.py:301
  32.3 3.1 %collective-permute-start.5 = (bf16[128,1024]{1,0:T(8,128)(2,1)S(1)}, bf16[128,1024]{1,0:T(8,128)(2,1)}, u32[]{:S(2)}, u32[]{:S(2)}) collective-permute-start(bf16[128,1024]{1,0:T(8,128)(2,1)S(1)} %copy-done.16), channel_id=1, source_target_pairs={{0,3},{1,2},{2,1},{3,0},{4,7},{5,6},{6,5},{7,4},{8,11},{9,10},{10,... | collective-permute-start | bytes 786440 | tf_op jit(solution)/shard_map/ppermute | solution.py:301
  36.5 4.4 %shard_map.199.inner = f32[128,1024]{1,0:T(8,128)} custom-call(bf16[128,1024]{1,0:T(8,128)(2,1)} %get-tuple-element.61.signal, f32[256,1024]{1,0:T(8,128)} %get-tuple-element.62.li_spec, bf16[256,512]{1,0:T(8,128)(2,1)} %constant.88.clone.ahead, bf16[256,768]{1,0:T(8,128)(2,1)} %constant.89.clone.back), custom_call_target="tpu_custom_call" | custom-call | tf_op jit(solution)/shard_map/pallas_call | solution.py:267
  40.9 11.2 %all-gather.states = f32[128,1024]{1,0:T(8,128)} all-gather(f32[16,1024]{1,0:T(8,128)S(1)} %copy-done.22), channel_id=2, replica_groups=mesh['ctx'=8,'fsdp'=4] {'ctx'}, dimensions={0}, use_global_device_ids=true | all-gather | bytes 589824 | tf_op jit(solution)/shard_map/all_gather | solution.py:438
  52.1 4.1 %shard_map.200 = (f32[128,1024]{1,0:T(8,128)}, bf16[128,1024]{1,0:T(8,128)(2,1)}) custom-call(f32[8]{0:T(128)} %subtract_convert_fusion.gaps, f32[128,1024]{1,0:T(8,128)} %shard_map.199.inner, bf16[128,1024]{1,0:T(8,128)(2,1)} %query.5, f32[16,1024]{1,0:T(8,128)} %get-tuple-element.119.rate, f32[16,1024]{1,0:T(8,128)} %get-tuple-element.115.coef, ...), custom_call_target="tpu_custom_call" | custom-call | tf_op jit(solution)/shard_map/pallas_call | solution.py:267
  63.0 14.8 %collective-permute-done.6.rest_1_ = bf16[128,1024]{1,0:T(8,128)(2,1)S(1)} collective-permute-done((bf16[128,1024]{1,0:T(8,128)(2,1)}, bf16[128,1024]{1,0:T(8,128)(2,1)S(1)}, u32[]{:S(2)}, u32[]{:S(2)}) %collective-permute-start.6) | collective-permute-done | bytes 262176 | tf_op jit(solution)/shard_map/ppermute | solution.py:296
  80.6 5.3 %shard_map.202 = (f32[128,1024]{1,0:T(8,128)}, bf16[128,1024]{1,0:T(8,128)(2,1)}) custom-call(s32[6]{0:T(128)} %stack.64.starts, bf16[128,2048]{1,0:T(8,128)(2,1)} %get-tuple-element.76.rest_0_, bf16[128,2048]{1,0:T(8,128)(2,1)} %collective-permute-done.7.rest_1_, bf16[512,1024]{1,0:T(8,128)(2,1)} %rest_2_.3, bf16[512,1024]{1,0:T(8,128)(2,1)} %copy-done.1, ...), custom_call_target="tpu_custom_call" | custom-call | flops 1073741824 | bytes 6029336 | tf_op jit(solution)/shard_map/pallas_call | solution.py:267
  87.5 6.0 %shard_map.203 = (bf16[128,2048]{1,0:T(8,128)(2,1)}, bf16[128,2048]{1,0:T(8,128)(2,1)}) custom-call(s32[6]{0:T(128)} %stack.64.starts, bf16[128,1024]{1,0:T(8,128)(2,1)} %get-tuple-element.80.rest_0_, bf16[128,1024]{1,0:T(8,128)(2,1)} %copy-done.4, bf16[512,1024]{1,0:T(8,128)(2,1)} %rest_2_.3, bf16[512,1024]{1,0:T(8,128)(2,1)} %copy-done.1, ...), custom_call_target="tpu_custom_call" | custom-call | tf_op jit(solution)/shard_map/pallas_call | solution.py:282
  93.5 4.9 %collective-permute-done.14 = bf16[256,1024]{1,0:T(8,128)(2,1)S(1)} collective-permute-done((bf16[256,1024]{1,0:T(8,128)(2,1)S(1)}, bf16[256,1024]{1,0:T(8,128)(2,1)S(1)}, u32[]{:S(2)}, u32[]{:S(2)}) %collective-permute-start.14) | collective-permute-done | bytes 524320 | tf_op jit(solution)/shard_map/ppermute | solution.py:296
  99.2 3.7 %shard_map.205 = (f32[128,1024]{1,0:T(8,128)}, f32[128,1024]{1,0:T(8,128)}, f32[16,1024]{1,0:T(8,128)}) custom-call(f32[128,1024]{1,0:T(8,128)} %get-tuple-element.84.own, bf16[128,1024]{1,0:T(8,128)(2,1)} %query.5, f32[16,1024]{1,0:T(8,128)} %get-tuple-element.119.rate, f32[128,1024]{1,0:T(8,128)} %get-tuple-element.85.li_out, bf16[128,1024]{1,0:T(8,128)(2,1)} %copy-done.15), custom_call_target="tpu_custom_call" | custom-call | flops 134217728 | bytes 2752512 | tf_op jit(solution)/shard_map/pallas_call | solution.py:267
  111.2 10.7 %collective-permute-done.18 = f32[16,1024]{1,0:T(8,128)S(1)} collective-permute-done((f32[16,1024]{1,0:T(8,128)S(1)}, f32[16,1024]{1,0:T(8,128)S(1)}, u32[]{:S(2)}, u32[]{:S(2)}) %collective-permute-start.18) | collective-permute-done | bytes 65568 | tf_op jit(solution)/shard_map/ppermute | solution.py:296
  124.3 2.3 %shard_map.204 = bf16[512,1024]{1,0:T(8,128)(2,1)} custom-call(s32[6]{0:T(128)} %stack.57.starts, bf16[128,2048]{1,0:T(8,128)(2,1)} %get-tuple-element.81.rest_0_, bf16[128,2048]{1,0:T(8,128)(2,1)} %copy-done.12), custom_call_target="tpu_custom_call" | custom-call | tf_op jit(solution)/shard_map/pallas_call | solution.py:282
  127.8 4.7 %shard_map.206.inner = f32[128,1024]{1,0:T(8,128)} custom-call(f32[128,1024]{1,0:T(8,128)} %get-tuple-element.87.grad_out, f32[256,1024]{1,0:T(8,128)} %get-tuple-element.62.li_spec, bf16[256,512]{1,0:T(8,128)(2,1)} %constant.88.clone.ahead, bf16[256,768]{1,0:T(8,128)(2,1)} %constant.89.clone.back), custom_call_target="tpu_custom_call" | custom-call | flops 402653184 | bytes 2752512 | tf_op jit(solution)/shard_map/pallas_call | solution.py:267
  132.6 5.8 %shard_map.207 = (f32[128,1024]{1,0:T(8,128)}, f32[128,1024]{1,0:T(8,128)}, f32[256,1024]{1,0:T(8,128)}, f32[128,1024]{1,0:T(8,128)}) custom-call(f32[128,1024]{1,0:T(8,128)} %shard_map.206.inner, f32[16,1024]{1,0:T(8,128)} %get-tuple-element.119.rate, f32[16,1024]{1,0:T(8,128)} %get-tuple-element.115.coef, f32[16,1024]{1,0:T(8,128)} %add_select_fusion.entering, ...), custom_call_target="tpu_custom_call" | custom-call | flops 536870912 | bytes 6160384 | tf_op jit(solution)/shard_map/pallas_call | solution.py:267
  148.0 3.6 %collective-permute-done.24 = bf16[64,1024]{1,0:T(8,128)(2,1)S(1)} collective-permute-done((bf16[64,1024]{1,0:T(8,128)(2,1)S(1)}, bf16[64,1024]{1,0:T(8,128)(2,1)S(1)}, u32[]{:S(2)}, u32[]{:S(2)}) %collective-permute-start.24) | collective-permute-done | bytes 131104 | tf_op jit(solution)/shard_map/ppermute | solution.py:296
  151.7 4.1 %shard_map.208 = (f32[128,1024]{1,0:T(8,128)}, bf16[128,1024]{1,0:T(8,128)(2,1)}) custom-call(f32[256,1024]{1,0:T(8,128)} %get-tuple-element.99.grad_spec, f32[256,1024]{1,0:T(8,128)} %get-tuple-element.60.mr_spec, bf16[256,768]{1,0:T(8,128)(2,1)} %constant.89.clone.back), custom_call_target="tpu_custom_call" | custom-call | flops 402653184 | bytes 3276800 | tf_op jit(solution)/shard_map/pallas_call | solution.py:267
  155.8 2.4 %collective-permute-start.21 = (bf16[128,1024]{1,0:T(8,128)(2,1)}, bf16[128,1024]{1,0:T(8,128)(2,1)S(1)}, u32[]{:S(2)}, u32[]{:S(2)}) collective-permute-start(bf16[128,1024]{1,0:T(8,128)(2,1)} %get-tuple-element.101), channel_id=1, source_target_pairs={{4,0},{8,4},{12,8},{16,12},{20,16},{24,20},{28,24},{5,1},{9,5},{13... | collective-permute-start | bytes 786440 | tf_op jit(solution)/shard_map/ppermute | solution.py:311
  164.4 3.4 %shard_map.209 = (f32[128,1024]{1,0:T(8,128)}, f32[128,1024]{1,0:T(8,128)}) custom-call(f32[128,1024]{1,0:T(8,128)} %get-tuple-element.100.own, bf16[128,1024]{1,0:T(8,128)(2,1)} %copy-done.14, bf16[128,1024]{1,0:T(8,128)(2,1)} %key.3, bf16[128,1024]{1,0:T(8,128)(2,1)} %value.1), custom_call_target="tpu_custom_call" | custom-call | flops 131072 | bytes 2359296 | tf_op jit(solution)/shard_map/pallas_call | solution.py:267
  168.6 3.6 %add_multiply_fusion = f32[512,1024]{1,0:T(8,128)} fusion(bf16[512,1024]{1,0:T(8,128)(2,1)} %collective-permute-done.27, bf16[512,1024]{1,0:T(8,128)(2,1)} %copy-done.8, bf16[512,1024]{1,0:T(8,128)(2,1)S(1)} %pad_maximum_fusion, s32[]{:T(128)S(6)} %select_n.99), kind=kOutput, calls=%fused_computation | convolution fusion | flops 538443776 | bytes 4718596 | tf_op jit(solution)/shard_map/dot_general | solution.py:583
  (123 shorter events, 50.4 us)
Async XLA Ops:
  1.8 7.8 %collective-permute-start = (bf16[128,1024]{1,0:T(8,128)(2,1)S(1)}, bf16[128,1024]{1,0:T(8,128)(2,1)S(1)}, u32[]{:S(2)}, u32[]{:S(2)}) collective-permute-start(bf16[128,1024]{1,0:T(8,128)(2,1)S(1)} %multiply_convert_fusion.product), channel_id=1, source_target_pairs={{0,4},{4,8},{8,12},{12,16},{16,20},{20,24},{24,28},{1,5},{5,9},{9,... | collective-permute-start | bytes 786440 | tf_op jit(solution)/shard_map/ppermute | solution.py:311
  9.6 15.4 %collective-permute-start.2 = (bf16[256,1024]{1,0:T(8,128)(2,1)S(1)}, bf16[256,1024]{1,0:T(8,128)(2,1)S(1)}, u32[]{:S(2)}, u32[]{:S(2)}) collective-permute-start(bf16[256,1024]{1,0:T(8,128)(2,1)S(1)} %get-tuple-element.64), channel_id=1, source_target_pairs={{0,8},{4,12},{8,0},{12,4},{16,24},{20,28},{24,16},{28,20},{1,9},{5... | collective-permute-start | bytes 1572872 | tf_op jit(solution)/shard_map/ppermute | solution.py:296
  10.9 6.5 %collective-permute-start.1 = (bf16[128,1024]{1,0:T(8,128)(2,1)S(1)}, bf16[128,1024]{1,0:T(8,128)(2,1)S(1)}, u32[]{:S(2)}, u32[]{:S(2)}) collective-permute-start(bf16[128,1024]{1,0:T(8,128)(2,1)S(1)} %copy-done.16), channel_id=1, source_target_pairs={{0,1},{1,0},{2,3},{3,2},{4,5},{5,4},{6,7},{7,6},{8,9},{9,8},{10,11... | collective-permute-start | bytes 786440 | tf_op jit(solution)/shard_map/ppermute | solution.py:301
  17.4 14.2 %collective-permute-start.4 = (bf16[128,1024]{1,0:T(8,128)(2,1)S(1)}, bf16[128,1024]{1,0:T(8,128)(2,1)S(1)}, u32[]{:S(2)}, u32[]{:S(2)}) collective-permute-start(bf16[128,1024]{1,0:T(8,128)(2,1)S(1)} %copy-done.16), channel_id=1, source_target_pairs={{0,2},{1,3},{2,0},{3,1},{4,6},{5,7},{6,4},{7,5},{8,10},{9,11},{10,... | collective-permute-start | bytes 786440 | tf_op jit(solution)/shard_map/ppermute | solution.py:301
  25.1 27.0 %collective-permute-start.3 = (bf16[256,1024]{1,0:T(8,128)(2,1)}, bf16[256,1024]{1,0:T(8,128)(2,1)S(1)}, u32[]{:S(2)}, u32[]{:S(2)}) collective-permute-start(bf16[256,1024]{1,0:T(8,128)(2,1)} %get-tuple-element.65), channel_id=1, source_target_pairs={{0,8},{4,12},{8,0},{12,4},{16,24},{20,28},{24,16},{28,20},{1,9},{5... | collective-permute-start | bytes 1572872 | tf_op jit(solution)/shard_map/ppermute | solution.py:296
  25.4 54.2 %collective-permute-start.8 = (bf16[512,1024]{1,0:T(8,128)(2,1)S(1)}, bf16[512,1024]{1,0:T(8,128)(2,1)S(1)}, u32[]{:S(2)}, u32[]{:S(2)}) collective-permute-start(bf16[512,1024]{1,0:T(8,128)(2,1)S(1)} %copy-done), channel_id=1, source_target_pairs={{0,4},{4,0},{8,12},{12,8},{16,20},{20,16},{24,28},{28,24},{1,5},{5... | collective-permute-start | bytes 3145736 | tf_op jit(solution)/shard_map/ppermute | solution.py:306
  32.3 19.8 %collective-permute-start.5 = (bf16[128,1024]{1,0:T(8,128)(2,1)S(1)}, bf16[128,1024]{1,0:T(8,128)(2,1)}, u32[]{:S(2)}, u32[]{:S(2)}) collective-permute-start(bf16[128,1024]{1,0:T(8,128)(2,1)S(1)} %copy-done.16), channel_id=1, source_target_pairs={{0,3},{1,2},{2,1},{3,0},{4,7},{5,6},{6,5},{7,4},{8,11},{9,10},{10,... | collective-permute-start | bytes 786440 | tf_op jit(solution)/shard_map/ppermute | solution.py:301
  58.5 19.2 %collective-permute-start.7 = (bf16[128,2048]{1,0:T(8,128)(2,1)}, bf16[128,2048]{1,0:T(8,128)(2,1)}, u32[]{:S(2)}, u32[]{:S(2)}) collective-permute-start(bf16[128,2048]{1,0:T(8,128)(2,1)} %get-tuple-element.77), channel_id=1, source_target_pairs={{0,16},{4,20},{8,24},{12,28},{16,0},{20,4},{24,8},{28,12},{1,17},{... | collective-permute-start | bytes 1572872 | tf_op jit(solution)/shard_map/ppermute | solution.py:296
  59.4 20.3 %collective-permute-start.9 = (bf16[256,1024]{1,0:T(8,128)(2,1)S(1)}, bf16[256,1024]{1,0:T(8,128)(2,1)}, u32[]{:S(2)}, u32[]{:S(2)}) collective-permute-start(bf16[256,1024]{1,0:T(8,128)(2,1)S(1)} %collective-permute-done.2.rest_4_), channel_id=1, source_target_pairs={{0,4},{4,0},{8,12},{12,8},{16,20},{20,16},{24,28},{28,24},{1,5},{5... | collective-permute-start | bytes 1572872 | tf_op jit(solution)/shard_map/ppermute | solution.py:306
  59.8 19.8 %collective-permute-start.10 = (bf16[256,1024]{1,0:T(8,128)(2,1)S(1)}, bf16[256,1024]{1,0:T(8,128)(2,1)}, u32[]{:S(2)}, u32[]{:S(2)}) collective-permute-start(bf16[256,1024]{1,0:T(8,128)(2,1)S(1)} %collective-permute-done.3.rest_5_), channel_id=1, source_target_pairs={{0,4},{4,0},{8,12},{12,8},{16,20},{20,16},{24,28},{28,24},{1,5},{5... | collective-permute-start | bytes 1572872 | tf_op jit(solution)/shard_map/ppermute | solution.py:306
  59.9 17.8 %collective-permute-start.6 = (bf16[128,1024]{1,0:T(8,128)(2,1)}, bf16[128,1024]{1,0:T(8,128)(2,1)S(1)}, u32[]{:S(2)}, u32[]{:S(2)}) collective-permute-start(bf16[128,1024]{1,0:T(8,128)(2,1)} %get-tuple-element.80.rest_0_), channel_id=1, source_target_pairs={{0,16},{4,20},{8,24},{12,28},{16,0},{20,4},{24,8},{28,12},{1,17},{... | collective-permute-start | bytes 786440 | tf_op jit(solution)/shard_map/ppermute | solution.py:296
  85.9 12.5 %collective-permute-start.14 = (bf16[256,1024]{1,0:T(8,128)(2,1)S(1)}, bf16[256,1024]{1,0:T(8,128)(2,1)S(1)}, u32[]{:S(2)}, u32[]{:S(2)}) collective-permute-start(bf16[256,1024]{1,0:T(8,128)(2,1)S(1)} %pad_maximum_fusion.1), channel_id=1, source_target_pairs={{0,8},{4,12},{8,0},{12,4},{16,24},{20,28},{24,16},{28,20},{1,9},{5... | collective-permute-start | bytes 1572872 | tf_op jit(solution)/shard_map/ppermute | solution.py:296
  86.8 11.6 %collective-permute-start.15 = (bf16[128,1024]{1,0:T(8,128)(2,1)}, bf16[128,1024]{1,0:T(8,128)(2,1)S(1)}, u32[]{:S(2)}, u32[]{:S(2)}) collective-permute-start(bf16[128,1024]{1,0:T(8,128)(2,1)} %get-tuple-element.86), channel_id=1, source_target_pairs={{0,16},{4,20},{8,24},{12,28},{16,0},{20,4},{24,8},{28,12},{1,17},{... | collective-permute-start | bytes 786440 | tf_op jit(solution)/shard_map/ppermute | solution.py:296
  105.3 18.2 %collective-permute-start.11 = (bf16[128,2048]{1,0:T(8,128)(2,1)}, bf16[128,2048]{1,0:T(8,128)(2,1)S(1)}, u32[]{:S(2)}, u32[]{:S(2)}) collective-permute-start(bf16[128,2048]{1,0:T(8,128)(2,1)} %get-tuple-element.82), channel_id=1, source_target_pairs={{0,16},{4,20},{8,24},{12,28},{16,0},{20,4},{24,8},{28,12},{1,17},{... | collective-permute-start | bytes 1572872 | tf_op jit(solution)/shard_map/ppermute | solution.py:296
  108.3 13.6 %collective-permute-start.18 = (f32[16,1024]{1,0:T(8,128)S(1)}, f32[16,1024]{1,0:T(8,128)S(1)}, u32[]{:S(2)}, u32[]{:S(2)}) collective-permute-start(f32[16,1024]{1,0:T(8,128)S(1)} %add_select_fusion.1), channel_id=1, source_target_pairs={{0,16},{4,20},{8,24},{12,28},{16,0},{20,4},{24,8},{28,12},{1,17},{... | collective-permute-start | bytes 196616 | tf_op jit(solution)/shard_map/ppermute | solution.py:296
  108.9 13.0 %collective-permute-start.17 = (f32[16,1024]{1,0:T(8,128)S(1)}, f32[16,1024]{1,0:T(8,128)S(1)}, u32[]{:S(2)}, u32[]{:S(2)}) collective-permute-start(f32[16,1024]{1,0:T(8,128)S(1)} %add_select_fusion.1), channel_id=1, source_target_pairs={{0,8},{4,12},{8,0},{12,4},{16,24},{20,28},{24,16},{28,20},{1,9},{5... | collective-permute-start | bytes 196616 | tf_op jit(solution)/shard_map/ppermute | solution.py:296
  122.6 18.0 %collective-permute-start.20 = (bf16[256,1024]{1,0:T(8,128)(2,1)S(1)}, bf16[256,1024]{1,0:T(8,128)(2,1)S(1)}, u32[]{:S(2)}, u32[]{:S(2)}) collective-permute-start(bf16[256,1024]{1,0:T(8,128)(2,1)S(1)} %pad_maximum_fusion.2), channel_id=1, source_target_pairs={{0,8},{4,12},{8,0},{12,4},{16,24},{20,28},{24,16},{28,20},{1,9},{5... | collective-permute-start | bytes 1572872 | tf_op jit(solution)/shard_map/ppermute | solution.py:296
  127.7 17.4 %collective-permute-start.12 = (bf16[256,1024]{1,0:T(8,128)(2,1)S(1)}, bf16[256,1024]{1,0:T(8,128)(2,1)S(1)}, u32[]{:S(2)}, u32[]{:S(2)}) collective-permute-start(bf16[256,1024]{1,0:T(8,128)(2,1)S(1)} %slice.26), channel_id=1, source_target_pairs={{0,1},{1,0},{2,3},{3,2},{4,5},{5,4},{6,7},{7,6},{8,9},{9,8},{10,11... | collective-permute-start | bytes 1572872 | tf_op jit(solution)/shard_map/ppermute | solution.py:301
  142.3 26.3 %collective-permute-start.27 = (bf16[512,1024]{1,0:T(8,128)(2,1)}, bf16[512,1024]{1,0:T(8,128)(2,1)}, u32[]{:S(2)}, u32[]{:S(2)}) collective-permute-start(bf16[512,1024]{1,0:T(8,128)(2,1)} %convolution_convert_fusion), channel_id=1, source_target_pairs={{0,4},{4,0},{8,12},{12,8},{16,20},{20,16},{24,28},{28,24},{1,5},{5... | collective-permute-start | bytes 3145736 | tf_op jit(solution)/shard_map/ppermute | solution.py:306
  143.7 7.9 %collective-permute-start.24 = (bf16[64,1024]{1,0:T(8,128)(2,1)S(1)}, bf16[64,1024]{1,0:T(8,128)(2,1)S(1)}, u32[]{:S(2)}, u32[]{:S(2)}) collective-permute-start(bf16[64,1024]{1,0:T(8,128)(2,1)S(1)} %fusion.2), channel_id=1, source_target_pairs={{0,16},{4,20},{8,24},{12,28},{16,0},{20,4},{24,8},{28,12},{1,17},{... | collective-permute-start | bytes 393224 | tf_op jit(solution)/shard_map/ppermute | solution.py:296
  144.3 7.3 %collective-permute-start.23 = (bf16[64,1024]{1,0:T(8,128)(2,1)S(1)}, bf16[64,1024]{1,0:T(8,128)(2,1)S(1)}, u32[]{:S(2)}, u32[]{:S(2)}) collective-permute-start(bf16[64,1024]{1,0:T(8,128)(2,1)S(1)} %fusion.2), channel_id=1, source_target_pairs={{0,8},{4,12},{8,0},{12,4},{16,24},{20,28},{24,16},{28,20},{1,9},{5... | collective-permute-start | bytes 393224 | tf_op jit(solution)/shard_map/ppermute | solution.py:296
  145.4 13.3 %collective-permute-start.13 = (bf16[128,1024]{1,0:T(8,128)(2,1)S(1)}, bf16[128,1024]{1,0:T(8,128)(2,1)S(1)}, u32[]{:S(2)}, u32[]{:S(2)}) collective-permute-start(bf16[128,1024]{1,0:T(8,128)(2,1)S(1)} %slice.32), channel_id=1, source_target_pairs={{0,2},{1,3},{2,0},{3,1},{4,6},{5,7},{6,4},{7,5},{8,10},{9,11},{10,... | collective-permute-start | bytes 786440 | tf_op jit(solution)/shard_map/ppermute | solution.py:301
  155.8 7.9 %collective-permute-start.21 = (bf16[128,1024]{1,0:T(8,128)(2,1)}, bf16[128,1024]{1,0:T(8,128)(2,1)S(1)}, u32[]{:S(2)}, u32[]{:S(2)}) collective-permute-start(bf16[128,1024]{1,0:T(8,128)(2,1)} %get-tuple-element.101), channel_id=1, source_target_pairs={{4,0},{8,4},{12,8},{16,12},{20,16},{24,20},{28,24},{5,1},{9,5},{13... | collective-permute-start | bytes 786440 | tf_op jit(solution)/shard_map/ppermute | solution.py:311
  158.7 9.1 %collective-permute-start.26 = (f32[64,1024]{1,0:T(8,128)S(1)}, f32[64,1024]{1,0:T(8,128)S(1)}, u32[]{:S(2)}, u32[]{:S(2)}) collective-permute-start(f32[64,1024]{1,0:T(8,128)S(1)} %add_multiply_fusion.1), channel_id=1, source_target_pairs={{0,4},{4,0},{8,12},{12,8},{16,20},{20,16},{24,28},{28,24},{1,5},{5... | collective-permute-start | bytes 786440 | tf_op jit(solution)/shard_map/ppermute | solution.py:306
  (29 other events, 291.8 us)

commit v11 on v10

--- a/solution.py
+++ b/solution.py
@@ -197,13 +197,14 @@
 
 
 def stack_body(count, starts, *rest):
-    pieces, stack, whole = rest[:-2], rest[-2], rest[-1]
+    pieces, stacks, whole = rest[:-3], rest[-3:-1], rest[-1]
     rows = whole.shape[0]
     for r, piece in enumerate(pieces):
         whole[:, pl.ds(pl.multiple_of(starts[r], 128), piece.shape[1])] = piece[...]
     for h in range(count):
         place = pl.multiple_of(starts[len(pieces) + h], 128)
-        stack[h * rows : (h + 1) * rows] = whole[:, pl.ds(place, stack.shape[1])]
+        stack, at = stacks[h // (count // 2)], h % (count // 2)
+        stack[at * rows : (at + 1) * rows] = whole[:, pl.ds(place, stack.shape[1])]
 
 
 def grad_gate_body(count, own, query, rate, li_out, *rest):
@@ -270,7 +271,7 @@
         in_specs=in_specs,
         out_specs=[pl.BlockSpec((rows, tile), lambda c: (0, c)) for rows, _ in outputs],
         out_shape=[jax.ShapeDtypeStruct((rows, columns), dtype) for rows, dtype in outputs],
-        compiler_params=pltpu.CompilerParams(vmem_limit_bytes=56 * 1024 * 1024),
+        compiler_params=pltpu.CompilerParams(vmem_limit_bytes=12 * 1024 * 1024),
         cost_estimate=pl.CostEstimate(flops=flops, bytes_accessed=moved if flops else 0, transcendentals=0),
     )(*[array for _, array in inputs])
 
@@ -286,7 +287,7 @@
         out_specs=[block(shape) for shape, _ in outputs],
         out_shape=[jax.ShapeDtypeStruct(shape, dtype) for shape, dtype in outputs],
         scratch_shapes=scratch,
-        compiler_params=pltpu.CompilerParams(vmem_limit_bytes=56 * 1024 * 1024),
+        compiler_params=pltpu.CompilerParams(vmem_limit_bytes=20 * 1024 * 1024),
         cost_estimate=pl.CostEstimate(flops=0, bytes_accessed=0, transcendentals=0),
     )(*inputs)
 
@@ -349,11 +350,12 @@
     return factors
 
 
-def entering_direct(ends, factors, here, backward):
+def entering_direct(ends, factors, here, backward, ready):
     block = factors[0]
     later_core = ((here & 1) != 0) != backward
     sibling = core_swap(ends)
     total = jnp.where(later_core, block * sibling + ends, block * ends + sibling)
+    total = after(total, *ready)
     entering = jnp.zeros_like(ends)
     for s, weight in enumerate(factors[1:], 1):
         entering = entering + weight * chip_swap(total, s)
@@ -397,15 +399,14 @@
     def line_go(numbers, *ready):
         return [line_swap(after(cotangent, *ready), r) for r in numbers]
 
-    middle = 1 + line_count // 2
     half = width // 2
     first_go = line_go(range(1, 2), mr_product)
-    first_rows = chip_swap(after(out_weight[:half], before), 1)
+    second_go = line_go(range(2, line_count), mr_product)
     pairs = chips // 2
     pair = chip // 2
     pair_width = 4 * width
 
-    rate = 1.0 / li_time
+    rate = 1.0 / after(li_time, mr_product)
     coef = li_residue * jnp.sqrt(-jnp.expm1(-2.0 * rate))
     back_factors = lax.optimization_barrier(direct_factors(rate, rows, here // 2, True))
     mr_spec, li_spec = run(
@@ -415,7 +416,7 @@
         [(2 * rows, F32), (2 * rows, F32)],
         0,
     )
-    second_go = line_go(range(2, middle), mr_spec, *first_go)
+    first_rows = chip_swap(after(out_weight[:half], mr_spec), 1)
     spec, mr_conv, mixed_mr, li_input, ends = run(
         short_body,
         columns,
@@ -433,38 +434,37 @@
         0,
     )
 
-    third_go = line_go(range(middle, line_count), ends, *second_go)
-    second_rows = chip_swap(after(out_weight[half:], ends, first_rows), 1)
-    states = lax.all_gather(after(ends, first_rows, *second_go), "ctx").reshape(-1, columns)
-    gaps = (here - 1 - jnp.arange(ctx_count, dtype=jnp.int32)).astype(F32)
-    (li_inner,) = run(
-        inner_body,
-        columns,
-        [tile(li_input), tile(li_spec), table("ahead"), table("back")],
-        [(rows, F32)],
-        0,
-    )
-    li_out, mixed_li = run(
-        long_body,
-        columns,
-        [("scalar", gaps), tile(after(li_inner, second_rows, *third_go)), tile(query_li), tile(rate), tile(coef), tile(states)],
-        [(rows, F32), (rows, BF16)],
-        0,
-    )
-
-    beside = [first_rows, second_rows]
-    cot_line = [after(piece, mixed_li) for piece in [cotangent] + first_go + second_go + third_go]
+    cot_line = [cotangent] + first_go + second_go
     line_width = cotangent.shape[1]
     whole_width = line_width * line_count
     split_starts = [(line ^ r) * line_width for r in range(line_count)]
     split_starts += [(pair ^ h) * pair_width for h in range(pairs)]
     cot_pairs = run_once(
         functools.partial(split_body, pairs),
-        [jnp.stack(split_starts)] + cot_line,
+        [jnp.stack(split_starts)] + [after(piece, ends) for piece in cot_line],
         [((rows, pair_width), BF16)] * pairs,
         [pltpu.VMEM((rows, whole_width), BF16)],
     )
     cot_parts = [cot_pairs[0]] + [chip_swap(cot_pairs[h], 2 * h) for h in range(1, pairs)]
+    second_rows = chip_swap(after(out_weight[half:], ends, first_rows), 1)
+    states = lax.all_gather(after(ends, first_rows, *cot_parts[:1]), "ctx").reshape(-1, columns)
+    gaps = (here - 1 - jnp.arange(ctx_count, dtype=jnp.int32)).astype(F32)
+    (li_inner,) = run(
+        inner_body,
+        columns,
+        [tile(li_input), tile(li_spec), table("ahead"), table("back")],
+        [(rows, F32)],
+        0,
+    )
+    li_out, mixed_li = run(
+        long_body,
+        columns,
+        [("scalar", gaps), tile(after(li_inner, second_rows)), tile(query_li), tile(rate), tile(coef), tile(states)],
+        [(rows, F32), (rows, BF16)],
+        0,
+    )
+
+    beside = [first_rows, second_rows]
     mixed_parts = [mixed_li] + [chip_swap(mixed_li, 2 * h) for h in range(1, pairs)]
     weights = [out_weight, core_swap(out_weight)] + beside + [core_swap(piece) for piece in beside]
     places = [(0, 0), (1, 0), (2, 0), (2, half), (3, 0), (3, half)]
@@ -474,11 +474,11 @@
     grad_own, *grad_sent = run(
         functools.partial(pair_grad_body, pairs),
         columns,
-        [("scalar", pair_starts)] + [("whole", after(part, *mixed_parts)) for part in cot_parts] + [tile(weight) for weight in weights],
+        [("scalar", pair_starts)] + [("whole", after(part, mixed_li)) for part in cot_parts] + [tile(weight) for weight in weights],
         [(rows, F32)] + [(rows, BF16)] * (pairs - 1),
         share_flops,
     )
-    grad_parts = [chip_swap(part, 2 * h) for h, part in enumerate(grad_sent, 1)]
+    grad_parts = [chip_swap(after(part, *mixed_parts[1:]), 2 * h) for h, part in enumerate(grad_sent, 1)]
 
     out_own, *out_sent = run_once(
         functools.partial(pair_out_body, pairs),
@@ -488,15 +488,14 @@
     out_pairs = [out_own] + [chip_swap(part, 2 * h) for h, part in enumerate(out_sent, 1)]
     out_starts = [(pair ^ h) * pair_width for h in range(pairs)]
     out_starts += [(line ^ r) * line_width for r in bit_reversed(line_count)]
-    (out_line,) = run_once(
+    kept, odd = run_once(
         functools.partial(stack_body, line_count),
         [jnp.stack(out_starts)] + out_pairs,
-        [((line_count * rows, line_width), BF16)],
+        [((line_count // 2 * rows, line_width), BF16)] * 2,
         [pltpu.VMEM((rows, whole_width), BF16)],
     )
     count, by = line_count // 2, 1
-    kept, arrived_out = out_line[: count * rows], line_swap(out_line[count * rows :], by)
-    first_out = arrived_out
+    first_out = arrived_out = line_swap(odd, by)
     while count > 1:
         count //= 2
         by *= 2
@@ -507,28 +506,46 @@
     side = chip % 2
     near_cot = jnp.concatenate([columns_at(part, side, chip_width) for part in cot_parts], axis=0)
     far_cot = jnp.concatenate([columns_at(part, 1 - side, chip_width) for part in cot_parts], axis=0)
-    got_cot = chip_swap(after(far_cot, grad_own), 1)
+    got_cot = chip_swap(far_cot, 1)
+    near_mixed = jnp.concatenate([after(part, grad_own) for part in mixed_parts], axis=0)
+    got_mixed = chip_swap(after(near_mixed, got_cot, grad_own), 1)
 
     grad_query_li, grad_li_out, back_ends = run(
         functools.partial(grad_gate_body, pairs - 1),
         columns,
-        [tile(after(grad_own, out_own, got_cot)), tile(query_li), tile(rate), tile(li_out)] + [tile(part) for part in grad_parts],
+        [tile(after(grad_own, out_own)), tile(query_li), tile(rate), tile(li_out)] + [tile(part) for part in grad_parts],
         [(rows, F32), (rows, F32), (rate.shape[0], F32)],
         pass_flops,
     )
-    back_entering = entering_direct(back_ends, back_factors, here, True)
     (grad_inner,) = run(
         grad_inner_body,
         columns,
-        [tile(grad_li_out), tile(li_spec), table("ahead"), table("back")],
+        [tile(after(grad_li_out, got_cot)), tile(li_spec), table("ahead"), table("back")],
         [(rows, F32)],
         3 * pass_flops,
     )
+    back_entering = entering_direct(
+        after(back_ends, grad_inner), back_factors, here, True, [got_mixed] + out_pairs[1:]
+    )
+    cot_rows = jnp.concatenate([near_cot, got_cot], axis=0)
+    mixed_rows = jnp.concatenate([near_mixed, got_mixed], axis=0)
+
+    def weight_share(which):
+        return lax.dot_general(
+            columns_at(cot_rows, which, width),
+            mixed_rows,
+            (((0,), (0,)), ((), ())),
+            preferred_element_type=F32,
+        )
+
+    sent_share = weight_share(1 - core).astype(BF16)
+    far_share = core_swap(sent_share)
+    grad_weight = (weight_share(core) + far_share.astype(F32)) * grad_scale
     grad_key_li, grad_query_mr, grad_spec, tap_partial = run(
         grad_long_body,
         columns,
         [
-            tile(grad_inner),
+            tile(after(grad_inner, sent_share)),
             tile(rate),
             tile(coef),
             tile(back_entering),
@@ -543,9 +560,7 @@
         [(rows, F32), (rows, F32), (2 * rows, F32), (rows, F32)],
         4 * pass_flops,
     )
-    near_mixed = jnp.concatenate(mixed_parts, axis=0)
-    got_mixed = chip_swap(after(near_mixed, back_entering), 1)
-    grad_spec = after(grad_spec, got_mixed, first_out)
+    grad_spec = after(grad_spec, first_out)
     own_product, prev_product = run(
         grad_taps_body,
         columns,
@@ -567,7 +582,7 @@
     own_half = lax.dynamic_index_in_dim(halves, core, 0, keepdims=False)
     far_half = lax.dynamic_index_in_dim(halves, 1 - core, 0, keepdims=False)
     chip_half = (own_half + core_swap(far_half)).astype(BF16)
-    everywhere = [chip_half] + [chip_swap(chip_half, s) for s in range(1, chips)]
+    everywhere = [after(chip_half, prev_product, grad_weight)] + [chip_swap(chip_half, s) for s in range(1, chips)]
     plane_half = pair_sum([part.astype(F32) for part in everywhere]) * grad_scale
     other_half = core_swap(after(plane_half, arrived_out))
     grad_taps = jnp.where(
@@ -576,19 +591,6 @@
         jnp.concatenate([other_half, plane_half], axis=0),
     )
 
-    cot_rows = jnp.concatenate([near_cot, got_cot], axis=0)
-    mixed_rows = jnp.concatenate([near_mixed, got_mixed], axis=0)
-
-    def weight_share(which):
-        return lax.dot_general(
-            columns_at(cot_rows, which, width),
-            mixed_rows,
-            (((0,), (0,)), ((), ())),
-            preferred_element_type=F32,
-        )
-
-    far_share = core_swap(weight_share(1 - core).astype(BF16))
-    grad_weight = (weight_share(core) + far_share.astype(F32)) * grad_scale
     return (
         output,
         grad_query_mr,

time: 173 us -> 163 us (0.942)
  Pallas kernels: 55.9 us -> 33.2 us
  blocking collectives: 11.2 us -> 17.3 us
  other arithmetic: 6.01 us -> 9.9 us
  starting transfers between devices: 34.7 us -> 37.8 us
    pallas_call x10, Pallas kernels: 45.2 us -> 25 us  [run(): pl.pallas_call(body, grid=(columns // tile,), in_specs=in_specs, out_spec...]
    ppermute x14, waiting for transfers between devices: 37.1 us -> 26.6 us  [chip_swap(): return lax.ppermute(x, 'ctx', [(i, i ^ 2 * by) for i in range(size)])]
    all_gather x1, blocking collectives: 11.2 us -> 17.3 us  [shards(): lax.all_gather(after(ends, first_rows, *cot_parts[:1]), 'ctx')]
    ppermute x2, waiting for transfers between devices: 3.4 us -> 8.11 us  [shifted(): lax.ppermute(x, 'ctx', [(i, i + by) for i in range(size) if 0 <= i + by <...]
    unnamed x52 -> x94, local copies, waits for them, and re-layouts: 3.97 us -> 8.36 us
    ppermute x5, starting transfers between devices: 7.84 us -> 11.5 us  [line_swap(): return lax.ppermute(x, 'fsdp', [(i, i ^ by) for i in range(size)])]
    ppermute x5, waiting for transfers between devices: 3.95 us -> 7.19 us  [line_swap(): return lax.ppermute(x, 'fsdp', [(i, i ^ by) for i in range(size)])]
    pallas_call x3, Pallas kernels: 10.6 us -> 8.26 us  [run_once(): pl.pallas_call(body, grid=(1,), in_specs=[pl.BlockSpec(memory_space=pltpu...]
  transfers between devices with their start and end apart: 28 -> 28, of which waited for: 10 -> 10; matrix products, arithmetic and copies ran while one was open for 10% -> 9% of each run, Pallas kernels for 27% -> 19%
where the time goes in v11:
time: 163 us; the launch traced here: 162 us
  waiting for transfers between devices  44.2 us (27%)
  starting transfers between devices  37.8 us (23%)
  Pallas kernels  33.2 us (20%)
  blocking collectives  17.3 us (11%)
  local copies, waits for them, and re-layouts  13.4 us (8%)
  other arithmetic  9.9 us (6%)
  matrix products  5.04 us (3%)
    ppermute x14, waiting for transfers between devices, chip_swap(): return lax.ppermute(x, 'ctx', [(i, i ^ 2 * by) for i in range(size)])  26.6 us
    pallas_call x10, Pallas kernels, run(): pl.pallas_call(body, grid=(columns // tile,), in_specs=in_specs, out_spec...  25 us
    all_gather x1, blocking collectives, shards(): lax.all_gather(after(ends, first_rows, *cot_parts[:1]), 'ctx')  17.3 us
    ppermute x14, starting transfers between devices, chip_swap(): return lax.ppermute(x, 'ctx', [(i, i ^ 2 * by) for i in range(size)])  12.7 us
    ppermute x5, starting transfers between devices, line_swap(): return lax.ppermute(x, 'fsdp', [(i, i ^ by) for i in range(size)])  11.5 us
    unnamed x94, local copies, waits for them, and re-layouts  8.36 us
    pallas_call x3, Pallas kernels, run_once(): pl.pallas_call(body, grid=(1,), in_specs=[pl.BlockSpec(memory_space=pltpu...  8.26 us
    ppermute x2, waiting for transfers between devices, shifted(): lax.ppermute(x, 'ctx', [(i, i + by) for i in range(size) if 0 <= i + by <...  8.11 us
  transfers between devices with their start and end apart: 28, of which 10 were waited for; matrix products, arithmetic and copies ran while one was open for 9% of the time, Pallas kernels for 19%

profile of v11, /device:TPU:1, one launch (start us, length us, event | category | flops | bytes accessed | tf_op | source)
XLA Modules:
  0.0 162.1 jit_solution(14800154697879464111)
XLA Ops:
  2.7 2.2 %fusion.5 = (bf16[256,1024]{1,0:T(8,128)(2,1)}, bf16[256,1024]{1,0:T(8,128)(2,1)}) fusion(bf16[512,1024]{1,0:T(8,128)(2,1)} %rest_2_.3), kind=kLoop, calls=%fused_computation.34 | loop fusion | bytes 2097152 | tf_op jit(solution)/shard_map/slice | solution.py:419
  5.7 2.0 %shard_map.197 = (f32[256,1024]{1,0:T(8,128)S(1)}, f32[256,1024]{1,0:T(8,128)S(1)}) custom-call(f32[128,1024]{1,0:T(8,128)S(1)} %copy-done.24, f32[16,1024]{1,0:T(8,128)S(1)} %get-tuple-element.133.rate, f32[16,1024]{1,0:T(8,128)S(1)} %get-tuple-element.129.coef, f32[1,1024]{1,0:T(1,128)S(1)} %bitcast.24, bf16[256,512]{1,0:T(8,128)(2,1)S(1)} %copy-done.1), custom_call_target="tpu_custom_call" | custom-call | tf_op jit(solution)/shard_map/pallas_call | solution.py:268
  8.7 2.0 %collective-permute-start.2 = (bf16[256,1024]{1,0:T(8,128)(2,1)}, bf16[256,1024]{1,0:T(8,128)(2,1)}, u32[]{:S(2)}, u32[]{:S(2)}) collective-permute-start(bf16[256,1024]{1,0:T(8,128)(2,1)} %get-tuple-element.72), channel_id=1, source_target_pairs={{0,8},{4,12},{8,0},{12,4},{16,24},{20,28},{24,16},{28,20},{1,9},{5... | collective-permute-start | bytes 1572872 | tf_op jit(solution)/shard_map/ppermute | solution.py:297
  10.7 2.6 %collective-permute-start = (bf16[128,1024]{1,0:T(8,128)(2,1)}, bf16[128,1024]{1,0:T(8,128)(2,1)}, u32[]{:S(2)}, u32[]{:S(2)}) collective-permute-start(bf16[128,1024]{1,0:T(8,128)(2,1)} %multiply_convert_fusion.product), channel_id=1, source_target_pairs={{0,4},{4,8},{8,12},{12,16},{16,20},{20,24},{24,28},{1,5},{5,9},{9,... | collective-permute-start | bytes 786440 | tf_op jit(solution)/shard_map/ppermute | solution.py:312
  15.1 2.3 %collective-permute-start.4 = (bf16[128,1024]{1,0:T(8,128)(2,1)}, bf16[128,1024]{1,0:T(8,128)(2,1)}, u32[]{:S(2)}, u32[]{:S(2)}) collective-permute-start(bf16[128,1024]{1,0:T(8,128)(2,1)} %rest_0_), channel_id=1, source_target_pairs={{0,2},{1,3},{2,0},{3,1},{4,6},{5,7},{6,4},{7,5},{8,10},{9,11},{10,... | collective-permute-start | bytes 786440 | tf_op jit(solution)/shard_map/ppermute | solution.py:302
  17.5 8.1 %collective-permute-done.before = bf16[128,1024]{1,0:T(8,128)(2,1)} collective-permute-done((bf16[128,1024]{1,0:T(8,128)(2,1)}, bf16[128,1024]{1,0:T(8,128)(2,1)}, u32[]{:S(2)}, u32[]{:S(2)}) %collective-permute-start) | collective-permute-done | bytes 262176 | tf_op jit(solution)/shard_map/ppermute | solution.py:312
  28.1 4.2 %shard_map.198 = (f32[256,1024]{1,0:T(8,128)S(1)}, f32[128,1024]{1,0:T(8,128)S(1)}, bf16[128,1024]{1,0:T(8,128)(2,1)S(1)}, bf16[128,1024]{1,0:T(8,128)(2,1)S(1)}, f32[16,1024]{1,0:T(8,128)S(1)}) custom-call(bf16[128,1024]{1,0:T(8,128)(2,1)} %collective-permute-done.before, bf16[128,1024]{1,0:T(8,128)(2,1)} %multiply_convert_fusion.product, ...), custom_call_target="tpu_custom_call" | custom-call | tf_op jit(solution)/shard_map/pallas_call | solution.py:268
  35.5 2.1 %shard_map.200 = (bf16[128,2048]{1,0:T(8,128)(2,1)S(1)}, bf16[128,2048]{1,0:T(8,128)(2,1)}) custom-call(s32[6]{0:T(128)S(1)} %stack.65.starts, bf16[128,1024]{1,0:T(8,128)(2,1)S(1)} %copy-done.30, bf16[128,1024]{1,0:T(8,128)(2,1)} %collective-permute-done.1.rest_1_, bf16[128,1024]{1,0:T(8,128)(2,1)} %collective-permute-done.4.rest_2_, ...), custom_call_target="tpu_custom_call" | custom-call | tf_op jit(solution)/shard_map/pallas_call | solution.py:283
  37.5 2.3 %collective-permute-start.3 = (bf16[256,1024]{1,0:T(8,128)(2,1)}, bf16[256,1024]{1,0:T(8,128)(2,1)}, u32[]{:S(2)}, u32[]{:S(2)}) collective-permute-start(bf16[256,1024]{1,0:T(8,128)(2,1)} %get-tuple-element.73), channel_id=1, source_target_pairs={{0,8},{4,12},{8,0},{12,4},{16,24},{20,28},{24,16},{28,20},{1,9},{5... | collective-permute-start | bytes 1572872 | tf_op jit(solution)/shard_map/ppermute | solution.py:297
  41.8 9.6 %collective-permute-done.3.rest_5_ = bf16[256,1024]{1,0:T(8,128)(2,1)} collective-permute-done((bf16[256,1024]{1,0:T(8,128)(2,1)}, bf16[256,1024]{1,0:T(8,128)(2,1)}, u32[]{:S(2)}, u32[]{:S(2)}) %collective-permute-start.3) | collective-permute-done | bytes 524320 | tf_op jit(solution)/shard_map/ppermute | solution.py:297
  56.3 2.0 %shard_map.199.inner = f32[128,1024]{1,0:T(8,128)S(1)} custom-call(bf16[128,1024]{1,0:T(8,128)(2,1)S(1)} %copy-done.29, f32[256,1024]{1,0:T(8,128)S(1)} %get-tuple-element.70.li_spec, bf16[256,512]{1,0:T(8,128)(2,1)S(1)} %copy-done.1, bf16[256,768]{1,0:T(8,128)(2,1)S(1)} %copy-done.2), custom_call_target="tpu_custom_call" | custom-call | tf_op jit(solution)/shard_map/pallas_call | solution.py:268
  58.3 17.3 %all-gather.states = f32[128,1024]{1,0:T(8,128)S(1)} all-gather(f32[16,1024]{1,0:T(8,128)S(1)} %get-tuple-element.80), channel_id=2, replica_groups=mesh['ctx'=8,'fsdp'=4] {'ctx'}, dimensions={0}, use_global_device_ids=true | all-gather | bytes 589824 | tf_op jit(solution)/shard_map/all_gather | solution.py:450
  80.0 4.2 %shard_map.202 = (f32[128,1024]{1,0:T(8,128)S(1)}, bf16[128,1024]{1,0:T(8,128)(2,1)S(1)}) custom-call(s32[6]{0:T(128)S(1)} %stack.64.starts, bf16[128,2048]{1,0:T(8,128)(2,1)S(1)} %copy-done.7, bf16[128,2048]{1,0:T(8,128)(2,1)} %collective-permute-done.6.rest_1_, bf16[512,1024]{1,0:T(8,128)(2,1)S(1)} %copy-done, ...), custom_call_target="tpu_custom_call" | custom-call | flops 1073741824 | bytes 6029336 | tf_op jit(solution)/shard_map/pallas_call | solution.py:268
  85.8 4.7 %shard_map.203 = (bf16[128,2048]{1,0:T(8,128)(2,1)S(1)}, bf16[128,2048]{1,0:T(8,128)(2,1)S(1)}) custom-call(s32[6]{0:T(128)S(1)} %stack.64.starts, bf16[128,1024]{1,0:T(8,128)(2,1)S(1)} %get-tuple-element.86.rest_0_, bf16[128,1024]{1,0:T(8,128)(2,1)S(1)} %collective-permute-done.10.rest_1_, bf16[512,1024]{1,0:T(8,128)(2,1)S(1)} %copy-done, ...), custom_call_target="tpu_custom_call" | custom-call | tf_op jit(solution)/shard_map/pallas_call | solution.py:283
  94.1 14.7 %collective-permute-done.14.rest_0_ = bf16[128,1024]{1,0:T(8,128)(2,1)S(1)} collective-permute-done((bf16[128,1024]{1,0:T(8,128)(2,1)S(1)}, bf16[128,1024]{1,0:T(8,128)(2,1)S(1)}, u32[]{:S(2)}, u32[]{:S(2)}) %collective-permute-start.14) | collective-permute-done | bytes 262176 | tf_op jit(solution)/shard_map/ppermute | solution.py:297
  110.5 2.3 %shard_map.206.inner = f32[128,1024]{1,0:T(8,128)S(1)} custom-call(f32[128,1024]{1,0:T(8,128)S(1)} %get-tuple-element.96.grad_out, f32[256,1024]{1,0:T(8,128)S(1)} %get-tuple-element.70.li_spec, bf16[256,512]{1,0:T(8,128)(2,1)S(1)} %copy-done.1, bf16[256,768]{1,0:T(8,128)(2,1)S(1)} %copy-done.2), custom_call_target="tpu_custom_call" | custom-call | flops 402653184 | bytes 2752512 | tf_op jit(solution)/shard_map/pallas_call | solution.py:268
  112.8 2.0 %collective-permute-start.17 = (f32[16,1024]{1,0:T(8,128)S(1)}, f32[16,1024]{1,0:T(8,128)S(1)}, u32[]{:S(2)}, u32[]{:S(2)}) collective-permute-start(f32[16,1024]{1,0:T(8,128)S(1)} %get-tuple-element.103), channel_id=1, source_target_pairs={{0,4},{4,0},{8,12},{12,8},{16,20},{20,16},{24,28},{28,24},{1,5},{5... | collective-permute-start | bytes 196616 | tf_op jit(solution)/shard_map/ppermute | solution.py:307
  123.0 5.2 %collective-permute-start.12 = (bf16[256,1024]{1,0:T(8,128)(2,1)}, bf16[256,1024]{1,0:T(8,128)(2,1)}, u32[]{:S(2)}, u32[]{:S(2)}) collective-permute-start(bf16[256,1024]{1,0:T(8,128)(2,1)} %get-tuple-element.90), channel_id=1, source_target_pairs={{0,1},{1,0},{2,3},{3,2},{4,5},{5,4},{6,7},{7,6},{8,9},{9,8},{10,11... | collective-permute-start | bytes 1572872 | tf_op jit(solution)/shard_map/ppermute | solution.py:302
  128.3 3.8 %shard_map.207 = (f32[128,1024]{1,0:T(8,128)}, f32[128,1024]{1,0:T(8,128)}, f32[256,1024]{1,0:T(8,128)S(1)}, f32[128,1024]{1,0:T(8,128)S(1)}) custom-call(f32[128,1024]{1,0:T(8,128)S(1)} %shard_map.206.inner, f32[16,1024]{1,0:T(8,128)S(1)} %get-tuple-element.133.rate, f32[16,1024]{1,0:T(8,128)S(1)} %get-tuple-element.129.coef, ...), custom_call_target="tpu_custom_call" | custom-call | flops 536870912 | bytes 6160384 | tf_op jit(solution)/shard_map/pallas_call | solution.py:268
  138.5 2.3 %collective-permute-done.12 = bf16[256,1024]{1,0:T(8,128)(2,1)} collective-permute-done((bf16[256,1024]{1,0:T(8,128)(2,1)}, bf16[256,1024]{1,0:T(8,128)(2,1)}, u32[]{:S(2)}, u32[]{:S(2)}) %collective-permute-start.12) | collective-permute-done | bytes 524320 | tf_op jit(solution)/shard_map/ppermute | solution.py:302
  142.4 2.3 %collective-permute-start.13 = (bf16[128,1024]{1,0:T(8,128)(2,1)S(1)}, bf16[128,1024]{1,0:T(8,128)(2,1)}, u32[]{:S(2)}, u32[]{:S(2)}) collective-permute-start(bf16[128,1024]{1,0:T(8,128)(2,1)S(1)} %slice.21), channel_id=1, source_target_pairs={{0,2},{1,3},{2,0},{3,1},{4,6},{5,7},{6,4},{7,5},{8,10},{9,11},{10,... | collective-permute-start | bytes 786440 | tf_op jit(solution)/shard_map/ppermute | solution.py:302
  146.1 3.1 %collective-permute-start.21 = (bf16[128,1024]{1,0:T(8,128)(2,1)S(1)}, bf16[128,1024]{1,0:T(8,128)(2,1)S(1)}, u32[]{:S(2)}, u32[]{:S(2)}) collective-permute-start(bf16[128,1024]{1,0:T(8,128)(2,1)S(1)} %get-tuple-element.114), channel_id=1, source_target_pairs={{4,0},{8,4},{12,8},{16,12},{20,16},{24,20},{28,24},{5,1},{9,5},{13... | collective-permute-start | bytes 786440 | tf_op jit(solution)/shard_map/ppermute | solution.py:312
  149.3 3.3 %add_multiply_fusion = f32[512,1024]{1,0:T(8,128)} fusion(bf16[512,1024]{1,0:T(8,128)(2,1)} %collective-permute-done.23, bf16[512,1024]{1,0:T(8,128)(2,1)S(1)} %copy-done.38, bf16[512,1024]{1,0:T(8,128)(2,1)S(1)} %copy-done.36, s32[]{:T(128)S(6)} %select_n.99), kind=kOutput, calls=%fused_computation | convolution fusion | flops 538443776 | bytes 4718596 | tf_op jit(solution)/shard_map/dot_general | solution.py:534
  152.7 3.7 %collective-permute-done.13 = bf16[128,1024]{1,0:T(8,128)(2,1)} collective-permute-done((bf16[128,1024]{1,0:T(8,128)(2,1)S(1)}, bf16[128,1024]{1,0:T(8,128)(2,1)}, u32[]{:S(2)}, u32[]{:S(2)}) %collective-permute-start.13) | collective-permute-done | bytes 262176 | tf_op jit(solution)/shard_map/ppermute | solution.py:302
  (164 shorter events, 52.6 us)
Async XLA Ops:
  8.7 28.8 %collective-permute-start.2 = (bf16[256,1024]{1,0:T(8,128)(2,1)}, bf16[256,1024]{1,0:T(8,128)(2,1)}, u32[]{:S(2)}, u32[]{:S(2)}) collective-permute-start(bf16[256,1024]{1,0:T(8,128)(2,1)} %get-tuple-element.72), channel_id=1, source_target_pairs={{0,8},{4,12},{8,0},{12,4},{16,24},{20,28},{24,16},{28,20},{1,9},{5... | collective-permute-start | bytes 1572872 | tf_op jit(solution)/shard_map/ppermute | solution.py:297
  10.7 14.9 %collective-permute-start = (bf16[128,1024]{1,0:T(8,128)(2,1)}, bf16[128,1024]{1,0:T(8,128)(2,1)}, u32[]{:S(2)}, u32[]{:S(2)}) collective-permute-start(bf16[128,1024]{1,0:T(8,128)(2,1)} %multiply_convert_fusion.product), channel_id=1, source_target_pairs={{0,4},{4,8},{8,12},{12,16},{16,20},{20,24},{24,28},{1,5},{5,9},{9,... | collective-permute-start | bytes 786440 | tf_op jit(solution)/shard_map/ppermute | solution.py:312
  13.3 13.5 %collective-permute-start.1 = (bf16[128,1024]{1,0:T(8,128)(2,1)}, bf16[128,1024]{1,0:T(8,128)(2,1)}, u32[]{:S(2)}, u32[]{:S(2)}) collective-permute-start(bf16[128,1024]{1,0:T(8,128)(2,1)} %rest_0_), channel_id=1, source_target_pairs={{0,1},{1,0},{2,3},{3,2},{4,5},{5,4},{6,7},{7,6},{8,9},{9,8},{10,11... | collective-permute-start | bytes 786440 | tf_op jit(solution)/shard_map/ppermute | solution.py:302
  15.1 20.4 %collective-permute-start.4 = (bf16[128,1024]{1,0:T(8,128)(2,1)}, bf16[128,1024]{1,0:T(8,128)(2,1)}, u32[]{:S(2)}, u32[]{:S(2)}) collective-permute-start(bf16[128,1024]{1,0:T(8,128)(2,1)} %rest_0_), channel_id=1, source_target_pairs={{0,2},{1,3},{2,0},{3,1},{4,6},{5,7},{6,4},{7,5},{8,10},{9,11},{10,... | collective-permute-start | bytes 786440 | tf_op jit(solution)/shard_map/ppermute | solution.py:302
  17.4 18.0 %collective-permute-start.5 = (bf16[128,1024]{1,0:T(8,128)(2,1)}, bf16[128,1024]{1,0:T(8,128)(2,1)}, u32[]{:S(2)}, u32[]{:S(2)}) collective-permute-start(bf16[128,1024]{1,0:T(8,128)(2,1)} %rest_0_), channel_id=1, source_target_pairs={{0,3},{1,2},{2,1},{3,0},{4,7},{5,6},{6,5},{7,4},{8,11},{9,10},{10,... | collective-permute-start | bytes 786440 | tf_op jit(solution)/shard_map/ppermute | solution.py:302
  37.5 13.9 %collective-permute-start.3 = (bf16[256,1024]{1,0:T(8,128)(2,1)}, bf16[256,1024]{1,0:T(8,128)(2,1)}, u32[]{:S(2)}, u32[]{:S(2)}) collective-permute-start(bf16[256,1024]{1,0:T(8,128)(2,1)} %get-tuple-element.73), channel_id=1, source_target_pairs={{0,8},{4,12},{8,0},{12,4},{16,24},{20,28},{24,16},{28,20},{1,9},{5... | collective-permute-start | bytes 1572872 | tf_op jit(solution)/shard_map/ppermute | solution.py:297
  39.9 13.9 %collective-permute-start.6 = (bf16[128,2048]{1,0:T(8,128)(2,1)}, bf16[128,2048]{1,0:T(8,128)(2,1)}, u32[]{:S(2)}, u32[]{:S(2)}) collective-permute-start(bf16[128,2048]{1,0:T(8,128)(2,1)} %get-tuple-element.83), channel_id=1, source_target_pairs={{0,16},{4,20},{8,24},{12,28},{16,0},{20,4},{24,8},{28,12},{1,17},{... | collective-permute-start | bytes 1572872 | tf_op jit(solution)/shard_map/ppermute | solution.py:297
  39.9 39.0 %collective-permute-start.7 = (bf16[512,1024]{1,0:T(8,128)(2,1)S(1)}, bf16[512,1024]{1,0:T(8,128)(2,1)}, u32[]{:S(2)}, u32[]{:S(2)}) collective-permute-start(bf16[512,1024]{1,0:T(8,128)(2,1)S(1)} %copy-done), channel_id=1, source_target_pairs={{0,4},{4,0},{8,12},{12,8},{16,20},{20,16},{24,28},{28,24},{1,5},{5... | collective-permute-start | bytes 3145736 | tf_op jit(solution)/shard_map/ppermute | solution.py:307
  41.8 37.1 %collective-permute-start.8 = (bf16[256,1024]{1,0:T(8,128)(2,1)}, bf16[256,1024]{1,0:T(8,128)(2,1)}, u32[]{:S(2)}, u32[]{:S(2)}) collective-permute-start(bf16[256,1024]{1,0:T(8,128)(2,1)} %collective-permute-done.2.rest_4_), channel_id=1, source_target_pairs={{0,4},{4,0},{8,12},{12,8},{16,20},{20,16},{24,28},{28,24},{1,5},{5... | collective-permute-start | bytes 1572872 | tf_op jit(solution)/shard_map/ppermute | solution.py:307
  51.4 27.5 %collective-permute-start.9 = (bf16[256,1024]{1,0:T(8,128)(2,1)}, bf16[256,1024]{1,0:T(8,128)(2,1)}, u32[]{:S(2)}, u32[]{:S(2)}) collective-permute-start(bf16[256,1024]{1,0:T(8,128)(2,1)} %collective-permute-done.3.rest_5_), channel_id=1, source_target_pairs={{0,4},{4,0},{8,12},{12,8},{16,20},{20,16},{24,28},{28,24},{1,5},{5... | collective-permute-start | bytes 1572872 | tf_op jit(solution)/shard_map/ppermute | solution.py:307
  56.3 35.8 %collective-permute-start.15 = (bf16[256,1024]{1,0:T(8,128)(2,1)}, bf16[256,1024]{1,0:T(8,128)(2,1)}, u32[]{:S(2)}, u32[]{:S(2)}) collective-permute-start(bf16[256,1024]{1,0:T(8,128)(2,1)} %pad_maximum_fusion.1), channel_id=1, source_target_pairs={{0,8},{4,12},{8,0},{12,4},{16,24},{20,28},{24,16},{28,20},{1,9},{5... | collective-permute-start | bytes 1572872 | tf_op jit(solution)/shard_map/ppermute | solution.py:297
  90.6 25.1 %collective-permute-start.11 = (bf16[128,2048]{1,0:T(8,128)(2,1)S(1)}, bf16[128,2048]{1,0:T(8,128)(2,1)S(1)}, u32[]{:S(2)}, u32[]{:S(2)}) collective-permute-start(bf16[128,2048]{1,0:T(8,128)(2,1)S(1)} %get-tuple-element.88), channel_id=1, source_target_pairs={{0,16},{4,20},{8,24},{12,28},{16,0},{20,4},{24,8},{28,12},{1,17},{... | collective-permute-start | bytes 1572872 | tf_op jit(solution)/shard_map/ppermute | solution.py:297
  91.3 17.4 %collective-permute-start.14 = (bf16[128,1024]{1,0:T(8,128)(2,1)S(1)}, bf16[128,1024]{1,0:T(8,128)(2,1)S(1)}, u32[]{:S(2)}, u32[]{:S(2)}) collective-permute-start(bf16[128,1024]{1,0:T(8,128)(2,1)S(1)} %get-tuple-element.94), channel_id=1, source_target_pairs={{0,16},{4,20},{8,24},{12,28},{16,0},{20,4},{24,8},{28,12},{1,17},{... | collective-permute-start | bytes 786440 | tf_op jit(solution)/shard_map/ppermute | solution.py:297
  92.2 23.5 %collective-permute-start.16 = (bf16[256,1024]{1,0:T(8,128)(2,1)S(1)}, bf16[256,1024]{1,0:T(8,128)(2,1)S(1)}, u32[]{:S(2)}, u32[]{:S(2)}) collective-permute-start(bf16[256,1024]{1,0:T(8,128)(2,1)S(1)} %pad_maximum_fusion.2), channel_id=1, source_target_pairs={{0,8},{4,12},{8,0},{12,4},{16,24},{20,28},{24,16},{28,20},{1,9},{5... | collective-permute-start | bytes 1572872 | tf_op jit(solution)/shard_map/ppermute | solution.py:297
  115.7 12.5 %collective-permute-start.20 = (f32[16,1024]{1,0:T(8,128)S(1)}, f32[16,1024]{1,0:T(8,128)S(1)}, u32[]{:S(2)}, u32[]{:S(2)}) collective-permute-start(f32[16,1024]{1,0:T(8,128)S(1)} %add_select_fusion.1), channel_id=1, source_target_pairs={{0,24},{4,28},{8,16},{12,20},{16,8},{20,12},{24,0},{28,4},{1,25},{... | collective-permute-start | bytes 196616 | tf_op jit(solution)/shard_map/ppermute | solution.py:297
  117.0 11.2 %collective-permute-start.19 = (f32[16,1024]{1,0:T(8,128)S(1)}, f32[16,1024]{1,0:T(8,128)S(1)}, u32[]{:S(2)}, u32[]{:S(2)}) collective-permute-start(f32[16,1024]{1,0:T(8,128)S(1)} %add_select_fusion.1), channel_id=1, source_target_pairs={{0,16},{4,20},{8,24},{12,28},{16,0},{20,4},{24,8},{28,12},{1,17},{... | collective-permute-start | bytes 196616 | tf_op jit(solution)/shard_map/ppermute | solution.py:297
  117.6 10.6 %collective-permute-start.18 = (f32[16,1024]{1,0:T(8,128)S(1)}, f32[16,1024]{1,0:T(8,128)S(1)}, u32[]{:S(2)}, u32[]{:S(2)}) collective-permute-start(f32[16,1024]{1,0:T(8,128)S(1)} %add_select_fusion.1), channel_id=1, source_target_pairs={{0,8},{4,12},{8,0},{12,4},{16,24},{20,28},{24,16},{28,20},{1,9},{5... | collective-permute-start | bytes 196616 | tf_op jit(solution)/shard_map/ppermute | solution.py:297
  120.3 25.8 %collective-permute-start.23 = (bf16[512,1024]{1,0:T(8,128)(2,1)}, bf16[512,1024]{1,0:T(8,128)(2,1)}, u32[]{:S(2)}, u32[]{:S(2)}) collective-permute-start(bf16[512,1024]{1,0:T(8,128)(2,1)} %convolution_convert_fusion), channel_id=1, source_target_pairs={{0,4},{4,0},{8,12},{12,8},{16,20},{20,16},{24,28},{28,24},{1,5},{5... | collective-permute-start | bytes 3145736 | tf_op jit(solution)/shard_map/ppermute | solution.py:307
  123.0 17.8 %collective-permute-start.12 = (bf16[256,1024]{1,0:T(8,128)(2,1)}, bf16[256,1024]{1,0:T(8,128)(2,1)}, u32[]{:S(2)}, u32[]{:S(2)}) collective-permute-start(bf16[256,1024]{1,0:T(8,128)(2,1)} %get-tuple-element.90), channel_id=1, source_target_pairs={{0,1},{1,0},{2,3},{3,2},{4,5},{5,4},{6,7},{7,6},{8,9},{9,8},{10,11... | collective-permute-start | bytes 1572872 | tf_op jit(solution)/shard_map/ppermute | solution.py:302
  135.8 16.8 %collective-permute-start.26 = (bf16[64,1024]{1,0:T(8,128)(2,1)S(1)}, bf16[64,1024]{1,0:T(8,128)(2,1)S(1)}, u32[]{:S(2)}, u32[]{:S(2)}) collective-permute-start(bf16[64,1024]{1,0:T(8,128)(2,1)S(1)} %fusion.2), channel_id=1, source_target_pairs={{0,24},{4,28},{8,16},{12,20},{16,8},{20,12},{24,0},{28,4},{1,25},{... | collective-permute-start | bytes 393224 | tf_op jit(solution)/shard_map/ppermute | solution.py:297
  137.1 15.5 %collective-permute-start.25 = (bf16[64,1024]{1,0:T(8,128)(2,1)S(1)}, bf16[64,1024]{1,0:T(8,128)(2,1)S(1)}, u32[]{:S(2)}, u32[]{:S(2)}) collective-permute-start(bf16[64,1024]{1,0:T(8,128)(2,1)S(1)} %fusion.2), channel_id=1, source_target_pairs={{0,16},{4,20},{8,24},{12,28},{16,0},{20,4},{24,8},{28,12},{1,17},{... | collective-permute-start | bytes 393224 | tf_op jit(solution)/shard_map/ppermute | solution.py:297
  137.2 15.3 %collective-permute-start.24 = (bf16[64,1024]{1,0:T(8,128)(2,1)S(1)}, bf16[64,1024]{1,0:T(8,128)(2,1)S(1)}, u32[]{:S(2)}, u32[]{:S(2)}) collective-permute-start(bf16[64,1024]{1,0:T(8,128)(2,1)S(1)} %fusion.2), channel_id=1, source_target_pairs={{0,8},{4,12},{8,0},{12,4},{16,24},{20,28},{24,16},{28,20},{1,9},{5... | collective-permute-start | bytes 393224 | tf_op jit(solution)/shard_map/ppermute | solution.py:297
  142.4 14.0 %collective-permute-start.13 = (bf16[128,1024]{1,0:T(8,128)(2,1)S(1)}, bf16[128,1024]{1,0:T(8,128)(2,1)}, u32[]{:S(2)}, u32[]{:S(2)}) collective-permute-start(bf16[128,1024]{1,0:T(8,128)(2,1)S(1)} %slice.21), channel_id=1, source_target_pairs={{0,2},{1,3},{2,0},{3,1},{4,6},{5,7},{6,4},{7,5},{8,10},{9,11},{10,... | collective-permute-start | bytes 786440 | tf_op jit(solution)/shard_map/ppermute | solution.py:302
  146.1 11.7 %collective-permute-start.21 = (bf16[128,1024]{1,0:T(8,128)(2,1)S(1)}, bf16[128,1024]{1,0:T(8,128)(2,1)S(1)}, u32[]{:S(2)}, u32[]{:S(2)}) collective-permute-start(bf16[128,1024]{1,0:T(8,128)(2,1)S(1)} %get-tuple-element.114), channel_id=1, source_target_pairs={{4,0},{8,4},{12,8},{16,12},{20,16},{24,20},{28,24},{5,1},{9,5},{13... | collective-permute-start | bytes 786440 | tf_op jit(solution)/shard_map/ppermute | solution.py:312
  (50 other events, 474.0 us)

commit v12 on v11

--- a/solution.py
+++ b/solution.py
@@ -178,7 +178,7 @@
 
 
 def pair_grad_body(count, starts, *rest):
-    parts, weights, (own, *others) = rest[:count], rest[count : count + 6], rest[count + 6 :]
+    parts, weights, (own, *others) = rest[:count], rest[count : count + 4], rest[count + 4 :]
     for part, result in zip(parts, (own, *others)):
         total = None
         for m, weight in enumerate(weights):
@@ -189,7 +189,7 @@
 
 
 def pair_out_body(count, starts, *rest):
-    mixed, weights, results = rest[:count], rest[count : count + 6], rest[count + 6 :]
+    mixed, weights, results = rest[:count], rest[count : count + 4], rest[count + 4 :]
     for rows, result in zip(mixed, results):
         for m, weight in enumerate(weights):
             found = lax.dot_general(rows[...], weight[...], (((1,), (1,)), ((), ())), preferred_element_type=F32)
@@ -396,12 +396,8 @@
 
     mr_product = (key_mr.astype(F32) * value_mr.astype(F32)).astype(BF16)
     before = shifted(mr_product, 1)
-    def line_go(numbers, *ready):
-        return [line_swap(after(cotangent, *ready), r) for r in numbers]
-
-    half = width // 2
-    first_go = line_go(range(1, 2), mr_product)
-    second_go = line_go(range(2, line_count), mr_product)
+    cot_line = [cotangent] + [line_swap(after(cotangent, mr_product), r) for r in range(1, line_count)]
+    beside = chip_swap(after(out_weight, before), 1)
     pairs = chips // 2
     pair = chip // 2
     pair_width = 4 * width
@@ -416,12 +412,11 @@
         [(2 * rows, F32), (2 * rows, F32)],
         0,
     )
-    first_rows = chip_swap(after(out_weight[:half], mr_spec), 1)
     spec, mr_conv, mixed_mr, li_input, ends = run(
         short_body,
         columns,
         [
-            tile(after(before, *first_go)),
+            tile(before),
             tile(mr_product),
             tile(query_mr),
             tile(key_li),
@@ -434,7 +429,6 @@
         0,
     )
 
-    cot_line = [cotangent] + first_go + second_go
     line_width = cotangent.shape[1]
     whole_width = line_width * line_count
     split_starts = [(line ^ r) * line_width for r in range(line_count)]
@@ -446,8 +440,7 @@
         [pltpu.VMEM((rows, whole_width), BF16)],
     )
     cot_parts = [cot_pairs[0]] + [chip_swap(cot_pairs[h], 2 * h) for h in range(1, pairs)]
-    second_rows = chip_swap(after(out_weight[half:], ends, first_rows), 1)
-    states = lax.all_gather(after(ends, first_rows, *cot_parts[:1]), "ctx").reshape(-1, columns)
+    states = lax.all_gather(after(ends, beside, *cot_parts[:1]), "ctx").reshape(-1, columns)
     gaps = (here - 1 - jnp.arange(ctx_count, dtype=jnp.int32)).astype(F32)
     (li_inner,) = run(
         inner_body,
@@ -459,16 +452,14 @@
     li_out, mixed_li = run(
         long_body,
         columns,
-        [("scalar", gaps), tile(after(li_inner, second_rows)), tile(query_li), tile(rate), tile(coef), tile(states)],
+        [("scalar", gaps), tile(li_inner), tile(query_li), tile(rate), tile(coef), tile(states)],
         [(rows, F32), (rows, BF16)],
         0,
     )
 
-    beside = [first_rows, second_rows]
     mixed_parts = [mixed_li] + [chip_swap(mixed_li, 2 * h) for h in range(1, pairs)]
-    weights = [out_weight, core_swap(out_weight)] + beside + [core_swap(piece) for piece in beside]
-    places = [(0, 0), (1, 0), (2, 0), (2, half), (3, 0), (3, half)]
-    pair_starts = jnp.stack([((here & 3) ^ m) * width + row for m, row in places])
+    weights = [out_weight, core_swap(out_weight), beside, core_swap(beside)]
+    pair_starts = jnp.stack([((here & 3) ^ m) * width for m in range(4)])
 
     share_flops = 2 * rows * columns * pair_width * pairs
     grad_own, *grad_sent = run(
@@ -478,14 +469,14 @@
         [(rows, F32)] + [(rows, BF16)] * (pairs - 1),
         share_flops,
     )
-    grad_parts = [chip_swap(after(part, *mixed_parts[1:]), 2 * h) for h, part in enumerate(grad_sent, 1)]
+    grad_parts = [chip_swap(part, 2 * h) for h, part in enumerate(grad_sent, 1)]
 
     out_own, *out_sent = run_once(
         functools.partial(pair_out_body, pairs),
         [pair_starts, after(mixed_parts[0], grad_own)] + mixed_parts[1:] + weights,
         [((rows, pair_width), BF16)] * pairs,
     )
-    out_pairs = [out_own] + [chip_swap(part, 2 * h) for h, part in enumerate(out_sent, 1)]
+    out_pairs = [out_own] + [chip_swap(after(part, *grad_parts), 2 * h) for h, part in enumerate(out_sent, 1)]
     out_starts = [(pair ^ h) * pair_width for h in range(pairs)]
     out_starts += [(line ^ r) * line_width for r in bit_reversed(line_count)]
     kept, odd = run_once(

time: 163 us -> 144 us (0.88)
  waiting for transfers between devices: 44.2 us -> 24.2 us
  local copies, waits for them, and re-layouts: 13.4 us -> 16.7 us
  other arithmetic: 9.9 us -> 8.21 us
    ppermute x14 -> x13, waiting for transfers between devices: 26.6 us -> 11.8 us  [chip_swap(): return lax.ppermute(x, 'ctx', [(i, i ^ 2 * by) for i in range(size)])]
    unnamed x94 -> x106, local copies, waits for them, and re-layouts: 8.36 us -> 14 us
    ppermute x2, waiting for transfers between devices: 8.11 us -> 3.3 us  [shifted(): lax.ppermute(x, 'ctx', [(i, i + by) for i in range(size) if 0 <= i + by <...]
    ppermute x14 -> x13, starting transfers between devices: 12.7 us -> 10.1 us  [chip_swap(): return lax.ppermute(x, 'ctx', [(i, i ^ 2 * by) for i in range(size)])]
    ppermute x7 -> x6, starting transfers between devices: 7.78 us -> 10.2 us  [core_swap(): return lax.ppermute(x, 'ctx', [(i, i ^ 1) for i in range(size)])]
    slice x1 -> x0, local copies, waits for them, and re-layouts: 2.23 us -> none  [shards(): first_rows = chip_swap(after(out_weight[:half], mr_spec), 1)]
    ppermute x2, starting transfers between devices: 5.69 us -> 7.61 us  [shifted(): lax.ppermute(x, 'ctx', [(i, i + by) for i in range(size) if 0 <= i + by <...]
  transfers between devices with their start and end apart: 28 -> 26, of which waited for: 10 -> 8; matrix products, arithmetic and copies ran while one was open for 9% -> 10% of each run, Pallas kernels for 19% -> 23%
where the time goes in v12:
time: 144 us; the launch traced here: 143 us
  starting transfers between devices  38.4 us (27%)
  Pallas kernels  32.3 us (22%)
  waiting for transfers between devices  24.2 us (17%)
  blocking collectives  17.2 us (12%)
  local copies, waits for them, and re-layouts  16.7 us (12%)
  other arithmetic  8.21 us (6%)
  matrix products  5.06 us (4%)
    pallas_call x10, Pallas kernels, run(): pl.pallas_call(body, grid=(columns // tile,), in_specs=in_specs, out_spec...  23.9 us
    all_gather x1, blocking collectives, shards(): lax.all_gather(after(ends, beside, *cot_parts[:1]), 'ctx')  17.2 us
    unnamed x106, local copies, waits for them, and re-layouts  14 us
    ppermute x13, waiting for transfers between devices, chip_swap(): return lax.ppermute(x, 'ctx', [(i, i ^ 2 * by) for i in range(size)])  11.8 us
    ppermute x5, starting transfers between devices, line_swap(): return lax.ppermute(x, 'fsdp', [(i, i ^ by) for i in range(size)])  10.5 us
    ppermute x6, starting transfers between devices, core_swap(): return lax.ppermute(x, 'ctx', [(i, i ^ 1) for i in range(size)])  10.2 us
    ppermute x13, starting transfers between devices, chip_swap(): return lax.ppermute(x, 'ctx', [(i, i ^ 2 * by) for i in range(size)])  10.1 us
    pallas_call x3, Pallas kernels, run_once(): pl.pallas_call(body, grid=(1,), in_specs=[pl.BlockSpec(memory_space=pltpu...  8.35 us
  transfers between devices with their start and end apart: 26, of which 8 were waited for; matrix products, arithmetic and copies ran while one was open for 10% of the time, Pallas kernels for 23%

profile of v12, /device:TPU:1, one launch (start us, length us, event | category | flops | bytes accessed | tf_op | source)
XLA Modules:
  0.0 143.3 jit_solution(1403218815685528877)
XLA Ops:
  1.9 4.5 %collective-permute-start = (bf16[128,1024]{1,0:T(8,128)(2,1)S(1)}, bf16[128,1024]{1,0:T(8,128)(2,1)S(1)}, u32[]{:S(2)}, u32[]{:S(2)}) collective-permute-start(bf16[128,1024]{1,0:T(8,128)(2,1)S(1)} %multiply_convert_fusion.product), channel_id=1, source_target_pairs={{0,4},{4,8},{8,12},{12,16},{16,20},{20,24},{24,28},{1,5},{5,9},{9,... | collective-permute-start | bytes 786440 | tf_op jit(solution)/shard_map/ppermute | solution.py:312
  6.4 3.3 %collective-permute-done.before = bf16[128,1024]{1,0:T(8,128)(2,1)S(1)} collective-permute-done((bf16[128,1024]{1,0:T(8,128)(2,1)S(1)}, bf16[128,1024]{1,0:T(8,128)(2,1)S(1)}, u32[]{:S(2)}, u32[]{:S(2)}) %collective-permute-start) | collective-permute-done | bytes 262176 | tf_op jit(solution)/shard_map/ppermute | solution.py:312
  12.2 2.3 %collective-permute-start.3 = (bf16[128,1024]{1,0:T(8,128)(2,1)}, bf16[128,1024]{1,0:T(8,128)(2,1)}, u32[]{:S(2)}, u32[]{:S(2)}) collective-permute-start(bf16[128,1024]{1,0:T(8,128)(2,1)} %rest_0_), channel_id=1, source_target_pairs={{0,2},{1,3},{2,0},{3,1},{4,6},{5,7},{6,4},{7,5},{8,10},{9,11},{10,... | collective-permute-start | bytes 786440 | tf_op jit(solution)/shard_map/ppermute | solution.py:302
  18.8 2.0 %shard_map.197 = (f32[256,1024]{1,0:T(8,128)S(1)}, f32[256,1024]{1,0:T(8,128)S(1)}) custom-call(f32[128,1024]{1,0:T(8,128)S(1)} %copy-done.30, f32[16,1024]{1,0:T(8,128)S(1)} %get-tuple-element.125.rate, f32[16,1024]{1,0:T(8,128)S(1)} %get-tuple-element.121.coef, f32[1,1024]{1,0:T(1,128)S(1)} %bitcast.22, bf16[256,512]{1,0:T(8,128)(2,1)S(1)} %copy-done), custom_call_target="tpu_custom_call" | custom-call | tf_op jit(solution)/shard_map/pallas_call | solution.py:268
  26.1 3.3 %shard_map.198 = (f32[256,1024]{1,0:T(8,128)S(1)}, f32[128,1024]{1,0:T(8,128)S(1)}, bf16[128,1024]{1,0:T(8,128)(2,1)S(1)}, bf16[128,1024]{1,0:T(8,128)(2,1)S(1)}, f32[16,1024]{1,0:T(8,128)S(1)}) custom-call(bf16[128,1024]{1,0:T(8,128)(2,1)S(1)} %copy-done.38, bf16[128,1024]{1,0:T(8,128)(2,1)S(1)} %copy-done.25, bf16[128,1024]{1,0:T(8,128)(2,1)S(1)} %copy-done.20, ...), custom_call_target="tpu_custom_call" | custom-call | tf_op jit(solution)/shard_map/pallas_call | solution.py:268
  32.6 2.1 %shard_map.200 = (bf16[128,2048]{1,0:T(8,128)(2,1)S(1)}, bf16[128,2048]{1,0:T(8,128)(2,1)}) custom-call(s32[6]{0:T(128)S(1)} %stack.57.starts, bf16[128,1024]{1,0:T(8,128)(2,1)S(1)} %copy-done.36, bf16[128,1024]{1,0:T(8,128)(2,1)} %collective-permute-done.2.rest_1_, bf16[128,1024]{1,0:T(8,128)(2,1)} %collective-permute-done.3.rest_2_, ...), custom_call_target="tpu_custom_call" | custom-call | tf_op jit(solution)/shard_map/pallas_call | solution.py:283
  34.7 3.9 %collective-permute-start.6 = (bf16[512,1024]{1,0:T(8,128)(2,1)S(1)}, bf16[512,1024]{1,0:T(8,128)(2,1)}, u32[]{:S(2)}, u32[]{:S(2)}) collective-permute-start(bf16[512,1024]{1,0:T(8,128)(2,1)S(1)} %copy-done.3), channel_id=1, source_target_pairs={{0,4},{4,0},{8,12},{12,8},{16,20},{20,16},{24,28},{28,24},{1,5},{5... | collective-permute-start | bytes 3145736 | tf_op jit(solution)/shard_map/ppermute | solution.py:307
  39.5 5.7 %collective-permute-done.5.rest_1_ = bf16[128,2048]{1,0:T(8,128)(2,1)} collective-permute-done((bf16[128,2048]{1,0:T(8,128)(2,1)}, bf16[128,2048]{1,0:T(8,128)(2,1)}, u32[]{:S(2)}, u32[]{:S(2)}) %collective-permute-start.5) | collective-permute-done | bytes 524320 | tf_op jit(solution)/shard_map/ppermute | solution.py:297
  45.2 1.8 %constant_dynamic-slice_fusion = (bf16[128,1024]{1,0:T(8,128)(2,1)}, bf16[128,1024]{1,0:T(8,128)(2,1)S(1)}) fusion(bf16[128,2048]{1,0:T(8,128)(2,1)} %collective-permute-done.5.rest_1_, s32[]{:T(128)S(6)} %select_n.84, s32[]{:T(128)S(6)} %select_n.83), kind=kLoop, calls=%fused_computation.29 | loop fusion | bytes 1048584 | tf_op jit(solution)/shard_map/dynamic_slice | solution.py:323
  48.2 2.0 %shard_map.199.inner = f32[128,1024]{1,0:T(8,128)S(1)} custom-call(bf16[128,1024]{1,0:T(8,128)(2,1)S(1)} %copy-done.35, f32[256,1024]{1,0:T(8,128)S(1)} %copy-done.5, bf16[256,512]{1,0:T(8,128)(2,1)S(1)} %copy-done.1, bf16[256,768]{1,0:T(8,128)(2,1)S(1)} %copy-done.2), custom_call_target="tpu_custom_call" | custom-call | tf_op jit(solution)/shard_map/pallas_call | solution.py:268
  50.2 17.2 %all-gather.states = f32[128,1024]{1,0:T(8,128)S(1)} all-gather(f32[16,1024]{1,0:T(8,128)S(1)} %get-tuple-element.74), channel_id=2, replica_groups=mesh['ctx'=8,'fsdp'=4] {'ctx'}, dimensions={0}, use_global_device_ids=true | all-gather | bytes 589824 | tf_op jit(solution)/shard_map/all_gather | solution.py:443
  72.1 4.0 %shard_map.202 = (f32[128,1024]{1,0:T(8,128)S(1)}, bf16[128,1024]{1,0:T(8,128)(2,1)S(1)}) custom-call(s32[4]{0:T(128)S(1)} %pad_add_fusion.starts, bf16[128,2048]{1,0:T(8,128)(2,1)S(1)} %copy-done.11, bf16[128,2048]{1,0:T(8,128)(2,1)} %collective-permute-done.5.rest_1_, bf16[512,1024]{1,0:T(8,128)(2,1)S(1)} %copy-done.3, ...), custom_call_target="tpu_custom_call" | custom-call | flops 1073741824 | bytes 6029328 | tf_op jit(solution)/shard_map/pallas_call | solution.py:268
  79.9 4.8 %shard_map.203 = (bf16[128,2048]{1,0:T(8,128)(2,1)S(1)}, bf16[128,2048]{1,0:T(8,128)(2,1)S(1)}) custom-call(s32[4]{0:T(128)S(1)} %pad_add_fusion.starts, bf16[128,1024]{1,0:T(8,128)(2,1)S(1)} %get-tuple-element.80.rest_0_, bf16[128,1024]{1,0:T(8,128)(2,1)S(1)} %collective-permute-done.8.rest_1_, bf16[512,1024]{1,0:T(8,128)(2,1)S(1)} %copy-done.3, ...), custom_call_target="tpu_custom_call" | custom-call | tf_op jit(solution)/shard_map/pallas_call | solution.py:283
  87.0 2.3 %shard_map.206.inner = f32[128,1024]{1,0:T(8,128)S(1)} custom-call(f32[128,1024]{1,0:T(8,128)S(1)} %get-tuple-element.90.grad_out, f32[256,1024]{1,0:T(8,128)S(1)} %copy-done.6, bf16[256,512]{1,0:T(8,128)(2,1)S(1)} %copy-done.1, bf16[256,768]{1,0:T(8,128)(2,1)S(1)} %copy-done.2), custom_call_target="tpu_custom_call" | custom-call | flops 402653184 | bytes 2752512 | tf_op jit(solution)/shard_map/pallas_call | solution.py:268
  92.0 5.1 %collective-permute-done.10.rest_1_ = bf16[128,2048]{1,0:T(8,128)(2,1)S(1)} collective-permute-done((bf16[128,2048]{1,0:T(8,128)(2,1)S(1)}, bf16[128,2048]{1,0:T(8,128)(2,1)S(1)}, u32[]{:S(2)}, u32[]{:S(2)}) %collective-permute-start.10) | collective-permute-done | bytes 524320 | tf_op jit(solution)/shard_map/ppermute | solution.py:297
  99.7 1.8 %convolution_convert_fusion = bf16[512,1024]{1,0:T(8,128)(2,1)} fusion(bf16[512,1024]{1,0:T(8,128)(2,1)S(1)} %constant_dynamic-update-slice_fusion, bf16[512,1024]{1,0:T(8,128)(2,1)S(1)} %pad_maximum_fusion, s32[]{:T(128)S(6)} %select_n.86), kind=kOutput, calls=%fused_computation.1 | convolution fusion | flops 537395200 | bytes 2621444 | tf_op jit(solution)/shard_map/dot_general | solution.py:525
  101.5 3.0 %collective-permute-start.21 = (bf16[512,1024]{1,0:T(8,128)(2,1)}, bf16[512,1024]{1,0:T(8,128)(2,1)}, u32[]{:S(2)}, u32[]{:S(2)}) collective-permute-start(bf16[512,1024]{1,0:T(8,128)(2,1)} %convolution_convert_fusion), channel_id=1, source_target_pairs={{0,4},{4,0},{8,12},{12,8},{16,20},{20,16},{24,28},{28,24},{1,5},{5... | collective-permute-start | bytes 3145736 | tf_op jit(solution)/shard_map/ppermute | solution.py:307
  105.9 4.3 %collective-permute-start.11 = (bf16[256,1024]{1,0:T(8,128)(2,1)}, bf16[256,1024]{1,0:T(8,128)(2,1)}, u32[]{:S(2)}, u32[]{:S(2)}) collective-permute-start(bf16[256,1024]{1,0:T(8,128)(2,1)} %get-tuple-element.86), channel_id=1, source_target_pairs={{0,1},{1,0},{2,3},{3,2},{4,5},{5,4},{6,7},{7,6},{8,9},{9,8},{10,11... | collective-permute-start | bytes 1572872 | tf_op jit(solution)/shard_map/ppermute | solution.py:302
  110.4 3.8 %shard_map.207 = (f32[128,1024]{1,0:T(8,128)}, f32[128,1024]{1,0:T(8,128)}, f32[256,1024]{1,0:T(8,128)S(1)}, f32[128,1024]{1,0:T(8,128)S(1)}) custom-call(f32[128,1024]{1,0:T(8,128)S(1)} %shard_map.206.inner, f32[16,1024]{1,0:T(8,128)S(1)} %get-tuple-element.125.rate, f32[16,1024]{1,0:T(8,128)S(1)} %get-tuple-element.121.coef, ...), custom_call_target="tpu_custom_call" | custom-call | flops 536870912 | bytes 6160384 | tf_op jit(solution)/shard_map/pallas_call | solution.py:268
  119.5 3.4 %collective-permute-done.11 = bf16[256,1024]{1,0:T(8,128)(2,1)} collective-permute-done((bf16[256,1024]{1,0:T(8,128)(2,1)}, bf16[256,1024]{1,0:T(8,128)(2,1)}, u32[]{:S(2)}, u32[]{:S(2)}) %collective-permute-start.11) | collective-permute-done | bytes 524320 | tf_op jit(solution)/shard_map/ppermute | solution.py:302
  124.4 2.6 %collective-permute-start.12 = (bf16[128,1024]{1,0:T(8,128)(2,1)S(1)}, bf16[128,1024]{1,0:T(8,128)(2,1)S(1)}, u32[]{:S(2)}, u32[]{:S(2)}) collective-permute-start(bf16[128,1024]{1,0:T(8,128)(2,1)S(1)} %slice.13), channel_id=1, source_target_pairs={{0,2},{1,3},{2,0},{3,1},{4,6},{5,7},{6,4},{7,5},{8,10},{9,11},{10,... | collective-permute-start | bytes 786440 | tf_op jit(solution)/shard_map/ppermute | solution.py:302
  128.5 3.1 %collective-permute-start.19 = (bf16[128,1024]{1,0:T(8,128)(2,1)S(1)}, bf16[128,1024]{1,0:T(8,128)(2,1)S(1)}, u32[]{:S(2)}, u32[]{:S(2)}) collective-permute-start(bf16[128,1024]{1,0:T(8,128)(2,1)S(1)} %get-tuple-element.108), channel_id=1, source_target_pairs={{4,0},{8,4},{12,8},{16,12},{20,16},{24,20},{28,24},{5,1},{9,5},{13... | collective-permute-start | bytes 786440 | tf_op jit(solution)/shard_map/ppermute | solution.py:312
  131.6 3.3 %add_multiply_fusion = f32[512,1024]{1,0:T(8,128)} fusion(bf16[512,1024]{1,0:T(8,128)(2,1)} %collective-permute-done.21, bf16[512,1024]{1,0:T(8,128)(2,1)S(1)} %copy-done.46, bf16[512,1024]{1,0:T(8,128)(2,1)S(1)} %copy-done.44, s32[]{:T(128)S(6)} %select_n.99), kind=kOutput, calls=%fused_computation | convolution fusion | flops 538443776 | bytes 4718596 | tf_op jit(solution)/shard_map/dot_general | solution.py:525
  135.0 3.6 %collective-permute-done.12 = bf16[128,1024]{1,0:T(8,128)(2,1)S(1)} collective-permute-done((bf16[128,1024]{1,0:T(8,128)(2,1)S(1)}, bf16[128,1024]{1,0:T(8,128)(2,1)S(1)}, u32[]{:S(2)}, u32[]{:S(2)}) %collective-permute-start.12) | collective-permute-done | bytes 262176 | tf_op jit(solution)/shard_map/ppermute | solution.py:302
  (171 shorter events, 49.0 us)
Async XLA Ops:
  1.9 7.8 %collective-permute-start = (bf16[128,1024]{1,0:T(8,128)(2,1)S(1)}, bf16[128,1024]{1,0:T(8,128)(2,1)S(1)}, u32[]{:S(2)}, u32[]{:S(2)}) collective-permute-start(bf16[128,1024]{1,0:T(8,128)(2,1)S(1)} %multiply_convert_fusion.product), channel_id=1, source_target_pairs={{0,4},{4,8},{8,12},{12,16},{16,20},{20,24},{24,28},{1,5},{5,9},{9,... | collective-permute-start | bytes 786440 | tf_op jit(solution)/shard_map/ppermute | solution.py:312
  9.7 29.0 %collective-permute-start.1 = (bf16[512,1024]{1,0:T(8,128)(2,1)}, bf16[512,1024]{1,0:T(8,128)(2,1)S(1)}, u32[]{:S(2)}, u32[]{:S(2)}) collective-permute-start(bf16[512,1024]{1,0:T(8,128)(2,1)} %rest_2_.3), channel_id=1, source_target_pairs={{0,8},{4,12},{8,0},{12,4},{16,24},{20,28},{24,16},{28,20},{1,9},{5... | collective-permute-start | bytes 3145736 | tf_op jit(solution)/shard_map/ppermute | solution.py:297
  10.9 21.7 %collective-permute-start.2 = (bf16[128,1024]{1,0:T(8,128)(2,1)}, bf16[128,1024]{1,0:T(8,128)(2,1)}, u32[]{:S(2)}, u32[]{:S(2)}) collective-permute-start(bf16[128,1024]{1,0:T(8,128)(2,1)} %rest_0_), channel_id=1, source_target_pairs={{0,1},{1,0},{2,3},{3,2},{4,5},{5,4},{6,7},{7,6},{8,9},{9,8},{10,11... | collective-permute-start | bytes 786440 | tf_op jit(solution)/shard_map/ppermute | solution.py:302
  12.2 20.4 %collective-permute-start.3 = (bf16[128,1024]{1,0:T(8,128)(2,1)}, bf16[128,1024]{1,0:T(8,128)(2,1)}, u32[]{:S(2)}, u32[]{:S(2)}) collective-permute-start(bf16[128,1024]{1,0:T(8,128)(2,1)} %rest_0_), channel_id=1, source_target_pairs={{0,2},{1,3},{2,0},{3,1},{4,6},{5,7},{6,4},{7,5},{8,10},{9,11},{10,... | collective-permute-start | bytes 786440 | tf_op jit(solution)/shard_map/ppermute | solution.py:302
  14.5 18.1 %collective-permute-start.4 = (bf16[128,1024]{1,0:T(8,128)(2,1)}, bf16[128,1024]{1,0:T(8,128)(2,1)}, u32[]{:S(2)}, u32[]{:S(2)}) collective-permute-start(bf16[128,1024]{1,0:T(8,128)(2,1)} %rest_0_), channel_id=1, source_target_pairs={{0,3},{1,2},{2,1},{3,0},{4,7},{5,6},{6,5},{7,4},{8,11},{9,10},{10,... | collective-permute-start | bytes 786440 | tf_op jit(solution)/shard_map/ppermute | solution.py:302
  34.7 10.5 %collective-permute-start.5 = (bf16[128,2048]{1,0:T(8,128)(2,1)}, bf16[128,2048]{1,0:T(8,128)(2,1)}, u32[]{:S(2)}, u32[]{:S(2)}) collective-permute-start(bf16[128,2048]{1,0:T(8,128)(2,1)} %get-tuple-element.77), channel_id=1, source_target_pairs={{0,16},{4,20},{8,24},{12,28},{16,0},{20,4},{24,8},{28,12},{1,17},{... | collective-permute-start | bytes 1572872 | tf_op jit(solution)/shard_map/ppermute | solution.py:297
  34.7 36.4 %collective-permute-start.6 = (bf16[512,1024]{1,0:T(8,128)(2,1)S(1)}, bf16[512,1024]{1,0:T(8,128)(2,1)}, u32[]{:S(2)}, u32[]{:S(2)}) collective-permute-start(bf16[512,1024]{1,0:T(8,128)(2,1)S(1)} %copy-done.3), channel_id=1, source_target_pairs={{0,4},{4,0},{8,12},{12,8},{16,20},{20,16},{24,28},{28,24},{1,5},{5... | collective-permute-start | bytes 3145736 | tf_op jit(solution)/shard_map/ppermute | solution.py:307
  38.7 32.4 %collective-permute-start.7 = (bf16[512,1024]{1,0:T(8,128)(2,1)S(1)}, bf16[512,1024]{1,0:T(8,128)(2,1)}, u32[]{:S(2)}, u32[]{:S(2)}) collective-permute-start(bf16[512,1024]{1,0:T(8,128)(2,1)S(1)} %collective-permute-done.1.rest_4_), channel_id=1, source_target_pairs={{0,4},{4,0},{8,12},{12,8},{16,20},{20,16},{24,28},{28,24},{1,5},{5... | collective-permute-start | bytes 3145736 | tf_op jit(solution)/shard_map/ppermute | solution.py:307
  47.8 29.8 %collective-permute-start.13 = (bf16[256,1024]{1,0:T(8,128)(2,1)}, bf16[256,1024]{1,0:T(8,128)(2,1)}, u32[]{:S(2)}, u32[]{:S(2)}) collective-permute-start(bf16[256,1024]{1,0:T(8,128)(2,1)} %pad_maximum_fusion.1), channel_id=1, source_target_pairs={{0,8},{4,12},{8,0},{12,4},{16,24},{20,28},{24,16},{28,20},{1,9},{5... | collective-permute-start | bytes 1572872 | tf_op jit(solution)/shard_map/ppermute | solution.py:297
  69.8 7.8 %collective-permute-start.8 = (bf16[128,1024]{1,0:T(8,128)(2,1)S(1)}, bf16[128,1024]{1,0:T(8,128)(2,1)S(1)}, u32[]{:S(2)}, u32[]{:S(2)}) collective-permute-start(bf16[128,1024]{1,0:T(8,128)(2,1)S(1)} %get-tuple-element.80.rest_0_), channel_id=1, source_target_pairs={{0,16},{4,20},{8,24},{12,28},{16,0},{20,4},{24,8},{28,12},{1,17},{... | collective-permute-start | bytes 786440 | tf_op jit(solution)/shard_map/ppermute | solution.py:297
  76.2 8.7 %collective-permute-start.9 = (bf16[128,1024]{1,0:T(8,128)(2,1)S(1)}, bf16[128,1024]{1,0:T(8,128)(2,1)S(1)}, u32[]{:S(2)}, u32[]{:S(2)}) collective-permute-start(bf16[128,1024]{1,0:T(8,128)(2,1)S(1)} %get-tuple-element.83), channel_id=1, source_target_pairs={{0,16},{4,20},{8,24},{12,28},{16,0},{20,4},{24,8},{28,12},{1,17},{... | collective-permute-start | bytes 786440 | tf_op jit(solution)/shard_map/ppermute | solution.py:297
  77.6 14.2 %collective-permute-start.14 = (bf16[256,1024]{1,0:T(8,128)(2,1)S(1)}, bf16[256,1024]{1,0:T(8,128)(2,1)S(1)}, u32[]{:S(2)}, u32[]{:S(2)}) collective-permute-start(bf16[256,1024]{1,0:T(8,128)(2,1)S(1)} %pad_maximum_fusion.2), channel_id=1, source_target_pairs={{0,8},{4,12},{8,0},{12,4},{16,24},{20,28},{24,16},{28,20},{1,9},{5... | collective-permute-start | bytes 1572872 | tf_op jit(solution)/shard_map/ppermute | solution.py:297
  84.8 12.2 %collective-permute-start.10 = (bf16[128,2048]{1,0:T(8,128)(2,1)S(1)}, bf16[128,2048]{1,0:T(8,128)(2,1)S(1)}, u32[]{:S(2)}, u32[]{:S(2)}) collective-permute-start(bf16[128,2048]{1,0:T(8,128)(2,1)S(1)} %get-tuple-element.84), channel_id=1, source_target_pairs={{0,16},{4,20},{8,24},{12,28},{16,0},{20,4},{24,8},{28,12},{1,17},{... | collective-permute-start | bytes 1572872 | tf_op jit(solution)/shard_map/ppermute | solution.py:297
  97.1 13.2 %collective-permute-start.18 = (f32[16,1024]{1,0:T(8,128)S(1)}, f32[16,1024]{1,0:T(8,128)S(1)}, u32[]{:S(2)}, u32[]{:S(2)}) collective-permute-start(f32[16,1024]{1,0:T(8,128)S(1)} %add_select_fusion.1), channel_id=1, source_target_pairs={{0,24},{4,28},{8,16},{12,20},{16,8},{20,12},{24,0},{28,4},{1,25},{... | collective-permute-start | bytes 196616 | tf_op jit(solution)/shard_map/ppermute | solution.py:297
  98.2 12.0 %collective-permute-start.17 = (f32[16,1024]{1,0:T(8,128)S(1)}, f32[16,1024]{1,0:T(8,128)S(1)}, u32[]{:S(2)}, u32[]{:S(2)}) collective-permute-start(f32[16,1024]{1,0:T(8,128)S(1)} %add_select_fusion.1), channel_id=1, source_target_pairs={{0,16},{4,20},{8,24},{12,28},{16,0},{20,4},{24,8},{28,12},{1,17},{... | collective-permute-start | bytes 196616 | tf_op jit(solution)/shard_map/ppermute | solution.py:297
  98.6 11.7 %collective-permute-start.16 = (f32[16,1024]{1,0:T(8,128)S(1)}, f32[16,1024]{1,0:T(8,128)S(1)}, u32[]{:S(2)}, u32[]{:S(2)}) collective-permute-start(f32[16,1024]{1,0:T(8,128)S(1)} %add_select_fusion.1), channel_id=1, source_target_pairs={{0,8},{4,12},{8,0},{12,4},{16,24},{20,28},{24,16},{28,20},{1,9},{5... | collective-permute-start | bytes 196616 | tf_op jit(solution)/shard_map/ppermute | solution.py:297
  101.5 27.0 %collective-permute-start.21 = (bf16[512,1024]{1,0:T(8,128)(2,1)}, bf16[512,1024]{1,0:T(8,128)(2,1)}, u32[]{:S(2)}, u32[]{:S(2)}) collective-permute-start(bf16[512,1024]{1,0:T(8,128)(2,1)} %convolution_convert_fusion), channel_id=1, source_target_pairs={{0,4},{4,0},{8,12},{12,8},{16,20},{20,16},{24,28},{28,24},{1,5},{5... | collective-permute-start | bytes 3145736 | tf_op jit(solution)/shard_map/ppermute | solution.py:307
  105.9 16.9 %collective-permute-start.11 = (bf16[256,1024]{1,0:T(8,128)(2,1)}, bf16[256,1024]{1,0:T(8,128)(2,1)}, u32[]{:S(2)}, u32[]{:S(2)}) collective-permute-start(bf16[256,1024]{1,0:T(8,128)(2,1)} %get-tuple-element.86), channel_id=1, source_target_pairs={{0,1},{1,0},{2,3},{3,2},{4,5},{5,4},{6,7},{7,6},{8,9},{9,8},{10,11... | collective-permute-start | bytes 1572872 | tf_op jit(solution)/shard_map/ppermute | solution.py:302
  116.8 18.1 %collective-permute-start.24 = (bf16[64,1024]{1,0:T(8,128)(2,1)S(1)}, bf16[64,1024]{1,0:T(8,128)(2,1)S(1)}, u32[]{:S(2)}, u32[]{:S(2)}) collective-permute-start(bf16[64,1024]{1,0:T(8,128)(2,1)S(1)} %fusion.2), channel_id=1, source_target_pairs={{0,24},{4,28},{8,16},{12,20},{16,8},{20,12},{24,0},{28,4},{1,25},{... | collective-permute-start | bytes 393224 | tf_op jit(solution)/shard_map/ppermute | solution.py:297
  118.0 16.9 %collective-permute-start.23 = (bf16[64,1024]{1,0:T(8,128)(2,1)S(1)}, bf16[64,1024]{1,0:T(8,128)(2,1)S(1)}, u32[]{:S(2)}, u32[]{:S(2)}) collective-permute-start(bf16[64,1024]{1,0:T(8,128)(2,1)S(1)} %fusion.2), channel_id=1, source_target_pairs={{0,16},{4,20},{8,24},{12,28},{16,0},{20,4},{24,8},{28,12},{1,17},{... | collective-permute-start | bytes 393224 | tf_op jit(solution)/shard_map/ppermute | solution.py:297
  119.4 15.6 %collective-permute-start.22 = (bf16[64,1024]{1,0:T(8,128)(2,1)S(1)}, bf16[64,1024]{1,0:T(8,128)(2,1)S(1)}, u32[]{:S(2)}, u32[]{:S(2)}) collective-permute-start(bf16[64,1024]{1,0:T(8,128)(2,1)S(1)} %fusion.2), channel_id=1, source_target_pairs={{0,8},{4,12},{8,0},{12,4},{16,24},{20,28},{24,16},{28,20},{1,9},{5... | collective-permute-start | bytes 393224 | tf_op jit(solution)/shard_map/ppermute | solution.py:297
  124.4 14.2 %collective-permute-start.12 = (bf16[128,1024]{1,0:T(8,128)(2,1)S(1)}, bf16[128,1024]{1,0:T(8,128)(2,1)S(1)}, u32[]{:S(2)}, u32[]{:S(2)}) collective-permute-start(bf16[128,1024]{1,0:T(8,128)(2,1)S(1)} %slice.13), channel_id=1, source_target_pairs={{0,2},{1,3},{2,0},{3,1},{4,6},{5,7},{6,4},{7,5},{8,10},{9,11},{10,... | collective-permute-start | bytes 786440 | tf_op jit(solution)/shard_map/ppermute | solution.py:302
  128.5 11.4 %collective-permute-start.19 = (bf16[128,1024]{1,0:T(8,128)(2,1)S(1)}, bf16[128,1024]{1,0:T(8,128)(2,1)S(1)}, u32[]{:S(2)}, u32[]{:S(2)}) collective-permute-start(bf16[128,1024]{1,0:T(8,128)(2,1)S(1)} %get-tuple-element.108), channel_id=1, source_target_pairs={{4,0},{8,4},{12,8},{16,12},{20,16},{24,20},{28,24},{5,1},{9,5},{13... | collective-permute-start | bytes 786440 | tf_op jit(solution)/shard_map/ppermute | solution.py:312
  138.6 3.9 %collective-permute-start.25 = (f32[64,1024]{1,0:T(8,128)S(1)}, f32[64,1024]{1,0:T(8,128)S(1)}, u32[]{:S(2)}, u32[]{:S(2)}) collective-permute-start(f32[64,1024]{1,0:T(8,128)S(1)} %add_multiply_fusion.1), channel_id=1, source_target_pairs={{0,4},{4,0},{8,12},{12,8},{16,20},{20,16},{24,28},{28,24},{1,5},{5... | collective-permute-start | bytes 786440 | tf_op jit(solution)/shard_map/ppermute | solution.py:307
  (54 other events, 505.9 us)

commit v13 on v12

--- a/solution.py
+++ b/solution.py
@@ -132,7 +132,7 @@
     li_spec[...] = to_spectrum(table, kernel)
 
 
-def short_body(before, product, query, key, mr_spec, rate, ahead, back, spec, conv, mixed, signal, ends):
+def short_body(before, product, query, key, mr_spec, li_spec, rate, ahead, back, spec, conv, mixed, inner, ends):
     rows = product.shape[0]
     x = jnp.concatenate([before[...], product[...]], axis=0)
     found = apply2(ahead[...], x)
@@ -142,13 +142,8 @@
     mixed_rows = (query[...].astype(F32) * filtered).astype(BF16)
     mixed[...] = mixed_rows
     rounded = (key[...].astype(F32) * mixed_rows.astype(F32)).astype(BF16)
-    signal[...] = rounded
     ends[...] = fold_modes(rounded.astype(F32), rate[...], False)
-
-
-def inner_body(signal, li_spec, ahead, back, inner):
-    rows = signal.shape[0]
-    inner[...] = apply3(back[:rows], times(to_spectrum_exact(ahead[...], signal[...]), li_spec[...]))
+    inner[...] = apply3(back[:rows], times(to_spectrum_exact(ahead[...], rounded), li_spec[...]))
 
 
 def gather_states(rate, gaps, states, rows):
@@ -207,20 +202,16 @@
         stack[at * rows : (at + 1) * rows] = whole[:, pl.ds(place, stack.shape[1])]
 
 
-def grad_gate_body(count, own, query, rate, li_out, *rest):
-    parts, (grad_query, grad_out, ends) = rest[:count], rest[count:]
+def grad_gate_body(count, own, query, rate, li_out, li_spec, ahead, back, *rest):
+    parts, (grad_query, ends, inner) = rest[:count], rest[count:]
+    rows = own.shape[0]
     total = own[...]
     for part in parts:
         total = total + part[...].astype(F32)
     grad_query[...] = total * li_out[...]
     gated = total * query[...].astype(F32)
-    grad_out[...] = gated
     ends[...] = fold_modes(gated, rate[...], True)
-
-
-def grad_inner_body(grad_out, li_spec, ahead, back, inner):
-    rows = grad_out.shape[0]
-    inner[...] = apply3(back[:rows], times_conj(to_spectrum(ahead[...], grad_out[...]), li_spec[...]))
+    inner[...] = apply3(back[:rows], times_conj(to_spectrum(ahead[...], gated), li_spec[...]))
 
 
 def grad_long_body(
@@ -397,12 +388,13 @@
     mr_product = (key_mr.astype(F32) * value_mr.astype(F32)).astype(BF16)
     before = shifted(mr_product, 1)
     cot_line = [cotangent] + [line_swap(after(cotangent, mr_product), r) for r in range(1, line_count)]
-    beside = chip_swap(after(out_weight, before), 1)
     pairs = chips // 2
     pair = chip // 2
     pair_width = 4 * width
 
+    sibling_weight = core_swap(out_weight)
     rate = 1.0 / after(li_time, mr_product)
+    beside = chip_swap(after(out_weight, before), 1)
     coef = li_residue * jnp.sqrt(-jnp.expm1(-2.0 * rate))
     back_factors = lax.optimization_barrier(direct_factors(rate, rows, here // 2, True))
     mr_spec, li_spec = run(
@@ -412,20 +404,21 @@
         [(2 * rows, F32), (2 * rows, F32)],
         0,
     )
-    spec, mr_conv, mixed_mr, li_input, ends = run(
+    spec, mr_conv, mixed_mr, li_inner, ends = run(
         short_body,
         columns,
         [
-            tile(before),
+            tile(after(before, sibling_weight)),
             tile(mr_product),
             tile(query_mr),
             tile(key_li),
             tile(mr_spec),
+            tile(li_spec),
             tile(rate),
             table("ahead"),
             table("back"),
         ],
-        [(2 * rows, F32), (rows, F32), (rows, BF16), (rows, BF16), (rate.shape[0], F32)],
+        [(2 * rows, F32), (rows, F32), (rows, BF16), (rows, F32), (rate.shape[0], F32)],
         0,
     )
 
@@ -442,13 +435,6 @@
     cot_parts = [cot_pairs[0]] + [chip_swap(cot_pairs[h], 2 * h) for h in range(1, pairs)]
     states = lax.all_gather(after(ends, beside, *cot_parts[:1]), "ctx").reshape(-1, columns)
     gaps = (here - 1 - jnp.arange(ctx_count, dtype=jnp.int32)).astype(F32)
-    (li_inner,) = run(
-        inner_body,
-        columns,
-        [tile(li_input), tile(li_spec), table("ahead"), table("back")],
-        [(rows, F32)],
-        0,
-    )
     li_out, mixed_li = run(
         long_body,
         columns,
@@ -458,7 +444,7 @@
     )
 
     mixed_parts = [mixed_li] + [chip_swap(mixed_li, 2 * h) for h in range(1, pairs)]
-    weights = [out_weight, core_swap(out_weight), beside, core_swap(beside)]
+    weights = [out_weight, sibling_weight, beside, core_swap(after(beside, cot_pairs[0]))]
     pair_starts = jnp.stack([((here & 3) ^ m) * width for m in range(4)])
 
     share_flops = 2 * rows * columns * pair_width * pairs
@@ -495,28 +481,31 @@
     output = kept.astype(F32) + arrived_out.astype(F32)
 
     side = chip % 2
-    near_cot = jnp.concatenate([columns_at(part, side, chip_width) for part in cot_parts], axis=0)
-    far_cot = jnp.concatenate([columns_at(part, 1 - side, chip_width) for part in cot_parts], axis=0)
+    used = [after(part, mixed_li) for part in cot_parts]
+    near_cot = jnp.concatenate([columns_at(part, side, chip_width) for part in used], axis=0)
+    far_cot = jnp.concatenate([columns_at(part, 1 - side, chip_width) for part in used], axis=0)
     got_cot = chip_swap(far_cot, 1)
     near_mixed = jnp.concatenate([after(part, grad_own) for part in mixed_parts], axis=0)
-    got_mixed = chip_swap(after(near_mixed, got_cot, grad_own), 1)
-
-    grad_query_li, grad_li_out, back_ends = run(
+    got_mixed = chip_swap(near_mixed, 1)
+
+    grad_query_li, back_ends, grad_inner = run(
         functools.partial(grad_gate_body, pairs - 1),
         columns,
-        [tile(after(grad_own, out_own)), tile(query_li), tile(rate), tile(li_out)] + [tile(part) for part in grad_parts],
-        [(rows, F32), (rows, F32), (rate.shape[0], F32)],
-        pass_flops,
-    )
-    (grad_inner,) = run(
-        grad_inner_body,
-        columns,
-        [tile(after(grad_li_out, got_cot)), tile(li_spec), table("ahead"), table("back")],
-        [(rows, F32)],
-        3 * pass_flops,
+        [
+            tile(after(grad_own, out_own)),
+            tile(query_li),
+            tile(rate),
+            tile(li_out),
+            tile(li_spec),
+            table("ahead"),
+            table("back"),
+        ]
+        + [tile(part) for part in grad_parts],
+        [(rows, F32), (rate.shape[0], F32), (rows, F32)],
+        4 * pass_flops,
     )
     back_entering = entering_direct(
-        after(back_ends, grad_inner), back_factors, here, True, [got_mixed] + out_pairs[1:]
+        back_ends, back_factors, here, True, [got_cot, got_mixed] + out_pairs[1:]
     )
     cot_rows = jnp.concatenate([near_cot, got_cot], axis=0)
     mixed_rows = jnp.concatenate([near_mixed, got_mixed], axis=0)

time: 144 us -> 146 us (1.014)
  local copies, waits for them, and re-layouts: 16.7 us -> 25.7 us
  waiting for transfers between devices: 24.2 us -> 18.3 us
  starting transfers between devices: 38.4 us -> 35.5 us
  other arithmetic: 8.21 us -> 11.1 us
  blocking collectives: 17.2 us -> 15.5 us
    unnamed x106 -> x116, local copies, waits for them, and re-layouts: 14 us -> 23.5 us
    ppermute x5, starting transfers between devices: 10.5 us -> 6.28 us  [line_swap(): return lax.ppermute(x, 'fsdp', [(i, i ^ by) for i in range(size)])]
    ppermute x13, waiting for transfers between devices: 11.8 us -> 8.68 us  [chip_swap(): return lax.ppermute(x, 'ctx', [(i, i ^ 2 * by) for i in range(size)])]
    all_gather x1, blocking collectives: 17.2 us -> 15.5 us  [shards(): lax.all_gather(after(ends, beside, *cot_parts[:1]), 'ctx')]
    pallas_call x10 -> x8, Pallas kernels: 23.9 us -> 24.6 us  [run(): pl.pallas_call(body, grid=(columns // tile,), in_specs=in_specs, out_spec...]
  transfers between devices with their start and end apart: 26 -> 26, of which waited for: 8 -> 7; matrix products, arithmetic and copies ran while one was open for 10% -> 13% of each run, Pallas kernels for 23% -> 23%
where the time goes in v13:
time: 146 us; the launch traced here: 145 us
  starting transfers between devices  35.5 us (24%)
  Pallas kernels  32.8 us (22%)
  local copies, waits for them, and re-layouts  25.7 us (18%)
  waiting for transfers between devices  18.3 us (13%)
  blocking collectives  15.5 us (11%)
  other arithmetic  11.1 us (8%)
  matrix products  5.05 us (3%)
    pallas_call x8, Pallas kernels, run(): pl.pallas_call(body, grid=(columns // tile,), in_specs=in_specs, out_spec...  24.6 us
    unnamed x116, local copies, waits for them, and re-layouts  23.5 us
    all_gather x1, blocking collectives, shards(): lax.all_gather(after(ends, beside, *cot_parts[:1]), 'ctx')  15.5 us
    ppermute x13, starting transfers between devices, chip_swap(): return lax.ppermute(x, 'ctx', [(i, i ^ 2 * by) for i in range(size)])  11 us
    ppermute x6, starting transfers between devices, core_swap(): return lax.ppermute(x, 'ctx', [(i, i ^ 1) for i in range(size)])  10.8 us
    ppermute x13, waiting for transfers between devices, chip_swap(): return lax.ppermute(x, 'ctx', [(i, i ^ 2 * by) for i in range(size)])  8.68 us
    pallas_call x3, Pallas kernels, run_once(): pl.pallas_call(body, grid=(1,), in_specs=[pl.BlockSpec(memory_space=pltpu...  8.2 us
    ppermute x2, starting transfers between devices, shifted(): lax.ppermute(x, 'ctx', [(i, i + by) for i in range(size) if 0 <= i + by <...  7.41 us
  transfers between devices with their start and end apart: 26, of which 7 were waited for; matrix products, arithmetic and copies ran while one was open for 13% of the time, Pallas kernels for 23%

profile of v13, /device:TPU:1, one launch (start us, length us, event | category | flops | bytes accessed | tf_op | source)
XLA Modules:
  0.0 145.0 jit_solution(8100806182626620403)
XLA Ops:
  1.8 4.5 %collective-permute-start = (bf16[128,1024]{1,0:T(8,128)(2,1)S(1)}, bf16[128,1024]{1,0:T(8,128)(2,1)S(1)}, u32[]{:S(2)}, u32[]{:S(2)}) collective-permute-start(bf16[128,1024]{1,0:T(8,128)(2,1)S(1)} %multiply_convert_fusion.product), channel_id=1, source_target_pairs={{0,4},{4,8},{8,12},{12,16},{16,20},{20,24},{24,28},{1,5},{5,9},{9,... | collective-permute-start | bytes 786440 | tf_op jit(solution)/shard_map/ppermute | solution.py:303
  7.0 2.6 %collective-permute-done.before = bf16[128,1024]{1,0:T(8,128)(2,1)S(1)} collective-permute-done((bf16[128,1024]{1,0:T(8,128)(2,1)S(1)}, bf16[128,1024]{1,0:T(8,128)(2,1)S(1)}, u32[]{:S(2)}, u32[]{:S(2)}) %collective-permute-start) | collective-permute-done | bytes 262176 | tf_op jit(solution)/shard_map/ppermute | solution.py:303
  12.8 2.3 %collective-permute-start.4 = (bf16[128,1024]{1,0:T(8,128)(2,1)}, bf16[128,1024]{1,0:T(8,128)(2,1)}, u32[]{:S(2)}, u32[]{:S(2)}) collective-permute-start(bf16[128,1024]{1,0:T(8,128)(2,1)} %rest_0_), channel_id=1, source_target_pairs={{0,2},{1,3},{2,0},{3,1},{4,6},{5,7},{6,4},{7,5},{8,10},{9,11},{10,... | collective-permute-start | bytes 786440 | tf_op jit(solution)/shard_map/ppermute | solution.py:293
  19.4 2.0 %shard_map.197 = (f32[256,1024]{1,0:T(8,128)S(1)}, f32[256,1024]{1,0:T(8,128)S(1)}) custom-call(f32[128,1024]{1,0:T(8,128)S(1)} %copy-done.30, f32[16,1024]{1,0:T(8,128)S(1)} %get-tuple-element.123.rate, f32[16,1024]{1,0:T(8,128)S(1)} %get-tuple-element.119.coef, f32[1,1024]{1,0:T(1,128)S(1)} %bitcast.22, bf16[256,512]{1,0:T(8,128)(2,1)S(1)} %copy-done.6), custom_call_target="tpu_custom_call" | custom-call | tf_op jit(solution)/shard_map/pallas_call | solution.py:259
  28.9 4.9 %shard_map.198 = (f32[256,1024]{1,0:T(8,128)S(1)}, f32[128,1024]{1,0:T(8,128)S(1)}, bf16[128,1024]{1,0:T(8,128)(2,1)S(1)}, f32[128,1024]{1,0:T(8,128)S(1)}, f32[16,1024]{1,0:T(8,128)S(1)}) custom-call(bf16[128,1024]{1,0:T(8,128)(2,1)S(1)} %copy-done.41, bf16[128,1024]{1,0:T(8,128)(2,1)S(1)} %copy-done.25, bf16[128,1024]{1,0:T(8,128)(2,1)S(1)} %copy-done.20, ...), custom_call_target="tpu_custom_call" | custom-call | tf_op jit(solution)/shard_map/pallas_call | solution.py:259
  37.7 2.1 %shard_map.199 = (bf16[128,2048]{1,0:T(8,128)(2,1)S(1)}, bf16[128,2048]{1,0:T(8,128)(2,1)}) custom-call(s32[6]{0:T(128)S(1)} %stack.57.starts, bf16[128,1024]{1,0:T(8,128)(2,1)S(1)} %copy-done.39, bf16[128,1024]{1,0:T(8,128)(2,1)} %collective-permute-done.3.rest_1_, bf16[128,1024]{1,0:T(8,128)(2,1)} %collective-permute-done.4.rest_2_, ...), custom_call_target="tpu_custom_call" | custom-call | tf_op jit(solution)/shard_map/pallas_call | solution.py:274
  40.6 3.9 %collective-permute-start.7 = (bf16[512,1024]{1,0:T(8,128)(2,1)S(1)}, bf16[512,1024]{1,0:T(8,128)(2,1)}, u32[]{:S(2)}, u32[]{:S(2)}) collective-permute-start(bf16[512,1024]{1,0:T(8,128)(2,1)S(1)} %collective-permute-done.2.rest_4_), channel_id=1, source_target_pairs={{0,4},{4,0},{8,12},{12,8},{16,20},{20,16},{24,28},{28,24},{1,5},{5... | collective-permute-start | bytes 3145736 | tf_op jit(solution)/shard_map/ppermute | solution.py:298
  44.5 15.5 %all-gather.states = f32[128,1024]{1,0:T(8,128)S(1)} all-gather(f32[16,1024]{1,0:T(8,128)} %copy-done.43), channel_id=2, replica_groups=mesh['ctx'=8,'fsdp'=4] {'ctx'}, dimensions={0}, use_global_device_ids=true | all-gather | bytes 589824 | tf_op jit(solution)/shard_map/all_gather | solution.py:436
  62.0 2.6 %shard_map.200 = (f32[128,1024]{1,0:T(8,128)S(1)}, bf16[128,1024]{1,0:T(8,128)(2,1)}) custom-call(f32[8]{0:T(128)S(1)} %subtract_convert_fusion.gaps, f32[128,1024]{1,0:T(8,128)S(1)} %copy-done.33, bf16[128,1024]{1,0:T(8,128)(2,1)S(1)} %copy-done.18, f32[16,1024]{1,0:T(8,128)S(1)} %get-tuple-element.123.rate, f32[16,1024]{1,0:T(8,128)S(1)} %get-tuple-element.119.coef, ...), custom_call_target="tpu_custom_call" | custom-call | tf_op jit(solution)/shard_map/pallas_call | solution.py:259
  65.4 1.9 %constant_dynamic-slice_fusion.2 = (bf16[128,1024]{1,0:T(8,128)(2,1)}, bf16[128,1024]{1,0:T(8,128)(2,1)S(1)}, bf16[128,1024]{1,0:T(8,128)(2,1)S(1)}, bf16[128,1024]{1,0:T(8,128)(2,1)}) fusion(bf16[128,2048]{1,0:T(8,128)(2,1)} %collective-permute-done.6.rest_1_, s32[]{:T(128)S(6)} %select_n.83, s32[]{:T(128)S(6)} %select_n.84, bf16[128,2048]{1,0:T(8,128)(2,1)S(1)} %copy-done.12), kind=kLoop, calls=%fused_computation.31 | loop fusion | bytes 2097160 | tf_op jit(solution)/shard_map/dynamic_slice | solution.py:314
  70.8 4.0 %shard_map.201 = (f32[128,1024]{1,0:T(8,128)S(1)}, bf16[128,1024]{1,0:T(8,128)(2,1)S(1)}) custom-call(s32[4]{0:T(128)S(1)} %pad_add_fusion.starts, bf16[128,2048]{1,0:T(8,128)(2,1)S(1)} %copy-done.13, bf16[128,2048]{1,0:T(8,128)(2,1)} %collective-permute-done.6.rest_1_, bf16[512,1024]{1,0:T(8,128)(2,1)S(1)} %copy-done, ...), custom_call_target="tpu_custom_call" | custom-call | flops 1073741824 | bytes 6029328 | tf_op jit(solution)/shard_map/pallas_call | solution.py:259
  78.5 3.3 %collective-permute-done.13 = bf16[256,1024]{1,0:T(8,128)(2,1)} collective-permute-done((bf16[256,1024]{1,0:T(8,128)(2,1)}, bf16[256,1024]{1,0:T(8,128)(2,1)}, u32[]{:S(2)}, u32[]{:S(2)}) %collective-permute-start.13) | collective-permute-done | bytes 524320 | tf_op jit(solution)/shard_map/ppermute | solution.py:288
  83.0 4.7 %shard_map.202 = (bf16[128,2048]{1,0:T(8,128)(2,1)S(1)}, bf16[128,2048]{1,0:T(8,128)(2,1)S(1)}) custom-call(s32[4]{0:T(128)S(1)} %pad_add_fusion.starts, bf16[128,1024]{1,0:T(8,128)(2,1)} %get-tuple-element.81.rest_0_, bf16[128,1024]{1,0:T(8,128)(2,1)} %collective-permute-done.8.rest_1_, bf16[512,1024]{1,0:T(8,128)(2,1)S(1)} %copy-done, ...), custom_call_target="tpu_custom_call" | custom-call | tf_op jit(solution)/shard_map/pallas_call | solution.py:274
  90.0 3.4 %shard_map.204 = (f32[128,1024]{1,0:T(8,128)}, f32[16,1024]{1,0:T(8,128)S(1)}, f32[128,1024]{1,0:T(8,128)S(1)}) custom-call(f32[128,1024]{1,0:T(8,128)S(1)} %get-tuple-element.88.own, bf16[128,1024]{1,0:T(8,128)(2,1)S(1)} %copy-done.19, f32[16,1024]{1,0:T(8,128)S(1)} %get-tuple-element.123.rate, f32[128,1024]{1,0:T(8,128)S(1)} %copy-done.29, ...), custom_call_target="tpu_custom_call" | custom-call | flops 536870912 | bytes 4456448 | tf_op jit(solution)/shard_map/pallas_call | solution.py:259
  93.4 1.9 %collective-permute-start.15 = (f32[16,1024]{1,0:T(8,128)S(1)}, f32[16,1024]{1,0:T(8,128)S(1)}, u32[]{:S(2)}, u32[]{:S(2)}) collective-permute-start(f32[16,1024]{1,0:T(8,128)S(1)} %get-tuple-element.95), channel_id=1, source_target_pairs={{0,4},{4,0},{8,12},{12,8},{16,20},{20,16},{24,28},{28,24},{1,5},{5... | collective-permute-start | bytes 196616 | tf_op jit(solution)/shard_map/ppermute | solution.py:298
  96.4 4.3 %collective-permute-done.10.rest_1_ = bf16[128,2048]{1,0:T(8,128)(2,1)S(1)} collective-permute-done((bf16[128,2048]{1,0:T(8,128)(2,1)S(1)}, bf16[128,2048]{1,0:T(8,128)(2,1)S(1)}, u32[]{:S(2)}, u32[]{:S(2)}) %collective-permute-start.10) | collective-permute-done | bytes 524320 | tf_op jit(solution)/shard_map/ppermute | solution.py:288
  105.1 3.3 %collective-permute-start.21 = (bf16[512,1024]{1,0:T(8,128)(2,1)}, bf16[512,1024]{1,0:T(8,128)(2,1)}, u32[]{:S(2)}, u32[]{:S(2)}) collective-permute-start(bf16[512,1024]{1,0:T(8,128)(2,1)} %convolution_convert_fusion), channel_id=1, source_target_pairs={{0,4},{4,0},{8,12},{12,8},{16,20},{20,16},{24,28},{28,24},{1,5},{5... | collective-permute-start | bytes 3145736 | tf_op jit(solution)/shard_map/ppermute | solution.py:298
  110.3 3.7 %shard_map.205 = (f32[128,1024]{1,0:T(8,128)}, f32[128,1024]{1,0:T(8,128)}, f32[256,1024]{1,0:T(8,128)S(1)}, f32[128,1024]{1,0:T(8,128)S(1)}) custom-call(f32[128,1024]{1,0:T(8,128)S(1)} %get-tuple-element.92.inner, f32[16,1024]{1,0:T(8,128)S(1)} %get-tuple-element.123.rate, f32[16,1024]{1,0:T(8,128)S(1)} %get-tuple-element.119.coef, ...), custom_call_target="tpu_custom_call" | custom-call | flops 536870912 | bytes 6160384 | tf_op jit(solution)/shard_map/pallas_call | solution.py:259
  120.2 3.5 %collective-permute-done.11 = bf16[256,1024]{1,0:T(8,128)(2,1)} collective-permute-done((bf16[256,1024]{1,0:T(8,128)(2,1)}, bf16[256,1024]{1,0:T(8,128)(2,1)}, u32[]{:S(2)}, u32[]{:S(2)}) %collective-permute-start.11) | collective-permute-done | bytes 524320 | tf_op jit(solution)/shard_map/ppermute | solution.py:293
  125.3 2.3 %collective-permute-start.12 = (bf16[128,1024]{1,0:T(8,128)(2,1)S(1)}, bf16[128,1024]{1,0:T(8,128)(2,1)}, u32[]{:S(2)}, u32[]{:S(2)}) collective-permute-start(bf16[128,1024]{1,0:T(8,128)(2,1)S(1)} %slice.13), channel_id=1, source_target_pairs={{0,2},{1,3},{2,0},{3,1},{4,6},{5,7},{6,4},{7,5},{8,10},{9,11},{10,... | collective-permute-start | bytes 786440 | tf_op jit(solution)/shard_map/ppermute | solution.py:293
  127.6 2.3 %shard_map.206 = (f32[128,1024]{1,0:T(8,128)S(1)}, bf16[128,1024]{1,0:T(8,128)(2,1)}) custom-call(f32[256,1024]{1,0:T(8,128)S(1)} %get-tuple-element.104.grad_spec, f32[256,1024]{1,0:T(8,128)S(1)} %copy-done.5, bf16[256,768]{1,0:T(8,128)(2,1)S(1)} %copy-done.10), custom_call_target="tpu_custom_call" | custom-call | flops 402653184 | bytes 3276800 | tf_op jit(solution)/shard_map/pallas_call | solution.py:259
  130.7 2.9 %collective-permute-start.19 = (bf16[128,1024]{1,0:T(8,128)(2,1)}, bf16[128,1024]{1,0:T(8,128)(2,1)S(1)}, u32[]{:S(2)}, u32[]{:S(2)}) collective-permute-start(bf16[128,1024]{1,0:T(8,128)(2,1)} %get-tuple-element.106), channel_id=1, source_target_pairs={{4,0},{8,4},{12,8},{16,12},{20,16},{24,20},{28,24},{5,1},{9,5},{13... | collective-permute-start | bytes 786440 | tf_op jit(solution)/shard_map/ppermute | solution.py:303
  133.6 3.3 %add_multiply_fusion = f32[512,1024]{1,0:T(8,128)} fusion(bf16[512,1024]{1,0:T(8,128)(2,1)} %collective-permute-done.21, bf16[512,1024]{1,0:T(8,128)(2,1)S(1)} %copy-done.50, bf16[512,1024]{1,0:T(8,128)(2,1)S(1)} %copy-done.48, s32[]{:T(128)S(6)} %select_n.99), kind=kOutput, calls=%fused_computation | convolution fusion | flops 538443776 | bytes 4718596 | tf_op jit(solution)/shard_map/dot_general | solution.py:514
  137.0 2.2 %collective-permute-done.12 = bf16[128,1024]{1,0:T(8,128)(2,1)} collective-permute-done((bf16[128,1024]{1,0:T(8,128)(2,1)S(1)}, bf16[128,1024]{1,0:T(8,128)(2,1)}, u32[]{:S(2)}, u32[]{:S(2)}) %collective-permute-start.12) | collective-permute-done | bytes 262176 | tf_op jit(solution)/shard_map/ppermute | solution.py:293
  (178 shorter events, 56.5 us)
Async XLA Ops:
  1.8 7.8 %collective-permute-start = (bf16[128,1024]{1,0:T(8,128)(2,1)S(1)}, bf16[128,1024]{1,0:T(8,128)(2,1)S(1)}, u32[]{:S(2)}, u32[]{:S(2)}) collective-permute-start(bf16[128,1024]{1,0:T(8,128)(2,1)S(1)} %multiply_convert_fusion.product), channel_id=1, source_target_pairs={{0,4},{4,8},{8,12},{12,16},{16,20},{20,24},{24,28},{1,5},{5,9},{9,... | collective-permute-start | bytes 786440 | tf_op jit(solution)/shard_map/ppermute | solution.py:303
  7.0 15.5 %collective-permute-start.1 = (bf16[512,1024]{1,0:T(8,128)(2,1)}, bf16[512,1024]{1,0:T(8,128)(2,1)S(1)}, u32[]{:S(2)}, u32[]{:S(2)}) collective-permute-start(bf16[512,1024]{1,0:T(8,128)(2,1)} %rest_2_.3), channel_id=1, source_target_pairs={{0,4},{4,0},{8,12},{12,8},{16,20},{20,16},{24,28},{28,24},{1,5},{5... | collective-permute-start | bytes 3145736 | tf_op jit(solution)/shard_map/ppermute | solution.py:298
  10.3 30.3 %collective-permute-start.2 = (bf16[512,1024]{1,0:T(8,128)(2,1)}, bf16[512,1024]{1,0:T(8,128)(2,1)S(1)}, u32[]{:S(2)}, u32[]{:S(2)}) collective-permute-start(bf16[512,1024]{1,0:T(8,128)(2,1)} %rest_2_.3), channel_id=1, source_target_pairs={{0,8},{4,12},{8,0},{12,4},{16,24},{20,28},{24,16},{28,20},{1,9},{5... | collective-permute-start | bytes 3145736 | tf_op jit(solution)/shard_map/ppermute | solution.py:288
  11.5 26.2 %collective-permute-start.3 = (bf16[128,1024]{1,0:T(8,128)(2,1)}, bf16[128,1024]{1,0:T(8,128)(2,1)}, u32[]{:S(2)}, u32[]{:S(2)}) collective-permute-start(bf16[128,1024]{1,0:T(8,128)(2,1)} %rest_0_), channel_id=1, source_target_pairs={{0,1},{1,0},{2,3},{3,2},{4,5},{5,4},{6,7},{7,6},{8,9},{9,8},{10,11... | collective-permute-start | bytes 786440 | tf_op jit(solution)/shard_map/ppermute | solution.py:293
  12.8 24.9 %collective-permute-start.4 = (bf16[128,1024]{1,0:T(8,128)(2,1)}, bf16[128,1024]{1,0:T(8,128)(2,1)}, u32[]{:S(2)}, u32[]{:S(2)}) collective-permute-start(bf16[128,1024]{1,0:T(8,128)(2,1)} %rest_0_), channel_id=1, source_target_pairs={{0,2},{1,3},{2,0},{3,1},{4,6},{5,7},{6,4},{7,5},{8,10},{9,11},{10,... | collective-permute-start | bytes 786440 | tf_op jit(solution)/shard_map/ppermute | solution.py:293
  15.1 22.6 %collective-permute-start.5 = (bf16[128,1024]{1,0:T(8,128)(2,1)}, bf16[128,1024]{1,0:T(8,128)(2,1)}, u32[]{:S(2)}, u32[]{:S(2)}) collective-permute-start(bf16[128,1024]{1,0:T(8,128)(2,1)} %rest_0_), channel_id=1, source_target_pairs={{0,3},{1,2},{2,1},{3,0},{4,7},{5,6},{6,5},{7,4},{8,11},{9,10},{10,... | collective-permute-start | bytes 786440 | tf_op jit(solution)/shard_map/ppermute | solution.py:293
  40.6 24.8 %collective-permute-start.6 = (bf16[128,2048]{1,0:T(8,128)(2,1)}, bf16[128,2048]{1,0:T(8,128)(2,1)}, u32[]{:S(2)}, u32[]{:S(2)}) collective-permute-start(bf16[128,2048]{1,0:T(8,128)(2,1)} %get-tuple-element.77), channel_id=1, source_target_pairs={{0,16},{4,20},{8,24},{12,28},{16,0},{20,4},{24,8},{28,12},{1,17},{... | collective-permute-start | bytes 1572872 | tf_op jit(solution)/shard_map/ppermute | solution.py:288
  40.6 29.2 %collective-permute-start.7 = (bf16[512,1024]{1,0:T(8,128)(2,1)S(1)}, bf16[512,1024]{1,0:T(8,128)(2,1)}, u32[]{:S(2)}, u32[]{:S(2)}) collective-permute-start(bf16[512,1024]{1,0:T(8,128)(2,1)S(1)} %collective-permute-done.2.rest_4_), channel_id=1, source_target_pairs={{0,4},{4,0},{8,12},{12,8},{16,20},{20,16},{24,28},{28,24},{1,5},{5... | collective-permute-start | bytes 3145736 | tf_op jit(solution)/shard_map/ppermute | solution.py:298
  68.1 13.7 %collective-permute-start.13 = (bf16[256,1024]{1,0:T(8,128)(2,1)}, bf16[256,1024]{1,0:T(8,128)(2,1)}, u32[]{:S(2)}, u32[]{:S(2)}) collective-permute-start(bf16[256,1024]{1,0:T(8,128)(2,1)} %pad_maximum_fusion.1), channel_id=1, source_target_pairs={{0,8},{4,12},{8,0},{12,4},{16,24},{20,28},{24,16},{28,20},{1,9},{5... | collective-permute-start | bytes 1572872 | tf_op jit(solution)/shard_map/ppermute | solution.py:288
  69.4 7.8 %collective-permute-start.8 = (bf16[128,1024]{1,0:T(8,128)(2,1)}, bf16[128,1024]{1,0:T(8,128)(2,1)}, u32[]{:S(2)}, u32[]{:S(2)}) collective-permute-start(bf16[128,1024]{1,0:T(8,128)(2,1)} %get-tuple-element.81.rest_0_), channel_id=1, source_target_pairs={{0,16},{4,20},{8,24},{12,28},{16,0},{20,4},{24,8},{28,12},{1,17},{... | collective-permute-start | bytes 786440 | tf_op jit(solution)/shard_map/ppermute | solution.py:288
  74.8 13.9 %collective-permute-start.9 = (bf16[128,1024]{1,0:T(8,128)(2,1)S(1)}, bf16[128,1024]{1,0:T(8,128)(2,1)S(1)}, u32[]{:S(2)}, u32[]{:S(2)}) collective-permute-start(bf16[128,1024]{1,0:T(8,128)(2,1)S(1)} %get-tuple-element.84), channel_id=1, source_target_pairs={{0,16},{4,20},{8,24},{12,28},{16,0},{20,4},{24,8},{28,12},{1,17},{... | collective-permute-start | bytes 786440 | tf_op jit(solution)/shard_map/ppermute | solution.py:288
  78.2 18.0 %collective-permute-start.14 = (bf16[256,1024]{1,0:T(8,128)(2,1)S(1)}, bf16[256,1024]{1,0:T(8,128)(2,1)S(1)}, u32[]{:S(2)}, u32[]{:S(2)}) collective-permute-start(bf16[256,1024]{1,0:T(8,128)(2,1)S(1)} %pad_maximum_fusion.2), channel_id=1, source_target_pairs={{0,8},{4,12},{8,0},{12,4},{16,24},{20,28},{24,16},{28,20},{1,9},{5... | collective-permute-start | bytes 1572872 | tf_op jit(solution)/shard_map/ppermute | solution.py:288
  88.7 12.0 %collective-permute-start.10 = (bf16[128,2048]{1,0:T(8,128)(2,1)S(1)}, bf16[128,2048]{1,0:T(8,128)(2,1)S(1)}, u32[]{:S(2)}, u32[]{:S(2)}) collective-permute-start(bf16[128,2048]{1,0:T(8,128)(2,1)S(1)} %get-tuple-element.85), channel_id=1, source_target_pairs={{0,16},{4,20},{8,24},{12,28},{16,0},{20,4},{24,8},{28,12},{1,17},{... | collective-permute-start | bytes 1572872 | tf_op jit(solution)/shard_map/ppermute | solution.py:288
  100.7 9.5 %collective-permute-start.18 = (f32[16,1024]{1,0:T(8,128)S(1)}, f32[16,1024]{1,0:T(8,128)S(1)}, u32[]{:S(2)}, u32[]{:S(2)}) collective-permute-start(f32[16,1024]{1,0:T(8,128)S(1)} %add_select_fusion.1), channel_id=1, source_target_pairs={{0,24},{4,28},{8,16},{12,20},{16,8},{20,12},{24,0},{28,4},{1,25},{... | collective-permute-start | bytes 196616 | tf_op jit(solution)/shard_map/ppermute | solution.py:288
  101.9 8.3 %collective-permute-start.17 = (f32[16,1024]{1,0:T(8,128)S(1)}, f32[16,1024]{1,0:T(8,128)S(1)}, u32[]{:S(2)}, u32[]{:S(2)}) collective-permute-start(f32[16,1024]{1,0:T(8,128)S(1)} %add_select_fusion.1), channel_id=1, source_target_pairs={{0,16},{4,20},{8,24},{12,28},{16,0},{20,4},{24,8},{28,12},{1,17},{... | collective-permute-start | bytes 196616 | tf_op jit(solution)/shard_map/ppermute | solution.py:288
  103.1 7.1 %collective-permute-start.16 = (f32[16,1024]{1,0:T(8,128)S(1)}, f32[16,1024]{1,0:T(8,128)S(1)}, u32[]{:S(2)}, u32[]{:S(2)}) collective-permute-start(f32[16,1024]{1,0:T(8,128)S(1)} %add_select_fusion.1), channel_id=1, source_target_pairs={{0,8},{4,12},{8,0},{12,4},{16,24},{20,28},{24,16},{28,20},{1,9},{5... | collective-permute-start | bytes 196616 | tf_op jit(solution)/shard_map/ppermute | solution.py:288
  105.1 25.6 %collective-permute-start.21 = (bf16[512,1024]{1,0:T(8,128)(2,1)}, bf16[512,1024]{1,0:T(8,128)(2,1)}, u32[]{:S(2)}, u32[]{:S(2)}) collective-permute-start(bf16[512,1024]{1,0:T(8,128)(2,1)} %convolution_convert_fusion), channel_id=1, source_target_pairs={{0,4},{4,0},{8,12},{12,8},{16,20},{20,16},{24,28},{28,24},{1,5},{5... | collective-permute-start | bytes 3145736 | tf_op jit(solution)/shard_map/ppermute | solution.py:298
  109.8 13.9 %collective-permute-start.11 = (bf16[256,1024]{1,0:T(8,128)(2,1)}, bf16[256,1024]{1,0:T(8,128)(2,1)}, u32[]{:S(2)}, u32[]{:S(2)}) collective-permute-start(bf16[256,1024]{1,0:T(8,128)(2,1)} %get-tuple-element.87), channel_id=1, source_target_pairs={{0,1},{1,0},{2,3},{3,2},{4,5},{5,4},{6,7},{7,6},{8,9},{9,8},{10,11... | collective-permute-start | bytes 1572872 | tf_op jit(solution)/shard_map/ppermute | solution.py:293
  117.5 19.5 %collective-permute-start.24 = (bf16[64,1024]{1,0:T(8,128)(2,1)S(1)}, bf16[64,1024]{1,0:T(8,128)(2,1)S(1)}, u32[]{:S(2)}, u32[]{:S(2)}) collective-permute-start(bf16[64,1024]{1,0:T(8,128)(2,1)S(1)} %fusion.2), channel_id=1, source_target_pairs={{0,24},{4,28},{8,16},{12,20},{16,8},{20,12},{24,0},{28,4},{1,25},{... | collective-permute-start | bytes 393224 | tf_op jit(solution)/shard_map/ppermute | solution.py:288
  118.7 18.2 %collective-permute-start.23 = (bf16[64,1024]{1,0:T(8,128)(2,1)S(1)}, bf16[64,1024]{1,0:T(8,128)(2,1)S(1)}, u32[]{:S(2)}, u32[]{:S(2)}) collective-permute-start(bf16[64,1024]{1,0:T(8,128)(2,1)S(1)} %fusion.2), channel_id=1, source_target_pairs={{0,16},{4,20},{8,24},{12,28},{16,0},{20,4},{24,8},{28,12},{1,17},{... | collective-permute-start | bytes 393224 | tf_op jit(solution)/shard_map/ppermute | solution.py:288
  120.0 17.0 %collective-permute-start.22 = (bf16[64,1024]{1,0:T(8,128)(2,1)S(1)}, bf16[64,1024]{1,0:T(8,128)(2,1)S(1)}, u32[]{:S(2)}, u32[]{:S(2)}) collective-permute-start(bf16[64,1024]{1,0:T(8,128)(2,1)S(1)} %fusion.2), channel_id=1, source_target_pairs={{0,8},{4,12},{8,0},{12,4},{16,24},{20,28},{24,16},{28,20},{1,9},{5... | collective-permute-start | bytes 393224 | tf_op jit(solution)/shard_map/ppermute | solution.py:288
  125.3 14.0 %collective-permute-start.12 = (bf16[128,1024]{1,0:T(8,128)(2,1)S(1)}, bf16[128,1024]{1,0:T(8,128)(2,1)}, u32[]{:S(2)}, u32[]{:S(2)}) collective-permute-start(bf16[128,1024]{1,0:T(8,128)(2,1)S(1)} %slice.13), channel_id=1, source_target_pairs={{0,2},{1,3},{2,0},{3,1},{4,6},{5,7},{6,4},{7,5},{8,10},{9,11},{10,... | collective-permute-start | bytes 786440 | tf_op jit(solution)/shard_map/ppermute | solution.py:293
  130.7 10.0 %collective-permute-start.19 = (bf16[128,1024]{1,0:T(8,128)(2,1)}, bf16[128,1024]{1,0:T(8,128)(2,1)S(1)}, u32[]{:S(2)}, u32[]{:S(2)}) collective-permute-start(bf16[128,1024]{1,0:T(8,128)(2,1)} %get-tuple-element.106), channel_id=1, source_target_pairs={{4,0},{8,4},{12,8},{16,12},{20,16},{24,20},{28,24},{5,1},{9,5},{13... | collective-permute-start | bytes 786440 | tf_op jit(solution)/shard_map/ppermute | solution.py:303
  139.3 4.9 %collective-permute-start.25 = (f32[64,1024]{1,0:T(8,128)S(1)}, f32[64,1024]{1,0:T(8,128)S(1)}, u32[]{:S(2)}, u32[]{:S(2)}) collective-permute-start(f32[64,1024]{1,0:T(8,128)S(1)} %add_multiply_fusion.1), channel_id=1, source_target_pairs={{0,4},{4,0},{8,12},{12,8},{16,20},{20,16},{24,28},{28,24},{1,5},{5... | collective-permute-start | bytes 786440 | tf_op jit(solution)/shard_map/ppermute | solution.py:298
  (59 other events, 413.6 us)

commit v14 on v13

--- a/solution.py
+++ b/solution.py
@@ -12,6 +12,7 @@
 
 F32 = jnp.float32
 BF16 = jnp.bfloat16
+BLOCK = 512
 TILE = 256
 GROUP = 8
 
@@ -243,12 +244,13 @@
 
 
 def run(body, columns, inputs, outputs, flops):
-    tile = min(TILE, columns)
+    block = min(BLOCK, columns)
+    tile = min(TILE, block)
     in_specs = []
     moved = 0
     for kind, array in inputs:
         if kind == "tile":
-            in_specs.append(pl.BlockSpec((array.shape[0], tile), lambda c: (0, c)))
+            in_specs.append(pl.BlockSpec((array.shape[0], block), lambda c: (0, c)))
         elif kind == "whole":
             in_specs.append(pl.BlockSpec(array.shape, lambda c: (0, 0)))
         else:
@@ -256,13 +258,19 @@
         moved += math.prod(array.shape) * array.dtype.itemsize
     for rows, dtype in outputs:
         moved += rows * columns * jnp.dtype(dtype).itemsize
+    tiled = [kind == "tile" for kind, _ in inputs] + [True] * len(outputs)
+
+    def body_by_tiles(*refs):
+        for first in range(0, block, tile):
+            body(*[ref.at[:, pl.ds(first, tile)] if cut else ref for ref, cut in zip(refs, tiled)])
+
     return pl.pallas_call(
-        body,
-        grid=(columns // tile,),
+        body_by_tiles,
+        grid=(columns // block,),
         in_specs=in_specs,
-        out_specs=[pl.BlockSpec((rows, tile), lambda c: (0, c)) for rows, _ in outputs],
+        out_specs=[pl.BlockSpec((rows, block), lambda c: (0, c)) for rows, _ in outputs],
         out_shape=[jax.ShapeDtypeStruct((rows, columns), dtype) for rows, dtype in outputs],
-        compiler_params=pltpu.CompilerParams(vmem_limit_bytes=12 * 1024 * 1024),
+        compiler_params=pltpu.CompilerParams(vmem_limit_bytes=56 * 1024 * 1024),
         cost_estimate=pl.CostEstimate(flops=flops, bytes_accessed=moved if flops else 0, transcendentals=0),
     )(*[array for _, array in inputs])
 
@@ -278,7 +286,7 @@
         out_specs=[block(shape) for shape, _ in outputs],
         out_shape=[jax.ShapeDtypeStruct(shape, dtype) for shape, dtype in outputs],
         scratch_shapes=scratch,
-        compiler_params=pltpu.CompilerParams(vmem_limit_bytes=20 * 1024 * 1024),
+        compiler_params=pltpu.CompilerParams(vmem_limit_bytes=56 * 1024 * 1024),
         cost_estimate=pl.CostEstimate(flops=0, bytes_accessed=0, transcendentals=0),
     )(*inputs)
 
@@ -507,8 +515,8 @@
     back_entering = entering_direct(
         back_ends, back_factors, here, True, [got_cot, got_mixed] + out_pairs[1:]
     )
-    cot_rows = jnp.concatenate([near_cot, got_cot], axis=0)
-    mixed_rows = jnp.concatenate([near_mixed, got_mixed], axis=0)
+    cot_rows = jnp.concatenate([near_cot, after(got_cot, back_ends)], axis=0)
+    mixed_rows = jnp.concatenate([near_mixed, after(got_mixed, back_ends)], axis=0)
 
     def weight_share(which):
         return lax.dot_general(

time: 146 us -> 140 us (0.959)
  local copies, waits for them, and re-layouts: 25.7 us -> 7.56 us
  Pallas kernels: 32.8 us -> 42.4 us
  starting transfers between devices: 35.5 us -> 39.7 us
  waiting for transfers between devices: 18.3 us -> 14.6 us
  blocking collectives: 15.5 us -> 18.7 us
    unnamed x116 -> x44, local copies, waits for them, and re-layouts: 23.5 us -> 4.26 us
    pallas_call x8, Pallas kernels: 24.6 us -> 31.8 us  [run(): pl.pallas_call(body_by_tiles, grid=(columns // block,), in_specs=in_specs...]
    ppermute x13, waiting for transfers between devices: 8.68 us -> 3.49 us  [chip_swap(): return lax.ppermute(x, 'ctx', [(i, i ^ 2 * by) for i in range(size)])]
    all_gather x1, blocking collectives: 15.5 us -> 18.7 us  [shards(): lax.all_gather(after(ends, beside, *cot_parts[:1]), 'ctx')]
    pallas_call x3, Pallas kernels: 8.2 us -> 10.7 us  [run_once(): pl.pallas_call(body, grid=(1,), in_specs=[pl.BlockSpec(memory_space=pltpu...]
    ppermute x5, starting transfers between devices: 6.28 us -> 8.48 us  [line_swap(): return lax.ppermute(x, 'fsdp', [(i, i ^ by) for i in range(size)])]
    ppermute x6, starting transfers between devices: 10.8 us -> 12.3 us  [core_swap(): return lax.ppermute(x, 'ctx', [(i, i ^ 1) for i in range(size)])]
  transfers between devices with their start and end apart: 26 -> 26, of which waited for: 7 -> 8; matrix products, arithmetic and copies ran while one was open for 13% -> 13% of each run, Pallas kernels for 23% -> 30%
where the time goes in v14:
time: 140 us
  Pallas kernels  42.4 us (30%)
  starting transfers between devices  39.7 us (28%)
  blocking collectives  18.7 us (13%)
  waiting for transfers between devices  14.6 us (10%)
  other arithmetic  10.6 us (8%)
  local copies, waits for them, and re-layouts  7.56 us (5%)
  matrix products  5.02 us (4%)
    pallas_call x8, Pallas kernels, run(): pl.pallas_call(body_by_tiles, grid=(columns // block,), in_specs=in_specs...  31.8 us
    all_gather x1, blocking collectives, shards(): lax.all_gather(after(ends, beside, *cot_parts[:1]), 'ctx')  18.7 us
    ppermute x6, starting transfers between devices, core_swap(): return lax.ppermute(x, 'ctx', [(i, i ^ 1) for i in range(size)])  12.3 us
    ppermute x13, starting transfers between devices, chip_swap(): return lax.ppermute(x, 'ctx', [(i, i ^ 2 * by) for i in range(size)])  11.4 us
    pallas_call x3, Pallas kernels, run_once(): pl.pallas_call(body, grid=(1,), in_specs=[pl.BlockSpec(memory_space=pltpu...  10.7 us
    ppermute x5, starting transfers between devices, line_swap(): return lax.ppermute(x, 'fsdp', [(i, i ^ by) for i in range(size)])  8.48 us
    ppermute x2, starting transfers between devices, shifted(): lax.ppermute(x, 'ctx', [(i, i + by) for i in range(size) if 0 <= i + by <...  7.47 us
    ppermute x5, waiting for transfers between devices, line_swap(): return lax.ppermute(x, 'fsdp', [(i, i ^ by) for i in range(size)])  6.66 us
  transfers between devices with their start and end apart: 26, of which 8 were waited for; matrix products, arithmetic and copies ran while one was open for 13% of the time, Pallas kernels for 30%

profile of v14, /device:TPU:1, one launch (start us, length us, event | category | flops | bytes accessed | tf_op | source)
XLA Modules:
  0.0 139.6 jit_solution(8719904651087421787)
XLA Ops:
  1.7 4.5 %collective-permute-start = (bf16[128,1024]{1,0:T(8,128)(2,1)S(1)}, bf16[128,1024]{1,0:T(8,128)(2,1)S(1)}, u32[]{:S(2)}, u32[]{:S(2)}) collective-permute-start(bf16[128,1024]{1,0:T(8,128)(2,1)S(1)} %multiply_convert_fusion.refs_1_), channel_id=1, source_target_pairs={{0,4},{4,8},{8,12},{12,16},{16,20},{20,24},{24,28},{1,5},{5,9},{9,... | collective-permute-start | bytes 786440 | tf_op jit(solution)/shard_map/ppermute | solution.py:311
  6.3 3.2 %collective-permute-done.refs_0_ = bf16[128,1024]{1,0:T(8,128)(2,1)S(1)} collective-permute-done((bf16[128,1024]{1,0:T(8,128)(2,1)S(1)}, bf16[128,1024]{1,0:T(8,128)(2,1)S(1)}, u32[]{:S(2)}, u32[]{:S(2)}) %collective-permute-start) | collective-permute-done | bytes 262176 | tf_op jit(solution)/shard_map/ppermute | solution.py:311
  12.1 2.3 %collective-permute-start.4 = (bf16[128,1024]{1,0:T(8,128)(2,1)}, bf16[128,1024]{1,0:T(8,128)(2,1)S(1)}, u32[]{:S(2)}, u32[]{:S(2)}) collective-permute-start(bf16[128,1024]{1,0:T(8,128)(2,1)} %rest_0_), channel_id=1, source_target_pairs={{0,2},{1,3},{2,0},{3,1},{4,6},{5,7},{6,4},{7,5},{8,10},{9,11},{10,... | collective-permute-start | bytes 786440 | tf_op jit(solution)/shard_map/ppermute | solution.py:301
  16.0 3.4 %shard_map.197 = (f32[256,1024]{1,0:T(8,128)}, f32[256,1024]{1,0:T(8,128)}) custom-call(f32[128,1024]{1,0:T(8,128)} %refs_0_.1, f32[16,1024]{1,0:T(8,128)} %get-tuple-element.127.refs_1_.refs_6_.refs_3_.refs_2_, f32[16,1024]{1,0:T(8,128)} %get-tuple-element.123.refs_2_.refs_4_, f32[1,1024]{1,0:T(1,128)} %bitcast.22, ...), custom_call_target="tpu_custom_call" | custom-call | tf_op jit(solution)/shard_map/pallas_call | solution.py:267
  20.1 6.1 %shard_map.198 = (f32[256,1024]{1,0:T(8,128)}, f32[128,1024]{1,0:T(8,128)}, bf16[128,1024]{1,0:T(8,128)(2,1)}, f32[128,1024]{1,0:T(8,128)}, f32[16,1024]{1,0:T(8,128)}) custom-call(bf16[128,1024]{1,0:T(8,128)(2,1)} %copy-done.19, bf16[128,1024]{1,0:T(8,128)(2,1)} %copy-done.8, bf16[128,1024]{1,0:T(8,128)(2,1)} %refs_6_.2, bf16[128,1024]{1,0:T(8,128)(2,1)} %refs_5_.2, ...), custom_call_target="tpu_custom_call" | custom-call | tf_op jit(solution)/shard_map/pallas_call | solution.py:267
  26.3 4.1 %collective-permute-done.5.rest_3_ = bf16[128,1024]{1,0:T(8,128)(2,1)S(1)} collective-permute-done((bf16[128,1024]{1,0:T(8,128)(2,1)}, bf16[128,1024]{1,0:T(8,128)(2,1)S(1)}, u32[]{:S(2)}, u32[]{:S(2)}) %collective-permute-start.5) | collective-permute-done | bytes 262176 | tf_op jit(solution)/shard_map/ppermute | solution.py:301
  31.1 2.3 %shard_map.199 = (bf16[128,2048]{1,0:T(8,128)(2,1)}, bf16[128,2048]{1,0:T(8,128)(2,1)}) custom-call(s32[6]{0:T(128)} %stack.57.starts, bf16[128,1024]{1,0:T(8,128)(2,1)} %rest_0_, bf16[128,1024]{1,0:T(8,128)(2,1)} %copy-done.14, bf16[128,1024]{1,0:T(8,128)(2,1)} %copy-done.15, bf16[128,1024]{1,0:T(8,128)(2,1)} %copy-done.16), custom_call_target="tpu_custom_call" | custom-call | tf_op jit(solution)/shard_map/pallas_call | solution.py:282
  33.6 5.8 %collective-permute-start.7 = (bf16[512,1024]{1,0:T(8,128)(2,1)S(1)}, bf16[512,1024]{1,0:T(8,128)(2,1)S(1)}, u32[]{:S(2)}, u32[]{:S(2)}) collective-permute-start(bf16[512,1024]{1,0:T(8,128)(2,1)S(1)} %collective-permute-done.2.refs_5_.rest_4_), channel_id=1, source_target_pairs={{0,4},{4,0},{8,12},{12,8},{16,20},{20,16},{24,28},{28,24},{1,5},{5... | collective-permute-start | bytes 3145736 | tf_op jit(solution)/shard_map/ppermute | solution.py:306
  40.4 18.7 %all-gather.refs_5_ = f32[128,1024]{1,0:T(8,128)} all-gather(f32[16,1024]{1,0:T(8,128)} %get-tuple-element.76), channel_id=2, replica_groups=mesh['ctx'=8,'fsdp'=4] {'ctx'}, dimensions={0}, use_global_device_ids=true | all-gather | bytes 589824 | tf_op jit(solution)/shard_map/all_gather | solution.py:444
  59.1 2.8 %shard_map.200 = (f32[128,1024]{1,0:T(8,128)}, bf16[128,1024]{1,0:T(8,128)(2,1)}) custom-call(f32[8]{0:T(128)} %subtract_convert_fusion.refs_0_, f32[128,1024]{1,0:T(8,128)} %get-tuple-element.67.refs_1_, bf16[128,1024]{1,0:T(8,128)(2,1)} %refs_1_.1, f32[16,1024]{1,0:T(8,128)} %get-tuple-element.127.refs_1_.refs_6_.refs_3_.refs_2_, ...), custom_call_target="tpu_custom_call" | custom-call | tf_op jit(solution)/shard_map/pallas_call | solution.py:267
  67.4 4.3 %shard_map.201 = (f32[128,1024]{1,0:T(8,128)}, bf16[128,1024]{1,0:T(8,128)(2,1)}) custom-call(s32[4]{0:T(128)} %pad_add_fusion.refs_0_.starts, bf16[128,2048]{1,0:T(8,128)(2,1)} %get-tuple-element.78.refs_1_, bf16[128,2048]{1,0:T(8,128)(2,1)} %copy-done.7, bf16[512,1024]{1,0:T(8,128)(2,1)} %rest_2_.1, bf16[512,1024]{1,0:T(8,128)(2,1)} %copy-done, ...), custom_call_target="tpu_custom_call" | custom-call | flops 1073741824 | bytes 6029328 | tf_op jit(solution)/shard_map/pallas_call | solution.py:267
  73.8 6.1 %shard_map.202 = (bf16[128,2048]{1,0:T(8,128)(2,1)}, bf16[128,2048]{1,0:T(8,128)(2,1)}) custom-call(s32[4]{0:T(128)} %pad_add_fusion.refs_0_.starts, bf16[128,1024]{1,0:T(8,128)(2,1)} %get-tuple-element.83.rest_0_, bf16[128,1024]{1,0:T(8,128)(2,1)} %copy-done.5, bf16[512,1024]{1,0:T(8,128)(2,1)} %rest_2_.1, bf16[512,1024]{1,0:T(8,128)(2,1)} %copy-done, ...), custom_call_target="tpu_custom_call" | custom-call | tf_op jit(solution)/shard_map/pallas_call | solution.py:282
  82.5 4.8 %shard_map.204 = (f32[128,1024]{1,0:T(8,128)}, f32[16,1024]{1,0:T(8,128)}, f32[128,1024]{1,0:T(8,128)}) custom-call(f32[128,1024]{1,0:T(8,128)} %get-tuple-element.90.refs_0_, bf16[128,1024]{1,0:T(8,128)(2,1)} %refs_1_.1, f32[16,1024]{1,0:T(8,128)} %get-tuple-element.127.refs_1_.refs_6_.refs_3_.refs_2_, f32[128,1024]{1,0:T(8,128)} %get-tuple-element.91.refs_3_, ...), custom_call_target="tpu_custom_call" | custom-call | flops 536870912 | bytes 4456448 | tf_op jit(solution)/shard_map/pallas_call | solution.py:267
  90.1 2.2 %collective-permute-done.14 = bf16[256,1024]{1,0:T(8,128)(2,1)S(1)} collective-permute-done((bf16[256,1024]{1,0:T(8,128)(2,1)S(1)}, bf16[256,1024]{1,0:T(8,128)(2,1)S(1)}, u32[]{:S(2)}, u32[]{:S(2)}) %collective-permute-start.14) | collective-permute-done | bytes 524320 | tf_op jit(solution)/shard_map/ppermute | solution.py:296
  97.8 3.0 %collective-permute-start.21 = (bf16[512,1024]{1,0:T(8,128)(2,1)}, bf16[512,1024]{1,0:T(8,128)(2,1)}, u32[]{:S(2)}, u32[]{:S(2)}) collective-permute-start(bf16[512,1024]{1,0:T(8,128)(2,1)} %convolution_convert_fusion), channel_id=1, source_target_pairs={{0,4},{4,0},{8,12},{12,8},{16,20},{20,16},{24,28},{28,24},{1,5},{5... | collective-permute-start | bytes 3145736 | tf_op jit(solution)/shard_map/ppermute | solution.py:306
  100.8 2.3 %shard_map.203 = (bf16[256,1024]{1,0:T(8,128)(2,1)}, bf16[256,1024]{1,0:T(8,128)(2,1)}) custom-call(s32[6]{0:T(128)} %stack.51.starts, bf16[128,2048]{1,0:T(8,128)(2,1)} %get-tuple-element.84.rest_0_, bf16[128,2048]{1,0:T(8,128)(2,1)} %copy-done.11), custom_call_target="tpu_custom_call" | custom-call | tf_op jit(solution)/shard_map/pallas_call | solution.py:282
  103.2 2.6 %collective-permute-start.11 = (bf16[256,1024]{1,0:T(8,128)(2,1)}, bf16[256,1024]{1,0:T(8,128)(2,1)S(1)}, u32[]{:S(2)}, u32[]{:S(2)}) collective-permute-start(bf16[256,1024]{1,0:T(8,128)(2,1)} %get-tuple-element.89), channel_id=1, source_target_pairs={{0,1},{1,0},{2,3},{3,2},{4,5},{5,4},{6,7},{7,6},{8,9},{9,8},{10,11... | collective-permute-start | bytes 1572872 | tf_op jit(solution)/shard_map/ppermute | solution.py:301
  106.4 5.1 %shard_map.205 = (f32[128,1024]{1,0:T(8,128)}, f32[128,1024]{1,0:T(8,128)}, f32[256,1024]{1,0:T(8,128)}, f32[128,1024]{1,0:T(8,128)}) custom-call(f32[128,1024]{1,0:T(8,128)} %get-tuple-element.97.refs_0_, f32[16,1024]{1,0:T(8,128)} %get-tuple-element.127.refs_1_.refs_6_.refs_3_.refs_2_, f32[16,1024]{1,0:T(8,128)} %get-tuple-element.123.refs_2_.refs_4_, ...), custom_call_target="tpu_custom_call" | custom-call | flops 536870912 | bytes 6160384 | tf_op jit(solution)/shard_map/pallas_call | solution.py:267
  120.4 2.3 %collective-permute-start.12 = (bf16[128,1024]{1,0:T(8,128)(2,1)S(1)}, bf16[128,1024]{1,0:T(8,128)(2,1)S(1)}, u32[]{:S(2)}, u32[]{:S(2)}) collective-permute-start(bf16[128,1024]{1,0:T(8,128)(2,1)S(1)} %slice.13), channel_id=1, source_target_pairs={{0,2},{1,3},{2,0},{3,1},{4,6},{5,7},{6,4},{7,5},{8,10},{9,11},{10,... | collective-permute-start | bytes 786440 | tf_op jit(solution)/shard_map/ppermute | solution.py:301
  122.8 3.1 %shard_map.206 = (f32[128,1024]{1,0:T(8,128)}, bf16[128,1024]{1,0:T(8,128)(2,1)}) custom-call(f32[256,1024]{1,0:T(8,128)} %get-tuple-element.108.refs_0_, f32[256,1024]{1,0:T(8,128)} %get-tuple-element.65.refs_4_.refs_1_, bf16[256,768]{1,0:T(8,128)(2,1)} %constant.89.clone.refs_8_.refs_6_.refs_2_), custom_call_target="tpu_custom_call" | custom-call | flops 402653184 | bytes 3276800 | tf_op jit(solution)/shard_map/pallas_call | solution.py:267
  125.8 3.0 %collective-permute-start.19 = (bf16[128,1024]{1,0:T(8,128)(2,1)}, bf16[128,1024]{1,0:T(8,128)(2,1)}, u32[]{:S(2)}, u32[]{:S(2)}) collective-permute-start(bf16[128,1024]{1,0:T(8,128)(2,1)} %get-tuple-element.110), channel_id=1, source_target_pairs={{4,0},{8,4},{12,8},{16,12},{20,16},{24,20},{28,24},{5,1},{9,5},{13... | collective-permute-start | bytes 786440 | tf_op jit(solution)/shard_map/ppermute | solution.py:311
  128.8 3.3 %add_multiply_fusion = f32[512,1024]{1,0:T(8,128)} fusion(bf16[512,1024]{1,0:T(8,128)(2,1)} %collective-permute-done.21, bf16[512,1024]{1,0:T(8,128)(2,1)S(1)} %constant_dynamic-update-slice_fusion, bf16[512,1024]{1,0:T(8,128)(2,1)S(1)} %pad_maximum_fusion, s32[]{:T(128)S(6)} %select_n.99), kind=kOutput, calls=%fused_computation | convolution fusion | flops 538443776 | bytes 4718596 | tf_op jit(solution)/shard_map/dot_general | solution.py:522
  132.2 2.0 %collective-permute-done.12 = bf16[128,1024]{1,0:T(8,128)(2,1)S(1)} collective-permute-done((bf16[128,1024]{1,0:T(8,128)(2,1)S(1)}, bf16[128,1024]{1,0:T(8,128)(2,1)S(1)}, u32[]{:S(2)}, u32[]{:S(2)}) %collective-permute-start.12) | collective-permute-done | bytes 262176 | tf_op jit(solution)/shard_map/ppermute | solution.py:301
  135.7 2.2 %shard_map.207 = (f32[128,1024]{1,0:T(8,128)}, f32[128,1024]{1,0:T(8,128)}) custom-call(f32[128,1024]{1,0:T(8,128)} %get-tuple-element.109.refs_0_, bf16[128,1024]{1,0:T(8,128)(2,1)} %collective-permute-done.19.refs_1_, bf16[128,1024]{1,0:T(8,128)(2,1)} %refs_2_.6, bf16[128,1024]{1,0:T(8,128)(2,1)} %refs_3_.5), custom_call_target="tpu_custom_call" | custom-call | flops 131072 | bytes 2359296 | tf_op jit(solution)/shard_map/pallas_call | solution.py:267
  (106 shorter events, 39.2 us)
Async XLA Ops:
  1.7 7.8 %collective-permute-start = (bf16[128,1024]{1,0:T(8,128)(2,1)S(1)}, bf16[128,1024]{1,0:T(8,128)(2,1)S(1)}, u32[]{:S(2)}, u32[]{:S(2)}) collective-permute-start(bf16[128,1024]{1,0:T(8,128)(2,1)S(1)} %multiply_convert_fusion.refs_1_), channel_id=1, source_target_pairs={{0,4},{4,8},{8,12},{12,16},{16,20},{20,24},{24,28},{1,5},{5,9},{9,... | collective-permute-start | bytes 786440 | tf_op jit(solution)/shard_map/ppermute | solution.py:311
  6.3 13.9 %collective-permute-start.1 = (bf16[512,1024]{1,0:T(8,128)(2,1)}, bf16[512,1024]{1,0:T(8,128)(2,1)S(1)}, u32[]{:S(2)}, u32[]{:S(2)}) collective-permute-start(bf16[512,1024]{1,0:T(8,128)(2,1)} %rest_2_.1), channel_id=1, source_target_pairs={{0,4},{4,0},{8,12},{12,8},{16,20},{20,16},{24,28},{28,24},{1,5},{5... | collective-permute-start | bytes 3145736 | tf_op jit(solution)/shard_map/ppermute | solution.py:306
  9.6 24.0 %collective-permute-start.2 = (bf16[512,1024]{1,0:T(8,128)(2,1)}, bf16[512,1024]{1,0:T(8,128)(2,1)S(1)}, u32[]{:S(2)}, u32[]{:S(2)}) collective-permute-start(bf16[512,1024]{1,0:T(8,128)(2,1)} %rest_2_.1), channel_id=1, source_target_pairs={{0,8},{4,12},{8,0},{12,4},{16,24},{20,28},{24,16},{28,20},{1,9},{5... | collective-permute-start | bytes 3145736 | tf_op jit(solution)/shard_map/ppermute | solution.py:296
  10.8 15.5 %collective-permute-start.3 = (bf16[128,1024]{1,0:T(8,128)(2,1)}, bf16[128,1024]{1,0:T(8,128)(2,1)S(1)}, u32[]{:S(2)}, u32[]{:S(2)}) collective-permute-start(bf16[128,1024]{1,0:T(8,128)(2,1)} %rest_0_), channel_id=1, source_target_pairs={{0,1},{1,0},{2,3},{3,2},{4,5},{5,4},{6,7},{7,6},{8,9},{9,8},{10,11... | collective-permute-start | bytes 786440 | tf_op jit(solution)/shard_map/ppermute | solution.py:301
  12.1 14.2 %collective-permute-start.4 = (bf16[128,1024]{1,0:T(8,128)(2,1)}, bf16[128,1024]{1,0:T(8,128)(2,1)S(1)}, u32[]{:S(2)}, u32[]{:S(2)}) collective-permute-start(bf16[128,1024]{1,0:T(8,128)(2,1)} %rest_0_), channel_id=1, source_target_pairs={{0,2},{1,3},{2,0},{3,1},{4,6},{5,7},{6,4},{7,5},{8,10},{9,11},{10,... | collective-permute-start | bytes 786440 | tf_op jit(solution)/shard_map/ppermute | solution.py:301
  14.4 16.0 %collective-permute-start.5 = (bf16[128,1024]{1,0:T(8,128)(2,1)}, bf16[128,1024]{1,0:T(8,128)(2,1)S(1)}, u32[]{:S(2)}, u32[]{:S(2)}) collective-permute-start(bf16[128,1024]{1,0:T(8,128)(2,1)} %rest_0_), channel_id=1, source_target_pairs={{0,3},{1,2},{2,1},{3,0},{4,7},{5,6},{6,5},{7,4},{8,11},{9,10},{10,... | collective-permute-start | bytes 786440 | tf_op jit(solution)/shard_map/ppermute | solution.py:301
  33.6 32.8 %collective-permute-start.7 = (bf16[512,1024]{1,0:T(8,128)(2,1)S(1)}, bf16[512,1024]{1,0:T(8,128)(2,1)S(1)}, u32[]{:S(2)}, u32[]{:S(2)}) collective-permute-start(bf16[512,1024]{1,0:T(8,128)(2,1)S(1)} %collective-permute-done.2.refs_5_.rest_4_), channel_id=1, source_target_pairs={{0,4},{4,0},{8,12},{12,8},{16,20},{20,16},{24,28},{28,24},{1,5},{5... | collective-permute-start | bytes 3145736 | tf_op jit(solution)/shard_map/ppermute | solution.py:306
  39.4 24.0 %collective-permute-start.6 = (bf16[128,2048]{1,0:T(8,128)(2,1)}, bf16[128,2048]{1,0:T(8,128)(2,1)S(1)}, u32[]{:S(2)}, u32[]{:S(2)}) collective-permute-start(bf16[128,2048]{1,0:T(8,128)(2,1)} %get-tuple-element.79), channel_id=1, source_target_pairs={{0,16},{4,20},{8,24},{12,28},{16,0},{20,4},{24,8},{28,12},{1,17},{... | collective-permute-start | bytes 1572872 | tf_op jit(solution)/shard_map/ppermute | solution.py:296
  61.9 11.2 %collective-permute-start.8 = (bf16[128,1024]{1,0:T(8,128)(2,1)}, bf16[128,1024]{1,0:T(8,128)(2,1)S(1)}, u32[]{:S(2)}, u32[]{:S(2)}) collective-permute-start(bf16[128,1024]{1,0:T(8,128)(2,1)} %get-tuple-element.83.rest_0_), channel_id=1, source_target_pairs={{0,16},{4,20},{8,24},{12,28},{16,0},{20,4},{24,8},{28,12},{1,17},{... | collective-permute-start | bytes 786440 | tf_op jit(solution)/shard_map/ppermute | solution.py:296
  65.2 23.8 %collective-permute-start.13 = (bf16[256,1024]{1,0:T(8,128)(2,1)}, bf16[256,1024]{1,0:T(8,128)(2,1)}, u32[]{:S(2)}, u32[]{:S(2)}) collective-permute-start(bf16[256,1024]{1,0:T(8,128)(2,1)} %pad_maximum_fusion.1), channel_id=1, source_target_pairs={{0,8},{4,12},{8,0},{12,4},{16,24},{20,28},{24,16},{28,20},{1,9},{5... | collective-permute-start | bytes 1572872 | tf_op jit(solution)/shard_map/ppermute | solution.py:296
  71.7 9.3 %collective-permute-start.9 = (bf16[128,1024]{1,0:T(8,128)(2,1)}, bf16[128,1024]{1,0:T(8,128)(2,1)S(1)}, u32[]{:S(2)}, u32[]{:S(2)}) collective-permute-start(bf16[128,1024]{1,0:T(8,128)(2,1)} %get-tuple-element.86), channel_id=1, source_target_pairs={{0,16},{4,20},{8,24},{12,28},{16,0},{20,4},{24,8},{28,12},{1,17},{... | collective-permute-start | bytes 786440 | tf_op jit(solution)/shard_map/ppermute | solution.py:296
  79.9 12.4 %collective-permute-start.14 = (bf16[256,1024]{1,0:T(8,128)(2,1)S(1)}, bf16[256,1024]{1,0:T(8,128)(2,1)S(1)}, u32[]{:S(2)}, u32[]{:S(2)}) collective-permute-start(bf16[256,1024]{1,0:T(8,128)(2,1)S(1)} %pad_maximum_fusion.2), channel_id=1, source_target_pairs={{0,8},{4,12},{8,0},{12,4},{16,24},{20,28},{24,16},{28,20},{1,9},{5... | collective-permute-start | bytes 1572872 | tf_op jit(solution)/shard_map/ppermute | solution.py:296
  81.0 12.5 %collective-permute-start.10 = (bf16[128,2048]{1,0:T(8,128)(2,1)}, bf16[128,2048]{1,0:T(8,128)(2,1)S(1)}, u32[]{:S(2)}, u32[]{:S(2)}) collective-permute-start(bf16[128,2048]{1,0:T(8,128)(2,1)} %get-tuple-element.87), channel_id=1, source_target_pairs={{0,16},{4,20},{8,24},{12,28},{16,0},{20,4},{24,8},{28,12},{1,17},{... | collective-permute-start | bytes 1572872 | tf_op jit(solution)/shard_map/ppermute | solution.py:296
  93.5 12.2 %collective-permute-start.18 = (f32[16,1024]{1,0:T(8,128)S(1)}, f32[16,1024]{1,0:T(8,128)S(1)}, u32[]{:S(2)}, u32[]{:S(2)}) collective-permute-start(f32[16,1024]{1,0:T(8,128)S(1)} %add_select_fusion.1), channel_id=1, source_target_pairs={{0,24},{4,28},{8,16},{12,20},{16,8},{20,12},{24,0},{28,4},{1,25},{... | collective-permute-start | bytes 196616 | tf_op jit(solution)/shard_map/ppermute | solution.py:296
  94.7 11.1 %collective-permute-start.17 = (f32[16,1024]{1,0:T(8,128)S(1)}, f32[16,1024]{1,0:T(8,128)S(1)}, u32[]{:S(2)}, u32[]{:S(2)}) collective-permute-start(f32[16,1024]{1,0:T(8,128)S(1)} %add_select_fusion.1), channel_id=1, source_target_pairs={{0,16},{4,20},{8,24},{12,28},{16,0},{20,4},{24,8},{28,12},{1,17},{... | collective-permute-start | bytes 196616 | tf_op jit(solution)/shard_map/ppermute | solution.py:296
  96.0 9.7 %collective-permute-start.16 = (f32[16,1024]{1,0:T(8,128)S(1)}, f32[16,1024]{1,0:T(8,128)S(1)}, u32[]{:S(2)}, u32[]{:S(2)}) collective-permute-start(f32[16,1024]{1,0:T(8,128)S(1)} %add_select_fusion.1), channel_id=1, source_target_pairs={{0,8},{4,12},{8,0},{12,4},{16,24},{20,28},{24,16},{28,20},{1,9},{5... | collective-permute-start | bytes 196616 | tf_op jit(solution)/shard_map/ppermute | solution.py:296
  97.8 28.0 %collective-permute-start.21 = (bf16[512,1024]{1,0:T(8,128)(2,1)}, bf16[512,1024]{1,0:T(8,128)(2,1)}, u32[]{:S(2)}, u32[]{:S(2)}) collective-permute-start(bf16[512,1024]{1,0:T(8,128)(2,1)} %convolution_convert_fusion), channel_id=1, source_target_pairs={{0,4},{4,0},{8,12},{12,8},{16,20},{20,16},{24,28},{28,24},{1,5},{5... | collective-permute-start | bytes 3145736 | tf_op jit(solution)/shard_map/ppermute | solution.py:306
  103.2 15.1 %collective-permute-start.11 = (bf16[256,1024]{1,0:T(8,128)(2,1)}, bf16[256,1024]{1,0:T(8,128)(2,1)S(1)}, u32[]{:S(2)}, u32[]{:S(2)}) collective-permute-start(bf16[256,1024]{1,0:T(8,128)(2,1)} %get-tuple-element.89), channel_id=1, source_target_pairs={{0,1},{1,0},{2,3},{3,2},{4,5},{5,4},{6,7},{7,6},{8,9},{9,8},{10,11... | collective-permute-start | bytes 1572872 | tf_op jit(solution)/shard_map/ppermute | solution.py:301
  115.0 17.1 %collective-permute-start.24 = (bf16[64,1024]{1,0:T(8,128)(2,1)S(1)}, bf16[64,1024]{1,0:T(8,128)(2,1)S(1)}, u32[]{:S(2)}, u32[]{:S(2)}) collective-permute-start(bf16[64,1024]{1,0:T(8,128)(2,1)S(1)} %fusion.2), channel_id=1, source_target_pairs={{0,24},{4,28},{8,16},{12,20},{16,8},{20,12},{24,0},{28,4},{1,25},{... | collective-permute-start | bytes 393224 | tf_op jit(solution)/shard_map/ppermute | solution.py:296
  116.3 15.8 %collective-permute-start.23 = (bf16[64,1024]{1,0:T(8,128)(2,1)S(1)}, bf16[64,1024]{1,0:T(8,128)(2,1)S(1)}, u32[]{:S(2)}, u32[]{:S(2)}) collective-permute-start(bf16[64,1024]{1,0:T(8,128)(2,1)S(1)} %fusion.2), channel_id=1, source_target_pairs={{0,16},{4,20},{8,24},{12,28},{16,0},{20,4},{24,8},{28,12},{1,17},{... | collective-permute-start | bytes 393224 | tf_op jit(solution)/shard_map/ppermute | solution.py:296
  117.5 14.6 %collective-permute-start.22 = (bf16[64,1024]{1,0:T(8,128)(2,1)S(1)}, bf16[64,1024]{1,0:T(8,128)(2,1)S(1)}, u32[]{:S(2)}, u32[]{:S(2)}) collective-permute-start(bf16[64,1024]{1,0:T(8,128)(2,1)S(1)} %fusion.2), channel_id=1, source_target_pairs={{0,8},{4,12},{8,0},{12,4},{16,24},{20,28},{24,16},{28,20},{1,9},{5... | collective-permute-start | bytes 393224 | tf_op jit(solution)/shard_map/ppermute | solution.py:296
  120.4 13.8 %collective-permute-start.12 = (bf16[128,1024]{1,0:T(8,128)(2,1)S(1)}, bf16[128,1024]{1,0:T(8,128)(2,1)S(1)}, u32[]{:S(2)}, u32[]{:S(2)}) collective-permute-start(bf16[128,1024]{1,0:T(8,128)(2,1)S(1)} %slice.13), channel_id=1, source_target_pairs={{0,2},{1,3},{2,0},{3,1},{4,6},{5,7},{6,4},{7,5},{8,10},{9,11},{10,... | collective-permute-start | bytes 786440 | tf_op jit(solution)/shard_map/ppermute | solution.py:301
  125.8 9.9 %collective-permute-start.19 = (bf16[128,1024]{1,0:T(8,128)(2,1)}, bf16[128,1024]{1,0:T(8,128)(2,1)}, u32[]{:S(2)}, u32[]{:S(2)}) collective-permute-start(bf16[128,1024]{1,0:T(8,128)(2,1)} %get-tuple-element.110), channel_id=1, source_target_pairs={{4,0},{8,4},{12,8},{16,12},{20,16},{24,20},{28,24},{5,1},{9,5},{13... | collective-permute-start | bytes 786440 | tf_op jit(solution)/shard_map/ppermute | solution.py:311
  134.3 4.5 %collective-permute-start.25 = (f32[64,1024]{1,0:T(8,128)S(1)}, f32[64,1024]{1,0:T(8,128)S(1)}, u32[]{:S(2)}, u32[]{:S(2)}) collective-permute-start(f32[64,1024]{1,0:T(8,128)S(1)} %add_multiply_fusion.1), channel_id=1, source_target_pairs={{0,4},{4,0},{8,12},{12,8},{16,20},{20,16},{24,28},{28,24},{1,5},{5... | collective-permute-start | bytes 786440 | tf_op jit(solution)/shard_map/ppermute | solution.py:306
  (23 other events, 192.0 us)

commit v15 on v14

--- a/solution.py
+++ b/solution.py
@@ -400,7 +400,6 @@
     pair = chip // 2
     pair_width = 4 * width
 
-    sibling_weight = core_swap(out_weight)
     rate = 1.0 / after(li_time, mr_product)
     beside = chip_swap(after(out_weight, before), 1)
     coef = li_residue * jnp.sqrt(-jnp.expm1(-2.0 * rate))
@@ -416,7 +415,7 @@
         short_body,
         columns,
         [
-            tile(after(before, sibling_weight)),
+            tile(before),
             tile(mr_product),
             tile(query_mr),
             tile(key_li),
@@ -430,18 +429,18 @@
         0,
     )
 
+    states = lax.all_gather(after(ends, beside, *cot_line), "ctx").reshape(-1, columns)
     line_width = cotangent.shape[1]
     whole_width = line_width * line_count
     split_starts = [(line ^ r) * line_width for r in range(line_count)]
     split_starts += [(pair ^ h) * pair_width for h in range(pairs)]
     cot_pairs = run_once(
         functools.partial(split_body, pairs),
-        [jnp.stack(split_starts)] + [after(piece, ends) for piece in cot_line],
+        [jnp.stack(split_starts)] + [after(piece, states) for piece in cot_line],
         [((rows, pair_width), BF16)] * pairs,
         [pltpu.VMEM((rows, whole_width), BF16)],
     )
     cot_parts = [cot_pairs[0]] + [chip_swap(cot_pairs[h], 2 * h) for h in range(1, pairs)]
-    states = lax.all_gather(after(ends, beside, *cot_parts[:1]), "ctx").reshape(-1, columns)
     gaps = (here - 1 - jnp.arange(ctx_count, dtype=jnp.int32)).astype(F32)
     li_out, mixed_li = run(
         long_body,
@@ -452,7 +451,7 @@
     )
 
     mixed_parts = [mixed_li] + [chip_swap(mixed_li, 2 * h) for h in range(1, pairs)]
-    weights = [out_weight, sibling_weight, beside, core_swap(after(beside, cot_pairs[0]))]
+    weights = [out_weight, core_swap(after(out_weight, mixed_li)), beside, core_swap(after(beside, mixed_li))]
     pair_starts = jnp.stack([((here & 3) ^ m) * width for m in range(4)])
 
     share_flops = 2 * rows * columns * pair_width * pairs
@@ -489,7 +488,7 @@
     output = kept.astype(F32) + arrived_out.astype(F32)
 
     side = chip % 2
-    used = [after(part, mixed_li) for part in cot_parts]
+    used = [after(part, grad_own) for part in cot_parts]
     near_cot = jnp.concatenate([columns_at(part, side, chip_width) for part in used], axis=0)
     far_cot = jnp.concatenate([columns_at(part, 1 - side, chip_width) for part in used], axis=0)
     got_cot = chip_swap(far_cot, 1)

time: 140 us -> 146 us (1.043)
  waiting for transfers between devices: 14.6 us -> 29.5 us
  blocking collectives: 18.7 us -> 13.1 us
  starting transfers between devices: 39.7 us -> 36.4 us
    ppermute x13, waiting for transfers between devices: 3.49 us -> 17.7 us  [chip_swap(): return lax.ppermute(x, 'ctx', [(i, i ^ 2 * by) for i in range(size)])]
    all_gather x1, blocking collectives: 18.7 us -> 13.1 us  [shards(): lax.all_gather(after(ends, beside, *cot_line), 'ctx').reshape(-1, columns)]
    ppermute x6, starting transfers between devices: 12.3 us -> 8.66 us  [core_swap(): return lax.ppermute(x, 'ctx', [(i, i ^ 1) for i in range(size)])]
    unnamed x44 -> x34, local copies, waits for them, and re-layouts: 4.26 us -> 2.82 us
  transfers between devices with their start and end apart: 26 -> 26, of which waited for: 8 -> 9; matrix products, arithmetic and copies ran while one was open for 13% -> 13% of each run, Pallas kernels for 30% -> 27%
where the time goes in v15:
time: 146 us; the launch traced here: 145 us
  Pallas kernels  42.1 us (29%)
  starting transfers between devices  36.4 us (25%)
  waiting for transfers between devices  29.5 us (20%)
  blocking collectives  13.1 us (9%)
  other arithmetic  11.7 us (8%)
  local copies, waits for them, and re-layouts  6.26 us (4%)
  matrix products  5.01 us (3%)
    pallas_call x8, Pallas kernels, run(): pl.pallas_call(body_by_tiles, grid=(columns // block,), in_specs=in_specs...  31.4 us
    ppermute x13, waiting for transfers between devices, chip_swap(): return lax.ppermute(x, 'ctx', [(i, i ^ 2 * by) for i in range(size)])  17.7 us
    all_gather x1, blocking collectives, shards(): lax.all_gather(after(ends, beside, *cot_line), 'ctx').reshape(-1, columns)  13.1 us
    ppermute x13, starting transfers between devices, chip_swap(): return lax.ppermute(x, 'ctx', [(i, i ^ 2 * by) for i in range(size)])  11.2 us
    pallas_call x3, Pallas kernels, run_once(): pl.pallas_call(body, grid=(1,), in_specs=[pl.BlockSpec(memory_space=pltpu...  10.7 us
    ppermute x5, starting transfers between devices, line_swap(): return lax.ppermute(x, 'fsdp', [(i, i ^ by) for i in range(size)])  9.01 us
    ppermute x6, starting transfers between devices, core_swap(): return lax.ppermute(x, 'ctx', [(i, i ^ 1) for i in range(size)])  8.66 us
    ppermute x2, starting transfers between devices, shifted(): lax.ppermute(x, 'ctx', [(i, i + by) for i in range(size) if 0 <= i + by <...  7.47 us
  transfers between devices with their start and end apart: 26, of which 9 were waited for; matrix products, arithmetic and copies ran while one was open for 13% of the time, Pallas kernels for 27%

profile of v15, /device:TPU:1, one launch (start us, length us, event | category | flops | bytes accessed | tf_op | source)
XLA Modules:
  0.0 145.0 jit_solution(18416828755664656731)
XLA Ops:
  1.7 4.5 %collective-permute-start = (bf16[128,1024]{1,0:T(8,128)(2,1)S(1)}, bf16[128,1024]{1,0:T(8,128)(2,1)S(1)}, u32[]{:S(2)}, u32[]{:S(2)}) collective-permute-start(bf16[128,1024]{1,0:T(8,128)(2,1)S(1)} %multiply_convert_fusion.refs_1_), channel_id=1, source_target_pairs={{0,4},{4,8},{8,12},{12,16},{16,20},{20,24},{24,28},{1,5},{5,9},{9,... | collective-permute-start | bytes 786440 | tf_op jit(solution)/shard_map/ppermute | solution.py:311
  6.3 3.3 %collective-permute-done.refs_0_ = bf16[128,1024]{1,0:T(8,128)(2,1)S(1)} collective-permute-done((bf16[128,1024]{1,0:T(8,128)(2,1)S(1)}, bf16[128,1024]{1,0:T(8,128)(2,1)S(1)}, u32[]{:S(2)}, u32[]{:S(2)}) %collective-permute-start) | collective-permute-done | bytes 262176 | tf_op jit(solution)/shard_map/ppermute | solution.py:311
  12.1 2.3 %collective-permute-start.3 = (bf16[128,1024]{1,0:T(8,128)(2,1)}, bf16[128,1024]{1,0:T(8,128)(2,1)S(1)}, u32[]{:S(2)}, u32[]{:S(2)}) collective-permute-start(bf16[128,1024]{1,0:T(8,128)(2,1)} %rest_0_), channel_id=1, source_target_pairs={{0,2},{1,3},{2,0},{3,1},{4,6},{5,7},{6,4},{7,5},{8,10},{9,11},{10,... | collective-permute-start | bytes 786440 | tf_op jit(solution)/shard_map/ppermute | solution.py:301
  16.0 3.4 %shard_map.197 = (f32[256,1024]{1,0:T(8,128)}, f32[256,1024]{1,0:T(8,128)}) custom-call(f32[128,1024]{1,0:T(8,128)} %refs_0_.1, f32[16,1024]{1,0:T(8,128)} %get-tuple-element.131.refs_1_.refs_6_.refs_3_.refs_2_, f32[16,1024]{1,0:T(8,128)} %get-tuple-element.127.refs_2_.refs_4_, f32[1,1024]{1,0:T(1,128)} %bitcast.22, ...), custom_call_target="tpu_custom_call" | custom-call | tf_op jit(solution)/shard_map/pallas_call | solution.py:267
  20.0 5.8 %shard_map.198 = (f32[256,1024]{1,0:T(8,128)}, f32[128,1024]{1,0:T(8,128)}, bf16[128,1024]{1,0:T(8,128)(2,1)}, f32[128,1024]{1,0:T(8,128)}, f32[16,1024]{1,0:T(8,128)}) custom-call(bf16[128,1024]{1,0:T(8,128)(2,1)} %copy-done.15, bf16[128,1024]{1,0:T(8,128)(2,1)} %copy-done.6, bf16[128,1024]{1,0:T(8,128)(2,1)} %refs_6_.2, bf16[128,1024]{1,0:T(8,128)(2,1)} %refs_5_.2, ...), custom_call_target="tpu_custom_call" | custom-call | tf_op jit(solution)/shard_map/pallas_call | solution.py:267
  25.8 4.6 %collective-permute-done.4.rest_3_ = bf16[128,1024]{1,0:T(8,128)(2,1)S(1)} collective-permute-done((bf16[128,1024]{1,0:T(8,128)(2,1)}, bf16[128,1024]{1,0:T(8,128)(2,1)S(1)}, u32[]{:S(2)}, u32[]{:S(2)}) %collective-permute-start.4) | collective-permute-done | bytes 262176 | tf_op jit(solution)/shard_map/ppermute | solution.py:301
  30.4 3.2 %collective-permute-done.1.refs_5_.rest_4_ = bf16[512,1024]{1,0:T(8,128)(2,1)S(1)} collective-permute-done((bf16[512,1024]{1,0:T(8,128)(2,1)}, bf16[512,1024]{1,0:T(8,128)(2,1)S(1)}, u32[]{:S(2)}, u32[]{:S(2)}) %collective-permute-start.1) | collective-permute-done | bytes 1048608 | tf_op jit(solution)/shard_map/ppermute | solution.py:296
  33.6 13.1 %all-gather.refs_5_ = f32[128,1024]{1,0:T(8,128)} all-gather(f32[16,1024]{1,0:T(8,128)} %get-tuple-element.72), channel_id=2, replica_groups=mesh['ctx'=8,'fsdp'=4] {'ctx'}, dimensions={0}, use_global_device_ids=true | all-gather | bytes 589824 | tf_op jit(solution)/shard_map/all_gather | solution.py:432
  46.7 2.8 %shard_map.199 = (f32[128,1024]{1,0:T(8,128)}, bf16[128,1024]{1,0:T(8,128)(2,1)}) custom-call(f32[8]{0:T(128)} %subtract_convert_fusion.refs_0_, f32[128,1024]{1,0:T(8,128)} %get-tuple-element.68.refs_1_, bf16[128,1024]{1,0:T(8,128)(2,1)} %refs_1_.1, f32[16,1024]{1,0:T(8,128)} %get-tuple-element.131.refs_1_.refs_6_.refs_3_.refs_2_, ...), custom_call_target="tpu_custom_call" | custom-call | tf_op jit(solution)/shard_map/pallas_call | solution.py:267
  50.7 2.3 %shard_map.200 = (bf16[128,2048]{1,0:T(8,128)(2,1)}, bf16[128,2048]{1,0:T(8,128)(2,1)}) custom-call(s32[6]{0:T(128)} %stack.57.starts, bf16[128,1024]{1,0:T(8,128)(2,1)} %rest_0_, bf16[128,1024]{1,0:T(8,128)(2,1)} %copy-done.10, bf16[128,1024]{1,0:T(8,128)(2,1)} %copy-done.11, bf16[128,1024]{1,0:T(8,128)(2,1)} %copy-done.12), custom_call_target="tpu_custom_call" | custom-call | tf_op jit(solution)/shard_map/pallas_call | solution.py:282
  55.1 11.6 %collective-permute-done.5.refs_2_ = bf16[128,2048]{1,0:T(8,128)(2,1)} collective-permute-done((bf16[128,2048]{1,0:T(8,128)(2,1)}, bf16[128,2048]{1,0:T(8,128)(2,1)}, u32[]{:S(2)}, u32[]{:S(2)}) %collective-permute-start.5) | collective-permute-done | bytes 524320 | tf_op jit(solution)/shard_map/ppermute | solution.py:296
  67.7 4.3 %shard_map.201 = (f32[128,1024]{1,0:T(8,128)}, bf16[128,1024]{1,0:T(8,128)(2,1)}) custom-call(s32[4]{0:T(128)} %pad_add_fusion.refs_0_.starts, bf16[128,2048]{1,0:T(8,128)(2,1)} %get-tuple-element.95.refs_1_, bf16[128,2048]{1,0:T(8,128)(2,1)} %collective-permute-done.5.refs_2_, bf16[512,1024]{1,0:T(8,128)(2,1)} %rest_2_.1, bf16[512,1024]{1,0:T(8,128)(2,1)} %copy-done.2, ...), custom_call_target="tpu_custom_call" | custom-call | flops 1073741824 | bytes 6029328 | tf_op jit(solution)/shard_map/pallas_call | solution.py:267
  76.9 6.1 %shard_map.202 = (bf16[128,2048]{1,0:T(8,128)(2,1)}, bf16[128,2048]{1,0:T(8,128)(2,1)}) custom-call(s32[4]{0:T(128)} %pad_add_fusion.refs_0_.starts, bf16[128,1024]{1,0:T(8,128)(2,1)} %get-tuple-element.85.rest_0_, bf16[128,1024]{1,0:T(8,128)(2,1)} %collective-permute-done.8.rest_1_, bf16[512,1024]{1,0:T(8,128)(2,1)} %rest_2_.1, ...), custom_call_target="tpu_custom_call" | custom-call | tf_op jit(solution)/shard_map/pallas_call | solution.py:282
  84.0 4.8 %shard_map.204 = (f32[128,1024]{1,0:T(8,128)}, f32[16,1024]{1,0:T(8,128)}, f32[128,1024]{1,0:T(8,128)}) custom-call(f32[128,1024]{1,0:T(8,128)} %get-tuple-element.92.refs_0_, bf16[128,1024]{1,0:T(8,128)(2,1)} %refs_1_.1, f32[16,1024]{1,0:T(8,128)} %get-tuple-element.131.refs_1_.refs_6_.refs_3_.refs_2_, f32[128,1024]{1,0:T(8,128)} %get-tuple-element.93.refs_3_, ...), custom_call_target="tpu_custom_call" | custom-call | flops 536870912 | bytes 4456448 | tf_op jit(solution)/shard_map/pallas_call | solution.py:267
  88.8 2.7 %collective-permute-start.15 = (f32[16,1024]{1,0:T(8,128)}, f32[16,1024]{1,0:T(8,128)S(1)}, u32[]{:S(2)}, u32[]{:S(2)}) collective-permute-start(f32[16,1024]{1,0:T(8,128)} %get-tuple-element.97), channel_id=1, source_target_pairs={{0,4},{4,0},{8,12},{12,8},{16,20},{20,16},{24,28},{28,24},{1,5},{5... | collective-permute-start | bytes 196616 | tf_op jit(solution)/shard_map/ppermute | solution.py:306
  93.5 3.0 %collective-permute-done.13 = bf16[256,1024]{1,0:T(8,128)(2,1)} collective-permute-done((bf16[256,1024]{1,0:T(8,128)(2,1)S(1)}, bf16[256,1024]{1,0:T(8,128)(2,1)}, u32[]{:S(2)}, u32[]{:S(2)}) %collective-permute-start.13) | collective-permute-done | bytes 524320 | tf_op jit(solution)/shard_map/ppermute | solution.py:296
  102.1 3.6 %collective-permute-start.21 = (bf16[512,1024]{1,0:T(8,128)(2,1)}, bf16[512,1024]{1,0:T(8,128)(2,1)}, u32[]{:S(2)}, u32[]{:S(2)}) collective-permute-start(bf16[512,1024]{1,0:T(8,128)(2,1)} %convolution_convert_fusion), channel_id=1, source_target_pairs={{0,4},{4,0},{8,12},{12,8},{16,20},{20,16},{24,28},{28,24},{1,5},{5... | collective-permute-start | bytes 3145736 | tf_op jit(solution)/shard_map/ppermute | solution.py:306
  105.7 2.3 %shard_map.203 = (bf16[256,1024]{1,0:T(8,128)(2,1)}, bf16[256,1024]{1,0:T(8,128)(2,1)}) custom-call(s32[6]{0:T(128)} %stack.51.starts, bf16[128,2048]{1,0:T(8,128)(2,1)} %get-tuple-element.86.rest_0_, bf16[128,2048]{1,0:T(8,128)(2,1)} %copy-done.7), custom_call_target="tpu_custom_call" | custom-call | tf_op jit(solution)/shard_map/pallas_call | solution.py:282
  108.0 3.1 %collective-permute-start.11 = (bf16[256,1024]{1,0:T(8,128)(2,1)}, bf16[256,1024]{1,0:T(8,128)(2,1)S(1)}, u32[]{:S(2)}, u32[]{:S(2)}) collective-permute-start(bf16[256,1024]{1,0:T(8,128)(2,1)} %get-tuple-element.91), channel_id=1, source_target_pairs={{0,1},{1,0},{2,3},{3,2},{4,5},{5,4},{6,7},{7,6},{8,9},{9,8},{10,11... | collective-permute-start | bytes 1572872 | tf_op jit(solution)/shard_map/ppermute | solution.py:301
  111.8 5.1 %shard_map.205 = (f32[128,1024]{1,0:T(8,128)}, f32[128,1024]{1,0:T(8,128)}, f32[256,1024]{1,0:T(8,128)}, f32[128,1024]{1,0:T(8,128)}) custom-call(f32[128,1024]{1,0:T(8,128)} %get-tuple-element.101.refs_0_, f32[16,1024]{1,0:T(8,128)} %get-tuple-element.131.refs_1_.refs_6_.refs_3_.refs_2_, f32[16,1024]{1,0:T(8,128)} %get-tuple-element.127.refs_2_.refs_4_, ...), custom_call_target="tpu_custom_call" | custom-call | flops 536870912 | bytes 6160384 | tf_op jit(solution)/shard_map/pallas_call | solution.py:267
  125.8 2.3 %collective-permute-start.12 = (bf16[128,1024]{1,0:T(8,128)(2,1)S(1)}, bf16[128,1024]{1,0:T(8,128)(2,1)S(1)}, u32[]{:S(2)}, u32[]{:S(2)}) collective-permute-start(bf16[128,1024]{1,0:T(8,128)(2,1)S(1)} %slice.13), channel_id=1, source_target_pairs={{0,2},{1,3},{2,0},{3,1},{4,6},{5,7},{6,4},{7,5},{8,10},{9,11},{10,... | collective-permute-start | bytes 786440 | tf_op jit(solution)/shard_map/ppermute | solution.py:301
  128.1 3.1 %shard_map.206 = (f32[128,1024]{1,0:T(8,128)}, bf16[128,1024]{1,0:T(8,128)(2,1)}) custom-call(f32[256,1024]{1,0:T(8,128)} %get-tuple-element.112.refs_0_, f32[256,1024]{1,0:T(8,128)} %get-tuple-element.66.refs_4_.refs_1_, bf16[256,768]{1,0:T(8,128)(2,1)} %constant.89.clone.refs_8_.refs_6_.refs_2_), custom_call_target="tpu_custom_call" | custom-call | flops 402653184 | bytes 3276800 | tf_op jit(solution)/shard_map/pallas_call | solution.py:267
  131.2 3.0 %collective-permute-start.19 = (bf16[128,1024]{1,0:T(8,128)(2,1)}, bf16[128,1024]{1,0:T(8,128)(2,1)}, u32[]{:S(2)}, u32[]{:S(2)}) collective-permute-start(bf16[128,1024]{1,0:T(8,128)(2,1)} %get-tuple-element.114), channel_id=1, source_target_pairs={{4,0},{8,4},{12,8},{16,12},{20,16},{24,20},{28,24},{5,1},{9,5},{13... | collective-permute-start | bytes 786440 | tf_op jit(solution)/shard_map/ppermute | solution.py:311
  134.2 3.3 %add_multiply_fusion = f32[512,1024]{1,0:T(8,128)} fusion(bf16[512,1024]{1,0:T(8,128)(2,1)} %collective-permute-done.21, bf16[512,1024]{1,0:T(8,128)(2,1)S(1)} %constant_dynamic-update-slice_fusion, bf16[512,1024]{1,0:T(8,128)(2,1)S(1)} %pad_maximum_fusion, s32[]{:T(128)S(6)} %select_n.99), kind=kOutput, calls=%fused_computation | convolution fusion | flops 538443776 | bytes 4718596 | tf_op jit(solution)/shard_map/dot_general | solution.py:521
  (96 shorter events, 40.7 us)
Async XLA Ops:
  1.7 7.8 %collective-permute-start = (bf16[128,1024]{1,0:T(8,128)(2,1)S(1)}, bf16[128,1024]{1,0:T(8,128)(2,1)S(1)}, u32[]{:S(2)}, u32[]{:S(2)}) collective-permute-start(bf16[128,1024]{1,0:T(8,128)(2,1)S(1)} %multiply_convert_fusion.refs_1_), channel_id=1, source_target_pairs={{0,4},{4,8},{8,12},{12,16},{16,20},{20,24},{24,28},{1,5},{5,9},{9,... | collective-permute-start | bytes 786440 | tf_op jit(solution)/shard_map/ppermute | solution.py:311
  9.6 24.0 %collective-permute-start.1 = (bf16[512,1024]{1,0:T(8,128)(2,1)}, bf16[512,1024]{1,0:T(8,128)(2,1)S(1)}, u32[]{:S(2)}, u32[]{:S(2)}) collective-permute-start(bf16[512,1024]{1,0:T(8,128)(2,1)} %rest_2_.1), channel_id=1, source_target_pairs={{0,8},{4,12},{8,0},{12,4},{16,24},{20,28},{24,16},{28,20},{1,9},{5... | collective-permute-start | bytes 3145736 | tf_op jit(solution)/shard_map/ppermute | solution.py:296
  10.8 15.0 %collective-permute-start.2 = (bf16[128,1024]{1,0:T(8,128)(2,1)}, bf16[128,1024]{1,0:T(8,128)(2,1)S(1)}, u32[]{:S(2)}, u32[]{:S(2)}) collective-permute-start(bf16[128,1024]{1,0:T(8,128)(2,1)} %rest_0_), channel_id=1, source_target_pairs={{0,1},{1,0},{2,3},{3,2},{4,5},{5,4},{6,7},{7,6},{8,9},{9,8},{10,11... | collective-permute-start | bytes 786440 | tf_op jit(solution)/shard_map/ppermute | solution.py:301
  12.1 13.7 %collective-permute-start.3 = (bf16[128,1024]{1,0:T(8,128)(2,1)}, bf16[128,1024]{1,0:T(8,128)(2,1)S(1)}, u32[]{:S(2)}, u32[]{:S(2)}) collective-permute-start(bf16[128,1024]{1,0:T(8,128)(2,1)} %rest_0_), channel_id=1, source_target_pairs={{0,2},{1,3},{2,0},{3,1},{4,6},{5,7},{6,4},{7,5},{8,10},{9,11},{10,... | collective-permute-start | bytes 786440 | tf_op jit(solution)/shard_map/ppermute | solution.py:301
  14.4 16.0 %collective-permute-start.4 = (bf16[128,1024]{1,0:T(8,128)(2,1)}, bf16[128,1024]{1,0:T(8,128)(2,1)S(1)}, u32[]{:S(2)}, u32[]{:S(2)}) collective-permute-start(bf16[128,1024]{1,0:T(8,128)(2,1)} %rest_0_), channel_id=1, source_target_pairs={{0,3},{1,2},{2,1},{3,0},{4,7},{5,6},{6,5},{7,4},{8,11},{9,10},{10,... | collective-permute-start | bytes 786440 | tf_op jit(solution)/shard_map/ppermute | solution.py:301
  49.5 17.2 %collective-permute-start.6 = (bf16[512,1024]{1,0:T(8,128)(2,1)S(1)}, bf16[512,1024]{1,0:T(8,128)(2,1)S(1)}, u32[]{:S(2)}, u32[]{:S(2)}) collective-permute-start(bf16[512,1024]{1,0:T(8,128)(2,1)S(1)} %copy-done), channel_id=1, source_target_pairs={{0,4},{4,0},{8,12},{12,8},{16,20},{20,16},{24,28},{28,24},{1,5},{5... | collective-permute-start | bytes 3145736 | tf_op jit(solution)/shard_map/ppermute | solution.py:306
  49.7 17.0 %collective-permute-start.7 = (bf16[512,1024]{1,0:T(8,128)(2,1)S(1)}, bf16[512,1024]{1,0:T(8,128)(2,1)}, u32[]{:S(2)}, u32[]{:S(2)}) collective-permute-start(bf16[512,1024]{1,0:T(8,128)(2,1)S(1)} %collective-permute-done.1.refs_5_.rest_4_), channel_id=1, source_target_pairs={{0,4},{4,0},{8,12},{12,8},{16,20},{20,16},{24,28},{28,24},{1,5},{5... | collective-permute-start | bytes 3145736 | tf_op jit(solution)/shard_map/ppermute | solution.py:306
  53.0 13.7 %collective-permute-start.5 = (bf16[128,2048]{1,0:T(8,128)(2,1)}, bf16[128,2048]{1,0:T(8,128)(2,1)}, u32[]{:S(2)}, u32[]{:S(2)}) collective-permute-start(bf16[128,2048]{1,0:T(8,128)(2,1)} %get-tuple-element.80), channel_id=1, source_target_pairs={{0,16},{4,20},{8,24},{12,28},{16,0},{20,4},{24,8},{28,12},{1,17},{... | collective-permute-start | bytes 1572872 | tf_op jit(solution)/shard_map/ppermute | solution.py:296
  53.5 18.9 %collective-permute-start.8 = (bf16[128,1024]{1,0:T(8,128)(2,1)}, bf16[128,1024]{1,0:T(8,128)(2,1)}, u32[]{:S(2)}, u32[]{:S(2)}) collective-permute-start(bf16[128,1024]{1,0:T(8,128)(2,1)} %get-tuple-element.85.rest_0_), channel_id=1, source_target_pairs={{0,16},{4,20},{8,24},{12,28},{16,0},{20,4},{24,8},{28,12},{1,17},{... | collective-permute-start | bytes 786440 | tf_op jit(solution)/shard_map/ppermute | solution.py:296
  71.9 11.0 %collective-permute-start.9 = (bf16[128,1024]{1,0:T(8,128)(2,1)}, bf16[128,1024]{1,0:T(8,128)(2,1)S(1)}, u32[]{:S(2)}, u32[]{:S(2)}) collective-permute-start(bf16[128,1024]{1,0:T(8,128)(2,1)} %get-tuple-element.88), channel_id=1, source_target_pairs={{0,16},{4,20},{8,24},{12,28},{16,0},{20,4},{24,8},{28,12},{1,17},{... | collective-permute-start | bytes 786440 | tf_op jit(solution)/shard_map/ppermute | solution.py:296
  73.4 20.0 %collective-permute-start.14 = (bf16[256,1024]{1,0:T(8,128)(2,1)S(1)}, bf16[256,1024]{1,0:T(8,128)(2,1)S(1)}, u32[]{:S(2)}, u32[]{:S(2)}) collective-permute-start(bf16[256,1024]{1,0:T(8,128)(2,1)S(1)} %pad_maximum_fusion.2), channel_id=1, source_target_pairs={{0,8},{4,12},{8,0},{12,4},{16,24},{20,28},{24,16},{28,20},{1,9},{5... | collective-permute-start | bytes 1572872 | tf_op jit(solution)/shard_map/ppermute | solution.py:296
  75.6 20.8 %collective-permute-start.13 = (bf16[256,1024]{1,0:T(8,128)(2,1)S(1)}, bf16[256,1024]{1,0:T(8,128)(2,1)}, u32[]{:S(2)}, u32[]{:S(2)}) collective-permute-start(bf16[256,1024]{1,0:T(8,128)(2,1)S(1)} %pad_maximum_fusion.1), channel_id=1, source_target_pairs={{0,8},{4,12},{8,0},{12,4},{16,24},{20,28},{24,16},{28,20},{1,9},{5... | collective-permute-start | bytes 1572872 | tf_op jit(solution)/shard_map/ppermute | solution.py:296
  83.0 14.6 %collective-permute-start.10 = (bf16[128,2048]{1,0:T(8,128)(2,1)}, bf16[128,2048]{1,0:T(8,128)(2,1)S(1)}, u32[]{:S(2)}, u32[]{:S(2)}) collective-permute-start(bf16[128,2048]{1,0:T(8,128)(2,1)} %get-tuple-element.89), channel_id=1, source_target_pairs={{0,16},{4,20},{8,24},{12,28},{16,0},{20,4},{24,8},{28,12},{1,17},{... | collective-permute-start | bytes 1572872 | tf_op jit(solution)/shard_map/ppermute | solution.py:296
  97.7 13.4 %collective-permute-start.18 = (f32[16,1024]{1,0:T(8,128)S(1)}, f32[16,1024]{1,0:T(8,128)S(1)}, u32[]{:S(2)}, u32[]{:S(2)}) collective-permute-start(f32[16,1024]{1,0:T(8,128)S(1)} %add_select_fusion.1), channel_id=1, source_target_pairs={{0,24},{4,28},{8,16},{12,20},{16,8},{20,12},{24,0},{28,4},{1,25},{... | collective-permute-start | bytes 196616 | tf_op jit(solution)/shard_map/ppermute | solution.py:296
  98.9 12.2 %collective-permute-start.17 = (f32[16,1024]{1,0:T(8,128)S(1)}, f32[16,1024]{1,0:T(8,128)S(1)}, u32[]{:S(2)}, u32[]{:S(2)}) collective-permute-start(f32[16,1024]{1,0:T(8,128)S(1)} %add_select_fusion.1), channel_id=1, source_target_pairs={{0,16},{4,20},{8,24},{12,28},{16,0},{20,4},{24,8},{28,12},{1,17},{... | collective-permute-start | bytes 196616 | tf_op jit(solution)/shard_map/ppermute | solution.py:296
  99.8 11.2 %collective-permute-start.16 = (f32[16,1024]{1,0:T(8,128)S(1)}, f32[16,1024]{1,0:T(8,128)S(1)}, u32[]{:S(2)}, u32[]{:S(2)}) collective-permute-start(f32[16,1024]{1,0:T(8,128)S(1)} %add_select_fusion.1), channel_id=1, source_target_pairs={{0,8},{4,12},{8,0},{12,4},{16,24},{20,28},{24,16},{28,20},{1,9},{5... | collective-permute-start | bytes 196616 | tf_op jit(solution)/shard_map/ppermute | solution.py:296
  102.1 29.1 %collective-permute-start.21 = (bf16[512,1024]{1,0:T(8,128)(2,1)}, bf16[512,1024]{1,0:T(8,128)(2,1)}, u32[]{:S(2)}, u32[]{:S(2)}) collective-permute-start(bf16[512,1024]{1,0:T(8,128)(2,1)} %convolution_convert_fusion), channel_id=1, source_target_pairs={{0,4},{4,0},{8,12},{12,8},{16,20},{20,16},{24,28},{28,24},{1,5},{5... | collective-permute-start | bytes 3145736 | tf_op jit(solution)/shard_map/ppermute | solution.py:306
  108.0 15.6 %collective-permute-start.11 = (bf16[256,1024]{1,0:T(8,128)(2,1)}, bf16[256,1024]{1,0:T(8,128)(2,1)S(1)}, u32[]{:S(2)}, u32[]{:S(2)}) collective-permute-start(bf16[256,1024]{1,0:T(8,128)(2,1)} %get-tuple-element.91), channel_id=1, source_target_pairs={{0,1},{1,0},{2,3},{3,2},{4,5},{5,4},{6,7},{7,6},{8,9},{9,8},{10,11... | collective-permute-start | bytes 1572872 | tf_op jit(solution)/shard_map/ppermute | solution.py:301
  120.4 17.1 %collective-permute-start.24 = (bf16[64,1024]{1,0:T(8,128)(2,1)S(1)}, bf16[64,1024]{1,0:T(8,128)(2,1)S(1)}, u32[]{:S(2)}, u32[]{:S(2)}) collective-permute-start(bf16[64,1024]{1,0:T(8,128)(2,1)S(1)} %fusion.2), channel_id=1, source_target_pairs={{0,24},{4,28},{8,16},{12,20},{16,8},{20,12},{24,0},{28,4},{1,25},{... | collective-permute-start | bytes 393224 | tf_op jit(solution)/shard_map/ppermute | solution.py:296
  121.6 15.8 %collective-permute-start.23 = (bf16[64,1024]{1,0:T(8,128)(2,1)S(1)}, bf16[64,1024]{1,0:T(8,128)(2,1)S(1)}, u32[]{:S(2)}, u32[]{:S(2)}) collective-permute-start(bf16[64,1024]{1,0:T(8,128)(2,1)S(1)} %fusion.2), channel_id=1, source_target_pairs={{0,16},{4,20},{8,24},{12,28},{16,0},{20,4},{24,8},{28,12},{1,17},{... | collective-permute-start | bytes 393224 | tf_op jit(solution)/shard_map/ppermute | solution.py:296
  122.7 14.7 %collective-permute-start.22 = (bf16[64,1024]{1,0:T(8,128)(2,1)S(1)}, bf16[64,1024]{1,0:T(8,128)(2,1)S(1)}, u32[]{:S(2)}, u32[]{:S(2)}) collective-permute-start(bf16[64,1024]{1,0:T(8,128)(2,1)S(1)} %fusion.2), channel_id=1, source_target_pairs={{0,8},{4,12},{8,0},{12,4},{16,24},{20,28},{24,16},{28,20},{1,9},{5... | collective-permute-start | bytes 393224 | tf_op jit(solution)/shard_map/ppermute | solution.py:296
  125.8 13.8 %collective-permute-start.12 = (bf16[128,1024]{1,0:T(8,128)(2,1)S(1)}, bf16[128,1024]{1,0:T(8,128)(2,1)S(1)}, u32[]{:S(2)}, u32[]{:S(2)}) collective-permute-start(bf16[128,1024]{1,0:T(8,128)(2,1)S(1)} %slice.13), channel_id=1, source_target_pairs={{0,2},{1,3},{2,0},{3,1},{4,6},{5,7},{6,4},{7,5},{8,10},{9,11},{10,... | collective-permute-start | bytes 786440 | tf_op jit(solution)/shard_map/ppermute | solution.py:301
  131.2 9.9 %collective-permute-start.19 = (bf16[128,1024]{1,0:T(8,128)(2,1)}, bf16[128,1024]{1,0:T(8,128)(2,1)}, u32[]{:S(2)}, u32[]{:S(2)}) collective-permute-start(bf16[128,1024]{1,0:T(8,128)(2,1)} %get-tuple-element.114), channel_id=1, source_target_pairs={{4,0},{8,4},{12,8},{16,12},{20,16},{24,20},{28,24},{5,1},{9,5},{13... | collective-permute-start | bytes 786440 | tf_op jit(solution)/shard_map/ppermute | solution.py:311
  139.6 4.5 %collective-permute-start.25 = (f32[64,1024]{1,0:T(8,128)S(1)}, f32[64,1024]{1,0:T(8,128)S(1)}, u32[]{:S(2)}, u32[]{:S(2)}) collective-permute-start(f32[64,1024]{1,0:T(8,128)S(1)} %add_multiply_fusion.1), channel_id=1, source_target_pairs={{0,4},{4,0},{8,12},{12,8},{16,20},{20,16},{24,28},{28,24},{1,5},{5... | collective-permute-start | bytes 786440 | tf_op jit(solution)/shard_map/ppermute | solution.py:306
  (18 other events, 244.7 us)

commit v16 on v14

--- a/solution.py
+++ b/solution.py
@@ -164,41 +164,46 @@
     mixed[...] = (query[...].astype(F32) * total).astype(BF16)
 
 
-def split_body(count, starts, *rest):
+def split_body(count, base, starts, *rest):
     pieces, parts, whole = rest[: -count - 1], rest[-count - 1 : -1], rest[-1]
     for r, piece in enumerate(pieces):
-        whole[:, pl.ds(pl.multiple_of(starts[r], 128), piece.shape[1])] = piece[...]
+        whole[:, pl.ds(pl.multiple_of(starts[base + r], 128), piece.shape[1])] = piece[...]
     for h, part in enumerate(parts):
-        place = pl.multiple_of(starts[len(pieces) + h], 128)
+        place = pl.multiple_of(starts[base + len(pieces) + h], 128)
         part[...] = whole[:, pl.ds(place, part.shape[1])]
 
 
-def pair_grad_body(count, starts, *rest):
-    parts, weights, (own, *others) = rest[:count], rest[count : count + 4], rest[count + 4 :]
-    for part, result in zip(parts, (own, *others)):
-        total = None
-        for m, weight in enumerate(weights):
-            block = part[:, pl.ds(pl.multiple_of(starts[m], 128), weight.shape[0])]
-            found = jnp.dot(block, weight[...], preferred_element_type=F32)
-            total = found if total is None else total + found
-        result[...] = total.astype(result.dtype)
-
-
-def pair_out_body(count, starts, *rest):
+def pair_grad_body(count, base, starts, *rest):
+    parts, weights, results = rest[:count], rest[count : count + 4], rest[count + 4 :]
+    rows = parts[0].shape[0]
+    total = None
+    for m, weight in enumerate(weights):
+        place = pl.ds(pl.multiple_of(starts[base + m], 128), weight.shape[0])
+        block = jnp.concatenate([part[:, place] for part in parts], axis=0)
+        found = jnp.dot(block, weight[...], preferred_element_type=F32)
+        total = found if total is None else total + found
+    for h, result in enumerate(results):
+        result[...] = total[h * rows : (h + 1) * rows].astype(result.dtype)
+
+
+def pair_out_body(count, base, starts, *rest):
     mixed, weights, results = rest[:count], rest[count : count + 4], rest[count + 4 :]
-    for rows, result in zip(mixed, results):
-        for m, weight in enumerate(weights):
-            found = lax.dot_general(rows[...], weight[...], (((1,), (1,)), ((), ())), preferred_element_type=F32)
-            result[:, pl.ds(pl.multiple_of(starts[m], 128), weight.shape[0])] = found.astype(BF16)
-
-
-def stack_body(count, starts, *rest):
+    rows = mixed[0].shape[0]
+    block = jnp.concatenate([part[...] for part in mixed], axis=0)
+    for m, weight in enumerate(weights):
+        place = pl.ds(pl.multiple_of(starts[base + m], 128), weight.shape[0])
+        found = lax.dot_general(block, weight[...], (((1,), (1,)), ((), ())), preferred_element_type=F32)
+        for h, result in enumerate(results):
+            result[:, place] = found[h * rows : (h + 1) * rows].astype(BF16)
+
+
+def stack_body(count, base, starts, *rest):
     pieces, stacks, whole = rest[:-3], rest[-3:-1], rest[-1]
     rows = whole.shape[0]
     for r, piece in enumerate(pieces):
-        whole[:, pl.ds(pl.multiple_of(starts[r], 128), piece.shape[1])] = piece[...]
+        whole[:, pl.ds(pl.multiple_of(starts[base + r], 128), piece.shape[1])] = piece[...]
     for h in range(count):
-        place = pl.multiple_of(starts[len(pieces) + h], 128)
+        place = pl.multiple_of(starts[base + len(pieces) + h], 128)
         stack, at = stacks[h // (count // 2)], h % (count // 2)
         stack[at * rows : (at + 1) * rows] = whole[:, pl.ds(place, stack.shape[1])]
 
@@ -401,6 +406,15 @@
     pair_width = 4 * width
 
     sibling_weight = core_swap(out_weight)
+    line_width = cotangent.shape[1]
+    places = [(line ^ r) * line_width for r in range(line_count)] + [(pair ^ h) * pair_width for h in range(pairs)]
+    pair_base = len(places)
+    places += [((here & 3) ^ m) * width for m in range(4)]
+    out_base = len(places)
+    places += [(pair ^ h) * pair_width for h in range(pairs)]
+    places += [(line ^ r) * line_width for r in bit_reversed(line_count)]
+    starts = jnp.stack(places)
+
     rate = 1.0 / after(li_time, mr_product)
     beside = chip_swap(after(out_weight, before), 1)
     coef = li_residue * jnp.sqrt(-jnp.expm1(-2.0 * rate))
@@ -430,13 +444,10 @@
         0,
     )
 
-    line_width = cotangent.shape[1]
     whole_width = line_width * line_count
-    split_starts = [(line ^ r) * line_width for r in range(line_count)]
-    split_starts += [(pair ^ h) * pair_width for h in range(pairs)]
     cot_pairs = run_once(
-        functools.partial(split_body, pairs),
-        [jnp.stack(split_starts)] + [after(piece, ends) for piece in cot_line],
+        functools.partial(split_body, pairs, 0),
+        [starts] + [after(piece, ends) for piece in cot_line],
         [((rows, pair_width), BF16)] * pairs,
         [pltpu.VMEM((rows, whole_width), BF16)],
     )
@@ -453,29 +464,26 @@
 
     mixed_parts = [mixed_li] + [chip_swap(mixed_li, 2 * h) for h in range(1, pairs)]
     weights = [out_weight, sibling_weight, beside, core_swap(after(beside, cot_pairs[0]))]
-    pair_starts = jnp.stack([((here & 3) ^ m) * width for m in range(4)])
 
     share_flops = 2 * rows * columns * pair_width * pairs
     grad_own, *grad_sent = run(
-        functools.partial(pair_grad_body, pairs),
-        columns,
-        [("scalar", pair_starts)] + [("whole", after(part, mixed_li)) for part in cot_parts] + [tile(weight) for weight in weights],
+        functools.partial(pair_grad_body, pairs, pair_base),
+        columns,
+        [("scalar", starts)] + [("whole", after(part, mixed_li)) for part in cot_parts] + [tile(weight) for weight in weights],
         [(rows, F32)] + [(rows, BF16)] * (pairs - 1),
         share_flops,
     )
     grad_parts = [chip_swap(part, 2 * h) for h, part in enumerate(grad_sent, 1)]
 
     out_own, *out_sent = run_once(
-        functools.partial(pair_out_body, pairs),
-        [pair_starts, after(mixed_parts[0], grad_own)] + mixed_parts[1:] + weights,
+        functools.partial(pair_out_body, pairs, pair_base),
+        [starts, after(mixed_parts[0], grad_own)] + mixed_parts[1:] + weights,
         [((rows, pair_width), BF16)] * pairs,
     )
     out_pairs = [out_own] + [chip_swap(after(part, *grad_parts), 2 * h) for h, part in enumerate(out_sent, 1)]
-    out_starts = [(pair ^ h) * pair_width for h in range(pairs)]
-    out_starts += [(line ^ r) * line_width for r in bit_reversed(line_count)]
     kept, odd = run_once(
-        functools.partial(stack_body, line_count),
-        [jnp.stack(out_starts)] + out_pairs,
+        functools.partial(stack_body, line_count, out_base),
+        [starts] + out_pairs,
         [((line_count // 2 * rows, line_width), BF16)] * 2,
         [pltpu.VMEM((rows, whole_width), BF16)],
     )

time: 140 us -> 138 us (0.986)
  Pallas kernels: 42.4 us -> 40.9 us
    pallas_call x3, Pallas kernels: 10.7 us -> 9.22 us  [run_once(): pl.pallas_call(body, grid=(1,), in_specs=[pl.BlockSpec(memory_space=pltpu...]
  transfers between devices with their start and end apart: 26 -> 26, of which waited for: 8 -> 8; matrix products, arithmetic and copies ran while one was open for 13% -> 12% of each run, Pallas kernels for 30% -> 30%
where the time goes in v16:
time: 138 us; the launch traced here: 137 us
  Pallas kernels  40.9 us (30%)
  starting transfers between devices  39.7 us (29%)
  blocking collectives  18.7 us (14%)
  waiting for transfers between devices  14.7 us (11%)
  other arithmetic  9.99 us (7%)
  local copies, waits for them, and re-layouts  6.89 us (5%)
  matrix products  5.02 us (4%)
    pallas_call x8, Pallas kernels, run(): pl.pallas_call(body_by_tiles, grid=(columns // block,), in_specs=in_specs...  31.7 us
    all_gather x1, blocking collectives, shards(): lax.all_gather(after(ends, beside, *cot_parts[:1]), 'ctx')  18.7 us
    ppermute x6, starting transfers between devices, core_swap(): return lax.ppermute(x, 'ctx', [(i, i ^ 1) for i in range(size)])  12.3 us
    ppermute x13, starting transfers between devices, chip_swap(): return lax.ppermute(x, 'ctx', [(i, i ^ 2 * by) for i in range(size)])  11.5 us
    pallas_call x3, Pallas kernels, run_once(): pl.pallas_call(body, grid=(1,), in_specs=[pl.BlockSpec(memory_space=pltpu...  9.22 us
    ppermute x5, starting transfers between devices, line_swap(): return lax.ppermute(x, 'fsdp', [(i, i ^ by) for i in range(size)])  8.48 us
    ppermute x2, starting transfers between devices, shifted(): lax.ppermute(x, 'ctx', [(i, i + by) for i in range(size) if 0 <= i + by <...  7.48 us
    ppermute x5, waiting for transfers between devices, line_swap(): return lax.ppermute(x, 'fsdp', [(i, i ^ by) for i in range(size)])  6.72 us
  transfers between devices with their start and end apart: 26, of which 8 were waited for; matrix products, arithmetic and copies ran while one was open for 12% of the time, Pallas kernels for 30%

profile of v16, /device:TPU:1, one launch (start us, length us, event | category | flops | bytes accessed | tf_op | source)
XLA Modules:
  0.0 136.9 jit_solution(7084592408695506719)
XLA Ops:
  1.7 4.5 %collective-permute-start = (bf16[128,1024]{1,0:T(8,128)(2,1)S(1)}, bf16[128,1024]{1,0:T(8,128)(2,1)S(1)}, u32[]{:S(2)}, u32[]{:S(2)}) collective-permute-start(bf16[128,1024]{1,0:T(8,128)(2,1)S(1)} %multiply_convert_fusion.refs_1_), channel_id=1, source_target_pairs={{0,4},{4,8},{8,12},{12,16},{16,20},{20,24},{24,28},{1,5},{5,9},{9,... | collective-permute-start | bytes 786440 | tf_op jit(solution)/shard_map/ppermute | solution.py:316
  6.3 3.2 %collective-permute-done.refs_0_ = bf16[128,1024]{1,0:T(8,128)(2,1)S(1)} collective-permute-done((bf16[128,1024]{1,0:T(8,128)(2,1)S(1)}, bf16[128,1024]{1,0:T(8,128)(2,1)S(1)}, u32[]{:S(2)}, u32[]{:S(2)}) %collective-permute-start) | collective-permute-done | bytes 262176 | tf_op jit(solution)/shard_map/ppermute | solution.py:316
  12.1 2.3 %collective-permute-start.4 = (bf16[128,1024]{1,0:T(8,128)(2,1)}, bf16[128,1024]{1,0:T(8,128)(2,1)S(1)}, u32[]{:S(2)}, u32[]{:S(2)}) collective-permute-start(bf16[128,1024]{1,0:T(8,128)(2,1)} %rest_0_), channel_id=1, source_target_pairs={{0,2},{1,3},{2,0},{3,1},{4,6},{5,7},{6,4},{7,5},{8,10},{9,11},{10,... | collective-permute-start | bytes 786440 | tf_op jit(solution)/shard_map/ppermute | solution.py:306
  16.0 3.4 %shard_map.197 = (f32[256,1024]{1,0:T(8,128)}, f32[256,1024]{1,0:T(8,128)}) custom-call(f32[128,1024]{1,0:T(8,128)} %refs_0_.1, f32[16,1024]{1,0:T(8,128)} %get-tuple-element.127.refs_1_.refs_6_.refs_3_.refs_2_, f32[16,1024]{1,0:T(8,128)} %get-tuple-element.123.refs_2_.refs_4_, f32[1,1024]{1,0:T(1,128)} %bitcast.22, ...), custom_call_target="tpu_custom_call" | custom-call | tf_op jit(solution)/shard_map/pallas_call | solution.py:272
  20.1 6.1 %shard_map.198 = (f32[256,1024]{1,0:T(8,128)}, f32[128,1024]{1,0:T(8,128)}, bf16[128,1024]{1,0:T(8,128)(2,1)}, f32[128,1024]{1,0:T(8,128)}, f32[16,1024]{1,0:T(8,128)}) custom-call(bf16[128,1024]{1,0:T(8,128)(2,1)} %copy-done.19, bf16[128,1024]{1,0:T(8,128)(2,1)} %copy-done.8, bf16[128,1024]{1,0:T(8,128)(2,1)} %refs_6_.2, bf16[128,1024]{1,0:T(8,128)(2,1)} %refs_5_.2, ...), custom_call_target="tpu_custom_call" | custom-call | tf_op jit(solution)/shard_map/pallas_call | solution.py:272
  26.2 4.2 %collective-permute-done.5.rest_3_ = bf16[128,1024]{1,0:T(8,128)(2,1)S(1)} collective-permute-done((bf16[128,1024]{1,0:T(8,128)(2,1)}, bf16[128,1024]{1,0:T(8,128)(2,1)S(1)}, u32[]{:S(2)}, u32[]{:S(2)}) %collective-permute-start.5) | collective-permute-done | bytes 262176 | tf_op jit(solution)/shard_map/ppermute | solution.py:306
  31.1 2.3 %shard_map.199 = (bf16[128,2048]{1,0:T(8,128)(2,1)}, bf16[128,2048]{1,0:T(8,128)(2,1)}) custom-call(s32[16]{0:T(128)} %stack.49.starts.refs_0_, bf16[128,1024]{1,0:T(8,128)(2,1)} %rest_0_, bf16[128,1024]{1,0:T(8,128)(2,1)} %copy-done.14, bf16[128,1024]{1,0:T(8,128)(2,1)} %copy-done.15, bf16[128,1024]{1,0:T(8,128)(2,1)} %copy-done.16), custom_call_target="tpu_custom_call" | custom-call | tf_op jit(solution)/shard_map/pallas_call | solution.py:287
  33.6 5.8 %collective-permute-start.7 = (bf16[512,1024]{1,0:T(8,128)(2,1)S(1)}, bf16[512,1024]{1,0:T(8,128)(2,1)S(1)}, u32[]{:S(2)}, u32[]{:S(2)}) collective-permute-start(bf16[512,1024]{1,0:T(8,128)(2,1)S(1)} %collective-permute-done.2.refs_5_.rest_4_), channel_id=1, source_target_pairs={{0,4},{4,0},{8,12},{12,8},{16,20},{20,16},{24,28},{28,24},{1,5},{5... | collective-permute-start | bytes 3145736 | tf_op jit(solution)/shard_map/ppermute | solution.py:311
  40.4 18.7 %all-gather.refs_5_ = f32[128,1024]{1,0:T(8,128)} all-gather(f32[16,1024]{1,0:T(8,128)} %get-tuple-element.76), channel_id=2, replica_groups=mesh['ctx'=8,'fsdp'=4] {'ctx'}, dimensions={0}, use_global_device_ids=true | all-gather | bytes 589824 | tf_op jit(solution)/shard_map/all_gather | solution.py:455
  59.1 2.8 %shard_map.200 = (f32[128,1024]{1,0:T(8,128)}, bf16[128,1024]{1,0:T(8,128)(2,1)}) custom-call(f32[8]{0:T(128)} %subtract_convert_fusion.refs_0_, f32[128,1024]{1,0:T(8,128)} %get-tuple-element.67.refs_1_, bf16[128,1024]{1,0:T(8,128)(2,1)} %refs_1_.1, f32[16,1024]{1,0:T(8,128)} %get-tuple-element.127.refs_1_.refs_6_.refs_3_.refs_2_, ...), custom_call_target="tpu_custom_call" | custom-call | tf_op jit(solution)/shard_map/pallas_call | solution.py:272
  66.2 4.2 %shard_map.201 = (f32[128,1024]{1,0:T(8,128)}, bf16[128,1024]{1,0:T(8,128)(2,1)}) custom-call(s32[16]{0:T(128)} %stack.49.starts.refs_0_, bf16[128,2048]{1,0:T(8,128)(2,1)} %get-tuple-element.78.refs_1_, bf16[128,2048]{1,0:T(8,128)(2,1)} %copy-done.7, bf16[512,1024]{1,0:T(8,128)(2,1)} %rest_2_.1, bf16[512,1024]{1,0:T(8,128)(2,1)} %copy-done, ...), custom_call_target="tpu_custom_call" | custom-call | flops 1073741824 | bytes 6029376 | tf_op jit(solution)/shard_map/pallas_call | solution.py:272
  72.5 4.6 %shard_map.202 = (bf16[128,2048]{1,0:T(8,128)(2,1)}, bf16[128,2048]{1,0:T(8,128)(2,1)}) custom-call(s32[16]{0:T(128)} %stack.49.starts.refs_0_, bf16[128,1024]{1,0:T(8,128)(2,1)} %get-tuple-element.83.rest_0_, bf16[128,1024]{1,0:T(8,128)(2,1)} %copy-done.5, bf16[512,1024]{1,0:T(8,128)(2,1)} %rest_2_.1, bf16[512,1024]{1,0:T(8,128)(2,1)} %copy-done, ...), custom_call_target="tpu_custom_call" | custom-call | tf_op jit(solution)/shard_map/pallas_call | solution.py:287
  79.7 4.8 %shard_map.204 = (f32[128,1024]{1,0:T(8,128)}, f32[16,1024]{1,0:T(8,128)}, f32[128,1024]{1,0:T(8,128)}) custom-call(f32[128,1024]{1,0:T(8,128)} %get-tuple-element.90.refs_0_, bf16[128,1024]{1,0:T(8,128)(2,1)} %refs_1_.1, f32[16,1024]{1,0:T(8,128)} %get-tuple-element.127.refs_1_.refs_6_.refs_3_.refs_2_, f32[128,1024]{1,0:T(8,128)} %get-tuple-element.91.refs_3_, ...), custom_call_target="tpu_custom_call" | custom-call | flops 536870912 | bytes 4456448 | tf_op jit(solution)/shard_map/pallas_call | solution.py:272
  87.4 2.2 %collective-permute-done.14 = bf16[256,1024]{1,0:T(8,128)(2,1)S(1)} collective-permute-done((bf16[256,1024]{1,0:T(8,128)(2,1)S(1)}, bf16[256,1024]{1,0:T(8,128)(2,1)S(1)}, u32[]{:S(2)}, u32[]{:S(2)}) %collective-permute-start.14) | collective-permute-done | bytes 524320 | tf_op jit(solution)/shard_map/ppermute | solution.py:301
  95.1 3.0 %collective-permute-start.21 = (bf16[512,1024]{1,0:T(8,128)(2,1)}, bf16[512,1024]{1,0:T(8,128)(2,1)}, u32[]{:S(2)}, u32[]{:S(2)}) collective-permute-start(bf16[512,1024]{1,0:T(8,128)(2,1)} %convolution_convert_fusion), channel_id=1, source_target_pairs={{0,4},{4,0},{8,12},{12,8},{16,20},{20,16},{24,28},{28,24},{1,5},{5... | collective-permute-start | bytes 3145736 | tf_op jit(solution)/shard_map/ppermute | solution.py:311
  98.1 2.3 %shard_map.203 = (bf16[256,1024]{1,0:T(8,128)(2,1)}, bf16[256,1024]{1,0:T(8,128)(2,1)}) custom-call(s32[16]{0:T(128)} %stack.49.starts.refs_0_, bf16[128,2048]{1,0:T(8,128)(2,1)} %get-tuple-element.84.rest_0_, bf16[128,2048]{1,0:T(8,128)(2,1)} %copy-done.11), custom_call_target="tpu_custom_call" | custom-call | tf_op jit(solution)/shard_map/pallas_call | solution.py:287
  100.4 2.6 %collective-permute-start.11 = (bf16[256,1024]{1,0:T(8,128)(2,1)}, bf16[256,1024]{1,0:T(8,128)(2,1)S(1)}, u32[]{:S(2)}, u32[]{:S(2)}) collective-permute-start(bf16[256,1024]{1,0:T(8,128)(2,1)} %get-tuple-element.89), channel_id=1, source_target_pairs={{0,1},{1,0},{2,3},{3,2},{4,5},{5,4},{6,7},{7,6},{8,9},{9,8},{10,11... | collective-permute-start | bytes 1572872 | tf_op jit(solution)/shard_map/ppermute | solution.py:306
  103.7 5.1 %shard_map.205 = (f32[128,1024]{1,0:T(8,128)}, f32[128,1024]{1,0:T(8,128)}, f32[256,1024]{1,0:T(8,128)}, f32[128,1024]{1,0:T(8,128)}) custom-call(f32[128,1024]{1,0:T(8,128)} %get-tuple-element.97.refs_0_, f32[16,1024]{1,0:T(8,128)} %get-tuple-element.127.refs_1_.refs_6_.refs_3_.refs_2_, f32[16,1024]{1,0:T(8,128)} %get-tuple-element.123.refs_2_.refs_4_, ...), custom_call_target="tpu_custom_call" | custom-call | flops 536870912 | bytes 6160384 | tf_op jit(solution)/shard_map/pallas_call | solution.py:272
  117.7 2.3 %collective-permute-start.12 = (bf16[128,1024]{1,0:T(8,128)(2,1)S(1)}, bf16[128,1024]{1,0:T(8,128)(2,1)S(1)}, u32[]{:S(2)}, u32[]{:S(2)}) collective-permute-start(bf16[128,1024]{1,0:T(8,128)(2,1)S(1)} %slice.13), channel_id=1, source_target_pairs={{0,2},{1,3},{2,0},{3,1},{4,6},{5,7},{6,4},{7,5},{8,10},{9,11},{10,... | collective-permute-start | bytes 786440 | tf_op jit(solution)/shard_map/ppermute | solution.py:306
  120.0 3.1 %shard_map.206 = (f32[128,1024]{1,0:T(8,128)}, bf16[128,1024]{1,0:T(8,128)(2,1)}) custom-call(f32[256,1024]{1,0:T(8,128)} %get-tuple-element.108.refs_0_, f32[256,1024]{1,0:T(8,128)} %get-tuple-element.65.refs_4_.refs_1_, bf16[256,768]{1,0:T(8,128)(2,1)} %constant.89.clone.refs_8_.refs_6_.refs_2_), custom_call_target="tpu_custom_call" | custom-call | flops 402653184 | bytes 3276800 | tf_op jit(solution)/shard_map/pallas_call | solution.py:272
  123.1 3.0 %collective-permute-start.19 = (bf16[128,1024]{1,0:T(8,128)(2,1)}, bf16[128,1024]{1,0:T(8,128)(2,1)}, u32[]{:S(2)}, u32[]{:S(2)}) collective-permute-start(bf16[128,1024]{1,0:T(8,128)(2,1)} %get-tuple-element.110), channel_id=1, source_target_pairs={{4,0},{8,4},{12,8},{16,12},{20,16},{24,20},{28,24},{5,1},{9,5},{13... | collective-permute-start | bytes 786440 | tf_op jit(solution)/shard_map/ppermute | solution.py:316
  126.1 3.3 %add_multiply_fusion = f32[512,1024]{1,0:T(8,128)} fusion(bf16[512,1024]{1,0:T(8,128)(2,1)} %collective-permute-done.21, bf16[512,1024]{1,0:T(8,128)(2,1)S(1)} %constant_dynamic-update-slice_fusion, bf16[512,1024]{1,0:T(8,128)(2,1)S(1)} %pad_maximum_fusion, s32[]{:T(128)S(6)} %select_n.99), kind=kOutput, calls=%fused_computation | convolution fusion | flops 538443776 | bytes 4718596 | tf_op jit(solution)/shard_map/dot_general | solution.py:530
  129.5 2.0 %collective-permute-done.12 = bf16[128,1024]{1,0:T(8,128)(2,1)S(1)} collective-permute-done((bf16[128,1024]{1,0:T(8,128)(2,1)S(1)}, bf16[128,1024]{1,0:T(8,128)(2,1)S(1)}, u32[]{:S(2)}, u32[]{:S(2)}) %collective-permute-start.12) | collective-permute-done | bytes 262176 | tf_op jit(solution)/shard_map/ppermute | solution.py:306
  133.0 2.2 %shard_map.207 = (f32[128,1024]{1,0:T(8,128)}, f32[128,1024]{1,0:T(8,128)}) custom-call(f32[128,1024]{1,0:T(8,128)} %get-tuple-element.109.refs_0_, bf16[128,1024]{1,0:T(8,128)(2,1)} %collective-permute-done.19.refs_1_, bf16[128,1024]{1,0:T(8,128)(2,1)} %refs_2_.6, bf16[128,1024]{1,0:T(8,128)(2,1)} %refs_3_.5), custom_call_target="tpu_custom_call" | custom-call | flops 131072 | bytes 2359296 | tf_op jit(solution)/shard_map/pallas_call | solution.py:272
  (104 shorter events, 37.9 us)
Async XLA Ops:
  1.7 7.8 %collective-permute-start = (bf16[128,1024]{1,0:T(8,128)(2,1)S(1)}, bf16[128,1024]{1,0:T(8,128)(2,1)S(1)}, u32[]{:S(2)}, u32[]{:S(2)}) collective-permute-start(bf16[128,1024]{1,0:T(8,128)(2,1)S(1)} %multiply_convert_fusion.refs_1_), channel_id=1, source_target_pairs={{0,4},{4,8},{8,12},{12,16},{16,20},{20,24},{24,28},{1,5},{5,9},{9,... | collective-permute-start | bytes 786440 | tf_op jit(solution)/shard_map/ppermute | solution.py:316
  6.3 13.8 %collective-permute-start.1 = (bf16[512,1024]{1,0:T(8,128)(2,1)}, bf16[512,1024]{1,0:T(8,128)(2,1)S(1)}, u32[]{:S(2)}, u32[]{:S(2)}) collective-permute-start(bf16[512,1024]{1,0:T(8,128)(2,1)} %rest_2_.1), channel_id=1, source_target_pairs={{0,4},{4,0},{8,12},{12,8},{16,20},{20,16},{24,28},{28,24},{1,5},{5... | collective-permute-start | bytes 3145736 | tf_op jit(solution)/shard_map/ppermute | solution.py:311
  9.6 24.0 %collective-permute-start.2 = (bf16[512,1024]{1,0:T(8,128)(2,1)}, bf16[512,1024]{1,0:T(8,128)(2,1)S(1)}, u32[]{:S(2)}, u32[]{:S(2)}) collective-permute-start(bf16[512,1024]{1,0:T(8,128)(2,1)} %rest_2_.1), channel_id=1, source_target_pairs={{0,8},{4,12},{8,0},{12,4},{16,24},{20,28},{24,16},{28,20},{1,9},{5... | collective-permute-start | bytes 3145736 | tf_op jit(solution)/shard_map/ppermute | solution.py:301
  10.8 15.4 %collective-permute-start.3 = (bf16[128,1024]{1,0:T(8,128)(2,1)}, bf16[128,1024]{1,0:T(8,128)(2,1)S(1)}, u32[]{:S(2)}, u32[]{:S(2)}) collective-permute-start(bf16[128,1024]{1,0:T(8,128)(2,1)} %rest_0_), channel_id=1, source_target_pairs={{0,1},{1,0},{2,3},{3,2},{4,5},{5,4},{6,7},{7,6},{8,9},{9,8},{10,11... | collective-permute-start | bytes 786440 | tf_op jit(solution)/shard_map/ppermute | solution.py:306
  12.1 14.1 %collective-permute-start.4 = (bf16[128,1024]{1,0:T(8,128)(2,1)}, bf16[128,1024]{1,0:T(8,128)(2,1)S(1)}, u32[]{:S(2)}, u32[]{:S(2)}) collective-permute-start(bf16[128,1024]{1,0:T(8,128)(2,1)} %rest_0_), channel_id=1, source_target_pairs={{0,2},{1,3},{2,0},{3,1},{4,6},{5,7},{6,4},{7,5},{8,10},{9,11},{10,... | collective-permute-start | bytes 786440 | tf_op jit(solution)/shard_map/ppermute | solution.py:306
  14.4 16.0 %collective-permute-start.5 = (bf16[128,1024]{1,0:T(8,128)(2,1)}, bf16[128,1024]{1,0:T(8,128)(2,1)S(1)}, u32[]{:S(2)}, u32[]{:S(2)}) collective-permute-start(bf16[128,1024]{1,0:T(8,128)(2,1)} %rest_0_), channel_id=1, source_target_pairs={{0,3},{1,2},{2,1},{3,0},{4,7},{5,6},{6,5},{7,4},{8,11},{9,10},{10,... | collective-permute-start | bytes 786440 | tf_op jit(solution)/shard_map/ppermute | solution.py:306
  33.6 31.6 %collective-permute-start.7 = (bf16[512,1024]{1,0:T(8,128)(2,1)S(1)}, bf16[512,1024]{1,0:T(8,128)(2,1)S(1)}, u32[]{:S(2)}, u32[]{:S(2)}) collective-permute-start(bf16[512,1024]{1,0:T(8,128)(2,1)S(1)} %collective-permute-done.2.refs_5_.rest_4_), channel_id=1, source_target_pairs={{0,4},{4,0},{8,12},{12,8},{16,20},{20,16},{24,28},{28,24},{1,5},{5... | collective-permute-start | bytes 3145736 | tf_op jit(solution)/shard_map/ppermute | solution.py:311
  39.4 24.0 %collective-permute-start.6 = (bf16[128,2048]{1,0:T(8,128)(2,1)}, bf16[128,2048]{1,0:T(8,128)(2,1)S(1)}, u32[]{:S(2)}, u32[]{:S(2)}) collective-permute-start(bf16[128,2048]{1,0:T(8,128)(2,1)} %get-tuple-element.79), channel_id=1, source_target_pairs={{0,16},{4,20},{8,24},{12,28},{16,0},{20,4},{24,8},{28,12},{1,17},{... | collective-permute-start | bytes 1572872 | tf_op jit(solution)/shard_map/ppermute | solution.py:301
  61.9 9.9 %collective-permute-start.8 = (bf16[128,1024]{1,0:T(8,128)(2,1)}, bf16[128,1024]{1,0:T(8,128)(2,1)S(1)}, u32[]{:S(2)}, u32[]{:S(2)}) collective-permute-start(bf16[128,1024]{1,0:T(8,128)(2,1)} %get-tuple-element.83.rest_0_), channel_id=1, source_target_pairs={{0,16},{4,20},{8,24},{12,28},{16,0},{20,4},{24,8},{28,12},{1,17},{... | collective-permute-start | bytes 786440 | tf_op jit(solution)/shard_map/ppermute | solution.py:301
  65.2 21.0 %collective-permute-start.13 = (bf16[256,1024]{1,0:T(8,128)(2,1)}, bf16[256,1024]{1,0:T(8,128)(2,1)}, u32[]{:S(2)}, u32[]{:S(2)}) collective-permute-start(bf16[256,1024]{1,0:T(8,128)(2,1)} %pad_maximum_fusion.1), channel_id=1, source_target_pairs={{0,8},{4,12},{8,0},{12,4},{16,24},{20,28},{24,16},{28,20},{1,9},{5... | collective-permute-start | bytes 1572872 | tf_op jit(solution)/shard_map/ppermute | solution.py:301
  70.4 7.8 %collective-permute-start.9 = (bf16[128,1024]{1,0:T(8,128)(2,1)}, bf16[128,1024]{1,0:T(8,128)(2,1)S(1)}, u32[]{:S(2)}, u32[]{:S(2)}) collective-permute-start(bf16[128,1024]{1,0:T(8,128)(2,1)} %get-tuple-element.86), channel_id=1, source_target_pairs={{0,16},{4,20},{8,24},{12,28},{16,0},{20,4},{24,8},{28,12},{1,17},{... | collective-permute-start | bytes 786440 | tf_op jit(solution)/shard_map/ppermute | solution.py:301
  77.1 12.4 %collective-permute-start.14 = (bf16[256,1024]{1,0:T(8,128)(2,1)S(1)}, bf16[256,1024]{1,0:T(8,128)(2,1)S(1)}, u32[]{:S(2)}, u32[]{:S(2)}) collective-permute-start(bf16[256,1024]{1,0:T(8,128)(2,1)S(1)} %pad_maximum_fusion.2), channel_id=1, source_target_pairs={{0,8},{4,12},{8,0},{12,4},{16,24},{20,28},{24,16},{28,20},{1,9},{5... | collective-permute-start | bytes 1572872 | tf_op jit(solution)/shard_map/ppermute | solution.py:301
  78.3 12.5 %collective-permute-start.10 = (bf16[128,2048]{1,0:T(8,128)(2,1)}, bf16[128,2048]{1,0:T(8,128)(2,1)S(1)}, u32[]{:S(2)}, u32[]{:S(2)}) collective-permute-start(bf16[128,2048]{1,0:T(8,128)(2,1)} %get-tuple-element.87), channel_id=1, source_target_pairs={{0,16},{4,20},{8,24},{12,28},{16,0},{20,4},{24,8},{28,12},{1,17},{... | collective-permute-start | bytes 1572872 | tf_op jit(solution)/shard_map/ppermute | solution.py:301
  90.7 12.2 %collective-permute-start.18 = (f32[16,1024]{1,0:T(8,128)S(1)}, f32[16,1024]{1,0:T(8,128)S(1)}, u32[]{:S(2)}, u32[]{:S(2)}) collective-permute-start(f32[16,1024]{1,0:T(8,128)S(1)} %add_select_fusion.1), channel_id=1, source_target_pairs={{0,24},{4,28},{8,16},{12,20},{16,8},{20,12},{24,0},{28,4},{1,25},{... | collective-permute-start | bytes 196616 | tf_op jit(solution)/shard_map/ppermute | solution.py:301
  91.9 11.1 %collective-permute-start.17 = (f32[16,1024]{1,0:T(8,128)S(1)}, f32[16,1024]{1,0:T(8,128)S(1)}, u32[]{:S(2)}, u32[]{:S(2)}) collective-permute-start(f32[16,1024]{1,0:T(8,128)S(1)} %add_select_fusion.1), channel_id=1, source_target_pairs={{0,16},{4,20},{8,24},{12,28},{16,0},{20,4},{24,8},{28,12},{1,17},{... | collective-permute-start | bytes 196616 | tf_op jit(solution)/shard_map/ppermute | solution.py:301
  93.2 9.7 %collective-permute-start.16 = (f32[16,1024]{1,0:T(8,128)S(1)}, f32[16,1024]{1,0:T(8,128)S(1)}, u32[]{:S(2)}, u32[]{:S(2)}) collective-permute-start(f32[16,1024]{1,0:T(8,128)S(1)} %add_select_fusion.1), channel_id=1, source_target_pairs={{0,8},{4,12},{8,0},{12,4},{16,24},{20,28},{24,16},{28,20},{1,9},{5... | collective-permute-start | bytes 196616 | tf_op jit(solution)/shard_map/ppermute | solution.py:301
  95.1 28.0 %collective-permute-start.21 = (bf16[512,1024]{1,0:T(8,128)(2,1)}, bf16[512,1024]{1,0:T(8,128)(2,1)}, u32[]{:S(2)}, u32[]{:S(2)}) collective-permute-start(bf16[512,1024]{1,0:T(8,128)(2,1)} %convolution_convert_fusion), channel_id=1, source_target_pairs={{0,4},{4,0},{8,12},{12,8},{16,20},{20,16},{24,28},{28,24},{1,5},{5... | collective-permute-start | bytes 3145736 | tf_op jit(solution)/shard_map/ppermute | solution.py:311
  100.4 15.1 %collective-permute-start.11 = (bf16[256,1024]{1,0:T(8,128)(2,1)}, bf16[256,1024]{1,0:T(8,128)(2,1)S(1)}, u32[]{:S(2)}, u32[]{:S(2)}) collective-permute-start(bf16[256,1024]{1,0:T(8,128)(2,1)} %get-tuple-element.89), channel_id=1, source_target_pairs={{0,1},{1,0},{2,3},{3,2},{4,5},{5,4},{6,7},{7,6},{8,9},{9,8},{10,11... | collective-permute-start | bytes 1572872 | tf_op jit(solution)/shard_map/ppermute | solution.py:306
  112.3 17.1 %collective-permute-start.24 = (bf16[64,1024]{1,0:T(8,128)(2,1)S(1)}, bf16[64,1024]{1,0:T(8,128)(2,1)S(1)}, u32[]{:S(2)}, u32[]{:S(2)}) collective-permute-start(bf16[64,1024]{1,0:T(8,128)(2,1)S(1)} %fusion.2), channel_id=1, source_target_pairs={{0,24},{4,28},{8,16},{12,20},{16,8},{20,12},{24,0},{28,4},{1,25},{... | collective-permute-start | bytes 393224 | tf_op jit(solution)/shard_map/ppermute | solution.py:301
  113.5 15.8 %collective-permute-start.23 = (bf16[64,1024]{1,0:T(8,128)(2,1)S(1)}, bf16[64,1024]{1,0:T(8,128)(2,1)S(1)}, u32[]{:S(2)}, u32[]{:S(2)}) collective-permute-start(bf16[64,1024]{1,0:T(8,128)(2,1)S(1)} %fusion.2), channel_id=1, source_target_pairs={{0,16},{4,20},{8,24},{12,28},{16,0},{20,4},{24,8},{28,12},{1,17},{... | collective-permute-start | bytes 393224 | tf_op jit(solution)/shard_map/ppermute | solution.py:301
  114.8 14.6 %collective-permute-start.22 = (bf16[64,1024]{1,0:T(8,128)(2,1)S(1)}, bf16[64,1024]{1,0:T(8,128)(2,1)S(1)}, u32[]{:S(2)}, u32[]{:S(2)}) collective-permute-start(bf16[64,1024]{1,0:T(8,128)(2,1)S(1)} %fusion.2), channel_id=1, source_target_pairs={{0,8},{4,12},{8,0},{12,4},{16,24},{20,28},{24,16},{28,20},{1,9},{5... | collective-permute-start | bytes 393224 | tf_op jit(solution)/shard_map/ppermute | solution.py:301
  117.7 13.8 %collective-permute-start.12 = (bf16[128,1024]{1,0:T(8,128)(2,1)S(1)}, bf16[128,1024]{1,0:T(8,128)(2,1)S(1)}, u32[]{:S(2)}, u32[]{:S(2)}) collective-permute-start(bf16[128,1024]{1,0:T(8,128)(2,1)S(1)} %slice.13), channel_id=1, source_target_pairs={{0,2},{1,3},{2,0},{3,1},{4,6},{5,7},{6,4},{7,5},{8,10},{9,11},{10,... | collective-permute-start | bytes 786440 | tf_op jit(solution)/shard_map/ppermute | solution.py:306
  123.1 9.9 %collective-permute-start.19 = (bf16[128,1024]{1,0:T(8,128)(2,1)}, bf16[128,1024]{1,0:T(8,128)(2,1)}, u32[]{:S(2)}, u32[]{:S(2)}) collective-permute-start(bf16[128,1024]{1,0:T(8,128)(2,1)} %get-tuple-element.110), channel_id=1, source_target_pairs={{4,0},{8,4},{12,8},{16,12},{20,16},{24,20},{28,24},{5,1},{9,5},{13... | collective-permute-start | bytes 786440 | tf_op jit(solution)/shard_map/ppermute | solution.py:316
  131.5 4.5 %collective-permute-start.25 = (f32[64,1024]{1,0:T(8,128)S(1)}, f32[64,1024]{1,0:T(8,128)S(1)}, u32[]{:S(2)}, u32[]{:S(2)}) collective-permute-start(f32[64,1024]{1,0:T(8,128)S(1)} %add_multiply_fusion.1), channel_id=1, source_target_pairs={{0,4},{4,0},{8,12},{12,8},{16,20},{20,16},{24,28},{28,24},{1,5},{5... | collective-permute-start | bytes 786440 | tf_op jit(solution)/shard_map/ppermute | solution.py:311
  (23 other events, 189.3 us)

commit v17 on v16

--- a/solution.py
+++ b/solution.py
@@ -580,7 +580,7 @@
     chip_half = (own_half + core_swap(far_half)).astype(BF16)
     everywhere = [after(chip_half, prev_product, grad_weight)] + [chip_swap(chip_half, s) for s in range(1, chips)]
     plane_half = pair_sum([part.astype(F32) for part in everywhere]) * grad_scale
-    other_half = core_swap(after(plane_half, arrived_out))
+    other_half = core_swap(after(plane_half, arrived_out, grad_key_mr))
     grad_taps = jnp.where(
         core == 0,
         jnp.concatenate([plane_half, other_half], axis=0),

time: 138 us -> 138 us (level)
  starting transfers between devices: 39.7 us -> 38.3 us
    ppermute x2, waiting for transfers between devices: 3.22 us -> 5.57 us  [shifted(): lax.ppermute(x, 'ctx', [(i, i + by) for i in range(size) if 0 <= i + by <...]
    ppermute x5, waiting for transfers between devices: 6.72 us -> 4.66 us  [line_swap(): return lax.ppermute(x, 'fsdp', [(i, i ^ by) for i in range(size)])]
    ppermute x6, starting transfers between devices: 12.3 us -> 10.9 us  [core_swap(): return lax.ppermute(x, 'ctx', [(i, i ^ 1) for i in range(size)])]
    unnamed x44 -> x46, local copies, waits for them, and re-layouts: 4.26 us -> 4.99 us
  transfers between devices with their start and end apart: 26 -> 26, of which waited for: 8 -> 9; matrix products, arithmetic and copies ran while one was open for 12% -> 12% of each run, Pallas kernels for 30% -> 30%
where the time goes in v17:
time: 138 us; the launch traced here: 137 us
  Pallas kernels  40.9 us (30%)
  starting transfers between devices  38.3 us (28%)
  blocking collectives  18.7 us (14%)
  waiting for transfers between devices  15.7 us (11%)
  other arithmetic  10 us (7%)
  local copies, waits for them, and re-layouts  7.63 us (6%)
  matrix products  5.02 us (4%)
    pallas_call x8, Pallas kernels, run(): pl.pallas_call(body_by_tiles, grid=(columns // block,), in_specs=in_specs...  31.6 us
    all_gather x1, blocking collectives, shards(): lax.all_gather(after(ends, beside, *cot_parts[:1]), 'ctx')  18.7 us
    ppermute x13, starting transfers between devices, chip_swap(): return lax.ppermute(x, 'ctx', [(i, i ^ 2 * by) for i in range(size)])  11.4 us
    ppermute x6, starting transfers between devices, core_swap(): return lax.ppermute(x, 'ctx', [(i, i ^ 1) for i in range(size)])  10.9 us
    pallas_call x3, Pallas kernels, run_once(): pl.pallas_call(body, grid=(1,), in_specs=[pl.BlockSpec(memory_space=pltpu...  9.24 us
    ppermute x5, starting transfers between devices, line_swap(): return lax.ppermute(x, 'fsdp', [(i, i ^ by) for i in range(size)])  8.48 us
    ppermute x2, starting transfers between devices, shifted(): lax.ppermute(x, 'ctx', [(i, i + by) for i in range(size) if 0 <= i + by <...  7.48 us
    ppermute x2, waiting for transfers between devices, shifted(): lax.ppermute(x, 'ctx', [(i, i + by) for i in range(size) if 0 <= i + by <...  5.57 us
  transfers between devices with their start and end apart: 26, of which 9 were waited for; matrix products, arithmetic and copies ran while one was open for 12% of the time, Pallas kernels for 30%

profile of v17, /device:TPU:1, one launch (start us, length us, event | category | flops | bytes accessed | tf_op | source)
XLA Modules:
  0.0 137.2 jit_solution(1785536401577260418)
XLA Ops:
  1.7 4.5 %collective-permute-start = (bf16[128,1024]{1,0:T(8,128)(2,1)S(1)}, bf16[128,1024]{1,0:T(8,128)(2,1)S(1)}, u32[]{:S(2)}, u32[]{:S(2)}) collective-permute-start(bf16[128,1024]{1,0:T(8,128)(2,1)S(1)} %multiply_convert_fusion.refs_1_), channel_id=1, source_target_pairs={{0,4},{4,8},{8,12},{12,16},{16,20},{20,24},{24,28},{1,5},{5,9},{9,... | collective-permute-start | bytes 786440 | tf_op jit(solution)/shard_map/ppermute | solution.py:316
  6.3 3.2 %collective-permute-done.refs_0_ = bf16[128,1024]{1,0:T(8,128)(2,1)S(1)} collective-permute-done((bf16[128,1024]{1,0:T(8,128)(2,1)S(1)}, bf16[128,1024]{1,0:T(8,128)(2,1)S(1)}, u32[]{:S(2)}, u32[]{:S(2)}) %collective-permute-start) | collective-permute-done | bytes 262176 | tf_op jit(solution)/shard_map/ppermute | solution.py:316
  12.1 2.3 %collective-permute-start.4 = (bf16[128,1024]{1,0:T(8,128)(2,1)}, bf16[128,1024]{1,0:T(8,128)(2,1)S(1)}, u32[]{:S(2)}, u32[]{:S(2)}) collective-permute-start(bf16[128,1024]{1,0:T(8,128)(2,1)} %rest_0_), channel_id=1, source_target_pairs={{0,2},{1,3},{2,0},{3,1},{4,6},{5,7},{6,4},{7,5},{8,10},{9,11},{10,... | collective-permute-start | bytes 786440 | tf_op jit(solution)/shard_map/ppermute | solution.py:306
  16.0 3.4 %shard_map.197 = (f32[256,1024]{1,0:T(8,128)}, f32[256,1024]{1,0:T(8,128)}) custom-call(f32[128,1024]{1,0:T(8,128)} %refs_0_.1, f32[16,1024]{1,0:T(8,128)} %get-tuple-element.127.refs_1_.refs_6_.refs_3_.refs_2_, f32[16,1024]{1,0:T(8,128)} %get-tuple-element.123.refs_2_.refs_4_, f32[1,1024]{1,0:T(1,128)} %bitcast.22, ...), custom_call_target="tpu_custom_call" | custom-call | tf_op jit(solution)/shard_map/pallas_call | solution.py:272
  20.1 6.1 %shard_map.198 = (f32[256,1024]{1,0:T(8,128)}, f32[128,1024]{1,0:T(8,128)}, bf16[128,1024]{1,0:T(8,128)(2,1)}, f32[128,1024]{1,0:T(8,128)}, f32[16,1024]{1,0:T(8,128)}) custom-call(bf16[128,1024]{1,0:T(8,128)(2,1)} %copy-done.20, bf16[128,1024]{1,0:T(8,128)(2,1)} %copy-done.8, bf16[128,1024]{1,0:T(8,128)(2,1)} %refs_6_.2, bf16[128,1024]{1,0:T(8,128)(2,1)} %refs_5_.2, ...), custom_call_target="tpu_custom_call" | custom-call | tf_op jit(solution)/shard_map/pallas_call | solution.py:272
  26.2 4.2 %collective-permute-done.5.rest_3_ = bf16[128,1024]{1,0:T(8,128)(2,1)S(1)} collective-permute-done((bf16[128,1024]{1,0:T(8,128)(2,1)}, bf16[128,1024]{1,0:T(8,128)(2,1)S(1)}, u32[]{:S(2)}, u32[]{:S(2)}) %collective-permute-start.5) | collective-permute-done | bytes 262176 | tf_op jit(solution)/shard_map/ppermute | solution.py:306
  31.1 2.3 %shard_map.199 = (bf16[128,2048]{1,0:T(8,128)(2,1)}, bf16[128,2048]{1,0:T(8,128)(2,1)}) custom-call(s32[16]{0:T(128)} %stack.49.starts.refs_0_, bf16[128,1024]{1,0:T(8,128)(2,1)} %rest_0_, bf16[128,1024]{1,0:T(8,128)(2,1)} %copy-done.15, bf16[128,1024]{1,0:T(8,128)(2,1)} %copy-done.16, bf16[128,1024]{1,0:T(8,128)(2,1)} %copy-done.17), custom_call_target="tpu_custom_call" | custom-call | tf_op jit(solution)/shard_map/pallas_call | solution.py:287
  33.6 5.8 %collective-permute-start.7 = (bf16[512,1024]{1,0:T(8,128)(2,1)S(1)}, bf16[512,1024]{1,0:T(8,128)(2,1)S(1)}, u32[]{:S(2)}, u32[]{:S(2)}) collective-permute-start(bf16[512,1024]{1,0:T(8,128)(2,1)S(1)} %collective-permute-done.2.refs_5_.rest_4_), channel_id=1, source_target_pairs={{0,4},{4,0},{8,12},{12,8},{16,20},{20,16},{24,28},{28,24},{1,5},{5... | collective-permute-start | bytes 3145736 | tf_op jit(solution)/shard_map/ppermute | solution.py:311
  40.4 18.7 %all-gather.refs_5_ = f32[128,1024]{1,0:T(8,128)} all-gather(f32[16,1024]{1,0:T(8,128)} %get-tuple-element.76), channel_id=2, replica_groups=mesh['ctx'=8,'fsdp'=4] {'ctx'}, dimensions={0}, use_global_device_ids=true | all-gather | bytes 589824 | tf_op jit(solution)/shard_map/all_gather | solution.py:455
  59.1 2.8 %shard_map.200 = (f32[128,1024]{1,0:T(8,128)}, bf16[128,1024]{1,0:T(8,128)(2,1)}) custom-call(f32[8]{0:T(128)} %subtract_convert_fusion.refs_0_, f32[128,1024]{1,0:T(8,128)} %get-tuple-element.67.refs_1_, bf16[128,1024]{1,0:T(8,128)(2,1)} %refs_1_.1, f32[16,1024]{1,0:T(8,128)} %get-tuple-element.127.refs_1_.refs_6_.refs_3_.refs_2_, ...), custom_call_target="tpu_custom_call" | custom-call | tf_op jit(solution)/shard_map/pallas_call | solution.py:272
  66.2 4.2 %shard_map.201 = (f32[128,1024]{1,0:T(8,128)}, bf16[128,1024]{1,0:T(8,128)(2,1)}) custom-call(s32[16]{0:T(128)} %stack.49.starts.refs_0_, bf16[128,2048]{1,0:T(8,128)(2,1)} %get-tuple-element.78.refs_1_, bf16[128,2048]{1,0:T(8,128)(2,1)} %copy-done.7, bf16[512,1024]{1,0:T(8,128)(2,1)} %rest_2_.1, bf16[512,1024]{1,0:T(8,128)(2,1)} %copy-done, ...), custom_call_target="tpu_custom_call" | custom-call | flops 1073741824 | bytes 6029376 | tf_op jit(solution)/shard_map/pallas_call | solution.py:272
  72.6 4.6 %shard_map.202 = (bf16[128,2048]{1,0:T(8,128)(2,1)}, bf16[128,2048]{1,0:T(8,128)(2,1)}) custom-call(s32[16]{0:T(128)} %stack.49.starts.refs_0_, bf16[128,1024]{1,0:T(8,128)(2,1)} %get-tuple-element.83.rest_0_, bf16[128,1024]{1,0:T(8,128)(2,1)} %copy-done.5, bf16[512,1024]{1,0:T(8,128)(2,1)} %rest_2_.1, bf16[512,1024]{1,0:T(8,128)(2,1)} %copy-done, ...), custom_call_target="tpu_custom_call" | custom-call | tf_op jit(solution)/shard_map/pallas_call | solution.py:287
  79.7 4.8 %shard_map.204 = (f32[128,1024]{1,0:T(8,128)}, f32[16,1024]{1,0:T(8,128)}, f32[128,1024]{1,0:T(8,128)}) custom-call(f32[128,1024]{1,0:T(8,128)} %get-tuple-element.90.refs_0_, bf16[128,1024]{1,0:T(8,128)(2,1)} %refs_1_.1, f32[16,1024]{1,0:T(8,128)} %get-tuple-element.127.refs_1_.refs_6_.refs_3_.refs_2_, f32[128,1024]{1,0:T(8,128)} %get-tuple-element.91.refs_3_, ...), custom_call_target="tpu_custom_call" | custom-call | flops 536870912 | bytes 4456448 | tf_op jit(solution)/shard_map/pallas_call | solution.py:272
  87.4 2.2 %collective-permute-done.14 = bf16[256,1024]{1,0:T(8,128)(2,1)S(1)} collective-permute-done((bf16[256,1024]{1,0:T(8,128)(2,1)S(1)}, bf16[256,1024]{1,0:T(8,128)(2,1)S(1)}, u32[]{:S(2)}, u32[]{:S(2)}) %collective-permute-start.14) | collective-permute-done | bytes 524320 | tf_op jit(solution)/shard_map/ppermute | solution.py:301
  95.1 3.0 %collective-permute-start.21 = (bf16[512,1024]{1,0:T(8,128)(2,1)}, bf16[512,1024]{1,0:T(8,128)(2,1)}, u32[]{:S(2)}, u32[]{:S(2)}) collective-permute-start(bf16[512,1024]{1,0:T(8,128)(2,1)} %convolution_convert_fusion), channel_id=1, source_target_pairs={{0,4},{4,0},{8,12},{12,8},{16,20},{20,16},{24,28},{28,24},{1,5},{5... | collective-permute-start | bytes 3145736 | tf_op jit(solution)/shard_map/ppermute | solution.py:311
  98.1 2.3 %shard_map.203 = (bf16[256,1024]{1,0:T(8,128)(2,1)}, bf16[256,1024]{1,0:T(8,128)(2,1)}) custom-call(s32[16]{0:T(128)} %stack.49.starts.refs_0_, bf16[128,2048]{1,0:T(8,128)(2,1)} %get-tuple-element.84.rest_0_, bf16[128,2048]{1,0:T(8,128)(2,1)} %copy-done.11), custom_call_target="tpu_custom_call" | custom-call | tf_op jit(solution)/shard_map/pallas_call | solution.py:287
  100.5 2.6 %collective-permute-start.11 = (bf16[256,1024]{1,0:T(8,128)(2,1)}, bf16[256,1024]{1,0:T(8,128)(2,1)S(1)}, u32[]{:S(2)}, u32[]{:S(2)}) collective-permute-start(bf16[256,1024]{1,0:T(8,128)(2,1)} %get-tuple-element.89), channel_id=1, source_target_pairs={{0,1},{1,0},{2,3},{3,2},{4,5},{5,4},{6,7},{7,6},{8,9},{9,8},{10,11... | collective-permute-start | bytes 1572872 | tf_op jit(solution)/shard_map/ppermute | solution.py:306
  103.7 5.1 %shard_map.205 = (f32[128,1024]{1,0:T(8,128)}, f32[128,1024]{1,0:T(8,128)}, f32[256,1024]{1,0:T(8,128)}, f32[128,1024]{1,0:T(8,128)}) custom-call(f32[128,1024]{1,0:T(8,128)} %get-tuple-element.97.refs_0_, f32[16,1024]{1,0:T(8,128)} %get-tuple-element.127.refs_1_.refs_6_.refs_3_.refs_2_, f32[16,1024]{1,0:T(8,128)} %get-tuple-element.123.refs_2_.refs_4_, ...), custom_call_target="tpu_custom_call" | custom-call | flops 536870912 | bytes 6160384 | tf_op jit(solution)/shard_map/pallas_call | solution.py:272
  117.7 2.3 %collective-permute-start.12 = (bf16[128,1024]{1,0:T(8,128)(2,1)S(1)}, bf16[128,1024]{1,0:T(8,128)(2,1)S(1)}, u32[]{:S(2)}, u32[]{:S(2)}) collective-permute-start(bf16[128,1024]{1,0:T(8,128)(2,1)S(1)} %slice.13), channel_id=1, source_target_pairs={{0,2},{1,3},{2,0},{3,1},{4,6},{5,7},{6,4},{7,5},{8,10},{9,11},{10,... | collective-permute-start | bytes 786440 | tf_op jit(solution)/shard_map/ppermute | solution.py:306
  120.0 3.1 %shard_map.206 = (f32[128,1024]{1,0:T(8,128)}, bf16[128,1024]{1,0:T(8,128)(2,1)}) custom-call(f32[256,1024]{1,0:T(8,128)} %get-tuple-element.108.refs_0_, f32[256,1024]{1,0:T(8,128)} %get-tuple-element.65.refs_4_.refs_1_, bf16[256,768]{1,0:T(8,128)(2,1)} %constant.89.clone.refs_8_.refs_6_.refs_2_), custom_call_target="tpu_custom_call" | custom-call | flops 402653184 | bytes 3276800 | tf_op jit(solution)/shard_map/pallas_call | solution.py:272
  123.1 3.0 %collective-permute-start.19 = (bf16[128,1024]{1,0:T(8,128)(2,1)}, bf16[128,1024]{1,0:T(8,128)(2,1)S(1)}, u32[]{:S(2)}, u32[]{:S(2)}) collective-permute-start(bf16[128,1024]{1,0:T(8,128)(2,1)} %get-tuple-element.110), channel_id=1, source_target_pairs={{4,0},{8,4},{12,8},{16,12},{20,16},{24,20},{28,24},{5,1},{9,5},{13... | collective-permute-start | bytes 786440 | tf_op jit(solution)/shard_map/ppermute | solution.py:316
  126.1 3.3 %add_multiply_fusion = f32[512,1024]{1,0:T(8,128)} fusion(bf16[512,1024]{1,0:T(8,128)(2,1)} %collective-permute-done.21, bf16[512,1024]{1,0:T(8,128)(2,1)S(1)} %constant_dynamic-update-slice_fusion, bf16[512,1024]{1,0:T(8,128)(2,1)S(1)} %pad_maximum_fusion, s32[]{:T(128)S(6)} %select_n.99), kind=kOutput, calls=%fused_computation | convolution fusion | flops 538443776 | bytes 4718596 | tf_op jit(solution)/shard_map/dot_general | solution.py:530
  129.4 2.4 %collective-permute-done.19.refs_1_ = bf16[128,1024]{1,0:T(8,128)(2,1)S(1)} collective-permute-done((bf16[128,1024]{1,0:T(8,128)(2,1)}, bf16[128,1024]{1,0:T(8,128)(2,1)S(1)}, u32[]{:S(2)}, u32[]{:S(2)}) %collective-permute-start.19) | collective-permute-done | bytes 262176 | tf_op jit(solution)/shard_map/ppermute | solution.py:316
  132.5 2.2 %shard_map.207 = (f32[128,1024]{1,0:T(8,128)}, f32[128,1024]{1,0:T(8,128)}) custom-call(f32[128,1024]{1,0:T(8,128)} %get-tuple-element.109.refs_0_, bf16[128,1024]{1,0:T(8,128)(2,1)} %copy-done.14, bf16[128,1024]{1,0:T(8,128)(2,1)} %refs_2_.6, bf16[128,1024]{1,0:T(8,128)(2,1)} %refs_3_.5), custom_call_target="tpu_custom_call" | custom-call | flops 131072 | bytes 2359296 | tf_op jit(solution)/shard_map/pallas_call | solution.py:272
  (106 shorter events, 37.9 us)
Async XLA Ops:
  1.7 7.8 %collective-permute-start = (bf16[128,1024]{1,0:T(8,128)(2,1)S(1)}, bf16[128,1024]{1,0:T(8,128)(2,1)S(1)}, u32[]{:S(2)}, u32[]{:S(2)}) collective-permute-start(bf16[128,1024]{1,0:T(8,128)(2,1)S(1)} %multiply_convert_fusion.refs_1_), channel_id=1, source_target_pairs={{0,4},{4,8},{8,12},{12,16},{16,20},{20,24},{24,28},{1,5},{5,9},{9,... | collective-permute-start | bytes 786440 | tf_op jit(solution)/shard_map/ppermute | solution.py:316
  6.3 13.8 %collective-permute-start.1 = (bf16[512,1024]{1,0:T(8,128)(2,1)}, bf16[512,1024]{1,0:T(8,128)(2,1)S(1)}, u32[]{:S(2)}, u32[]{:S(2)}) collective-permute-start(bf16[512,1024]{1,0:T(8,128)(2,1)} %rest_2_.1), channel_id=1, source_target_pairs={{0,4},{4,0},{8,12},{12,8},{16,20},{20,16},{24,28},{28,24},{1,5},{5... | collective-permute-start | bytes 3145736 | tf_op jit(solution)/shard_map/ppermute | solution.py:311
  9.6 24.0 %collective-permute-start.2 = (bf16[512,1024]{1,0:T(8,128)(2,1)}, bf16[512,1024]{1,0:T(8,128)(2,1)S(1)}, u32[]{:S(2)}, u32[]{:S(2)}) collective-permute-start(bf16[512,1024]{1,0:T(8,128)(2,1)} %rest_2_.1), channel_id=1, source_target_pairs={{0,8},{4,12},{8,0},{12,4},{16,24},{20,28},{24,16},{28,20},{1,9},{5... | collective-permute-start | bytes 3145736 | tf_op jit(solution)/shard_map/ppermute | solution.py:301
  10.8 15.4 %collective-permute-start.3 = (bf16[128,1024]{1,0:T(8,128)(2,1)}, bf16[128,1024]{1,0:T(8,128)(2,1)S(1)}, u32[]{:S(2)}, u32[]{:S(2)}) collective-permute-start(bf16[128,1024]{1,0:T(8,128)(2,1)} %rest_0_), channel_id=1, source_target_pairs={{0,1},{1,0},{2,3},{3,2},{4,5},{5,4},{6,7},{7,6},{8,9},{9,8},{10,11... | collective-permute-start | bytes 786440 | tf_op jit(solution)/shard_map/ppermute | solution.py:306
  12.1 14.2 %collective-permute-start.4 = (bf16[128,1024]{1,0:T(8,128)(2,1)}, bf16[128,1024]{1,0:T(8,128)(2,1)S(1)}, u32[]{:S(2)}, u32[]{:S(2)}) collective-permute-start(bf16[128,1024]{1,0:T(8,128)(2,1)} %rest_0_), channel_id=1, source_target_pairs={{0,2},{1,3},{2,0},{3,1},{4,6},{5,7},{6,4},{7,5},{8,10},{9,11},{10,... | collective-permute-start | bytes 786440 | tf_op jit(solution)/shard_map/ppermute | solution.py:306
  14.4 16.0 %collective-permute-start.5 = (bf16[128,1024]{1,0:T(8,128)(2,1)}, bf16[128,1024]{1,0:T(8,128)(2,1)S(1)}, u32[]{:S(2)}, u32[]{:S(2)}) collective-permute-start(bf16[128,1024]{1,0:T(8,128)(2,1)} %rest_0_), channel_id=1, source_target_pairs={{0,3},{1,2},{2,1},{3,0},{4,7},{5,6},{6,5},{7,4},{8,11},{9,10},{10,... | collective-permute-start | bytes 786440 | tf_op jit(solution)/shard_map/ppermute | solution.py:306
  33.6 31.6 %collective-permute-start.7 = (bf16[512,1024]{1,0:T(8,128)(2,1)S(1)}, bf16[512,1024]{1,0:T(8,128)(2,1)S(1)}, u32[]{:S(2)}, u32[]{:S(2)}) collective-permute-start(bf16[512,1024]{1,0:T(8,128)(2,1)S(1)} %collective-permute-done.2.refs_5_.rest_4_), channel_id=1, source_target_pairs={{0,4},{4,0},{8,12},{12,8},{16,20},{20,16},{24,28},{28,24},{1,5},{5... | collective-permute-start | bytes 3145736 | tf_op jit(solution)/shard_map/ppermute | solution.py:311
  39.4 24.0 %collective-permute-start.6 = (bf16[128,2048]{1,0:T(8,128)(2,1)}, bf16[128,2048]{1,0:T(8,128)(2,1)S(1)}, u32[]{:S(2)}, u32[]{:S(2)}) collective-permute-start(bf16[128,2048]{1,0:T(8,128)(2,1)} %get-tuple-element.79), channel_id=1, source_target_pairs={{0,16},{4,20},{8,24},{12,28},{16,0},{20,4},{24,8},{28,12},{1,17},{... | collective-permute-start | bytes 1572872 | tf_op jit(solution)/shard_map/ppermute | solution.py:301
  61.9 10.0 %collective-permute-start.8 = (bf16[128,1024]{1,0:T(8,128)(2,1)}, bf16[128,1024]{1,0:T(8,128)(2,1)S(1)}, u32[]{:S(2)}, u32[]{:S(2)}) collective-permute-start(bf16[128,1024]{1,0:T(8,128)(2,1)} %get-tuple-element.83.rest_0_), channel_id=1, source_target_pairs={{0,16},{4,20},{8,24},{12,28},{16,0},{20,4},{24,8},{28,12},{1,17},{... | collective-permute-start | bytes 786440 | tf_op jit(solution)/shard_map/ppermute | solution.py:301
  65.2 21.0 %collective-permute-start.13 = (bf16[256,1024]{1,0:T(8,128)(2,1)}, bf16[256,1024]{1,0:T(8,128)(2,1)}, u32[]{:S(2)}, u32[]{:S(2)}) collective-permute-start(bf16[256,1024]{1,0:T(8,128)(2,1)} %pad_maximum_fusion.1), channel_id=1, source_target_pairs={{0,8},{4,12},{8,0},{12,4},{16,24},{20,28},{24,16},{28,20},{1,9},{5... | collective-permute-start | bytes 1572872 | tf_op jit(solution)/shard_map/ppermute | solution.py:301
  70.4 7.9 %collective-permute-start.9 = (bf16[128,1024]{1,0:T(8,128)(2,1)}, bf16[128,1024]{1,0:T(8,128)(2,1)S(1)}, u32[]{:S(2)}, u32[]{:S(2)}) collective-permute-start(bf16[128,1024]{1,0:T(8,128)(2,1)} %get-tuple-element.86), channel_id=1, source_target_pairs={{0,16},{4,20},{8,24},{12,28},{16,0},{20,4},{24,8},{28,12},{1,17},{... | collective-permute-start | bytes 786440 | tf_op jit(solution)/shard_map/ppermute | solution.py:301
  77.2 12.4 %collective-permute-start.14 = (bf16[256,1024]{1,0:T(8,128)(2,1)S(1)}, bf16[256,1024]{1,0:T(8,128)(2,1)S(1)}, u32[]{:S(2)}, u32[]{:S(2)}) collective-permute-start(bf16[256,1024]{1,0:T(8,128)(2,1)S(1)} %pad_maximum_fusion.2), channel_id=1, source_target_pairs={{0,8},{4,12},{8,0},{12,4},{16,24},{20,28},{24,16},{28,20},{1,9},{5... | collective-permute-start | bytes 1572872 | tf_op jit(solution)/shard_map/ppermute | solution.py:301
  78.3 12.5 %collective-permute-start.10 = (bf16[128,2048]{1,0:T(8,128)(2,1)}, bf16[128,2048]{1,0:T(8,128)(2,1)S(1)}, u32[]{:S(2)}, u32[]{:S(2)}) collective-permute-start(bf16[128,2048]{1,0:T(8,128)(2,1)} %get-tuple-element.87), channel_id=1, source_target_pairs={{0,16},{4,20},{8,24},{12,28},{16,0},{20,4},{24,8},{28,12},{1,17},{... | collective-permute-start | bytes 1572872 | tf_op jit(solution)/shard_map/ppermute | solution.py:301
  84.6 2.8 %collective-permute-start.15 = (f32[16,1024]{1,0:T(8,128)}, f32[16,1024]{1,0:T(8,128)S(1)}, u32[]{:S(2)}, u32[]{:S(2)}) collective-permute-start(f32[16,1024]{1,0:T(8,128)} %get-tuple-element.93), channel_id=1, source_target_pairs={{0,4},{4,0},{8,12},{12,8},{16,20},{20,16},{24,28},{28,24},{1,5},{5... | collective-permute-start | bytes 196616 | tf_op jit(solution)/shard_map/ppermute | solution.py:311
  90.7 12.3 %collective-permute-start.18 = (f32[16,1024]{1,0:T(8,128)S(1)}, f32[16,1024]{1,0:T(8,128)S(1)}, u32[]{:S(2)}, u32[]{:S(2)}) collective-permute-start(f32[16,1024]{1,0:T(8,128)S(1)} %add_select_fusion.1), channel_id=1, source_target_pairs={{0,24},{4,28},{8,16},{12,20},{16,8},{20,12},{24,0},{28,4},{1,25},{... | collective-permute-start | bytes 196616 | tf_op jit(solution)/shard_map/ppermute | solution.py:301
  91.9 11.1 %collective-permute-start.17 = (f32[16,1024]{1,0:T(8,128)S(1)}, f32[16,1024]{1,0:T(8,128)S(1)}, u32[]{:S(2)}, u32[]{:S(2)}) collective-permute-start(f32[16,1024]{1,0:T(8,128)S(1)} %add_select_fusion.1), channel_id=1, source_target_pairs={{0,16},{4,20},{8,24},{12,28},{16,0},{20,4},{24,8},{28,12},{1,17},{... | collective-permute-start | bytes 196616 | tf_op jit(solution)/shard_map/ppermute | solution.py:301
  93.3 9.8 %collective-permute-start.16 = (f32[16,1024]{1,0:T(8,128)S(1)}, f32[16,1024]{1,0:T(8,128)S(1)}, u32[]{:S(2)}, u32[]{:S(2)}) collective-permute-start(f32[16,1024]{1,0:T(8,128)S(1)} %add_select_fusion.1), channel_id=1, source_target_pairs={{0,8},{4,12},{8,0},{12,4},{16,24},{20,28},{24,16},{28,20},{1,9},{5... | collective-permute-start | bytes 196616 | tf_op jit(solution)/shard_map/ppermute | solution.py:301
  95.1 28.0 %collective-permute-start.21 = (bf16[512,1024]{1,0:T(8,128)(2,1)}, bf16[512,1024]{1,0:T(8,128)(2,1)}, u32[]{:S(2)}, u32[]{:S(2)}) collective-permute-start(bf16[512,1024]{1,0:T(8,128)(2,1)} %convolution_convert_fusion), channel_id=1, source_target_pairs={{0,4},{4,0},{8,12},{12,8},{16,20},{20,16},{24,28},{28,24},{1,5},{5... | collective-permute-start | bytes 3145736 | tf_op jit(solution)/shard_map/ppermute | solution.py:311
  100.5 15.1 %collective-permute-start.11 = (bf16[256,1024]{1,0:T(8,128)(2,1)}, bf16[256,1024]{1,0:T(8,128)(2,1)S(1)}, u32[]{:S(2)}, u32[]{:S(2)}) collective-permute-start(bf16[256,1024]{1,0:T(8,128)(2,1)} %get-tuple-element.89), channel_id=1, source_target_pairs={{0,1},{1,0},{2,3},{3,2},{4,5},{5,4},{6,7},{7,6},{8,9},{9,8},{10,11... | collective-permute-start | bytes 1572872 | tf_op jit(solution)/shard_map/ppermute | solution.py:306
  112.3 22.3 %collective-permute-start.24 = (bf16[64,1024]{1,0:T(8,128)(2,1)S(1)}, bf16[64,1024]{1,0:T(8,128)(2,1)S(1)}, u32[]{:S(2)}, u32[]{:S(2)}) collective-permute-start(bf16[64,1024]{1,0:T(8,128)(2,1)S(1)} %fusion.2), channel_id=1, source_target_pairs={{0,24},{4,28},{8,16},{12,20},{16,8},{20,12},{24,0},{28,4},{1,25},{... | collective-permute-start | bytes 393224 | tf_op jit(solution)/shard_map/ppermute | solution.py:301
  113.6 21.1 %collective-permute-start.23 = (bf16[64,1024]{1,0:T(8,128)(2,1)S(1)}, bf16[64,1024]{1,0:T(8,128)(2,1)S(1)}, u32[]{:S(2)}, u32[]{:S(2)}) collective-permute-start(bf16[64,1024]{1,0:T(8,128)(2,1)S(1)} %fusion.2), channel_id=1, source_target_pairs={{0,16},{4,20},{8,24},{12,28},{16,0},{20,4},{24,8},{28,12},{1,17},{... | collective-permute-start | bytes 393224 | tf_op jit(solution)/shard_map/ppermute | solution.py:301
  114.8 19.8 %collective-permute-start.22 = (bf16[64,1024]{1,0:T(8,128)(2,1)S(1)}, bf16[64,1024]{1,0:T(8,128)(2,1)S(1)}, u32[]{:S(2)}, u32[]{:S(2)}) collective-permute-start(bf16[64,1024]{1,0:T(8,128)(2,1)S(1)} %fusion.2), channel_id=1, source_target_pairs={{0,8},{4,12},{8,0},{12,4},{16,24},{20,28},{24,16},{28,20},{1,9},{5... | collective-permute-start | bytes 393224 | tf_op jit(solution)/shard_map/ppermute | solution.py:301
  117.7 17.0 %collective-permute-start.12 = (bf16[128,1024]{1,0:T(8,128)(2,1)S(1)}, bf16[128,1024]{1,0:T(8,128)(2,1)S(1)}, u32[]{:S(2)}, u32[]{:S(2)}) collective-permute-start(bf16[128,1024]{1,0:T(8,128)(2,1)S(1)} %slice.13), channel_id=1, source_target_pairs={{0,2},{1,3},{2,0},{3,1},{4,6},{5,7},{6,4},{7,5},{8,10},{9,11},{10,... | collective-permute-start | bytes 786440 | tf_op jit(solution)/shard_map/ppermute | solution.py:306
  123.1 8.6 %collective-permute-start.19 = (bf16[128,1024]{1,0:T(8,128)(2,1)}, bf16[128,1024]{1,0:T(8,128)(2,1)S(1)}, u32[]{:S(2)}, u32[]{:S(2)}) collective-permute-start(bf16[128,1024]{1,0:T(8,128)(2,1)} %get-tuple-element.110), channel_id=1, source_target_pairs={{4,0},{8,4},{12,8},{16,12},{20,16},{24,20},{28,24},{5,1},{9,5},{13... | collective-permute-start | bytes 786440 | tf_op jit(solution)/shard_map/ppermute | solution.py:316
  (24 other events, 188.9 us)

commit v18 on v16

--- a/solution.py
+++ b/solution.py
@@ -523,25 +523,11 @@
     back_entering = entering_direct(
         back_ends, back_factors, here, True, [got_cot, got_mixed] + out_pairs[1:]
     )
-    cot_rows = jnp.concatenate([near_cot, after(got_cot, back_ends)], axis=0)
-    mixed_rows = jnp.concatenate([near_mixed, after(got_mixed, back_ends)], axis=0)
-
-    def weight_share(which):
-        return lax.dot_general(
-            columns_at(cot_rows, which, width),
-            mixed_rows,
-            (((0,), (0,)), ((), ())),
-            preferred_element_type=F32,
-        )
-
-    sent_share = weight_share(1 - core).astype(BF16)
-    far_share = core_swap(sent_share)
-    grad_weight = (weight_share(core) + far_share.astype(F32)) * grad_scale
     grad_key_li, grad_query_mr, grad_spec, tap_partial = run(
         grad_long_body,
         columns,
         [
-            tile(after(grad_inner, sent_share)),
+            tile(after(grad_inner, odd)),
             tile(rate),
             tile(coef),
             tile(back_entering),
@@ -556,6 +542,20 @@
         [(rows, F32), (rows, F32), (2 * rows, F32), (rows, F32)],
         4 * pass_flops,
     )
+    cot_rows = jnp.concatenate([near_cot, after(got_cot, back_ends)], axis=0)
+    mixed_rows = jnp.concatenate([near_mixed, after(got_mixed, tap_partial)], axis=0)
+
+    def weight_share(which):
+        return lax.dot_general(
+            columns_at(cot_rows, which, width),
+            mixed_rows,
+            (((0,), (0,)), ((), ())),
+            preferred_element_type=F32,
+        )
+
+    sent_share = weight_share(1 - core).astype(BF16)
+    far_share = core_swap(sent_share)
+    grad_weight = (weight_share(core) + far_share.astype(F32)) * grad_scale
     grad_spec = after(grad_spec, first_out)
     own_product, prev_product = run(
         grad_taps_body,
@@ -577,7 +577,7 @@
     halves = tap_partial.reshape(2, tap_half, columns)
     own_half = lax.dynamic_index_in_dim(halves, core, 0, keepdims=False)
     far_half = lax.dynamic_index_in_dim(halves, 1 - core, 0, keepdims=False)
-    chip_half = (own_half + core_swap(far_half)).astype(BF16)
+    chip_half = (own_half + core_swap(after(far_half, first_out))).astype(BF16)
     everywhere = [after(chip_half, prev_product, grad_weight)] + [chip_swap(chip_half, s) for s in range(1, chips)]
     plane_half = pair_sum([part.astype(F32) for part in everywhere]) * grad_scale
     other_half = core_swap(after(plane_half, arrived_out))

time: 138 us -> 143 us (1.036)
  waiting for transfers between devices: 14.7 us -> 19.9 us
  starting transfers between devices: 39.7 us -> 42.1 us
    ppermute x13, waiting for transfers between devices: 3.49 us -> 11.4 us  [chip_swap(): return lax.ppermute(x, 'ctx', [(i, i ^ 2 * by) for i in range(size)])]
    ppermute x6, starting transfers between devices: 12.3 us -> 16.5 us  [core_swap(): return lax.ppermute(x, 'ctx', [(i, i ^ 1) for i in range(size)])]
    ppermute x5, waiting for transfers between devices: 6.72 us -> 4.21 us  [line_swap(): return lax.ppermute(x, 'fsdp', [(i, i ^ by) for i in range(size)])]
    unnamed x44 -> x40, local copies, waits for them, and re-layouts: 4.26 us -> 2.96 us
  transfers between devices with their start and end apart: 26 -> 26, of which waited for: 8 -> 7; matrix products, arithmetic and copies ran while one was open for 12% -> 10% of each run, Pallas kernels for 30% -> 29%
where the time goes in v18:
time: 143 us; the launch traced here: 142 us
  starting transfers between devices  42.1 us (29%)
  Pallas kernels  40.9 us (29%)
  waiting for transfers between devices  19.9 us (14%)
  blocking collectives  18.7 us (13%)
  other arithmetic  9.13 us (6%)
  local copies, waits for them, and re-layouts  5.51 us (4%)
  matrix products  5.06 us (4%)
    pallas_call x8, Pallas kernels, run(): pl.pallas_call(body_by_tiles, grid=(columns // block,), in_specs=in_specs...  31.7 us
    all_gather x1, blocking collectives, shards(): lax.all_gather(after(ends, beside, *cot_parts[:1]), 'ctx')  18.7 us
    ppermute x6, starting transfers between devices, core_swap(): return lax.ppermute(x, 'ctx', [(i, i ^ 1) for i in range(size)])  16.5 us
    ppermute x13, waiting for transfers between devices, chip_swap(): return lax.ppermute(x, 'ctx', [(i, i ^ 2 * by) for i in range(size)])  11.4 us
    ppermute x13, starting transfers between devices, chip_swap(): return lax.ppermute(x, 'ctx', [(i, i ^ 2 * by) for i in range(size)])  10.2 us
    pallas_call x3, Pallas kernels, run_once(): pl.pallas_call(body, grid=(1,), in_specs=[pl.BlockSpec(memory_space=pltpu...  9.18 us
    ppermute x5, starting transfers between devices, line_swap(): return lax.ppermute(x, 'fsdp', [(i, i ^ by) for i in range(size)])  8.69 us
    ppermute x2, starting transfers between devices, shifted(): lax.ppermute(x, 'ctx', [(i, i + by) for i in range(size) if 0 <= i + by <...  6.69 us
  transfers between devices with their start and end apart: 26, of which 7 were waited for; matrix products, arithmetic and copies ran while one was open for 10% of the time, Pallas kernels for 29%

profile of v18, /device:TPU:1, one launch (start us, length us, event | category | flops | bytes accessed | tf_op | source)
XLA Modules:
  0.0 142.2 jit_solution(13670534100099226516)
XLA Ops:
  1.7 4.5 %collective-permute-start = (bf16[128,1024]{1,0:T(8,128)(2,1)S(1)}, bf16[128,1024]{1,0:T(8,128)(2,1)S(1)}, u32[]{:S(2)}, u32[]{:S(2)}) collective-permute-start(bf16[128,1024]{1,0:T(8,128)(2,1)S(1)} %multiply_convert_fusion.refs_1_), channel_id=1, source_target_pairs={{0,4},{4,8},{8,12},{12,16},{16,20},{20,24},{24,28},{1,5},{5,9},{9,... | collective-permute-start | bytes 786440 | tf_op jit(solution)/shard_map/ppermute | solution.py:316
  6.3 3.2 %collective-permute-done.refs_0_ = bf16[128,1024]{1,0:T(8,128)(2,1)S(1)} collective-permute-done((bf16[128,1024]{1,0:T(8,128)(2,1)S(1)}, bf16[128,1024]{1,0:T(8,128)(2,1)S(1)}, u32[]{:S(2)}, u32[]{:S(2)}) %collective-permute-start) | collective-permute-done | bytes 262176 | tf_op jit(solution)/shard_map/ppermute | solution.py:316
  12.1 2.3 %collective-permute-start.4 = (bf16[128,1024]{1,0:T(8,128)(2,1)}, bf16[128,1024]{1,0:T(8,128)(2,1)S(1)}, u32[]{:S(2)}, u32[]{:S(2)}) collective-permute-start(bf16[128,1024]{1,0:T(8,128)(2,1)} %rest_0_), channel_id=1, source_target_pairs={{0,2},{1,3},{2,0},{3,1},{4,6},{5,7},{6,4},{7,5},{8,10},{9,11},{10,... | collective-permute-start | bytes 786440 | tf_op jit(solution)/shard_map/ppermute | solution.py:306
  16.0 3.4 %shard_map.197 = (f32[256,1024]{1,0:T(8,128)}, f32[256,1024]{1,0:T(8,128)}) custom-call(f32[128,1024]{1,0:T(8,128)} %refs_0_.1, f32[16,1024]{1,0:T(8,128)} %get-tuple-element.129.refs_1_.refs_6_.refs_3_.refs_2_, f32[16,1024]{1,0:T(8,128)} %get-tuple-element.125.refs_2_.refs_4_, f32[1,1024]{1,0:T(1,128)} %bitcast.22, ...), custom_call_target="tpu_custom_call" | custom-call | tf_op jit(solution)/shard_map/pallas_call | solution.py:272
  20.1 6.1 %shard_map.198 = (f32[256,1024]{1,0:T(8,128)}, f32[128,1024]{1,0:T(8,128)}, bf16[128,1024]{1,0:T(8,128)(2,1)}, f32[128,1024]{1,0:T(8,128)}, f32[16,1024]{1,0:T(8,128)}) custom-call(bf16[128,1024]{1,0:T(8,128)(2,1)} %copy-done.18, bf16[128,1024]{1,0:T(8,128)(2,1)} %copy-done.8, bf16[128,1024]{1,0:T(8,128)(2,1)} %refs_6_.2, bf16[128,1024]{1,0:T(8,128)(2,1)} %refs_5_.2, ...), custom_call_target="tpu_custom_call" | custom-call | tf_op jit(solution)/shard_map/pallas_call | solution.py:272
  26.2 4.2 %collective-permute-done.5.rest_3_ = bf16[128,1024]{1,0:T(8,128)(2,1)S(1)} collective-permute-done((bf16[128,1024]{1,0:T(8,128)(2,1)}, bf16[128,1024]{1,0:T(8,128)(2,1)S(1)}, u32[]{:S(2)}, u32[]{:S(2)}) %collective-permute-start.5) | collective-permute-done | bytes 262176 | tf_op jit(solution)/shard_map/ppermute | solution.py:306
  31.1 2.3 %shard_map.199 = (bf16[128,2048]{1,0:T(8,128)(2,1)}, bf16[128,2048]{1,0:T(8,128)(2,1)}) custom-call(s32[16]{0:T(128)} %stack.49.starts.refs_0_, bf16[128,1024]{1,0:T(8,128)(2,1)} %rest_0_, bf16[128,1024]{1,0:T(8,128)(2,1)} %copy-done.13, bf16[128,1024]{1,0:T(8,128)(2,1)} %copy-done.14, bf16[128,1024]{1,0:T(8,128)(2,1)} %copy-done.15), custom_call_target="tpu_custom_call" | custom-call | tf_op jit(solution)/shard_map/pallas_call | solution.py:287
  33.6 5.8 %collective-permute-start.7 = (bf16[512,1024]{1,0:T(8,128)(2,1)S(1)}, bf16[512,1024]{1,0:T(8,128)(2,1)S(1)}, u32[]{:S(2)}, u32[]{:S(2)}) collective-permute-start(bf16[512,1024]{1,0:T(8,128)(2,1)S(1)} %collective-permute-done.2.refs_5_.rest_4_), channel_id=1, source_target_pairs={{0,4},{4,0},{8,12},{12,8},{16,20},{20,16},{24,28},{28,24},{1,5},{5... | collective-permute-start | bytes 3145736 | tf_op jit(solution)/shard_map/ppermute | solution.py:311
  40.4 18.7 %all-gather.refs_5_ = f32[128,1024]{1,0:T(8,128)} all-gather(f32[16,1024]{1,0:T(8,128)} %get-tuple-element.77), channel_id=2, replica_groups=mesh['ctx'=8,'fsdp'=4] {'ctx'}, dimensions={0}, use_global_device_ids=true | all-gather | bytes 589824 | tf_op jit(solution)/shard_map/all_gather | solution.py:455
  59.1 2.8 %shard_map.200 = (f32[128,1024]{1,0:T(8,128)}, bf16[128,1024]{1,0:T(8,128)(2,1)}) custom-call(f32[8]{0:T(128)} %subtract_convert_fusion.refs_0_, f32[128,1024]{1,0:T(8,128)} %get-tuple-element.68.refs_1_, bf16[128,1024]{1,0:T(8,128)(2,1)} %refs_1_.1, f32[16,1024]{1,0:T(8,128)} %get-tuple-element.129.refs_1_.refs_6_.refs_3_.refs_2_, ...), custom_call_target="tpu_custom_call" | custom-call | tf_op jit(solution)/shard_map/pallas_call | solution.py:272
  66.2 4.2 %shard_map.201 = (f32[128,1024]{1,0:T(8,128)}, bf16[128,1024]{1,0:T(8,128)(2,1)}) custom-call(s32[16]{0:T(128)} %stack.49.starts.refs_0_, bf16[128,2048]{1,0:T(8,128)(2,1)} %get-tuple-element.79.refs_1_, bf16[128,2048]{1,0:T(8,128)(2,1)} %collective-permute-done.6.refs_2_, bf16[512,1024]{1,0:T(8,128)(2,1)} %rest_2_.1, bf16[512,1024]{1,0:T(8,128)(2,1)} %copy-done, ...), custom_call_target="tpu_custom_call" | custom-call | flops 1073741824 | bytes 6029376 | tf_op jit(solution)/shard_map/pallas_call | solution.py:272
  72.6 4.6 %shard_map.202 = (bf16[128,2048]{1,0:T(8,128)(2,1)}, bf16[128,2048]{1,0:T(8,128)(2,1)}) custom-call(s32[16]{0:T(128)} %stack.49.starts.refs_0_, bf16[128,1024]{1,0:T(8,128)(2,1)} %get-tuple-element.84.rest_0_, bf16[128,1024]{1,0:T(8,128)(2,1)} %copy-done.3, bf16[512,1024]{1,0:T(8,128)(2,1)} %rest_2_.1, bf16[512,1024]{1,0:T(8,128)(2,1)} %copy-done, ...), custom_call_target="tpu_custom_call" | custom-call | tf_op jit(solution)/shard_map/pallas_call | solution.py:287
  78.8 4.9 %shard_map.204 = (f32[128,1024]{1,0:T(8,128)}, f32[16,1024]{1,0:T(8,128)}, f32[128,1024]{1,0:T(8,128)}) custom-call(f32[128,1024]{1,0:T(8,128)} %get-tuple-element.91.refs_0_, bf16[128,1024]{1,0:T(8,128)(2,1)} %refs_1_.1, f32[16,1024]{1,0:T(8,128)} %get-tuple-element.129.refs_1_.refs_6_.refs_3_.refs_2_, f32[128,1024]{1,0:T(8,128)} %get-tuple-element.92.refs_3_, ...), custom_call_target="tpu_custom_call" | custom-call | flops 536870912 | bytes 4456448 | tf_op jit(solution)/shard_map/pallas_call | solution.py:272
  87.0 7.5 %collective-permute-done.15 = bf16[256,1024]{1,0:T(8,128)(2,1)S(1)} collective-permute-done((bf16[256,1024]{1,0:T(8,128)(2,1)S(1)}, bf16[256,1024]{1,0:T(8,128)(2,1)S(1)}, u32[]{:S(2)}, u32[]{:S(2)}) %collective-permute-start.15) | collective-permute-done | bytes 524320 | tf_op jit(solution)/shard_map/ppermute | solution.py:301
  98.3 2.3 %shard_map.203 = (bf16[256,1024]{1,0:T(8,128)(2,1)}, bf16[256,1024]{1,0:T(8,128)(2,1)}) custom-call(s32[16]{0:T(128)} %stack.49.starts.refs_0_, bf16[128,2048]{1,0:T(8,128)(2,1)} %get-tuple-element.85.rest_0_, bf16[128,2048]{1,0:T(8,128)(2,1)} %collective-permute-done.10.rest_1_), custom_call_target="tpu_custom_call" | custom-call | tf_op jit(solution)/shard_map/pallas_call | solution.py:287
  100.6 2.6 %collective-permute-start.11 = (bf16[256,1024]{1,0:T(8,128)(2,1)}, bf16[256,1024]{1,0:T(8,128)(2,1)}, u32[]{:S(2)}, u32[]{:S(2)}) collective-permute-start(bf16[256,1024]{1,0:T(8,128)(2,1)} %get-tuple-element.90), channel_id=1, source_target_pairs={{0,1},{1,0},{2,3},{3,2},{4,5},{5,4},{6,7},{7,6},{8,9},{9,8},{10,11... | collective-permute-start | bytes 1572872 | tf_op jit(solution)/shard_map/ppermute | solution.py:306
  103.8 5.1 %shard_map.205 = (f32[128,1024]{1,0:T(8,128)}, f32[128,1024]{1,0:T(8,128)}, f32[256,1024]{1,0:T(8,128)}, f32[128,1024]{1,0:T(8,128)}) custom-call(f32[128,1024]{1,0:T(8,128)} %get-tuple-element.94.refs_0_, f32[16,1024]{1,0:T(8,128)} %get-tuple-element.129.refs_1_.refs_6_.refs_3_.refs_2_, f32[16,1024]{1,0:T(8,128)} %get-tuple-element.125.refs_2_.refs_4_, ...), custom_call_target="tpu_custom_call" | custom-call | flops 536870912 | bytes 6160384 | tf_op jit(solution)/shard_map/pallas_call | solution.py:272
  110.7 2.7 %collective-permute-start.21 = (bf16[512,1024]{1,0:T(8,128)(2,1)}, bf16[512,1024]{1,0:T(8,128)(2,1)}, u32[]{:S(2)}, u32[]{:S(2)}) collective-permute-start(bf16[512,1024]{1,0:T(8,128)(2,1)} %convolution_convert_fusion), channel_id=1, source_target_pairs={{0,4},{4,0},{8,12},{12,8},{16,20},{20,16},{24,28},{28,24},{1,5},{5... | collective-permute-start | bytes 3145736 | tf_op jit(solution)/shard_map/ppermute | solution.py:311
  113.5 2.9 %collective-permute-start.20 = (f32[64,1024]{1,0:T(8,128)S(1)}, f32[64,1024]{1,0:T(8,128)S(1)}, u32[]{:S(2)}, u32[]{:S(2)}) collective-permute-start(f32[64,1024]{1,0:T(8,128)S(1)} %dynamic-slice_bitcast_fusion), channel_id=1, source_target_pairs={{0,4},{4,0},{8,12},{12,8},{16,20},{20,16},{24,28},{28,24},{1,5},{5... | collective-permute-start | bytes 786440 | tf_op jit(solution)/shard_map/ppermute | solution.py:311
  117.8 2.5 %collective-permute-start.12 = (bf16[128,1024]{1,0:T(8,128)(2,1)S(1)}, bf16[128,1024]{1,0:T(8,128)(2,1)S(1)}, u32[]{:S(2)}, u32[]{:S(2)}) collective-permute-start(bf16[128,1024]{1,0:T(8,128)(2,1)S(1)} %slice.13), channel_id=1, source_target_pairs={{0,2},{1,3},{2,0},{3,1},{4,6},{5,7},{6,4},{7,5},{8,10},{9,11},{10,... | collective-permute-start | bytes 786440 | tf_op jit(solution)/shard_map/ppermute | solution.py:306
  120.3 3.1 %shard_map.206 = (f32[128,1024]{1,0:T(8,128)}, bf16[128,1024]{1,0:T(8,128)(2,1)}) custom-call(f32[256,1024]{1,0:T(8,128)} %get-tuple-element.107.refs_0_, f32[256,1024]{1,0:T(8,128)} %get-tuple-element.66.refs_4_.refs_1_, bf16[256,768]{1,0:T(8,128)(2,1)} %constant.89.clone.refs_8_.refs_6_.refs_2_), custom_call_target="tpu_custom_call" | custom-call | flops 402653184 | bytes 3276800 | tf_op jit(solution)/shard_map/pallas_call | solution.py:272
  128.4 3.3 %add_multiply_fusion = f32[512,1024]{1,0:T(8,128)} fusion(bf16[512,1024]{1,0:T(8,128)(2,1)} %collective-permute-done.21, bf16[512,1024]{1,0:T(8,128)(2,1)S(1)} %constant_dynamic-update-slice_fusion, bf16[512,1024]{1,0:T(8,128)(2,1)S(1)} %pad_maximum_fusion, s32[]{:T(128)S(6)} %select_n.98), kind=kOutput, calls=%fused_computation | convolution fusion | flops 538443776 | bytes 4718596 | tf_op jit(solution)/shard_map/dot_general | solution.py:549
  131.7 2.8 %collective-permute-done.24 = bf16[64,1024]{1,0:T(8,128)(2,1)S(1)} collective-permute-done((bf16[64,1024]{1,0:T(8,128)(2,1)S(1)}, bf16[64,1024]{1,0:T(8,128)(2,1)S(1)}, u32[]{:S(2)}, u32[]{:S(2)}) %collective-permute-start.24) | collective-permute-done | bytes 131104 | tf_op jit(solution)/shard_map/ppermute | solution.py:301
  134.5 3.8 %collective-permute-start.25 = (f32[64,1024]{1,0:T(8,128)S(1)}, f32[64,1024]{1,0:T(8,128)S(1)}, u32[]{:S(2)}, u32[]{:S(2)}) collective-permute-start(f32[64,1024]{1,0:T(8,128)S(1)} %add_multiply_fusion.1), channel_id=1, source_target_pairs={{0,4},{4,0},{8,12},{12,8},{16,20},{20,16},{24,28},{28,24},{1,5},{5... | collective-permute-start | bytes 786440 | tf_op jit(solution)/shard_map/ppermute | solution.py:311
  (100 shorter events, 35.7 us)
Async XLA Ops:
  1.7 7.8 %collective-permute-start = (bf16[128,1024]{1,0:T(8,128)(2,1)S(1)}, bf16[128,1024]{1,0:T(8,128)(2,1)S(1)}, u32[]{:S(2)}, u32[]{:S(2)}) collective-permute-start(bf16[128,1024]{1,0:T(8,128)(2,1)S(1)} %multiply_convert_fusion.refs_1_), channel_id=1, source_target_pairs={{0,4},{4,8},{8,12},{12,16},{16,20},{20,24},{24,28},{1,5},{5,9},{9,... | collective-permute-start | bytes 786440 | tf_op jit(solution)/shard_map/ppermute | solution.py:316
  6.3 13.8 %collective-permute-start.1 = (bf16[512,1024]{1,0:T(8,128)(2,1)}, bf16[512,1024]{1,0:T(8,128)(2,1)S(1)}, u32[]{:S(2)}, u32[]{:S(2)}) collective-permute-start(bf16[512,1024]{1,0:T(8,128)(2,1)} %rest_2_.1), channel_id=1, source_target_pairs={{0,4},{4,0},{8,12},{12,8},{16,20},{20,16},{24,28},{28,24},{1,5},{5... | collective-permute-start | bytes 3145736 | tf_op jit(solution)/shard_map/ppermute | solution.py:311
  9.6 24.0 %collective-permute-start.2 = (bf16[512,1024]{1,0:T(8,128)(2,1)}, bf16[512,1024]{1,0:T(8,128)(2,1)S(1)}, u32[]{:S(2)}, u32[]{:S(2)}) collective-permute-start(bf16[512,1024]{1,0:T(8,128)(2,1)} %rest_2_.1), channel_id=1, source_target_pairs={{0,8},{4,12},{8,0},{12,4},{16,24},{20,28},{24,16},{28,20},{1,9},{5... | collective-permute-start | bytes 3145736 | tf_op jit(solution)/shard_map/ppermute | solution.py:301
  10.8 15.4 %collective-permute-start.3 = (bf16[128,1024]{1,0:T(8,128)(2,1)}, bf16[128,1024]{1,0:T(8,128)(2,1)S(1)}, u32[]{:S(2)}, u32[]{:S(2)}) collective-permute-start(bf16[128,1024]{1,0:T(8,128)(2,1)} %rest_0_), channel_id=1, source_target_pairs={{0,1},{1,0},{2,3},{3,2},{4,5},{5,4},{6,7},{7,6},{8,9},{9,8},{10,11... | collective-permute-start | bytes 786440 | tf_op jit(solution)/shard_map/ppermute | solution.py:306
  12.1 14.1 %collective-permute-start.4 = (bf16[128,1024]{1,0:T(8,128)(2,1)}, bf16[128,1024]{1,0:T(8,128)(2,1)S(1)}, u32[]{:S(2)}, u32[]{:S(2)}) collective-permute-start(bf16[128,1024]{1,0:T(8,128)(2,1)} %rest_0_), channel_id=1, source_target_pairs={{0,2},{1,3},{2,0},{3,1},{4,6},{5,7},{6,4},{7,5},{8,10},{9,11},{10,... | collective-permute-start | bytes 786440 | tf_op jit(solution)/shard_map/ppermute | solution.py:306
  14.4 16.0 %collective-permute-start.5 = (bf16[128,1024]{1,0:T(8,128)(2,1)}, bf16[128,1024]{1,0:T(8,128)(2,1)S(1)}, u32[]{:S(2)}, u32[]{:S(2)}) collective-permute-start(bf16[128,1024]{1,0:T(8,128)(2,1)} %rest_0_), channel_id=1, source_target_pairs={{0,3},{1,2},{2,1},{3,0},{4,7},{5,6},{6,5},{7,4},{8,11},{9,10},{10,... | collective-permute-start | bytes 786440 | tf_op jit(solution)/shard_map/ppermute | solution.py:306
  33.6 31.6 %collective-permute-start.7 = (bf16[512,1024]{1,0:T(8,128)(2,1)S(1)}, bf16[512,1024]{1,0:T(8,128)(2,1)S(1)}, u32[]{:S(2)}, u32[]{:S(2)}) collective-permute-start(bf16[512,1024]{1,0:T(8,128)(2,1)S(1)} %collective-permute-done.2.refs_5_.rest_4_), channel_id=1, source_target_pairs={{0,4},{4,0},{8,12},{12,8},{16,20},{20,16},{24,28},{28,24},{1,5},{5... | collective-permute-start | bytes 3145736 | tf_op jit(solution)/shard_map/ppermute | solution.py:311
  39.4 24.0 %collective-permute-start.6 = (bf16[128,2048]{1,0:T(8,128)(2,1)}, bf16[128,2048]{1,0:T(8,128)(2,1)}, u32[]{:S(2)}, u32[]{:S(2)}) collective-permute-start(bf16[128,2048]{1,0:T(8,128)(2,1)} %get-tuple-element.80), channel_id=1, source_target_pairs={{0,16},{4,20},{8,24},{12,28},{16,0},{20,4},{24,8},{28,12},{1,17},{... | collective-permute-start | bytes 1572872 | tf_op jit(solution)/shard_map/ppermute | solution.py:301
  61.9 10.0 %collective-permute-start.8 = (bf16[128,1024]{1,0:T(8,128)(2,1)}, bf16[128,1024]{1,0:T(8,128)(2,1)S(1)}, u32[]{:S(2)}, u32[]{:S(2)}) collective-permute-start(bf16[128,1024]{1,0:T(8,128)(2,1)} %get-tuple-element.84.rest_0_), channel_id=1, source_target_pairs={{0,16},{4,20},{8,24},{12,28},{16,0},{20,4},{24,8},{28,12},{1,17},{... | collective-permute-start | bytes 786440 | tf_op jit(solution)/shard_map/ppermute | solution.py:301
  70.4 7.8 %collective-permute-start.9 = (bf16[128,1024]{1,0:T(8,128)(2,1)}, bf16[128,1024]{1,0:T(8,128)(2,1)S(1)}, u32[]{:S(2)}, u32[]{:S(2)}) collective-permute-start(bf16[128,1024]{1,0:T(8,128)(2,1)} %get-tuple-element.87), channel_id=1, source_target_pairs={{0,16},{4,20},{8,24},{12,28},{16,0},{20,4},{24,8},{28,12},{1,17},{... | collective-permute-start | bytes 786440 | tf_op jit(solution)/shard_map/ppermute | solution.py:301
  70.4 14.6 %collective-permute-start.14 = (bf16[256,1024]{1,0:T(8,128)(2,1)S(1)}, bf16[256,1024]{1,0:T(8,128)(2,1)}, u32[]{:S(2)}, u32[]{:S(2)}) collective-permute-start(bf16[256,1024]{1,0:T(8,128)(2,1)S(1)} %pad_maximum_fusion.1), channel_id=1, source_target_pairs={{0,8},{4,12},{8,0},{12,4},{16,24},{20,28},{24,16},{28,20},{1,9},{5... | collective-permute-start | bytes 1572872 | tf_op jit(solution)/shard_map/ppermute | solution.py:301
  72.0 22.5 %collective-permute-start.15 = (bf16[256,1024]{1,0:T(8,128)(2,1)S(1)}, bf16[256,1024]{1,0:T(8,128)(2,1)S(1)}, u32[]{:S(2)}, u32[]{:S(2)}) collective-permute-start(bf16[256,1024]{1,0:T(8,128)(2,1)S(1)} %pad_maximum_fusion.2), channel_id=1, source_target_pairs={{0,8},{4,12},{8,0},{12,4},{16,24},{20,28},{24,16},{28,20},{1,9},{5... | collective-permute-start | bytes 1572872 | tf_op jit(solution)/shard_map/ppermute | solution.py:301
  78.1 16.4 %collective-permute-start.10 = (bf16[128,2048]{1,0:T(8,128)(2,1)}, bf16[128,2048]{1,0:T(8,128)(2,1)}, u32[]{:S(2)}, u32[]{:S(2)}) collective-permute-start(bf16[128,2048]{1,0:T(8,128)(2,1)} %get-tuple-element.88), channel_id=1, source_target_pairs={{0,16},{4,20},{8,24},{12,28},{16,0},{20,4},{24,8},{28,12},{1,17},{... | collective-permute-start | bytes 1572872 | tf_op jit(solution)/shard_map/ppermute | solution.py:301
  94.5 8.7 %collective-permute-start.16 = (f32[16,1024]{1,0:T(8,128)S(1)}, f32[16,1024]{1,0:T(8,128)S(1)}, u32[]{:S(2)}, u32[]{:S(2)}) collective-permute-start(f32[16,1024]{1,0:T(8,128)S(1)} %add_select_fusion.1), channel_id=1, source_target_pairs={{0,8},{4,12},{8,0},{12,4},{16,24},{20,28},{24,16},{28,20},{1,9},{5... | collective-permute-start | bytes 196616 | tf_op jit(solution)/shard_map/ppermute | solution.py:301
  95.9 7.2 %collective-permute-start.17 = (f32[16,1024]{1,0:T(8,128)S(1)}, f32[16,1024]{1,0:T(8,128)S(1)}, u32[]{:S(2)}, u32[]{:S(2)}) collective-permute-start(f32[16,1024]{1,0:T(8,128)S(1)} %add_select_fusion.1), channel_id=1, source_target_pairs={{0,16},{4,20},{8,24},{12,28},{16,0},{20,4},{24,8},{28,12},{1,17},{... | collective-permute-start | bytes 196616 | tf_op jit(solution)/shard_map/ppermute | solution.py:301
  96.0 7.2 %collective-permute-start.18 = (f32[16,1024]{1,0:T(8,128)S(1)}, f32[16,1024]{1,0:T(8,128)S(1)}, u32[]{:S(2)}, u32[]{:S(2)}) collective-permute-start(f32[16,1024]{1,0:T(8,128)S(1)} %add_select_fusion.1), channel_id=1, source_target_pairs={{0,24},{4,28},{8,16},{12,20},{16,8},{20,12},{24,0},{28,4},{1,25},{... | collective-permute-start | bytes 196616 | tf_op jit(solution)/shard_map/ppermute | solution.py:301
  100.6 12.9 %collective-permute-start.11 = (bf16[256,1024]{1,0:T(8,128)(2,1)}, bf16[256,1024]{1,0:T(8,128)(2,1)}, u32[]{:S(2)}, u32[]{:S(2)}) collective-permute-start(bf16[256,1024]{1,0:T(8,128)(2,1)} %get-tuple-element.90), channel_id=1, source_target_pairs={{0,1},{1,0},{2,3},{3,2},{4,5},{5,4},{6,7},{7,6},{8,9},{9,8},{10,11... | collective-permute-start | bytes 1572872 | tf_op jit(solution)/shard_map/ppermute | solution.py:306
  110.7 17.2 %collective-permute-start.21 = (bf16[512,1024]{1,0:T(8,128)(2,1)}, bf16[512,1024]{1,0:T(8,128)(2,1)}, u32[]{:S(2)}, u32[]{:S(2)}) collective-permute-start(bf16[512,1024]{1,0:T(8,128)(2,1)} %convolution_convert_fusion), channel_id=1, source_target_pairs={{0,4},{4,0},{8,12},{12,8},{16,20},{20,16},{24,28},{28,24},{1,5},{5... | collective-permute-start | bytes 3145736 | tf_op jit(solution)/shard_map/ppermute | solution.py:311
  113.5 12.1 %collective-permute-start.20 = (f32[64,1024]{1,0:T(8,128)S(1)}, f32[64,1024]{1,0:T(8,128)S(1)}, u32[]{:S(2)}, u32[]{:S(2)}) collective-permute-start(f32[64,1024]{1,0:T(8,128)S(1)} %dynamic-slice_bitcast_fusion), channel_id=1, source_target_pairs={{0,4},{4,0},{8,12},{12,8},{16,20},{20,16},{24,28},{28,24},{1,5},{5... | collective-permute-start | bytes 786440 | tf_op jit(solution)/shard_map/ppermute | solution.py:311
  117.8 16.7 %collective-permute-start.12 = (bf16[128,1024]{1,0:T(8,128)(2,1)S(1)}, bf16[128,1024]{1,0:T(8,128)(2,1)S(1)}, u32[]{:S(2)}, u32[]{:S(2)}) collective-permute-start(bf16[128,1024]{1,0:T(8,128)(2,1)S(1)} %slice.13), channel_id=1, source_target_pairs={{0,2},{1,3},{2,0},{3,1},{4,6},{5,7},{6,4},{7,5},{8,10},{9,11},{10,... | collective-permute-start | bytes 786440 | tf_op jit(solution)/shard_map/ppermute | solution.py:306
  123.4 15.0 %collective-permute-start.19 = (bf16[128,1024]{1,0:T(8,128)(2,1)}, bf16[128,1024]{1,0:T(8,128)(2,1)}, u32[]{:S(2)}, u32[]{:S(2)}) collective-permute-start(bf16[128,1024]{1,0:T(8,128)(2,1)} %get-tuple-element.109), channel_id=1, source_target_pairs={{4,0},{8,4},{12,8},{16,12},{20,16},{24,20},{28,24},{5,1},{9,5},{13... | collective-permute-start | bytes 786440 | tf_op jit(solution)/shard_map/ppermute | solution.py:316
  125.7 6.0 %collective-permute-start.22 = (bf16[64,1024]{1,0:T(8,128)(2,1)S(1)}, bf16[64,1024]{1,0:T(8,128)(2,1)S(1)}, u32[]{:S(2)}, u32[]{:S(2)}) collective-permute-start(bf16[64,1024]{1,0:T(8,128)(2,1)S(1)} %fusion.2), channel_id=1, source_target_pairs={{0,8},{4,12},{8,0},{12,4},{16,24},{20,28},{24,16},{28,20},{1,9},{5... | collective-permute-start | bytes 393224 | tf_op jit(solution)/shard_map/ppermute | solution.py:301
  127.9 6.6 %collective-permute-start.24 = (bf16[64,1024]{1,0:T(8,128)(2,1)S(1)}, bf16[64,1024]{1,0:T(8,128)(2,1)S(1)}, u32[]{:S(2)}, u32[]{:S(2)}) collective-permute-start(bf16[64,1024]{1,0:T(8,128)(2,1)S(1)} %fusion.2), channel_id=1, source_target_pairs={{0,24},{4,28},{8,16},{12,20},{16,8},{20,12},{24,0},{28,4},{1,25},{... | collective-permute-start | bytes 393224 | tf_op jit(solution)/shard_map/ppermute | solution.py:301
  134.5 6.8 %collective-permute-start.25 = (f32[64,1024]{1,0:T(8,128)S(1)}, f32[64,1024]{1,0:T(8,128)S(1)}, u32[]{:S(2)}, u32[]{:S(2)}) collective-permute-start(f32[64,1024]{1,0:T(8,128)S(1)} %add_multiply_fusion.1), channel_id=1, source_target_pairs={{0,4},{4,0},{8,12},{12,8},{16,20},{20,16},{24,28},{28,24},{1,5},{5... | collective-permute-start | bytes 786440 | tf_op jit(solution)/shard_map/ppermute | solution.py:311
  (21 other events, 214.7 us)

commit v19 on v16

--- a/solution.py
+++ b/solution.py
@@ -12,7 +12,7 @@
 
 F32 = jnp.float32
 BF16 = jnp.bfloat16
-BLOCK = 512
+BLOCK = 1024
 TILE = 256
 GROUP = 8
 

time: 138 us -> 138 us (level)
  Pallas kernels: 40.9 us -> 42.3 us
  transfers between devices with their start and end apart: 26 -> 26, of which waited for: 8 -> 8; matrix products, arithmetic and copies ran while one was open for 12% -> 12% of each run, Pallas kernels for 30% -> 31%
where the time goes in v19:
time: 138 us
  Pallas kernels  42.3 us (31%)
  starting transfers between devices  39.7 us (29%)
  blocking collectives  18.7 us (14%)
  waiting for transfers between devices  14.3 us (10%)
  other arithmetic  9.99 us (7%)
  local copies, waits for them, and re-layouts  6.88 us (5%)
  matrix products  5.02 us (4%)
    pallas_call x8, Pallas kernels, run(): pl.pallas_call(body_by_tiles, grid=(columns // block,), in_specs=in_specs...  33 us
    all_gather x1, blocking collectives, shards(): lax.all_gather(after(ends, beside, *cot_parts[:1]), 'ctx')  18.7 us
    ppermute x6, starting transfers between devices, core_swap(): return lax.ppermute(x, 'ctx', [(i, i ^ 1) for i in range(size)])  12.3 us
    ppermute x13, starting transfers between devices, chip_swap(): return lax.ppermute(x, 'ctx', [(i, i ^ 2 * by) for i in range(size)])  11.4 us
    pallas_call x3, Pallas kernels, run_once(): pl.pallas_call(body, grid=(1,), in_specs=[pl.BlockSpec(memory_space=pltpu...  9.22 us
    ppermute x5, starting transfers between devices, line_swap(): return lax.ppermute(x, 'fsdp', [(i, i ^ by) for i in range(size)])  8.48 us
    ppermute x2, starting transfers between devices, shifted(): lax.ppermute(x, 'ctx', [(i, i + by) for i in range(size) if 0 <= i + by <...  7.49 us
    ppermute x5, waiting for transfers between devices, line_swap(): return lax.ppermute(x, 'fsdp', [(i, i ^ by) for i in range(size)])  6.42 us
  transfers between devices with their start and end apart: 26, of which 8 were waited for; matrix products, arithmetic and copies ran while one was open for 12% of the time, Pallas kernels for 31%

profile of v19, /device:TPU:1, one launch (start us, length us, event | category | flops | bytes accessed | tf_op | source)
XLA Modules:
  0.0 137.7 jit_solution(8989613330235133368)
XLA Ops:
  1.7 4.5 %collective-permute-start = (bf16[128,1024]{1,0:T(8,128)(2,1)S(1)}, bf16[128,1024]{1,0:T(8,128)(2,1)S(1)}, u32[]{:S(2)}, u32[]{:S(2)}) collective-permute-start(bf16[128,1024]{1,0:T(8,128)(2,1)S(1)} %multiply_convert_fusion.refs_1_), channel_id=1, source_target_pairs={{0,4},{4,8},{8,12},{12,16},{16,20},{20,24},{24,28},{1,5},{5,9},{9,... | collective-permute-start | bytes 786440 | tf_op jit(solution)/shard_map/ppermute | solution.py:316
  6.3 3.2 %collective-permute-done.refs_0_ = bf16[128,1024]{1,0:T(8,128)(2,1)S(1)} collective-permute-done((bf16[128,1024]{1,0:T(8,128)(2,1)S(1)}, bf16[128,1024]{1,0:T(8,128)(2,1)S(1)}, u32[]{:S(2)}, u32[]{:S(2)}) %collective-permute-start) | collective-permute-done | bytes 262176 | tf_op jit(solution)/shard_map/ppermute | solution.py:316
  12.1 2.3 %collective-permute-start.4 = (bf16[128,1024]{1,0:T(8,128)(2,1)}, bf16[128,1024]{1,0:T(8,128)(2,1)S(1)}, u32[]{:S(2)}, u32[]{:S(2)}) collective-permute-start(bf16[128,1024]{1,0:T(8,128)(2,1)} %rest_0_), channel_id=1, source_target_pairs={{0,2},{1,3},{2,0},{3,1},{4,6},{5,7},{6,4},{7,5},{8,10},{9,11},{10,... | collective-permute-start | bytes 786440 | tf_op jit(solution)/shard_map/ppermute | solution.py:306
  16.0 3.5 %shard_map.197 = (f32[256,1024]{1,0:T(8,128)}, f32[256,1024]{1,0:T(8,128)}) custom-call(f32[128,1024]{1,0:T(8,128)} %refs_0_.1, f32[16,1024]{1,0:T(8,128)} %get-tuple-element.127.refs_1_.refs_6_.refs_3_.refs_2_, f32[16,1024]{1,0:T(8,128)} %get-tuple-element.123.refs_2_.refs_4_, f32[1,1024]{1,0:T(1,128)} %bitcast.22, ...), custom_call_target="tpu_custom_call" | custom-call | tf_op jit(solution)/shard_map/pallas_call | solution.py:272
  20.1 6.0 %shard_map.198 = (f32[256,1024]{1,0:T(8,128)}, f32[128,1024]{1,0:T(8,128)}, bf16[128,1024]{1,0:T(8,128)(2,1)}, f32[128,1024]{1,0:T(8,128)}, f32[16,1024]{1,0:T(8,128)}) custom-call(bf16[128,1024]{1,0:T(8,128)(2,1)} %copy-done.19, bf16[128,1024]{1,0:T(8,128)(2,1)} %copy-done.8, bf16[128,1024]{1,0:T(8,128)(2,1)} %refs_6_.2, bf16[128,1024]{1,0:T(8,128)(2,1)} %refs_5_.2, ...), custom_call_target="tpu_custom_call" | custom-call | tf_op jit(solution)/shard_map/pallas_call | solution.py:272
  26.2 4.2 %collective-permute-done.5.rest_3_ = bf16[128,1024]{1,0:T(8,128)(2,1)S(1)} collective-permute-done((bf16[128,1024]{1,0:T(8,128)(2,1)}, bf16[128,1024]{1,0:T(8,128)(2,1)S(1)}, u32[]{:S(2)}, u32[]{:S(2)}) %collective-permute-start.5) | collective-permute-done | bytes 262176 | tf_op jit(solution)/shard_map/ppermute | solution.py:306
  31.1 2.3 %shard_map.199 = (bf16[128,2048]{1,0:T(8,128)(2,1)}, bf16[128,2048]{1,0:T(8,128)(2,1)}) custom-call(s32[16]{0:T(128)} %stack.49.starts.refs_0_, bf16[128,1024]{1,0:T(8,128)(2,1)} %rest_0_, bf16[128,1024]{1,0:T(8,128)(2,1)} %copy-done.14, bf16[128,1024]{1,0:T(8,128)(2,1)} %copy-done.15, bf16[128,1024]{1,0:T(8,128)(2,1)} %copy-done.16), custom_call_target="tpu_custom_call" | custom-call | tf_op jit(solution)/shard_map/pallas_call | solution.py:287
  33.6 5.8 %collective-permute-start.7 = (bf16[512,1024]{1,0:T(8,128)(2,1)S(1)}, bf16[512,1024]{1,0:T(8,128)(2,1)S(1)}, u32[]{:S(2)}, u32[]{:S(2)}) collective-permute-start(bf16[512,1024]{1,0:T(8,128)(2,1)S(1)} %collective-permute-done.2.refs_5_.rest_4_), channel_id=1, source_target_pairs={{0,4},{4,0},{8,12},{12,8},{16,20},{20,16},{24,28},{28,24},{1,5},{5... | collective-permute-start | bytes 3145736 | tf_op jit(solution)/shard_map/ppermute | solution.py:311
  40.4 18.7 %all-gather.refs_5_ = f32[128,1024]{1,0:T(8,128)} all-gather(f32[16,1024]{1,0:T(8,128)} %get-tuple-element.76), channel_id=2, replica_groups=mesh['ctx'=8,'fsdp'=4] {'ctx'}, dimensions={0}, use_global_device_ids=true | all-gather | bytes 589824 | tf_op jit(solution)/shard_map/all_gather | solution.py:455
  59.1 3.1 %shard_map.200 = (f32[128,1024]{1,0:T(8,128)}, bf16[128,1024]{1,0:T(8,128)(2,1)}) custom-call(f32[8]{0:T(128)} %subtract_convert_fusion.refs_0_, f32[128,1024]{1,0:T(8,128)} %get-tuple-element.67.refs_1_, bf16[128,1024]{1,0:T(8,128)(2,1)} %refs_1_.1, f32[16,1024]{1,0:T(8,128)} %get-tuple-element.127.refs_1_.refs_6_.refs_3_.refs_2_, ...), custom_call_target="tpu_custom_call" | custom-call | tf_op jit(solution)/shard_map/pallas_call | solution.py:272
  66.4 4.6 %shard_map.201 = (f32[128,1024]{1,0:T(8,128)}, bf16[128,1024]{1,0:T(8,128)(2,1)}) custom-call(s32[16]{0:T(128)} %stack.49.starts.refs_0_, bf16[128,2048]{1,0:T(8,128)(2,1)} %get-tuple-element.78.refs_1_, bf16[128,2048]{1,0:T(8,128)(2,1)} %copy-done.7, bf16[512,1024]{1,0:T(8,128)(2,1)} %rest_2_.1, bf16[512,1024]{1,0:T(8,128)(2,1)} %copy-done, ...), custom_call_target="tpu_custom_call" | custom-call | flops 1073741824 | bytes 6029376 | tf_op jit(solution)/shard_map/pallas_call | solution.py:272
  73.2 4.6 %shard_map.202 = (bf16[128,2048]{1,0:T(8,128)(2,1)}, bf16[128,2048]{1,0:T(8,128)(2,1)}) custom-call(s32[16]{0:T(128)} %stack.49.starts.refs_0_, bf16[128,1024]{1,0:T(8,128)(2,1)} %get-tuple-element.83.rest_0_, bf16[128,1024]{1,0:T(8,128)(2,1)} %copy-done.5, bf16[512,1024]{1,0:T(8,128)(2,1)} %rest_2_.1, bf16[512,1024]{1,0:T(8,128)(2,1)} %copy-done, ...), custom_call_target="tpu_custom_call" | custom-call | tf_op jit(solution)/shard_map/pallas_call | solution.py:287
  80.4 5.0 %shard_map.204 = (f32[128,1024]{1,0:T(8,128)}, f32[16,1024]{1,0:T(8,128)}, f32[128,1024]{1,0:T(8,128)}) custom-call(f32[128,1024]{1,0:T(8,128)} %get-tuple-element.90.refs_0_, bf16[128,1024]{1,0:T(8,128)(2,1)} %refs_1_.1, f32[16,1024]{1,0:T(8,128)} %get-tuple-element.127.refs_1_.refs_6_.refs_3_.refs_2_, f32[128,1024]{1,0:T(8,128)} %get-tuple-element.91.refs_3_, ...), custom_call_target="tpu_custom_call" | custom-call | flops 536870912 | bytes 4456448 | tf_op jit(solution)/shard_map/pallas_call | solution.py:272
  88.1 2.1 %collective-permute-done.14 = bf16[256,1024]{1,0:T(8,128)(2,1)S(1)} collective-permute-done((bf16[256,1024]{1,0:T(8,128)(2,1)S(1)}, bf16[256,1024]{1,0:T(8,128)(2,1)S(1)}, u32[]{:S(2)}, u32[]{:S(2)}) %collective-permute-start.14) | collective-permute-done | bytes 524320 | tf_op jit(solution)/shard_map/ppermute | solution.py:301
  95.8 3.0 %collective-permute-start.21 = (bf16[512,1024]{1,0:T(8,128)(2,1)}, bf16[512,1024]{1,0:T(8,128)(2,1)}, u32[]{:S(2)}, u32[]{:S(2)}) collective-permute-start(bf16[512,1024]{1,0:T(8,128)(2,1)} %convolution_convert_fusion), channel_id=1, source_target_pairs={{0,4},{4,0},{8,12},{12,8},{16,20},{20,16},{24,28},{28,24},{1,5},{5... | collective-permute-start | bytes 3145736 | tf_op jit(solution)/shard_map/ppermute | solution.py:311
  98.8 2.3 %shard_map.203 = (bf16[256,1024]{1,0:T(8,128)(2,1)}, bf16[256,1024]{1,0:T(8,128)(2,1)}) custom-call(s32[16]{0:T(128)} %stack.49.starts.refs_0_, bf16[128,2048]{1,0:T(8,128)(2,1)} %get-tuple-element.84.rest_0_, bf16[128,2048]{1,0:T(8,128)(2,1)} %copy-done.11), custom_call_target="tpu_custom_call" | custom-call | tf_op jit(solution)/shard_map/pallas_call | solution.py:287
  101.1 2.6 %collective-permute-start.11 = (bf16[256,1024]{1,0:T(8,128)(2,1)}, bf16[256,1024]{1,0:T(8,128)(2,1)S(1)}, u32[]{:S(2)}, u32[]{:S(2)}) collective-permute-start(bf16[256,1024]{1,0:T(8,128)(2,1)} %get-tuple-element.89), channel_id=1, source_target_pairs={{0,1},{1,0},{2,3},{3,2},{4,5},{5,4},{6,7},{7,6},{8,9},{9,8},{10,11... | collective-permute-start | bytes 1572872 | tf_op jit(solution)/shard_map/ppermute | solution.py:306
  104.4 5.3 %shard_map.205 = (f32[128,1024]{1,0:T(8,128)}, f32[128,1024]{1,0:T(8,128)}, f32[256,1024]{1,0:T(8,128)}, f32[128,1024]{1,0:T(8,128)}) custom-call(f32[128,1024]{1,0:T(8,128)} %get-tuple-element.97.refs_0_, f32[16,1024]{1,0:T(8,128)} %get-tuple-element.127.refs_1_.refs_6_.refs_3_.refs_2_, f32[16,1024]{1,0:T(8,128)} %get-tuple-element.123.refs_2_.refs_4_, ...), custom_call_target="tpu_custom_call" | custom-call | flops 536870912 | bytes 6160384 | tf_op jit(solution)/shard_map/pallas_call | solution.py:272
  118.4 2.3 %collective-permute-start.12 = (bf16[128,1024]{1,0:T(8,128)(2,1)S(1)}, bf16[128,1024]{1,0:T(8,128)(2,1)S(1)}, u32[]{:S(2)}, u32[]{:S(2)}) collective-permute-start(bf16[128,1024]{1,0:T(8,128)(2,1)S(1)} %slice.13), channel_id=1, source_target_pairs={{0,2},{1,3},{2,0},{3,1},{4,6},{5,7},{6,4},{7,5},{8,10},{9,11},{10,... | collective-permute-start | bytes 786440 | tf_op jit(solution)/shard_map/ppermute | solution.py:306
  120.7 3.2 %shard_map.206 = (f32[128,1024]{1,0:T(8,128)}, bf16[128,1024]{1,0:T(8,128)(2,1)}) custom-call(f32[256,1024]{1,0:T(8,128)} %get-tuple-element.108.refs_0_, f32[256,1024]{1,0:T(8,128)} %get-tuple-element.65.refs_4_.refs_1_, bf16[256,768]{1,0:T(8,128)(2,1)} %constant.89.clone.refs_8_.refs_6_.refs_2_), custom_call_target="tpu_custom_call" | custom-call | flops 402653184 | bytes 3276800 | tf_op jit(solution)/shard_map/pallas_call | solution.py:272
  123.9 3.0 %collective-permute-start.19 = (bf16[128,1024]{1,0:T(8,128)(2,1)}, bf16[128,1024]{1,0:T(8,128)(2,1)}, u32[]{:S(2)}, u32[]{:S(2)}) collective-permute-start(bf16[128,1024]{1,0:T(8,128)(2,1)} %get-tuple-element.110), channel_id=1, source_target_pairs={{4,0},{8,4},{12,8},{16,12},{20,16},{24,20},{28,24},{5,1},{9,5},{13... | collective-permute-start | bytes 786440 | tf_op jit(solution)/shard_map/ppermute | solution.py:316
  126.8 3.3 %add_multiply_fusion = f32[512,1024]{1,0:T(8,128)} fusion(bf16[512,1024]{1,0:T(8,128)(2,1)} %collective-permute-done.21, bf16[512,1024]{1,0:T(8,128)(2,1)S(1)} %constant_dynamic-update-slice_fusion, bf16[512,1024]{1,0:T(8,128)(2,1)S(1)} %pad_maximum_fusion, s32[]{:T(128)S(6)} %select_n.99), kind=kOutput, calls=%fused_computation | convolution fusion | flops 538443776 | bytes 4718596 | tf_op jit(solution)/shard_map/dot_general | solution.py:530
  130.2 1.9 %collective-permute-done.12 = bf16[128,1024]{1,0:T(8,128)(2,1)S(1)} collective-permute-done((bf16[128,1024]{1,0:T(8,128)(2,1)S(1)}, bf16[128,1024]{1,0:T(8,128)(2,1)S(1)}, u32[]{:S(2)}, u32[]{:S(2)}) %collective-permute-start.12) | collective-permute-done | bytes 262176 | tf_op jit(solution)/shard_map/ppermute | solution.py:306
  133.7 2.3 %shard_map.207 = (f32[128,1024]{1,0:T(8,128)}, f32[128,1024]{1,0:T(8,128)}) custom-call(f32[128,1024]{1,0:T(8,128)} %get-tuple-element.109.refs_0_, bf16[128,1024]{1,0:T(8,128)(2,1)} %collective-permute-done.19.refs_1_, bf16[128,1024]{1,0:T(8,128)(2,1)} %refs_2_.6, bf16[128,1024]{1,0:T(8,128)(2,1)} %refs_3_.5), custom_call_target="tpu_custom_call" | custom-call | flops 131072 | bytes 2359296 | tf_op jit(solution)/shard_map/pallas_call | solution.py:272
  (104 shorter events, 37.6 us)
Async XLA Ops:
  1.7 7.8 %collective-permute-start = (bf16[128,1024]{1,0:T(8,128)(2,1)S(1)}, bf16[128,1024]{1,0:T(8,128)(2,1)S(1)}, u32[]{:S(2)}, u32[]{:S(2)}) collective-permute-start(bf16[128,1024]{1,0:T(8,128)(2,1)S(1)} %multiply_convert_fusion.refs_1_), channel_id=1, source_target_pairs={{0,4},{4,8},{8,12},{12,16},{16,20},{20,24},{24,28},{1,5},{5,9},{9,... | collective-permute-start | bytes 786440 | tf_op jit(solution)/shard_map/ppermute | solution.py:316
  6.3 13.9 %collective-permute-start.1 = (bf16[512,1024]{1,0:T(8,128)(2,1)}, bf16[512,1024]{1,0:T(8,128)(2,1)S(1)}, u32[]{:S(2)}, u32[]{:S(2)}) collective-permute-start(bf16[512,1024]{1,0:T(8,128)(2,1)} %rest_2_.1), channel_id=1, source_target_pairs={{0,4},{4,0},{8,12},{12,8},{16,20},{20,16},{24,28},{28,24},{1,5},{5... | collective-permute-start | bytes 3145736 | tf_op jit(solution)/shard_map/ppermute | solution.py:311
  9.6 24.0 %collective-permute-start.2 = (bf16[512,1024]{1,0:T(8,128)(2,1)}, bf16[512,1024]{1,0:T(8,128)(2,1)S(1)}, u32[]{:S(2)}, u32[]{:S(2)}) collective-permute-start(bf16[512,1024]{1,0:T(8,128)(2,1)} %rest_2_.1), channel_id=1, source_target_pairs={{0,8},{4,12},{8,0},{12,4},{16,24},{20,28},{24,16},{28,20},{1,9},{5... | collective-permute-start | bytes 3145736 | tf_op jit(solution)/shard_map/ppermute | solution.py:301
  10.8 15.4 %collective-permute-start.3 = (bf16[128,1024]{1,0:T(8,128)(2,1)}, bf16[128,1024]{1,0:T(8,128)(2,1)S(1)}, u32[]{:S(2)}, u32[]{:S(2)}) collective-permute-start(bf16[128,1024]{1,0:T(8,128)(2,1)} %rest_0_), channel_id=1, source_target_pairs={{0,1},{1,0},{2,3},{3,2},{4,5},{5,4},{6,7},{7,6},{8,9},{9,8},{10,11... | collective-permute-start | bytes 786440 | tf_op jit(solution)/shard_map/ppermute | solution.py:306
  12.1 14.1 %collective-permute-start.4 = (bf16[128,1024]{1,0:T(8,128)(2,1)}, bf16[128,1024]{1,0:T(8,128)(2,1)S(1)}, u32[]{:S(2)}, u32[]{:S(2)}) collective-permute-start(bf16[128,1024]{1,0:T(8,128)(2,1)} %rest_0_), channel_id=1, source_target_pairs={{0,2},{1,3},{2,0},{3,1},{4,6},{5,7},{6,4},{7,5},{8,10},{9,11},{10,... | collective-permute-start | bytes 786440 | tf_op jit(solution)/shard_map/ppermute | solution.py:306
  14.4 16.0 %collective-permute-start.5 = (bf16[128,1024]{1,0:T(8,128)(2,1)}, bf16[128,1024]{1,0:T(8,128)(2,1)S(1)}, u32[]{:S(2)}, u32[]{:S(2)}) collective-permute-start(bf16[128,1024]{1,0:T(8,128)(2,1)} %rest_0_), channel_id=1, source_target_pairs={{0,3},{1,2},{2,1},{3,0},{4,7},{5,6},{6,5},{7,4},{8,11},{9,10},{10,... | collective-permute-start | bytes 786440 | tf_op jit(solution)/shard_map/ppermute | solution.py:306
  33.6 31.8 %collective-permute-start.7 = (bf16[512,1024]{1,0:T(8,128)(2,1)S(1)}, bf16[512,1024]{1,0:T(8,128)(2,1)S(1)}, u32[]{:S(2)}, u32[]{:S(2)}) collective-permute-start(bf16[512,1024]{1,0:T(8,128)(2,1)S(1)} %collective-permute-done.2.refs_5_.rest_4_), channel_id=1, source_target_pairs={{0,4},{4,0},{8,12},{12,8},{16,20},{20,16},{24,28},{28,24},{1,5},{5... | collective-permute-start | bytes 3145736 | tf_op jit(solution)/shard_map/ppermute | solution.py:311
  39.4 24.2 %collective-permute-start.6 = (bf16[128,2048]{1,0:T(8,128)(2,1)}, bf16[128,2048]{1,0:T(8,128)(2,1)S(1)}, u32[]{:S(2)}, u32[]{:S(2)}) collective-permute-start(bf16[128,2048]{1,0:T(8,128)(2,1)} %get-tuple-element.79), channel_id=1, source_target_pairs={{0,16},{4,20},{8,24},{12,28},{16,0},{20,4},{24,8},{28,12},{1,17},{... | collective-permute-start | bytes 1572872 | tf_op jit(solution)/shard_map/ppermute | solution.py:301
  62.1 10.4 %collective-permute-start.8 = (bf16[128,1024]{1,0:T(8,128)(2,1)}, bf16[128,1024]{1,0:T(8,128)(2,1)S(1)}, u32[]{:S(2)}, u32[]{:S(2)}) collective-permute-start(bf16[128,1024]{1,0:T(8,128)(2,1)} %get-tuple-element.83.rest_0_), channel_id=1, source_target_pairs={{0,16},{4,20},{8,24},{12,28},{16,0},{20,4},{24,8},{28,12},{1,17},{... | collective-permute-start | bytes 786440 | tf_op jit(solution)/shard_map/ppermute | solution.py:301
  65.4 21.6 %collective-permute-start.13 = (bf16[256,1024]{1,0:T(8,128)(2,1)}, bf16[256,1024]{1,0:T(8,128)(2,1)}, u32[]{:S(2)}, u32[]{:S(2)}) collective-permute-start(bf16[256,1024]{1,0:T(8,128)(2,1)} %pad_maximum_fusion.1), channel_id=1, source_target_pairs={{0,8},{4,12},{8,0},{12,4},{16,24},{20,28},{24,16},{28,20},{1,9},{5... | collective-permute-start | bytes 1572872 | tf_op jit(solution)/shard_map/ppermute | solution.py:301
  71.1 7.9 %collective-permute-start.9 = (bf16[128,1024]{1,0:T(8,128)(2,1)}, bf16[128,1024]{1,0:T(8,128)(2,1)S(1)}, u32[]{:S(2)}, u32[]{:S(2)}) collective-permute-start(bf16[128,1024]{1,0:T(8,128)(2,1)} %get-tuple-element.86), channel_id=1, source_target_pairs={{0,16},{4,20},{8,24},{12,28},{16,0},{20,4},{24,8},{28,12},{1,17},{... | collective-permute-start | bytes 786440 | tf_op jit(solution)/shard_map/ppermute | solution.py:301
  77.8 12.4 %collective-permute-start.14 = (bf16[256,1024]{1,0:T(8,128)(2,1)S(1)}, bf16[256,1024]{1,0:T(8,128)(2,1)S(1)}, u32[]{:S(2)}, u32[]{:S(2)}) collective-permute-start(bf16[256,1024]{1,0:T(8,128)(2,1)S(1)} %pad_maximum_fusion.2), channel_id=1, source_target_pairs={{0,8},{4,12},{8,0},{12,4},{16,24},{20,28},{24,16},{28,20},{1,9},{5... | collective-permute-start | bytes 1572872 | tf_op jit(solution)/shard_map/ppermute | solution.py:301
  78.9 12.5 %collective-permute-start.10 = (bf16[128,2048]{1,0:T(8,128)(2,1)}, bf16[128,2048]{1,0:T(8,128)(2,1)S(1)}, u32[]{:S(2)}, u32[]{:S(2)}) collective-permute-start(bf16[128,2048]{1,0:T(8,128)(2,1)} %get-tuple-element.87), channel_id=1, source_target_pairs={{0,16},{4,20},{8,24},{12,28},{16,0},{20,4},{24,8},{28,12},{1,17},{... | collective-permute-start | bytes 1572872 | tf_op jit(solution)/shard_map/ppermute | solution.py:301
  91.4 12.2 %collective-permute-start.18 = (f32[16,1024]{1,0:T(8,128)S(1)}, f32[16,1024]{1,0:T(8,128)S(1)}, u32[]{:S(2)}, u32[]{:S(2)}) collective-permute-start(f32[16,1024]{1,0:T(8,128)S(1)} %add_select_fusion.1), channel_id=1, source_target_pairs={{0,24},{4,28},{8,16},{12,20},{16,8},{20,12},{24,0},{28,4},{1,25},{... | collective-permute-start | bytes 196616 | tf_op jit(solution)/shard_map/ppermute | solution.py:301
  92.6 11.1 %collective-permute-start.17 = (f32[16,1024]{1,0:T(8,128)S(1)}, f32[16,1024]{1,0:T(8,128)S(1)}, u32[]{:S(2)}, u32[]{:S(2)}) collective-permute-start(f32[16,1024]{1,0:T(8,128)S(1)} %add_select_fusion.1), channel_id=1, source_target_pairs={{0,16},{4,20},{8,24},{12,28},{16,0},{20,4},{24,8},{28,12},{1,17},{... | collective-permute-start | bytes 196616 | tf_op jit(solution)/shard_map/ppermute | solution.py:301
  93.9 9.7 %collective-permute-start.16 = (f32[16,1024]{1,0:T(8,128)S(1)}, f32[16,1024]{1,0:T(8,128)S(1)}, u32[]{:S(2)}, u32[]{:S(2)}) collective-permute-start(f32[16,1024]{1,0:T(8,128)S(1)} %add_select_fusion.1), channel_id=1, source_target_pairs={{0,8},{4,12},{8,0},{12,4},{16,24},{20,28},{24,16},{28,20},{1,9},{5... | collective-permute-start | bytes 196616 | tf_op jit(solution)/shard_map/ppermute | solution.py:301
  95.8 28.1 %collective-permute-start.21 = (bf16[512,1024]{1,0:T(8,128)(2,1)}, bf16[512,1024]{1,0:T(8,128)(2,1)}, u32[]{:S(2)}, u32[]{:S(2)}) collective-permute-start(bf16[512,1024]{1,0:T(8,128)(2,1)} %convolution_convert_fusion), channel_id=1, source_target_pairs={{0,4},{4,0},{8,12},{12,8},{16,20},{20,16},{24,28},{28,24},{1,5},{5... | collective-permute-start | bytes 3145736 | tf_op jit(solution)/shard_map/ppermute | solution.py:311
  101.1 15.1 %collective-permute-start.11 = (bf16[256,1024]{1,0:T(8,128)(2,1)}, bf16[256,1024]{1,0:T(8,128)(2,1)S(1)}, u32[]{:S(2)}, u32[]{:S(2)}) collective-permute-start(bf16[256,1024]{1,0:T(8,128)(2,1)} %get-tuple-element.89), channel_id=1, source_target_pairs={{0,1},{1,0},{2,3},{3,2},{4,5},{5,4},{6,7},{7,6},{8,9},{9,8},{10,11... | collective-permute-start | bytes 1572872 | tf_op jit(solution)/shard_map/ppermute | solution.py:306
  113.2 17.0 %collective-permute-start.24 = (bf16[64,1024]{1,0:T(8,128)(2,1)S(1)}, bf16[64,1024]{1,0:T(8,128)(2,1)S(1)}, u32[]{:S(2)}, u32[]{:S(2)}) collective-permute-start(bf16[64,1024]{1,0:T(8,128)(2,1)S(1)} %fusion.2), channel_id=1, source_target_pairs={{0,24},{4,28},{8,16},{12,20},{16,8},{20,12},{24,0},{28,4},{1,25},{... | collective-permute-start | bytes 393224 | tf_op jit(solution)/shard_map/ppermute | solution.py:301
  114.4 15.8 %collective-permute-start.23 = (bf16[64,1024]{1,0:T(8,128)(2,1)S(1)}, bf16[64,1024]{1,0:T(8,128)(2,1)S(1)}, u32[]{:S(2)}, u32[]{:S(2)}) collective-permute-start(bf16[64,1024]{1,0:T(8,128)(2,1)S(1)} %fusion.2), channel_id=1, source_target_pairs={{0,16},{4,20},{8,24},{12,28},{16,0},{20,4},{24,8},{28,12},{1,17},{... | collective-permute-start | bytes 393224 | tf_op jit(solution)/shard_map/ppermute | solution.py:301
  115.6 14.5 %collective-permute-start.22 = (bf16[64,1024]{1,0:T(8,128)(2,1)S(1)}, bf16[64,1024]{1,0:T(8,128)(2,1)S(1)}, u32[]{:S(2)}, u32[]{:S(2)}) collective-permute-start(bf16[64,1024]{1,0:T(8,128)(2,1)S(1)} %fusion.2), channel_id=1, source_target_pairs={{0,8},{4,12},{8,0},{12,4},{16,24},{20,28},{24,16},{28,20},{1,9},{5... | collective-permute-start | bytes 393224 | tf_op jit(solution)/shard_map/ppermute | solution.py:301
  118.4 13.8 %collective-permute-start.12 = (bf16[128,1024]{1,0:T(8,128)(2,1)S(1)}, bf16[128,1024]{1,0:T(8,128)(2,1)S(1)}, u32[]{:S(2)}, u32[]{:S(2)}) collective-permute-start(bf16[128,1024]{1,0:T(8,128)(2,1)S(1)} %slice.13), channel_id=1, source_target_pairs={{0,2},{1,3},{2,0},{3,1},{4,6},{5,7},{6,4},{7,5},{8,10},{9,11},{10,... | collective-permute-start | bytes 786440 | tf_op jit(solution)/shard_map/ppermute | solution.py:306
  123.9 9.8 %collective-permute-start.19 = (bf16[128,1024]{1,0:T(8,128)(2,1)}, bf16[128,1024]{1,0:T(8,128)(2,1)}, u32[]{:S(2)}, u32[]{:S(2)}) collective-permute-start(bf16[128,1024]{1,0:T(8,128)(2,1)} %get-tuple-element.110), channel_id=1, source_target_pairs={{4,0},{8,4},{12,8},{16,12},{20,16},{24,20},{28,24},{5,1},{9,5},{13... | collective-permute-start | bytes 786440 | tf_op jit(solution)/shard_map/ppermute | solution.py:316
  132.2 4.7 %collective-permute-start.25 = (f32[64,1024]{1,0:T(8,128)S(1)}, f32[64,1024]{1,0:T(8,128)S(1)}, u32[]{:S(2)}, u32[]{:S(2)}) collective-permute-start(f32[64,1024]{1,0:T(8,128)S(1)} %add_multiply_fusion.1), channel_id=1, source_target_pairs={{0,4},{4,0},{8,12},{12,8},{16,20},{20,16},{24,28},{28,24},{1,5},{5... | collective-permute-start | bytes 786440 | tf_op jit(solution)/shard_map/ppermute | solution.py:311
  (23 other events, 190.4 us)
